TPU v7x, 32 devices: a whole 2x2x4 slice. The times are simulated.
32 devices in a mesh: dp: 8 (over z, x), expert: 4 (over y, core).
Axes of the slice: x: 2, y: 2, z: 4, core: 2. Of those that a mesh axis runs over, the one named last changes fastest.
Arguments:
- grads: bfloat16 [8, 4, 512, 1024], P('dp', 'expert'), may hold values from -100 to 100
- signs: int32 [4, 1024], P('expert'), may hold values from -1 to 1, as said below
- weights: bfloat16 [4, 512, 1024], P('expert', 'dp'), may hold values from -4 to 4
- compensation: bfloat16 [4, 512, 1024], P('expert', 'dp'), may hold values from -0.099609375 to 0.099609375
Outputs:
- new_weights: bfloat16 [4, 512, 1024], P('expert')
- update_grad: float32 [4, 512, 1024], P('expert', 'dp')
Inputs may be any that keep to these rules, and one draw needn't show every extreme that they name: `signs`: each entry is -1 or +1.
All inputs are finite; a program needn't handle non-finite values.
Results may differ from a plain program's by a relative error of at most 0.0018.
The roundings to bfloat16 on the way count: a program that leaves them out, or rounds other values in their place, can miss the bound.
Values may be sent and summed in bfloat16 or wider, within the bound.
No kernel may reach another device: no remote copies, remote signals or barrier semaphores. Data moves between devices by JAX's collectives and lax.ppermute only.
A program may use at most 64 MiB of HBM per device.

v0:
```python
import math

import jax
import jax.numpy as jnp
from jax import lax
from jax.sharding import PartitionSpec as P

clamp_level = 2.0
target_rms = 0.2
learn_rate = 0.02


def hadamard(width):
    counter = lax.iota(jnp.int32, width)
    common = counter[:, None] & counter[None, :]
    parity = jnp.zeros((width, width), jnp.int32)
    for position in range(width.bit_length() - 1):
        parity = parity ^ common >> position & 1
    return (1 - 2 * parity).astype(jnp.float32)


def on_device(grads, signs, weights, compensation):
    width = grads.shape[3]
    local_grads = grads.reshape(grads.shape[2], width)
    replicas = lax.axis_size("dp")
    owned = local_grads.shape[0] // replicas
    inverse_root = 1.0 / math.sqrt(width)
    sign_row = signs.reshape(width).astype(jnp.float32)
    matrix = hadamard(width)
    forward = (sign_row[:, None] * matrix).astype(jnp.bfloat16)
    rotated = jnp.dot(local_grads, forward, preferred_element_type=jnp.float32) * inverse_root
    rms = jnp.sqrt(jnp.mean(rotated * rotated, axis=1) + 1e-06)
    scale = lax.pmax(rms, "dp")
    levels_all = jnp.clip(rotated / scale[:, None], -clamp_level, clamp_level).astype(jnp.bfloat16)
    received = lax.all_to_all(
        levels_all.reshape(replicas, owned, width), "dp", split_axis=0, concat_axis=0, tiled=True
    )
    total = jnp.sum(received.astype(jnp.float32), axis=0)
    own_scale = lax.dynamic_slice_in_dim(scale, lax.axis_index("dp") * owned, owned, 0)
    mean_rot = total * own_scale[:, None] / replicas
    unrot = (
        jnp.dot(
            mean_rot, matrix, precision=lax.Precision.HIGHEST, preferred_element_type=jnp.float32
        )
        * inverse_root
        * sign_row[None, :]
    )
    local_squares = jnp.sum(unrot * unrot)
    squares = lax.psum(local_squares, ("dp", "expert"))
    limit = target_rms * math.sqrt(owned * width * replicas * lax.axis_size("expert"))
    factor = limit / jnp.maximum(jnp.sqrt(squares), limit)
    update_grad = (unrot * factor).reshape(weights.shape)
    summed = weights.astype(jnp.float32) + (
        compensation.astype(jnp.float32) - learn_rate * update_grad
    )
    new_weights = summed.astype(jnp.bfloat16)
    gathered = lax.all_gather(new_weights, "dp", axis=1, tiled=True)
    return (gathered, update_grad)


def solution(mesh):
    in_specs = (
        P("dp", "expert", None, None),
        P("expert", None),
        P("expert", "dp", None),
        P("expert", "dp", None),
    )
    out_specs = (P("expert", None, None), P("expert", "dp", None))
    return jax.shard_map(
        on_device, mesh=mesh, in_specs=in_specs, out_specs=out_specs, check_vma=False
    )
```

profile of v0, /device:TPU:0, one launch (start us, length us, event | category | flops | bytes accessed | tf_op | source)
XLA Modules:
  0.0 162.3 jit_solution(5252858663743451353)
XLA Ops:
  7.2 0.0 copy-start
  7.2 0.8 convert_element_type.39
  8.0 0.5 copy-done
  8.4 5.6 %multiply_reduce_fusion = (f32[512]{0:T(512)S(1)}, f32[1024,512]{0,1:T(8,128)S(1)}) fusion(f32[1024]{0:T(1024)S(1)} %bitcast.19, bf16[1,1,512,1024]{3,2,1,0:T(8,128)(2,1)S(1)} %copy-done), kind=kOutput, calls=%fused_computation.7 | convolution fusion | flops 1112014336 | bytes 3151872 | tf_op jit(solution)/shard_map/dot_general | solution.py:31
  14.0 23.1 %pmax.7 = f32[512]{0:T(512)S(1)} all-reduce(f32[512]{0:T(512)S(1)} %add_sqrt_fusion), channel_id=1, replica_groups=mesh['dp'=8,'expert'=4] {'dp'}, use_global_device_ids=true, to_apply=%region_1.0 | all-reduce | flops 512 | bytes 4096 | tf_op jit(solution)/shard_map/pmax | solution.py:33
  37.1 0.0 copy-start.3
  37.1 1.4 clamp_convert_fusion
  38.5 3.6 %all-to-all-start = ((bf16[8,64,1024]{2,1,0:T(8,128)(2,1)}), bf16[8,64,1024]{2,1,0:T(8,128)(2,1)S(1)}, u32[]{:S(2)}, u32[]{:S(2)}) async-start(bf16[8,64,1024]{2,1,0:T(8,128)(2,1)} %bitcast.3), calls=%async_computation | async-start | bytes 2097152 | tf_op jit(solution)/shard_map/all_to_all | solution.py:35
  42.0 0.0 all-gather.2.cloned.1.call-start
  42.1 0.1 dynamic_slice.3
  42.2 0.0 copy-done.3
  42.2 22.3 %all-to-all-done = bf16[8,64,1024]{2,1,0:T(8,128)(2,1)S(1)} async-done(((bf16[8,64,1024]{2,1,0:T(8,128)(2,1)}), bf16[8,64,1024]{2,1,0:T(8,128)(2,1)S(1)}, u32[]{:S(2)}, u32[]{:S(2)}) %all-to-all-start) | async-done | bytes 1048608 | tf_op jit(solution)/shard_map/all_to_all | solution.py:35
  64.4 0.2 convert_reduce_fusion
  64.6 0.0 copy-start.1
  64.6 0.0 copy-start.2
  64.6 8.1 %multiply_reduce_fusion.1 = (f32[]{:T(128)}, f32[64,1024]{1,0:T(8,128)S(1)}) fusion(f32[1024]{0:T(1024)S(1)} %bitcast.18, f32[64,1024]{1,0:T(8,128)S(1)} %convert_reduce_fusion, f32[64]{0:T(128)S(1)} %dynamic_slice.3), kind=kOutput, calls=%fused_computation.14 | convolution fusion | flops 840237056 | bytes 528644 | tf_op jit(solution)/shard_map/dot_general | solution.py:42
  72.7 37.9 %psum.7 = f32[]{:T(128)} all-reduce(f32[]{:T(128)} %get-tuple-element.4), channel_id=1, replica_groups=mesh['dp'=8,'expert'=4] {'dp','expert'}, use_global_device_ids=true, to_apply=%region_4.5 | all-reduce | flops 1 | bytes 8 | tf_op jit(solution)/shard_map/psum | solution.py:49
  111.3 0.0 copy-done.1
  111.3 0.0 copy-done.2
  111.3 0.7 fusion.9
  112.0 0.0 all-gather.2.cloned.1.call-update
  112.1 0.7 multiply_bitcast_fusion
  112.8 40.4 %all-gather.2.cloned.1.call-done = bf16[1,512,1024]{2,1,0:T(8,128)(2,1)} async-done(((bf16[1,64,1024]{2,1,0:T(8,128)(2,1)}), bf16[1,512,1024]{2,1,0:T(8,128)(2,1)}) %all-gather.2.cloned.1.call-update) | async-done | bytes 1048592 | tf_op jit(solution)/shard_map/all_gather | solution.py:57
  153.2 2.3 %copy.7 = bf16[1,512,1024]{2,1,0:T(8,128)(2,1)} copy(bf16[1,512,1024]{2,1,0:T(8,128)(2,1)} %all-gather.2.cloned.1.call-done) | data formatting | bytes 2097152
  (2 shorter events, 0.0 us)
Async XLA Ops:
  7.2 1.2 copy-start
  37.1 5.1 %copy-start.3 = (s32[1,1024]{1,0:T(1,128)S(1)}, s32[1,1024]{1,0:T(1,128)}, u32[]{:S(2)}) copy-start(s32[1,1024]{1,0:T(1,128)} %param.5) | copy-start | bytes 12292
  38.5 26.0 %all-to-all-start = ((bf16[8,64,1024]{2,1,0:T(8,128)(2,1)}), bf16[8,64,1024]{2,1,0:T(8,128)(2,1)S(1)}, u32[]{:S(2)}, u32[]{:S(2)}) async-start(bf16[8,64,1024]{2,1,0:T(8,128)(2,1)} %bitcast.3), calls=%async_computation | async-start | bytes 2097152 | tf_op jit(solution)/shard_map/all_to_all | solution.py:35
  42.0 111.1 %all-gather.2.cloned.1.call-start = ((), (), s32[]{:S(2)}) async-start(), calls=%async_computation.1 | async-start | bytes 1179648 | tf_op jit(solution)/shard_map/all_gather | solution.py:57
  64.6 46.7 %copy-start.1 = (bf16[1,64,1024]{2,1,0:T(8,128)(2,1)S(1)}, bf16[1,64,1024]{2,1,0:T(8,128)(2,1)}, u32[]{:S(2)}) copy-start(bf16[1,64,1024]{2,1,0:T(8,128)(2,1)} %param.7) | copy-start | bytes 393220
  64.6 46.7 %copy-start.2 = (bf16[1,64,1024]{2,1,0:T(8,128)(2,1)S(1)}, bf16[1,64,1024]{2,1,0:T(8,128)(2,1)}, u32[]{:S(2)}) copy-start(bf16[1,64,1024]{2,1,0:T(8,128)(2,1)} %param.6) | copy-start | bytes 393220
Sparse Core Ops, SparseCore 0:
  112.2 40.9 all-gather.1
where the time goes:
time: 163 us; the launch traced here: 162 us
  waiting for transfers between devices  62.7 us (38%)
  blocking collectives  60.9 us (37%)
  between operations  14.8 us (9%)
  matrix products  13.6 us (8%)
  other arithmetic  3.81 us (2%)
  starting transfers between devices  3.6 us (2%)
  local copies, waits for them, and re-layouts  2.81 us (2%)
    all_gather x1, waiting for transfers between devices, on_device(): gathered = lax.all_gather(new_weights, 'dp', axis=1, tiled=True)  40.4 us
    psum x1, blocking collectives, on_device(): squares = lax.psum(local_squares, ('dp', 'expert'))  37.9 us
    pmax x1, blocking collectives, on_device(): scale = lax.pmax(rms, 'dp')  23.1 us
    all_to_all x1, waiting for transfers between devices, on_device(): lax.all_to_all(levels_all.reshape(replicas, owned, width), 'dp', split_ax...  22.3 us
    dot_general x1, matrix products, on_device(): jnp.dot(mean_rot, matrix, precision=lax.Precision.HIGHEST, preferred_elem...  8.06 us
    dot_general x1, matrix products, on_device(): jnp.dot(local_grads, forward, preferred_element_type=jnp.float32)  5.56 us
    all_to_all x1, starting transfers between devices, on_device(): lax.all_to_all(levels_all.reshape(replicas, owned, width), 'dp', split_ax...  3.56 us
  transfers between devices with their start and end apart: 2, of which 2 were waited for; matrix products, arithmetic and copies ran while one was open for 0% of the time, Pallas kernels for 0%

commit v1 on v0

v1 whole, which is shorter than its diff:
```python
import functools
import math

import jax
import jax.numpy as jnp
import numpy as np
from jax import lax
from jax.experimental import pallas as pl
from jax.experimental.pallas import tpu as pltpu
from jax.sharding import PartitionSpec as P

clamp_level = 2.0
target_rms = 0.2
learn_rate = 0.02
lanes = 128
vmem_bytes = 40 * 1024 * 1024


def hadamard(width):
    matrix = np.ones((1, 1), np.float32)
    while matrix.shape[0] < width:
        matrix = np.block([[matrix, matrix], [matrix, -matrix]])
    return matrix


def butterfly(groups):
    half = 1
    groups = list(groups)
    while half < len(groups):
        for start in range(0, len(groups), 2 * half):
            for i in range(start, start + half):
                upper, lower = groups[i], groups[i + half]
                groups[i], groups[i + half] = upper + lower, upper - lower
        half *= 2
    return groups


def rotate_groups(pieces, matrix, base):
    count = pieces[0].shape[1] // base
    groups = []
    for g in range(count):
        part = None
        for piece in pieces:
            term = jnp.dot(
                piece[:, g * base : (g + 1) * base], matrix, preferred_element_type=jnp.float32
            )
            part = term if part is None else part + term
        groups.append(part)
    return butterfly(groups)


def reduce_kernel(replicas, base, x_ref, sign_ref, matrix_ref, unrot_ref, square_ref, rotated):
    owned, width = x_ref.shape[1:]
    count = width // base
    matrix = matrix_ref[...]
    signs = sign_ref[...].astype(jnp.float32)
    sign_half = signs.astype(jnp.bfloat16)
    biggest = jnp.zeros((owned, 1), jnp.float32)

    def forward(r, biggest):
        groups = rotate_groups([x_ref[r] * sign_half], matrix, base)
        squares = None
        for g, group in enumerate(groups):
            rotated[r, :, g * base : (g + 1) * base] = group
            term = group * group
            squares = term if squares is None else squares + term
        return jnp.maximum(biggest, jnp.sum(squares, axis=1, keepdims=True))

    biggest = lax.fori_loop(0, replicas, forward, biggest, unroll=replicas <= 8)
    scale = jnp.sqrt(biggest * (1.0 / (width * width)) + 1e-06)
    inverse = (1.0 / math.sqrt(width)) / scale

    def add(r, total):
        level = jnp.clip(rotated[r] * inverse, -clamp_level, clamp_level)
        return total + level.astype(jnp.bfloat16).astype(jnp.float32)

    total = lax.fori_loop(
        0, replicas, add, jnp.zeros((owned, width), jnp.float32), unroll=replicas <= 8
    )
    mean_scale = scale / replicas
    mean_rot = total * mean_scale
    squares = jnp.sum(mean_rot * mean_rot)
    square_ref[...] = jnp.full(square_ref.shape, squares, jnp.float32)
    high = total.astype(jnp.bfloat16)
    low = (total - high.astype(jnp.float32)).astype(jnp.bfloat16)
    groups = rotate_groups([high, low], matrix, base)
    back = mean_scale * (1.0 / math.sqrt(width))
    for g in range(count):
        cut = slice(g * base, (g + 1) * base)
        unrot_ref[:, cut] = groups[g] * back * signs[:, cut]


def update_kernel(limit, square_ref, unrot_ref, weight_ref, comp_ref, new_ref, update_ref):
    squares = jnp.sum(square_ref[...], axis=0, keepdims=True)[:, 0:1]
    factor = limit / jnp.maximum(jnp.sqrt(squares), limit)
    update = unrot_ref[...] * factor
    update_ref[...] = update
    summed = weight_ref[...].astype(jnp.float32) + (
        comp_ref[...].astype(jnp.float32) - learn_rate * update
    )
    new_ref[...] = summed.astype(jnp.bfloat16)


def gather_blocks(block, replicas):
    x_count = 1 << ((replicas.bit_length() - 1) // 2)
    z_count = replicas // x_count
    me = lax.axis_index("dp")

    def swap(value, mask):
        return lax.ppermute(value, "dp", [(i, i ^ mask) for i in range(replicas)])

    pieces = {0: block}
    for x in range(1, x_count):
        pieces[x] = swap(block, x)
    for z in range(1, z_count):
        pieces[z * x_count] = swap(block, z * x_count)
    for z in range(1, z_count):
        for x in range(1, x_count):
            pieces[z * x_count + x] = swap(pieces[z * x_count], x)
    owned, width = block.shape
    out = jnp.zeros((replicas, owned, width), block.dtype)
    for mask, piece in pieces.items():
        out = lax.dynamic_update_slice(out, piece[None], (me ^ mask, 0, 0))
    return out.reshape(1, replicas * owned, width)


def on_device(grads, signs, weights, compensation):
    blocks, width = grads.shape[2:]
    replicas = lax.axis_size("dp")
    devices = replicas * lax.axis_size("expert")
    owned = blocks // replicas
    base = min(width, 256)
    matrix = jnp.asarray(hadamard(base), jnp.bfloat16)
    received = lax.all_to_all(
        grads.reshape(replicas, owned, width), "dp", split_axis=0, concat_axis=0, tiled=True
    )
    unrot, squares = pl.pallas_call(
        functools.partial(reduce_kernel, replicas, base),
        out_shape=(
            jax.ShapeDtypeStruct((owned, width), jnp.float32),
            jax.ShapeDtypeStruct((devices, 1, lanes), jnp.float32),
        ),
        scratch_shapes=[pltpu.VMEM((replicas, owned, width), jnp.float32)],
        compiler_params=pltpu.CompilerParams(vmem_limit_bytes=vmem_bytes),
        cost_estimate=pl.CostEstimate(
            flops=2 * blocks * width * base, bytes_accessed=2 * blocks * width, transcendentals=0
        ),
        name="reduce_blocks",
    )(received, signs, matrix)
    squares = lax.all_to_all(squares, ("dp", "expert"), split_axis=0, concat_axis=0, tiled=True)
    limit = target_rms * math.sqrt(blocks * width * lax.axis_size("expert"))
    new_weights, update_grad = pl.pallas_call(
        functools.partial(update_kernel, limit),
        out_shape=(
            jax.ShapeDtypeStruct((owned, width), jnp.bfloat16),
            jax.ShapeDtypeStruct((owned, width), jnp.float32),
        ),
        compiler_params=pltpu.CompilerParams(vmem_limit_bytes=vmem_bytes),
        name="update_blocks",
    )(
        squares.reshape(devices, lanes),
        unrot,
        weights.reshape(owned, width),
        compensation.reshape(owned, width),
    )
    return gather_blocks(new_weights, replicas), update_grad.reshape(weights.shape)


def solution(mesh):
    in_specs = (
        P("dp", "expert", None, None),
        P("expert", None),
        P("expert", "dp", None),
        P("expert", "dp", None),
    )
    out_specs = (P("expert", None, None), P("expert", "dp", None))
    return jax.shard_map(
        on_device, mesh=mesh, in_specs=in_specs, out_specs=out_specs, check_vma=False
    )
```

time: 163 us -> 68.9 us (0.42)
  waiting for transfers between devices: 62.7 us -> 18.4 us
  blocking collectives: 60.9 us -> 33.2 us
  between operations: 14.8 us -> 0.79 us
  matrix products: 13.6 us -> 0 us
  starting transfers between devices: 3.6 us -> 12.1 us
  other arithmetic: 3.81 us -> 0 us
  Pallas kernels: 0 us -> 3.05 us
    all_gather x1 -> x0, waiting for transfers between devices: 40.4 us -> none  [on_device(): gathered = lax.all_gather(new_weights, 'dp', axis=1, tiled=True)]
    psum x1 -> x0, blocking collectives: 37.9 us -> none  [on_device(): squares = lax.psum(local_squares, ('dp', 'expert'))]
    all_to_all x0 -> x1, blocking collectives: none -> 33.2 us  [on_device(): lax.all_to_all(grads.reshape(replicas, owned, width), 'dp', split_axis=0,...]
    pmax x1 -> x0, blocking collectives: 23.1 us -> none  [on_device(): scale = lax.pmax(rms, 'dp')]
    all_to_all x1, waiting for transfers between devices: 22.3 us -> 7.03 us  [on_device(): lax.all_to_all(squares, ('dp', 'expert'), split_axis=0, concat_axis=0, ti...]
    dot_general x2 -> x0, matrix products: 13.6 us -> none  [the longest x1 8.06 us: on_device(): jnp.dot(mean_rot, matrix, precision=lax.Precision.HIGHEST, preferred_elem...]
    ppermute x0 -> x7, waiting for transfers between devices: none -> 11.3 us  [swap(): return lax.ppermute(value, 'dp', [(i, i ^ mask) for i in range(replicas)])]
    ppermute x0 -> x7, starting transfers between devices: none -> 8.49 us  [swap(): return lax.ppermute(value, 'dp', [(i, i ^ mask) for i in range(replicas)])]
  transfers between devices with their start and end apart: 2 -> 8, of which waited for: 2 -> 5; matrix products, arithmetic and copies ran while one was open for 0% -> 0% of each run, Pallas kernels for 0% -> 0%
where the time goes in v1:
time: 68.9 us; the launch traced here: 68.7 us
  blocking collectives  33.2 us (48%)
  waiting for transfers between devices  18.4 us (27%)
  starting transfers between devices  12.1 us (18%)
  Pallas kernels  3.05 us (4%)
  local copies, waits for them, and re-layouts  1.21 us (2%)
  between operations  0.79 us (1%)
    all_to_all x1, blocking collectives, on_device(): lax.all_to_all(grads.reshape(replicas, owned, width), 'dp', split_axis=0,...  33.2 us
    ppermute x7, waiting for transfers between devices, swap(): return lax.ppermute(value, 'dp', [(i, i ^ mask) for i in range(replicas)])  11.3 us
    ppermute x7, starting transfers between devices, swap(): return lax.ppermute(value, 'dp', [(i, i ^ mask) for i in range(replicas)])  8.49 us
    all_to_all x1, waiting for transfers between devices, on_device(): lax.all_to_all(squares, ('dp', 'expert'), split_axis=0, concat_axis=0, ti...  7.03 us
    all_to_all x1, starting transfers between devices, on_device(): lax.all_to_all(squares, ('dp', 'expert'), split_axis=0, concat_axis=0, ti...  3.63 us
    pallas_call x1, Pallas kernels, on_device(): pl.pallas_call(functools.partial(reduce_kernel, replicas, base), out_shap...  2.23 us
  transfers between devices with their start and end apart: 8, of which 5 were waited for; matrix products, arithmetic and copies ran while one was open for 0% of the time, Pallas kernels for 0%

profile of v1, /device:TPU:0, one launch (start us, length us, event | category | flops | bytes accessed | tf_op | source)
XLA Modules:
  0.0 68.7 jit_solution(6962049603977833870)
XLA Ops:
  0.6 0.0 copy-start
  0.6 0.0 copy-start.3
  0.7 33.2 %all_to_all.10.x_ref = bf16[8,64,1024]{2,1,0:T(8,128)(2,1)S(1)} all-to-all(bf16[8,64,1024]{2,1,0:T(8,128)(2,1)} %bitcast.25), channel_id=1, replica_groups=mesh['dp'=8,'expert'=4] {'dp'}, dimensions={0} | all-to-all | bytes 2097152 | tf_op jit(solution)/shard_map/all_to_all | solution.py:134
  33.8 2.2 %reduce_blocks.1 = (f32[64,1024]{1,0:T(8,128)S(1)}, f32[32,1,128]{2,1,0:T(1,128)}) custom-call(bf16[8,64,1024]{2,1,0:T(8,128)(2,1)S(1)} %all_to_all.10.x_ref, s32[1,1024]{1,0:T(1,128)S(1)} %copy-done.3, bf16[256,256]{1,0:T(8,128)(2,1)S(1)} %copy-done), custom_call_target="tpu_custom_call" | custom-call | flops 268435456 | bytes 1048576 | tf_op jit(solution)/shard_map/reduce_blocks/pallas_call | solution.py:137
  36.1 3.6 %all-to-all-start.1 = ((f32[32,1,128]{2,1,0:T(1,128)}), f32[32,1,128]{2,1,0:T(1,128)S(1)}, u32[]{:S(2)}, u32[]{:S(2)}) async-start(f32[32,1,128]{2,1,0:T(1,128)} %get-tuple-element.6), calls=%async_computation.1 | async-start | bytes 32768 | tf_op jit(solution)/shard_map/all_to_all | solution.py:150
  39.7 7.0 %all-to-all-done.1 = f32[32,1,128]{2,1,0:T(1,128)S(1)} async-done(((f32[32,1,128]{2,1,0:T(1,128)}), f32[32,1,128]{2,1,0:T(1,128)S(1)}, u32[]{:S(2)}, u32[]{:S(2)}) %all-to-all-start.1) | async-done | bytes 16416 | tf_op jit(solution)/shard_map/all_to_all | solution.py:150
  46.8 0.8 %update_blocks.1 = (bf16[64,1024]{1,0:T(8,128)(2,1)S(1)}, f32[64,1024]{1,0:T(8,128)}) custom-call(f32[32,128]{1,0:T(8,128)S(1)} %bitcast.24, f32[64,1024]{1,0:T(8,128)S(1)} %get-tuple-element.7.unrot_ref, bf16[64,1024]{1,0:T(8,128)(2,1)S(1)} %bitcast.22, bf16[64,1024]{1,0:T(8,128)(2,1)S(1)} %bitcast.23), custom_call_target="tpu_custom_call" | custom-call | tf_op jit(solution)/shard_map/update_blocks/pallas_call | solution.py:152
  47.6 0.6 collective-permute-start
  48.2 0.6 collective-permute-start.1
  48.7 0.5 collective-permute-start.2
  49.3 3.3 %collective-permute-start.3 = (bf16[64,1024]{1,0:T(8,128)(2,1)S(1)}, bf16[64,1024]{1,0:T(8,128)(2,1)S(1)}, u32[]{:S(2)}, u32[]{:S(2)}) collective-permute-start(bf16[64,1024]{1,0:T(8,128)(2,1)S(1)} %get-tuple-element.8), channel_id=1, source_target_pairs={{0,24},{4,28},{8,16},{12,20},{16,8},{20,12},{24,0},{28,4},{1,25},{... | collective-permute-start | bytes 393224 | tf_op jit(solution)/shard_map/ppermute | solution.py:110
  52.6 0.1 broadcast_in_dim.27
  52.7 2.0 %collective-permute-done.1 = bf16[64,1024]{1,0:T(8,128)(2,1)S(1)} collective-permute-done((bf16[64,1024]{1,0:T(8,128)(2,1)S(1)}, bf16[64,1024]{1,0:T(8,128)(2,1)S(1)}, u32[]{:S(2)}, u32[]{:S(2)}) %collective-permute-start.1) | collective-permute-done | bytes 131104 | tf_op jit(solution)/shard_map/ppermute | solution.py:110
  54.7 1.5 %collective-permute-start.4 = (bf16[64,1024]{1,0:T(8,128)(2,1)S(1)}, bf16[64,1024]{1,0:T(8,128)(2,1)S(1)}, u32[]{:S(2)}, u32[]{:S(2)}) collective-permute-start(bf16[64,1024]{1,0:T(8,128)(2,1)S(1)} %collective-permute-done.1), channel_id=1, source_target_pairs={{0,4},{4,0},{8,12},{12,8},{16,20},{20,16},{24,28},{28,24},{1,5},{5... | collective-permute-start | bytes 393224 | tf_op jit(solution)/shard_map/ppermute | solution.py:110
  56.2 5.1 %collective-permute-done.2 = bf16[64,1024]{1,0:T(8,128)(2,1)S(1)} collective-permute-done((bf16[64,1024]{1,0:T(8,128)(2,1)S(1)}, bf16[64,1024]{1,0:T(8,128)(2,1)S(1)}, u32[]{:S(2)}, u32[]{:S(2)}) %collective-permute-start.2) | collective-permute-done | bytes 131104 | tf_op jit(solution)/shard_map/ppermute | solution.py:110
  61.2 1.5 %collective-permute-start.5 = (bf16[64,1024]{1,0:T(8,128)(2,1)S(1)}, bf16[64,1024]{1,0:T(8,128)(2,1)S(1)}, u32[]{:S(2)}, u32[]{:S(2)}) collective-permute-start(bf16[64,1024]{1,0:T(8,128)(2,1)S(1)} %collective-permute-done.2), channel_id=1, source_target_pairs={{0,4},{4,0},{8,12},{12,8},{16,20},{20,16},{24,28},{28,24},{1,5},{5... | collective-permute-start | bytes 393224 | tf_op jit(solution)/shard_map/ppermute | solution.py:110
  62.7 0.0 collective-permute-done.3
  62.7 0.5 collective-permute-start.6
  63.3 0.0 collective-permute-done
  63.4 0.0 collective-permute-done.4
  63.4 2.8 %collective-permute-done.5 = bf16[64,1024]{1,0:T(8,128)(2,1)S(1)} collective-permute-done((bf16[64,1024]{1,0:T(8,128)(2,1)S(1)}, bf16[64,1024]{1,0:T(8,128)(2,1)S(1)}, u32[]{:S(2)}, u32[]{:S(2)}) %collective-permute-start.5) | collective-permute-done | bytes 131104 | tf_op jit(solution)/shard_map/ppermute | solution.py:110
  66.2 1.5 %collective-permute-done.6 = bf16[64,1024]{1,0:T(8,128)(2,1)S(1)} collective-permute-done((bf16[64,1024]{1,0:T(8,128)(2,1)S(1)}, bf16[64,1024]{1,0:T(8,128)(2,1)S(1)}, u32[]{:S(2)}, u32[]{:S(2)}) %collective-permute-start.6) | collective-permute-done | bytes 131104 | tf_op jit(solution)/shard_map/ppermute | solution.py:110
  67.7 0.0 copy-start.4
  67.7 1.0 %copy-done.4 = bf16[8,64,1024]{2,1,0:T(8,128)(2,1)} copy-done((bf16[8,64,1024]{2,1,0:T(8,128)(2,1)}, bf16[8,64,1024]{2,1,0:T(8,128)(2,1)S(1)}, u32[]{:S(2)}) %copy-start.4) | copy-done | bytes 1048600
  (14 shorter events, 0.1 us)
Async XLA Ops:
  0.6 33.2 %copy-start = (bf16[256,256]{1,0:T(8,128)(2,1)S(1)}, bf16[256,256]{1,0:T(8,128)(2,1)}, u32[]{:S(2)}) copy-start(bf16[256,256]{1,0:T(8,128)(2,1)} %constant.28.clone.matrix_ref) | copy-start | bytes 393220
  0.6 33.2 %copy-start.3 = (s32[1,1024]{1,0:T(1,128)S(1)}, s32[1,1024]{1,0:T(1,128)}, u32[]{:S(2)}) copy-start(s32[1,1024]{1,0:T(1,128)} %sign_ref.1) | copy-start | bytes 12292
  33.8 13.0 %copy-start.1 = (bf16[1,64,1024]{2,1,0:T(8,128)(2,1)S(1)}, bf16[1,64,1024]{2,1,0:T(8,128)(2,1)}, u32[]{:S(2)}) copy-start(bf16[1,64,1024]{2,1,0:T(8,128)(2,1)} %param.7) | copy-start | bytes 393220
  33.8 13.0 %copy-start.2 = (bf16[1,64,1024]{2,1,0:T(8,128)(2,1)S(1)}, bf16[1,64,1024]{2,1,0:T(8,128)(2,1)}, u32[]{:S(2)}) copy-start(bf16[1,64,1024]{2,1,0:T(8,128)(2,1)} %param.8) | copy-start | bytes 393220
  36.1 10.7 %all-to-all-start.1 = ((f32[32,1,128]{2,1,0:T(1,128)}), f32[32,1,128]{2,1,0:T(1,128)S(1)}, u32[]{:S(2)}, u32[]{:S(2)}) async-start(f32[32,1,128]{2,1,0:T(1,128)} %get-tuple-element.6), calls=%async_computation.1 | async-start | bytes 32768 | tf_op jit(solution)/shard_map/all_to_all | solution.py:150
  47.6 15.7 %collective-permute-start = (bf16[64,1024]{1,0:T(8,128)(2,1)S(1)}, bf16[64,1024]{1,0:T(8,128)(2,1)S(1)}, u32[]{:S(2)}, u32[]{:S(2)}) collective-permute-start(bf16[64,1024]{1,0:T(8,128)(2,1)S(1)} %get-tuple-element.8), channel_id=1, source_target_pairs={{0,4},{4,0},{8,12},{12,8},{16,20},{20,16},{24,28},{28,24},{1,5},{5... | collective-permute-start | bytes 393224 | tf_op jit(solution)/shard_map/ppermute | solution.py:110
  48.2 6.5 %collective-permute-start.1 = (bf16[64,1024]{1,0:T(8,128)(2,1)S(1)}, bf16[64,1024]{1,0:T(8,128)(2,1)S(1)}, u32[]{:S(2)}, u32[]{:S(2)}) collective-permute-start(bf16[64,1024]{1,0:T(8,128)(2,1)S(1)} %get-tuple-element.8), channel_id=1, source_target_pairs={{0,8},{4,12},{8,0},{12,4},{16,24},{20,28},{24,16},{28,20},{1,9},{5... | collective-permute-start | bytes 393224 | tf_op jit(solution)/shard_map/ppermute | solution.py:110
  48.7 12.5 %collective-permute-start.2 = (bf16[64,1024]{1,0:T(8,128)(2,1)S(1)}, bf16[64,1024]{1,0:T(8,128)(2,1)S(1)}, u32[]{:S(2)}, u32[]{:S(2)}) collective-permute-start(bf16[64,1024]{1,0:T(8,128)(2,1)S(1)} %get-tuple-element.8), channel_id=1, source_target_pairs={{0,16},{4,20},{8,24},{12,28},{16,0},{20,4},{24,8},{28,12},{1,17},{... | collective-permute-start | bytes 393224 | tf_op jit(solution)/shard_map/ppermute | solution.py:110
  49.3 13.5 %collective-permute-start.3 = (bf16[64,1024]{1,0:T(8,128)(2,1)S(1)}, bf16[64,1024]{1,0:T(8,128)(2,1)S(1)}, u32[]{:S(2)}, u32[]{:S(2)}) collective-permute-start(bf16[64,1024]{1,0:T(8,128)(2,1)S(1)} %get-tuple-element.8), channel_id=1, source_target_pairs={{0,24},{4,28},{8,16},{12,20},{16,8},{20,12},{24,0},{28,4},{1,25},{... | collective-permute-start | bytes 393224 | tf_op jit(solution)/shard_map/ppermute | solution.py:110
  54.7 8.7 %collective-permute-start.4 = (bf16[64,1024]{1,0:T(8,128)(2,1)S(1)}, bf16[64,1024]{1,0:T(8,128)(2,1)S(1)}, u32[]{:S(2)}, u32[]{:S(2)}) collective-permute-start(bf16[64,1024]{1,0:T(8,128)(2,1)S(1)} %collective-permute-done.1), channel_id=1, source_target_pairs={{0,4},{4,0},{8,12},{12,8},{16,20},{20,16},{24,28},{28,24},{1,5},{5... | collective-permute-start | bytes 393224 | tf_op jit(solution)/shard_map/ppermute | solution.py:110
  61.2 5.0 %collective-permute-start.5 = (bf16[64,1024]{1,0:T(8,128)(2,1)S(1)}, bf16[64,1024]{1,0:T(8,128)(2,1)S(1)}, u32[]{:S(2)}, u32[]{:S(2)}) collective-permute-start(bf16[64,1024]{1,0:T(8,128)(2,1)S(1)} %collective-permute-done.2), channel_id=1, source_target_pairs={{0,4},{4,0},{8,12},{12,8},{16,20},{20,16},{24,28},{28,24},{1,5},{5... | collective-permute-start | bytes 393224 | tf_op jit(solution)/shard_map/ppermute | solution.py:110
  62.7 5.0 %collective-permute-start.6 = (bf16[64,1024]{1,0:T(8,128)(2,1)S(1)}, bf16[64,1024]{1,0:T(8,128)(2,1)S(1)}, u32[]{:S(2)}, u32[]{:S(2)}) collective-permute-start(bf16[64,1024]{1,0:T(8,128)(2,1)S(1)} %collective-permute-done.3), channel_id=1, source_target_pairs={{0,4},{4,0},{8,12},{12,8},{16,20},{20,16},{24,28},{28,24},{1,5},{5... | collective-permute-start | bytes 393224 | tf_op jit(solution)/shard_map/ppermute | solution.py:110
  67.7 1.0 %copy-start.4 = (bf16[8,64,1024]{2,1,0:T(8,128)(2,1)}, bf16[8,64,1024]{2,1,0:T(8,128)(2,1)S(1)}, u32[]{:S(2)}) copy-start(bf16[8,64,1024]{2,1,0:T(8,128)(2,1)S(1)} %bitcast_dynamic-update-slice_fusion) | copy-start | bytes 3145732

commit v2 on v1

--- a/solution.py
+++ b/solution.py
@@ -49,45 +49,56 @@
     return butterfly(groups)
 
 
-def reduce_kernel(replicas, base, x_ref, sign_ref, matrix_ref, unrot_ref, square_ref, rotated):
-    owned, width = x_ref.shape[1:]
-    count = width // base
+def rotate_kernel(count, base, *refs):
+    pieces, (sign_ref, matrix_ref, rotated, biggest_ref) = refs[:count], refs[count:]
+    rotate_pieces(pieces, sign_ref, matrix_ref, rotated, biggest_ref, None, base)
+
+
+def rotate_pieces(pieces, sign_ref, matrix_ref, rotated, biggest_ref, biggest, base):
     matrix = matrix_ref[...]
-    signs = sign_ref[...].astype(jnp.float32)
-    sign_half = signs.astype(jnp.bfloat16)
-    biggest = jnp.zeros((owned, 1), jnp.float32)
-
-    def forward(r, biggest):
-        groups = rotate_groups([x_ref[r] * sign_half], matrix, base)
+    signs = sign_ref[...].astype(jnp.float32).astype(jnp.bfloat16)
+    for r, piece in enumerate(pieces):
+        groups = rotate_groups([piece[...] * signs], matrix, base)
         squares = None
         for g, group in enumerate(groups):
             rotated[r, :, g * base : (g + 1) * base] = group
             term = group * group
             squares = term if squares is None else squares + term
-        return jnp.maximum(biggest, jnp.sum(squares, axis=1, keepdims=True))
-
-    biggest = lax.fori_loop(0, replicas, forward, biggest, unroll=replicas <= 8)
+        squares = jnp.sum(squares, axis=1, keepdims=True)
+        biggest = squares if biggest is None else jnp.maximum(biggest, squares)
+    if biggest_ref is not None:
+        biggest_ref[...] = jnp.broadcast_to(biggest, biggest_ref.shape)
+    return biggest
+
+
+def reduce_kernel(count, base, *refs):
+    pieces, rest = refs[:count], refs[count:]
+    near_ref, biggest_ref, sign_ref, matrix_ref, unrot_ref, square_ref, rotated = rest
+    owned, width = unrot_ref.shape
+    near = near_ref.shape[0]
+    replicas = near + count
+    biggest = rotate_pieces(
+        pieces, sign_ref, matrix_ref, rotated, None, biggest_ref[:, 0:1], base
+    )
     scale = jnp.sqrt(biggest * (1.0 / (width * width)) + 1e-06)
     inverse = (1.0 / math.sqrt(width)) / scale
-
-    def add(r, total):
-        level = jnp.clip(rotated[r] * inverse, -clamp_level, clamp_level)
-        return total + level.astype(jnp.bfloat16).astype(jnp.float32)
-
-    total = lax.fori_loop(
-        0, replicas, add, jnp.zeros((owned, width), jnp.float32), unroll=replicas <= 8
-    )
+    total = None
+    for source, r in [(near_ref, r) for r in range(near)] + [(rotated, r) for r in range(count)]:
+        level = jnp.clip(source[r] * inverse, -clamp_level, clamp_level)
+        level = level.astype(jnp.bfloat16).astype(jnp.float32)
+        total = level if total is None else total + level
     mean_scale = scale / replicas
     mean_rot = total * mean_scale
     squares = jnp.sum(mean_rot * mean_rot)
     square_ref[...] = jnp.full(square_ref.shape, squares, jnp.float32)
     high = total.astype(jnp.bfloat16)
     low = (total - high.astype(jnp.float32)).astype(jnp.bfloat16)
-    groups = rotate_groups([high, low], matrix, base)
+    groups = rotate_groups([high, low], matrix_ref[...], base)
     back = mean_scale * (1.0 / math.sqrt(width))
-    for g in range(count):
+    signs = sign_ref[...].astype(jnp.float32)
+    for g, group in enumerate(groups):
         cut = slice(g * base, (g + 1) * base)
-        unrot_ref[:, cut] = groups[g] * back * signs[:, cut]
+        unrot_ref[:, cut] = group * back * signs[:, cut]
 
 
 def update_kernel(limit, square_ref, unrot_ref, weight_ref, comp_ref, new_ref, update_ref):
@@ -101,13 +112,15 @@
     new_ref[...] = summed.astype(jnp.bfloat16)
 
 
+def swap(value, mask):
+    size = lax.axis_size("dp")
+    return lax.ppermute(value, "dp", [(i, i ^ mask) for i in range(size)])
+
+
 def gather_blocks(block, replicas):
     x_count = 1 << ((replicas.bit_length() - 1) // 2)
     z_count = replicas // x_count
     me = lax.axis_index("dp")
-
-    def swap(value, mask):
-        return lax.ppermute(value, "dp", [(i, i ^ mask) for i in range(replicas)])
 
     pieces = {0: block}
     for x in range(1, x_count):
@@ -131,22 +144,43 @@
     owned = blocks // replicas
     base = min(width, 256)
     matrix = jnp.asarray(hadamard(base), jnp.bfloat16)
-    received = lax.all_to_all(
-        grads.reshape(replicas, owned, width), "dp", split_axis=0, concat_axis=0, tiled=True
-    )
+    me = lax.axis_index("dp")
+    local = grads.reshape(replicas, owned, width)
+
+    def block_of(index):
+        return lax.dynamic_slice_in_dim(local, index, 1, 0).reshape(owned, width)
+
+    near = max(replicas // 2, 1)
+    pieces = {}
+    for mask in list(range(near, replicas)) + list(range(1, near)):
+        pieces[mask] = swap(block_of(me ^ mask), mask)
+    pieces[0] = block_of(me)
+    params = pltpu.CompilerParams(vmem_limit_bytes=vmem_bytes)
+    cost = pl.CostEstimate(
+        flops=blocks * width * base, bytes_accessed=3 * blocks * width, transcendentals=0
+    )
+    near_rotated, biggest = pl.pallas_call(
+        functools.partial(rotate_kernel, near, base),
+        out_shape=(
+            jax.ShapeDtypeStruct((near, owned, width), jnp.float32),
+            jax.ShapeDtypeStruct((owned, lanes), jnp.float32),
+        ),
+        compiler_params=params,
+        cost_estimate=cost,
+        name="rotate_near",
+    )(*[pieces[mask] for mask in range(near)], signs, matrix)
+    far = replicas - near
     unrot, squares = pl.pallas_call(
-        functools.partial(reduce_kernel, replicas, base),
+        functools.partial(reduce_kernel, far, base),
         out_shape=(
             jax.ShapeDtypeStruct((owned, width), jnp.float32),
             jax.ShapeDtypeStruct((devices, 1, lanes), jnp.float32),
         ),
-        scratch_shapes=[pltpu.VMEM((replicas, owned, width), jnp.float32)],
-        compiler_params=pltpu.CompilerParams(vmem_limit_bytes=vmem_bytes),
-        cost_estimate=pl.CostEstimate(
-            flops=2 * blocks * width * base, bytes_accessed=2 * blocks * width, transcendentals=0
-        ),
+        scratch_shapes=[pltpu.VMEM((max(far, 1), owned, width), jnp.float32)],
+        compiler_params=params,
+        cost_estimate=cost,
         name="reduce_blocks",
-    )(received, signs, matrix)
+    )(*[pieces[mask] for mask in range(near, replicas)], near_rotated, biggest, signs, matrix)
     squares = lax.all_to_all(squares, ("dp", "expert"), split_axis=0, concat_axis=0, tiled=True)
     limit = target_rms * math.sqrt(blocks * width * lax.axis_size("expert"))
     new_weights, update_grad = pl.pallas_call(

time: 68.9 us -> 67.4 us (0.978)
  blocking collectives: 33.2 us -> 14.9 us
  starting transfers between devices: 12.1 us -> 21.8 us
  waiting for transfers between devices: 18.4 us -> 24.5 us
  local copies, waits for them, and re-layouts: 1.21 us -> 2.61 us
    all_to_all x1, blocking collectives: 33.2 us -> 14.9 us  [on_device(): lax.all_to_all(squares, ('dp', 'expert'), split_axis=0, concat_axis=0, ti...]
    ppermute x7 -> x14, starting transfers between devices: 8.49 us -> 21.8 us  [swap(): return lax.ppermute(value, 'dp', [(i, i ^ mask) for i in range(size)])]
    ppermute x7 -> x14, waiting for transfers between devices: 11.3 us -> 24.5 us  [swap(): return lax.ppermute(value, 'dp', [(i, i ^ mask) for i in range(size)])]
    all_to_all x1 -> x0, waiting for transfers between devices: 7.03 us -> none  [on_device(): lax.all_to_all(squares, ('dp', 'expert'), split_axis=0, concat_axis=0, ti...]
    all_to_all x1 -> x0, starting transfers between devices: 3.63 us -> none  [on_device(): lax.all_to_all(squares, ('dp', 'expert'), split_axis=0, concat_axis=0, ti...]
    reshape x0 -> x1, local copies, waits for them, and re-layouts: none -> 1.4 us  [block_of(): return lax.dynamic_slice_in_dim(local, index, 1, 0).reshape(owned, width)]
    pallas_call x1 -> x2, Pallas kernels: 2.23 us -> 1.83 us  [the longest x1 1.23 us: on_device(): pl.pallas_call(functools.partial(reduce_kernel, far, base), out_shape=(ja...]
  transfers between devices with their start and end apart: 8 -> 14, of which waited for: 5 -> 6; matrix products, arithmetic and copies ran while one was open for 0% -> 0% of each run, Pallas kernels for 0% -> 1%
where the time goes in v2:
time: 67.4 us; the launch traced here: 67.2 us
  waiting for transfers between devices  24.5 us (36%)
  starting transfers between devices  21.8 us (32%)
  blocking collectives  14.9 us (22%)
  Pallas kernels  2.65 us (4%)
  local copies, waits for them, and re-layouts  2.61 us (4%)
  between operations  0.8 us (1%)
    ppermute x14, waiting for transfers between devices, swap(): return lax.ppermute(value, 'dp', [(i, i ^ mask) for i in range(size)])  24.5 us
    ppermute x14, starting transfers between devices, swap(): return lax.ppermute(value, 'dp', [(i, i ^ mask) for i in range(size)])  21.8 us
    all_to_all x1, blocking collectives, on_device(): lax.all_to_all(squares, ('dp', 'expert'), split_axis=0, concat_axis=0, ti...  14.9 us
    reshape x1, local copies, waits for them, and re-layouts, block_of(): return lax.dynamic_slice_in_dim(local, index, 1, 0).reshape(owned, width)  1.4 us
  transfers between devices with their start and end apart: 14, of which 6 were waited for; matrix products, arithmetic and copies ran while one was open for 0% of the time, Pallas kernels for 1%

profile of v2, /device:TPU:0, one launch (start us, length us, event | category | flops | bytes accessed | tf_op | source)
XLA Modules:
  0.0 67.2 jit_solution(9742046434496081580)
XLA Ops:
  0.7 1.4 %dynamic-slice_bitcast_fusion = (bf16[64,1024]{1,0:T(8,128)(2,1)S(1)}, bf16[64,1024]{1,0:T(8,128)(2,1)S(1)}, bf16[64,1024]{1,0:T(8,128)(2,1)S(1)}, bf16[64,1024]...) fusion(bf16[8,64,1024]{2,1,0:T(8,128)(2,1)} %bitcast.41, ...), kind=kLoop, calls=%fused_computation.8 | loop fusion | bytes 2097184 | tf_op jit(solution)/shard_map/reshape | solution.py:151
  2.1 3.0 %collective-permute-start.4 = (bf16[64,1024]{1,0:T(8,128)(2,1)S(1)}, bf16[64,1024]{1,0:T(8,128)(2,1)S(1)}, u32[]{:S(2)}, u32[]{:S(2)}) collective-permute-start(bf16[64,1024]{1,0:T(8,128)(2,1)S(1)} %get-tuple-element.16), channel_id=1, source_target_pairs={{0,4},{4,0},{8,12},{12,8},{16,20},{20,16},{24,28},{28,24},{1,5},{5... | collective-permute-start | bytes 393224 | tf_op jit(solution)/shard_map/ppermute | solution.py:117
  5.1 1.6 %collective-permute-start.5 = (bf16[64,1024]{1,0:T(8,128)(2,1)S(1)}, bf16[64,1024]{1,0:T(8,128)(2,1)S(1)}, u32[]{:S(2)}, u32[]{:S(2)}) collective-permute-start(bf16[64,1024]{1,0:T(8,128)(2,1)S(1)} %get-tuple-element.15), channel_id=1, source_target_pairs={{0,8},{4,12},{8,0},{12,4},{16,24},{20,28},{24,16},{28,20},{1,9},{5... | collective-permute-start | bytes 393224 | tf_op jit(solution)/shard_map/ppermute | solution.py:117
  6.7 3.0 %collective-permute-start = (bf16[64,1024]{1,0:T(8,128)(2,1)S(1)}, bf16[64,1024]{1,0:T(8,128)(2,1)S(1)}, u32[]{:S(2)}, u32[]{:S(2)}) collective-permute-start(bf16[64,1024]{1,0:T(8,128)(2,1)S(1)} %get-tuple-element.21), channel_id=1, source_target_pairs={{0,16},{4,20},{8,24},{12,28},{16,0},{20,4},{24,8},{28,12},{1,17},{... | collective-permute-start | bytes 393224 | tf_op jit(solution)/shard_map/ppermute | solution.py:117
  9.7 1.3 %collective-permute-start.1 = (bf16[64,1024]{1,0:T(8,128)(2,1)S(1)}, bf16[64,1024]{1,0:T(8,128)(2,1)S(1)}, u32[]{:S(2)}, u32[]{:S(2)}) collective-permute-start(bf16[64,1024]{1,0:T(8,128)(2,1)S(1)} %get-tuple-element.20), channel_id=1, source_target_pairs={{0,20},{4,16},{8,28},{12,24},{16,4},{20,0},{24,12},{28,8},{1,21},{... | collective-permute-start | bytes 393224 | tf_op jit(solution)/shard_map/ppermute | solution.py:117
  10.9 3.6 %collective-permute-start.2 = (bf16[64,1024]{1,0:T(8,128)(2,1)S(1)}, bf16[64,1024]{1,0:T(8,128)(2,1)S(1)}, u32[]{:S(2)}, u32[]{:S(2)}) collective-permute-start(bf16[64,1024]{1,0:T(8,128)(2,1)S(1)} %get-tuple-element.19), channel_id=1, source_target_pairs={{0,24},{4,28},{8,16},{12,20},{16,8},{20,12},{24,0},{28,4},{1,25},{... | collective-permute-start | bytes 393224 | tf_op jit(solution)/shard_map/ppermute | solution.py:117
  14.6 1.3 %collective-permute-done.5.refs_2_ = bf16[64,1024]{1,0:T(8,128)(2,1)S(1)} collective-permute-done((bf16[64,1024]{1,0:T(8,128)(2,1)S(1)}, bf16[64,1024]{1,0:T(8,128)(2,1)S(1)}, u32[]{:S(2)}, u32[]{:S(2)}) %collective-permute-start.5) | collective-permute-done | bytes 131104 | tf_op jit(solution)/shard_map/ppermute | solution.py:117
  15.8 0.7 %collective-permute-start.3 = (bf16[64,1024]{1,0:T(8,128)(2,1)S(1)}, bf16[64,1024]{1,0:T(8,128)(2,1)S(1)}, u32[]{:S(2)}, u32[]{:S(2)}) collective-permute-start(bf16[64,1024]{1,0:T(8,128)(2,1)S(1)} %get-tuple-element.18), channel_id=1, source_target_pairs={{0,28},{4,24},{8,20},{12,16},{16,12},{20,8},{24,4},{28,0},{1,29},{... | collective-permute-start | bytes 393224 | tf_op jit(solution)/shard_map/ppermute | solution.py:117
  16.6 0.6 rotate_near.1
  17.2 11.9 %collective-permute-done.1.refs_1_ = bf16[64,1024]{1,0:T(8,128)(2,1)S(1)} collective-permute-done((bf16[64,1024]{1,0:T(8,128)(2,1)S(1)}, bf16[64,1024]{1,0:T(8,128)(2,1)S(1)}, u32[]{:S(2)}, u32[]{:S(2)}) %collective-permute-start.1) | collective-permute-done | bytes 131104 | tf_op jit(solution)/shard_map/ppermute | solution.py:117
  29.1 1.2 %reduce_blocks.1 = (f32[64,1024]{1,0:T(8,128)S(1)}, f32[32,1,128]{2,1,0:T(1,128)S(1)}) custom-call(bf16[64,1024]{1,0:T(8,128)(2,1)S(1)} %collective-permute-done.refs_0_, bf16[64,1024]{1,0:T(8,128)(2,1)S(1)} %collective-permute-done.1.refs_1_, bf16[64,1024]{1,0:T(8,128)(2,1)S(1)} %collective-permute-done.2.refs_2_, ...), custom_call_target="tpu_custom_call" | custom-call | flops 134217728 | bytes 1572864 | tf_op jit(solution)/shard_map/reduce_blocks/pallas_call | solution.py:173
  30.3 14.9 %all_to_all.5 = f32[32,1,128]{2,1,0:T(1,128)S(1)} all-to-all(f32[32,1,128]{2,1,0:T(1,128)S(1)} %get-tuple-element.10), channel_id=1, replica_groups=mesh['dp'=8,'expert'=4] {'dp','expert'}, dimensions={0} | all-to-all | bytes 32768 | tf_op jit(solution)/shard_map/all_to_all | solution.py:184
  45.2 0.8 %update_blocks.1 = (bf16[64,1024]{1,0:T(8,128)(2,1)S(1)}, f32[64,1024]{1,0:T(8,128)}) custom-call(f32[32,128]{1,0:T(8,128)S(1)} %bitcast.40, f32[64,1024]{1,0:T(8,128)S(1)} %get-tuple-element.11.unrot_ref, bf16[64,1024]{1,0:T(8,128)(2,1)S(1)} %bitcast.38, bf16[64,1024]{1,0:T(8,128)(2,1)S(1)} %bitcast.39), custom_call_target="tpu_custom_call" | custom-call | tf_op jit(solution)/shard_map/update_blocks/pallas_call | solution.py:186
  46.0 0.6 collective-permute-start.7
  46.6 0.6 collective-permute-start.8
  47.7 3.3 %collective-permute-start.10 = (bf16[64,1024]{1,0:T(8,128)(2,1)S(1)}, bf16[64,1024]{1,0:T(8,128)(2,1)S(1)}, u32[]{:S(2)}, u32[]{:S(2)}) collective-permute-start(bf16[64,1024]{1,0:T(8,128)(2,1)S(1)} %get-tuple-element.12), channel_id=1, source_target_pairs={{0,24},{4,28},{8,16},{12,20},{16,8},{20,12},{24,0},{28,4},{1,25},{... | collective-permute-start | bytes 393224 | tf_op jit(solution)/shard_map/ppermute | solution.py:117
  51.1 2.0 %collective-permute-done.8 = bf16[64,1024]{1,0:T(8,128)(2,1)S(1)} collective-permute-done((bf16[64,1024]{1,0:T(8,128)(2,1)S(1)}, bf16[64,1024]{1,0:T(8,128)(2,1)S(1)}, u32[]{:S(2)}, u32[]{:S(2)}) %collective-permute-start.8) | collective-permute-done | bytes 131104 | tf_op jit(solution)/shard_map/ppermute | solution.py:117
  53.1 1.5 %collective-permute-start.11 = (bf16[64,1024]{1,0:T(8,128)(2,1)S(1)}, bf16[64,1024]{1,0:T(8,128)(2,1)S(1)}, u32[]{:S(2)}, u32[]{:S(2)}) collective-permute-start(bf16[64,1024]{1,0:T(8,128)(2,1)S(1)} %collective-permute-done.8), channel_id=1, source_target_pairs={{0,4},{4,0},{8,12},{12,8},{16,20},{20,16},{24,28},{28,24},{1,5},{5... | collective-permute-start | bytes 393224 | tf_op jit(solution)/shard_map/ppermute | solution.py:117
  54.7 5.0 %collective-permute-done.9 = bf16[64,1024]{1,0:T(8,128)(2,1)S(1)} collective-permute-done((bf16[64,1024]{1,0:T(8,128)(2,1)S(1)}, bf16[64,1024]{1,0:T(8,128)(2,1)S(1)}, u32[]{:S(2)}, u32[]{:S(2)}) %collective-permute-start.9) | collective-permute-done | bytes 131104 | tf_op jit(solution)/shard_map/ppermute | solution.py:117
  59.7 1.5 %collective-permute-start.12 = (bf16[64,1024]{1,0:T(8,128)(2,1)S(1)}, bf16[64,1024]{1,0:T(8,128)(2,1)S(1)}, u32[]{:S(2)}, u32[]{:S(2)}) collective-permute-start(bf16[64,1024]{1,0:T(8,128)(2,1)S(1)} %collective-permute-done.9), channel_id=1, source_target_pairs={{0,4},{4,0},{8,12},{12,8},{16,20},{20,16},{24,28},{28,24},{1,5},{5... | collective-permute-start | bytes 393224 | tf_op jit(solution)/shard_map/ppermute | solution.py:117
  61.2 0.6 collective-permute-start.13
  61.9 2.8 %collective-permute-done.12 = bf16[64,1024]{1,0:T(8,128)(2,1)S(1)} collective-permute-done((bf16[64,1024]{1,0:T(8,128)(2,1)S(1)}, bf16[64,1024]{1,0:T(8,128)(2,1)S(1)}, u32[]{:S(2)}, u32[]{:S(2)}) %collective-permute-start.12) | collective-permute-done | bytes 131104 | tf_op jit(solution)/shard_map/ppermute | solution.py:117
  64.7 1.6 %collective-permute-done.13 = bf16[64,1024]{1,0:T(8,128)(2,1)S(1)} collective-permute-done((bf16[64,1024]{1,0:T(8,128)(2,1)S(1)}, bf16[64,1024]{1,0:T(8,128)(2,1)S(1)}, u32[]{:S(2)}, u32[]{:S(2)}) %collective-permute-start.13) | collective-permute-done | bytes 131104 | tf_op jit(solution)/shard_map/ppermute | solution.py:117
  66.3 1.0 %copy-done.4 = bf16[8,64,1024]{2,1,0:T(8,128)(2,1)} copy-done((bf16[8,64,1024]{2,1,0:T(8,128)(2,1)}, bf16[8,64,1024]{2,1,0:T(8,128)(2,1)S(1)}, u32[]{:S(2)}) %copy-start.4) | copy-done | bytes 1048600
  (28 shorter events, 0.8 us)
Async XLA Ops:
  0.7 15.9 %copy-start = (bf16[256,256]{1,0:T(8,128)(2,1)S(1)}, bf16[256,256]{1,0:T(8,128)(2,1)}, u32[]{:S(2)}) copy-start(bf16[256,256]{1,0:T(8,128)(2,1)} %constant.28.clone.refs_5_.refs_7_) | copy-start | bytes 393220
  2.1 8.9 %collective-permute-start.4 = (bf16[64,1024]{1,0:T(8,128)(2,1)S(1)}, bf16[64,1024]{1,0:T(8,128)(2,1)S(1)}, u32[]{:S(2)}, u32[]{:S(2)}) collective-permute-start(bf16[64,1024]{1,0:T(8,128)(2,1)S(1)} %get-tuple-element.16), channel_id=1, source_target_pairs={{0,4},{4,0},{8,12},{12,8},{16,20},{20,16},{24,28},{28,24},{1,5},{5... | collective-permute-start | bytes 393224 | tf_op jit(solution)/shard_map/ppermute | solution.py:117
  5.1 10.7 %collective-permute-start.5 = (bf16[64,1024]{1,0:T(8,128)(2,1)S(1)}, bf16[64,1024]{1,0:T(8,128)(2,1)S(1)}, u32[]{:S(2)}, u32[]{:S(2)}) collective-permute-start(bf16[64,1024]{1,0:T(8,128)(2,1)S(1)} %get-tuple-element.15), channel_id=1, source_target_pairs={{0,8},{4,12},{8,0},{12,4},{16,24},{20,28},{24,16},{28,20},{1,9},{5... | collective-permute-start | bytes 393224 | tf_op jit(solution)/shard_map/ppermute | solution.py:117
  6.7 9.9 %collective-permute-start.6 = (bf16[64,1024]{1,0:T(8,128)(2,1)S(1)}, bf16[64,1024]{1,0:T(8,128)(2,1)S(1)}, u32[]{:S(2)}, u32[]{:S(2)}) collective-permute-start(bf16[64,1024]{1,0:T(8,128)(2,1)S(1)} %get-tuple-element.14), channel_id=1, source_target_pairs={{0,12},{4,8},{8,4},{12,0},{16,28},{20,24},{24,20},{28,16},{1,13},{... | collective-permute-start | bytes 393224 | tf_op jit(solution)/shard_map/ppermute | solution.py:117
  6.7 9.9 %copy-start.3 = (s32[1,1024]{1,0:T(1,128)S(1)}, s32[1,1024]{1,0:T(1,128)}, u32[]{:S(2)}) copy-start(s32[1,1024]{1,0:T(1,128)} %refs_6_.1) | copy-start | bytes 12292
  6.7 10.5 %collective-permute-start = (bf16[64,1024]{1,0:T(8,128)(2,1)S(1)}, bf16[64,1024]{1,0:T(8,128)(2,1)S(1)}, u32[]{:S(2)}, u32[]{:S(2)}) collective-permute-start(bf16[64,1024]{1,0:T(8,128)(2,1)S(1)} %get-tuple-element.21), channel_id=1, source_target_pairs={{0,16},{4,20},{8,24},{12,28},{16,0},{20,4},{24,8},{28,12},{1,17},{... | collective-permute-start | bytes 393224 | tf_op jit(solution)/shard_map/ppermute | solution.py:117
  9.7 19.4 %collective-permute-start.1 = (bf16[64,1024]{1,0:T(8,128)(2,1)S(1)}, bf16[64,1024]{1,0:T(8,128)(2,1)S(1)}, u32[]{:S(2)}, u32[]{:S(2)}) collective-permute-start(bf16[64,1024]{1,0:T(8,128)(2,1)S(1)} %get-tuple-element.20), channel_id=1, source_target_pairs={{0,20},{4,16},{8,28},{12,24},{16,4},{20,0},{24,12},{28,8},{1,21},{... | collective-permute-start | bytes 393224 | tf_op jit(solution)/shard_map/ppermute | solution.py:117
  10.9 18.1 %collective-permute-start.2 = (bf16[64,1024]{1,0:T(8,128)(2,1)S(1)}, bf16[64,1024]{1,0:T(8,128)(2,1)S(1)}, u32[]{:S(2)}, u32[]{:S(2)}) collective-permute-start(bf16[64,1024]{1,0:T(8,128)(2,1)S(1)} %get-tuple-element.19), channel_id=1, source_target_pairs={{0,24},{4,28},{8,16},{12,20},{16,8},{20,12},{24,0},{28,4},{1,25},{... | collective-permute-start | bytes 393224 | tf_op jit(solution)/shard_map/ppermute | solution.py:117
  15.8 13.3 %collective-permute-start.3 = (bf16[64,1024]{1,0:T(8,128)(2,1)S(1)}, bf16[64,1024]{1,0:T(8,128)(2,1)S(1)}, u32[]{:S(2)}, u32[]{:S(2)}) collective-permute-start(bf16[64,1024]{1,0:T(8,128)(2,1)S(1)} %get-tuple-element.18), channel_id=1, source_target_pairs={{0,28},{4,24},{8,20},{12,16},{16,12},{20,8},{24,4},{28,0},{1,29},{... | collective-permute-start | bytes 393224 | tf_op jit(solution)/shard_map/ppermute | solution.py:117
  29.1 16.1 %copy-start.1 = (bf16[1,64,1024]{2,1,0:T(8,128)(2,1)S(1)}, bf16[1,64,1024]{2,1,0:T(8,128)(2,1)}, u32[]{:S(2)}) copy-start(bf16[1,64,1024]{2,1,0:T(8,128)(2,1)} %param.7) | copy-start | bytes 393220
  29.1 16.1 %copy-start.2 = (bf16[1,64,1024]{2,1,0:T(8,128)(2,1)S(1)}, bf16[1,64,1024]{2,1,0:T(8,128)(2,1)}, u32[]{:S(2)}) copy-start(bf16[1,64,1024]{2,1,0:T(8,128)(2,1)} %param.8) | copy-start | bytes 393220
  46.0 8.6 %collective-permute-start.7 = (bf16[64,1024]{1,0:T(8,128)(2,1)S(1)}, bf16[64,1024]{1,0:T(8,128)(2,1)S(1)}, u32[]{:S(2)}, u32[]{:S(2)}) collective-permute-start(bf16[64,1024]{1,0:T(8,128)(2,1)S(1)} %get-tuple-element.12), channel_id=1, source_target_pairs={{0,4},{4,0},{8,12},{12,8},{16,20},{20,16},{24,28},{28,24},{1,5},{5... | collective-permute-start | bytes 393224 | tf_op jit(solution)/shard_map/ppermute | solution.py:117
  46.6 6.5 %collective-permute-start.8 = (bf16[64,1024]{1,0:T(8,128)(2,1)S(1)}, bf16[64,1024]{1,0:T(8,128)(2,1)S(1)}, u32[]{:S(2)}, u32[]{:S(2)}) collective-permute-start(bf16[64,1024]{1,0:T(8,128)(2,1)S(1)} %get-tuple-element.12), channel_id=1, source_target_pairs={{0,8},{4,12},{8,0},{12,4},{16,24},{20,28},{24,16},{28,20},{1,9},{5... | collective-permute-start | bytes 393224 | tf_op jit(solution)/shard_map/ppermute | solution.py:117
  47.2 12.5 %collective-permute-start.9 = (bf16[64,1024]{1,0:T(8,128)(2,1)S(1)}, bf16[64,1024]{1,0:T(8,128)(2,1)S(1)}, u32[]{:S(2)}, u32[]{:S(2)}) collective-permute-start(bf16[64,1024]{1,0:T(8,128)(2,1)S(1)} %get-tuple-element.12), channel_id=1, source_target_pairs={{0,16},{4,20},{8,24},{12,28},{16,0},{20,4},{24,8},{28,12},{1,17},{... | collective-permute-start | bytes 393224 | tf_op jit(solution)/shard_map/ppermute | solution.py:117
  47.7 13.5 %collective-permute-start.10 = (bf16[64,1024]{1,0:T(8,128)(2,1)S(1)}, bf16[64,1024]{1,0:T(8,128)(2,1)S(1)}, u32[]{:S(2)}, u32[]{:S(2)}) collective-permute-start(bf16[64,1024]{1,0:T(8,128)(2,1)S(1)} %get-tuple-element.12), channel_id=1, source_target_pairs={{0,24},{4,28},{8,16},{12,20},{16,8},{20,12},{24,0},{28,4},{1,25},{... | collective-permute-start | bytes 393224 | tf_op jit(solution)/shard_map/ppermute | solution.py:117
  53.1 8.7 %collective-permute-start.11 = (bf16[64,1024]{1,0:T(8,128)(2,1)S(1)}, bf16[64,1024]{1,0:T(8,128)(2,1)S(1)}, u32[]{:S(2)}, u32[]{:S(2)}) collective-permute-start(bf16[64,1024]{1,0:T(8,128)(2,1)S(1)} %collective-permute-done.8), channel_id=1, source_target_pairs={{0,4},{4,0},{8,12},{12,8},{16,20},{20,16},{24,28},{28,24},{1,5},{5... | collective-permute-start | bytes 393224 | tf_op jit(solution)/shard_map/ppermute | solution.py:117
  59.7 5.0 %collective-permute-start.12 = (bf16[64,1024]{1,0:T(8,128)(2,1)S(1)}, bf16[64,1024]{1,0:T(8,128)(2,1)S(1)}, u32[]{:S(2)}, u32[]{:S(2)}) collective-permute-start(bf16[64,1024]{1,0:T(8,128)(2,1)S(1)} %collective-permute-done.9), channel_id=1, source_target_pairs={{0,4},{4,0},{8,12},{12,8},{16,20},{20,16},{24,28},{28,24},{1,5},{5... | collective-permute-start | bytes 393224 | tf_op jit(solution)/shard_map/ppermute | solution.py:117
  61.2 5.0 %collective-permute-start.13 = (bf16[64,1024]{1,0:T(8,128)(2,1)S(1)}, bf16[64,1024]{1,0:T(8,128)(2,1)S(1)}, u32[]{:S(2)}, u32[]{:S(2)}) collective-permute-start(bf16[64,1024]{1,0:T(8,128)(2,1)S(1)} %collective-permute-done.10), channel_id=1, source_target_pairs={{0,4},{4,0},{8,12},{12,8},{16,20},{20,16},{24,28},{28,24},{1,5},{5... | collective-permute-start | bytes 393224 | tf_op jit(solution)/shard_map/ppermute | solution.py:117
  66.3 1.0 %copy-start.4 = (bf16[8,64,1024]{2,1,0:T(8,128)(2,1)}, bf16[8,64,1024]{2,1,0:T(8,128)(2,1)S(1)}, u32[]{:S(2)}) copy-start(bf16[8,64,1024]{2,1,0:T(8,128)(2,1)S(1)} %bitcast_dynamic-update-slice_fusion) | copy-start | bytes 3145732

commit v3 on v2

--- a/solution.py
+++ b/solution.py
@@ -119,17 +119,22 @@
 
 def gather_blocks(block, replicas):
     x_count = 1 << ((replicas.bit_length() - 1) // 2)
-    z_count = replicas // x_count
+    near = max(replicas // 2, 1)
     me = lax.axis_index("dp")
-
     pieces = {0: block}
-    for x in range(1, x_count):
-        pieces[x] = swap(block, x)
-    for z in range(1, z_count):
-        pieces[z * x_count] = swap(block, z * x_count)
-    for z in range(1, z_count):
-        for x in range(1, x_count):
-            pieces[z * x_count + x] = swap(pieces[z * x_count], x)
+
+    def spread(start):
+        for z in range(x_count, near, x_count):
+            pieces[start + z] = swap(pieces[start], z)
+        for z in range(0, near, x_count):
+            for x in range(1, min(x_count, near)):
+                pieces[start + z + x] = swap(pieces[start + z], x)
+
+    if replicas > 1:
+        pieces[near] = swap(block, near)
+    spread(0)
+    if replicas > 1:
+        spread(near)
     owned, width = block.shape
     out = jnp.zeros((replicas, owned, width), block.dtype)
     for mask, piece in pieces.items():

time: 67.4 us -> 67.1 us (level)
  starting transfers between devices: 21.8 us -> 17.6 us
  waiting for transfers between devices: 24.5 us -> 28.4 us
    ppermute x14, starting transfers between devices: 21.8 us -> 17.6 us  [swap(): return lax.ppermute(value, 'dp', [(i, i ^ mask) for i in range(size)])]
    ppermute x14, waiting for transfers between devices: 24.5 us -> 28.4 us  [swap(): return lax.ppermute(value, 'dp', [(i, i ^ mask) for i in range(size)])]
where the time goes in v3:
time: 67.1 us; the launch traced here: 66.9 us
  waiting for transfers between devices  28.4 us (42%)
  starting transfers between devices  17.6 us (26%)
  blocking collectives  14.9 us (22%)
  Pallas kernels  2.65 us (4%)
  local copies, waits for them, and re-layouts  2.61 us (4%)
  between operations  0.82 us (1%)
    ppermute x14, waiting for transfers between devices, swap(): return lax.ppermute(value, 'dp', [(i, i ^ mask) for i in range(size)])  28.4 us
    ppermute x14, starting transfers between devices, swap(): return lax.ppermute(value, 'dp', [(i, i ^ mask) for i in range(size)])  17.6 us
    all_to_all x1, blocking collectives, on_device(): lax.all_to_all(squares, ('dp', 'expert'), split_axis=0, concat_axis=0, ti...  14.9 us
    reshape x1, local copies, waits for them, and re-layouts, block_of(): return lax.dynamic_slice_in_dim(local, index, 1, 0).reshape(owned, width)  1.4 us
  transfers between devices with their start and end apart: 14, of which 6 were waited for; matrix products, arithmetic and copies ran while one was open for 0% of the time, Pallas kernels for 1%

profile of v3, /device:TPU:0, one launch (start us, length us, event | category | flops | bytes accessed | tf_op | source)
XLA Modules:
  0.0 66.9 jit_solution(16515122198699906685)
XLA Ops:
  0.7 1.4 %dynamic-slice_bitcast_fusion = (bf16[64,1024]{1,0:T(8,128)(2,1)S(1)}, bf16[64,1024]{1,0:T(8,128)(2,1)S(1)}, bf16[64,1024]{1,0:T(8,128)(2,1)S(1)}, bf16[64,1024]...) fusion(bf16[8,64,1024]{2,1,0:T(8,128)(2,1)} %bitcast.41, ...), kind=kLoop, calls=%fused_computation.8 | loop fusion | bytes 2097184 | tf_op jit(solution)/shard_map/reshape | solution.py:156
  2.1 3.0 %collective-permute-start.4 = (bf16[64,1024]{1,0:T(8,128)(2,1)S(1)}, bf16[64,1024]{1,0:T(8,128)(2,1)S(1)}, u32[]{:S(2)}, u32[]{:S(2)}) collective-permute-start(bf16[64,1024]{1,0:T(8,128)(2,1)S(1)} %get-tuple-element.16), channel_id=1, source_target_pairs={{0,4},{4,0},{8,12},{12,8},{16,20},{20,16},{24,28},{28,24},{1,5},{5... | collective-permute-start | bytes 393224 | tf_op jit(solution)/shard_map/ppermute | solution.py:117
  5.1 1.6 %collective-permute-start.5 = (bf16[64,1024]{1,0:T(8,128)(2,1)S(1)}, bf16[64,1024]{1,0:T(8,128)(2,1)S(1)}, u32[]{:S(2)}, u32[]{:S(2)}) collective-permute-start(bf16[64,1024]{1,0:T(8,128)(2,1)S(1)} %get-tuple-element.15), channel_id=1, source_target_pairs={{0,8},{4,12},{8,0},{12,4},{16,24},{20,28},{24,16},{28,20},{1,9},{5... | collective-permute-start | bytes 393224 | tf_op jit(solution)/shard_map/ppermute | solution.py:117
  6.7 3.0 %collective-permute-start = (bf16[64,1024]{1,0:T(8,128)(2,1)S(1)}, bf16[64,1024]{1,0:T(8,128)(2,1)S(1)}, u32[]{:S(2)}, u32[]{:S(2)}) collective-permute-start(bf16[64,1024]{1,0:T(8,128)(2,1)S(1)} %get-tuple-element.21), channel_id=1, source_target_pairs={{0,16},{4,20},{8,24},{12,28},{16,0},{20,4},{24,8},{28,12},{1,17},{... | collective-permute-start | bytes 393224 | tf_op jit(solution)/shard_map/ppermute | solution.py:117
  9.7 1.3 %collective-permute-start.1 = (bf16[64,1024]{1,0:T(8,128)(2,1)S(1)}, bf16[64,1024]{1,0:T(8,128)(2,1)S(1)}, u32[]{:S(2)}, u32[]{:S(2)}) collective-permute-start(bf16[64,1024]{1,0:T(8,128)(2,1)S(1)} %get-tuple-element.20), channel_id=1, source_target_pairs={{0,20},{4,16},{8,28},{12,24},{16,4},{20,0},{24,12},{28,8},{1,21},{... | collective-permute-start | bytes 393224 | tf_op jit(solution)/shard_map/ppermute | solution.py:117
  10.9 3.6 %collective-permute-start.2 = (bf16[64,1024]{1,0:T(8,128)(2,1)S(1)}, bf16[64,1024]{1,0:T(8,128)(2,1)S(1)}, u32[]{:S(2)}, u32[]{:S(2)}) collective-permute-start(bf16[64,1024]{1,0:T(8,128)(2,1)S(1)} %get-tuple-element.19), channel_id=1, source_target_pairs={{0,24},{4,28},{8,16},{12,20},{16,8},{20,12},{24,0},{28,4},{1,25},{... | collective-permute-start | bytes 393224 | tf_op jit(solution)/shard_map/ppermute | solution.py:117
  14.6 1.3 %collective-permute-done.5.refs_2_ = bf16[64,1024]{1,0:T(8,128)(2,1)S(1)} collective-permute-done((bf16[64,1024]{1,0:T(8,128)(2,1)S(1)}, bf16[64,1024]{1,0:T(8,128)(2,1)S(1)}, u32[]{:S(2)}, u32[]{:S(2)}) %collective-permute-start.5) | collective-permute-done | bytes 131104 | tf_op jit(solution)/shard_map/ppermute | solution.py:117
  15.8 0.7 %collective-permute-start.3 = (bf16[64,1024]{1,0:T(8,128)(2,1)S(1)}, bf16[64,1024]{1,0:T(8,128)(2,1)S(1)}, u32[]{:S(2)}, u32[]{:S(2)}) collective-permute-start(bf16[64,1024]{1,0:T(8,128)(2,1)S(1)} %get-tuple-element.18), channel_id=1, source_target_pairs={{0,28},{4,24},{8,20},{12,16},{16,12},{20,8},{24,4},{28,0},{1,29},{... | collective-permute-start | bytes 393224 | tf_op jit(solution)/shard_map/ppermute | solution.py:117
  16.6 0.6 rotate_near.1
  17.2 11.9 %collective-permute-done.1.refs_1_ = bf16[64,1024]{1,0:T(8,128)(2,1)S(1)} collective-permute-done((bf16[64,1024]{1,0:T(8,128)(2,1)S(1)}, bf16[64,1024]{1,0:T(8,128)(2,1)S(1)}, u32[]{:S(2)}, u32[]{:S(2)}) %collective-permute-start.1) | collective-permute-done | bytes 131104 | tf_op jit(solution)/shard_map/ppermute | solution.py:117
  29.1 1.2 %reduce_blocks.1 = (f32[64,1024]{1,0:T(8,128)S(1)}, f32[32,1,128]{2,1,0:T(1,128)S(1)}) custom-call(bf16[64,1024]{1,0:T(8,128)(2,1)S(1)} %collective-permute-done.refs_0_, bf16[64,1024]{1,0:T(8,128)(2,1)S(1)} %collective-permute-done.1.refs_1_, bf16[64,1024]{1,0:T(8,128)(2,1)S(1)} %collective-permute-done.2.refs_2_, ...), custom_call_target="tpu_custom_call" | custom-call | flops 134217728 | bytes 1572864 | tf_op jit(solution)/shard_map/reduce_blocks/pallas_call | solution.py:178
  30.3 14.9 %all_to_all.5 = f32[32,1,128]{2,1,0:T(1,128)S(1)} all-to-all(f32[32,1,128]{2,1,0:T(1,128)S(1)} %get-tuple-element.10), channel_id=1, replica_groups=mesh['dp'=8,'expert'=4] {'dp','expert'}, dimensions={0} | all-to-all | bytes 32768 | tf_op jit(solution)/shard_map/all_to_all | solution.py:189
  45.2 0.8 %update_blocks.1 = (bf16[64,1024]{1,0:T(8,128)(2,1)S(1)}, f32[64,1024]{1,0:T(8,128)}) custom-call(f32[32,128]{1,0:T(8,128)S(1)} %bitcast.40, f32[64,1024]{1,0:T(8,128)S(1)} %get-tuple-element.11.unrot_ref, bf16[64,1024]{1,0:T(8,128)(2,1)S(1)} %bitcast.38, bf16[64,1024]{1,0:T(8,128)(2,1)S(1)} %bitcast.39), custom_call_target="tpu_custom_call" | custom-call | tf_op jit(solution)/shard_map/update_blocks/pallas_call | solution.py:191
  46.0 0.6 collective-permute-start.7
  46.6 0.5 collective-permute-start.8
  47.2 0.5 collective-permute-start.9
  47.9 7.0 %collective-permute-done.7 = bf16[64,1024]{1,0:T(8,128)(2,1)S(1)} collective-permute-done((bf16[64,1024]{1,0:T(8,128)(2,1)S(1)}, bf16[64,1024]{1,0:T(8,128)(2,1)S(1)}, u32[]{:S(2)}, u32[]{:S(2)}) %collective-permute-start.7) | collective-permute-done | bytes 131104 | tf_op jit(solution)/shard_map/ppermute | solution.py:117
  54.9 0.6 collective-permute-start.12
  55.6 1.5 %collective-permute-start.10 = (bf16[64,1024]{1,0:T(8,128)(2,1)S(1)}, bf16[64,1024]{1,0:T(8,128)(2,1)S(1)}, u32[]{:S(2)}, u32[]{:S(2)}) collective-permute-start(bf16[64,1024]{1,0:T(8,128)(2,1)S(1)} %collective-permute-done.8), channel_id=1, source_target_pairs={{0,4},{4,0},{8,12},{12,8},{16,20},{20,16},{24,28},{28,24},{1,5},{5... | collective-permute-start | bytes 393224 | tf_op jit(solution)/shard_map/ppermute | solution.py:117
  57.1 3.2 %collective-permute-done.11 = bf16[64,1024]{1,0:T(8,128)(2,1)S(1)} collective-permute-done((bf16[64,1024]{1,0:T(8,128)(2,1)S(1)}, bf16[64,1024]{1,0:T(8,128)(2,1)S(1)}, u32[]{:S(2)}, u32[]{:S(2)}) %collective-permute-start.11) | collective-permute-done | bytes 131104 | tf_op jit(solution)/shard_map/ppermute | solution.py:117
  60.3 0.6 collective-permute-start.13
  60.9 3.1 %collective-permute-done.10 = bf16[64,1024]{1,0:T(8,128)(2,1)S(1)} collective-permute-done((bf16[64,1024]{1,0:T(8,128)(2,1)S(1)}, bf16[64,1024]{1,0:T(8,128)(2,1)S(1)}, u32[]{:S(2)}, u32[]{:S(2)}) %collective-permute-start.10) | collective-permute-done | bytes 131104 | tf_op jit(solution)/shard_map/ppermute | solution.py:117
  64.2 1.8 %collective-permute-done.13 = bf16[64,1024]{1,0:T(8,128)(2,1)S(1)} collective-permute-done((bf16[64,1024]{1,0:T(8,128)(2,1)S(1)}, bf16[64,1024]{1,0:T(8,128)(2,1)S(1)}, u32[]{:S(2)}, u32[]{:S(2)}) %collective-permute-start.13) | collective-permute-done | bytes 131104 | tf_op jit(solution)/shard_map/ppermute | solution.py:117
  66.0 1.0 %copy-done.4 = bf16[8,64,1024]{2,1,0:T(8,128)(2,1)} copy-done((bf16[8,64,1024]{2,1,0:T(8,128)(2,1)}, bf16[8,64,1024]{2,1,0:T(8,128)(2,1)S(1)}, u32[]{:S(2)}) %copy-start.4) | copy-done | bytes 1048600
  (28 shorter events, 0.3 us)
Async XLA Ops:
  0.7 15.9 %copy-start = (bf16[256,256]{1,0:T(8,128)(2,1)S(1)}, bf16[256,256]{1,0:T(8,128)(2,1)}, u32[]{:S(2)}) copy-start(bf16[256,256]{1,0:T(8,128)(2,1)} %constant.28.clone.refs_5_.refs_7_) | copy-start | bytes 393220
  2.1 8.9 %collective-permute-start.4 = (bf16[64,1024]{1,0:T(8,128)(2,1)S(1)}, bf16[64,1024]{1,0:T(8,128)(2,1)S(1)}, u32[]{:S(2)}, u32[]{:S(2)}) collective-permute-start(bf16[64,1024]{1,0:T(8,128)(2,1)S(1)} %get-tuple-element.16), channel_id=1, source_target_pairs={{0,4},{4,0},{8,12},{12,8},{16,20},{20,16},{24,28},{28,24},{1,5},{5... | collective-permute-start | bytes 393224 | tf_op jit(solution)/shard_map/ppermute | solution.py:117
  5.1 10.7 %collective-permute-start.5 = (bf16[64,1024]{1,0:T(8,128)(2,1)S(1)}, bf16[64,1024]{1,0:T(8,128)(2,1)S(1)}, u32[]{:S(2)}, u32[]{:S(2)}) collective-permute-start(bf16[64,1024]{1,0:T(8,128)(2,1)S(1)} %get-tuple-element.15), channel_id=1, source_target_pairs={{0,8},{4,12},{8,0},{12,4},{16,24},{20,28},{24,16},{28,20},{1,9},{5... | collective-permute-start | bytes 393224 | tf_op jit(solution)/shard_map/ppermute | solution.py:117
  6.7 9.9 %collective-permute-start.6 = (bf16[64,1024]{1,0:T(8,128)(2,1)S(1)}, bf16[64,1024]{1,0:T(8,128)(2,1)S(1)}, u32[]{:S(2)}, u32[]{:S(2)}) collective-permute-start(bf16[64,1024]{1,0:T(8,128)(2,1)S(1)} %get-tuple-element.14), channel_id=1, source_target_pairs={{0,12},{4,8},{8,4},{12,0},{16,28},{20,24},{24,20},{28,16},{1,13},{... | collective-permute-start | bytes 393224 | tf_op jit(solution)/shard_map/ppermute | solution.py:117
  6.7 9.9 %copy-start.3 = (s32[1,1024]{1,0:T(1,128)S(1)}, s32[1,1024]{1,0:T(1,128)}, u32[]{:S(2)}) copy-start(s32[1,1024]{1,0:T(1,128)} %refs_6_.1) | copy-start | bytes 12292
  6.7 10.5 %collective-permute-start = (bf16[64,1024]{1,0:T(8,128)(2,1)S(1)}, bf16[64,1024]{1,0:T(8,128)(2,1)S(1)}, u32[]{:S(2)}, u32[]{:S(2)}) collective-permute-start(bf16[64,1024]{1,0:T(8,128)(2,1)S(1)} %get-tuple-element.21), channel_id=1, source_target_pairs={{0,16},{4,20},{8,24},{12,28},{16,0},{20,4},{24,8},{28,12},{1,17},{... | collective-permute-start | bytes 393224 | tf_op jit(solution)/shard_map/ppermute | solution.py:117
  9.7 19.4 %collective-permute-start.1 = (bf16[64,1024]{1,0:T(8,128)(2,1)S(1)}, bf16[64,1024]{1,0:T(8,128)(2,1)S(1)}, u32[]{:S(2)}, u32[]{:S(2)}) collective-permute-start(bf16[64,1024]{1,0:T(8,128)(2,1)S(1)} %get-tuple-element.20), channel_id=1, source_target_pairs={{0,20},{4,16},{8,28},{12,24},{16,4},{20,0},{24,12},{28,8},{1,21},{... | collective-permute-start | bytes 393224 | tf_op jit(solution)/shard_map/ppermute | solution.py:117
  10.9 18.1 %collective-permute-start.2 = (bf16[64,1024]{1,0:T(8,128)(2,1)S(1)}, bf16[64,1024]{1,0:T(8,128)(2,1)S(1)}, u32[]{:S(2)}, u32[]{:S(2)}) collective-permute-start(bf16[64,1024]{1,0:T(8,128)(2,1)S(1)} %get-tuple-element.19), channel_id=1, source_target_pairs={{0,24},{4,28},{8,16},{12,20},{16,8},{20,12},{24,0},{28,4},{1,25},{... | collective-permute-start | bytes 393224 | tf_op jit(solution)/shard_map/ppermute | solution.py:117
  15.8 13.3 %collective-permute-start.3 = (bf16[64,1024]{1,0:T(8,128)(2,1)S(1)}, bf16[64,1024]{1,0:T(8,128)(2,1)S(1)}, u32[]{:S(2)}, u32[]{:S(2)}) collective-permute-start(bf16[64,1024]{1,0:T(8,128)(2,1)S(1)} %get-tuple-element.18), channel_id=1, source_target_pairs={{0,28},{4,24},{8,20},{12,16},{16,12},{20,8},{24,4},{28,0},{1,29},{... | collective-permute-start | bytes 393224 | tf_op jit(solution)/shard_map/ppermute | solution.py:117
  29.1 16.1 %copy-start.1 = (bf16[1,64,1024]{2,1,0:T(8,128)(2,1)S(1)}, bf16[1,64,1024]{2,1,0:T(8,128)(2,1)}, u32[]{:S(2)}) copy-start(bf16[1,64,1024]{2,1,0:T(8,128)(2,1)} %param.7) | copy-start | bytes 393220
  29.1 16.1 %copy-start.2 = (bf16[1,64,1024]{2,1,0:T(8,128)(2,1)S(1)}, bf16[1,64,1024]{2,1,0:T(8,128)(2,1)}, u32[]{:S(2)}) copy-start(bf16[1,64,1024]{2,1,0:T(8,128)(2,1)} %param.8) | copy-start | bytes 393220
  46.0 8.9 %collective-permute-start.7 = (bf16[64,1024]{1,0:T(8,128)(2,1)S(1)}, bf16[64,1024]{1,0:T(8,128)(2,1)S(1)}, u32[]{:S(2)}, u32[]{:S(2)}) collective-permute-start(bf16[64,1024]{1,0:T(8,128)(2,1)S(1)} %get-tuple-element.12), channel_id=1, source_target_pairs={{0,16},{4,20},{8,24},{12,28},{16,0},{20,4},{24,8},{28,12},{1,17},{... | collective-permute-start | bytes 393224 | tf_op jit(solution)/shard_map/ppermute | solution.py:117
  46.6 8.9 %collective-permute-start.8 = (bf16[64,1024]{1,0:T(8,128)(2,1)S(1)}, bf16[64,1024]{1,0:T(8,128)(2,1)S(1)}, u32[]{:S(2)}, u32[]{:S(2)}) collective-permute-start(bf16[64,1024]{1,0:T(8,128)(2,1)S(1)} %get-tuple-element.12), channel_id=1, source_target_pairs={{0,8},{4,12},{8,0},{12,4},{16,24},{20,28},{24,16},{28,20},{1,9},{5... | collective-permute-start | bytes 393224 | tf_op jit(solution)/shard_map/ppermute | solution.py:117
  47.2 9.9 %collective-permute-start.9 = (bf16[64,1024]{1,0:T(8,128)(2,1)S(1)}, bf16[64,1024]{1,0:T(8,128)(2,1)S(1)}, u32[]{:S(2)}, u32[]{:S(2)}) collective-permute-start(bf16[64,1024]{1,0:T(8,128)(2,1)S(1)} %get-tuple-element.12), channel_id=1, source_target_pairs={{0,4},{4,0},{8,12},{12,8},{16,20},{20,16},{24,28},{28,24},{1,5},{5... | collective-permute-start | bytes 393224 | tf_op jit(solution)/shard_map/ppermute | solution.py:117
  54.9 5.4 %collective-permute-start.11 = (bf16[64,1024]{1,0:T(8,128)(2,1)S(1)}, bf16[64,1024]{1,0:T(8,128)(2,1)S(1)}, u32[]{:S(2)}, u32[]{:S(2)}) collective-permute-start(bf16[64,1024]{1,0:T(8,128)(2,1)S(1)} %collective-permute-done.7), channel_id=1, source_target_pairs={{0,8},{4,12},{8,0},{12,4},{16,24},{20,28},{24,16},{28,20},{1,9},{5... | collective-permute-start | bytes 393224 | tf_op jit(solution)/shard_map/ppermute | solution.py:117
  54.9 9.2 %collective-permute-start.12 = (bf16[64,1024]{1,0:T(8,128)(2,1)S(1)}, bf16[64,1024]{1,0:T(8,128)(2,1)S(1)}, u32[]{:S(2)}, u32[]{:S(2)}) collective-permute-start(bf16[64,1024]{1,0:T(8,128)(2,1)S(1)} %collective-permute-done.7), channel_id=1, source_target_pairs={{0,4},{4,0},{8,12},{12,8},{16,20},{20,16},{24,28},{28,24},{1,5},{5... | collective-permute-start | bytes 393224 | tf_op jit(solution)/shard_map/ppermute | solution.py:117
  55.6 8.5 %collective-permute-start.10 = (bf16[64,1024]{1,0:T(8,128)(2,1)S(1)}, bf16[64,1024]{1,0:T(8,128)(2,1)S(1)}, u32[]{:S(2)}, u32[]{:S(2)}) collective-permute-start(bf16[64,1024]{1,0:T(8,128)(2,1)S(1)} %collective-permute-done.8), channel_id=1, source_target_pairs={{0,4},{4,0},{8,12},{12,8},{16,20},{20,16},{24,28},{28,24},{1,5},{5... | collective-permute-start | bytes 393224 | tf_op jit(solution)/shard_map/ppermute | solution.py:117
  60.3 5.6 %collective-permute-start.13 = (bf16[64,1024]{1,0:T(8,128)(2,1)S(1)}, bf16[64,1024]{1,0:T(8,128)(2,1)S(1)}, u32[]{:S(2)}, u32[]{:S(2)}) collective-permute-start(bf16[64,1024]{1,0:T(8,128)(2,1)S(1)} %collective-permute-done.11), channel_id=1, source_target_pairs={{0,4},{4,0},{8,12},{12,8},{16,20},{20,16},{24,28},{28,24},{1,5},{5... | collective-permute-start | bytes 393224 | tf_op jit(solution)/shard_map/ppermute | solution.py:117
  66.0 1.0 %copy-start.4 = (bf16[8,64,1024]{2,1,0:T(8,128)(2,1)}, bf16[8,64,1024]{2,1,0:T(8,128)(2,1)S(1)}, u32[]{:S(2)}) copy-start(bf16[8,64,1024]{2,1,0:T(8,128)(2,1)S(1)} %bitcast_dynamic-update-slice_fusion) | copy-start | bytes 3145732

commit v4 on v3

--- a/solution.py
+++ b/solution.py
@@ -49,45 +49,82 @@
     return butterfly(groups)
 
 
-def rotate_kernel(count, base, *refs):
-    pieces, (sign_ref, matrix_ref, rotated, biggest_ref) = refs[:count], refs[count:]
-    rotate_pieces(pieces, sign_ref, matrix_ref, rotated, biggest_ref, None, base)
-
-
-def rotate_pieces(pieces, sign_ref, matrix_ref, rotated, biggest_ref, biggest, base):
+def square_rows(groups):
+    squares = None
+    for group in groups:
+        squares = group * group if squares is None else squares + group * group
+    return jnp.sum(squares, axis=1, keepdims=True)
+
+
+def sums_kernel(base, x_ref, sign_ref, matrix_ref, sums_ref):
+    owned, width = x_ref.shape[2:]
+    signs = sign_ref[...].astype(jnp.float32).astype(jnp.bfloat16)
+    rows = x_ref[...].reshape(2 * owned, width) * signs
+    squares = square_rows(rotate_groups([rows], matrix_ref[...], base))
+    shape = (2 * owned, 2 * owned)
+    row, lane = (lax.broadcasted_iota(jnp.int32, shape, axis) for axis in (0, 1))
+    line = jnp.sum(jnp.where(row == lane, squares, 0.0), axis=0, keepdims=True)
+    sums_ref[...] = jnp.broadcast_to(line, sums_ref.shape)
+
+
+def scale_rows(sums_ref, offset, owned, width, near):
+    biggest = jnp.max(sums_ref[...], axis=0, keepdims=True)
+    shape = (owned, 2 * owned)
+    row, lane = (lax.broadcasted_iota(jnp.int32, shape, axis) for axis in (0, 1))
+    biggest = jnp.sum(jnp.where(lane == row + offset, biggest, 0.0), axis=1, keepdims=True)
+    mean = biggest * (1.0 / (width * width))
+    scale = jnp.sqrt(mean + 1e-06)
+    peak = jnp.sqrt(mean * width) / scale
+    step = near * jnp.where(
+        peak >= clamp_level, clamp_level / 32768.0, jnp.maximum(peak, 1e-20) / 32767.0
+    )
+    return scale, step
+
+
+def add_levels(pieces, scale, sign_ref, matrix_ref, base):
+    width = pieces[0].shape[1]
+    signs = sign_ref[...].astype(jnp.float32).astype(jnp.bfloat16)
     matrix = matrix_ref[...]
-    signs = sign_ref[...].astype(jnp.float32).astype(jnp.bfloat16)
-    for r, piece in enumerate(pieces):
+    inverse = (1.0 / math.sqrt(width)) / scale
+    totals = None
+    for piece in pieces:
         groups = rotate_groups([piece[...] * signs], matrix, base)
-        squares = None
-        for g, group in enumerate(groups):
-            rotated[r, :, g * base : (g + 1) * base] = group
-            term = group * group
-            squares = term if squares is None else squares + term
-        squares = jnp.sum(squares, axis=1, keepdims=True)
-        biggest = squares if biggest is None else jnp.maximum(biggest, squares)
-    if biggest_ref is not None:
-        biggest_ref[...] = jnp.broadcast_to(biggest, biggest_ref.shape)
-    return biggest
-
-
-def reduce_kernel(count, base, *refs):
-    pieces, rest = refs[:count], refs[count:]
-    near_ref, biggest_ref, sign_ref, matrix_ref, unrot_ref, square_ref, rotated = rest
-    owned, width = unrot_ref.shape
-    near = near_ref.shape[0]
-    replicas = near + count
-    biggest = rotate_pieces(
-        pieces, sign_ref, matrix_ref, rotated, None, biggest_ref[:, 0:1], base
-    )
-    scale = jnp.sqrt(biggest * (1.0 / (width * width)) + 1e-06)
-    inverse = (1.0 / math.sqrt(width)) / scale
-    total = None
-    for source, r in [(near_ref, r) for r in range(near)] + [(rotated, r) for r in range(count)]:
-        level = jnp.clip(source[r] * inverse, -clamp_level, clamp_level)
-        level = level.astype(jnp.bfloat16).astype(jnp.float32)
-        total = level if total is None else total + level
-    mean_scale = scale / replicas
+        levels = [
+            jnp.clip(group * inverse, -clamp_level, clamp_level)
+            .astype(jnp.bfloat16)
+            .astype(jnp.float32)
+            for group in groups
+        ]
+        totals = levels if totals is None else [t + v for t, v in zip(totals, levels)]
+    return totals
+
+
+def proxy_kernel(near, base, offset_ref, *refs):
+    pieces, (sums_ref, sign_ref, matrix_ref, sent_ref) = refs[:near], refs[near:]
+    owned, width = sent_ref.shape
+    scale, step = scale_rows(sums_ref, owned - offset_ref[0, 0], owned, width, near)
+    totals = add_levels(pieces, scale, sign_ref, matrix_ref, base)
+    for g, total in enumerate(totals):
+        value = jnp.clip(jnp.round(total / step), -32767.0, 32767.0)
+        sent_ref[:, g * base : (g + 1) * base] = value.astype(jnp.int16)
+
+
+def owner_kernel(near, base, offset_ref, *refs):
+    pieces, (sums_ref, sign_ref, matrix_ref, total_ref) = refs[:near], refs[near:]
+    owned, width = total_ref.shape
+    scale, _ = scale_rows(sums_ref, offset_ref[0, 0], owned, width, near)
+    totals = add_levels(pieces, scale, sign_ref, matrix_ref, base)
+    for g, total in enumerate(totals):
+        total_ref[:, g * base : (g + 1) * base] = total
+
+
+def finish_kernel(
+    near, base, offset_ref, near_ref, far_ref, sums_ref, sign_ref, matrix_ref, unrot_ref, square_ref
+):
+    owned, width = near_ref.shape
+    scale, step = scale_rows(sums_ref, offset_ref[0, 0], owned, width, near)
+    total = near_ref[...] + far_ref[...].astype(jnp.float32) * step
+    mean_scale = scale / (2 * near)
     mean_rot = total * mean_scale
     squares = jnp.sum(mean_rot * mean_rot)
     square_ref[...] = jnp.full(square_ref.shape, squares, jnp.float32)
@@ -150,42 +187,62 @@
     base = min(width, 256)
     matrix = jnp.asarray(hadamard(base), jnp.bfloat16)
     me = lax.axis_index("dp")
-    local = grads.reshape(replicas, owned, width)
-
-    def block_of(index):
-        return lax.dynamic_slice_in_dim(local, index, 1, 0).reshape(owned, width)
-
-    near = max(replicas // 2, 1)
-    pieces = {}
-    for mask in list(range(near, replicas)) + list(range(1, near)):
-        pieces[mask] = swap(block_of(me ^ mask), mask)
-    pieces[0] = block_of(me)
+    near = replicas // 2
+    offset = (me // near * owned).astype(jnp.int32).reshape(1, 1)
     params = pltpu.CompilerParams(vmem_limit_bytes=vmem_bytes)
-    cost = pl.CostEstimate(
-        flops=blocks * width * base, bytes_accessed=3 * blocks * width, transcendentals=0
-    )
-    near_rotated, biggest = pl.pallas_call(
-        functools.partial(rotate_kernel, near, base),
-        out_shape=(
-            jax.ShapeDtypeStruct((near, owned, width), jnp.float32),
-            jax.ShapeDtypeStruct((owned, lanes), jnp.float32),
-        ),
-        compiler_params=params,
-        cost_estimate=cost,
-        name="rotate_near",
-    )(*[pieces[mask] for mask in range(near)], signs, matrix)
-    far = replicas - near
+    scalar = pl.BlockSpec(memory_space=pltpu.SMEM)
+    array = pl.BlockSpec(memory_space=pltpu.VMEM)
+
+    def block_of(source, index):
+        source = source.reshape(replicas, owned, width)
+        return lax.dynamic_slice_in_dim(source, index, 1, 0).reshape(owned, width)
+
+    far_pieces = [swap(block_of(grads, me ^ mask ^ near), mask) for mask in range(1, near)]
+    far_pieces.append(block_of(grads, me ^ near))
+    sums = pl.pallas_call(
+        functools.partial(sums_kernel, base),
+        grid=(near,),
+        in_specs=[
+            pl.BlockSpec((2, 1, owned, width), lambda j: (0, j, 0, 0)),
+            pl.BlockSpec((1, width), lambda j: (0, 0)),
+            pl.BlockSpec((base, base), lambda j: (0, 0)),
+        ],
+        out_specs=pl.BlockSpec((2, 1, 1, 2 * owned), lambda j: (0, j, 0, 0)),
+        out_shape=jax.ShapeDtypeStruct((2, near, 1, 2 * owned), jnp.float32),
+        compiler_params=params,
+        name="sum_squares",
+    )(grads.reshape(2, near, owned, width), signs, matrix)
+    grads, sums = lax.optimization_barrier((grads, sums))
+    sums = lax.all_to_all(
+        sums.reshape(replicas, 1, 2 * owned), "dp", split_axis=0, concat_axis=0, tiled=True
+    ).reshape(replicas, 2 * owned)
+    near_pieces = [swap(block_of(grads, me ^ mask), mask) for mask in range(1, near)]
+    near_pieces.append(block_of(grads, me))
+    sent = pl.pallas_call(
+        functools.partial(proxy_kernel, near, base),
+        in_specs=[scalar] + [array] * (near + 3),
+        out_shape=jax.ShapeDtypeStruct((owned, width), jnp.int16),
+        compiler_params=params,
+        name="proxy_blocks",
+    )(offset, *far_pieces, sums, signs, matrix)
+    far_total = swap(sent, near)
+    near_total = pl.pallas_call(
+        functools.partial(owner_kernel, near, base),
+        in_specs=[scalar] + [array] * (near + 3),
+        out_shape=jax.ShapeDtypeStruct((owned, width), jnp.float32),
+        compiler_params=params,
+        name="owner_blocks",
+    )(offset, *near_pieces, sums, signs, matrix)
     unrot, squares = pl.pallas_call(
-        functools.partial(reduce_kernel, far, base),
+        functools.partial(finish_kernel, near, base),
+        in_specs=[scalar] + [array] * 5,
         out_shape=(
             jax.ShapeDtypeStruct((owned, width), jnp.float32),
             jax.ShapeDtypeStruct((devices, 1, lanes), jnp.float32),
         ),
-        scratch_shapes=[pltpu.VMEM((max(far, 1), owned, width), jnp.float32)],
-        compiler_params=params,
-        cost_estimate=cost,
-        name="reduce_blocks",
-    )(*[pieces[mask] for mask in range(near, replicas)], near_rotated, biggest, signs, matrix)
+        compiler_params=params,
+        name="finish_blocks",
+    )(offset, near_total, far_total, sums, signs, matrix)
     squares = lax.all_to_all(squares, ("dp", "expert"), split_axis=0, concat_axis=0, tiled=True)
     limit = target_rms * math.sqrt(blocks * width * lax.axis_size("expert"))
     new_weights, update_grad = pl.pallas_call(

time: 67.1 us -> 63.5 us (0.946)
  blocking collectives: 14.9 us -> 0 us
  starting transfers between devices: 17.6 us -> 22.7 us
  waiting for transfers between devices: 28.4 us -> 31.2 us
  Pallas kernels: 2.65 us -> 5.2 us
  local copies, waits for them, and re-layouts: 2.61 us -> 3.38 us
    all_to_all x1 -> x0, blocking collectives: 14.9 us -> none  [on_device(): lax.all_to_all(squares, ('dp', 'expert'), split_axis=0, concat_axis=0, ti...]
    all_to_all x0 -> x2, waiting for transfers between devices: none -> 9.77 us  [the longest x1 7.05 us: on_device(): lax.all_to_all(squares, ('dp', 'expert'), split_axis=0, concat_axis=0, ti...]
    all_to_all x0 -> x2, starting transfers between devices: none -> 9.48 us  [the longest x1 6.22 us: on_device(): lax.all_to_all(sums.reshape(replicas, 1, 2 * owned), 'dp', split_axis=0,...]
    ppermute x14, waiting for transfers between devices: 28.4 us -> 21.4 us  [swap(): return lax.ppermute(value, 'dp', [(i, i ^ mask) for i in range(size)])]
    ppermute x14, starting transfers between devices: 17.6 us -> 13.2 us  [swap(): return lax.ppermute(value, 'dp', [(i, i ^ mask) for i in range(size)])]
    pallas_call x2 -> x4, Pallas kernels: 1.83 us -> 4.38 us  [the longest x1 2.26 us: on_device(): pl.pallas_call(functools.partial(sums_kernel, base), grid=(near,), in_spe...]
    unnamed x10 -> x14, local copies, waits for them, and re-layouts: 0.99 us -> 1.89 us
    reshape x1 -> x2, local copies, waits for them, and re-layouts: 1.4 us -> 1.26 us  [block_of(): return lax.dynamic_slice_in_dim(source, index, 1, 0).reshape(owned, width)]
  transfers between devices with their start and end apart: 14 -> 16, of which waited for: 6 -> 8; matrix products, arithmetic and copies ran while one was open for 0% -> 0% of each run, Pallas kernels for 1% -> 5%
where the time goes in v4:
time: 63.5 us; the launch traced here: 63.3 us
  waiting for transfers between devices  31.2 us (49%)
  starting transfers between devices  22.7 us (36%)
  Pallas kernels  5.2 us (8%)
  local copies, waits for them, and re-layouts  3.38 us (5%)
  between operations  0.85 us (1%)
    ppermute x14, waiting for transfers between devices, swap(): return lax.ppermute(value, 'dp', [(i, i ^ mask) for i in range(size)])  21.4 us
    ppermute x14, starting transfers between devices, swap(): return lax.ppermute(value, 'dp', [(i, i ^ mask) for i in range(size)])  13.2 us
    all_to_all x1, waiting for transfers between devices, on_device(): lax.all_to_all(squares, ('dp', 'expert'), split_axis=0, concat_axis=0, ti...  7.05 us
    all_to_all x1, starting transfers between devices, on_device(): lax.all_to_all(sums.reshape(replicas, 1, 2 * owned), 'dp', split_axis=0,...  6.22 us
    all_to_all x1, starting transfers between devices, on_device(): lax.all_to_all(squares, ('dp', 'expert'), split_axis=0, concat_axis=0, ti...  3.26 us
    all_to_all x1, waiting for transfers between devices, on_device(): lax.all_to_all(sums.reshape(replicas, 1, 2 * owned), 'dp', split_axis=0,...  2.72 us
    pallas_call x1, Pallas kernels, on_device(): pl.pallas_call(functools.partial(sums_kernel, base), grid=(near,), in_spe...  2.26 us
    unnamed x14, local copies, waits for them, and re-layouts  1.89 us
  transfers between devices with their start and end apart: 16, of which 8 were waited for; matrix products, arithmetic and copies ran while one was open for 0% of the time, Pallas kernels for 5%

profile of v4, /device:TPU:0, one launch (start us, length us, event | category | flops | bytes accessed | tf_op | source)
XLA Modules:
  0.0 63.3 jit_solution(4277102553091369958)
XLA Ops:
  0.7 1.2 %dynamic-slice_bitcast_fusion = (bf16[64,1024]{1,0:T(8,128)(2,1)S(1)}, bf16[64,1024]{1,0:T(8,128)(2,1)S(1)}, bf16[64,1024]{1,0:T(8,128)(2,1)S(1)}, bf16[64,1024]{1,0:T(8,128)(2,1)S(1)}) fusion(bf16[8,64,1024]{2,1,0:T(8,128)(2,1)} %bitcast.45, s32[]{:T(128)S(6)} %select_n.51, s32[]{:T(128)S(6)} %select_n.50, s32[]{:T(128)S(6)} %select_n.49, s32[]{:T(128)S(6)} %select_n.48), kind=kLoop, calls=%fused_computation.8 | loop fusion | bytes 1048592 | tf_op jit(solution)/shard_map/reshape | solution.py:198
  1.9 3.0 %collective-permute-start.3 = (bf16[64,1024]{1,0:T(8,128)(2,1)S(1)}, bf16[64,1024]{1,0:T(8,128)(2,1)S(1)}, u32[]{:S(2)}, u32[]{:S(2)}) collective-permute-start(bf16[64,1024]{1,0:T(8,128)(2,1)S(1)} %get-tuple-element.17), channel_id=1, source_target_pairs={{0,4},{4,0},{8,12},{12,8},{16,20},{20,16},{24,28},{28,24},{1,5},{5... | collective-permute-start | bytes 393224 | tf_op jit(solution)/shard_map/ppermute | solution.py:154
  4.9 1.6 %collective-permute-start.4 = (bf16[64,1024]{1,0:T(8,128)(2,1)S(1)}, bf16[64,1024]{1,0:T(8,128)(2,1)S(1)}, u32[]{:S(2)}, u32[]{:S(2)}) collective-permute-start(bf16[64,1024]{1,0:T(8,128)(2,1)S(1)} %get-tuple-element.16), channel_id=1, source_target_pairs={{0,8},{4,12},{8,0},{12,4},{16,24},{20,28},{24,16},{28,20},{1,9},{5... | collective-permute-start | bytes 393224 | tf_op jit(solution)/shard_map/ppermute | solution.py:154
  6.5 0.9 %copy-done.1 = bf16[256,256]{1,0:T(8,128)(2,1)S(1)} copy-done((bf16[256,256]{1,0:T(8,128)(2,1)S(1)}, bf16[256,256]{1,0:T(8,128)(2,1)}, u32[]{:S(2)}) %copy-start.1) | copy-done | bytes 131096
  7.4 2.3 %sum_squares.1 = f32[2,4,1,128]{3,2,1,0:T(1,128)} custom-call(bf16[2,4,64,1024]{3,2,1,0:T(8,128)(2,1)S(1)} %bitcast.46, s32[1,1024]{1,0:T(1,128)S(1)} %copy-done.5, bf16[256,256]{1,0:T(8,128)(2,1)S(1)} %copy-done.1), custom_call_target="tpu_custom_call" | custom-call | tf_op jit(solution)/shard_map/sum_squares/pallas_call | solution.py:202
  9.7 6.2 %all-to-all-start = ((f32[8,1,128]{2,1,0:T(1,128)}), f32[8,1,128]{2,1,0:T(1,128)S(1)}, u32[]{:S(2)}, u32[]{:S(2)}) async-start(f32[8,1,128]{2,1,0:T(1,128)} %bitcast.8), calls=%async_computation | async-start | bytes 8192 | tf_op jit(solution)/shard_map/all_to_all | solution.py:216
  15.9 2.1 %collective-permute-start = (bf16[64,1024]{1,0:T(8,128)(2,1)S(1)}, bf16[64,1024]{1,0:T(8,128)(2,1)S(1)}, u32[]{:S(2)}, u32[]{:S(2)}) collective-permute-start(bf16[64,1024]{1,0:T(8,128)(2,1)S(1)} %get-tuple-element.21), channel_id=1, source_target_pairs={{0,4},{4,0},{8,12},{12,8},{16,20},{20,16},{24,28},{28,24},{1,5},{5... | collective-permute-start | bytes 393224 | tf_op jit(solution)/shard_map/ppermute | solution.py:154
  18.0 1.5 %collective-permute-start.1 = (bf16[64,1024]{1,0:T(8,128)(2,1)S(1)}, bf16[64,1024]{1,0:T(8,128)(2,1)S(1)}, u32[]{:S(2)}, u32[]{:S(2)}) collective-permute-start(bf16[64,1024]{1,0:T(8,128)(2,1)S(1)} %get-tuple-element.20), channel_id=1, source_target_pairs={{0,8},{4,12},{8,0},{12,4},{16,24},{20,28},{24,16},{28,20},{1,9},{5... | collective-permute-start | bytes 393224 | tf_op jit(solution)/shard_map/ppermute | solution.py:154
  19.6 2.7 %all-to-all-done = f32[8,1,128]{2,1,0:T(1,128)S(1)} async-done(((f32[8,1,128]{2,1,0:T(1,128)}), f32[8,1,128]{2,1,0:T(1,128)S(1)}, u32[]{:S(2)}, u32[]{:S(2)}) %all-to-all-start) | async-done | bytes 4128 | tf_op jit(solution)/shard_map/all_to_all | solution.py:216
  22.9 0.6 collective-permute-start.6
  23.5 3.2 %collective-permute-done.2.refs_2_ = bf16[64,1024]{1,0:T(8,128)(2,1)S(1)} collective-permute-done((bf16[64,1024]{1,0:T(8,128)(2,1)S(1)}, bf16[64,1024]{1,0:T(8,128)(2,1)S(1)}, u32[]{:S(2)}, u32[]{:S(2)}) %collective-permute-start.2) | collective-permute-done | bytes 131104 | tf_op jit(solution)/shard_map/ppermute | solution.py:154
  27.3 2.9 %collective-permute-done.6.far_ref = s16[64,1024]{1,0:T(8,128)(2,1)S(1)} collective-permute-done((s16[64,1024]{1,0:T(8,128)(2,1)S(1)}, s16[64,1024]{1,0:T(8,128)(2,1)S(1)}, u32[]{:S(2)}, u32[]{:S(2)}) %collective-permute-start.6) | collective-permute-done | bytes 131104 | tf_op jit(solution)/shard_map/ppermute | solution.py:154
  30.2 1.0 %finish_blocks.1 = (f32[64,1024]{1,0:T(8,128)S(1)}, f32[32,1,128]{2,1,0:T(1,128)}) custom-call(s32[1,1]{1,0:T(1,128)} %bitcast.offset_ref, f32[64,1024]{1,0:T(8,128)S(1)} %owner_blocks.1.near_ref, s16[64,1024]{1,0:T(8,128)(2,1)S(1)} %collective-permute-done.6.far_ref, f32[8,128]{1,0:T(8,128)S(1)} %bitcast.52, s32[1,1024]{1,0:T(1,128)S(1)} %copy-done.5, ...), custom_call_target="tpu_custom_call" | custom-call | tf_op jit(solution)/shard_map/finish_blocks/pallas_call | solution.py:236
  31.2 3.3 %all-to-all-start.1 = ((f32[32,1,128]{2,1,0:T(1,128)}), f32[32,1,128]{2,1,0:T(1,128)S(1)}, u32[]{:S(2)}, u32[]{:S(2)}) async-start(f32[32,1,128]{2,1,0:T(1,128)} %get-tuple-element.10), calls=%async_computation.1 | async-start | bytes 32768 | tf_op jit(solution)/shard_map/all_to_all | solution.py:246
  34.5 7.1 %all-to-all-done.1 = f32[32,1,128]{2,1,0:T(1,128)S(1)} async-done(((f32[32,1,128]{2,1,0:T(1,128)}), f32[32,1,128]{2,1,0:T(1,128)S(1)}, u32[]{:S(2)}, u32[]{:S(2)}) %all-to-all-start.1) | async-done | bytes 16416 | tf_op jit(solution)/shard_map/all_to_all | solution.py:246
  41.6 0.8 %update_blocks.1 = (bf16[64,1024]{1,0:T(8,128)(2,1)S(1)}, f32[64,1024]{1,0:T(8,128)}) custom-call(f32[32,128]{1,0:T(8,128)S(1)} %bitcast.53, f32[64,1024]{1,0:T(8,128)S(1)} %get-tuple-element.11.unrot_ref, bf16[64,1024]{1,0:T(8,128)(2,1)S(1)} %bitcast.48, bf16[64,1024]{1,0:T(8,128)(2,1)S(1)} %bitcast.49), custom_call_target="tpu_custom_call" | custom-call | tf_op jit(solution)/shard_map/update_blocks/pallas_call | solution.py:248
  44.2 7.0 %collective-permute-done.7 = bf16[64,1024]{1,0:T(8,128)(2,1)S(1)} collective-permute-done((bf16[64,1024]{1,0:T(8,128)(2,1)S(1)}, bf16[64,1024]{1,0:T(8,128)(2,1)S(1)}, u32[]{:S(2)}, u32[]{:S(2)}) %collective-permute-start.7) | collective-permute-done | bytes 131104 | tf_op jit(solution)/shard_map/ppermute | solution.py:154
  51.2 0.6 collective-permute-start.12
  51.9 1.5 %collective-permute-start.10 = (bf16[64,1024]{1,0:T(8,128)(2,1)S(1)}, bf16[64,1024]{1,0:T(8,128)(2,1)S(1)}, u32[]{:S(2)}, u32[]{:S(2)}) collective-permute-start(bf16[64,1024]{1,0:T(8,128)(2,1)S(1)} %collective-permute-done.8), channel_id=1, source_target_pairs={{0,4},{4,0},{8,12},{12,8},{16,20},{20,16},{24,28},{28,24},{1,5},{5... | collective-permute-start | bytes 393224 | tf_op jit(solution)/shard_map/ppermute | solution.py:154
  53.4 3.2 %collective-permute-done.11 = bf16[64,1024]{1,0:T(8,128)(2,1)S(1)} collective-permute-done((bf16[64,1024]{1,0:T(8,128)(2,1)S(1)}, bf16[64,1024]{1,0:T(8,128)(2,1)S(1)}, u32[]{:S(2)}, u32[]{:S(2)}) %collective-permute-start.11) | collective-permute-done | bytes 131104 | tf_op jit(solution)/shard_map/ppermute | solution.py:154
  56.6 0.6 collective-permute-start.13
  57.3 3.1 %collective-permute-done.10 = bf16[64,1024]{1,0:T(8,128)(2,1)S(1)} collective-permute-done((bf16[64,1024]{1,0:T(8,128)(2,1)S(1)}, bf16[64,1024]{1,0:T(8,128)(2,1)S(1)}, u32[]{:S(2)}, u32[]{:S(2)}) %collective-permute-start.10) | collective-permute-done | bytes 131104 | tf_op jit(solution)/shard_map/ppermute | solution.py:154
  60.5 1.8 %collective-permute-done.13 = bf16[64,1024]{1,0:T(8,128)(2,1)S(1)} collective-permute-done((bf16[64,1024]{1,0:T(8,128)(2,1)S(1)}, bf16[64,1024]{1,0:T(8,128)(2,1)S(1)}, u32[]{:S(2)}, u32[]{:S(2)}) %collective-permute-start.13) | collective-permute-done | bytes 131104 | tf_op jit(solution)/shard_map/ppermute | solution.py:154
  62.3 1.0 %copy-done.6 = bf16[8,64,1024]{2,1,0:T(8,128)(2,1)} copy-done((bf16[8,64,1024]{2,1,0:T(8,128)(2,1)}, bf16[8,64,1024]{2,1,0:T(8,128)(2,1)S(1)}, u32[]{:S(2)}) %copy-start.6) | copy-done | bytes 1048600
  (38 shorter events, 3.2 us)
Async XLA Ops:
  0.6 5.9 %copy-start = (bf16[1,1,512,1024]{3,2,1,0:T(8,128)(2,1)S(1)}, bf16[1,1,512,1024]{3,2,1,0:T(8,128)(2,1)}, u32[]{:S(2)}) copy-start(bf16[1,1,512,1024]{3,2,1,0:T(8,128)(2,1)} %param.5) | copy-start | bytes 3145732
  1.9 4.6 %copy-start.5 = (s32[1,1024]{1,0:T(1,128)S(1)}, s32[1,1024]{1,0:T(1,128)}, u32[]{:S(2)}) copy-start(s32[1,1024]{1,0:T(1,128)} %sign_ref.3) | copy-start | bytes 12292
  1.9 17.6 %collective-permute-start.3 = (bf16[64,1024]{1,0:T(8,128)(2,1)S(1)}, bf16[64,1024]{1,0:T(8,128)(2,1)S(1)}, u32[]{:S(2)}, u32[]{:S(2)}) collective-permute-start(bf16[64,1024]{1,0:T(8,128)(2,1)S(1)} %get-tuple-element.17), channel_id=1, source_target_pairs={{0,4},{4,0},{8,12},{12,8},{16,20},{20,16},{24,28},{28,24},{1,5},{5... | collective-permute-start | bytes 393224 | tf_op jit(solution)/shard_map/ppermute | solution.py:154
  4.9 17.4 %collective-permute-start.4 = (bf16[64,1024]{1,0:T(8,128)(2,1)S(1)}, bf16[64,1024]{1,0:T(8,128)(2,1)S(1)}, u32[]{:S(2)}, u32[]{:S(2)}) collective-permute-start(bf16[64,1024]{1,0:T(8,128)(2,1)S(1)} %get-tuple-element.16), channel_id=1, source_target_pairs={{0,8},{4,12},{8,0},{12,4},{16,24},{20,28},{24,16},{28,20},{1,9},{5... | collective-permute-start | bytes 393224 | tf_op jit(solution)/shard_map/ppermute | solution.py:154
  6.5 15.8 %collective-permute-start.5 = (bf16[64,1024]{1,0:T(8,128)(2,1)S(1)}, bf16[64,1024]{1,0:T(8,128)(2,1)S(1)}, u32[]{:S(2)}, u32[]{:S(2)}) collective-permute-start(bf16[64,1024]{1,0:T(8,128)(2,1)S(1)} %get-tuple-element.15), channel_id=1, source_target_pairs={{0,12},{4,8},{8,4},{12,0},{16,28},{20,24},{24,20},{28,16},{1,13},{... | collective-permute-start | bytes 393224 | tf_op jit(solution)/shard_map/ppermute | solution.py:154
  6.5 0.9 %copy-start.1 = (bf16[256,256]{1,0:T(8,128)(2,1)S(1)}, bf16[256,256]{1,0:T(8,128)(2,1)}, u32[]{:S(2)}) copy-start(bf16[256,256]{1,0:T(8,128)(2,1)} %constant.41.clone.matrix_ref.refs_6_) | copy-start | bytes 393220
  9.7 12.6 %all-to-all-start = ((f32[8,1,128]{2,1,0:T(1,128)}), f32[8,1,128]{2,1,0:T(1,128)S(1)}, u32[]{:S(2)}, u32[]{:S(2)}) async-start(f32[8,1,128]{2,1,0:T(1,128)} %bitcast.8), calls=%async_computation | async-start | bytes 8192 | tf_op jit(solution)/shard_map/all_to_all | solution.py:216
  15.9 6.4 %copy-start.2 = (bf16[256,256]{1,0:T(8,128)(2,1)S(1)}, bf16[256,256]{1,0:T(8,128)(2,1)}, u32[]{:S(2)}) copy-start(bf16[256,256]{1,0:T(8,128)(2,1)} %constant.41.clone.matrix_ref.refs_6_) | copy-start | bytes 393220
  15.9 7.6 %collective-permute-start = (bf16[64,1024]{1,0:T(8,128)(2,1)S(1)}, bf16[64,1024]{1,0:T(8,128)(2,1)S(1)}, u32[]{:S(2)}, u32[]{:S(2)}) collective-permute-start(bf16[64,1024]{1,0:T(8,128)(2,1)S(1)} %get-tuple-element.21), channel_id=1, source_target_pairs={{0,4},{4,0},{8,12},{12,8},{16,20},{20,16},{24,28},{28,24},{1,5},{5... | collective-permute-start | bytes 393224 | tf_op jit(solution)/shard_map/ppermute | solution.py:154
  18.0 5.5 %collective-permute-start.1 = (bf16[64,1024]{1,0:T(8,128)(2,1)S(1)}, bf16[64,1024]{1,0:T(8,128)(2,1)S(1)}, u32[]{:S(2)}, u32[]{:S(2)}) collective-permute-start(bf16[64,1024]{1,0:T(8,128)(2,1)S(1)} %get-tuple-element.20), channel_id=1, source_target_pairs={{0,8},{4,12},{8,0},{12,4},{16,24},{20,28},{24,16},{28,20},{1,9},{5... | collective-permute-start | bytes 393224 | tf_op jit(solution)/shard_map/ppermute | solution.py:154
  19.5 7.3 %collective-permute-start.2 = (bf16[64,1024]{1,0:T(8,128)(2,1)S(1)}, bf16[64,1024]{1,0:T(8,128)(2,1)S(1)}, u32[]{:S(2)}, u32[]{:S(2)}) collective-permute-start(bf16[64,1024]{1,0:T(8,128)(2,1)S(1)} %get-tuple-element.19), channel_id=1, source_target_pairs={{0,12},{4,8},{8,4},{12,0},{16,28},{20,24},{24,20},{28,16},{1,13},{... | collective-permute-start | bytes 393224 | tf_op jit(solution)/shard_map/ppermute | solution.py:154
  22.9 7.3 %collective-permute-start.6 = (s16[64,1024]{1,0:T(8,128)(2,1)S(1)}, s16[64,1024]{1,0:T(8,128)(2,1)S(1)}, u32[]{:S(2)}, u32[]{:S(2)}) collective-permute-start(s16[64,1024]{1,0:T(8,128)(2,1)S(1)} %proxy_blocks.1), channel_id=1, source_target_pairs={{0,16},{4,20},{8,24},{12,28},{16,0},{20,4},{24,8},{28,12},{1,17},{... | collective-permute-start | bytes 393224 | tf_op jit(solution)/shard_map/ppermute | solution.py:154
  30.2 11.3 %copy-start.3 = (bf16[1,64,1024]{2,1,0:T(8,128)(2,1)S(1)}, bf16[1,64,1024]{2,1,0:T(8,128)(2,1)}, u32[]{:S(2)}) copy-start(bf16[1,64,1024]{2,1,0:T(8,128)(2,1)} %param.7) | copy-start | bytes 393220
  30.2 11.3 %copy-start.4 = (bf16[1,64,1024]{2,1,0:T(8,128)(2,1)S(1)}, bf16[1,64,1024]{2,1,0:T(8,128)(2,1)}, u32[]{:S(2)}) copy-start(bf16[1,64,1024]{2,1,0:T(8,128)(2,1)} %param.8) | copy-start | bytes 393220
  31.2 10.3 %all-to-all-start.1 = ((f32[32,1,128]{2,1,0:T(1,128)}), f32[32,1,128]{2,1,0:T(1,128)S(1)}, u32[]{:S(2)}, u32[]{:S(2)}) async-start(f32[32,1,128]{2,1,0:T(1,128)} %get-tuple-element.10), calls=%async_computation.1 | async-start | bytes 32768 | tf_op jit(solution)/shard_map/all_to_all | solution.py:246
  42.4 8.9 %collective-permute-start.7 = (bf16[64,1024]{1,0:T(8,128)(2,1)S(1)}, bf16[64,1024]{1,0:T(8,128)(2,1)S(1)}, u32[]{:S(2)}, u32[]{:S(2)}) collective-permute-start(bf16[64,1024]{1,0:T(8,128)(2,1)S(1)} %get-tuple-element.12), channel_id=1, source_target_pairs={{0,16},{4,20},{8,24},{12,28},{16,0},{20,4},{24,8},{28,12},{1,17},{... | collective-permute-start | bytes 393224 | tf_op jit(solution)/shard_map/ppermute | solution.py:154
  43.0 8.9 %collective-permute-start.8 = (bf16[64,1024]{1,0:T(8,128)(2,1)S(1)}, bf16[64,1024]{1,0:T(8,128)(2,1)S(1)}, u32[]{:S(2)}, u32[]{:S(2)}) collective-permute-start(bf16[64,1024]{1,0:T(8,128)(2,1)S(1)} %get-tuple-element.12), channel_id=1, source_target_pairs={{0,8},{4,12},{8,0},{12,4},{16,24},{20,28},{24,16},{28,20},{1,9},{5... | collective-permute-start | bytes 393224 | tf_op jit(solution)/shard_map/ppermute | solution.py:154
  43.5 9.9 %collective-permute-start.9 = (bf16[64,1024]{1,0:T(8,128)(2,1)S(1)}, bf16[64,1024]{1,0:T(8,128)(2,1)S(1)}, u32[]{:S(2)}, u32[]{:S(2)}) collective-permute-start(bf16[64,1024]{1,0:T(8,128)(2,1)S(1)} %get-tuple-element.12), channel_id=1, source_target_pairs={{0,4},{4,0},{8,12},{12,8},{16,20},{20,16},{24,28},{28,24},{1,5},{5... | collective-permute-start | bytes 393224 | tf_op jit(solution)/shard_map/ppermute | solution.py:154
  51.2 5.4 %collective-permute-start.11 = (bf16[64,1024]{1,0:T(8,128)(2,1)S(1)}, bf16[64,1024]{1,0:T(8,128)(2,1)S(1)}, u32[]{:S(2)}, u32[]{:S(2)}) collective-permute-start(bf16[64,1024]{1,0:T(8,128)(2,1)S(1)} %collective-permute-done.7), channel_id=1, source_target_pairs={{0,8},{4,12},{8,0},{12,4},{16,24},{20,28},{24,16},{28,20},{1,9},{5... | collective-permute-start | bytes 393224 | tf_op jit(solution)/shard_map/ppermute | solution.py:154
  51.2 9.2 %collective-permute-start.12 = (bf16[64,1024]{1,0:T(8,128)(2,1)S(1)}, bf16[64,1024]{1,0:T(8,128)(2,1)S(1)}, u32[]{:S(2)}, u32[]{:S(2)}) collective-permute-start(bf16[64,1024]{1,0:T(8,128)(2,1)S(1)} %collective-permute-done.7), channel_id=1, source_target_pairs={{0,4},{4,0},{8,12},{12,8},{16,20},{20,16},{24,28},{28,24},{1,5},{5... | collective-permute-start | bytes 393224 | tf_op jit(solution)/shard_map/ppermute | solution.py:154
  51.9 8.5 %collective-permute-start.10 = (bf16[64,1024]{1,0:T(8,128)(2,1)S(1)}, bf16[64,1024]{1,0:T(8,128)(2,1)S(1)}, u32[]{:S(2)}, u32[]{:S(2)}) collective-permute-start(bf16[64,1024]{1,0:T(8,128)(2,1)S(1)} %collective-permute-done.8), channel_id=1, source_target_pairs={{0,4},{4,0},{8,12},{12,8},{16,20},{20,16},{24,28},{28,24},{1,5},{5... | collective-permute-start | bytes 393224 | tf_op jit(solution)/shard_map/ppermute | solution.py:154
  56.6 5.6 %collective-permute-start.13 = (bf16[64,1024]{1,0:T(8,128)(2,1)S(1)}, bf16[64,1024]{1,0:T(8,128)(2,1)S(1)}, u32[]{:S(2)}, u32[]{:S(2)}) collective-permute-start(bf16[64,1024]{1,0:T(8,128)(2,1)S(1)} %collective-permute-done.11), channel_id=1, source_target_pairs={{0,4},{4,0},{8,12},{12,8},{16,20},{20,16},{24,28},{28,24},{1,5},{5... | collective-permute-start | bytes 393224 | tf_op jit(solution)/shard_map/ppermute | solution.py:154
  62.3 1.0 %copy-start.6 = (bf16[8,64,1024]{2,1,0:T(8,128)(2,1)}, bf16[8,64,1024]{2,1,0:T(8,128)(2,1)S(1)}, u32[]{:S(2)}) copy-start(bf16[8,64,1024]{2,1,0:T(8,128)(2,1)S(1)} %bitcast_dynamic-update-slice_fusion) | copy-start | bytes 3145732

commit v5 on v4

--- a/solution.py
+++ b/solution.py
@@ -49,18 +49,10 @@
     return butterfly(groups)
 
 
-def square_rows(groups):
-    squares = None
-    for group in groups:
-        squares = group * group if squares is None else squares + group * group
-    return jnp.sum(squares, axis=1, keepdims=True)
-
-
-def sums_kernel(base, x_ref, sign_ref, matrix_ref, sums_ref):
+def sums_kernel(x_ref, sums_ref):
     owned, width = x_ref.shape[2:]
-    signs = sign_ref[...].astype(jnp.float32).astype(jnp.bfloat16)
-    rows = x_ref[...].reshape(2 * owned, width) * signs
-    squares = square_rows(rotate_groups([rows], matrix_ref[...], base))
+    rows = x_ref[...].reshape(2 * owned, width).astype(jnp.float32)
+    squares = jnp.sum(rows * rows, axis=1, keepdims=True)
     shape = (2 * owned, 2 * owned)
     row, lane = (lax.broadcasted_iota(jnp.int32, shape, axis) for axis in (0, 1))
     line = jnp.sum(jnp.where(row == lane, squares, 0.0), axis=0, keepdims=True)
@@ -72,7 +64,7 @@
     shape = (owned, 2 * owned)
     row, lane = (lax.broadcasted_iota(jnp.int32, shape, axis) for axis in (0, 1))
     biggest = jnp.sum(jnp.where(lane == row + offset, biggest, 0.0), axis=1, keepdims=True)
-    mean = biggest * (1.0 / (width * width))
+    mean = biggest * (1.0 / width)
     scale = jnp.sqrt(mean + 1e-06)
     peak = jnp.sqrt(mean * width) / scale
     step = near * jnp.where(
@@ -119,7 +111,7 @@
 
 
 def finish_kernel(
-    near, base, offset_ref, near_ref, far_ref, sums_ref, sign_ref, matrix_ref, unrot_ref, square_ref
+    near, offset_ref, near_ref, far_ref, sums_ref, total_ref, scale_ref, square_ref
 ):
     owned, width = near_ref.shape
     scale, step = scale_rows(sums_ref, offset_ref[0, 0], owned, width, near)
@@ -128,10 +120,17 @@
     mean_rot = total * mean_scale
     squares = jnp.sum(mean_rot * mean_rot)
     square_ref[...] = jnp.full(square_ref.shape, squares, jnp.float32)
+    total_ref[...] = total
+    scale_ref[...] = jnp.broadcast_to(mean_scale, scale_ref.shape)
+
+
+def back_kernel(base, total_ref, scale_ref, sign_ref, matrix_ref, unrot_ref):
+    owned, width = total_ref.shape
+    total = total_ref[...]
     high = total.astype(jnp.bfloat16)
     low = (total - high.astype(jnp.float32)).astype(jnp.bfloat16)
     groups = rotate_groups([high, low], matrix_ref[...], base)
-    back = mean_scale * (1.0 / math.sqrt(width))
+    back = scale_ref[:, 0:1] * (1.0 / math.sqrt(width))
     signs = sign_ref[...].astype(jnp.float32)
     for g, group in enumerate(groups):
         cut = slice(g * base, (g + 1) * base)
@@ -197,25 +196,21 @@
         source = source.reshape(replicas, owned, width)
         return lax.dynamic_slice_in_dim(source, index, 1, 0).reshape(owned, width)
 
-    far_pieces = [swap(block_of(grads, me ^ mask ^ near), mask) for mask in range(1, near)]
-    far_pieces.append(block_of(grads, me ^ near))
     sums = pl.pallas_call(
-        functools.partial(sums_kernel, base),
+        sums_kernel,
         grid=(near,),
-        in_specs=[
-            pl.BlockSpec((2, 1, owned, width), lambda j: (0, j, 0, 0)),
-            pl.BlockSpec((1, width), lambda j: (0, 0)),
-            pl.BlockSpec((base, base), lambda j: (0, 0)),
-        ],
+        in_specs=[pl.BlockSpec((2, 1, owned, width), lambda j: (0, j, 0, 0))],
         out_specs=pl.BlockSpec((2, 1, 1, 2 * owned), lambda j: (0, j, 0, 0)),
         out_shape=jax.ShapeDtypeStruct((2, near, 1, 2 * owned), jnp.float32),
         compiler_params=params,
         name="sum_squares",
-    )(grads.reshape(2, near, owned, width), signs, matrix)
+    )(grads.reshape(2, near, owned, width))
     grads, sums = lax.optimization_barrier((grads, sums))
     sums = lax.all_to_all(
         sums.reshape(replicas, 1, 2 * owned), "dp", split_axis=0, concat_axis=0, tiled=True
     ).reshape(replicas, 2 * owned)
+    far_pieces = [swap(block_of(grads, me ^ mask ^ near), mask) for mask in range(1, near)]
+    far_pieces.append(block_of(grads, me ^ near))
     near_pieces = [swap(block_of(grads, me ^ mask), mask) for mask in range(1, near)]
     near_pieces.append(block_of(grads, me))
     sent = pl.pallas_call(
@@ -233,16 +228,23 @@
         compiler_params=params,
         name="owner_blocks",
     )(offset, *near_pieces, sums, signs, matrix)
-    unrot, squares = pl.pallas_call(
-        functools.partial(finish_kernel, near, base),
-        in_specs=[scalar] + [array] * 5,
+    total, mean_scale, squares = pl.pallas_call(
+        functools.partial(finish_kernel, near),
+        in_specs=[scalar] + [array] * 3,
         out_shape=(
             jax.ShapeDtypeStruct((owned, width), jnp.float32),
+            jax.ShapeDtypeStruct((owned, lanes), jnp.float32),
             jax.ShapeDtypeStruct((devices, 1, lanes), jnp.float32),
         ),
         compiler_params=params,
         name="finish_blocks",
-    )(offset, near_total, far_total, sums, signs, matrix)
+    )(offset, near_total, far_total, sums)
+    unrot = pl.pallas_call(
+        functools.partial(back_kernel, base),
+        out_shape=jax.ShapeDtypeStruct((owned, width), jnp.float32),
+        compiler_params=params,
+        name="rotate_back",
+    )(total, mean_scale, signs, matrix)
     squares = lax.all_to_all(squares, ("dp", "expert"), split_axis=0, concat_axis=0, tiled=True)
     limit = target_rms * math.sqrt(blocks * width * lax.axis_size("expert"))
     new_weights, update_grad = pl.pallas_call(

time: 63.5 us -> 61.9 us (0.975)
  local copies, waits for them, and re-layouts: 3.38 us -> 2.52 us
    reshape x2 -> x1, local copies, waits for them, and re-layouts: 1.26 us -> 0.08 us  [block_of(): return lax.dynamic_slice_in_dim(source, index, 1, 0).reshape(owned, width)]
    pallas_call x2 -> x3, Pallas kernels: 3.23 us -> 2.84 us  [the longest x1 1.61 us: on_device(): pl.pallas_call(sums_kernel, grid=(near,), in_specs=[pl.BlockSpec((2, 1, o...]
  transfers between devices with their start and end apart: 16 -> 16, of which waited for: 8 -> 8; matrix products, arithmetic and copies ran while one was open for 0% -> 0% of each run, Pallas kernels for 5% -> 2%
where the time goes in v5:
time: 61.9 us; the launch traced here: 61.6 us
  waiting for transfers between devices  30.9 us (50%)
  starting transfers between devices  22.5 us (36%)
  Pallas kernels  4.82 us (8%)
  local copies, waits for them, and re-layouts  2.52 us (4%)
  between operations  0.86 us (1%)
    ppermute x14, waiting for transfers between devices, swap(): return lax.ppermute(value, 'dp', [(i, i ^ mask) for i in range(size)])  21.4 us
    ppermute x14, starting transfers between devices, swap(): return lax.ppermute(value, 'dp', [(i, i ^ mask) for i in range(size)])  13.1 us
    all_to_all x1, waiting for transfers between devices, on_device(): lax.all_to_all(squares, ('dp', 'expert'), split_axis=0, concat_axis=0, ti...  6.71 us
    all_to_all x1, starting transfers between devices, on_device(): lax.all_to_all(sums.reshape(replicas, 1, 2 * owned), 'dp', split_axis=0,...  6.22 us
    all_to_all x1, starting transfers between devices, on_device(): lax.all_to_all(squares, ('dp', 'expert'), split_axis=0, concat_axis=0, ti...  3.15 us
    all_to_all x1, waiting for transfers between devices, on_device(): lax.all_to_all(sums.reshape(replicas, 1, 2 * owned), 'dp', split_axis=0,...  2.83 us
    unnamed x14, local copies, waits for them, and re-layouts  2.21 us
    pallas_call x1, Pallas kernels, on_device(): pl.pallas_call(sums_kernel, grid=(near,), in_specs=[pl.BlockSpec((2, 1, o...  1.61 us
  transfers between devices with their start and end apart: 16, of which 8 were waited for; matrix products, arithmetic and copies ran while one was open for 0% of the time, Pallas kernels for 2%

profile of v5, /device:TPU:0, one launch (start us, length us, event | category | flops | bytes accessed | tf_op | source)
XLA Modules:
  0.0 61.6 jit_solution(10018439461229924716)
XLA Ops:
  0.7 1.2 %copy-done = bf16[1,1,512,1024]{3,2,1,0:T(8,128)(2,1)S(1)} copy-done((bf16[1,1,512,1024]{3,2,1,0:T(8,128)(2,1)S(1)}, bf16[1,1,512,1024]{3,2,1,0:T(8,128)(2,1)}, u32[]{:S(2)}) %copy-start) | copy-done | bytes 1048600
  1.9 1.6 %sum_squares.1 = f32[2,4,1,128]{3,2,1,0:T(1,128)} custom-call(bf16[2,4,64,1024]{3,2,1,0:T(8,128)(2,1)S(1)} %bitcast.44), custom_call_target="tpu_custom_call" | custom-call | tf_op jit(solution)/shard_map/sum_squares/pallas_call | solution.py:199
  3.6 3.0 %collective-permute-start.3 = (bf16[64,1024]{1,0:T(8,128)(2,1)S(1)}, bf16[64,1024]{1,0:T(8,128)(2,1)S(1)}, u32[]{:S(2)}, u32[]{:S(2)}) collective-permute-start(bf16[64,1024]{1,0:T(8,128)(2,1)S(1)} %get-tuple-element.19), channel_id=1, source_target_pairs={{0,4},{4,0},{8,12},{12,8},{16,20},{20,16},{24,28},{28,24},{1,5},{5... | collective-permute-start | bytes 393224 | tf_op jit(solution)/shard_map/ppermute | solution.py:153
  6.6 1.6 %collective-permute-start.4 = (bf16[64,1024]{1,0:T(8,128)(2,1)S(1)}, bf16[64,1024]{1,0:T(8,128)(2,1)S(1)}, u32[]{:S(2)}, u32[]{:S(2)}) collective-permute-start(bf16[64,1024]{1,0:T(8,128)(2,1)S(1)} %get-tuple-element.18), channel_id=1, source_target_pairs={{0,8},{4,12},{8,0},{12,4},{16,24},{20,28},{24,16},{28,20},{1,9},{5... | collective-permute-start | bytes 393224 | tf_op jit(solution)/shard_map/ppermute | solution.py:153
  8.2 6.2 %all-to-all-start = ((f32[8,1,128]{2,1,0:T(1,128)}), f32[8,1,128]{2,1,0:T(1,128)S(1)}, u32[]{:S(2)}, u32[]{:S(2)}) async-start(f32[8,1,128]{2,1,0:T(1,128)} %bitcast.8), calls=%async_computation | async-start | bytes 8192 | tf_op jit(solution)/shard_map/all_to_all | solution.py:209
  14.4 2.0 %collective-permute-start = (bf16[64,1024]{1,0:T(8,128)(2,1)S(1)}, bf16[64,1024]{1,0:T(8,128)(2,1)S(1)}, u32[]{:S(2)}, u32[]{:S(2)}) collective-permute-start(bf16[64,1024]{1,0:T(8,128)(2,1)S(1)} %get-tuple-element.23), channel_id=1, source_target_pairs={{0,4},{4,0},{8,12},{12,8},{16,20},{20,16},{24,28},{28,24},{1,5},{5... | collective-permute-start | bytes 393224 | tf_op jit(solution)/shard_map/ppermute | solution.py:153
  16.4 1.5 %collective-permute-start.1 = (bf16[64,1024]{1,0:T(8,128)(2,1)S(1)}, bf16[64,1024]{1,0:T(8,128)(2,1)S(1)}, u32[]{:S(2)}, u32[]{:S(2)}) collective-permute-start(bf16[64,1024]{1,0:T(8,128)(2,1)S(1)} %get-tuple-element.22), channel_id=1, source_target_pairs={{0,8},{4,12},{8,0},{12,4},{16,24},{20,28},{24,16},{28,20},{1,9},{5... | collective-permute-start | bytes 393224 | tf_op jit(solution)/shard_map/ppermute | solution.py:153
  18.0 2.8 %all-to-all-done = f32[8,1,128]{2,1,0:T(1,128)S(1)} async-done(((f32[8,1,128]{2,1,0:T(1,128)}), f32[8,1,128]{2,1,0:T(1,128)S(1)}, u32[]{:S(2)}, u32[]{:S(2)}) %all-to-all-start) | async-done | bytes 4128 | tf_op jit(solution)/shard_map/all_to_all | solution.py:209
  20.8 0.6 proxy_blocks.1
  21.4 0.6 %collective-permute-start.6 = (s16[64,1024]{1,0:T(8,128)(2,1)S(1)}, s16[64,1024]{1,0:T(8,128)(2,1)S(1)}, u32[]{:S(2)}, u32[]{:S(2)}) collective-permute-start(s16[64,1024]{1,0:T(8,128)(2,1)S(1)} %proxy_blocks.1), channel_id=1, source_target_pairs={{0,16},{4,20},{8,24},{12,28},{16,0},{20,4},{24,8},{28,12},{1,17},{... | collective-permute-start | bytes 393224 | tf_op jit(solution)/shard_map/ppermute | solution.py:153
  22.1 3.1 %collective-permute-done.2.refs_2_ = bf16[64,1024]{1,0:T(8,128)(2,1)S(1)} collective-permute-done((bf16[64,1024]{1,0:T(8,128)(2,1)S(1)}, bf16[64,1024]{1,0:T(8,128)(2,1)S(1)}, u32[]{:S(2)}, u32[]{:S(2)}) %collective-permute-start.2) | collective-permute-done | bytes 131104 | tf_op jit(solution)/shard_map/ppermute | solution.py:153
  25.7 3.0 %collective-permute-done.6.far_ref = s16[64,1024]{1,0:T(8,128)(2,1)S(1)} collective-permute-done((s16[64,1024]{1,0:T(8,128)(2,1)S(1)}, s16[64,1024]{1,0:T(8,128)(2,1)S(1)}, u32[]{:S(2)}, u32[]{:S(2)}) %collective-permute-start.6) | collective-permute-done | bytes 131104 | tf_op jit(solution)/shard_map/ppermute | solution.py:153
  28.8 0.9 %finish_blocks.1 = (f32[64,1024]{1,0:T(8,128)S(1)}, f32[64,128]{1,0:T(8,128)S(1)}, f32[32,1,128]{2,1,0:T(1,128)}) custom-call(s32[1,1]{1,0:T(1,128)} %bitcast.offset_ref, f32[64,1024]{1,0:T(8,128)S(1)} %owner_blocks.1.near_ref, s16[64,1024]{1,0:T(8,128)(2,1)S(1)} %collective-permute-done.6.far_ref, f32[8,128]{1,0:T(8,128)S(1)} %bitcast.50), custom_call_target="tpu_custom_call" | custom-call | tf_op jit(solution)/shard_map/finish_blocks/pallas_call | solution.py:231
  29.7 3.2 %all-to-all-start.1 = ((f32[32,1,128]{2,1,0:T(1,128)}), f32[32,1,128]{2,1,0:T(1,128)S(1)}, u32[]{:S(2)}, u32[]{:S(2)}) async-start(f32[32,1,128]{2,1,0:T(1,128)} %get-tuple-element.11), calls=%async_computation.1 | async-start | bytes 32768 | tf_op jit(solution)/shard_map/all_to_all | solution.py:248
  33.2 6.7 %all-to-all-done.1 = f32[32,1,128]{2,1,0:T(1,128)S(1)} async-done(((f32[32,1,128]{2,1,0:T(1,128)}), f32[32,1,128]{2,1,0:T(1,128)S(1)}, u32[]{:S(2)}, u32[]{:S(2)}) %all-to-all-start.1) | async-done | bytes 16416 | tf_op jit(solution)/shard_map/all_to_all | solution.py:248
  39.9 0.8 %update_blocks.1 = (bf16[64,1024]{1,0:T(8,128)(2,1)S(1)}, f32[64,1024]{1,0:T(8,128)}) custom-call(f32[32,128]{1,0:T(8,128)S(1)} %bitcast.51, f32[64,1024]{1,0:T(8,128)S(1)} %rotate_back.1.unrot_ref, bf16[64,1024]{1,0:T(8,128)(2,1)S(1)} %bitcast.46, bf16[64,1024]{1,0:T(8,128)(2,1)S(1)} %bitcast.47), custom_call_target="tpu_custom_call" | custom-call | tf_op jit(solution)/shard_map/update_blocks/pallas_call | solution.py:250
  42.6 7.0 %collective-permute-done.7 = bf16[64,1024]{1,0:T(8,128)(2,1)S(1)} collective-permute-done((bf16[64,1024]{1,0:T(8,128)(2,1)S(1)}, bf16[64,1024]{1,0:T(8,128)(2,1)S(1)}, u32[]{:S(2)}, u32[]{:S(2)}) %collective-permute-start.7) | collective-permute-done | bytes 131104 | tf_op jit(solution)/shard_map/ppermute | solution.py:153
  49.6 0.6 %collective-permute-start.12 = (bf16[64,1024]{1,0:T(8,128)(2,1)S(1)}, bf16[64,1024]{1,0:T(8,128)(2,1)S(1)}, u32[]{:S(2)}, u32[]{:S(2)}) collective-permute-start(bf16[64,1024]{1,0:T(8,128)(2,1)S(1)} %collective-permute-done.7), channel_id=1, source_target_pairs={{0,4},{4,0},{8,12},{12,8},{16,20},{20,16},{24,28},{28,24},{1,5},{5... | collective-permute-start | bytes 393224 | tf_op jit(solution)/shard_map/ppermute | solution.py:153
  50.3 1.5 %collective-permute-start.10 = (bf16[64,1024]{1,0:T(8,128)(2,1)S(1)}, bf16[64,1024]{1,0:T(8,128)(2,1)S(1)}, u32[]{:S(2)}, u32[]{:S(2)}) collective-permute-start(bf16[64,1024]{1,0:T(8,128)(2,1)S(1)} %collective-permute-done.8), channel_id=1, source_target_pairs={{0,4},{4,0},{8,12},{12,8},{16,20},{20,16},{24,28},{28,24},{1,5},{5... | collective-permute-start | bytes 393224 | tf_op jit(solution)/shard_map/ppermute | solution.py:153
  51.8 3.2 %collective-permute-done.11 = bf16[64,1024]{1,0:T(8,128)(2,1)S(1)} collective-permute-done((bf16[64,1024]{1,0:T(8,128)(2,1)S(1)}, bf16[64,1024]{1,0:T(8,128)(2,1)S(1)}, u32[]{:S(2)}, u32[]{:S(2)}) %collective-permute-start.11) | collective-permute-done | bytes 131104 | tf_op jit(solution)/shard_map/ppermute | solution.py:153
  55.0 0.6 collective-permute-start.13
  55.6 3.1 %collective-permute-done.10 = bf16[64,1024]{1,0:T(8,128)(2,1)S(1)} collective-permute-done((bf16[64,1024]{1,0:T(8,128)(2,1)S(1)}, bf16[64,1024]{1,0:T(8,128)(2,1)S(1)}, u32[]{:S(2)}, u32[]{:S(2)}) %collective-permute-start.10) | collective-permute-done | bytes 131104 | tf_op jit(solution)/shard_map/ppermute | solution.py:153
  58.9 1.8 %collective-permute-done.13 = bf16[64,1024]{1,0:T(8,128)(2,1)S(1)} collective-permute-done((bf16[64,1024]{1,0:T(8,128)(2,1)S(1)}, bf16[64,1024]{1,0:T(8,128)(2,1)S(1)}, u32[]{:S(2)}, u32[]{:S(2)}) %collective-permute-start.13) | collective-permute-done | bytes 131104 | tf_op jit(solution)/shard_map/ppermute | solution.py:153
  60.7 1.0 %copy-done.6 = bf16[8,64,1024]{2,1,0:T(8,128)(2,1)} copy-done((bf16[8,64,1024]{2,1,0:T(8,128)(2,1)}, bf16[8,64,1024]{2,1,0:T(8,128)(2,1)S(1)}, u32[]{:S(2)}) %copy-start.6) | copy-done | bytes 1048600
  (38 shorter events, 3.0 us)
Async XLA Ops:
  0.7 1.2 %copy-start = (bf16[1,1,512,1024]{3,2,1,0:T(8,128)(2,1)S(1)}, bf16[1,1,512,1024]{3,2,1,0:T(8,128)(2,1)}, u32[]{:S(2)}) copy-start(bf16[1,1,512,1024]{3,2,1,0:T(8,128)(2,1)} %param.5) | copy-start | bytes 3145732
  1.9 1.6 %copy-start.1 = (bf16[1,1,512,1024]{3,2,1,0:T(8,128)(2,1)S(1)}, bf16[1,1,512,1024]{3,2,1,0:T(8,128)(2,1)}, u32[]{:S(2)}) copy-start(bf16[1,1,512,1024]{3,2,1,0:T(8,128)(2,1)} %param.5) | copy-start | bytes 3145732
  3.5 17.3 %copy-start.2 = (bf16[256,256]{1,0:T(8,128)(2,1)S(1)}, bf16[256,256]{1,0:T(8,128)(2,1)}, u32[]{:S(2)}) copy-start(bf16[256,256]{1,0:T(8,128)(2,1)} %constant.41.clone.refs_6_.matrix_ref) | copy-start | bytes 393220
  3.6 14.3 %collective-permute-start.3 = (bf16[64,1024]{1,0:T(8,128)(2,1)S(1)}, bf16[64,1024]{1,0:T(8,128)(2,1)S(1)}, u32[]{:S(2)}, u32[]{:S(2)}) collective-permute-start(bf16[64,1024]{1,0:T(8,128)(2,1)S(1)} %get-tuple-element.19), channel_id=1, source_target_pairs={{0,4},{4,0},{8,12},{12,8},{16,20},{20,16},{24,28},{28,24},{1,5},{5... | collective-permute-start | bytes 393224 | tf_op jit(solution)/shard_map/ppermute | solution.py:153
  6.6 14.2 %collective-permute-start.4 = (bf16[64,1024]{1,0:T(8,128)(2,1)S(1)}, bf16[64,1024]{1,0:T(8,128)(2,1)S(1)}, u32[]{:S(2)}, u32[]{:S(2)}) collective-permute-start(bf16[64,1024]{1,0:T(8,128)(2,1)S(1)} %get-tuple-element.18), channel_id=1, source_target_pairs={{0,8},{4,12},{8,0},{12,4},{16,24},{20,28},{24,16},{28,20},{1,9},{5... | collective-permute-start | bytes 393224 | tf_op jit(solution)/shard_map/ppermute | solution.py:153
  8.2 12.6 %collective-permute-start.5 = (bf16[64,1024]{1,0:T(8,128)(2,1)S(1)}, bf16[64,1024]{1,0:T(8,128)(2,1)S(1)}, u32[]{:S(2)}, u32[]{:S(2)}) collective-permute-start(bf16[64,1024]{1,0:T(8,128)(2,1)S(1)} %get-tuple-element.17), channel_id=1, source_target_pairs={{0,12},{4,8},{8,4},{12,0},{16,28},{20,24},{24,20},{28,16},{1,13},{... | collective-permute-start | bytes 393224 | tf_op jit(solution)/shard_map/ppermute | solution.py:153
  8.2 12.6 %all-to-all-start = ((f32[8,1,128]{2,1,0:T(1,128)}), f32[8,1,128]{2,1,0:T(1,128)S(1)}, u32[]{:S(2)}, u32[]{:S(2)}) async-start(f32[8,1,128]{2,1,0:T(1,128)} %bitcast.8), calls=%async_computation | async-start | bytes 8192 | tf_op jit(solution)/shard_map/all_to_all | solution.py:209
  14.4 7.7 %collective-permute-start = (bf16[64,1024]{1,0:T(8,128)(2,1)S(1)}, bf16[64,1024]{1,0:T(8,128)(2,1)S(1)}, u32[]{:S(2)}, u32[]{:S(2)}) collective-permute-start(bf16[64,1024]{1,0:T(8,128)(2,1)S(1)} %get-tuple-element.23), channel_id=1, source_target_pairs={{0,4},{4,0},{8,12},{12,8},{16,20},{20,16},{24,28},{28,24},{1,5},{5... | collective-permute-start | bytes 393224 | tf_op jit(solution)/shard_map/ppermute | solution.py:153
  16.4 5.6 %collective-permute-start.1 = (bf16[64,1024]{1,0:T(8,128)(2,1)S(1)}, bf16[64,1024]{1,0:T(8,128)(2,1)S(1)}, u32[]{:S(2)}, u32[]{:S(2)}) collective-permute-start(bf16[64,1024]{1,0:T(8,128)(2,1)S(1)} %get-tuple-element.22), channel_id=1, source_target_pairs={{0,8},{4,12},{8,0},{12,4},{16,24},{20,28},{24,16},{28,20},{1,9},{5... | collective-permute-start | bytes 393224 | tf_op jit(solution)/shard_map/ppermute | solution.py:153
  17.9 2.9 %copy-start.5 = (s32[1,1024]{1,0:T(1,128)S(1)}, s32[1,1024]{1,0:T(1,128)}, u32[]{:S(2)}) copy-start(s32[1,1024]{1,0:T(1,128)} %sign_ref.1) | copy-start | bytes 12292
  17.9 7.3 %collective-permute-start.2 = (bf16[64,1024]{1,0:T(8,128)(2,1)S(1)}, bf16[64,1024]{1,0:T(8,128)(2,1)S(1)}, u32[]{:S(2)}, u32[]{:S(2)}) collective-permute-start(bf16[64,1024]{1,0:T(8,128)(2,1)S(1)} %get-tuple-element.21), channel_id=1, source_target_pairs={{0,12},{4,8},{8,4},{12,0},{16,28},{20,24},{24,20},{28,16},{1,13},{... | collective-permute-start | bytes 393224 | tf_op jit(solution)/shard_map/ppermute | solution.py:153
  21.4 7.3 %collective-permute-start.6 = (s16[64,1024]{1,0:T(8,128)(2,1)S(1)}, s16[64,1024]{1,0:T(8,128)(2,1)S(1)}, u32[]{:S(2)}, u32[]{:S(2)}) collective-permute-start(s16[64,1024]{1,0:T(8,128)(2,1)S(1)} %proxy_blocks.1), channel_id=1, source_target_pairs={{0,16},{4,20},{8,24},{12,28},{16,0},{20,4},{24,8},{28,12},{1,17},{... | collective-permute-start | bytes 393224 | tf_op jit(solution)/shard_map/ppermute | solution.py:153
  29.7 10.2 %all-to-all-start.1 = ((f32[32,1,128]{2,1,0:T(1,128)}), f32[32,1,128]{2,1,0:T(1,128)S(1)}, u32[]{:S(2)}, u32[]{:S(2)}) async-start(f32[32,1,128]{2,1,0:T(1,128)} %get-tuple-element.11), calls=%async_computation.1 | async-start | bytes 32768 | tf_op jit(solution)/shard_map/all_to_all | solution.py:248
  32.9 7.1 %copy-start.3 = (bf16[1,64,1024]{2,1,0:T(8,128)(2,1)S(1)}, bf16[1,64,1024]{2,1,0:T(8,128)(2,1)}, u32[]{:S(2)}) copy-start(bf16[1,64,1024]{2,1,0:T(8,128)(2,1)} %param.7) | copy-start | bytes 393220
  32.9 7.0 %copy-start.4 = (bf16[1,64,1024]{2,1,0:T(8,128)(2,1)S(1)}, bf16[1,64,1024]{2,1,0:T(8,128)(2,1)}, u32[]{:S(2)}) copy-start(bf16[1,64,1024]{2,1,0:T(8,128)(2,1)} %param.8) | copy-start | bytes 393220
  40.7 8.9 %collective-permute-start.7 = (bf16[64,1024]{1,0:T(8,128)(2,1)S(1)}, bf16[64,1024]{1,0:T(8,128)(2,1)S(1)}, u32[]{:S(2)}, u32[]{:S(2)}) collective-permute-start(bf16[64,1024]{1,0:T(8,128)(2,1)S(1)} %get-tuple-element.14), channel_id=1, source_target_pairs={{0,16},{4,20},{8,24},{12,28},{16,0},{20,4},{24,8},{28,12},{1,17},{... | collective-permute-start | bytes 393224 | tf_op jit(solution)/shard_map/ppermute | solution.py:153
  41.3 8.9 %collective-permute-start.8 = (bf16[64,1024]{1,0:T(8,128)(2,1)S(1)}, bf16[64,1024]{1,0:T(8,128)(2,1)S(1)}, u32[]{:S(2)}, u32[]{:S(2)}) collective-permute-start(bf16[64,1024]{1,0:T(8,128)(2,1)S(1)} %get-tuple-element.14), channel_id=1, source_target_pairs={{0,8},{4,12},{8,0},{12,4},{16,24},{20,28},{24,16},{28,20},{1,9},{5... | collective-permute-start | bytes 393224 | tf_op jit(solution)/shard_map/ppermute | solution.py:153
  41.9 9.9 %collective-permute-start.9 = (bf16[64,1024]{1,0:T(8,128)(2,1)S(1)}, bf16[64,1024]{1,0:T(8,128)(2,1)S(1)}, u32[]{:S(2)}, u32[]{:S(2)}) collective-permute-start(bf16[64,1024]{1,0:T(8,128)(2,1)S(1)} %get-tuple-element.14), channel_id=1, source_target_pairs={{0,4},{4,0},{8,12},{12,8},{16,20},{20,16},{24,28},{28,24},{1,5},{5... | collective-permute-start | bytes 393224 | tf_op jit(solution)/shard_map/ppermute | solution.py:153
  49.6 5.4 %collective-permute-start.11 = (bf16[64,1024]{1,0:T(8,128)(2,1)S(1)}, bf16[64,1024]{1,0:T(8,128)(2,1)S(1)}, u32[]{:S(2)}, u32[]{:S(2)}) collective-permute-start(bf16[64,1024]{1,0:T(8,128)(2,1)S(1)} %collective-permute-done.7), channel_id=1, source_target_pairs={{0,8},{4,12},{8,0},{12,4},{16,24},{20,28},{24,16},{28,20},{1,9},{5... | collective-permute-start | bytes 393224 | tf_op jit(solution)/shard_map/ppermute | solution.py:153
  49.6 9.2 %collective-permute-start.12 = (bf16[64,1024]{1,0:T(8,128)(2,1)S(1)}, bf16[64,1024]{1,0:T(8,128)(2,1)S(1)}, u32[]{:S(2)}, u32[]{:S(2)}) collective-permute-start(bf16[64,1024]{1,0:T(8,128)(2,1)S(1)} %collective-permute-done.7), channel_id=1, source_target_pairs={{0,4},{4,0},{8,12},{12,8},{16,20},{20,16},{24,28},{28,24},{1,5},{5... | collective-permute-start | bytes 393224 | tf_op jit(solution)/shard_map/ppermute | solution.py:153
  50.3 8.5 %collective-permute-start.10 = (bf16[64,1024]{1,0:T(8,128)(2,1)S(1)}, bf16[64,1024]{1,0:T(8,128)(2,1)S(1)}, u32[]{:S(2)}, u32[]{:S(2)}) collective-permute-start(bf16[64,1024]{1,0:T(8,128)(2,1)S(1)} %collective-permute-done.8), channel_id=1, source_target_pairs={{0,4},{4,0},{8,12},{12,8},{16,20},{20,16},{24,28},{28,24},{1,5},{5... | collective-permute-start | bytes 393224 | tf_op jit(solution)/shard_map/ppermute | solution.py:153
  55.0 5.6 %collective-permute-start.13 = (bf16[64,1024]{1,0:T(8,128)(2,1)S(1)}, bf16[64,1024]{1,0:T(8,128)(2,1)S(1)}, u32[]{:S(2)}, u32[]{:S(2)}) collective-permute-start(bf16[64,1024]{1,0:T(8,128)(2,1)S(1)} %collective-permute-done.11), channel_id=1, source_target_pairs={{0,4},{4,0},{8,12},{12,8},{16,20},{20,16},{24,28},{28,24},{1,5},{5... | collective-permute-start | bytes 393224 | tf_op jit(solution)/shard_map/ppermute | solution.py:153
  60.7 1.0 %copy-start.6 = (bf16[8,64,1024]{2,1,0:T(8,128)(2,1)}, bf16[8,64,1024]{2,1,0:T(8,128)(2,1)S(1)}, u32[]{:S(2)}) copy-start(bf16[8,64,1024]{2,1,0:T(8,128)(2,1)S(1)} %bitcast_dynamic-update-slice_fusion) | copy-start | bytes 3145732

commit v6 on v5

--- a/solution.py
+++ b/solution.py
@@ -50,13 +50,15 @@
 
 
 def sums_kernel(x_ref, sums_ref):
-    owned, width = x_ref.shape[2:]
-    rows = x_ref[...].reshape(2 * owned, width).astype(jnp.float32)
-    squares = jnp.sum(rows * rows, axis=1, keepdims=True)
+    near, owned, width = x_ref.shape[1:]
     shape = (2 * owned, 2 * owned)
     row, lane = (lax.broadcasted_iota(jnp.int32, shape, axis) for axis in (0, 1))
-    line = jnp.sum(jnp.where(row == lane, squares, 0.0), axis=0, keepdims=True)
-    sums_ref[...] = jnp.broadcast_to(line, sums_ref.shape)
+    for j in range(near):
+        rows = x_ref[:, j].reshape(2 * owned, width).astype(jnp.float32)
+        squares = jnp.sum(rows * rows, axis=1, keepdims=True)
+        line = jnp.sum(jnp.where(row == lane, squares, 0.0), axis=0, keepdims=True)
+        sums_ref[0, j] = line
+        sums_ref[1, j] = line
 
 
 def scale_rows(sums_ref, offset, owned, width, near):
@@ -196,23 +198,21 @@
         source = source.reshape(replicas, owned, width)
         return lax.dynamic_slice_in_dim(source, index, 1, 0).reshape(owned, width)
 
+    far_pieces = [swap(block_of(grads, me ^ mask ^ near), mask) for mask in range(1, near)]
     sums = pl.pallas_call(
         sums_kernel,
-        grid=(near,),
-        in_specs=[pl.BlockSpec((2, 1, owned, width), lambda j: (0, j, 0, 0))],
-        out_specs=pl.BlockSpec((2, 1, 1, 2 * owned), lambda j: (0, j, 0, 0)),
+        in_specs=[array],
         out_shape=jax.ShapeDtypeStruct((2, near, 1, 2 * owned), jnp.float32),
         compiler_params=params,
         name="sum_squares",
     )(grads.reshape(2, near, owned, width))
-    grads, sums = lax.optimization_barrier((grads, sums))
+    later, sums = lax.optimization_barrier((grads, sums))
     sums = lax.all_to_all(
         sums.reshape(replicas, 1, 2 * owned), "dp", split_axis=0, concat_axis=0, tiled=True
     ).reshape(replicas, 2 * owned)
-    far_pieces = [swap(block_of(grads, me ^ mask ^ near), mask) for mask in range(1, near)]
-    far_pieces.append(block_of(grads, me ^ near))
-    near_pieces = [swap(block_of(grads, me ^ mask), mask) for mask in range(1, near)]
-    near_pieces.append(block_of(grads, me))
+    near_pieces = [swap(block_of(later, me ^ mask), mask) for mask in range(1, near)]
+    far_pieces.append(block_of(later, me ^ near))
+    near_pieces.append(block_of(later, me))
     sent = pl.pallas_call(
         functools.partial(proxy_kernel, near, base),
         in_specs=[scalar] + [array] * (near + 3),

time: 61.9 us -> 62.2 us (level)
  local copies, waits for them, and re-layouts: 2.52 us -> 3.57 us
  Pallas kernels: 4.82 us -> 4.09 us
    reshape x1 -> x2, local copies, waits for them, and re-layouts: 0.08 us -> 1.13 us  [block_of(): return lax.dynamic_slice_in_dim(source, index, 1, 0).reshape(owned, width)]
    pallas_call x1, Pallas kernels: 1.61 us -> 0.87 us  [on_device(): pl.pallas_call(sums_kernel, in_specs=[array], out_shape=jax.ShapeDtypeStr...]
  transfers between devices with their start and end apart: 16 -> 16, of which waited for: 8 -> 8; matrix products, arithmetic and copies ran while one was open for 0% -> 0% of each run, Pallas kernels for 2% -> 4%
where the time goes in v6:
time: 62.2 us; the launch traced here: 62 us
  waiting for transfers between devices  30.8 us (50%)
  starting transfers between devices  22.7 us (36%)
  Pallas kernels  4.09 us (7%)
  local copies, waits for them, and re-layouts  3.57 us (6%)
  between operations  0.86 us (1%)
    ppermute x14, waiting for transfers between devices, swap(): return lax.ppermute(value, 'dp', [(i, i ^ mask) for i in range(size)])  21.4 us
    ppermute x14, starting transfers between devices, swap(): return lax.ppermute(value, 'dp', [(i, i ^ mask) for i in range(size)])  13.2 us
    all_to_all x1, waiting for transfers between devices, on_device(): lax.all_to_all(squares, ('dp', 'expert'), split_axis=0, concat_axis=0, ti...  6.71 us
    all_to_all x1, starting transfers between devices, on_device(): lax.all_to_all(sums.reshape(replicas, 1, 2 * owned), 'dp', split_axis=0,...  6.22 us
    all_to_all x1, starting transfers between devices, on_device(): lax.all_to_all(squares, ('dp', 'expert'), split_axis=0, concat_axis=0, ti...  3.29 us
    all_to_all x1, waiting for transfers between devices, on_device(): lax.all_to_all(sums.reshape(replicas, 1, 2 * owned), 'dp', split_axis=0,...  2.69 us
    unnamed x14, local copies, waits for them, and re-layouts  2.22 us
  transfers between devices with their start and end apart: 16, of which 8 were waited for; matrix products, arithmetic and copies ran while one was open for 0% of the time, Pallas kernels for 4%

profile of v6, /device:TPU:0, one launch (start us, length us, event | category | flops | bytes accessed | tf_op | source)
XLA Modules:
  0.0 62.0 jit_solution(8857127372430991657)
XLA Ops:
  0.7 1.1 %dynamic-slice_bitcast_fusion.1 = (bf16[64,1024]{1,0:T(8,128)(2,1)S(1)}, bf16[64,1024]{1,0:T(8,128)(2,1)S(1)}, bf16[64,1024]{1,0:T(8,128)(2,1)S(1)}) fusion(bf16[8,64,1024]{2,1,0:T(8,128)(2,1)} %bitcast.45, s32[]{:T(128)S(6)} %select_n.50, s32[]{:T(128)S(6)} %select_n.49, s32[]{:T(128)S(6)} %select_n.48), kind=kLoop, calls=%fused_computation.9 | loop fusion | bytes 786444 | tf_op jit(solution)/shard_map/reshape | solution.py:199
  1.7 3.0 %collective-permute-start.3 = (bf16[64,1024]{1,0:T(8,128)(2,1)S(1)}, bf16[64,1024]{1,0:T(8,128)(2,1)S(1)}, u32[]{:S(2)}, u32[]{:S(2)}) collective-permute-start(bf16[64,1024]{1,0:T(8,128)(2,1)S(1)} %get-tuple-element.23), channel_id=1, source_target_pairs={{0,4},{4,0},{8,12},{12,8},{16,20},{20,16},{24,28},{28,24},{1,5},{5... | collective-permute-start | bytes 393224 | tf_op jit(solution)/shard_map/ppermute | solution.py:155
  4.7 1.6 %collective-permute-start.4 = (bf16[64,1024]{1,0:T(8,128)(2,1)S(1)}, bf16[64,1024]{1,0:T(8,128)(2,1)S(1)}, u32[]{:S(2)}, u32[]{:S(2)}) collective-permute-start(bf16[64,1024]{1,0:T(8,128)(2,1)S(1)} %get-tuple-element.22), channel_id=1, source_target_pairs={{0,8},{4,12},{8,0},{12,4},{16,24},{20,28},{24,16},{28,20},{1,9},{5... | collective-permute-start | bytes 393224 | tf_op jit(solution)/shard_map/ppermute | solution.py:155
  6.3 1.2 %copy-done = bf16[1,1,512,1024]{3,2,1,0:T(8,128)(2,1)S(1)} copy-done((bf16[1,1,512,1024]{3,2,1,0:T(8,128)(2,1)S(1)}, bf16[1,1,512,1024]{3,2,1,0:T(8,128)(2,1)}, u32[]{:S(2)}) %copy-start) | copy-done | bytes 1048600
  7.5 0.9 %sum_squares.1 = f32[2,4,1,128]{3,2,1,0:T(1,128)} custom-call(bf16[2,4,64,1024]{3,2,1,0:T(8,128)(2,1)S(1)} %bitcast.46), custom_call_target="tpu_custom_call" | custom-call | tf_op jit(solution)/shard_map/sum_squares/pallas_call | solution.py:202
  8.4 6.2 %all-to-all-start = ((f32[8,1,128]{2,1,0:T(1,128)}), f32[8,1,128]{2,1,0:T(1,128)S(1)}, u32[]{:S(2)}, u32[]{:S(2)}) async-start(f32[8,1,128]{2,1,0:T(1,128)} %bitcast.8), calls=%async_computation | async-start | bytes 8192 | tf_op jit(solution)/shard_map/all_to_all | solution.py:210
  14.7 2.1 %collective-permute-start = (bf16[64,1024]{1,0:T(8,128)(2,1)S(1)}, bf16[64,1024]{1,0:T(8,128)(2,1)S(1)}, u32[]{:S(2)}, u32[]{:S(2)}) collective-permute-start(bf16[64,1024]{1,0:T(8,128)(2,1)S(1)} %get-tuple-element.20), channel_id=1, source_target_pairs={{0,4},{4,0},{8,12},{12,8},{16,20},{20,16},{24,28},{28,24},{1,5},{5... | collective-permute-start | bytes 393224 | tf_op jit(solution)/shard_map/ppermute | solution.py:155
  16.8 1.5 %collective-permute-start.1 = (bf16[64,1024]{1,0:T(8,128)(2,1)S(1)}, bf16[64,1024]{1,0:T(8,128)(2,1)S(1)}, u32[]{:S(2)}, u32[]{:S(2)}) collective-permute-start(bf16[64,1024]{1,0:T(8,128)(2,1)S(1)} %get-tuple-element.19), channel_id=1, source_target_pairs={{0,8},{4,12},{8,0},{12,4},{16,24},{20,28},{24,16},{28,20},{1,9},{5... | collective-permute-start | bytes 393224 | tf_op jit(solution)/shard_map/ppermute | solution.py:155
  18.3 2.7 %all-to-all-done = f32[8,1,128]{2,1,0:T(1,128)S(1)} async-done(((f32[8,1,128]{2,1,0:T(1,128)}), f32[8,1,128]{2,1,0:T(1,128)S(1)}, u32[]{:S(2)}, u32[]{:S(2)}) %all-to-all-start) | async-done | bytes 4128 | tf_op jit(solution)/shard_map/all_to_all | solution.py:210
  21.7 0.6 %collective-permute-start.6 = (s16[64,1024]{1,0:T(8,128)(2,1)S(1)}, s16[64,1024]{1,0:T(8,128)(2,1)S(1)}, u32[]{:S(2)}, u32[]{:S(2)}) collective-permute-start(s16[64,1024]{1,0:T(8,128)(2,1)S(1)} %proxy_blocks.1), channel_id=1, source_target_pairs={{0,16},{4,20},{8,24},{12,28},{16,0},{20,4},{24,8},{28,12},{1,17},{... | collective-permute-start | bytes 393224 | tf_op jit(solution)/shard_map/ppermute | solution.py:155
  22.3 3.2 %collective-permute-done.2.refs_2_ = bf16[64,1024]{1,0:T(8,128)(2,1)S(1)} collective-permute-done((bf16[64,1024]{1,0:T(8,128)(2,1)S(1)}, bf16[64,1024]{1,0:T(8,128)(2,1)S(1)}, u32[]{:S(2)}, u32[]{:S(2)}) %collective-permute-start.2) | collective-permute-done | bytes 131104 | tf_op jit(solution)/shard_map/ppermute | solution.py:155
  26.1 2.9 %collective-permute-done.6.far_ref = s16[64,1024]{1,0:T(8,128)(2,1)S(1)} collective-permute-done((s16[64,1024]{1,0:T(8,128)(2,1)S(1)}, s16[64,1024]{1,0:T(8,128)(2,1)S(1)}, u32[]{:S(2)}, u32[]{:S(2)}) %collective-permute-start.6) | collective-permute-done | bytes 131104 | tf_op jit(solution)/shard_map/ppermute | solution.py:155
  29.0 0.9 %finish_blocks.1 = (f32[64,1024]{1,0:T(8,128)S(1)}, f32[64,128]{1,0:T(8,128)S(1)}, f32[32,1,128]{2,1,0:T(1,128)}) custom-call(s32[1,1]{1,0:T(1,128)} %bitcast.offset_ref, f32[64,1024]{1,0:T(8,128)S(1)} %owner_blocks.1.near_ref, s16[64,1024]{1,0:T(8,128)(2,1)S(1)} %collective-permute-done.6.far_ref, f32[8,128]{1,0:T(8,128)S(1)} %bitcast.52), custom_call_target="tpu_custom_call" | custom-call | tf_op jit(solution)/shard_map/finish_blocks/pallas_call | solution.py:231
  29.9 3.3 %all-to-all-start.1 = ((f32[32,1,128]{2,1,0:T(1,128)}), f32[32,1,128]{2,1,0:T(1,128)S(1)}, u32[]{:S(2)}, u32[]{:S(2)}) async-start(f32[32,1,128]{2,1,0:T(1,128)} %get-tuple-element.11), calls=%async_computation.1 | async-start | bytes 32768 | tf_op jit(solution)/shard_map/all_to_all | solution.py:248
  33.6 6.7 %all-to-all-done.1 = f32[32,1,128]{2,1,0:T(1,128)S(1)} async-done(((f32[32,1,128]{2,1,0:T(1,128)}), f32[32,1,128]{2,1,0:T(1,128)S(1)}, u32[]{:S(2)}, u32[]{:S(2)}) %all-to-all-start.1) | async-done | bytes 16416 | tf_op jit(solution)/shard_map/all_to_all | solution.py:248
  40.3 0.8 %update_blocks.1 = (bf16[64,1024]{1,0:T(8,128)(2,1)S(1)}, f32[64,1024]{1,0:T(8,128)}) custom-call(f32[32,128]{1,0:T(8,128)S(1)} %bitcast.53, f32[64,1024]{1,0:T(8,128)S(1)} %rotate_back.1.unrot_ref, bf16[64,1024]{1,0:T(8,128)(2,1)S(1)} %bitcast.48, bf16[64,1024]{1,0:T(8,128)(2,1)S(1)} %bitcast.49), custom_call_target="tpu_custom_call" | custom-call | tf_op jit(solution)/shard_map/update_blocks/pallas_call | solution.py:250
  42.9 7.0 %collective-permute-done.7 = bf16[64,1024]{1,0:T(8,128)(2,1)S(1)} collective-permute-done((bf16[64,1024]{1,0:T(8,128)(2,1)S(1)}, bf16[64,1024]{1,0:T(8,128)(2,1)S(1)}, u32[]{:S(2)}, u32[]{:S(2)}) %collective-permute-start.7) | collective-permute-done | bytes 131104 | tf_op jit(solution)/shard_map/ppermute | solution.py:155
  50.0 0.6 %collective-permute-start.12 = (bf16[64,1024]{1,0:T(8,128)(2,1)S(1)}, bf16[64,1024]{1,0:T(8,128)(2,1)S(1)}, u32[]{:S(2)}, u32[]{:S(2)}) collective-permute-start(bf16[64,1024]{1,0:T(8,128)(2,1)S(1)} %collective-permute-done.7), channel_id=1, source_target_pairs={{0,4},{4,0},{8,12},{12,8},{16,20},{20,16},{24,28},{28,24},{1,5},{5... | collective-permute-start | bytes 393224 | tf_op jit(solution)/shard_map/ppermute | solution.py:155
  50.6 1.5 %collective-permute-start.10 = (bf16[64,1024]{1,0:T(8,128)(2,1)S(1)}, bf16[64,1024]{1,0:T(8,128)(2,1)S(1)}, u32[]{:S(2)}, u32[]{:S(2)}) collective-permute-start(bf16[64,1024]{1,0:T(8,128)(2,1)S(1)} %collective-permute-done.8), channel_id=1, source_target_pairs={{0,4},{4,0},{8,12},{12,8},{16,20},{20,16},{24,28},{28,24},{1,5},{5... | collective-permute-start | bytes 393224 | tf_op jit(solution)/shard_map/ppermute | solution.py:155
  52.1 3.2 %collective-permute-done.11 = bf16[64,1024]{1,0:T(8,128)(2,1)S(1)} collective-permute-done((bf16[64,1024]{1,0:T(8,128)(2,1)S(1)}, bf16[64,1024]{1,0:T(8,128)(2,1)S(1)}, u32[]{:S(2)}, u32[]{:S(2)}) %collective-permute-start.11) | collective-permute-done | bytes 131104 | tf_op jit(solution)/shard_map/ppermute | solution.py:155
  55.4 0.6 collective-permute-start.13
  56.0 3.1 %collective-permute-done.10 = bf16[64,1024]{1,0:T(8,128)(2,1)S(1)} collective-permute-done((bf16[64,1024]{1,0:T(8,128)(2,1)S(1)}, bf16[64,1024]{1,0:T(8,128)(2,1)S(1)}, u32[]{:S(2)}, u32[]{:S(2)}) %collective-permute-start.10) | collective-permute-done | bytes 131104 | tf_op jit(solution)/shard_map/ppermute | solution.py:155
  59.2 1.8 %collective-permute-done.13 = bf16[64,1024]{1,0:T(8,128)(2,1)S(1)} collective-permute-done((bf16[64,1024]{1,0:T(8,128)(2,1)S(1)}, bf16[64,1024]{1,0:T(8,128)(2,1)S(1)}, u32[]{:S(2)}, u32[]{:S(2)}) %collective-permute-start.13) | collective-permute-done | bytes 131104 | tf_op jit(solution)/shard_map/ppermute | solution.py:155
  61.0 1.0 %copy-done.6 = bf16[8,64,1024]{2,1,0:T(8,128)(2,1)} copy-done((bf16[8,64,1024]{2,1,0:T(8,128)(2,1)}, bf16[8,64,1024]{2,1,0:T(8,128)(2,1)S(1)}, u32[]{:S(2)}) %copy-start.6) | copy-done | bytes 1048600
  (39 shorter events, 3.6 us)
Async XLA Ops:
  1.7 16.5 %collective-permute-start.3 = (bf16[64,1024]{1,0:T(8,128)(2,1)S(1)}, bf16[64,1024]{1,0:T(8,128)(2,1)S(1)}, u32[]{:S(2)}, u32[]{:S(2)}) collective-permute-start(bf16[64,1024]{1,0:T(8,128)(2,1)S(1)} %get-tuple-element.23), channel_id=1, source_target_pairs={{0,4},{4,0},{8,12},{12,8},{16,20},{20,16},{24,28},{28,24},{1,5},{5... | collective-permute-start | bytes 393224 | tf_op jit(solution)/shard_map/ppermute | solution.py:155
  4.7 16.3 %collective-permute-start.4 = (bf16[64,1024]{1,0:T(8,128)(2,1)S(1)}, bf16[64,1024]{1,0:T(8,128)(2,1)S(1)}, u32[]{:S(2)}, u32[]{:S(2)}) collective-permute-start(bf16[64,1024]{1,0:T(8,128)(2,1)S(1)} %get-tuple-element.22), channel_id=1, source_target_pairs={{0,8},{4,12},{8,0},{12,4},{16,24},{20,28},{24,16},{28,20},{1,9},{5... | collective-permute-start | bytes 393224 | tf_op jit(solution)/shard_map/ppermute | solution.py:155
  6.3 14.7 %collective-permute-start.5 = (bf16[64,1024]{1,0:T(8,128)(2,1)S(1)}, bf16[64,1024]{1,0:T(8,128)(2,1)S(1)}, u32[]{:S(2)}, u32[]{:S(2)}) collective-permute-start(bf16[64,1024]{1,0:T(8,128)(2,1)S(1)} %get-tuple-element.21), channel_id=1, source_target_pairs={{0,12},{4,8},{8,4},{12,0},{16,28},{20,24},{24,20},{28,16},{1,13},{... | collective-permute-start | bytes 393224 | tf_op jit(solution)/shard_map/ppermute | solution.py:155
  6.3 1.2 %copy-start = (bf16[1,1,512,1024]{3,2,1,0:T(8,128)(2,1)S(1)}, bf16[1,1,512,1024]{3,2,1,0:T(8,128)(2,1)}, u32[]{:S(2)}) copy-start(bf16[1,1,512,1024]{3,2,1,0:T(8,128)(2,1)} %param.5) | copy-start | bytes 3145732
  7.5 7.1 %copy-start.1 = (bf16[1,1,512,1024]{3,2,1,0:T(8,128)(2,1)S(1)}, bf16[1,1,512,1024]{3,2,1,0:T(8,128)(2,1)}, u32[]{:S(2)}) copy-start(bf16[1,1,512,1024]{3,2,1,0:T(8,128)(2,1)} %param.5) | copy-start | bytes 3145732
  8.4 12.6 %all-to-all-start = ((f32[8,1,128]{2,1,0:T(1,128)}), f32[8,1,128]{2,1,0:T(1,128)S(1)}, u32[]{:S(2)}, u32[]{:S(2)}) async-start(f32[8,1,128]{2,1,0:T(1,128)} %bitcast.8), calls=%async_computation | async-start | bytes 8192 | tf_op jit(solution)/shard_map/all_to_all | solution.py:210
  14.6 6.4 %copy-start.2 = (bf16[256,256]{1,0:T(8,128)(2,1)S(1)}, bf16[256,256]{1,0:T(8,128)(2,1)}, u32[]{:S(2)}) copy-start(bf16[256,256]{1,0:T(8,128)(2,1)} %constant.41.clone.refs_6_.matrix_ref) | copy-start | bytes 393220
  14.7 7.6 %collective-permute-start = (bf16[64,1024]{1,0:T(8,128)(2,1)S(1)}, bf16[64,1024]{1,0:T(8,128)(2,1)S(1)}, u32[]{:S(2)}, u32[]{:S(2)}) collective-permute-start(bf16[64,1024]{1,0:T(8,128)(2,1)S(1)} %get-tuple-element.20), channel_id=1, source_target_pairs={{0,4},{4,0},{8,12},{12,8},{16,20},{20,16},{24,28},{28,24},{1,5},{5... | collective-permute-start | bytes 393224 | tf_op jit(solution)/shard_map/ppermute | solution.py:155
  16.8 5.5 %collective-permute-start.1 = (bf16[64,1024]{1,0:T(8,128)(2,1)S(1)}, bf16[64,1024]{1,0:T(8,128)(2,1)S(1)}, u32[]{:S(2)}, u32[]{:S(2)}) collective-permute-start(bf16[64,1024]{1,0:T(8,128)(2,1)S(1)} %get-tuple-element.19), channel_id=1, source_target_pairs={{0,8},{4,12},{8,0},{12,4},{16,24},{20,28},{24,16},{28,20},{1,9},{5... | collective-permute-start | bytes 393224 | tf_op jit(solution)/shard_map/ppermute | solution.py:155
  18.3 2.8 %copy-start.5 = (s32[1,1024]{1,0:T(1,128)S(1)}, s32[1,1024]{1,0:T(1,128)}, u32[]{:S(2)}) copy-start(s32[1,1024]{1,0:T(1,128)} %sign_ref.1) | copy-start | bytes 12292
  18.3 7.3 %collective-permute-start.2 = (bf16[64,1024]{1,0:T(8,128)(2,1)S(1)}, bf16[64,1024]{1,0:T(8,128)(2,1)S(1)}, u32[]{:S(2)}, u32[]{:S(2)}) collective-permute-start(bf16[64,1024]{1,0:T(8,128)(2,1)S(1)} %get-tuple-element.18), channel_id=1, source_target_pairs={{0,12},{4,8},{8,4},{12,0},{16,28},{20,24},{24,20},{28,16},{1,13},{... | collective-permute-start | bytes 393224 | tf_op jit(solution)/shard_map/ppermute | solution.py:155
  21.7 7.3 %collective-permute-start.6 = (s16[64,1024]{1,0:T(8,128)(2,1)S(1)}, s16[64,1024]{1,0:T(8,128)(2,1)S(1)}, u32[]{:S(2)}, u32[]{:S(2)}) collective-permute-start(s16[64,1024]{1,0:T(8,128)(2,1)S(1)} %proxy_blocks.1), channel_id=1, source_target_pairs={{0,16},{4,20},{8,24},{12,28},{16,0},{20,4},{24,8},{28,12},{1,17},{... | collective-permute-start | bytes 393224 | tf_op jit(solution)/shard_map/ppermute | solution.py:155
  29.9 10.4 %all-to-all-start.1 = ((f32[32,1,128]{2,1,0:T(1,128)}), f32[32,1,128]{2,1,0:T(1,128)S(1)}, u32[]{:S(2)}, u32[]{:S(2)}) async-start(f32[32,1,128]{2,1,0:T(1,128)} %get-tuple-element.11), calls=%async_computation.1 | async-start | bytes 32768 | tf_op jit(solution)/shard_map/all_to_all | solution.py:248
  33.2 7.1 %copy-start.3 = (bf16[1,64,1024]{2,1,0:T(8,128)(2,1)S(1)}, bf16[1,64,1024]{2,1,0:T(8,128)(2,1)}, u32[]{:S(2)}) copy-start(bf16[1,64,1024]{2,1,0:T(8,128)(2,1)} %param.7) | copy-start | bytes 393220
  33.2 7.0 %copy-start.4 = (bf16[1,64,1024]{2,1,0:T(8,128)(2,1)S(1)}, bf16[1,64,1024]{2,1,0:T(8,128)(2,1)}, u32[]{:S(2)}) copy-start(bf16[1,64,1024]{2,1,0:T(8,128)(2,1)} %param.8) | copy-start | bytes 393220
  41.1 8.9 %collective-permute-start.7 = (bf16[64,1024]{1,0:T(8,128)(2,1)S(1)}, bf16[64,1024]{1,0:T(8,128)(2,1)S(1)}, u32[]{:S(2)}, u32[]{:S(2)}) collective-permute-start(bf16[64,1024]{1,0:T(8,128)(2,1)S(1)} %get-tuple-element.14), channel_id=1, source_target_pairs={{0,16},{4,20},{8,24},{12,28},{16,0},{20,4},{24,8},{28,12},{1,17},{... | collective-permute-start | bytes 393224 | tf_op jit(solution)/shard_map/ppermute | solution.py:155
  41.7 8.9 %collective-permute-start.8 = (bf16[64,1024]{1,0:T(8,128)(2,1)S(1)}, bf16[64,1024]{1,0:T(8,128)(2,1)S(1)}, u32[]{:S(2)}, u32[]{:S(2)}) collective-permute-start(bf16[64,1024]{1,0:T(8,128)(2,1)S(1)} %get-tuple-element.14), channel_id=1, source_target_pairs={{0,8},{4,12},{8,0},{12,4},{16,24},{20,28},{24,16},{28,20},{1,9},{5... | collective-permute-start | bytes 393224 | tf_op jit(solution)/shard_map/ppermute | solution.py:155
  42.2 9.9 %collective-permute-start.9 = (bf16[64,1024]{1,0:T(8,128)(2,1)S(1)}, bf16[64,1024]{1,0:T(8,128)(2,1)S(1)}, u32[]{:S(2)}, u32[]{:S(2)}) collective-permute-start(bf16[64,1024]{1,0:T(8,128)(2,1)S(1)} %get-tuple-element.14), channel_id=1, source_target_pairs={{0,4},{4,0},{8,12},{12,8},{16,20},{20,16},{24,28},{28,24},{1,5},{5... | collective-permute-start | bytes 393224 | tf_op jit(solution)/shard_map/ppermute | solution.py:155
  50.0 5.4 %collective-permute-start.11 = (bf16[64,1024]{1,0:T(8,128)(2,1)S(1)}, bf16[64,1024]{1,0:T(8,128)(2,1)S(1)}, u32[]{:S(2)}, u32[]{:S(2)}) collective-permute-start(bf16[64,1024]{1,0:T(8,128)(2,1)S(1)} %collective-permute-done.7), channel_id=1, source_target_pairs={{0,8},{4,12},{8,0},{12,4},{16,24},{20,28},{24,16},{28,20},{1,9},{5... | collective-permute-start | bytes 393224 | tf_op jit(solution)/shard_map/ppermute | solution.py:155
  50.0 9.2 %collective-permute-start.12 = (bf16[64,1024]{1,0:T(8,128)(2,1)S(1)}, bf16[64,1024]{1,0:T(8,128)(2,1)S(1)}, u32[]{:S(2)}, u32[]{:S(2)}) collective-permute-start(bf16[64,1024]{1,0:T(8,128)(2,1)S(1)} %collective-permute-done.7), channel_id=1, source_target_pairs={{0,4},{4,0},{8,12},{12,8},{16,20},{20,16},{24,28},{28,24},{1,5},{5... | collective-permute-start | bytes 393224 | tf_op jit(solution)/shard_map/ppermute | solution.py:155
  50.6 8.5 %collective-permute-start.10 = (bf16[64,1024]{1,0:T(8,128)(2,1)S(1)}, bf16[64,1024]{1,0:T(8,128)(2,1)S(1)}, u32[]{:S(2)}, u32[]{:S(2)}) collective-permute-start(bf16[64,1024]{1,0:T(8,128)(2,1)S(1)} %collective-permute-done.8), channel_id=1, source_target_pairs={{0,4},{4,0},{8,12},{12,8},{16,20},{20,16},{24,28},{28,24},{1,5},{5... | collective-permute-start | bytes 393224 | tf_op jit(solution)/shard_map/ppermute | solution.py:155
  55.4 5.6 %collective-permute-start.13 = (bf16[64,1024]{1,0:T(8,128)(2,1)S(1)}, bf16[64,1024]{1,0:T(8,128)(2,1)S(1)}, u32[]{:S(2)}, u32[]{:S(2)}) collective-permute-start(bf16[64,1024]{1,0:T(8,128)(2,1)S(1)} %collective-permute-done.11), channel_id=1, source_target_pairs={{0,4},{4,0},{8,12},{12,8},{16,20},{20,16},{24,28},{28,24},{1,5},{5... | collective-permute-start | bytes 393224 | tf_op jit(solution)/shard_map/ppermute | solution.py:155
  61.0 1.0 %copy-start.6 = (bf16[8,64,1024]{2,1,0:T(8,128)(2,1)}, bf16[8,64,1024]{2,1,0:T(8,128)(2,1)S(1)}, u32[]{:S(2)}) copy-start(bf16[8,64,1024]{2,1,0:T(8,128)(2,1)S(1)} %bitcast_dynamic-update-slice_fusion) | copy-start | bytes 3145732

commit v7 on v6

--- a/solution.py
+++ b/solution.py
@@ -157,26 +157,30 @@
 
 def gather_blocks(block, replicas):
     x_count = 1 << ((replicas.bit_length() - 1) // 2)
-    near = max(replicas // 2, 1)
+    near = replicas // 2
     me = lax.axis_index("dp")
-    pieces = {0: block}
-
-    def spread(start):
+    owned, width = block.shape
+    parts = 2 if owned % 32 == 0 else 1
+    rows = owned // parts
+    pieces = []
+
+    def spread(start, piece, row):
+        pieces.append((start, row, piece))
+        along = {0: piece}
         for z in range(x_count, near, x_count):
-            pieces[start + z] = swap(pieces[start], z)
+            along[z] = swap(piece, z)
+            pieces.append((start + z, row, along[z]))
         for z in range(0, near, x_count):
-            for x in range(1, min(x_count, near)):
-                pieces[start + z + x] = swap(pieces[start + z], x)
-
-    if replicas > 1:
-        pieces[near] = swap(block, near)
-    spread(0)
-    if replicas > 1:
-        spread(near)
-    owned, width = block.shape
+            for x in range(1, x_count):
+                pieces.append((start + z + x, row, swap(along[z], x)))
+
+    across = [swap(block[p * rows : (p + 1) * rows], near) for p in range(parts)]
+    spread(0, block, 0)
+    for p, piece in enumerate(across):
+        spread(near, piece, p * rows)
     out = jnp.zeros((replicas, owned, width), block.dtype)
-    for mask, piece in pieces.items():
-        out = lax.dynamic_update_slice(out, piece[None], (me ^ mask, 0, 0))
+    for mask, row, piece in pieces:
+        out = lax.dynamic_update_slice(out, piece[None], (me ^ mask, row, 0))
     return out.reshape(1, replicas * owned, width)
 
 

time: 62.2 us -> 61.8 us (level)
  waiting for transfers between devices: 30.8 us -> 22.9 us
  starting transfers between devices: 22.7 us -> 30 us
    ppermute x14 -> x18, waiting for transfers between devices: 21.4 us -> 13.5 us  [swap(): return lax.ppermute(value, 'dp', [(i, i ^ mask) for i in range(size)])]
    ppermute x14 -> x18, starting transfers between devices: 13.2 us -> 20.5 us  [swap(): return lax.ppermute(value, 'dp', [(i, i ^ mask) for i in range(size)])]
  transfers between devices with their start and end apart: 16 -> 20, of which waited for: 8 -> 8; matrix products, arithmetic and copies ran while one was open for 0% -> 1% of each run, Pallas kernels for 4% -> 4%
where the time goes in v7:
time: 61.8 us; the launch traced here: 61.5 us
  starting transfers between devices  30 us (49%)
  waiting for transfers between devices  22.9 us (37%)
  Pallas kernels  4.09 us (7%)
  local copies, waits for them, and re-layouts  3.61 us (6%)
  between operations  0.89 us (1%)
    ppermute x18, starting transfers between devices, swap(): return lax.ppermute(value, 'dp', [(i, i ^ mask) for i in range(size)])  20.5 us
    ppermute x18, waiting for transfers between devices, swap(): return lax.ppermute(value, 'dp', [(i, i ^ mask) for i in range(size)])  13.5 us
    all_to_all x1, waiting for transfers between devices, on_device(): lax.all_to_all(squares, ('dp', 'expert'), split_axis=0, concat_axis=0, ti...  6.71 us
    all_to_all x1, starting transfers between devices, on_device(): lax.all_to_all(sums.reshape(replicas, 1, 2 * owned), 'dp', split_axis=0,...  6.22 us
    all_to_all x1, starting transfers between devices, on_device(): lax.all_to_all(squares, ('dp', 'expert'), split_axis=0, concat_axis=0, ti...  3.29 us
    all_to_all x1, waiting for transfers between devices, on_device(): lax.all_to_all(sums.reshape(replicas, 1, 2 * owned), 'dp', split_axis=0,...  2.69 us
    unnamed x14, local copies, waits for them, and re-layouts  2.22 us
  transfers between devices with their start and end apart: 20, of which 8 were waited for; matrix products, arithmetic and copies ran while one was open for 1% of the time, Pallas kernels for 4%

profile of v7, /device:TPU:0, one launch (start us, length us, event | category | flops | bytes accessed | tf_op | source)
XLA Modules:
  0.0 61.5 jit_solution(6314455640977102825)
XLA Ops:
  0.7 1.1 %dynamic-slice_bitcast_fusion.1 = (bf16[64,1024]{1,0:T(8,128)(2,1)S(1)}, bf16[64,1024]{1,0:T(8,128)(2,1)S(1)}, bf16[64,1024]{1,0:T(8,128)(2,1)S(1)}) fusion(bf16[8,64,1024]{2,1,0:T(8,128)(2,1)} %bitcast.53, s32[]{:T(128)S(6)} %select_n.54, s32[]{:T(128)S(6)} %select_n.53, s32[]{:T(128)S(6)} %select_n.52), kind=kLoop, calls=%fused_computation.5 | loop fusion | bytes 786444 | tf_op jit(solution)/shard_map/reshape | solution.py:203
  1.7 3.0 %collective-permute-start.3 = (bf16[64,1024]{1,0:T(8,128)(2,1)S(1)}, bf16[64,1024]{1,0:T(8,128)(2,1)S(1)}, u32[]{:S(2)}, u32[]{:S(2)}) collective-permute-start(bf16[64,1024]{1,0:T(8,128)(2,1)S(1)} %get-tuple-element.23), channel_id=1, source_target_pairs={{0,4},{4,0},{8,12},{12,8},{16,20},{20,16},{24,28},{28,24},{1,5},{5... | collective-permute-start | bytes 393224 | tf_op jit(solution)/shard_map/ppermute | solution.py:155
  4.7 1.6 %collective-permute-start.4 = (bf16[64,1024]{1,0:T(8,128)(2,1)S(1)}, bf16[64,1024]{1,0:T(8,128)(2,1)S(1)}, u32[]{:S(2)}, u32[]{:S(2)}) collective-permute-start(bf16[64,1024]{1,0:T(8,128)(2,1)S(1)} %get-tuple-element.22), channel_id=1, source_target_pairs={{0,8},{4,12},{8,0},{12,4},{16,24},{20,28},{24,16},{28,20},{1,9},{5... | collective-permute-start | bytes 393224 | tf_op jit(solution)/shard_map/ppermute | solution.py:155
  6.3 1.2 %copy-done = bf16[1,1,512,1024]{3,2,1,0:T(8,128)(2,1)S(1)} copy-done((bf16[1,1,512,1024]{3,2,1,0:T(8,128)(2,1)S(1)}, bf16[1,1,512,1024]{3,2,1,0:T(8,128)(2,1)}, u32[]{:S(2)}) %copy-start) | copy-done | bytes 1048600
  7.5 0.9 %sum_squares.1 = f32[2,4,1,128]{3,2,1,0:T(1,128)} custom-call(bf16[2,4,64,1024]{3,2,1,0:T(8,128)(2,1)S(1)} %bitcast.54), custom_call_target="tpu_custom_call" | custom-call | tf_op jit(solution)/shard_map/sum_squares/pallas_call | solution.py:206
  8.4 6.2 %all-to-all-start = ((f32[8,1,128]{2,1,0:T(1,128)}), f32[8,1,128]{2,1,0:T(1,128)S(1)}, u32[]{:S(2)}, u32[]{:S(2)}) async-start(f32[8,1,128]{2,1,0:T(1,128)} %bitcast.8), calls=%async_computation | async-start | bytes 8192 | tf_op jit(solution)/shard_map/all_to_all | solution.py:214
  14.7 2.1 %collective-permute-start = (bf16[64,1024]{1,0:T(8,128)(2,1)S(1)}, bf16[64,1024]{1,0:T(8,128)(2,1)S(1)}, u32[]{:S(2)}, u32[]{:S(2)}) collective-permute-start(bf16[64,1024]{1,0:T(8,128)(2,1)S(1)} %get-tuple-element.20), channel_id=1, source_target_pairs={{0,4},{4,0},{8,12},{12,8},{16,20},{20,16},{24,28},{28,24},{1,5},{5... | collective-permute-start | bytes 393224 | tf_op jit(solution)/shard_map/ppermute | solution.py:155
  16.8 1.5 %collective-permute-start.1 = (bf16[64,1024]{1,0:T(8,128)(2,1)S(1)}, bf16[64,1024]{1,0:T(8,128)(2,1)S(1)}, u32[]{:S(2)}, u32[]{:S(2)}) collective-permute-start(bf16[64,1024]{1,0:T(8,128)(2,1)S(1)} %get-tuple-element.19), channel_id=1, source_target_pairs={{0,8},{4,12},{8,0},{12,4},{16,24},{20,28},{24,16},{28,20},{1,9},{5... | collective-permute-start | bytes 393224 | tf_op jit(solution)/shard_map/ppermute | solution.py:155
  18.3 2.7 %all-to-all-done = f32[8,1,128]{2,1,0:T(1,128)S(1)} async-done(((f32[8,1,128]{2,1,0:T(1,128)}), f32[8,1,128]{2,1,0:T(1,128)S(1)}, u32[]{:S(2)}, u32[]{:S(2)}) %all-to-all-start) | async-done | bytes 4128 | tf_op jit(solution)/shard_map/all_to_all | solution.py:214
  22.3 3.2 %collective-permute-done.2.refs_2_ = bf16[64,1024]{1,0:T(8,128)(2,1)S(1)} collective-permute-done((bf16[64,1024]{1,0:T(8,128)(2,1)S(1)}, bf16[64,1024]{1,0:T(8,128)(2,1)S(1)}, u32[]{:S(2)}, u32[]{:S(2)}) %collective-permute-start.2) | collective-permute-done | bytes 131104 | tf_op jit(solution)/shard_map/ppermute | solution.py:155
  26.1 2.9 %collective-permute-done.6.far_ref = s16[64,1024]{1,0:T(8,128)(2,1)S(1)} collective-permute-done((s16[64,1024]{1,0:T(8,128)(2,1)S(1)}, s16[64,1024]{1,0:T(8,128)(2,1)S(1)}, u32[]{:S(2)}, u32[]{:S(2)}) %collective-permute-start.6) | collective-permute-done | bytes 131104 | tf_op jit(solution)/shard_map/ppermute | solution.py:155
  29.0 0.9 %finish_blocks.1 = (f32[64,1024]{1,0:T(8,128)S(1)}, f32[64,128]{1,0:T(8,128)S(1)}, f32[32,1,128]{2,1,0:T(1,128)}) custom-call(s32[1,1]{1,0:T(1,128)} %bitcast.offset_ref, f32[64,1024]{1,0:T(8,128)S(1)} %owner_blocks.1.near_ref, s16[64,1024]{1,0:T(8,128)(2,1)S(1)} %collective-permute-done.6.far_ref, f32[8,128]{1,0:T(8,128)S(1)} %bitcast.60), custom_call_target="tpu_custom_call" | custom-call | tf_op jit(solution)/shard_map/finish_blocks/pallas_call | solution.py:235
  29.9 3.3 %all-to-all-start.1 = ((f32[32,1,128]{2,1,0:T(1,128)}), f32[32,1,128]{2,1,0:T(1,128)S(1)}, u32[]{:S(2)}, u32[]{:S(2)}) async-start(f32[32,1,128]{2,1,0:T(1,128)} %get-tuple-element.11), calls=%async_computation.1 | async-start | bytes 32768 | tf_op jit(solution)/shard_map/all_to_all | solution.py:252
  33.6 6.7 %all-to-all-done.1 = f32[32,1,128]{2,1,0:T(1,128)S(1)} async-done(((f32[32,1,128]{2,1,0:T(1,128)}), f32[32,1,128]{2,1,0:T(1,128)S(1)}, u32[]{:S(2)}, u32[]{:S(2)}) %all-to-all-start.1) | async-done | bytes 16416 | tf_op jit(solution)/shard_map/all_to_all | solution.py:252
  40.3 0.8 %update_blocks.1 = (bf16[64,1024]{1,0:T(8,128)(2,1)S(1)}, f32[64,1024]{1,0:T(8,128)}) custom-call(f32[32,128]{1,0:T(8,128)S(1)} %bitcast.61, f32[64,1024]{1,0:T(8,128)S(1)} %rotate_back.1.unrot_ref, bf16[64,1024]{1,0:T(8,128)(2,1)S(1)} %bitcast.56, bf16[64,1024]{1,0:T(8,128)(2,1)S(1)} %bitcast.57), custom_call_target="tpu_custom_call" | custom-call | tf_op jit(solution)/shard_map/update_blocks/pallas_call | solution.py:254
  42.8 2.4 %collective-permute-start.14 = (bf16[32,1024]{1,0:T(8,128)(2,1)S(1)}, bf16[32,1024]{1,0:T(8,128)(2,1)S(1)}, u32[]{:S(2)}, u32[]{:S(2)}) collective-permute-start(bf16[32,1024]{1,0:T(8,128)(2,1)S(1)} %get-tuple-element.24), channel_id=1, source_target_pairs={{0,16},{4,20},{8,24},{12,28},{16,0},{20,4},{24,8},{28,12},{1,17},{... | collective-permute-start | bytes 196616 | tf_op jit(solution)/shard_map/ppermute | solution.py:155
  45.4 4.6 %collective-permute-done.10 = bf16[32,1024]{1,0:T(8,128)(2,1)S(1)} collective-permute-done((bf16[32,1024]{1,0:T(8,128)(2,1)S(1)}, bf16[32,1024]{1,0:T(8,128)(2,1)S(1)}, u32[]{:S(2)}, u32[]{:S(2)}) %collective-permute-start.10) | collective-permute-done | bytes 65568 | tf_op jit(solution)/shard_map/ppermute | solution.py:155
  50.0 1.4 %collective-permute-start.12 = (bf16[32,1024]{1,0:T(8,128)(2,1)S(1)}, bf16[32,1024]{1,0:T(8,128)(2,1)S(1)}, u32[]{:S(2)}, u32[]{:S(2)}) collective-permute-start(bf16[32,1024]{1,0:T(8,128)(2,1)S(1)} %collective-permute-done.10), channel_id=1, source_target_pairs={{0,4},{4,0},{8,12},{12,8},{16,20},{20,16},{24,28},{28,24},{1,5},{5... | collective-permute-start | bytes 196616 | tf_op jit(solution)/shard_map/ppermute | solution.py:155
  51.4 2.0 %collective-permute-start.15 = (bf16[32,1024]{1,0:T(8,128)(2,1)S(1)}, bf16[32,1024]{1,0:T(8,128)(2,1)S(1)}, u32[]{:S(2)}, u32[]{:S(2)}) collective-permute-start(bf16[32,1024]{1,0:T(8,128)(2,1)S(1)} %collective-permute-done.14), channel_id=1, source_target_pairs={{0,8},{4,12},{8,0},{12,4},{16,24},{20,28},{24,16},{28,20},{1,9},{5... | collective-permute-start | bytes 196616 | tf_op jit(solution)/shard_map/ppermute | solution.py:155
  54.1 1.5 %collective-permute-start.9 = (bf16[64,1024]{1,0:T(8,128)(2,1)S(1)}, bf16[64,1024]{1,0:T(8,128)(2,1)S(1)}, u32[]{:S(2)}, u32[]{:S(2)}) collective-permute-start(bf16[64,1024]{1,0:T(8,128)(2,1)S(1)} %collective-permute-done.7), channel_id=1, source_target_pairs={{0,4},{4,0},{8,12},{12,8},{16,20},{20,16},{24,28},{28,24},{1,5},{5... | collective-permute-start | bytes 393224 | tf_op jit(solution)/shard_map/ppermute | solution.py:155
  56.2 1.4 %collective-permute-start.17 = (bf16[32,1024]{1,0:T(8,128)(2,1)S(1)}, bf16[32,1024]{1,0:T(8,128)(2,1)S(1)}, u32[]{:S(2)}, u32[]{:S(2)}) collective-permute-start(bf16[32,1024]{1,0:T(8,128)(2,1)S(1)} %collective-permute-done.15), channel_id=1, source_target_pairs={{0,4},{4,0},{8,12},{12,8},{16,20},{20,16},{24,28},{28,24},{1,5},{5... | collective-permute-start | bytes 196616 | tf_op jit(solution)/shard_map/ppermute | solution.py:155
  57.6 1.5 %collective-permute-done.9 = bf16[64,1024]{1,0:T(8,128)(2,1)S(1)} collective-permute-done((bf16[64,1024]{1,0:T(8,128)(2,1)S(1)}, bf16[64,1024]{1,0:T(8,128)(2,1)S(1)}, u32[]{:S(2)}, u32[]{:S(2)}) %collective-permute-start.9) | collective-permute-done | bytes 131104 | tf_op jit(solution)/shard_map/ppermute | solution.py:155
  59.2 0.6 %collective-permute-done.13 = bf16[32,1024]{1,0:T(8,128)(2,1)S(1)} collective-permute-done((bf16[32,1024]{1,0:T(8,128)(2,1)S(1)}, bf16[32,1024]{1,0:T(8,128)(2,1)S(1)}, u32[]{:S(2)}, u32[]{:S(2)}) %collective-permute-start.13) | collective-permute-done | bytes 65568 | tf_op jit(solution)/shard_map/ppermute | solution.py:155
  60.6 1.0 %copy-done.6 = bf16[8,64,1024]{2,1,0:T(8,128)(2,1)} copy-done((bf16[8,64,1024]{2,1,0:T(8,128)(2,1)}, bf16[8,64,1024]{2,1,0:T(8,128)(2,1)S(1)}, u32[]{:S(2)}) %copy-start.6) | copy-done | bytes 1048600
  (52 shorter events, 6.1 us)
Async XLA Ops:
  1.7 16.5 %collective-permute-start.3 = (bf16[64,1024]{1,0:T(8,128)(2,1)S(1)}, bf16[64,1024]{1,0:T(8,128)(2,1)S(1)}, u32[]{:S(2)}, u32[]{:S(2)}) collective-permute-start(bf16[64,1024]{1,0:T(8,128)(2,1)S(1)} %get-tuple-element.23), channel_id=1, source_target_pairs={{0,4},{4,0},{8,12},{12,8},{16,20},{20,16},{24,28},{28,24},{1,5},{5... | collective-permute-start | bytes 393224 | tf_op jit(solution)/shard_map/ppermute | solution.py:155
  4.7 16.3 %collective-permute-start.4 = (bf16[64,1024]{1,0:T(8,128)(2,1)S(1)}, bf16[64,1024]{1,0:T(8,128)(2,1)S(1)}, u32[]{:S(2)}, u32[]{:S(2)}) collective-permute-start(bf16[64,1024]{1,0:T(8,128)(2,1)S(1)} %get-tuple-element.22), channel_id=1, source_target_pairs={{0,8},{4,12},{8,0},{12,4},{16,24},{20,28},{24,16},{28,20},{1,9},{5... | collective-permute-start | bytes 393224 | tf_op jit(solution)/shard_map/ppermute | solution.py:155
  6.3 14.7 %collective-permute-start.5 = (bf16[64,1024]{1,0:T(8,128)(2,1)S(1)}, bf16[64,1024]{1,0:T(8,128)(2,1)S(1)}, u32[]{:S(2)}, u32[]{:S(2)}) collective-permute-start(bf16[64,1024]{1,0:T(8,128)(2,1)S(1)} %get-tuple-element.21), channel_id=1, source_target_pairs={{0,12},{4,8},{8,4},{12,0},{16,28},{20,24},{24,20},{28,16},{1,13},{... | collective-permute-start | bytes 393224 | tf_op jit(solution)/shard_map/ppermute | solution.py:155
  7.5 7.1 %copy-start.1 = (bf16[1,1,512,1024]{3,2,1,0:T(8,128)(2,1)S(1)}, bf16[1,1,512,1024]{3,2,1,0:T(8,128)(2,1)}, u32[]{:S(2)}) copy-start(bf16[1,1,512,1024]{3,2,1,0:T(8,128)(2,1)} %param.5) | copy-start | bytes 3145732
  8.4 12.6 %all-to-all-start = ((f32[8,1,128]{2,1,0:T(1,128)}), f32[8,1,128]{2,1,0:T(1,128)S(1)}, u32[]{:S(2)}, u32[]{:S(2)}) async-start(f32[8,1,128]{2,1,0:T(1,128)} %bitcast.8), calls=%async_computation | async-start | bytes 8192 | tf_op jit(solution)/shard_map/all_to_all | solution.py:214
  14.6 6.4 %copy-start.2 = (bf16[256,256]{1,0:T(8,128)(2,1)S(1)}, bf16[256,256]{1,0:T(8,128)(2,1)}, u32[]{:S(2)}) copy-start(bf16[256,256]{1,0:T(8,128)(2,1)} %constant.43.clone.refs_6_.matrix_ref) | copy-start | bytes 393220
  14.7 7.6 %collective-permute-start = (bf16[64,1024]{1,0:T(8,128)(2,1)S(1)}, bf16[64,1024]{1,0:T(8,128)(2,1)S(1)}, u32[]{:S(2)}, u32[]{:S(2)}) collective-permute-start(bf16[64,1024]{1,0:T(8,128)(2,1)S(1)} %get-tuple-element.20), channel_id=1, source_target_pairs={{0,4},{4,0},{8,12},{12,8},{16,20},{20,16},{24,28},{28,24},{1,5},{5... | collective-permute-start | bytes 393224 | tf_op jit(solution)/shard_map/ppermute | solution.py:155
  16.8 5.5 %collective-permute-start.1 = (bf16[64,1024]{1,0:T(8,128)(2,1)S(1)}, bf16[64,1024]{1,0:T(8,128)(2,1)S(1)}, u32[]{:S(2)}, u32[]{:S(2)}) collective-permute-start(bf16[64,1024]{1,0:T(8,128)(2,1)S(1)} %get-tuple-element.19), channel_id=1, source_target_pairs={{0,8},{4,12},{8,0},{12,4},{16,24},{20,28},{24,16},{28,20},{1,9},{5... | collective-permute-start | bytes 393224 | tf_op jit(solution)/shard_map/ppermute | solution.py:155
  18.3 7.3 %collective-permute-start.2 = (bf16[64,1024]{1,0:T(8,128)(2,1)S(1)}, bf16[64,1024]{1,0:T(8,128)(2,1)S(1)}, u32[]{:S(2)}, u32[]{:S(2)}) collective-permute-start(bf16[64,1024]{1,0:T(8,128)(2,1)S(1)} %get-tuple-element.18), channel_id=1, source_target_pairs={{0,12},{4,8},{8,4},{12,0},{16,28},{20,24},{24,20},{28,16},{1,13},{... | collective-permute-start | bytes 393224 | tf_op jit(solution)/shard_map/ppermute | solution.py:155
  21.7 7.3 %collective-permute-start.6 = (s16[64,1024]{1,0:T(8,128)(2,1)S(1)}, s16[64,1024]{1,0:T(8,128)(2,1)S(1)}, u32[]{:S(2)}, u32[]{:S(2)}) collective-permute-start(s16[64,1024]{1,0:T(8,128)(2,1)S(1)} %proxy_blocks.1), channel_id=1, source_target_pairs={{0,16},{4,20},{8,24},{12,28},{16,0},{20,4},{24,8},{28,12},{1,17},{... | collective-permute-start | bytes 393224 | tf_op jit(solution)/shard_map/ppermute | solution.py:155
  29.9 10.4 %all-to-all-start.1 = ((f32[32,1,128]{2,1,0:T(1,128)}), f32[32,1,128]{2,1,0:T(1,128)S(1)}, u32[]{:S(2)}, u32[]{:S(2)}) async-start(f32[32,1,128]{2,1,0:T(1,128)} %get-tuple-element.11), calls=%async_computation.1 | async-start | bytes 32768 | tf_op jit(solution)/shard_map/all_to_all | solution.py:252
  33.2 7.1 %copy-start.3 = (bf16[1,64,1024]{2,1,0:T(8,128)(2,1)S(1)}, bf16[1,64,1024]{2,1,0:T(8,128)(2,1)}, u32[]{:S(2)}) copy-start(bf16[1,64,1024]{2,1,0:T(8,128)(2,1)} %param.7) | copy-start | bytes 393220
  33.2 7.0 %copy-start.4 = (bf16[1,64,1024]{2,1,0:T(8,128)(2,1)S(1)}, bf16[1,64,1024]{2,1,0:T(8,128)(2,1)}, u32[]{:S(2)}) copy-start(bf16[1,64,1024]{2,1,0:T(8,128)(2,1)} %param.8) | copy-start | bytes 393220
  41.1 12.3 %collective-permute-start.7 = (bf16[64,1024]{1,0:T(8,128)(2,1)S(1)}, bf16[64,1024]{1,0:T(8,128)(2,1)S(1)}, u32[]{:S(2)}, u32[]{:S(2)}) collective-permute-start(bf16[64,1024]{1,0:T(8,128)(2,1)S(1)} %get-tuple-element.14), channel_id=1, source_target_pairs={{0,8},{4,12},{8,0},{12,4},{16,24},{20,28},{24,16},{28,20},{1,9},{5... | collective-permute-start | bytes 393224 | tf_op jit(solution)/shard_map/ppermute | solution.py:155
  41.7 12.4 %collective-permute-start.8 = (bf16[64,1024]{1,0:T(8,128)(2,1)S(1)}, bf16[64,1024]{1,0:T(8,128)(2,1)S(1)}, u32[]{:S(2)}, u32[]{:S(2)}) collective-permute-start(bf16[64,1024]{1,0:T(8,128)(2,1)S(1)} %get-tuple-element.14), channel_id=1, source_target_pairs={{0,4},{4,0},{8,12},{12,8},{16,20},{20,16},{24,28},{28,24},{1,5},{5... | collective-permute-start | bytes 393224 | tf_op jit(solution)/shard_map/ppermute | solution.py:155
  42.3 7.7 %collective-permute-start.10 = (bf16[32,1024]{1,0:T(8,128)(2,1)S(1)}, bf16[32,1024]{1,0:T(8,128)(2,1)S(1)}, u32[]{:S(2)}, u32[]{:S(2)}) collective-permute-start(bf16[32,1024]{1,0:T(8,128)(2,1)S(1)} %get-tuple-element.25), channel_id=1, source_target_pairs={{0,16},{4,20},{8,24},{12,28},{16,0},{20,4},{24,8},{28,12},{1,17},{... | collective-permute-start | bytes 196616 | tf_op jit(solution)/shard_map/ppermute | solution.py:155
  42.8 8.6 %collective-permute-start.14 = (bf16[32,1024]{1,0:T(8,128)(2,1)S(1)}, bf16[32,1024]{1,0:T(8,128)(2,1)S(1)}, u32[]{:S(2)}, u32[]{:S(2)}) collective-permute-start(bf16[32,1024]{1,0:T(8,128)(2,1)S(1)} %get-tuple-element.24), channel_id=1, source_target_pairs={{0,16},{4,20},{8,24},{12,28},{16,0},{20,4},{24,8},{28,12},{1,17},{... | collective-permute-start | bytes 196616 | tf_op jit(solution)/shard_map/ppermute | solution.py:155
  50.0 5.6 %collective-permute-start.11 = (bf16[32,1024]{1,0:T(8,128)(2,1)S(1)}, bf16[32,1024]{1,0:T(8,128)(2,1)S(1)}, u32[]{:S(2)}, u32[]{:S(2)}) collective-permute-start(bf16[32,1024]{1,0:T(8,128)(2,1)S(1)} %collective-permute-done.10), channel_id=1, source_target_pairs={{0,8},{4,12},{8,0},{12,4},{16,24},{20,28},{24,16},{28,20},{1,9},{5... | collective-permute-start | bytes 196616 | tf_op jit(solution)/shard_map/ppermute | solution.py:155
  50.0 9.2 %collective-permute-start.12 = (bf16[32,1024]{1,0:T(8,128)(2,1)S(1)}, bf16[32,1024]{1,0:T(8,128)(2,1)S(1)}, u32[]{:S(2)}, u32[]{:S(2)}) collective-permute-start(bf16[32,1024]{1,0:T(8,128)(2,1)S(1)} %collective-permute-done.10), channel_id=1, source_target_pairs={{0,4},{4,0},{8,12},{12,8},{16,20},{20,16},{24,28},{28,24},{1,5},{5... | collective-permute-start | bytes 196616 | tf_op jit(solution)/shard_map/ppermute | solution.py:155
  51.4 4.7 %collective-permute-start.15 = (bf16[32,1024]{1,0:T(8,128)(2,1)S(1)}, bf16[32,1024]{1,0:T(8,128)(2,1)S(1)}, u32[]{:S(2)}, u32[]{:S(2)}) collective-permute-start(bf16[32,1024]{1,0:T(8,128)(2,1)S(1)} %collective-permute-done.14), channel_id=1, source_target_pairs={{0,8},{4,12},{8,0},{12,4},{16,24},{20,28},{24,16},{28,20},{1,9},{5... | collective-permute-start | bytes 196616 | tf_op jit(solution)/shard_map/ppermute | solution.py:155
  53.5 6.4 %collective-permute-start.16 = (bf16[32,1024]{1,0:T(8,128)(2,1)S(1)}, bf16[32,1024]{1,0:T(8,128)(2,1)S(1)}, u32[]{:S(2)}, u32[]{:S(2)}) collective-permute-start(bf16[32,1024]{1,0:T(8,128)(2,1)S(1)} %collective-permute-done.14), channel_id=1, source_target_pairs={{0,4},{4,0},{8,12},{12,8},{16,20},{20,16},{24,28},{28,24},{1,5},{5... | collective-permute-start | bytes 196616 | tf_op jit(solution)/shard_map/ppermute | solution.py:155
  54.1 5.1 %collective-permute-start.9 = (bf16[64,1024]{1,0:T(8,128)(2,1)S(1)}, bf16[64,1024]{1,0:T(8,128)(2,1)S(1)}, u32[]{:S(2)}, u32[]{:S(2)}) collective-permute-start(bf16[64,1024]{1,0:T(8,128)(2,1)S(1)} %collective-permute-done.7), channel_id=1, source_target_pairs={{0,4},{4,0},{8,12},{12,8},{16,20},{20,16},{24,28},{28,24},{1,5},{5... | collective-permute-start | bytes 393224 | tf_op jit(solution)/shard_map/ppermute | solution.py:155
  55.6 4.3 %collective-permute-start.13 = (bf16[32,1024]{1,0:T(8,128)(2,1)S(1)}, bf16[32,1024]{1,0:T(8,128)(2,1)S(1)}, u32[]{:S(2)}, u32[]{:S(2)}) collective-permute-start(bf16[32,1024]{1,0:T(8,128)(2,1)S(1)} %collective-permute-done.11), channel_id=1, source_target_pairs={{0,4},{4,0},{8,12},{12,8},{16,20},{20,16},{24,28},{28,24},{1,5},{5... | collective-permute-start | bytes 196616 | tf_op jit(solution)/shard_map/ppermute | solution.py:155
  56.2 4.4 %collective-permute-start.17 = (bf16[32,1024]{1,0:T(8,128)(2,1)S(1)}, bf16[32,1024]{1,0:T(8,128)(2,1)S(1)}, u32[]{:S(2)}, u32[]{:S(2)}) collective-permute-start(bf16[32,1024]{1,0:T(8,128)(2,1)S(1)} %collective-permute-done.15), channel_id=1, source_target_pairs={{0,4},{4,0},{8,12},{12,8},{16,20},{20,16},{24,28},{28,24},{1,5},{5... | collective-permute-start | bytes 196616 | tf_op jit(solution)/shard_map/ppermute | solution.py:155
  (3 other events, 5.0 us)

commit v8 on v7

--- a/solution.py
+++ b/solution.py
@@ -75,14 +75,14 @@
     return scale, step
 
 
-def add_levels(pieces, scale, sign_ref, matrix_ref, base):
-    width = pieces[0].shape[1]
+def add_levels(pieces, half, scale, sign_ref, matrix_ref, base):
+    width = pieces[0].shape[2]
     signs = sign_ref[...].astype(jnp.float32).astype(jnp.bfloat16)
     matrix = matrix_ref[...]
     inverse = (1.0 / math.sqrt(width)) / scale
     totals = None
     for piece in pieces:
-        groups = rotate_groups([piece[...] * signs], matrix, base)
+        groups = rotate_groups([piece[half] * signs], matrix, base)
         levels = [
             jnp.clip(group * inverse, -clamp_level, clamp_level)
             .astype(jnp.bfloat16)
@@ -93,30 +93,32 @@
     return totals
 
 
-def proxy_kernel(near, base, offset_ref, *refs):
+def proxy_kernel(near, base, half_ref, *refs):
     pieces, (sums_ref, sign_ref, matrix_ref, sent_ref) = refs[:near], refs[near:]
     owned, width = sent_ref.shape
-    scale, step = scale_rows(sums_ref, owned - offset_ref[0, 0], owned, width, near)
-    totals = add_levels(pieces, scale, sign_ref, matrix_ref, base)
+    half = 1 - half_ref[0, 0]
+    scale, step = scale_rows(sums_ref, half * owned, owned, width, near)
+    totals = add_levels(pieces, half, scale, sign_ref, matrix_ref, base)
     for g, total in enumerate(totals):
         value = jnp.clip(jnp.round(total / step), -32767.0, 32767.0)
         sent_ref[:, g * base : (g + 1) * base] = value.astype(jnp.int16)
 
 
-def owner_kernel(near, base, offset_ref, *refs):
+def owner_kernel(near, base, half_ref, *refs):
     pieces, (sums_ref, sign_ref, matrix_ref, total_ref) = refs[:near], refs[near:]
     owned, width = total_ref.shape
-    scale, _ = scale_rows(sums_ref, offset_ref[0, 0], owned, width, near)
-    totals = add_levels(pieces, scale, sign_ref, matrix_ref, base)
+    half = half_ref[0, 0]
+    scale, _ = scale_rows(sums_ref, half * owned, owned, width, near)
+    totals = add_levels(pieces, half, scale, sign_ref, matrix_ref, base)
     for g, total in enumerate(totals):
         total_ref[:, g * base : (g + 1) * base] = total
 
 
 def finish_kernel(
-    near, offset_ref, near_ref, far_ref, sums_ref, total_ref, scale_ref, square_ref
+    near, half_ref, near_ref, far_ref, sums_ref, total_ref, scale_ref, square_ref
 ):
     owned, width = near_ref.shape
-    scale, step = scale_rows(sums_ref, offset_ref[0, 0], owned, width, near)
+    scale, step = scale_rows(sums_ref, half_ref[0, 0] * owned, owned, width, near)
     total = near_ref[...] + far_ref[...].astype(jnp.float32) * step
     mean_scale = scale / (2 * near)
     mean_rot = total * mean_scale
@@ -193,37 +195,34 @@
     matrix = jnp.asarray(hadamard(base), jnp.bfloat16)
     me = lax.axis_index("dp")
     near = replicas // 2
-    offset = (me // near * owned).astype(jnp.int32).reshape(1, 1)
+    half = (me // near).astype(jnp.int32).reshape(1, 1)
     params = pltpu.CompilerParams(vmem_limit_bytes=vmem_bytes)
     scalar = pl.BlockSpec(memory_space=pltpu.SMEM)
     array = pl.BlockSpec(memory_space=pltpu.VMEM)
 
-    def block_of(source, index):
-        source = source.reshape(replicas, owned, width)
-        return lax.dynamic_slice_in_dim(source, index, 1, 0).reshape(owned, width)
-
-    far_pieces = [swap(block_of(grads, me ^ mask ^ near), mask) for mask in range(1, near)]
+    halves = grads.reshape(2, near, owned, width)
+
+    def pair_of(index):
+        return lax.dynamic_slice_in_dim(halves, index % near, 1, 1).reshape(2, owned, width)
+
+    pieces = [swap(pair_of(me ^ mask), mask) for mask in range(1, near)] + [pair_of(me)]
     sums = pl.pallas_call(
         sums_kernel,
         in_specs=[array],
         out_shape=jax.ShapeDtypeStruct((2, near, 1, 2 * owned), jnp.float32),
         compiler_params=params,
         name="sum_squares",
-    )(grads.reshape(2, near, owned, width))
-    later, sums = lax.optimization_barrier((grads, sums))
+    )(halves)
     sums = lax.all_to_all(
         sums.reshape(replicas, 1, 2 * owned), "dp", split_axis=0, concat_axis=0, tiled=True
     ).reshape(replicas, 2 * owned)
-    near_pieces = [swap(block_of(later, me ^ mask), mask) for mask in range(1, near)]
-    far_pieces.append(block_of(later, me ^ near))
-    near_pieces.append(block_of(later, me))
     sent = pl.pallas_call(
         functools.partial(proxy_kernel, near, base),
         in_specs=[scalar] + [array] * (near + 3),
         out_shape=jax.ShapeDtypeStruct((owned, width), jnp.int16),
         compiler_params=params,
         name="proxy_blocks",
-    )(offset, *far_pieces, sums, signs, matrix)
+    )(half, *pieces, sums, signs, matrix)
     far_total = swap(sent, near)
     near_total = pl.pallas_call(
         functools.partial(owner_kernel, near, base),
@@ -231,7 +230,7 @@
         out_shape=jax.ShapeDtypeStruct((owned, width), jnp.float32),
         compiler_params=params,
         name="owner_blocks",
-    )(offset, *near_pieces, sums, signs, matrix)
+    )(half, *pieces, sums, signs, matrix)
     total, mean_scale, squares = pl.pallas_call(
         functools.partial(finish_kernel, near),
         in_specs=[scalar] + [array] * 3,
@@ -242,7 +241,7 @@
         ),
         compiler_params=params,
         name="finish_blocks",
-    )(offset, near_total, far_total, sums)
+    )(half, near_total, far_total, sums)
     unrot = pl.pallas_call(
         functools.partial(back_kernel, base),
         out_shape=jax.ShapeDtypeStruct((owned, width), jnp.float32),

time: 61.8 us -> 64.7 us (1.047)
  waiting for transfers between devices: 22.9 us -> 32 us
  starting transfers between devices: 30 us -> 24.8 us
  local copies, waits for them, and re-layouts: 3.61 us -> 2.61 us
    ppermute x18 -> x15, starting transfers between devices: 20.5 us -> 14.6 us  [swap(): return lax.ppermute(value, 'dp', [(i, i ^ mask) for i in range(size)])]
    ppermute x18 -> x15, waiting for transfers between devices: 13.5 us -> 18.6 us  [swap(): return lax.ppermute(value, 'dp', [(i, i ^ mask) for i in range(size)])]
    all_to_all x1, waiting for transfers between devices: 2.69 us -> 6.74 us  [on_device(): lax.all_to_all(sums.reshape(replicas, 1, 2 * owned), 'dp', split_axis=0,...]
    unnamed x14 -> x12, local copies, waits for them, and re-layouts: 2.22 us -> 0.99 us
    all_to_all x1, starting transfers between devices: 3.29 us -> 3.96 us  [on_device(): lax.all_to_all(squares, ('dp', 'expert'), split_axis=0, concat_axis=0, ti...]
    reshape x2 -> x1, local copies, waits for them, and re-layouts: 1.13 us -> 1.36 us  [pair_of(): lax.dynamic_slice_in_dim(halves, index % near, 1, 1)]
  transfers between devices with their start and end apart: 20 -> 17, of which waited for: 8 -> 8; matrix products, arithmetic and copies ran while one was open for 1% -> 0% of each run, Pallas kernels for 4% -> 3%
where the time goes in v8:
time: 64.7 us; the launch traced here: 64.5 us
  waiting for transfers between devices  32 us (49%)
  starting transfers between devices  24.8 us (38%)
  Pallas kernels  4.07 us (6%)
  local copies, waits for them, and re-layouts  2.61 us (4%)
  between operations  0.95 us (1%)
    ppermute x15, waiting for transfers between devices, swap(): return lax.ppermute(value, 'dp', [(i, i ^ mask) for i in range(size)])  18.6 us
    ppermute x15, starting transfers between devices, swap(): return lax.ppermute(value, 'dp', [(i, i ^ mask) for i in range(size)])  14.6 us
    all_to_all x1, waiting for transfers between devices, on_device(): lax.all_to_all(sums.reshape(replicas, 1, 2 * owned), 'dp', split_axis=0,...  6.74 us
    all_to_all x1, waiting for transfers between devices, on_device(): lax.all_to_all(squares, ('dp', 'expert'), split_axis=0, concat_axis=0, ti...  6.72 us
    all_to_all x1, starting transfers between devices, on_device(): lax.all_to_all(sums.reshape(replicas, 1, 2 * owned), 'dp', split_axis=0,...  6.22 us
    all_to_all x1, starting transfers between devices, on_device(): lax.all_to_all(squares, ('dp', 'expert'), split_axis=0, concat_axis=0, ti...  3.96 us
    reshape x1, local copies, waits for them, and re-layouts, pair_of(): lax.dynamic_slice_in_dim(halves, index % near, 1, 1)  1.36 us
  transfers between devices with their start and end apart: 17, of which 8 were waited for; matrix products, arithmetic and copies ran while one was open for 0% of the time, Pallas kernels for 3%

profile of v8, /device:TPU:0, one launch (start us, length us, event | category | flops | bytes accessed | tf_op | source)
XLA Modules:
  0.0 64.5 jit_solution(12193242038138491069)
XLA Ops:
  0.7 1.4 %dynamic-slice_bitcast_fusion = (bf16[2,64,1024]{2,1,0:T(8,128)(2,1)S(1)}, bf16[2,64,1024]{2,1,0:T(8,128)(2,1)S(1)}, bf16[2,64,1024]{2,1,0:T(8,128)(2,1)S(1)}, bf16[2,64,1024]{2,1,0:T(8,128)(2,1)S(1)}) fusion(bf16[2,4,64,1024]{3,2,1,0:T(8,128)(2,1)} %bitcast.43, s32[]{:T(128)S(6)} %select_n.71, s32[]{:T(128)S(6)} %select_n.69, s32[]{:T(128)S(6)} %select_n.67, ...), kind=kLoop, calls=%fused_computation | loop fusion | bytes 2097168 | tf_op jit(solution)/shard_map/reshape | solution.py:206
  2.1 3.0 %collective-permute-start = (bf16[2,64,1024]{2,1,0:T(8,128)(2,1)S(1)}, bf16[2,64,1024]{2,1,0:T(8,128)(2,1)S(1)}, u32[]{:S(2)}, u32[]{:S(2)}) collective-permute-start(bf16[2,64,1024]{2,1,0:T(8,128)(2,1)S(1)} %get-tuple-element.15), channel_id=1, source_target_pairs={{0,4},{4,0},{8,12},{12,8},{16,20},{20,16},{24,28},{28,24},{1,5},{5... | collective-permute-start | bytes 786440 | tf_op jit(solution)/shard_map/ppermute | solution.py:157
  5.1 1.6 %collective-permute-start.1 = (bf16[2,64,1024]{2,1,0:T(8,128)(2,1)S(1)}, bf16[2,64,1024]{2,1,0:T(8,128)(2,1)S(1)}, u32[]{:S(2)}, u32[]{:S(2)}) collective-permute-start(bf16[2,64,1024]{2,1,0:T(8,128)(2,1)S(1)} %get-tuple-element.14), channel_id=1, source_target_pairs={{0,8},{4,12},{8,0},{12,4},{16,24},{20,28},{24,16},{28,20},{1,9},{5... | collective-permute-start | bytes 786440 | tf_op jit(solution)/shard_map/ppermute | solution.py:157
  6.7 0.9 %sum_squares.1 = f32[2,4,1,128]{3,2,1,0:T(1,128)} custom-call(bf16[2,4,64,1024]{3,2,1,0:T(8,128)(2,1)S(1)} %bitcast.44), custom_call_target="tpu_custom_call" | custom-call | tf_op jit(solution)/shard_map/sum_squares/pallas_call | solution.py:209
  7.5 6.2 %all-to-all-start = ((f32[8,1,128]{2,1,0:T(1,128)}), f32[8,1,128]{2,1,0:T(1,128)S(1)}, u32[]{:S(2)}, u32[]{:S(2)}) async-start(f32[8,1,128]{2,1,0:T(1,128)} %bitcast.7), calls=%async_computation | async-start | bytes 8192 | tf_op jit(solution)/shard_map/all_to_all | solution.py:216
  13.8 6.7 %all-to-all-done = f32[8,1,128]{2,1,0:T(1,128)S(1)} async-done(((f32[8,1,128]{2,1,0:T(1,128)}), f32[8,1,128]{2,1,0:T(1,128)S(1)}, u32[]{:S(2)}, u32[]{:S(2)}) %all-to-all-start) | async-done | bytes 4128 | tf_op jit(solution)/shard_map/all_to_all | solution.py:216
  21.2 0.7 %collective-permute-start.3 = (s16[64,1024]{1,0:T(8,128)(2,1)S(1)}, s16[64,1024]{1,0:T(8,128)(2,1)S(1)}, u32[]{:S(2)}, u32[]{:S(2)}) collective-permute-start(s16[64,1024]{1,0:T(8,128)(2,1)S(1)} %proxy_blocks.1), channel_id=1, source_target_pairs={{0,16},{4,20},{8,24},{12,28},{16,0},{20,4},{24,8},{28,12},{1,17},{... | collective-permute-start | bytes 393224 | tf_op jit(solution)/shard_map/ppermute | solution.py:157
  22.4 6.3 %collective-permute-done.3.far_ref = s16[64,1024]{1,0:T(8,128)(2,1)S(1)} collective-permute-done((s16[64,1024]{1,0:T(8,128)(2,1)S(1)}, s16[64,1024]{1,0:T(8,128)(2,1)S(1)}, u32[]{:S(2)}, u32[]{:S(2)}) %collective-permute-start.3) | collective-permute-done | bytes 131104 | tf_op jit(solution)/shard_map/ppermute | solution.py:157
  28.7 0.9 %finish_blocks.1 = (f32[64,1024]{1,0:T(8,128)S(1)}, f32[64,128]{1,0:T(8,128)S(1)}, f32[32,1,128]{2,1,0:T(1,128)}) custom-call(s32[1,1]{1,0:T(1,128)} %bitcast.half_ref, f32[64,1024]{1,0:T(8,128)S(1)} %owner_blocks.1.near_ref, s16[64,1024]{1,0:T(8,128)(2,1)S(1)} %collective-permute-done.3.far_ref, f32[8,128]{1,0:T(8,128)S(1)} %bitcast.49), custom_call_target="tpu_custom_call" | custom-call | tf_op jit(solution)/shard_map/finish_blocks/pallas_call | solution.py:234
  29.6 4.0 %all-to-all-start.1 = ((f32[32,1,128]{2,1,0:T(1,128)}), f32[32,1,128]{2,1,0:T(1,128)S(1)}, u32[]{:S(2)}, u32[]{:S(2)}) async-start(f32[32,1,128]{2,1,0:T(1,128)} %get-tuple-element.7), calls=%async_computation.1 | async-start | bytes 32768 | tf_op jit(solution)/shard_map/all_to_all | solution.py:251
  33.9 6.7 %all-to-all-done.1 = f32[32,1,128]{2,1,0:T(1,128)S(1)} async-done(((f32[32,1,128]{2,1,0:T(1,128)}), f32[32,1,128]{2,1,0:T(1,128)S(1)}, u32[]{:S(2)}, u32[]{:S(2)}) %all-to-all-start.1) | async-done | bytes 16416 | tf_op jit(solution)/shard_map/all_to_all | solution.py:251
  40.6 0.8 %update_blocks.1 = (bf16[64,1024]{1,0:T(8,128)(2,1)S(1)}, f32[64,1024]{1,0:T(8,128)}) custom-call(f32[32,128]{1,0:T(8,128)S(1)} %bitcast.50, f32[64,1024]{1,0:T(8,128)S(1)} %rotate_back.1.unrot_ref, bf16[64,1024]{1,0:T(8,128)(2,1)S(1)} %bitcast.45, bf16[64,1024]{1,0:T(8,128)(2,1)S(1)} %bitcast.46), custom_call_target="tpu_custom_call" | custom-call | tf_op jit(solution)/shard_map/update_blocks/pallas_call | solution.py:253
  42.1 2.3 %collective-permute-start.11 = (bf16[32,1024]{1,0:T(8,128)(2,1)S(1)}, bf16[32,1024]{1,0:T(8,128)(2,1)S(1)}, u32[]{:S(2)}, u32[]{:S(2)}) collective-permute-start(bf16[32,1024]{1,0:T(8,128)(2,1)S(1)} %get-tuple-element.16), channel_id=1, source_target_pairs={{0,16},{4,20},{8,24},{12,28},{16,0},{20,4},{24,8},{28,12},{1,17},{... | collective-permute-start | bytes 196616 | tf_op jit(solution)/shard_map/ppermute | solution.py:157
  45.6 3.6 %collective-permute-done.7 = bf16[32,1024]{1,0:T(8,128)(2,1)S(1)} collective-permute-done((bf16[32,1024]{1,0:T(8,128)(2,1)S(1)}, bf16[32,1024]{1,0:T(8,128)(2,1)S(1)}, u32[]{:S(2)}, u32[]{:S(2)}) %collective-permute-start.7) | collective-permute-done | bytes 65568 | tf_op jit(solution)/shard_map/ppermute | solution.py:157
  49.2 1.3 %collective-permute-done.11 = bf16[32,1024]{1,0:T(8,128)(2,1)S(1)} collective-permute-done((bf16[32,1024]{1,0:T(8,128)(2,1)S(1)}, bf16[32,1024]{1,0:T(8,128)(2,1)S(1)}, u32[]{:S(2)}, u32[]{:S(2)}) %collective-permute-start.11) | collective-permute-done | bytes 65568 | tf_op jit(solution)/shard_map/ppermute | solution.py:157
  50.5 0.7 %collective-permute-start.12 = (bf16[32,1024]{1,0:T(8,128)(2,1)S(1)}, bf16[32,1024]{1,0:T(8,128)(2,1)S(1)}, u32[]{:S(2)}, u32[]{:S(2)}) collective-permute-start(bf16[32,1024]{1,0:T(8,128)(2,1)S(1)} %collective-permute-done.11), channel_id=1, source_target_pairs={{0,8},{4,12},{8,0},{12,4},{16,24},{20,28},{24,16},{28,20},{1,9},{5... | collective-permute-start | bytes 196616 | tf_op jit(solution)/shard_map/ppermute | solution.py:157
  51.4 0.7 %collective-permute-start.9 = (bf16[32,1024]{1,0:T(8,128)(2,1)S(1)}, bf16[32,1024]{1,0:T(8,128)(2,1)S(1)}, u32[]{:S(2)}, u32[]{:S(2)}) collective-permute-start(bf16[32,1024]{1,0:T(8,128)(2,1)S(1)} %collective-permute-done.7), channel_id=1, source_target_pairs={{0,4},{4,0},{8,12},{12,8},{16,20},{20,16},{24,28},{28,24},{1,5},{5... | collective-permute-start | bytes 196616 | tf_op jit(solution)/shard_map/ppermute | solution.py:157
  52.1 1.8 %collective-permute-done.8 = bf16[32,1024]{1,0:T(8,128)(2,1)S(1)} collective-permute-done((bf16[32,1024]{1,0:T(8,128)(2,1)S(1)}, bf16[32,1024]{1,0:T(8,128)(2,1)S(1)}, u32[]{:S(2)}, u32[]{:S(2)}) %collective-permute-start.8) | collective-permute-done | bytes 65568 | tf_op jit(solution)/shard_map/ppermute | solution.py:157
  53.8 0.7 %collective-permute-start.13 = (bf16[32,1024]{1,0:T(8,128)(2,1)S(1)}, bf16[32,1024]{1,0:T(8,128)(2,1)S(1)}, u32[]{:S(2)}, u32[]{:S(2)}) collective-permute-start(bf16[32,1024]{1,0:T(8,128)(2,1)S(1)} %collective-permute-done.11), channel_id=1, source_target_pairs={{0,4},{4,0},{8,12},{12,8},{16,20},{20,16},{24,28},{28,24},{1,5},{5... | collective-permute-start | bytes 196616 | tf_op jit(solution)/shard_map/ppermute | solution.py:157
  54.9 1.0 %collective-permute-start.10 = (bf16[32,1024]{1,0:T(8,128)(2,1)S(1)}, bf16[32,1024]{1,0:T(8,128)(2,1)S(1)}, u32[]{:S(2)}, u32[]{:S(2)}) collective-permute-start(bf16[32,1024]{1,0:T(8,128)(2,1)S(1)} %collective-permute-done.8), channel_id=1, source_target_pairs={{0,4},{4,0},{8,12},{12,8},{16,20},{20,16},{24,28},{28,24},{1,5},{5... | collective-permute-start | bytes 196616 | tf_op jit(solution)/shard_map/ppermute | solution.py:157
  55.9 1.0 %collective-permute-start.14 = (bf16[32,1024]{1,0:T(8,128)(2,1)S(1)}, bf16[32,1024]{1,0:T(8,128)(2,1)S(1)}, u32[]{:S(2)}, u32[]{:S(2)}) collective-permute-start(bf16[32,1024]{1,0:T(8,128)(2,1)S(1)} %collective-permute-done.12), channel_id=1, source_target_pairs={{0,4},{4,0},{8,12},{12,8},{16,20},{20,16},{24,28},{28,24},{1,5},{5... | collective-permute-start | bytes 196616 | tf_op jit(solution)/shard_map/ppermute | solution.py:157
  56.9 1.1 %collective-permute-start.6 = (bf16[64,1024]{1,0:T(8,128)(2,1)S(1)}, bf16[64,1024]{1,0:T(8,128)(2,1)S(1)}, u32[]{:S(2)}, u32[]{:S(2)}) collective-permute-start(bf16[64,1024]{1,0:T(8,128)(2,1)S(1)} %collective-permute-done.4), channel_id=1, source_target_pairs={{0,4},{4,0},{8,12},{12,8},{16,20},{20,16},{24,28},{28,24},{1,5},{5... | collective-permute-start | bytes 393224 | tf_op jit(solution)/shard_map/ppermute | solution.py:157
  58.0 5.3 %collective-permute-done.6 = bf16[64,1024]{1,0:T(8,128)(2,1)S(1)} collective-permute-done((bf16[64,1024]{1,0:T(8,128)(2,1)S(1)}, bf16[64,1024]{1,0:T(8,128)(2,1)S(1)}, u32[]{:S(2)}, u32[]{:S(2)}) %collective-permute-start.6) | collective-permute-done | bytes 131104 | tf_op jit(solution)/shard_map/ppermute | solution.py:157
  63.5 1.0 %copy-done.5 = bf16[8,64,1024]{2,1,0:T(8,128)(2,1)} copy-done((bf16[8,64,1024]{2,1,0:T(8,128)(2,1)}, bf16[8,64,1024]{2,1,0:T(8,128)(2,1)S(1)}, u32[]{:S(2)}) %copy-start.5) | copy-done | bytes 1048600
  (43 shorter events, 3.9 us)
Async XLA Ops:
  0.7 6.0 %copy-start = (bf16[1,1,512,1024]{3,2,1,0:T(8,128)(2,1)S(1)}, bf16[1,1,512,1024]{3,2,1,0:T(8,128)(2,1)}, u32[]{:S(2)}) copy-start(bf16[1,1,512,1024]{3,2,1,0:T(8,128)(2,1)} %param.5) | copy-start | bytes 3145732
  2.1 18.4 %collective-permute-start = (bf16[2,64,1024]{2,1,0:T(8,128)(2,1)S(1)}, bf16[2,64,1024]{2,1,0:T(8,128)(2,1)S(1)}, u32[]{:S(2)}, u32[]{:S(2)}) collective-permute-start(bf16[2,64,1024]{2,1,0:T(8,128)(2,1)S(1)} %get-tuple-element.15), channel_id=1, source_target_pairs={{0,4},{4,0},{8,12},{12,8},{16,20},{20,16},{24,28},{28,24},{1,5},{5... | collective-permute-start | bytes 786440 | tf_op jit(solution)/shard_map/ppermute | solution.py:157
  5.1 15.4 %collective-permute-start.1 = (bf16[2,64,1024]{2,1,0:T(8,128)(2,1)S(1)}, bf16[2,64,1024]{2,1,0:T(8,128)(2,1)S(1)}, u32[]{:S(2)}, u32[]{:S(2)}) collective-permute-start(bf16[2,64,1024]{2,1,0:T(8,128)(2,1)S(1)} %get-tuple-element.14), channel_id=1, source_target_pairs={{0,8},{4,12},{8,0},{12,4},{16,24},{20,28},{24,16},{28,20},{1,9},{5... | collective-permute-start | bytes 786440 | tf_op jit(solution)/shard_map/ppermute | solution.py:157
  6.7 13.9 %copy-start.1 = (bf16[256,256]{1,0:T(8,128)(2,1)S(1)}, bf16[256,256]{1,0:T(8,128)(2,1)}, u32[]{:S(2)}) copy-start(bf16[256,256]{1,0:T(8,128)(2,1)} %constant.62.clone.refs_6_.matrix_ref) | copy-start | bytes 393220
  6.7 13.9 %collective-permute-start.2 = (bf16[2,64,1024]{2,1,0:T(8,128)(2,1)S(1)}, bf16[2,64,1024]{2,1,0:T(8,128)(2,1)S(1)}, u32[]{:S(2)}, u32[]{:S(2)}) collective-permute-start(bf16[2,64,1024]{2,1,0:T(8,128)(2,1)S(1)} %get-tuple-element.13), channel_id=1, source_target_pairs={{0,12},{4,8},{8,4},{12,0},{16,28},{20,24},{24,20},{28,16},{1,13},{... | collective-permute-start | bytes 786440 | tf_op jit(solution)/shard_map/ppermute | solution.py:157
  7.5 13.0 %all-to-all-start = ((f32[8,1,128]{2,1,0:T(1,128)}), f32[8,1,128]{2,1,0:T(1,128)S(1)}, u32[]{:S(2)}, u32[]{:S(2)}) async-start(f32[8,1,128]{2,1,0:T(1,128)} %bitcast.7), calls=%async_computation | async-start | bytes 8192 | tf_op jit(solution)/shard_map/all_to_all | solution.py:216
  13.8 6.8 %copy-start.4 = (s32[1,1024]{1,0:T(1,128)S(1)}, s32[1,1024]{1,0:T(1,128)}, u32[]{:S(2)}) copy-start(s32[1,1024]{1,0:T(1,128)} %sign_ref.1) | copy-start | bytes 12292
  21.2 7.5 %collective-permute-start.3 = (s16[64,1024]{1,0:T(8,128)(2,1)S(1)}, s16[64,1024]{1,0:T(8,128)(2,1)S(1)}, u32[]{:S(2)}, u32[]{:S(2)}) collective-permute-start(s16[64,1024]{1,0:T(8,128)(2,1)S(1)} %proxy_blocks.1), channel_id=1, source_target_pairs={{0,16},{4,20},{8,24},{12,28},{16,0},{20,4},{24,8},{28,12},{1,17},{... | collective-permute-start | bytes 393224 | tf_op jit(solution)/shard_map/ppermute | solution.py:157
  29.6 11.0 %all-to-all-start.1 = ((f32[32,1,128]{2,1,0:T(1,128)}), f32[32,1,128]{2,1,0:T(1,128)S(1)}, u32[]{:S(2)}, u32[]{:S(2)}) async-start(f32[32,1,128]{2,1,0:T(1,128)} %get-tuple-element.7), calls=%async_computation.1 | async-start | bytes 32768 | tf_op jit(solution)/shard_map/all_to_all | solution.py:251
  33.6 7.1 %copy-start.2 = (bf16[1,64,1024]{2,1,0:T(8,128)(2,1)S(1)}, bf16[1,64,1024]{2,1,0:T(8,128)(2,1)}, u32[]{:S(2)}) copy-start(bf16[1,64,1024]{2,1,0:T(8,128)(2,1)} %param.7) | copy-start | bytes 393220
  33.6 7.1 %copy-start.3 = (bf16[1,64,1024]{2,1,0:T(8,128)(2,1)S(1)}, bf16[1,64,1024]{2,1,0:T(8,128)(2,1)}, u32[]{:S(2)}) copy-start(bf16[1,64,1024]{2,1,0:T(8,128)(2,1)} %param.8) | copy-start | bytes 393220
  41.5 7.7 %collective-permute-start.7 = (bf16[32,1024]{1,0:T(8,128)(2,1)S(1)}, bf16[32,1024]{1,0:T(8,128)(2,1)S(1)}, u32[]{:S(2)}, u32[]{:S(2)}) collective-permute-start(bf16[32,1024]{1,0:T(8,128)(2,1)S(1)} %get-tuple-element.17), channel_id=1, source_target_pairs={{0,16},{4,20},{8,24},{12,28},{16,0},{20,4},{24,8},{28,12},{1,17},{... | collective-permute-start | bytes 196616 | tf_op jit(solution)/shard_map/ppermute | solution.py:157
  42.1 8.4 %collective-permute-start.11 = (bf16[32,1024]{1,0:T(8,128)(2,1)S(1)}, bf16[32,1024]{1,0:T(8,128)(2,1)S(1)}, u32[]{:S(2)}, u32[]{:S(2)}) collective-permute-start(bf16[32,1024]{1,0:T(8,128)(2,1)S(1)} %get-tuple-element.16), channel_id=1, source_target_pairs={{0,16},{4,20},{8,24},{12,28},{16,0},{20,4},{24,8},{28,12},{1,17},{... | collective-permute-start | bytes 196616 | tf_op jit(solution)/shard_map/ppermute | solution.py:157
  44.5 11.4 %collective-permute-start.4 = (bf16[64,1024]{1,0:T(8,128)(2,1)S(1)}, bf16[64,1024]{1,0:T(8,128)(2,1)S(1)}, u32[]{:S(2)}, u32[]{:S(2)}) collective-permute-start(bf16[64,1024]{1,0:T(8,128)(2,1)S(1)} %get-tuple-element.10), channel_id=1, source_target_pairs={{0,8},{4,12},{8,0},{12,4},{16,24},{20,28},{24,16},{28,20},{1,9},{5... | collective-permute-start | bytes 393224 | tf_op jit(solution)/shard_map/ppermute | solution.py:157
  45.0 11.9 %collective-permute-start.5 = (bf16[64,1024]{1,0:T(8,128)(2,1)S(1)}, bf16[64,1024]{1,0:T(8,128)(2,1)S(1)}, u32[]{:S(2)}, u32[]{:S(2)}) collective-permute-start(bf16[64,1024]{1,0:T(8,128)(2,1)S(1)} %get-tuple-element.10), channel_id=1, source_target_pairs={{0,4},{4,0},{8,12},{12,8},{16,20},{20,16},{24,28},{28,24},{1,5},{5... | collective-permute-start | bytes 393224 | tf_op jit(solution)/shard_map/ppermute | solution.py:157
  49.2 4.7 %collective-permute-start.8 = (bf16[32,1024]{1,0:T(8,128)(2,1)S(1)}, bf16[32,1024]{1,0:T(8,128)(2,1)S(1)}, u32[]{:S(2)}, u32[]{:S(2)}) collective-permute-start(bf16[32,1024]{1,0:T(8,128)(2,1)S(1)} %collective-permute-done.7), channel_id=1, source_target_pairs={{0,8},{4,12},{8,0},{12,4},{16,24},{20,28},{24,16},{28,20},{1,9},{5... | collective-permute-start | bytes 196616 | tf_op jit(solution)/shard_map/ppermute | solution.py:157
  50.5 4.4 %collective-permute-start.12 = (bf16[32,1024]{1,0:T(8,128)(2,1)S(1)}, bf16[32,1024]{1,0:T(8,128)(2,1)S(1)}, u32[]{:S(2)}, u32[]{:S(2)}) collective-permute-start(bf16[32,1024]{1,0:T(8,128)(2,1)S(1)} %collective-permute-done.11), channel_id=1, source_target_pairs={{0,8},{4,12},{8,0},{12,4},{16,24},{20,28},{24,16},{28,20},{1,9},{5... | collective-permute-start | bytes 196616 | tf_op jit(solution)/shard_map/ppermute | solution.py:157
  51.4 12.0 %collective-permute-start.9 = (bf16[32,1024]{1,0:T(8,128)(2,1)S(1)}, bf16[32,1024]{1,0:T(8,128)(2,1)S(1)}, u32[]{:S(2)}, u32[]{:S(2)}) collective-permute-start(bf16[32,1024]{1,0:T(8,128)(2,1)S(1)} %collective-permute-done.7), channel_id=1, source_target_pairs={{0,4},{4,0},{8,12},{12,8},{16,20},{20,16},{24,28},{28,24},{1,5},{5... | collective-permute-start | bytes 196616 | tf_op jit(solution)/shard_map/ppermute | solution.py:157
  53.8 9.6 %collective-permute-start.13 = (bf16[32,1024]{1,0:T(8,128)(2,1)S(1)}, bf16[32,1024]{1,0:T(8,128)(2,1)S(1)}, u32[]{:S(2)}, u32[]{:S(2)}) collective-permute-start(bf16[32,1024]{1,0:T(8,128)(2,1)S(1)} %collective-permute-done.11), channel_id=1, source_target_pairs={{0,4},{4,0},{8,12},{12,8},{16,20},{20,16},{24,28},{28,24},{1,5},{5... | collective-permute-start | bytes 196616 | tf_op jit(solution)/shard_map/ppermute | solution.py:157
  54.9 8.5 %collective-permute-start.10 = (bf16[32,1024]{1,0:T(8,128)(2,1)S(1)}, bf16[32,1024]{1,0:T(8,128)(2,1)S(1)}, u32[]{:S(2)}, u32[]{:S(2)}) collective-permute-start(bf16[32,1024]{1,0:T(8,128)(2,1)S(1)} %collective-permute-done.8), channel_id=1, source_target_pairs={{0,4},{4,0},{8,12},{12,8},{16,20},{20,16},{24,28},{28,24},{1,5},{5... | collective-permute-start | bytes 196616 | tf_op jit(solution)/shard_map/ppermute | solution.py:157
  55.9 7.6 %collective-permute-start.14 = (bf16[32,1024]{1,0:T(8,128)(2,1)S(1)}, bf16[32,1024]{1,0:T(8,128)(2,1)S(1)}, u32[]{:S(2)}, u32[]{:S(2)}) collective-permute-start(bf16[32,1024]{1,0:T(8,128)(2,1)S(1)} %collective-permute-done.12), channel_id=1, source_target_pairs={{0,4},{4,0},{8,12},{12,8},{16,20},{20,16},{24,28},{28,24},{1,5},{5... | collective-permute-start | bytes 196616 | tf_op jit(solution)/shard_map/ppermute | solution.py:157
  56.9 6.4 %collective-permute-start.6 = (bf16[64,1024]{1,0:T(8,128)(2,1)S(1)}, bf16[64,1024]{1,0:T(8,128)(2,1)S(1)}, u32[]{:S(2)}, u32[]{:S(2)}) collective-permute-start(bf16[64,1024]{1,0:T(8,128)(2,1)S(1)} %collective-permute-done.4), channel_id=1, source_target_pairs={{0,4},{4,0},{8,12},{12,8},{16,20},{20,16},{24,28},{28,24},{1,5},{5... | collective-permute-start | bytes 393224 | tf_op jit(solution)/shard_map/ppermute | solution.py:157
  63.5 1.0 %copy-start.5 = (bf16[8,64,1024]{2,1,0:T(8,128)(2,1)}, bf16[8,64,1024]{2,1,0:T(8,128)(2,1)S(1)}, u32[]{:S(2)}) copy-start(bf16[8,64,1024]{2,1,0:T(8,128)(2,1)S(1)} %bitcast_dynamic-update-slice_fusion.4) | copy-start | bytes 3145732

commit v9 on v8

--- a/solution.py
+++ b/solution.py
@@ -152,37 +152,55 @@
     new_ref[...] = summed.astype(jnp.bfloat16)
 
 
-def swap(value, mask):
-    size = lax.axis_size("dp")
-    return lax.ppermute(value, "dp", [(i, i ^ mask) for i in range(size)])
+def swap(value, even, odd=None):
+    odd = even if odd is None else odd
+    size, experts = lax.axis_size("dp"), lax.axis_size("expert")
+    pairs = []
+    for i in range(size):
+        for e in range(experts):
+            mask = odd if e % 2 else even
+            pairs.append((i * experts + e, (i ^ mask) * experts + e))
+    return lax.ppermute(value, ("dp", "expert"), pairs)
+
+
+def near_masks(replicas):
+    x_count = 1 << ((replicas.bit_length() - 1) // 2)
+    z_count = replicas // 2 // x_count
+    along_x = list(range(1, x_count))
+    along_z = [z * x_count for z in range(1, z_count)]
+    if len(along_x) == len(along_z):
+        return along_z, along_x, along_x, along_z
+    return along_z, along_x, along_z, along_x
 
 
 def gather_blocks(block, replicas):
-    x_count = 1 << ((replicas.bit_length() - 1) // 2)
     near = replicas // 2
     me = lax.axis_index("dp")
+    odd = lax.axis_index("expert") % 2 == 1
     owned, width = block.shape
-    parts = 2 if owned % 32 == 0 else 1
-    rows = owned // parts
+    first_even, second_even, first_odd, second_odd = near_masks(replicas)
     pieces = []
 
-    def spread(start, piece, row):
-        pieces.append((start, row, piece))
-        along = {0: piece}
-        for z in range(x_count, near, x_count):
-            along[z] = swap(piece, z)
-            pieces.append((start + z, row, along[z]))
-        for z in range(0, near, x_count):
-            for x in range(1, x_count):
-                pieces.append((start + z + x, row, swap(along[z], x)))
-
-    across = [swap(block[p * rows : (p + 1) * rows], near) for p in range(parts)]
-    spread(0, block, 0)
-    for p, piece in enumerate(across):
-        spread(near, piece, p * rows)
+    def keep(even_mask, odd_mask, piece):
+        pieces.append((jnp.where(odd, me ^ odd_mask, me ^ even_mask), piece))
+
+    def spread(start, piece):
+        keep(start, start, piece)
+        firsts = [(a, b, swap(piece, a, b)) for a, b in zip(first_even, first_odd)]
+        for a, b, value in firsts:
+            keep(start + a, start + b, value)
+        for c, d in zip(second_even, second_odd):
+            keep(start + c, start + d, swap(piece, c, d))
+        for a, b, value in firsts:
+            for c, d in zip(second_even, second_odd):
+                keep(start + a + c, start + b + d, swap(value, c, d))
+
+    across = swap(block, near)
+    spread(0, block)
+    spread(near, across)
     out = jnp.zeros((replicas, owned, width), block.dtype)
-    for mask, row, piece in pieces:
-        out = lax.dynamic_update_slice(out, piece[None], (me ^ mask, row, 0))
+    for index, piece in pieces:
+        out = lax.dynamic_update_slice(out, piece[None], (index, 0, 0))
     return out.reshape(1, replicas * owned, width)
 
 
@@ -205,7 +223,16 @@
     def pair_of(index):
         return lax.dynamic_slice_in_dim(halves, index % near, 1, 1).reshape(2, owned, width)
 
-    pieces = [swap(pair_of(me ^ mask), mask) for mask in range(1, near)] + [pair_of(me)]
+    odd = lax.axis_index("expert") % 2 == 1
+
+    def pair_to(even, odd_mask):
+        return swap(pair_of(jnp.where(odd, me ^ odd_mask, me ^ even)), even, odd_mask)
+
+    first_even, second_even, first_odd, second_odd = near_masks(replicas)
+    pieces = [pair_to(a, b) for a, b in zip(first_even, first_odd)]
+    pieces += [pair_to(c, d) for c, d in zip(second_even, second_odd)]
+    pieces += [pair_to(a + c, a + c) for a in first_even for c in second_even]
+    pieces.append(pair_of(me))
     sums = pl.pallas_call(
         sums_kernel,
         in_specs=[array],

time: 64.7 us -> 64.8 us (level)
  waiting for transfers between devices: 32 us -> 36.6 us
  starting transfers between devices: 24.8 us -> 20.4 us
    ppermute x15 -> x11, waiting for transfers between devices: 18.6 us -> 23.2 us  [swap(): return lax.ppermute(value, ('dp', 'expert'), pairs)]
    ppermute x15 -> x11, starting transfers between devices: 14.6 us -> 10.3 us  [swap(): return lax.ppermute(value, ('dp', 'expert'), pairs)]
  transfers between devices with their start and end apart: 17 -> 13, of which waited for: 8 -> 6; matrix products, arithmetic and copies ran while one was open for 0% -> 0% of each run, Pallas kernels for 3% -> 3%
where the time goes in v9:
time: 64.8 us; the launch traced here: 64.6 us
  waiting for transfers between devices  36.6 us (56%)
  starting transfers between devices  20.4 us (31%)
  Pallas kernels  4.08 us (6%)
  local copies, waits for them, and re-layouts  2.58 us (4%)
  between operations  0.97 us (1%)
    ppermute x11, waiting for transfers between devices, swap(): return lax.ppermute(value, ('dp', 'expert'), pairs)  23.2 us
    ppermute x11, starting transfers between devices, swap(): return lax.ppermute(value, ('dp', 'expert'), pairs)  10.3 us
    all_to_all x1, waiting for transfers between devices, on_device(): lax.all_to_all(sums.reshape(replicas, 1, 2 * owned), 'dp', split_axis=0,...  6.72 us
    all_to_all x1, waiting for transfers between devices, on_device(): lax.all_to_all(squares, ('dp', 'expert'), split_axis=0, concat_axis=0, ti...  6.66 us
    all_to_all x1, starting transfers between devices, on_device(): lax.all_to_all(sums.reshape(replicas, 1, 2 * owned), 'dp', split_axis=0,...  6.18 us
    all_to_all x1, starting transfers between devices, on_device(): lax.all_to_all(squares, ('dp', 'expert'), split_axis=0, concat_axis=0, ti...  3.87 us
    reshape x1, local copies, waits for them, and re-layouts, pair_of(): lax.dynamic_slice_in_dim(halves, index % near, 1, 1)  1.36 us
  transfers between devices with their start and end apart: 13, of which 6 were waited for; matrix products, arithmetic and copies ran while one was open for 0% of the time, Pallas kernels for 3%

profile of v9, /device:TPU:0, one launch (start us, length us, event | category | flops | bytes accessed | tf_op | source)
XLA Modules:
  0.0 64.6 jit_solution(7478549974640449381)
XLA Ops:
  0.7 1.4 %dynamic-slice_bitcast_fusion = (bf16[2,64,1024]{2,1,0:T(8,128)(2,1)S(1)}, bf16[2,64,1024]{2,1,0:T(8,128)(2,1)S(1)}, bf16[2,64,1024]{2,1,0:T(8,128)(2,1)S(1)}, bf16[2,64,1024]{2,1,0:T(8,128)(2,1)S(1)}) fusion(bf16[2,4,64,1024]{3,2,1,0:T(8,128)(2,1)} %bitcast.35, s32[]{:T(128)S(6)} %select_n.95, s32[]{:T(128)S(6)} %select_n.93, s32[]{:T(128)S(6)} %select_n.91, ...), kind=kLoop, calls=%fused_computation | loop fusion | bytes 2097168 | tf_op jit(solution)/shard_map/reshape | solution.py:224
  2.1 3.1 %collective-permute-start = (bf16[2,64,1024]{2,1,0:T(8,128)(2,1)S(1)}, bf16[2,64,1024]{2,1,0:T(8,128)(2,1)S(1)}, u32[]{:S(2)}, u32[]{:S(2)}) collective-permute-start(bf16[2,64,1024]{2,1,0:T(8,128)(2,1)S(1)} %get-tuple-element.15), channel_id=1, source_target_pairs={{0,8},{1,5},{2,10},{3,7},{4,12},{5,1},{6,14},{7,3},{8,0},{9,13},{1... | collective-permute-start | bytes 786440 | tf_op jit(solution)/shard_map/ppermute | solution.py:163
  5.2 1.5 %collective-permute-start.1 = (bf16[2,64,1024]{2,1,0:T(8,128)(2,1)S(1)}, bf16[2,64,1024]{2,1,0:T(8,128)(2,1)S(1)}, u32[]{:S(2)}, u32[]{:S(2)}) collective-permute-start(bf16[2,64,1024]{2,1,0:T(8,128)(2,1)S(1)} %get-tuple-element.14), channel_id=1, source_target_pairs={{0,4},{1,9},{2,6},{3,11},{4,0},{5,13},{6,2},{7,15},{8,12},{9,1},{1... | collective-permute-start | bytes 786440 | tf_op jit(solution)/shard_map/ppermute | solution.py:163
  6.7 0.9 %sum_squares.1 = f32[2,4,1,128]{3,2,1,0:T(1,128)} custom-call(bf16[2,4,64,1024]{3,2,1,0:T(8,128)(2,1)S(1)} %bitcast.36), custom_call_target="tpu_custom_call" | custom-call | tf_op jit(solution)/shard_map/sum_squares/pallas_call | solution.py:236
  7.6 6.2 %all-to-all-start = ((f32[8,1,128]{2,1,0:T(1,128)}), f32[8,1,128]{2,1,0:T(1,128)S(1)}, u32[]{:S(2)}, u32[]{:S(2)}) async-start(f32[8,1,128]{2,1,0:T(1,128)} %bitcast.7), calls=%async_computation | async-start | bytes 8192 | tf_op jit(solution)/shard_map/all_to_all | solution.py:243
  13.8 6.7 %all-to-all-done = f32[8,1,128]{2,1,0:T(1,128)S(1)} async-done(((f32[8,1,128]{2,1,0:T(1,128)}), f32[8,1,128]{2,1,0:T(1,128)S(1)}, u32[]{:S(2)}, u32[]{:S(2)}) %all-to-all-start) | async-done | bytes 4128 | tf_op jit(solution)/shard_map/all_to_all | solution.py:243
  20.5 0.6 proxy_blocks.1
  21.1 0.7 %collective-permute-start.3 = (s16[64,1024]{1,0:T(8,128)(2,1)S(1)}, s16[64,1024]{1,0:T(8,128)(2,1)S(1)}, u32[]{:S(2)}, u32[]{:S(2)}) collective-permute-start(s16[64,1024]{1,0:T(8,128)(2,1)S(1)} %proxy_blocks.1), channel_id=1, source_target_pairs={{0,16},{1,17},{2,18},{3,19},{4,20},{5,21},{6,22},{7,23},{8,24},{9,... | collective-permute-start | bytes 393224 | tf_op jit(solution)/shard_map/ppermute | solution.py:163
  21.9 0.6 owner_blocks.1.near_ref
  22.4 7.7 %collective-permute-done.3.far_ref = s16[64,1024]{1,0:T(8,128)(2,1)S(1)} collective-permute-done((s16[64,1024]{1,0:T(8,128)(2,1)S(1)}, s16[64,1024]{1,0:T(8,128)(2,1)S(1)}, u32[]{:S(2)}, u32[]{:S(2)}) %collective-permute-start.3) | collective-permute-done | bytes 131104 | tf_op jit(solution)/shard_map/ppermute | solution.py:163
  30.1 0.9 %finish_blocks.1 = (f32[64,1024]{1,0:T(8,128)S(1)}, f32[64,128]{1,0:T(8,128)S(1)}, f32[32,1,128]{2,1,0:T(1,128)}) custom-call(s32[1,1]{1,0:T(1,128)} %bitcast.half_ref, f32[64,1024]{1,0:T(8,128)S(1)} %owner_blocks.1.near_ref, s16[64,1024]{1,0:T(8,128)(2,1)S(1)} %collective-permute-done.3.far_ref, f32[8,128]{1,0:T(8,128)S(1)} %bitcast.41), custom_call_target="tpu_custom_call" | custom-call | tf_op jit(solution)/shard_map/finish_blocks/pallas_call | solution.py:261
  31.0 3.9 %all-to-all-start.1 = ((f32[32,1,128]{2,1,0:T(1,128)}), f32[32,1,128]{2,1,0:T(1,128)S(1)}, u32[]{:S(2)}, u32[]{:S(2)}) async-start(f32[32,1,128]{2,1,0:T(1,128)} %get-tuple-element.7), calls=%async_computation.1 | async-start | bytes 32768 | tf_op jit(solution)/shard_map/all_to_all | solution.py:278
  35.3 6.7 %all-to-all-done.1 = f32[32,1,128]{2,1,0:T(1,128)S(1)} async-done(((f32[32,1,128]{2,1,0:T(1,128)}), f32[32,1,128]{2,1,0:T(1,128)S(1)}, u32[]{:S(2)}, u32[]{:S(2)}) %all-to-all-start.1) | async-done | bytes 16416 | tf_op jit(solution)/shard_map/all_to_all | solution.py:278
  42.0 0.8 %update_blocks.1 = (bf16[64,1024]{1,0:T(8,128)(2,1)S(1)}, f32[64,1024]{1,0:T(8,128)}) custom-call(f32[32,128]{1,0:T(8,128)S(1)} %bitcast.42, f32[64,1024]{1,0:T(8,128)S(1)} %rotate_back.1.unrot_ref, bf16[64,1024]{1,0:T(8,128)(2,1)S(1)} %bitcast.37, bf16[64,1024]{1,0:T(8,128)(2,1)S(1)} %bitcast.38), custom_call_target="tpu_custom_call" | custom-call | tf_op jit(solution)/shard_map/update_blocks/pallas_call | solution.py:280
  42.8 0.6 collective-permute-start.4
  43.4 0.6 collective-permute-start.5
  43.9 0.5 collective-permute-start.7
  44.6 7.7 %collective-permute-done.7 = bf16[64,1024]{1,0:T(8,128)(2,1)S(1)} collective-permute-done((bf16[64,1024]{1,0:T(8,128)(2,1)S(1)}, bf16[64,1024]{1,0:T(8,128)(2,1)S(1)}, u32[]{:S(2)}, u32[]{:S(2)}) %collective-permute-start.7) | collective-permute-done | bytes 131104 | tf_op jit(solution)/shard_map/ppermute | solution.py:163
  52.3 1.7 %collective-permute-start.9 = (bf16[64,1024]{1,0:T(8,128)(2,1)S(1)}, bf16[64,1024]{1,0:T(8,128)(2,1)S(1)}, u32[]{:S(2)}, u32[]{:S(2)}) collective-permute-start(bf16[64,1024]{1,0:T(8,128)(2,1)S(1)} %collective-permute-done.7), channel_id=1, source_target_pairs={{0,4},{1,9},{2,6},{3,11},{4,0},{5,13},{6,2},{7,15},{8,12},{9,1},{1... | collective-permute-start | bytes 393224 | tf_op jit(solution)/shard_map/ppermute | solution.py:163
  54.0 0.4 collective-permute-start.6
  54.4 4.2 %collective-permute-done.8 = bf16[64,1024]{1,0:T(8,128)(2,1)S(1)} collective-permute-done((bf16[64,1024]{1,0:T(8,128)(2,1)S(1)}, bf16[64,1024]{1,0:T(8,128)(2,1)S(1)}, u32[]{:S(2)}, u32[]{:S(2)}) %collective-permute-start.8) | collective-permute-done | bytes 131104 | tf_op jit(solution)/shard_map/ppermute | solution.py:163
  58.6 1.3 %collective-permute-start.10 = (bf16[64,1024]{1,0:T(8,128)(2,1)S(1)}, bf16[64,1024]{1,0:T(8,128)(2,1)S(1)}, u32[]{:S(2)}, u32[]{:S(2)}) collective-permute-start(bf16[64,1024]{1,0:T(8,128)(2,1)S(1)} %collective-permute-done.8), channel_id=1, source_target_pairs={{0,4},{1,9},{2,6},{3,11},{4,0},{5,13},{6,2},{7,15},{8,12},{9,1},{1... | collective-permute-start | bytes 393224 | tf_op jit(solution)/shard_map/ppermute | solution.py:163
  60.0 3.6 %collective-permute-done.10 = bf16[64,1024]{1,0:T(8,128)(2,1)S(1)} collective-permute-done((bf16[64,1024]{1,0:T(8,128)(2,1)S(1)}, bf16[64,1024]{1,0:T(8,128)(2,1)S(1)}, u32[]{:S(2)}, u32[]{:S(2)}) %collective-permute-start.10) | collective-permute-done | bytes 131104 | tf_op jit(solution)/shard_map/ppermute | solution.py:163
  63.6 1.0 %copy-done.5 = bf16[8,64,1024]{2,1,0:T(8,128)(2,1)} copy-done((bf16[8,64,1024]{2,1,0:T(8,128)(2,1)}, bf16[8,64,1024]{2,1,0:T(8,128)(2,1)S(1)}, u32[]{:S(2)}) %copy-start.5) | copy-done | bytes 1048600
  (30 shorter events, 0.6 us)
Async XLA Ops:
  0.7 6.0 %copy-start = (bf16[1,1,512,1024]{3,2,1,0:T(8,128)(2,1)S(1)}, bf16[1,1,512,1024]{3,2,1,0:T(8,128)(2,1)}, u32[]{:S(2)}) copy-start(bf16[1,1,512,1024]{3,2,1,0:T(8,128)(2,1)} %param.5) | copy-start | bytes 3145732
  2.1 18.4 %collective-permute-start = (bf16[2,64,1024]{2,1,0:T(8,128)(2,1)S(1)}, bf16[2,64,1024]{2,1,0:T(8,128)(2,1)S(1)}, u32[]{:S(2)}, u32[]{:S(2)}) collective-permute-start(bf16[2,64,1024]{2,1,0:T(8,128)(2,1)S(1)} %get-tuple-element.15), channel_id=1, source_target_pairs={{0,8},{1,5},{2,10},{3,7},{4,12},{5,1},{6,14},{7,3},{8,0},{9,13},{1... | collective-permute-start | bytes 786440 | tf_op jit(solution)/shard_map/ppermute | solution.py:163
  5.2 15.3 %collective-permute-start.1 = (bf16[2,64,1024]{2,1,0:T(8,128)(2,1)S(1)}, bf16[2,64,1024]{2,1,0:T(8,128)(2,1)S(1)}, u32[]{:S(2)}, u32[]{:S(2)}) collective-permute-start(bf16[2,64,1024]{2,1,0:T(8,128)(2,1)S(1)} %get-tuple-element.14), channel_id=1, source_target_pairs={{0,4},{1,9},{2,6},{3,11},{4,0},{5,13},{6,2},{7,15},{8,12},{9,1},{1... | collective-permute-start | bytes 786440 | tf_op jit(solution)/shard_map/ppermute | solution.py:163
  6.7 13.8 %copy-start.1 = (bf16[256,256]{1,0:T(8,128)(2,1)S(1)}, bf16[256,256]{1,0:T(8,128)(2,1)}, u32[]{:S(2)}) copy-start(bf16[256,256]{1,0:T(8,128)(2,1)} %constant.72.clone.refs_6_.matrix_ref) | copy-start | bytes 393220
  6.7 13.8 %collective-permute-start.2 = (bf16[2,64,1024]{2,1,0:T(8,128)(2,1)S(1)}, bf16[2,64,1024]{2,1,0:T(8,128)(2,1)S(1)}, u32[]{:S(2)}, u32[]{:S(2)}) collective-permute-start(bf16[2,64,1024]{2,1,0:T(8,128)(2,1)S(1)} %get-tuple-element.13), channel_id=1, source_target_pairs={{0,12},{1,13},{2,14},{3,15},{4,8},{5,9},{6,10},{7,11},{8,4},{9,5},... | collective-permute-start | bytes 786440 | tf_op jit(solution)/shard_map/ppermute | solution.py:163
  7.6 12.9 %all-to-all-start = ((f32[8,1,128]{2,1,0:T(1,128)}), f32[8,1,128]{2,1,0:T(1,128)S(1)}, u32[]{:S(2)}, u32[]{:S(2)}) async-start(f32[8,1,128]{2,1,0:T(1,128)} %bitcast.7), calls=%async_computation | async-start | bytes 8192 | tf_op jit(solution)/shard_map/all_to_all | solution.py:243
  13.8 6.8 %copy-start.4 = (s32[1,1024]{1,0:T(1,128)S(1)}, s32[1,1024]{1,0:T(1,128)}, u32[]{:S(2)}) copy-start(s32[1,1024]{1,0:T(1,128)} %sign_ref.1) | copy-start | bytes 12292
  21.1 8.9 %collective-permute-start.3 = (s16[64,1024]{1,0:T(8,128)(2,1)S(1)}, s16[64,1024]{1,0:T(8,128)(2,1)S(1)}, u32[]{:S(2)}, u32[]{:S(2)}) collective-permute-start(s16[64,1024]{1,0:T(8,128)(2,1)S(1)} %proxy_blocks.1), channel_id=1, source_target_pairs={{0,16},{1,17},{2,18},{3,19},{4,20},{5,21},{6,22},{7,23},{8,24},{9,... | collective-permute-start | bytes 393224 | tf_op jit(solution)/shard_map/ppermute | solution.py:163
  31.0 11.0 %all-to-all-start.1 = ((f32[32,1,128]{2,1,0:T(1,128)}), f32[32,1,128]{2,1,0:T(1,128)S(1)}, u32[]{:S(2)}, u32[]{:S(2)}) async-start(f32[32,1,128]{2,1,0:T(1,128)} %get-tuple-element.7), calls=%async_computation.1 | async-start | bytes 32768 | tf_op jit(solution)/shard_map/all_to_all | solution.py:278
  35.0 7.0 %copy-start.2 = (bf16[1,64,1024]{2,1,0:T(8,128)(2,1)S(1)}, bf16[1,64,1024]{2,1,0:T(8,128)(2,1)}, u32[]{:S(2)}) copy-start(bf16[1,64,1024]{2,1,0:T(8,128)(2,1)} %param.7) | copy-start | bytes 393220
  35.0 7.0 %copy-start.3 = (bf16[1,64,1024]{2,1,0:T(8,128)(2,1)S(1)}, bf16[1,64,1024]{2,1,0:T(8,128)(2,1)}, u32[]{:S(2)}) copy-start(bf16[1,64,1024]{2,1,0:T(8,128)(2,1)} %param.8) | copy-start | bytes 393220
  42.8 11.2 %collective-permute-start.4 = (bf16[64,1024]{1,0:T(8,128)(2,1)S(1)}, bf16[64,1024]{1,0:T(8,128)(2,1)S(1)}, u32[]{:S(2)}, u32[]{:S(2)}) collective-permute-start(bf16[64,1024]{1,0:T(8,128)(2,1)S(1)} %get-tuple-element.10), channel_id=1, source_target_pairs={{0,8},{1,5},{2,10},{3,7},{4,12},{5,1},{6,14},{7,3},{8,0},{9,13},{1... | collective-permute-start | bytes 393224 | tf_op jit(solution)/shard_map/ppermute | solution.py:163
  43.4 11.0 %collective-permute-start.5 = (bf16[64,1024]{1,0:T(8,128)(2,1)S(1)}, bf16[64,1024]{1,0:T(8,128)(2,1)S(1)}, u32[]{:S(2)}, u32[]{:S(2)}) collective-permute-start(bf16[64,1024]{1,0:T(8,128)(2,1)S(1)} %get-tuple-element.10), channel_id=1, source_target_pairs={{0,4},{1,9},{2,6},{3,11},{4,0},{5,13},{6,2},{7,15},{8,12},{9,1},{1... | collective-permute-start | bytes 393224 | tf_op jit(solution)/shard_map/ppermute | solution.py:163
  43.9 8.4 %collective-permute-start.7 = (bf16[64,1024]{1,0:T(8,128)(2,1)S(1)}, bf16[64,1024]{1,0:T(8,128)(2,1)S(1)}, u32[]{:S(2)}, u32[]{:S(2)}) collective-permute-start(bf16[64,1024]{1,0:T(8,128)(2,1)S(1)} %get-tuple-element.10), channel_id=1, source_target_pairs={{0,16},{1,17},{2,18},{3,19},{4,20},{5,21},{6,22},{7,23},{8,24},{9,... | collective-permute-start | bytes 393224 | tf_op jit(solution)/shard_map/ppermute | solution.py:163
  52.3 6.3 %collective-permute-start.8 = (bf16[64,1024]{1,0:T(8,128)(2,1)S(1)}, bf16[64,1024]{1,0:T(8,128)(2,1)S(1)}, u32[]{:S(2)}, u32[]{:S(2)}) collective-permute-start(bf16[64,1024]{1,0:T(8,128)(2,1)S(1)} %collective-permute-done.7), channel_id=1, source_target_pairs={{0,8},{1,5},{2,10},{3,7},{4,12},{5,1},{6,14},{7,3},{8,0},{9,13},{1... | collective-permute-start | bytes 393224 | tf_op jit(solution)/shard_map/ppermute | solution.py:163
  52.3 7.7 %collective-permute-start.9 = (bf16[64,1024]{1,0:T(8,128)(2,1)S(1)}, bf16[64,1024]{1,0:T(8,128)(2,1)S(1)}, u32[]{:S(2)}, u32[]{:S(2)}) collective-permute-start(bf16[64,1024]{1,0:T(8,128)(2,1)S(1)} %collective-permute-done.7), channel_id=1, source_target_pairs={{0,4},{1,9},{2,6},{3,11},{4,0},{5,13},{6,2},{7,15},{8,12},{9,1},{1... | collective-permute-start | bytes 393224 | tf_op jit(solution)/shard_map/ppermute | solution.py:163
  54.0 5.9 %collective-permute-start.6 = (bf16[64,1024]{1,0:T(8,128)(2,1)S(1)}, bf16[64,1024]{1,0:T(8,128)(2,1)S(1)}, u32[]{:S(2)}, u32[]{:S(2)}) collective-permute-start(bf16[64,1024]{1,0:T(8,128)(2,1)S(1)} %collective-permute-done.4), channel_id=1, source_target_pairs={{0,4},{1,9},{2,6},{3,11},{4,0},{5,13},{6,2},{7,15},{8,12},{9,1},{1... | collective-permute-start | bytes 393224 | tf_op jit(solution)/shard_map/ppermute | solution.py:163
  58.6 5.0 %collective-permute-start.10 = (bf16[64,1024]{1,0:T(8,128)(2,1)S(1)}, bf16[64,1024]{1,0:T(8,128)(2,1)S(1)}, u32[]{:S(2)}, u32[]{:S(2)}) collective-permute-start(bf16[64,1024]{1,0:T(8,128)(2,1)S(1)} %collective-permute-done.8), channel_id=1, source_target_pairs={{0,4},{1,9},{2,6},{3,11},{4,0},{5,13},{6,2},{7,15},{8,12},{9,1},{1... | collective-permute-start | bytes 393224 | tf_op jit(solution)/shard_map/ppermute | solution.py:163
  63.6 1.0 %copy-start.5 = (bf16[8,64,1024]{2,1,0:T(8,128)(2,1)}, bf16[8,64,1024]{2,1,0:T(8,128)(2,1)S(1)}, u32[]{:S(2)}) copy-start(bf16[8,64,1024]{2,1,0:T(8,128)(2,1)S(1)} %bitcast_dynamic-update-slice_fusion) | copy-start | bytes 3145732

commit v10 on v7

--- a/solution.py
+++ b/solution.py
@@ -139,15 +139,24 @@
         unrot_ref[:, cut] = group * back * signs[:, cut]
 
 
-def update_kernel(limit, square_ref, unrot_ref, weight_ref, comp_ref, new_ref, update_ref):
+def clip_factor(limit, square_ref):
     squares = jnp.sum(square_ref[...], axis=0, keepdims=True)[:, 0:1]
-    factor = limit / jnp.maximum(jnp.sqrt(squares), limit)
-    update = unrot_ref[...] * factor
-    update_ref[...] = update
+    return limit / jnp.maximum(jnp.sqrt(squares), limit)
+
+
+def weights_kernel(limit, square_ref, unrot_ref, weight_ref, comp_ref, new_ref, *part_refs):
+    update = unrot_ref[...] * clip_factor(limit, square_ref)
     summed = weight_ref[...].astype(jnp.float32) + (
         comp_ref[...].astype(jnp.float32) - learn_rate * update
     )
     new_ref[...] = summed.astype(jnp.bfloat16)
+    for p, part_ref in enumerate(part_refs):
+        rows = part_ref.shape[0]
+        part_ref[...] = summed[p * rows : (p + 1) * rows].astype(jnp.bfloat16)
+
+
+def update_kernel(limit, square_ref, unrot_ref, update_ref):
+    update_ref[...] = unrot_ref[...] * clip_factor(limit, square_ref)
 
 
 def swap(value, mask):
@@ -155,29 +164,29 @@
     return lax.ppermute(value, "dp", [(i, i ^ mask) for i in range(size)])
 
 
-def gather_blocks(block, replicas):
+def gather_blocks(block, parts, replicas):
     x_count = 1 << ((replicas.bit_length() - 1) // 2)
     near = replicas // 2
     me = lax.axis_index("dp")
     owned, width = block.shape
-    parts = 2 if owned % 32 == 0 else 1
-    rows = owned // parts
-    pieces = []
-
-    def spread(start, piece, row):
-        pieces.append((start, row, piece))
-        along = {0: piece}
-        for z in range(x_count, near, x_count):
-            along[z] = swap(piece, z)
-            pieces.append((start + z, row, along[z]))
-        for z in range(0, near, x_count):
-            for x in range(1, x_count):
-                pieces.append((start + z + x, row, swap(along[z], x)))
-
-    across = [swap(block[p * rows : (p + 1) * rows], near) for p in range(parts)]
-    spread(0, block, 0)
+    rows = owned // len(parts)
+    along_x = range(1, x_count)
+    along_z = range(x_count, near, x_count)
+    across = [swap(part, near) for part in parts]
+    pieces = [(near, p * rows, piece) for p, piece in enumerate(across)] + [(0, 0, block)]
+    own_x = {x: swap(block, x) for x in along_x}
+    own_z = {z: swap(block, z) for z in along_z}
+    pieces += [(mask, 0, piece) for mask, piece in (own_x | own_z).items()]
     for p, piece in enumerate(across):
-        spread(near, piece, p * rows)
+        row = p * rows
+        moved = {z: swap(piece, z) for z in along_z}
+        pieces += [(near + z, row, value) for z, value in moved.items()]
+        moved[0] = piece
+        for z, value in moved.items():
+            pieces += [(near + z + x, row, swap(value, x)) for x in along_x]
+    for x, piece in own_x.items():
+        piece, _ = lax.optimization_barrier((piece, across[-1]))
+        pieces += [(x + z, 0, swap(piece, z)) for z in along_z]
     out = jnp.zeros((replicas, owned, width), block.dtype)
     for mask, row, piece in pieces:
         out = lax.dynamic_update_slice(out, piece[None], (me ^ mask, row, 0))
@@ -251,21 +260,22 @@
     )(total, mean_scale, signs, matrix)
     squares = lax.all_to_all(squares, ("dp", "expert"), split_axis=0, concat_axis=0, tiled=True)
     limit = target_rms * math.sqrt(blocks * width * lax.axis_size("expert"))
-    new_weights, update_grad = pl.pallas_call(
+    squares = squares.reshape(devices, lanes)
+    count = 2 if owned % 32 == 0 else 1
+    new_weights, *parts = pl.pallas_call(
+        functools.partial(weights_kernel, limit),
+        out_shape=[jax.ShapeDtypeStruct((owned, width), jnp.bfloat16)]
+        + [jax.ShapeDtypeStruct((owned // count, width), jnp.bfloat16)] * count,
+        compiler_params=params,
+        name="new_weights",
+    )(squares, unrot, weights.reshape(owned, width), compensation.reshape(owned, width))
+    update_grad = pl.pallas_call(
         functools.partial(update_kernel, limit),
-        out_shape=(
-            jax.ShapeDtypeStruct((owned, width), jnp.bfloat16),
-            jax.ShapeDtypeStruct((owned, width), jnp.float32),
-        ),
-        compiler_params=pltpu.CompilerParams(vmem_limit_bytes=vmem_bytes),
-        name="update_blocks",
-    )(
-        squares.reshape(devices, lanes),
-        unrot,
-        weights.reshape(owned, width),
-        compensation.reshape(owned, width),
-    )
-    return gather_blocks(new_weights, replicas), update_grad.reshape(weights.shape)
+        out_shape=jax.ShapeDtypeStruct((owned, width), jnp.float32),
+        compiler_params=params,
+        name="update_grad",
+    )(squares, unrot)
+    return gather_blocks(new_weights, parts, replicas), update_grad.reshape(weights.shape)
 
 
 def solution(mesh):

time: 61.8 us -> 59.6 us (0.964)
  waiting for transfers between devices: 22.9 us -> 21.2 us
    ppermute x18, waiting for transfers between devices: 13.5 us -> 11.8 us  [swap(): return lax.ppermute(value, 'dp', [(i, i ^ mask) for i in range(size)])]
  transfers between devices with their start and end apart: 20 -> 20, of which waited for: 8 -> 9; matrix products, arithmetic and copies ran while one was open for 1% -> 1% of each run, Pallas kernels for 4% -> 5%
where the time goes in v10:
time: 59.6 us; the launch traced here: 59.4 us
  starting transfers between devices  29.4 us (49%)
  waiting for transfers between devices  21.2 us (36%)
  Pallas kernels  4.25 us (7%)
  local copies, waits for them, and re-layouts  3.6 us (6%)
  between operations  0.9 us (2%)
    ppermute x18, starting transfers between devices, swap(): return lax.ppermute(value, 'dp', [(i, i ^ mask) for i in range(size)])  19.9 us
    ppermute x18, waiting for transfers between devices, swap(): return lax.ppermute(value, 'dp', [(i, i ^ mask) for i in range(size)])  11.8 us
    all_to_all x1, waiting for transfers between devices, on_device(): lax.all_to_all(squares, ('dp', 'expert'), split_axis=0, concat_axis=0, ti...  6.72 us
    all_to_all x1, starting transfers between devices, on_device(): lax.all_to_all(sums.reshape(replicas, 1, 2 * owned), 'dp', split_axis=0,...  6.22 us
    all_to_all x1, starting transfers between devices, on_device(): lax.all_to_all(squares, ('dp', 'expert'), split_axis=0, concat_axis=0, ti...  3.29 us
    all_to_all x1, waiting for transfers between devices, on_device(): lax.all_to_all(sums.reshape(replicas, 1, 2 * owned), 'dp', split_axis=0,...  2.69 us
    unnamed x14, local copies, waits for them, and re-layouts  2.22 us
  transfers between devices with their start and end apart: 20, of which 9 were waited for; matrix products, arithmetic and copies ran while one was open for 1% of the time, Pallas kernels for 5%

profile of v10, /device:TPU:0, one launch (start us, length us, event | category | flops | bytes accessed | tf_op | source)
XLA Modules:
  0.0 59.4 jit_solution(17139437884248980857)
XLA Ops:
  0.7 1.1 %dynamic-slice_bitcast_fusion.1 = (bf16[64,1024]{1,0:T(8,128)(2,1)S(1)}, bf16[64,1024]{1,0:T(8,128)(2,1)S(1)}, bf16[64,1024]{1,0:T(8,128)(2,1)S(1)}) fusion(bf16[8,64,1024]{2,1,0:T(8,128)(2,1)} %bitcast.53, s32[]{:T(128)S(6)} %select_n.54, s32[]{:T(128)S(6)} %select_n.53, s32[]{:T(128)S(6)} %select_n.52), kind=kLoop, calls=%fused_computation.5 | loop fusion | bytes 786444 | tf_op jit(solution)/shard_map/reshape | solution.py:212
  1.7 3.0 %collective-permute-start.3 = (bf16[64,1024]{1,0:T(8,128)(2,1)S(1)}, bf16[64,1024]{1,0:T(8,128)(2,1)S(1)}, u32[]{:S(2)}, u32[]{:S(2)}) collective-permute-start(bf16[64,1024]{1,0:T(8,128)(2,1)S(1)} %get-tuple-element.27), channel_id=1, source_target_pairs={{0,4},{4,0},{8,12},{12,8},{16,20},{20,16},{24,28},{28,24},{1,5},{5... | collective-permute-start | bytes 393224 | tf_op jit(solution)/shard_map/ppermute | solution.py:164
  4.7 1.6 %collective-permute-start.4 = (bf16[64,1024]{1,0:T(8,128)(2,1)S(1)}, bf16[64,1024]{1,0:T(8,128)(2,1)S(1)}, u32[]{:S(2)}, u32[]{:S(2)}) collective-permute-start(bf16[64,1024]{1,0:T(8,128)(2,1)S(1)} %get-tuple-element.26), channel_id=1, source_target_pairs={{0,8},{4,12},{8,0},{12,4},{16,24},{20,28},{24,16},{28,20},{1,9},{5... | collective-permute-start | bytes 393224 | tf_op jit(solution)/shard_map/ppermute | solution.py:164
  6.3 1.2 %copy-done = bf16[1,1,512,1024]{3,2,1,0:T(8,128)(2,1)S(1)} copy-done((bf16[1,1,512,1024]{3,2,1,0:T(8,128)(2,1)S(1)}, bf16[1,1,512,1024]{3,2,1,0:T(8,128)(2,1)}, u32[]{:S(2)}) %copy-start) | copy-done | bytes 1048600
  7.5 0.9 %sum_squares.1 = f32[2,4,1,128]{3,2,1,0:T(1,128)} custom-call(bf16[2,4,64,1024]{3,2,1,0:T(8,128)(2,1)S(1)} %bitcast.54), custom_call_target="tpu_custom_call" | custom-call | tf_op jit(solution)/shard_map/sum_squares/pallas_call | solution.py:215
  8.4 6.2 %all-to-all-start = ((f32[8,1,128]{2,1,0:T(1,128)}), f32[8,1,128]{2,1,0:T(1,128)S(1)}, u32[]{:S(2)}, u32[]{:S(2)}) async-start(f32[8,1,128]{2,1,0:T(1,128)} %bitcast.8), calls=%async_computation | async-start | bytes 8192 | tf_op jit(solution)/shard_map/all_to_all | solution.py:223
  14.7 2.1 %collective-permute-start = (bf16[64,1024]{1,0:T(8,128)(2,1)S(1)}, bf16[64,1024]{1,0:T(8,128)(2,1)S(1)}, u32[]{:S(2)}, u32[]{:S(2)}) collective-permute-start(bf16[64,1024]{1,0:T(8,128)(2,1)S(1)} %get-tuple-element.24), channel_id=1, source_target_pairs={{0,4},{4,0},{8,12},{12,8},{16,20},{20,16},{24,28},{28,24},{1,5},{5... | collective-permute-start | bytes 393224 | tf_op jit(solution)/shard_map/ppermute | solution.py:164
  16.8 1.5 %collective-permute-start.1 = (bf16[64,1024]{1,0:T(8,128)(2,1)S(1)}, bf16[64,1024]{1,0:T(8,128)(2,1)S(1)}, u32[]{:S(2)}, u32[]{:S(2)}) collective-permute-start(bf16[64,1024]{1,0:T(8,128)(2,1)S(1)} %get-tuple-element.23), channel_id=1, source_target_pairs={{0,8},{4,12},{8,0},{12,4},{16,24},{20,28},{24,16},{28,20},{1,9},{5... | collective-permute-start | bytes 393224 | tf_op jit(solution)/shard_map/ppermute | solution.py:164
  18.3 2.7 %all-to-all-done = f32[8,1,128]{2,1,0:T(1,128)S(1)} async-done(((f32[8,1,128]{2,1,0:T(1,128)}), f32[8,1,128]{2,1,0:T(1,128)S(1)}, u32[]{:S(2)}, u32[]{:S(2)}) %all-to-all-start) | async-done | bytes 4128 | tf_op jit(solution)/shard_map/all_to_all | solution.py:223
  22.3 3.2 %collective-permute-done.2.refs_2_ = bf16[64,1024]{1,0:T(8,128)(2,1)S(1)} collective-permute-done((bf16[64,1024]{1,0:T(8,128)(2,1)S(1)}, bf16[64,1024]{1,0:T(8,128)(2,1)S(1)}, u32[]{:S(2)}, u32[]{:S(2)}) %collective-permute-start.2) | collective-permute-done | bytes 131104 | tf_op jit(solution)/shard_map/ppermute | solution.py:164
  26.1 2.9 %collective-permute-done.6.far_ref = s16[64,1024]{1,0:T(8,128)(2,1)S(1)} collective-permute-done((s16[64,1024]{1,0:T(8,128)(2,1)S(1)}, s16[64,1024]{1,0:T(8,128)(2,1)S(1)}, u32[]{:S(2)}, u32[]{:S(2)}) %collective-permute-start.6) | collective-permute-done | bytes 131104 | tf_op jit(solution)/shard_map/ppermute | solution.py:164
  29.0 0.9 %finish_blocks.1 = (f32[64,1024]{1,0:T(8,128)S(1)}, f32[64,128]{1,0:T(8,128)S(1)}, f32[32,1,128]{2,1,0:T(1,128)}) custom-call(s32[1,1]{1,0:T(1,128)} %bitcast.offset_ref, f32[64,1024]{1,0:T(8,128)S(1)} %owner_blocks.1.near_ref, s16[64,1024]{1,0:T(8,128)(2,1)S(1)} %collective-permute-done.6.far_ref, f32[8,128]{1,0:T(8,128)S(1)} %bitcast.62), custom_call_target="tpu_custom_call" | custom-call | tf_op jit(solution)/shard_map/finish_blocks/pallas_call | solution.py:244
  29.9 3.3 %all-to-all-start.1 = ((f32[32,1,128]{2,1,0:T(1,128)}), f32[32,1,128]{2,1,0:T(1,128)S(1)}, u32[]{:S(2)}, u32[]{:S(2)}) async-start(f32[32,1,128]{2,1,0:T(1,128)} %get-tuple-element.13), calls=%async_computation.1 | async-start | bytes 32768 | tf_op jit(solution)/shard_map/all_to_all | solution.py:261
  33.6 6.7 %all-to-all-done.1 = f32[32,1,128]{2,1,0:T(1,128)S(1)} async-done(((f32[32,1,128]{2,1,0:T(1,128)}), f32[32,1,128]{2,1,0:T(1,128)S(1)}, u32[]{:S(2)}, u32[]{:S(2)}) %all-to-all-start.1) | async-done | bytes 16416 | tf_op jit(solution)/shard_map/all_to_all | solution.py:261
  43.0 2.4 %collective-permute-start.8 = (bf16[32,1024]{1,0:T(8,128)(2,1)S(1)}, bf16[32,1024]{1,0:T(8,128)(2,1)S(1)}, u32[]{:S(2)}, u32[]{:S(2)}) collective-permute-start(bf16[32,1024]{1,0:T(8,128)(2,1)S(1)} %get-tuple-element.17), channel_id=1, source_target_pairs={{0,16},{4,20},{8,24},{12,28},{16,0},{20,4},{24,8},{28,12},{1,17},{... | collective-permute-start | bytes 196616 | tf_op jit(solution)/shard_map/ppermute | solution.py:164
  45.4 1.8 %collective-permute-done.7 = bf16[32,1024]{1,0:T(8,128)(2,1)S(1)} collective-permute-done((bf16[32,1024]{1,0:T(8,128)(2,1)S(1)}, bf16[32,1024]{1,0:T(8,128)(2,1)S(1)}, u32[]{:S(2)}, u32[]{:S(2)}) %collective-permute-start.7) | collective-permute-done | bytes 65568 | tf_op jit(solution)/shard_map/ppermute | solution.py:164
  47.2 1.2 %collective-permute-start.13 = (bf16[32,1024]{1,0:T(8,128)(2,1)S(1)}, bf16[32,1024]{1,0:T(8,128)(2,1)S(1)}, u32[]{:S(2)}, u32[]{:S(2)}) collective-permute-start(bf16[32,1024]{1,0:T(8,128)(2,1)S(1)} %collective-permute-done.7), channel_id=1, source_target_pairs={{0,4},{4,0},{8,12},{12,8},{16,20},{20,16},{24,28},{28,24},{1,5},{5... | collective-permute-start | bytes 196616 | tf_op jit(solution)/shard_map/ppermute | solution.py:164
  48.7 2.5 %collective-permute-start.14 = (bf16[32,1024]{1,0:T(8,128)(2,1)S(1)}, bf16[32,1024]{1,0:T(8,128)(2,1)S(1)}, u32[]{:S(2)}, u32[]{:S(2)}) collective-permute-start(bf16[32,1024]{1,0:T(8,128)(2,1)S(1)} %collective-permute-done.8), channel_id=1, source_target_pairs={{0,8},{4,12},{8,0},{12,4},{16,24},{20,28},{24,16},{28,20},{1,9},{5... | collective-permute-start | bytes 196616 | tf_op jit(solution)/shard_map/ppermute | solution.py:164
  51.2 1.2 %collective-permute-start.16 = (bf16[32,1024]{1,0:T(8,128)(2,1)S(1)}, bf16[32,1024]{1,0:T(8,128)(2,1)S(1)}, u32[]{:S(2)}, u32[]{:S(2)}) collective-permute-start(bf16[32,1024]{1,0:T(8,128)(2,1)S(1)} %collective-permute-done.8), channel_id=1, source_target_pairs={{0,4},{4,0},{8,12},{12,8},{16,20},{20,16},{24,28},{28,24},{1,5},{5... | collective-permute-start | bytes 196616 | tf_op jit(solution)/shard_map/ppermute | solution.py:164
  52.5 1.0 %collective-permute-start.12 = (bf16[32,1024]{1,0:T(8,128)(2,1)S(1)}, bf16[32,1024]{1,0:T(8,128)(2,1)S(1)}, u32[]{:S(2)}, u32[]{:S(2)}) collective-permute-start(bf16[32,1024]{1,0:T(8,128)(2,1)S(1)} %collective-permute-done.11), channel_id=1, source_target_pairs={{0,4},{4,0},{8,12},{12,8},{16,20},{20,16},{24,28},{28,24},{1,5},{5... | collective-permute-start | bytes 196616 | tf_op jit(solution)/shard_map/ppermute | solution.py:164
  54.1 1.1 %collective-permute-start.15 = (bf16[32,1024]{1,0:T(8,128)(2,1)S(1)}, bf16[32,1024]{1,0:T(8,128)(2,1)S(1)}, u32[]{:S(2)}, u32[]{:S(2)}) collective-permute-start(bf16[32,1024]{1,0:T(8,128)(2,1)S(1)} %collective-permute-done.14), channel_id=1, source_target_pairs={{0,4},{4,0},{8,12},{12,8},{16,20},{20,16},{24,28},{28,24},{1,5},{5... | collective-permute-start | bytes 196616 | tf_op jit(solution)/shard_map/ppermute | solution.py:164
  55.2 1.6 %collective-permute-done.12 = bf16[32,1024]{1,0:T(8,128)(2,1)S(1)} collective-permute-done((bf16[32,1024]{1,0:T(8,128)(2,1)S(1)}, bf16[32,1024]{1,0:T(8,128)(2,1)S(1)}, u32[]{:S(2)}, u32[]{:S(2)}) %collective-permute-start.12) | collective-permute-done | bytes 65568 | tf_op jit(solution)/shard_map/ppermute | solution.py:164
  56.9 1.4 %collective-permute-done.15 = bf16[32,1024]{1,0:T(8,128)(2,1)S(1)} collective-permute-done((bf16[32,1024]{1,0:T(8,128)(2,1)S(1)}, bf16[32,1024]{1,0:T(8,128)(2,1)S(1)}, u32[]{:S(2)}, u32[]{:S(2)}) %collective-permute-start.15) | collective-permute-done | bytes 65568 | tf_op jit(solution)/shard_map/ppermute | solution.py:164
  58.4 1.0 %copy-done.6 = bf16[8,64,1024]{2,1,0:T(8,128)(2,1)} copy-done((bf16[8,64,1024]{2,1,0:T(8,128)(2,1)}, bf16[8,64,1024]{2,1,0:T(8,128)(2,1)S(1)}, u32[]{:S(2)}) %copy-start.6) | copy-done | bytes 1048600
  (52 shorter events, 6.2 us)
Async XLA Ops:
  1.7 16.5 %collective-permute-start.3 = (bf16[64,1024]{1,0:T(8,128)(2,1)S(1)}, bf16[64,1024]{1,0:T(8,128)(2,1)S(1)}, u32[]{:S(2)}, u32[]{:S(2)}) collective-permute-start(bf16[64,1024]{1,0:T(8,128)(2,1)S(1)} %get-tuple-element.27), channel_id=1, source_target_pairs={{0,4},{4,0},{8,12},{12,8},{16,20},{20,16},{24,28},{28,24},{1,5},{5... | collective-permute-start | bytes 393224 | tf_op jit(solution)/shard_map/ppermute | solution.py:164
  4.7 16.3 %collective-permute-start.4 = (bf16[64,1024]{1,0:T(8,128)(2,1)S(1)}, bf16[64,1024]{1,0:T(8,128)(2,1)S(1)}, u32[]{:S(2)}, u32[]{:S(2)}) collective-permute-start(bf16[64,1024]{1,0:T(8,128)(2,1)S(1)} %get-tuple-element.26), channel_id=1, source_target_pairs={{0,8},{4,12},{8,0},{12,4},{16,24},{20,28},{24,16},{28,20},{1,9},{5... | collective-permute-start | bytes 393224 | tf_op jit(solution)/shard_map/ppermute | solution.py:164
  6.3 14.7 %collective-permute-start.5 = (bf16[64,1024]{1,0:T(8,128)(2,1)S(1)}, bf16[64,1024]{1,0:T(8,128)(2,1)S(1)}, u32[]{:S(2)}, u32[]{:S(2)}) collective-permute-start(bf16[64,1024]{1,0:T(8,128)(2,1)S(1)} %get-tuple-element.25), channel_id=1, source_target_pairs={{0,12},{4,8},{8,4},{12,0},{16,28},{20,24},{24,20},{28,16},{1,13},{... | collective-permute-start | bytes 393224 | tf_op jit(solution)/shard_map/ppermute | solution.py:164
  7.5 7.1 %copy-start.1 = (bf16[1,1,512,1024]{3,2,1,0:T(8,128)(2,1)S(1)}, bf16[1,1,512,1024]{3,2,1,0:T(8,128)(2,1)}, u32[]{:S(2)}) copy-start(bf16[1,1,512,1024]{3,2,1,0:T(8,128)(2,1)} %param.5) | copy-start | bytes 3145732
  8.4 12.6 %all-to-all-start = ((f32[8,1,128]{2,1,0:T(1,128)}), f32[8,1,128]{2,1,0:T(1,128)S(1)}, u32[]{:S(2)}, u32[]{:S(2)}) async-start(f32[8,1,128]{2,1,0:T(1,128)} %bitcast.8), calls=%async_computation | async-start | bytes 8192 | tf_op jit(solution)/shard_map/all_to_all | solution.py:223
  14.6 6.4 %copy-start.2 = (bf16[256,256]{1,0:T(8,128)(2,1)S(1)}, bf16[256,256]{1,0:T(8,128)(2,1)}, u32[]{:S(2)}) copy-start(bf16[256,256]{1,0:T(8,128)(2,1)} %constant.43.clone.refs_6_.matrix_ref) | copy-start | bytes 393220
  14.7 7.6 %collective-permute-start = (bf16[64,1024]{1,0:T(8,128)(2,1)S(1)}, bf16[64,1024]{1,0:T(8,128)(2,1)S(1)}, u32[]{:S(2)}, u32[]{:S(2)}) collective-permute-start(bf16[64,1024]{1,0:T(8,128)(2,1)S(1)} %get-tuple-element.24), channel_id=1, source_target_pairs={{0,4},{4,0},{8,12},{12,8},{16,20},{20,16},{24,28},{28,24},{1,5},{5... | collective-permute-start | bytes 393224 | tf_op jit(solution)/shard_map/ppermute | solution.py:164
  16.8 5.5 %collective-permute-start.1 = (bf16[64,1024]{1,0:T(8,128)(2,1)S(1)}, bf16[64,1024]{1,0:T(8,128)(2,1)S(1)}, u32[]{:S(2)}, u32[]{:S(2)}) collective-permute-start(bf16[64,1024]{1,0:T(8,128)(2,1)S(1)} %get-tuple-element.23), channel_id=1, source_target_pairs={{0,8},{4,12},{8,0},{12,4},{16,24},{20,28},{24,16},{28,20},{1,9},{5... | collective-permute-start | bytes 393224 | tf_op jit(solution)/shard_map/ppermute | solution.py:164
  18.3 7.3 %collective-permute-start.2 = (bf16[64,1024]{1,0:T(8,128)(2,1)S(1)}, bf16[64,1024]{1,0:T(8,128)(2,1)S(1)}, u32[]{:S(2)}, u32[]{:S(2)}) collective-permute-start(bf16[64,1024]{1,0:T(8,128)(2,1)S(1)} %get-tuple-element.22), channel_id=1, source_target_pairs={{0,12},{4,8},{8,4},{12,0},{16,28},{20,24},{24,20},{28,16},{1,13},{... | collective-permute-start | bytes 393224 | tf_op jit(solution)/shard_map/ppermute | solution.py:164
  21.7 7.3 %collective-permute-start.6 = (s16[64,1024]{1,0:T(8,128)(2,1)S(1)}, s16[64,1024]{1,0:T(8,128)(2,1)S(1)}, u32[]{:S(2)}, u32[]{:S(2)}) collective-permute-start(s16[64,1024]{1,0:T(8,128)(2,1)S(1)} %proxy_blocks.1), channel_id=1, source_target_pairs={{0,16},{4,20},{8,24},{12,28},{16,0},{20,4},{24,8},{28,12},{1,17},{... | collective-permute-start | bytes 393224 | tf_op jit(solution)/shard_map/ppermute | solution.py:164
  29.9 10.4 %all-to-all-start.1 = ((f32[32,1,128]{2,1,0:T(1,128)}), f32[32,1,128]{2,1,0:T(1,128)S(1)}, u32[]{:S(2)}, u32[]{:S(2)}) async-start(f32[32,1,128]{2,1,0:T(1,128)} %get-tuple-element.13), calls=%async_computation.1 | async-start | bytes 32768 | tf_op jit(solution)/shard_map/all_to_all | solution.py:261
  33.2 7.1 %copy-start.3 = (bf16[1,64,1024]{2,1,0:T(8,128)(2,1)S(1)}, bf16[1,64,1024]{2,1,0:T(8,128)(2,1)}, u32[]{:S(2)}) copy-start(bf16[1,64,1024]{2,1,0:T(8,128)(2,1)} %param.7) | copy-start | bytes 393220
  33.2 7.1 %copy-start.4 = (bf16[1,64,1024]{2,1,0:T(8,128)(2,1)S(1)}, bf16[1,64,1024]{2,1,0:T(8,128)(2,1)}, u32[]{:S(2)}) copy-start(bf16[1,64,1024]{2,1,0:T(8,128)(2,1)} %param.8) | copy-start | bytes 393220
  40.5 6.7 %collective-permute-start.7 = (bf16[32,1024]{1,0:T(8,128)(2,1)S(1)}, bf16[32,1024]{1,0:T(8,128)(2,1)S(1)}, u32[]{:S(2)}, u32[]{:S(2)}) collective-permute-start(bf16[32,1024]{1,0:T(8,128)(2,1)S(1)} %get-tuple-element.16), channel_id=1, source_target_pairs={{0,16},{4,20},{8,24},{12,28},{16,0},{20,4},{24,8},{28,12},{1,17},{... | collective-permute-start | bytes 196616 | tf_op jit(solution)/shard_map/ppermute | solution.py:164
  41.1 10.1 %collective-permute-start.9 = (bf16[64,1024]{1,0:T(8,128)(2,1)S(1)}, bf16[64,1024]{1,0:T(8,128)(2,1)S(1)}, u32[]{:S(2)}, u32[]{:S(2)}) collective-permute-start(bf16[64,1024]{1,0:T(8,128)(2,1)S(1)} %get-tuple-element.18), channel_id=1, source_target_pairs={{0,4},{4,0},{8,12},{12,8},{16,20},{20,16},{24,28},{28,24},{1,5},{5... | collective-permute-start | bytes 393224 | tf_op jit(solution)/shard_map/ppermute | solution.py:164
  41.7 10.8 %collective-permute-start.10 = (bf16[64,1024]{1,0:T(8,128)(2,1)S(1)}, bf16[64,1024]{1,0:T(8,128)(2,1)S(1)}, u32[]{:S(2)}, u32[]{:S(2)}) collective-permute-start(bf16[64,1024]{1,0:T(8,128)(2,1)S(1)} %get-tuple-element.18), channel_id=1, source_target_pairs={{0,8},{4,12},{8,0},{12,4},{16,24},{20,28},{24,16},{28,20},{1,9},{5... | collective-permute-start | bytes 393224 | tf_op jit(solution)/shard_map/ppermute | solution.py:164
  43.0 5.7 %collective-permute-start.8 = (bf16[32,1024]{1,0:T(8,128)(2,1)S(1)}, bf16[32,1024]{1,0:T(8,128)(2,1)S(1)}, u32[]{:S(2)}, u32[]{:S(2)}) collective-permute-start(bf16[32,1024]{1,0:T(8,128)(2,1)S(1)} %get-tuple-element.17), channel_id=1, source_target_pairs={{0,16},{4,20},{8,24},{12,28},{16,0},{20,4},{24,8},{28,12},{1,17},{... | collective-permute-start | bytes 196616 | tf_op jit(solution)/shard_map/ppermute | solution.py:164
  47.2 5.4 %collective-permute-start.11 = (bf16[32,1024]{1,0:T(8,128)(2,1)S(1)}, bf16[32,1024]{1,0:T(8,128)(2,1)S(1)}, u32[]{:S(2)}, u32[]{:S(2)}) collective-permute-start(bf16[32,1024]{1,0:T(8,128)(2,1)S(1)} %collective-permute-done.7), channel_id=1, source_target_pairs={{0,8},{4,12},{8,0},{12,4},{16,24},{20,28},{24,16},{28,20},{1,9},{5... | collective-permute-start | bytes 196616 | tf_op jit(solution)/shard_map/ppermute | solution.py:164
  47.2 9.7 %collective-permute-start.13 = (bf16[32,1024]{1,0:T(8,128)(2,1)S(1)}, bf16[32,1024]{1,0:T(8,128)(2,1)S(1)}, u32[]{:S(2)}, u32[]{:S(2)}) collective-permute-start(bf16[32,1024]{1,0:T(8,128)(2,1)S(1)} %collective-permute-done.7), channel_id=1, source_target_pairs={{0,4},{4,0},{8,12},{12,8},{16,20},{20,16},{24,28},{28,24},{1,5},{5... | collective-permute-start | bytes 196616 | tf_op jit(solution)/shard_map/ppermute | solution.py:164
  48.7 5.4 %collective-permute-start.14 = (bf16[32,1024]{1,0:T(8,128)(2,1)S(1)}, bf16[32,1024]{1,0:T(8,128)(2,1)S(1)}, u32[]{:S(2)}, u32[]{:S(2)}) collective-permute-start(bf16[32,1024]{1,0:T(8,128)(2,1)S(1)} %collective-permute-done.8), channel_id=1, source_target_pairs={{0,8},{4,12},{8,0},{12,4},{16,24},{20,28},{24,16},{28,20},{1,9},{5... | collective-permute-start | bytes 196616 | tf_op jit(solution)/shard_map/ppermute | solution.py:164
  51.2 7.1 %collective-permute-start.16 = (bf16[32,1024]{1,0:T(8,128)(2,1)S(1)}, bf16[32,1024]{1,0:T(8,128)(2,1)S(1)}, u32[]{:S(2)}, u32[]{:S(2)}) collective-permute-start(bf16[32,1024]{1,0:T(8,128)(2,1)S(1)} %collective-permute-done.8), channel_id=1, source_target_pairs={{0,4},{4,0},{8,12},{12,8},{16,20},{20,16},{24,28},{28,24},{1,5},{5... | collective-permute-start | bytes 196616 | tf_op jit(solution)/shard_map/ppermute | solution.py:164
  52.4 6.0 %collective-permute-start.17 = (bf16[64,1024]{1,0:T(8,128)(2,1)S(1)}, bf16[64,1024]{1,0:T(8,128)(2,1)S(1)}, u32[]{:S(2)}, u32[]{:S(2)}) collective-permute-start(bf16[64,1024]{1,0:T(8,128)(2,1)S(1)} %collective-permute-done.9), channel_id=1, source_target_pairs={{0,8},{4,12},{8,0},{12,4},{16,24},{20,28},{24,16},{28,20},{1,9},{5... | collective-permute-start | bytes 393224 | tf_op jit(solution)/shard_map/ppermute | solution.py:164
  52.5 4.3 %collective-permute-start.12 = (bf16[32,1024]{1,0:T(8,128)(2,1)S(1)}, bf16[32,1024]{1,0:T(8,128)(2,1)S(1)}, u32[]{:S(2)}, u32[]{:S(2)}) collective-permute-start(bf16[32,1024]{1,0:T(8,128)(2,1)S(1)} %collective-permute-done.11), channel_id=1, source_target_pairs={{0,4},{4,0},{8,12},{12,8},{16,20},{20,16},{24,28},{28,24},{1,5},{5... | collective-permute-start | bytes 196616 | tf_op jit(solution)/shard_map/ppermute | solution.py:164
  54.1 4.3 %collective-permute-start.15 = (bf16[32,1024]{1,0:T(8,128)(2,1)S(1)}, bf16[32,1024]{1,0:T(8,128)(2,1)S(1)}, u32[]{:S(2)}, u32[]{:S(2)}) collective-permute-start(bf16[32,1024]{1,0:T(8,128)(2,1)S(1)} %collective-permute-done.14), channel_id=1, source_target_pairs={{0,4},{4,0},{8,12},{12,8},{16,20},{20,16},{24,28},{28,24},{1,5},{5... | collective-permute-start | bytes 196616 | tf_op jit(solution)/shard_map/ppermute | solution.py:164
  (3 other events, 5.0 us)

commit v11 on v10

--- a/solution.py
+++ b/solution.py
@@ -49,23 +49,35 @@
     return butterfly(groups)
 
 
-def sums_kernel(x_ref, sums_ref):
-    near, owned, width = x_ref.shape[1:]
+def sums_kernel(near, place_ref, *refs):
+    own_refs, far_refs, sums_ref = refs[:near], refs[near : 2 * near], refs[2 * near]
+    owned, width = own_refs[0].shape
+    half, column = place_ref[0, 0], place_ref[0, 1]
     shape = (2 * owned, 2 * owned)
     row, lane = (lax.broadcasted_iota(jnp.int32, shape, axis) for axis in (0, 1))
-    for j in range(near):
-        rows = x_ref[:, j].reshape(2 * owned, width).astype(jnp.float32)
-        squares = jnp.sum(rows * rows, axis=1, keepdims=True)
-        line = jnp.sum(jnp.where(row == lane, squares, 0.0), axis=0, keepdims=True)
-        sums_ref[0, j] = line
-        sums_ref[1, j] = line
-
-
-def scale_rows(sums_ref, offset, owned, width, near):
-    biggest = jnp.max(sums_ref[...], axis=0, keepdims=True)
+    target = row + half * owned
+    target = jnp.where(target >= 2 * owned, target - 2 * owned, target)
+    place = lax.broadcasted_iota(jnp.int32, sums_ref.shape, 0)
+    sums = jnp.zeros(sums_ref.shape, jnp.float32)
+    for mask in range(near):
+        pair = []
+        for ref in (own_refs[mask], far_refs[mask]):
+            rows = ref[...].astype(jnp.float32)
+            pair.append(jnp.sum(rows * rows, axis=1, keepdims=True))
+        squares = jnp.concatenate(pair, axis=0)
+        line = jnp.sum(jnp.where(lane == target, squares, 0.0), axis=0, keepdims=True)
+        sums = jnp.where(place == (column ^ mask), line, sums)
+    sums_ref[...] = sums
+
+
+def scale_rows(sums_ref, column, half, owned, width, near):
+    place = lax.broadcasted_iota(jnp.int32, sums_ref.shape, 0)
+    biggest = jnp.where(place == column, sums_ref[...], 0.0)
+    biggest = jnp.sum(biggest, axis=0, keepdims=True)
     shape = (owned, 2 * owned)
     row, lane = (lax.broadcasted_iota(jnp.int32, shape, axis) for axis in (0, 1))
-    biggest = jnp.sum(jnp.where(lane == row + offset, biggest, 0.0), axis=1, keepdims=True)
+    target = row + half * owned
+    biggest = jnp.sum(jnp.where(lane == target, biggest, 0.0), axis=1, keepdims=True)
     mean = biggest * (1.0 / width)
     scale = jnp.sqrt(mean + 1e-06)
     peak = jnp.sqrt(mean * width) / scale
@@ -93,30 +105,36 @@
     return totals
 
 
-def proxy_kernel(near, base, offset_ref, *refs):
+def proxy_kernel(near, base, place_ref, *refs):
     pieces, (sums_ref, sign_ref, matrix_ref, sent_ref) = refs[:near], refs[near:]
     owned, width = sent_ref.shape
-    scale, step = scale_rows(sums_ref, owned - offset_ref[0, 0], owned, width, near)
+    scale, step = scale_rows(
+        sums_ref, place_ref[0, 1], 1 - place_ref[0, 0], owned, width, near
+    )
     totals = add_levels(pieces, scale, sign_ref, matrix_ref, base)
     for g, total in enumerate(totals):
         value = jnp.clip(jnp.round(total / step), -32767.0, 32767.0)
         sent_ref[:, g * base : (g + 1) * base] = value.astype(jnp.int16)
 
 
-def owner_kernel(near, base, offset_ref, *refs):
+def owner_kernel(near, base, place_ref, *refs):
     pieces, (sums_ref, sign_ref, matrix_ref, total_ref) = refs[:near], refs[near:]
     owned, width = total_ref.shape
-    scale, _ = scale_rows(sums_ref, offset_ref[0, 0], owned, width, near)
+    scale, _ = scale_rows(
+        sums_ref, place_ref[0, 1], place_ref[0, 0], owned, width, near
+    )
     totals = add_levels(pieces, scale, sign_ref, matrix_ref, base)
     for g, total in enumerate(totals):
         total_ref[:, g * base : (g + 1) * base] = total
 
 
 def finish_kernel(
-    near, offset_ref, near_ref, far_ref, sums_ref, total_ref, scale_ref, square_ref
+    near, place_ref, near_ref, far_ref, sums_ref, total_ref, scale_ref, square_ref
 ):
     owned, width = near_ref.shape
-    scale, step = scale_rows(sums_ref, offset_ref[0, 0], owned, width, near)
+    scale, step = scale_rows(
+        sums_ref, place_ref[0, 1], place_ref[0, 0], owned, width, near
+    )
     total = near_ref[...] + far_ref[...].astype(jnp.float32) * step
     mean_scale = scale / (2 * near)
     mean_rot = total * mean_scale
@@ -202,7 +220,7 @@
     matrix = jnp.asarray(hadamard(base), jnp.bfloat16)
     me = lax.axis_index("dp")
     near = replicas // 2
-    offset = (me // near * owned).astype(jnp.int32).reshape(1, 1)
+    place = jnp.stack([me // near, me % near]).astype(jnp.int32).reshape(1, 2)
     params = pltpu.CompilerParams(vmem_limit_bytes=vmem_bytes)
     scalar = pl.BlockSpec(memory_space=pltpu.SMEM)
     array = pl.BlockSpec(memory_space=pltpu.VMEM)
@@ -211,28 +229,30 @@
         source = source.reshape(replicas, owned, width)
         return lax.dynamic_slice_in_dim(source, index, 1, 0).reshape(owned, width)
 
-    far_pieces = [swap(block_of(grads, me ^ mask ^ near), mask) for mask in range(1, near)]
+    own_slices = [block_of(grads, me ^ mask) for mask in range(near)]
+    far_slices = [block_of(grads, me ^ mask ^ near) for mask in range(near)]
+    far_pieces = [far_slices[0]] + [swap(far_slices[mask], mask) for mask in range(1, near)]
     sums = pl.pallas_call(
-        sums_kernel,
-        in_specs=[array],
-        out_shape=jax.ShapeDtypeStruct((2, near, 1, 2 * owned), jnp.float32),
+        functools.partial(sums_kernel, near),
+        in_specs=[scalar] + [array] * (2 * near),
+        out_shape=jax.ShapeDtypeStruct((near, 2 * owned), jnp.float32),
         compiler_params=params,
         name="sum_squares",
-    )(grads.reshape(2, near, owned, width))
-    later, sums = lax.optimization_barrier((grads, sums))
-    sums = lax.all_to_all(
-        sums.reshape(replicas, 1, 2 * owned), "dp", split_axis=0, concat_axis=0, tiled=True
-    ).reshape(replicas, 2 * owned)
-    near_pieces = [swap(block_of(later, me ^ mask), mask) for mask in range(1, near)]
-    far_pieces.append(block_of(later, me ^ near))
-    near_pieces.append(block_of(later, me))
+    )(place, *own_slices, *far_slices)
+    mask = 1
+    while mask < replicas:
+        if mask == near:
+            sums, own_slices = lax.optimization_barrier((sums, own_slices))
+        sums = jnp.maximum(sums, swap(sums, mask))
+        mask *= 2
+    near_pieces = [own_slices[0]] + [swap(own_slices[mask], mask) for mask in range(1, near)]
     sent = pl.pallas_call(
         functools.partial(proxy_kernel, near, base),
         in_specs=[scalar] + [array] * (near + 3),
         out_shape=jax.ShapeDtypeStruct((owned, width), jnp.int16),
         compiler_params=params,
         name="proxy_blocks",
-    )(offset, *far_pieces, sums, signs, matrix)
+    )(place, *far_pieces, sums, signs, matrix)
     far_total = swap(sent, near)
     near_total = pl.pallas_call(
         functools.partial(owner_kernel, near, base),
@@ -240,7 +260,7 @@
         out_shape=jax.ShapeDtypeStruct((owned, width), jnp.float32),
         compiler_params=params,
         name="owner_blocks",
-    )(offset, *near_pieces, sums, signs, matrix)
+    )(place, *near_pieces, sums, signs, matrix)
     total, mean_scale, squares = pl.pallas_call(
         functools.partial(finish_kernel, near),
         in_specs=[scalar] + [array] * 3,
@@ -251,7 +271,7 @@
         ),
         compiler_params=params,
         name="finish_blocks",
-    )(offset, near_total, far_total, sums)
+    )(place, near_total, far_total, sums)
     unrot = pl.pallas_call(
         functools.partial(back_kernel, base),
         out_shape=jax.ShapeDtypeStruct((owned, width), jnp.float32),

time: 59.6 us -> 64.2 us (1.077)
  starting transfers between devices: 29.4 us -> 34.9 us
  Pallas kernels: 4.25 us -> 5.91 us
  waiting for transfers between devices: 21.2 us -> 19.6 us
  local copies, waits for them, and re-layouts: 3.6 us -> 2.64 us
    ppermute x18 -> x21, starting transfers between devices: 19.9 us -> 30 us  [swap(): return lax.ppermute(value, 'dp', [(i, i ^ mask) for i in range(size)])]
    all_to_all x1 -> x0, starting transfers between devices: 6.22 us -> none  [on_device(): lax.all_to_all(sums.reshape(replicas, 1, 2 * owned), 'dp', split_axis=0,...]
    all_to_all x1 -> x0, waiting for transfers between devices: 2.69 us -> none  [on_device(): lax.all_to_all(sums.reshape(replicas, 1, 2 * owned), 'dp', split_axis=0,...]
    all_to_all x1, starting transfers between devices: 3.29 us -> 4.89 us  [on_device(): lax.all_to_all(squares, ('dp', 'expert'), split_axis=0, concat_axis=0, ti...]
    unnamed x14 -> x10, local copies, waits for them, and re-layouts: 2.22 us -> 0.99 us
    ppermute x18 -> x21, waiting for transfers between devices: 11.8 us -> 12.8 us  [swap(): return lax.ppermute(value, 'dp', [(i, i ^ mask) for i in range(size)])]
    reshape x2 -> x1, local copies, waits for them, and re-layouts: 1.13 us -> 1.4 us  [block_of(): return lax.dynamic_slice_in_dim(source, index, 1, 0).reshape(owned, width)]
  transfers between devices with their start and end apart: 20 -> 22, of which waited for: 9 -> 11; matrix products, arithmetic and copies ran while one was open for 1% -> 1% of each run, Pallas kernels for 5% -> 7%
where the time goes in v11:
time: 64.2 us; the launch traced here: 64 us
  starting transfers between devices  34.9 us (54%)
  waiting for transfers between devices  19.6 us (31%)
  Pallas kernels  5.91 us (9%)
  local copies, waits for them, and re-layouts  2.64 us (4%)
  between operations  0.92 us (1%)
    ppermute x21, starting transfers between devices, swap(): return lax.ppermute(value, 'dp', [(i, i ^ mask) for i in range(size)])  30 us
    ppermute x21, waiting for transfers between devices, swap(): return lax.ppermute(value, 'dp', [(i, i ^ mask) for i in range(size)])  12.8 us
    all_to_all x1, waiting for transfers between devices, on_device(): lax.all_to_all(squares, ('dp', 'expert'), split_axis=0, concat_axis=0, ti...  6.73 us
    all_to_all x1, starting transfers between devices, on_device(): lax.all_to_all(squares, ('dp', 'expert'), split_axis=0, concat_axis=0, ti...  4.89 us
    pallas_call x1, Pallas kernels, on_device(): pl.pallas_call(functools.partial(finish_kernel, near), in_specs=[scalar]...  1.46 us
    reshape x1, local copies, waits for them, and re-layouts, block_of(): return lax.dynamic_slice_in_dim(source, index, 1, 0).reshape(owned, width)  1.4 us
  transfers between devices with their start and end apart: 22, of which 11 were waited for; matrix products, arithmetic and copies ran while one was open for 1% of the time, Pallas kernels for 7%

profile of v11, /device:TPU:0, one launch (start us, length us, event | category | flops | bytes accessed | tf_op | source)
XLA Modules:
  0.0 64.0 jit_solution(4869143504566070686)
XLA Ops:
  0.7 1.4 %dynamic-slice_bitcast_fusion = (bf16[64,1024]{1,0:T(8,128)(2,1)S(1)}, bf16[64,1024]{1,0:T(8,128)(2,1)S(1)}, bf16[64,1024]{1,0:T(8,128)(2,1)S(1)}, bf16[64,1024]...) fusion(bf16[8,64,1024]{2,1,0:T(8,128)(2,1)} %bitcast.54, ...), kind=kLoop, calls=%fused_computation.4 | loop fusion | bytes 2097184 | tf_op jit(solution)/shard_map/reshape | solution.py:230
  2.1 3.0 %collective-permute-start.6 = (bf16[64,1024]{1,0:T(8,128)(2,1)S(1)}, bf16[64,1024]{1,0:T(8,128)(2,1)S(1)}, u32[]{:S(2)}, u32[]{:S(2)}) collective-permute-start(bf16[64,1024]{1,0:T(8,128)(2,1)S(1)} %get-tuple-element.28.refs_5_), channel_id=1, source_target_pairs={{0,4},{4,0},{8,12},{12,8},{16,20},{20,16},{24,28},{28,24},{1,5},{5... | collective-permute-start | bytes 393224 | tf_op jit(solution)/shard_map/ppermute | solution.py:182
  5.1 1.6 %collective-permute-start.7 = (bf16[64,1024]{1,0:T(8,128)(2,1)S(1)}, bf16[64,1024]{1,0:T(8,128)(2,1)S(1)}, u32[]{:S(2)}, u32[]{:S(2)}) collective-permute-start(bf16[64,1024]{1,0:T(8,128)(2,1)S(1)} %get-tuple-element.27.refs_6_), channel_id=1, source_target_pairs={{0,8},{4,12},{8,0},{12,4},{16,24},{20,28},{24,16},{28,20},{1,9},{5... | collective-permute-start | bytes 393224 | tf_op jit(solution)/shard_map/ppermute | solution.py:182
  7.7 2.0 %collective-permute-start = (f32[4,128]{1,0:T(4,128)S(1)}, f32[4,128]{1,0:T(4,128)S(1)}, u32[]{:S(2)}, u32[]{:S(2)}) collective-permute-start(f32[4,128]{1,0:T(4,128)S(1)} %sum_squares.1), channel_id=1, source_target_pairs={{0,4},{4,0},{8,12},{12,8},{16,20},{20,16},{24,28},{28,24},{1,5},{5... | collective-permute-start | bytes 6152 | tf_op jit(solution)/shard_map/ppermute | solution.py:182
  9.6 1.9 %collective-permute-done = f32[4,128]{1,0:T(4,128)S(1)} collective-permute-done((f32[4,128]{1,0:T(4,128)S(1)}, f32[4,128]{1,0:T(4,128)S(1)}, u32[]{:S(2)}, u32[]{:S(2)}) %collective-permute-start) | collective-permute-done | bytes 2080 | tf_op jit(solution)/shard_map/ppermute | solution.py:182
  11.5 2.0 %collective-permute-start.1 = (f32[4,128]{1,0:T(4,128)S(1)}, f32[4,128]{1,0:T(4,128)S(1)}, u32[]{:S(2)}, u32[]{:S(2)}) collective-permute-start(f32[4,128]{1,0:T(4,128)S(1)} %max.9), channel_id=1, source_target_pairs={{0,8},{4,12},{8,0},{12,4},{16,24},{20,28},{24,16},{28,20},{1,9},{5... | collective-permute-start | bytes 6152 | tf_op jit(solution)/shard_map/ppermute | solution.py:182
  13.5 1.6 %collective-permute-done.1 = f32[4,128]{1,0:T(4,128)S(1)} collective-permute-done((f32[4,128]{1,0:T(4,128)S(1)}, f32[4,128]{1,0:T(4,128)S(1)}, u32[]{:S(2)}, u32[]{:S(2)}) %collective-permute-start.1) | collective-permute-done | bytes 2080 | tf_op jit(solution)/shard_map/ppermute | solution.py:182
  15.1 3.0 %collective-permute-start.5 = (f32[4,128]{1,0:T(4,128)S(1)}, f32[4,128]{1,0:T(4,128)S(1)}, u32[]{:S(2)}, u32[]{:S(2)}) collective-permute-start(f32[4,128]{1,0:T(4,128)S(1)} %max.10), channel_id=1, source_target_pairs={{0,16},{4,20},{8,24},{12,28},{16,0},{20,4},{24,8},{28,12},{1,17},{... | collective-permute-start | bytes 6152 | tf_op jit(solution)/shard_map/ppermute | solution.py:182
  18.1 1.5 %collective-permute-start.2 = (bf16[64,1024]{1,0:T(8,128)(2,1)S(1)}, bf16[64,1024]{1,0:T(8,128)(2,1)S(1)}, u32[]{:S(2)}, u32[]{:S(2)}) collective-permute-start(bf16[64,1024]{1,0:T(8,128)(2,1)S(1)} %get-tuple-element.15.refs_1_), channel_id=1, source_target_pairs={{0,4},{4,0},{8,12},{12,8},{16,20},{20,16},{24,28},{28,24},{1,5},{5... | collective-permute-start | bytes 393224 | tf_op jit(solution)/shard_map/ppermute | solution.py:182
  19.8 1.8 %collective-permute-start.3 = (bf16[64,1024]{1,0:T(8,128)(2,1)S(1)}, bf16[64,1024]{1,0:T(8,128)(2,1)S(1)}, u32[]{:S(2)}, u32[]{:S(2)}) collective-permute-start(bf16[64,1024]{1,0:T(8,128)(2,1)S(1)} %get-tuple-element.16.refs_2_), channel_id=1, source_target_pairs={{0,8},{4,12},{8,0},{12,4},{16,24},{20,28},{24,16},{28,20},{1,9},{5... | collective-permute-start | bytes 393224 | tf_op jit(solution)/shard_map/ppermute | solution.py:182
  21.6 1.4 %collective-permute-start.4 = (bf16[64,1024]{1,0:T(8,128)(2,1)S(1)}, bf16[64,1024]{1,0:T(8,128)(2,1)S(1)}, u32[]{:S(2)}, u32[]{:S(2)}) collective-permute-start(bf16[64,1024]{1,0:T(8,128)(2,1)S(1)} %get-tuple-element.17.refs_3_), channel_id=1, source_target_pairs={{0,12},{4,8},{8,4},{12,0},{16,28},{20,24},{24,20},{28,16},{1,13},{... | collective-permute-start | bytes 393224 | tf_op jit(solution)/shard_map/ppermute | solution.py:182
  23.0 1.1 %proxy_blocks.1 = s16[64,1024]{1,0:T(8,128)(2,1)S(1)} custom-call(s32[1,2]{1,0:T(1,128)S(1)} %add_bitcast_fusion.place_ref, bf16[64,1024]{1,0:T(8,128)(2,1)S(1)} %get-tuple-element.29.refs_4_.refs_0_, bf16[64,1024]{1,0:T(8,128)(2,1)S(1)} %collective-permute-done.6.refs_1_, bf16[64,1024]{1,0:T(8,128)(2,1)S(1)} %collective-permute-done.7.refs_2_, ...), custom_call_target="tpu_custom_call" | custom-call | tf_op jit(solution)/shard_map/proxy_blocks/pallas_call | solution.py:249
  24.1 2.7 %collective-permute-start.9 = (s16[64,1024]{1,0:T(8,128)(2,1)S(1)}, s16[64,1024]{1,0:T(8,128)(2,1)S(1)}, u32[]{:S(2)}, u32[]{:S(2)}) collective-permute-start(s16[64,1024]{1,0:T(8,128)(2,1)S(1)} %proxy_blocks.1), channel_id=1, source_target_pairs={{0,16},{4,20},{8,24},{12,28},{16,0},{20,4},{24,8},{28,12},{1,17},{... | collective-permute-start | bytes 393224 | tf_op jit(solution)/shard_map/ppermute | solution.py:182
  28.6 2.8 %collective-permute-done.9.far_ref = s16[64,1024]{1,0:T(8,128)(2,1)S(1)} collective-permute-done((s16[64,1024]{1,0:T(8,128)(2,1)S(1)}, s16[64,1024]{1,0:T(8,128)(2,1)S(1)}, u32[]{:S(2)}, u32[]{:S(2)}) %collective-permute-start.9) | collective-permute-done | bytes 131104 | tf_op jit(solution)/shard_map/ppermute | solution.py:182
  31.5 1.5 %finish_blocks.1 = (f32[64,1024]{1,0:T(8,128)S(1)}, f32[64,128]{1,0:T(8,128)S(1)}, f32[32,1,128]{2,1,0:T(1,128)}) custom-call(s32[1,2]{1,0:T(1,128)S(1)} %add_bitcast_fusion.place_ref, f32[64,1024]{1,0:T(8,128)S(1)} %owner_blocks.1.near_ref, s16[64,1024]{1,0:T(8,128)(2,1)S(1)} %collective-permute-done.9.far_ref, f32[4,128]{1,0:T(4,128)S(1)} %max.11.refs_4_.sums_ref), custom_call_target="tpu_custom_call" | custom-call | tf_op jit(solution)/shard_map/finish_blocks/pallas_call | solution.py:264
  32.9 4.9 %all-to-all-start = ((f32[32,1,128]{2,1,0:T(1,128)}), f32[32,1,128]{2,1,0:T(1,128)S(1)}, u32[]{:S(2)}, u32[]{:S(2)}) async-start(f32[32,1,128]{2,1,0:T(1,128)} %get-tuple-element.19), calls=%async_computation | async-start | bytes 32768 | tf_op jit(solution)/shard_map/all_to_all | solution.py:281
  38.2 6.7 %all-to-all-done = f32[32,1,128]{2,1,0:T(1,128)S(1)} async-done(((f32[32,1,128]{2,1,0:T(1,128)}), f32[32,1,128]{2,1,0:T(1,128)S(1)}, u32[]{:S(2)}, u32[]{:S(2)}) %all-to-all-start) | async-done | bytes 16416 | tf_op jit(solution)/shard_map/all_to_all | solution.py:281
  47.6 2.4 %collective-permute-start.11 = (bf16[32,1024]{1,0:T(8,128)(2,1)S(1)}, bf16[32,1024]{1,0:T(8,128)(2,1)S(1)}, u32[]{:S(2)}, u32[]{:S(2)}) collective-permute-start(bf16[32,1024]{1,0:T(8,128)(2,1)S(1)} %get-tuple-element.23), channel_id=1, source_target_pairs={{0,16},{4,20},{8,24},{12,28},{16,0},{20,4},{24,8},{28,12},{1,17},{... | collective-permute-start | bytes 196616 | tf_op jit(solution)/shard_map/ppermute | solution.py:182
  50.0 1.8 %collective-permute-done.10 = bf16[32,1024]{1,0:T(8,128)(2,1)S(1)} collective-permute-done((bf16[32,1024]{1,0:T(8,128)(2,1)S(1)}, bf16[32,1024]{1,0:T(8,128)(2,1)S(1)}, u32[]{:S(2)}, u32[]{:S(2)}) %collective-permute-start.10) | collective-permute-done | bytes 65568 | tf_op jit(solution)/shard_map/ppermute | solution.py:182
  51.8 1.2 %collective-permute-start.16 = (bf16[32,1024]{1,0:T(8,128)(2,1)S(1)}, bf16[32,1024]{1,0:T(8,128)(2,1)S(1)}, u32[]{:S(2)}, u32[]{:S(2)}) collective-permute-start(bf16[32,1024]{1,0:T(8,128)(2,1)S(1)} %collective-permute-done.10), channel_id=1, source_target_pairs={{0,4},{4,0},{8,12},{12,8},{16,20},{20,16},{24,28},{28,24},{1,5},{5... | collective-permute-start | bytes 196616 | tf_op jit(solution)/shard_map/ppermute | solution.py:182
  53.3 2.5 %collective-permute-start.17 = (bf16[32,1024]{1,0:T(8,128)(2,1)S(1)}, bf16[32,1024]{1,0:T(8,128)(2,1)S(1)}, u32[]{:S(2)}, u32[]{:S(2)}) collective-permute-start(bf16[32,1024]{1,0:T(8,128)(2,1)S(1)} %collective-permute-done.11), channel_id=1, source_target_pairs={{0,8},{4,12},{8,0},{12,4},{16,24},{20,28},{24,16},{28,20},{1,9},{5... | collective-permute-start | bytes 196616 | tf_op jit(solution)/shard_map/ppermute | solution.py:182
  55.9 1.2 %collective-permute-start.19 = (bf16[32,1024]{1,0:T(8,128)(2,1)S(1)}, bf16[32,1024]{1,0:T(8,128)(2,1)S(1)}, u32[]{:S(2)}, u32[]{:S(2)}) collective-permute-start(bf16[32,1024]{1,0:T(8,128)(2,1)S(1)} %collective-permute-done.11), channel_id=1, source_target_pairs={{0,4},{4,0},{8,12},{12,8},{16,20},{20,16},{24,28},{28,24},{1,5},{5... | collective-permute-start | bytes 196616 | tf_op jit(solution)/shard_map/ppermute | solution.py:182
  59.9 1.6 %collective-permute-done.15 = bf16[32,1024]{1,0:T(8,128)(2,1)S(1)} collective-permute-done((bf16[32,1024]{1,0:T(8,128)(2,1)S(1)}, bf16[32,1024]{1,0:T(8,128)(2,1)S(1)}, u32[]{:S(2)}, u32[]{:S(2)}) %collective-permute-start.15) | collective-permute-done | bytes 65568 | tf_op jit(solution)/shard_map/ppermute | solution.py:182
  61.5 1.4 %collective-permute-done.18 = bf16[32,1024]{1,0:T(8,128)(2,1)S(1)} collective-permute-done((bf16[32,1024]{1,0:T(8,128)(2,1)S(1)}, bf16[32,1024]{1,0:T(8,128)(2,1)S(1)}, u32[]{:S(2)}, u32[]{:S(2)}) %collective-permute-start.18) | collective-permute-done | bytes 65568 | tf_op jit(solution)/shard_map/ppermute | solution.py:182
  (55 shorter events, 10.2 us)
Async XLA Ops:
  2.1 19.5 %collective-permute-start.6 = (bf16[64,1024]{1,0:T(8,128)(2,1)S(1)}, bf16[64,1024]{1,0:T(8,128)(2,1)S(1)}, u32[]{:S(2)}, u32[]{:S(2)}) collective-permute-start(bf16[64,1024]{1,0:T(8,128)(2,1)S(1)} %get-tuple-element.28.refs_5_), channel_id=1, source_target_pairs={{0,4},{4,0},{8,12},{12,8},{16,20},{20,16},{24,28},{28,24},{1,5},{5... | collective-permute-start | bytes 393224 | tf_op jit(solution)/shard_map/ppermute | solution.py:182
  5.1 17.9 %collective-permute-start.7 = (bf16[64,1024]{1,0:T(8,128)(2,1)S(1)}, bf16[64,1024]{1,0:T(8,128)(2,1)S(1)}, u32[]{:S(2)}, u32[]{:S(2)}) collective-permute-start(bf16[64,1024]{1,0:T(8,128)(2,1)S(1)} %get-tuple-element.27.refs_6_), channel_id=1, source_target_pairs={{0,8},{4,12},{8,0},{12,4},{16,24},{20,28},{24,16},{28,20},{1,9},{5... | collective-permute-start | bytes 393224 | tf_op jit(solution)/shard_map/ppermute | solution.py:182
  6.7 16.3 %collective-permute-start.8 = (bf16[64,1024]{1,0:T(8,128)(2,1)S(1)}, bf16[64,1024]{1,0:T(8,128)(2,1)S(1)}, u32[]{:S(2)}, u32[]{:S(2)}) collective-permute-start(bf16[64,1024]{1,0:T(8,128)(2,1)S(1)} %get-tuple-element.26.refs_7_), channel_id=1, source_target_pairs={{0,12},{4,8},{8,4},{12,0},{16,28},{20,24},{24,20},{28,16},{1,13},{... | collective-permute-start | bytes 393224 | tf_op jit(solution)/shard_map/ppermute | solution.py:182
  6.7 16.2 %copy-start = (bf16[256,256]{1,0:T(8,128)(2,1)S(1)}, bf16[256,256]{1,0:T(8,128)(2,1)}, u32[]{:S(2)}) copy-start(bf16[256,256]{1,0:T(8,128)(2,1)} %constant.50.clone.refs_6_.matrix_ref) | copy-start | bytes 393220
  7.7 3.9 %collective-permute-start = (f32[4,128]{1,0:T(4,128)S(1)}, f32[4,128]{1,0:T(4,128)S(1)}, u32[]{:S(2)}, u32[]{:S(2)}) collective-permute-start(f32[4,128]{1,0:T(4,128)S(1)} %sum_squares.1), channel_id=1, source_target_pairs={{0,4},{4,0},{8,12},{12,8},{16,20},{20,16},{24,28},{28,24},{1,5},{5... | collective-permute-start | bytes 6152 | tf_op jit(solution)/shard_map/ppermute | solution.py:182
  11.5 3.6 %collective-permute-start.1 = (f32[4,128]{1,0:T(4,128)S(1)}, f32[4,128]{1,0:T(4,128)S(1)}, u32[]{:S(2)}, u32[]{:S(2)}) collective-permute-start(f32[4,128]{1,0:T(4,128)S(1)} %max.9), channel_id=1, source_target_pairs={{0,8},{4,12},{8,0},{12,4},{16,24},{20,28},{24,16},{28,20},{1,9},{5... | collective-permute-start | bytes 6152 | tf_op jit(solution)/shard_map/ppermute | solution.py:182
  15.1 7.9 %copy-start.3 = (s32[1,1024]{1,0:T(1,128)S(1)}, s32[1,1024]{1,0:T(1,128)}, u32[]{:S(2)}) copy-start(s32[1,1024]{1,0:T(1,128)} %sign_ref.1) | copy-start | bytes 12292
  15.1 4.7 %collective-permute-start.5 = (f32[4,128]{1,0:T(4,128)S(1)}, f32[4,128]{1,0:T(4,128)S(1)}, u32[]{:S(2)}, u32[]{:S(2)}) collective-permute-start(f32[4,128]{1,0:T(4,128)S(1)} %max.10), channel_id=1, source_target_pairs={{0,16},{4,20},{8,24},{12,28},{16,0},{20,4},{24,8},{28,12},{1,17},{... | collective-permute-start | bytes 6152 | tf_op jit(solution)/shard_map/ppermute | solution.py:182
  18.1 8.8 %collective-permute-start.2 = (bf16[64,1024]{1,0:T(8,128)(2,1)S(1)}, bf16[64,1024]{1,0:T(8,128)(2,1)S(1)}, u32[]{:S(2)}, u32[]{:S(2)}) collective-permute-start(bf16[64,1024]{1,0:T(8,128)(2,1)S(1)} %get-tuple-element.15.refs_1_), channel_id=1, source_target_pairs={{0,4},{4,0},{8,12},{12,8},{16,20},{20,16},{24,28},{28,24},{1,5},{5... | collective-permute-start | bytes 393224 | tf_op jit(solution)/shard_map/ppermute | solution.py:182
  19.8 7.1 %collective-permute-start.3 = (bf16[64,1024]{1,0:T(8,128)(2,1)S(1)}, bf16[64,1024]{1,0:T(8,128)(2,1)S(1)}, u32[]{:S(2)}, u32[]{:S(2)}) collective-permute-start(bf16[64,1024]{1,0:T(8,128)(2,1)S(1)} %get-tuple-element.16.refs_2_), channel_id=1, source_target_pairs={{0,8},{4,12},{8,0},{12,4},{16,24},{20,28},{24,16},{28,20},{1,9},{5... | collective-permute-start | bytes 393224 | tf_op jit(solution)/shard_map/ppermute | solution.py:182
  21.6 5.9 %collective-permute-start.4 = (bf16[64,1024]{1,0:T(8,128)(2,1)S(1)}, bf16[64,1024]{1,0:T(8,128)(2,1)S(1)}, u32[]{:S(2)}, u32[]{:S(2)}) collective-permute-start(bf16[64,1024]{1,0:T(8,128)(2,1)S(1)} %get-tuple-element.17.refs_3_), channel_id=1, source_target_pairs={{0,12},{4,8},{8,4},{12,0},{16,28},{20,24},{24,20},{28,16},{1,13},{... | collective-permute-start | bytes 393224 | tf_op jit(solution)/shard_map/ppermute | solution.py:182
  24.1 7.3 %collective-permute-start.9 = (s16[64,1024]{1,0:T(8,128)(2,1)S(1)}, s16[64,1024]{1,0:T(8,128)(2,1)S(1)}, u32[]{:S(2)}, u32[]{:S(2)}) collective-permute-start(s16[64,1024]{1,0:T(8,128)(2,1)S(1)} %proxy_blocks.1), channel_id=1, source_target_pairs={{0,16},{4,20},{8,24},{12,28},{16,0},{20,4},{24,8},{28,12},{1,17},{... | collective-permute-start | bytes 393224 | tf_op jit(solution)/shard_map/ppermute | solution.py:182
  32.9 12.0 %all-to-all-start = ((f32[32,1,128]{2,1,0:T(1,128)}), f32[32,1,128]{2,1,0:T(1,128)S(1)}, u32[]{:S(2)}, u32[]{:S(2)}) async-start(f32[32,1,128]{2,1,0:T(1,128)} %get-tuple-element.19), calls=%async_computation | async-start | bytes 32768 | tf_op jit(solution)/shard_map/all_to_all | solution.py:281
  45.1 6.7 %collective-permute-start.10 = (bf16[32,1024]{1,0:T(8,128)(2,1)S(1)}, bf16[32,1024]{1,0:T(8,128)(2,1)S(1)}, u32[]{:S(2)}, u32[]{:S(2)}) collective-permute-start(bf16[32,1024]{1,0:T(8,128)(2,1)S(1)} %get-tuple-element.22), channel_id=1, source_target_pairs={{0,16},{4,20},{8,24},{12,28},{16,0},{20,4},{24,8},{28,12},{1,17},{... | collective-permute-start | bytes 196616 | tf_op jit(solution)/shard_map/ppermute | solution.py:182
  45.7 10.1 %collective-permute-start.12 = (bf16[64,1024]{1,0:T(8,128)(2,1)S(1)}, bf16[64,1024]{1,0:T(8,128)(2,1)S(1)}, u32[]{:S(2)}, u32[]{:S(2)}) collective-permute-start(bf16[64,1024]{1,0:T(8,128)(2,1)S(1)} %get-tuple-element.24), channel_id=1, source_target_pairs={{0,4},{4,0},{8,12},{12,8},{16,20},{20,16},{24,28},{28,24},{1,5},{5... | collective-permute-start | bytes 393224 | tf_op jit(solution)/shard_map/ppermute | solution.py:182
  46.3 10.8 %collective-permute-start.13 = (bf16[64,1024]{1,0:T(8,128)(2,1)S(1)}, bf16[64,1024]{1,0:T(8,128)(2,1)S(1)}, u32[]{:S(2)}, u32[]{:S(2)}) collective-permute-start(bf16[64,1024]{1,0:T(8,128)(2,1)S(1)} %get-tuple-element.24), channel_id=1, source_target_pairs={{0,8},{4,12},{8,0},{12,4},{16,24},{20,28},{24,16},{28,20},{1,9},{5... | collective-permute-start | bytes 393224 | tf_op jit(solution)/shard_map/ppermute | solution.py:182
  47.6 5.7 %collective-permute-start.11 = (bf16[32,1024]{1,0:T(8,128)(2,1)S(1)}, bf16[32,1024]{1,0:T(8,128)(2,1)S(1)}, u32[]{:S(2)}, u32[]{:S(2)}) collective-permute-start(bf16[32,1024]{1,0:T(8,128)(2,1)S(1)} %get-tuple-element.23), channel_id=1, source_target_pairs={{0,16},{4,20},{8,24},{12,28},{16,0},{20,4},{24,8},{28,12},{1,17},{... | collective-permute-start | bytes 196616 | tf_op jit(solution)/shard_map/ppermute | solution.py:182
  51.8 5.4 %collective-permute-start.14 = (bf16[32,1024]{1,0:T(8,128)(2,1)S(1)}, bf16[32,1024]{1,0:T(8,128)(2,1)S(1)}, u32[]{:S(2)}, u32[]{:S(2)}) collective-permute-start(bf16[32,1024]{1,0:T(8,128)(2,1)S(1)} %collective-permute-done.10), channel_id=1, source_target_pairs={{0,8},{4,12},{8,0},{12,4},{16,24},{20,28},{24,16},{28,20},{1,9},{5... | collective-permute-start | bytes 196616 | tf_op jit(solution)/shard_map/ppermute | solution.py:182
  51.8 9.7 %collective-permute-start.16 = (bf16[32,1024]{1,0:T(8,128)(2,1)S(1)}, bf16[32,1024]{1,0:T(8,128)(2,1)S(1)}, u32[]{:S(2)}, u32[]{:S(2)}) collective-permute-start(bf16[32,1024]{1,0:T(8,128)(2,1)S(1)} %collective-permute-done.10), channel_id=1, source_target_pairs={{0,4},{4,0},{8,12},{12,8},{16,20},{20,16},{24,28},{28,24},{1,5},{5... | collective-permute-start | bytes 196616 | tf_op jit(solution)/shard_map/ppermute | solution.py:182
  53.3 5.4 %collective-permute-start.17 = (bf16[32,1024]{1,0:T(8,128)(2,1)S(1)}, bf16[32,1024]{1,0:T(8,128)(2,1)S(1)}, u32[]{:S(2)}, u32[]{:S(2)}) collective-permute-start(bf16[32,1024]{1,0:T(8,128)(2,1)S(1)} %collective-permute-done.11), channel_id=1, source_target_pairs={{0,8},{4,12},{8,0},{12,4},{16,24},{20,28},{24,16},{28,20},{1,9},{5... | collective-permute-start | bytes 196616 | tf_op jit(solution)/shard_map/ppermute | solution.py:182
  55.9 7.1 %collective-permute-start.19 = (bf16[32,1024]{1,0:T(8,128)(2,1)S(1)}, bf16[32,1024]{1,0:T(8,128)(2,1)S(1)}, u32[]{:S(2)}, u32[]{:S(2)}) collective-permute-start(bf16[32,1024]{1,0:T(8,128)(2,1)S(1)} %collective-permute-done.11), channel_id=1, source_target_pairs={{0,4},{4,0},{8,12},{12,8},{16,20},{20,16},{24,28},{28,24},{1,5},{5... | collective-permute-start | bytes 196616 | tf_op jit(solution)/shard_map/ppermute | solution.py:182
  57.1 6.0 %collective-permute-start.20 = (bf16[64,1024]{1,0:T(8,128)(2,1)S(1)}, bf16[64,1024]{1,0:T(8,128)(2,1)S(1)}, u32[]{:S(2)}, u32[]{:S(2)}) collective-permute-start(bf16[64,1024]{1,0:T(8,128)(2,1)S(1)} %collective-permute-done.12), channel_id=1, source_target_pairs={{0,8},{4,12},{8,0},{12,4},{16,24},{20,28},{24,16},{28,20},{1,9},{5... | collective-permute-start | bytes 393224 | tf_op jit(solution)/shard_map/ppermute | solution.py:182
  57.2 4.3 %collective-permute-start.15 = (bf16[32,1024]{1,0:T(8,128)(2,1)S(1)}, bf16[32,1024]{1,0:T(8,128)(2,1)S(1)}, u32[]{:S(2)}, u32[]{:S(2)}) collective-permute-start(bf16[32,1024]{1,0:T(8,128)(2,1)S(1)} %collective-permute-done.14), channel_id=1, source_target_pairs={{0,4},{4,0},{8,12},{12,8},{16,20},{20,16},{24,28},{28,24},{1,5},{5... | collective-permute-start | bytes 196616 | tf_op jit(solution)/shard_map/ppermute | solution.py:182
  58.7 4.3 %collective-permute-start.18 = (bf16[32,1024]{1,0:T(8,128)(2,1)S(1)}, bf16[32,1024]{1,0:T(8,128)(2,1)S(1)}, u32[]{:S(2)}, u32[]{:S(2)}) collective-permute-start(bf16[32,1024]{1,0:T(8,128)(2,1)S(1)} %collective-permute-done.17), channel_id=1, source_target_pairs={{0,4},{4,0},{8,12},{12,8},{16,20},{20,16},{24,28},{28,24},{1,5},{5... | collective-permute-start | bytes 196616 | tf_op jit(solution)/shard_map/ppermute | solution.py:182
  (3 other events, 15.1 us)

commit v12 on v10

--- a/solution.py
+++ b/solution.py
@@ -75,14 +75,15 @@
     return scale, step
 
 
-def add_levels(pieces, scale, sign_ref, matrix_ref, base):
-    width = pieces[0].shape[1]
+def add_levels(pieces, half, scale, sign_ref, matrix_ref, base):
+    width = pieces[0].shape[-1]
     signs = sign_ref[...].astype(jnp.float32).astype(jnp.bfloat16)
     matrix = matrix_ref[...]
     inverse = (1.0 / math.sqrt(width)) / scale
     totals = None
     for piece in pieces:
-        groups = rotate_groups([piece[...] * signs], matrix, base)
+        rows = piece[...] if len(piece.shape) == 2 else piece[half]
+        groups = rotate_groups([rows * signs], matrix, base)
         levels = [
             jnp.clip(group * inverse, -clamp_level, clamp_level)
             .astype(jnp.bfloat16)
@@ -93,30 +94,32 @@
     return totals
 
 
-def proxy_kernel(near, base, offset_ref, *refs):
+def proxy_kernel(near, base, half_ref, *refs):
     pieces, (sums_ref, sign_ref, matrix_ref, sent_ref) = refs[:near], refs[near:]
     owned, width = sent_ref.shape
-    scale, step = scale_rows(sums_ref, owned - offset_ref[0, 0], owned, width, near)
-    totals = add_levels(pieces, scale, sign_ref, matrix_ref, base)
+    half = 1 - half_ref[0, 0]
+    scale, step = scale_rows(sums_ref, half * owned, owned, width, near)
+    totals = add_levels(pieces, half, scale, sign_ref, matrix_ref, base)
     for g, total in enumerate(totals):
         value = jnp.clip(jnp.round(total / step), -32767.0, 32767.0)
         sent_ref[:, g * base : (g + 1) * base] = value.astype(jnp.int16)
 
 
-def owner_kernel(near, base, offset_ref, *refs):
+def owner_kernel(near, base, half_ref, *refs):
     pieces, (sums_ref, sign_ref, matrix_ref, total_ref) = refs[:near], refs[near:]
     owned, width = total_ref.shape
-    scale, _ = scale_rows(sums_ref, offset_ref[0, 0], owned, width, near)
-    totals = add_levels(pieces, scale, sign_ref, matrix_ref, base)
+    half = half_ref[0, 0]
+    scale, _ = scale_rows(sums_ref, half * owned, owned, width, near)
+    totals = add_levels(pieces, half, scale, sign_ref, matrix_ref, base)
     for g, total in enumerate(totals):
         total_ref[:, g * base : (g + 1) * base] = total
 
 
 def finish_kernel(
-    near, offset_ref, near_ref, far_ref, sums_ref, total_ref, scale_ref, square_ref
+    near, half_ref, near_ref, far_ref, sums_ref, total_ref, scale_ref, square_ref
 ):
     owned, width = near_ref.shape
-    scale, step = scale_rows(sums_ref, offset_ref[0, 0], owned, width, near)
+    scale, step = scale_rows(sums_ref, half_ref[0, 0] * owned, owned, width, near)
     total = near_ref[...] + far_ref[...].astype(jnp.float32) * step
     mean_scale = scale / (2 * near)
     mean_rot = total * mean_scale
@@ -159,13 +162,17 @@
     update_ref[...] = unrot_ref[...] * clip_factor(limit, square_ref)
 
 
+def chips_along_x(replicas):
+    return 1 << ((replicas.bit_length() - 1) // 2)
+
+
 def swap(value, mask):
     size = lax.axis_size("dp")
     return lax.ppermute(value, "dp", [(i, i ^ mask) for i in range(size)])
 
 
 def gather_blocks(block, parts, replicas):
-    x_count = 1 << ((replicas.bit_length() - 1) // 2)
+    x_count = chips_along_x(replicas)
     near = replicas // 2
     me = lax.axis_index("dp")
     owned, width = block.shape
@@ -202,37 +209,44 @@
     matrix = jnp.asarray(hadamard(base), jnp.bfloat16)
     me = lax.axis_index("dp")
     near = replicas // 2
-    offset = (me // near * owned).astype(jnp.int32).reshape(1, 1)
+    half = (me // near).astype(jnp.int32).reshape(1, 1)
     params = pltpu.CompilerParams(vmem_limit_bytes=vmem_bytes)
     scalar = pl.BlockSpec(memory_space=pltpu.SMEM)
     array = pl.BlockSpec(memory_space=pltpu.VMEM)
 
+    halves = grads.reshape(2, near, owned, width)
+
+    def pair_of(index):
+        return lax.dynamic_slice_in_dim(halves, index % near, 1, 1).reshape(2, owned, width)
+
     def block_of(source, index):
         source = source.reshape(replicas, owned, width)
         return lax.dynamic_slice_in_dim(source, index, 1, 0).reshape(owned, width)
 
-    far_pieces = [swap(block_of(grads, me ^ mask ^ near), mask) for mask in range(1, near)]
+    x_count = chips_along_x(replicas)
+    aligned = [m for m in range(1, near) if m % x_count == 0 or m < x_count]
+    diagonal = [m for m in range(1, near) if m not in aligned]
+    pairs = [pair_of(me)] + [swap(pair_of(me ^ mask), mask) for mask in aligned]
+    far_pieces = pairs + [swap(block_of(grads, me ^ mask ^ near), mask) for mask in diagonal]
     sums = pl.pallas_call(
         sums_kernel,
         in_specs=[array],
         out_shape=jax.ShapeDtypeStruct((2, near, 1, 2 * owned), jnp.float32),
         compiler_params=params,
         name="sum_squares",
-    )(grads.reshape(2, near, owned, width))
+    )(halves)
     later, sums = lax.optimization_barrier((grads, sums))
     sums = lax.all_to_all(
         sums.reshape(replicas, 1, 2 * owned), "dp", split_axis=0, concat_axis=0, tiled=True
     ).reshape(replicas, 2 * owned)
-    near_pieces = [swap(block_of(later, me ^ mask), mask) for mask in range(1, near)]
-    far_pieces.append(block_of(later, me ^ near))
-    near_pieces.append(block_of(later, me))
+    near_pieces = pairs + [swap(block_of(later, me ^ mask), mask) for mask in diagonal]
     sent = pl.pallas_call(
         functools.partial(proxy_kernel, near, base),
         in_specs=[scalar] + [array] * (near + 3),
         out_shape=jax.ShapeDtypeStruct((owned, width), jnp.int16),
         compiler_params=params,
         name="proxy_blocks",
-    )(offset, *far_pieces, sums, signs, matrix)
+    )(half, *far_pieces, sums, signs, matrix)
     far_total = swap(sent, near)
     near_total = pl.pallas_call(
         functools.partial(owner_kernel, near, base),
@@ -240,7 +254,7 @@
         out_shape=jax.ShapeDtypeStruct((owned, width), jnp.float32),
         compiler_params=params,
         name="owner_blocks",
-    )(offset, *near_pieces, sums, signs, matrix)
+    )(half, *near_pieces, sums, signs, matrix)
     total, mean_scale, squares = pl.pallas_call(
         functools.partial(finish_kernel, near),
         in_specs=[scalar] + [array] * 3,
@@ -251,7 +265,7 @@
         ),
         compiler_params=params,
         name="finish_blocks",
-    )(offset, near_total, far_total, sums)
+    )(half, near_total, far_total, sums)
     unrot = pl.pallas_call(
         functools.partial(back_kernel, base),
         out_shape=jax.ShapeDtypeStruct((owned, width), jnp.float32),

time: 59.6 us -> 60.9 us (1.022)
  waiting for transfers between devices: 21.2 us -> 26.9 us
  starting transfers between devices: 29.4 us -> 26.1 us
  local copies, waits for them, and re-layouts: 3.6 us -> 2.51 us
    ppermute x18 -> x16, waiting for transfers between devices: 11.8 us -> 16.8 us  [swap(): return lax.ppermute(value, 'dp', [(i, i ^ mask) for i in range(size)])]
    ppermute x18 -> x16, starting transfers between devices: 19.9 us -> 17.4 us  [swap(): return lax.ppermute(value, 'dp', [(i, i ^ mask) for i in range(size)])]
    reshape x0 -> x1, local copies, waits for them, and re-layouts: none -> 1.24 us  [pair_of(): lax.dynamic_slice_in_dim(halves, index % near, 1, 1)]
    unnamed x14 -> x12, local copies, waits for them, and re-layouts: 2.22 us -> 0.99 us
    reshape x2, local copies, waits for them, and re-layouts: 1.13 us -> 0.03 us  [block_of(): return lax.dynamic_slice_in_dim(source, index, 1, 0).reshape(owned, width)]
    all_to_all x1, starting transfers between devices: 3.29 us -> 2.54 us  [on_device(): lax.all_to_all(squares, ('dp', 'expert'), split_axis=0, concat_axis=0, ti...]
    all_to_all x1, waiting for transfers between devices: 2.69 us -> 3.39 us  [on_device(): lax.all_to_all(sums.reshape(replicas, 1, 2 * owned), 'dp', split_axis=0,...]
  transfers between devices with their start and end apart: 20 -> 18, of which waited for: 9 -> 9; matrix products, arithmetic and copies ran while one was open for 1% -> 0% of each run, Pallas kernels for 5% -> 5%
where the time goes in v12:
time: 60.9 us; the launch traced here: 60.7 us
  waiting for transfers between devices  26.9 us (44%)
  starting transfers between devices  26.1 us (43%)
  Pallas kernels  4.25 us (7%)
  local copies, waits for them, and re-layouts  2.51 us (4%)
  between operations  0.93 us (2%)
    ppermute x16, starting transfers between devices, swap(): return lax.ppermute(value, 'dp', [(i, i ^ mask) for i in range(size)])  17.4 us
    ppermute x16, waiting for transfers between devices, swap(): return lax.ppermute(value, 'dp', [(i, i ^ mask) for i in range(size)])  16.8 us
    all_to_all x1, waiting for transfers between devices, on_device(): lax.all_to_all(squares, ('dp', 'expert'), split_axis=0, concat_axis=0, ti...  6.72 us
    all_to_all x1, starting transfers between devices, on_device(): lax.all_to_all(sums.reshape(replicas, 1, 2 * owned), 'dp', split_axis=0,...  6.21 us
    all_to_all x1, waiting for transfers between devices, on_device(): lax.all_to_all(sums.reshape(replicas, 1, 2 * owned), 'dp', split_axis=0,...  3.39 us
    all_to_all x1, starting transfers between devices, on_device(): lax.all_to_all(squares, ('dp', 'expert'), split_axis=0, concat_axis=0, ti...  2.54 us
    reshape x1, local copies, waits for them, and re-layouts, pair_of(): lax.dynamic_slice_in_dim(halves, index % near, 1, 1)  1.24 us
  transfers between devices with their start and end apart: 18, of which 9 were waited for; matrix products, arithmetic and copies ran while one was open for 0% of the time, Pallas kernels for 5%

profile of v12, /device:TPU:0, one launch (start us, length us, event | category | flops | bytes accessed | tf_op | source)
XLA Modules:
  0.0 60.7 jit_solution(12417233275703643682)
XLA Ops:
  0.7 1.2 %dynamic-slice_bitcast_fusion = (bf16[2,64,1024]{2,1,0:T(8,128)(2,1)S(1)}, bf16[2,64,1024]{2,1,0:T(8,128)(2,1)S(1)}, bf16[2,64,1024]{2,1,0:T(8,128)(2,1)S(1)}) fusion(bf16[2,4,64,1024]{3,2,1,0:T(8,128)(2,1)} %bitcast.47, s32[]{:T(128)S(6)} %select_n.66, s32[]{:T(128)S(6)} %select_n.64, s32[]{:T(128)S(6)} %select_n.62), kind=kLoop, calls=%fused_computation | loop fusion | bytes 1572876 | tf_op jit(solution)/shard_map/reshape | solution.py:220
  1.9 3.0 %collective-permute-start = (bf16[2,64,1024]{2,1,0:T(8,128)(2,1)S(1)}, bf16[2,64,1024]{2,1,0:T(8,128)(2,1)S(1)}, u32[]{:S(2)}, u32[]{:S(2)}) collective-permute-start(bf16[2,64,1024]{2,1,0:T(8,128)(2,1)S(1)} %get-tuple-element.21), channel_id=1, source_target_pairs={{0,4},{4,0},{8,12},{12,8},{16,20},{20,16},{24,28},{28,24},{1,5},{5... | collective-permute-start | bytes 786440 | tf_op jit(solution)/shard_map/ppermute | solution.py:171
  5.0 1.6 %collective-permute-start.1 = (bf16[2,64,1024]{2,1,0:T(8,128)(2,1)S(1)}, bf16[2,64,1024]{2,1,0:T(8,128)(2,1)S(1)}, u32[]{:S(2)}, u32[]{:S(2)}) collective-permute-start(bf16[2,64,1024]{2,1,0:T(8,128)(2,1)S(1)} %get-tuple-element.20), channel_id=1, source_target_pairs={{0,8},{4,12},{8,0},{12,4},{16,24},{20,28},{24,16},{28,20},{1,9},{5... | collective-permute-start | bytes 786440 | tf_op jit(solution)/shard_map/ppermute | solution.py:171
  6.6 0.9 %sum_squares.1 = f32[2,4,1,128]{3,2,1,0:T(1,128)} custom-call(bf16[2,4,64,1024]{3,2,1,0:T(8,128)(2,1)S(1)} %bitcast.49), custom_call_target="tpu_custom_call" | custom-call | tf_op jit(solution)/shard_map/sum_squares/pallas_call | solution.py:231
  7.5 6.2 %all-to-all-start = ((f32[8,1,128]{2,1,0:T(1,128)}), f32[8,1,128]{2,1,0:T(1,128)S(1)}, u32[]{:S(2)}, u32[]{:S(2)}) async-start(f32[8,1,128]{2,1,0:T(1,128)} %bitcast.8), calls=%async_computation | async-start | bytes 8192 | tf_op jit(solution)/shard_map/all_to_all | solution.py:239
  13.7 3.0 %collective-permute-start.2 = (bf16[64,1024]{1,0:T(8,128)(2,1)S(1)}, bf16[64,1024]{1,0:T(8,128)(2,1)S(1)}, u32[]{:S(2)}, u32[]{:S(2)}) collective-permute-start(bf16[64,1024]{1,0:T(8,128)(2,1)S(1)} %dynamic-slice_bitcast_fusion.4), channel_id=1, source_target_pairs={{0,12},{4,8},{8,4},{12,0},{16,28},{20,24},{24,20},{28,16},{1,13},{... | collective-permute-start | bytes 393224 | tf_op jit(solution)/shard_map/ppermute | solution.py:171
  16.7 3.4 %all-to-all-done = f32[8,1,128]{2,1,0:T(1,128)S(1)} async-done(((f32[8,1,128]{2,1,0:T(1,128)}), f32[8,1,128]{2,1,0:T(1,128)S(1)}, u32[]{:S(2)}, u32[]{:S(2)}) %all-to-all-start) | async-done | bytes 4128 | tf_op jit(solution)/shard_map/all_to_all | solution.py:239
  21.9 6.1 %collective-permute-done.4.far_ref = s16[64,1024]{1,0:T(8,128)(2,1)S(1)} collective-permute-done((s16[64,1024]{1,0:T(8,128)(2,1)S(1)}, s16[64,1024]{1,0:T(8,128)(2,1)S(1)}, u32[]{:S(2)}, u32[]{:S(2)}) %collective-permute-start.4) | collective-permute-done | bytes 131104 | tf_op jit(solution)/shard_map/ppermute | solution.py:171
  28.1 0.9 %finish_blocks.1 = (f32[64,1024]{1,0:T(8,128)S(1)}, f32[64,128]{1,0:T(8,128)S(1)}, f32[32,1,128]{2,1,0:T(1,128)}) custom-call(s32[1,1]{1,0:T(1,128)} %bitcast.half_ref, f32[64,1024]{1,0:T(8,128)S(1)} %owner_blocks.1.near_ref, s16[64,1024]{1,0:T(8,128)(2,1)S(1)} %collective-permute-done.4.far_ref, f32[8,128]{1,0:T(8,128)S(1)} %bitcast.57), custom_call_target="tpu_custom_call" | custom-call | tf_op jit(solution)/shard_map/finish_blocks/pallas_call | solution.py:258
  29.0 2.5 %all-to-all-start.1 = ((f32[32,1,128]{2,1,0:T(1,128)}), f32[32,1,128]{2,1,0:T(1,128)S(1)}, u32[]{:S(2)}, u32[]{:S(2)}) async-start(f32[32,1,128]{2,1,0:T(1,128)} %get-tuple-element.13), calls=%async_computation.1 | async-start | bytes 32768 | tf_op jit(solution)/shard_map/all_to_all | solution.py:275
  31.9 6.7 %all-to-all-done.1 = f32[32,1,128]{2,1,0:T(1,128)S(1)} async-done(((f32[32,1,128]{2,1,0:T(1,128)}), f32[32,1,128]{2,1,0:T(1,128)S(1)}, u32[]{:S(2)}, u32[]{:S(2)}) %all-to-all-start.1) | async-done | bytes 16416 | tf_op jit(solution)/shard_map/all_to_all | solution.py:275
  39.4 2.3 %collective-permute-start.6 = (bf16[32,1024]{1,0:T(8,128)(2,1)S(1)}, bf16[32,1024]{1,0:T(8,128)(2,1)S(1)}, u32[]{:S(2)}, u32[]{:S(2)}) collective-permute-start(bf16[32,1024]{1,0:T(8,128)(2,1)S(1)} %get-tuple-element.17), channel_id=1, source_target_pairs={{0,16},{4,20},{8,24},{12,28},{16,0},{20,4},{24,8},{28,12},{1,17},{... | collective-permute-start | bytes 196616 | tf_op jit(solution)/shard_map/ppermute | solution.py:171
  42.9 0.8 %update_grad.1 = f32[64,1024]{1,0:T(8,128)} custom-call(f32[32,128]{1,0:T(8,128)S(1)} %bitcast.52, f32[64,1024]{1,0:T(8,128)S(1)} %rotate_back.1.unrot_ref), custom_call_target="tpu_custom_call" | custom-call | tf_op jit(solution)/shard_map/update_grad/pallas_call | solution.py:286
  43.7 2.8 %collective-permute-done.5 = bf16[32,1024]{1,0:T(8,128)(2,1)S(1)} collective-permute-done((bf16[32,1024]{1,0:T(8,128)(2,1)S(1)}, bf16[32,1024]{1,0:T(8,128)(2,1)S(1)}, u32[]{:S(2)}, u32[]{:S(2)}) %collective-permute-start.5) | collective-permute-done | bytes 65568 | tf_op jit(solution)/shard_map/ppermute | solution.py:171
  46.5 1.3 %collective-permute-done.6 = bf16[32,1024]{1,0:T(8,128)(2,1)S(1)} collective-permute-done((bf16[32,1024]{1,0:T(8,128)(2,1)S(1)}, bf16[32,1024]{1,0:T(8,128)(2,1)S(1)}, u32[]{:S(2)}, u32[]{:S(2)}) %collective-permute-start.6) | collective-permute-done | bytes 65568 | tf_op jit(solution)/shard_map/ppermute | solution.py:171
  47.8 0.7 %collective-permute-start.12 = (bf16[32,1024]{1,0:T(8,128)(2,1)S(1)}, bf16[32,1024]{1,0:T(8,128)(2,1)S(1)}, u32[]{:S(2)}, u32[]{:S(2)}) collective-permute-start(bf16[32,1024]{1,0:T(8,128)(2,1)S(1)} %collective-permute-done.6), channel_id=1, source_target_pairs={{0,8},{4,12},{8,0},{12,4},{16,24},{20,28},{24,16},{28,20},{1,9},{5... | collective-permute-start | bytes 196616 | tf_op jit(solution)/shard_map/ppermute | solution.py:171
  48.7 0.7 %collective-permute-start.11 = (bf16[32,1024]{1,0:T(8,128)(2,1)S(1)}, bf16[32,1024]{1,0:T(8,128)(2,1)S(1)}, u32[]{:S(2)}, u32[]{:S(2)}) collective-permute-start(bf16[32,1024]{1,0:T(8,128)(2,1)S(1)} %collective-permute-done.5), channel_id=1, source_target_pairs={{0,4},{4,0},{8,12},{12,8},{16,20},{20,16},{24,28},{28,24},{1,5},{5... | collective-permute-start | bytes 196616 | tf_op jit(solution)/shard_map/ppermute | solution.py:171
  49.4 1.9 %collective-permute-done.9 = bf16[32,1024]{1,0:T(8,128)(2,1)S(1)} collective-permute-done((bf16[32,1024]{1,0:T(8,128)(2,1)S(1)}, bf16[32,1024]{1,0:T(8,128)(2,1)S(1)}, u32[]{:S(2)}, u32[]{:S(2)}) %collective-permute-start.9) | collective-permute-done | bytes 65568 | tf_op jit(solution)/shard_map/ppermute | solution.py:171
  51.3 1.4 %collective-permute-start.14 = (bf16[32,1024]{1,0:T(8,128)(2,1)S(1)}, bf16[32,1024]{1,0:T(8,128)(2,1)S(1)}, u32[]{:S(2)}, u32[]{:S(2)}) collective-permute-start(bf16[32,1024]{1,0:T(8,128)(2,1)S(1)} %collective-permute-done.6), channel_id=1, source_target_pairs={{0,4},{4,0},{8,12},{12,8},{16,20},{20,16},{24,28},{28,24},{1,5},{5... | collective-permute-start | bytes 196616 | tf_op jit(solution)/shard_map/ppermute | solution.py:171
  52.6 1.1 %collective-permute-start.10 = (bf16[32,1024]{1,0:T(8,128)(2,1)S(1)}, bf16[32,1024]{1,0:T(8,128)(2,1)S(1)}, u32[]{:S(2)}, u32[]{:S(2)}) collective-permute-start(bf16[32,1024]{1,0:T(8,128)(2,1)S(1)} %collective-permute-done.9), channel_id=1, source_target_pairs={{0,4},{4,0},{8,12},{12,8},{16,20},{20,16},{24,28},{28,24},{1,5},{5... | collective-permute-start | bytes 196616 | tf_op jit(solution)/shard_map/ppermute | solution.py:171
  53.7 0.9 %collective-permute-start.13 = (bf16[32,1024]{1,0:T(8,128)(2,1)S(1)}, bf16[32,1024]{1,0:T(8,128)(2,1)S(1)}, u32[]{:S(2)}, u32[]{:S(2)}) collective-permute-start(bf16[32,1024]{1,0:T(8,128)(2,1)S(1)} %collective-permute-done.12), channel_id=1, source_target_pairs={{0,4},{4,0},{8,12},{12,8},{16,20},{20,16},{24,28},{28,24},{1,5},{5... | collective-permute-start | bytes 196616 | tf_op jit(solution)/shard_map/ppermute | solution.py:171
  55.0 2.3 %collective-permute-done.10 = bf16[32,1024]{1,0:T(8,128)(2,1)S(1)} collective-permute-done((bf16[32,1024]{1,0:T(8,128)(2,1)S(1)}, bf16[32,1024]{1,0:T(8,128)(2,1)S(1)}, u32[]{:S(2)}, u32[]{:S(2)}) %collective-permute-start.10) | collective-permute-done | bytes 65568 | tf_op jit(solution)/shard_map/ppermute | solution.py:171
  58.0 1.7 %collective-permute-done.15 = bf16[64,1024]{1,0:T(8,128)(2,1)S(1)} collective-permute-done((bf16[64,1024]{1,0:T(8,128)(2,1)S(1)}, bf16[64,1024]{1,0:T(8,128)(2,1)S(1)}, u32[]{:S(2)}, u32[]{:S(2)}) %collective-permute-start.15) | collective-permute-done | bytes 131104 | tf_op jit(solution)/shard_map/ppermute | solution.py:171
  59.8 1.0 %copy-done.5 = bf16[8,64,1024]{2,1,0:T(8,128)(2,1)} copy-done((bf16[8,64,1024]{2,1,0:T(8,128)(2,1)}, bf16[8,64,1024]{2,1,0:T(8,128)(2,1)S(1)}, u32[]{:S(2)}) %copy-start.5) | copy-done | bytes 1048600
  (47 shorter events, 5.4 us)
Async XLA Ops:
  0.6 5.9 %copy-start = (bf16[1,1,512,1024]{3,2,1,0:T(8,128)(2,1)S(1)}, bf16[1,1,512,1024]{3,2,1,0:T(8,128)(2,1)}, u32[]{:S(2)}) copy-start(bf16[1,1,512,1024]{3,2,1,0:T(8,128)(2,1)} %param.5) | copy-start | bytes 3145732
  1.9 18.2 %collective-permute-start = (bf16[2,64,1024]{2,1,0:T(8,128)(2,1)S(1)}, bf16[2,64,1024]{2,1,0:T(8,128)(2,1)S(1)}, u32[]{:S(2)}, u32[]{:S(2)}) collective-permute-start(bf16[2,64,1024]{2,1,0:T(8,128)(2,1)S(1)} %get-tuple-element.21), channel_id=1, source_target_pairs={{0,4},{4,0},{8,12},{12,8},{16,20},{20,16},{24,28},{28,24},{1,5},{5... | collective-permute-start | bytes 786440 | tf_op jit(solution)/shard_map/ppermute | solution.py:171
  5.0 15.2 %collective-permute-start.1 = (bf16[2,64,1024]{2,1,0:T(8,128)(2,1)S(1)}, bf16[2,64,1024]{2,1,0:T(8,128)(2,1)S(1)}, u32[]{:S(2)}, u32[]{:S(2)}) collective-permute-start(bf16[2,64,1024]{2,1,0:T(8,128)(2,1)S(1)} %get-tuple-element.20), channel_id=1, source_target_pairs={{0,8},{4,12},{8,0},{12,4},{16,24},{20,28},{24,16},{28,20},{1,9},{5... | collective-permute-start | bytes 786440 | tf_op jit(solution)/shard_map/ppermute | solution.py:171
  6.5 13.6 %collective-permute-start.3 = (bf16[64,1024]{1,0:T(8,128)(2,1)S(1)}, bf16[64,1024]{1,0:T(8,128)(2,1)S(1)}, u32[]{:S(2)}, u32[]{:S(2)}) collective-permute-start(bf16[64,1024]{1,0:T(8,128)(2,1)S(1)} %dynamic-slice_bitcast_fusion.3), channel_id=1, source_target_pairs={{0,12},{4,8},{8,4},{12,0},{16,28},{20,24},{24,20},{28,16},{1,13},{... | collective-permute-start | bytes 393224 | tf_op jit(solution)/shard_map/ppermute | solution.py:171
  7.5 12.6 %all-to-all-start = ((f32[8,1,128]{2,1,0:T(1,128)}), f32[8,1,128]{2,1,0:T(1,128)S(1)}, u32[]{:S(2)}, u32[]{:S(2)}) async-start(f32[8,1,128]{2,1,0:T(1,128)} %bitcast.8), calls=%async_computation | async-start | bytes 8192 | tf_op jit(solution)/shard_map/all_to_all | solution.py:239
  13.7 6.4 %copy-start.1 = (bf16[256,256]{1,0:T(8,128)(2,1)S(1)}, bf16[256,256]{1,0:T(8,128)(2,1)}, u32[]{:S(2)}) copy-start(bf16[256,256]{1,0:T(8,128)(2,1)} %constant.58.clone.refs_6_.matrix_ref) | copy-start | bytes 393220
  13.7 7.6 %collective-permute-start.2 = (bf16[64,1024]{1,0:T(8,128)(2,1)S(1)}, bf16[64,1024]{1,0:T(8,128)(2,1)S(1)}, u32[]{:S(2)}, u32[]{:S(2)}) collective-permute-start(bf16[64,1024]{1,0:T(8,128)(2,1)S(1)} %dynamic-slice_bitcast_fusion.4), channel_id=1, source_target_pairs={{0,12},{4,8},{8,4},{12,0},{16,28},{20,24},{24,20},{28,16},{1,13},{... | collective-permute-start | bytes 393224 | tf_op jit(solution)/shard_map/ppermute | solution.py:171
  16.7 3.4 %copy-start.4 = (s32[1,1024]{1,0:T(1,128)S(1)}, s32[1,1024]{1,0:T(1,128)}, u32[]{:S(2)}) copy-start(s32[1,1024]{1,0:T(1,128)} %sign_ref.1) | copy-start | bytes 12292
  20.7 7.3 %collective-permute-start.4 = (s16[64,1024]{1,0:T(8,128)(2,1)S(1)}, s16[64,1024]{1,0:T(8,128)(2,1)S(1)}, u32[]{:S(2)}, u32[]{:S(2)}) collective-permute-start(s16[64,1024]{1,0:T(8,128)(2,1)S(1)} %proxy_blocks.1), channel_id=1, source_target_pairs={{0,16},{4,20},{8,24},{12,28},{16,0},{20,4},{24,8},{28,12},{1,17},{... | collective-permute-start | bytes 393224 | tf_op jit(solution)/shard_map/ppermute | solution.py:171
  29.0 9.6 %all-to-all-start.1 = ((f32[32,1,128]{2,1,0:T(1,128)}), f32[32,1,128]{2,1,0:T(1,128)S(1)}, u32[]{:S(2)}, u32[]{:S(2)}) async-start(f32[32,1,128]{2,1,0:T(1,128)} %get-tuple-element.13), calls=%async_computation.1 | async-start | bytes 32768 | tf_op jit(solution)/shard_map/all_to_all | solution.py:275
  31.5 7.1 %copy-start.2 = (bf16[1,64,1024]{2,1,0:T(8,128)(2,1)S(1)}, bf16[1,64,1024]{2,1,0:T(8,128)(2,1)}, u32[]{:S(2)}) copy-start(bf16[1,64,1024]{2,1,0:T(8,128)(2,1)} %param.7) | copy-start | bytes 393220
  31.5 7.1 %copy-start.3 = (bf16[1,64,1024]{2,1,0:T(8,128)(2,1)S(1)}, bf16[1,64,1024]{2,1,0:T(8,128)(2,1)}, u32[]{:S(2)}) copy-start(bf16[1,64,1024]{2,1,0:T(8,128)(2,1)} %param.8) | copy-start | bytes 393220
  38.8 7.7 %collective-permute-start.5 = (bf16[32,1024]{1,0:T(8,128)(2,1)S(1)}, bf16[32,1024]{1,0:T(8,128)(2,1)S(1)}, u32[]{:S(2)}, u32[]{:S(2)}) collective-permute-start(bf16[32,1024]{1,0:T(8,128)(2,1)S(1)} %get-tuple-element.16), channel_id=1, source_target_pairs={{0,16},{4,20},{8,24},{12,28},{16,0},{20,4},{24,8},{28,12},{1,17},{... | collective-permute-start | bytes 196616 | tf_op jit(solution)/shard_map/ppermute | solution.py:171
  39.4 8.4 %collective-permute-start.6 = (bf16[32,1024]{1,0:T(8,128)(2,1)S(1)}, bf16[32,1024]{1,0:T(8,128)(2,1)S(1)}, u32[]{:S(2)}, u32[]{:S(2)}) collective-permute-start(bf16[32,1024]{1,0:T(8,128)(2,1)S(1)} %get-tuple-element.17), channel_id=1, source_target_pairs={{0,16},{4,20},{8,24},{12,28},{16,0},{20,4},{24,8},{28,12},{1,17},{... | collective-permute-start | bytes 196616 | tf_op jit(solution)/shard_map/ppermute | solution.py:171
  41.8 12.0 %collective-permute-start.7 = (bf16[64,1024]{1,0:T(8,128)(2,1)S(1)}, bf16[64,1024]{1,0:T(8,128)(2,1)S(1)}, u32[]{:S(2)}, u32[]{:S(2)}) collective-permute-start(bf16[64,1024]{1,0:T(8,128)(2,1)S(1)} %get-tuple-element.18), channel_id=1, source_target_pairs={{0,4},{4,0},{8,12},{12,8},{16,20},{20,16},{24,28},{28,24},{1,5},{5... | collective-permute-start | bytes 393224 | tf_op jit(solution)/shard_map/ppermute | solution.py:171
  42.3 12.4 %collective-permute-start.8 = (bf16[64,1024]{1,0:T(8,128)(2,1)S(1)}, bf16[64,1024]{1,0:T(8,128)(2,1)S(1)}, u32[]{:S(2)}, u32[]{:S(2)}) collective-permute-start(bf16[64,1024]{1,0:T(8,128)(2,1)S(1)} %get-tuple-element.18), channel_id=1, source_target_pairs={{0,8},{4,12},{8,0},{12,4},{16,24},{20,28},{24,16},{28,20},{1,9},{5... | collective-permute-start | bytes 393224 | tf_op jit(solution)/shard_map/ppermute | solution.py:171
  46.5 4.8 %collective-permute-start.9 = (bf16[32,1024]{1,0:T(8,128)(2,1)S(1)}, bf16[32,1024]{1,0:T(8,128)(2,1)S(1)}, u32[]{:S(2)}, u32[]{:S(2)}) collective-permute-start(bf16[32,1024]{1,0:T(8,128)(2,1)S(1)} %collective-permute-done.5), channel_id=1, source_target_pairs={{0,8},{4,12},{8,0},{12,4},{16,24},{20,28},{24,16},{28,20},{1,9},{5... | collective-permute-start | bytes 196616 | tf_op jit(solution)/shard_map/ppermute | solution.py:171
  47.8 4.8 %collective-permute-start.12 = (bf16[32,1024]{1,0:T(8,128)(2,1)S(1)}, bf16[32,1024]{1,0:T(8,128)(2,1)S(1)}, u32[]{:S(2)}, u32[]{:S(2)}) collective-permute-start(bf16[32,1024]{1,0:T(8,128)(2,1)S(1)} %collective-permute-done.6), channel_id=1, source_target_pairs={{0,8},{4,12},{8,0},{12,4},{16,24},{20,28},{24,16},{28,20},{1,9},{5... | collective-permute-start | bytes 196616 | tf_op jit(solution)/shard_map/ppermute | solution.py:171
  48.7 8.6 %collective-permute-start.11 = (bf16[32,1024]{1,0:T(8,128)(2,1)S(1)}, bf16[32,1024]{1,0:T(8,128)(2,1)S(1)}, u32[]{:S(2)}, u32[]{:S(2)}) collective-permute-start(bf16[32,1024]{1,0:T(8,128)(2,1)S(1)} %collective-permute-done.5), channel_id=1, source_target_pairs={{0,4},{4,0},{8,12},{12,8},{16,20},{20,16},{24,28},{28,24},{1,5},{5... | collective-permute-start | bytes 196616 | tf_op jit(solution)/shard_map/ppermute | solution.py:171
  51.3 6.7 %collective-permute-start.14 = (bf16[32,1024]{1,0:T(8,128)(2,1)S(1)}, bf16[32,1024]{1,0:T(8,128)(2,1)S(1)}, u32[]{:S(2)}, u32[]{:S(2)}) collective-permute-start(bf16[32,1024]{1,0:T(8,128)(2,1)S(1)} %collective-permute-done.6), channel_id=1, source_target_pairs={{0,4},{4,0},{8,12},{12,8},{16,20},{20,16},{24,28},{28,24},{1,5},{5... | collective-permute-start | bytes 196616 | tf_op jit(solution)/shard_map/ppermute | solution.py:171
  52.6 4.6 %collective-permute-start.10 = (bf16[32,1024]{1,0:T(8,128)(2,1)S(1)}, bf16[32,1024]{1,0:T(8,128)(2,1)S(1)}, u32[]{:S(2)}, u32[]{:S(2)}) collective-permute-start(bf16[32,1024]{1,0:T(8,128)(2,1)S(1)} %collective-permute-done.9), channel_id=1, source_target_pairs={{0,4},{4,0},{8,12},{12,8},{16,20},{20,16},{24,28},{28,24},{1,5},{5... | collective-permute-start | bytes 196616 | tf_op jit(solution)/shard_map/ppermute | solution.py:171
  53.7 4.3 %collective-permute-start.13 = (bf16[32,1024]{1,0:T(8,128)(2,1)S(1)}, bf16[32,1024]{1,0:T(8,128)(2,1)S(1)}, u32[]{:S(2)}, u32[]{:S(2)}) collective-permute-start(bf16[32,1024]{1,0:T(8,128)(2,1)S(1)} %collective-permute-done.12), channel_id=1, source_target_pairs={{0,4},{4,0},{8,12},{12,8},{16,20},{20,16},{24,28},{28,24},{1,5},{5... | collective-permute-start | bytes 196616 | tf_op jit(solution)/shard_map/ppermute | solution.py:171
  54.7 5.0 %collective-permute-start.15 = (bf16[64,1024]{1,0:T(8,128)(2,1)S(1)}, bf16[64,1024]{1,0:T(8,128)(2,1)S(1)}, u32[]{:S(2)}, u32[]{:S(2)}) collective-permute-start(bf16[64,1024]{1,0:T(8,128)(2,1)S(1)} %collective-permute-done.7), channel_id=1, source_target_pairs={{0,8},{4,12},{8,0},{12,4},{16,24},{20,28},{24,16},{28,20},{1,9},{5... | collective-permute-start | bytes 393224 | tf_op jit(solution)/shard_map/ppermute | solution.py:171
  59.8 1.0 %copy-start.5 = (bf16[8,64,1024]{2,1,0:T(8,128)(2,1)}, bf16[8,64,1024]{2,1,0:T(8,128)(2,1)S(1)}, u32[]{:S(2)}) copy-start(bf16[8,64,1024]{2,1,0:T(8,128)(2,1)S(1)} %bitcast_dynamic-update-slice_fusion) | copy-start | bytes 3145732

commit v13 on v12

--- a/solution.py
+++ b/solution.py
@@ -147,15 +147,12 @@
     return limit / jnp.maximum(jnp.sqrt(squares), limit)
 
 
-def weights_kernel(limit, square_ref, unrot_ref, weight_ref, comp_ref, new_ref, *part_refs):
+def weights_kernel(limit, square_ref, unrot_ref, weight_ref, comp_ref, new_ref):
     update = unrot_ref[...] * clip_factor(limit, square_ref)
     summed = weight_ref[...].astype(jnp.float32) + (
         comp_ref[...].astype(jnp.float32) - learn_rate * update
     )
     new_ref[...] = summed.astype(jnp.bfloat16)
-    for p, part_ref in enumerate(part_refs):
-        rows = part_ref.shape[0]
-        part_ref[...] = summed[p * rows : (p + 1) * rows].astype(jnp.bfloat16)
 
 
 def update_kernel(limit, square_ref, unrot_ref, update_ref):
@@ -171,32 +168,73 @@
     return lax.ppermute(value, "dp", [(i, i ^ mask) for i in range(size)])
 
 
-def gather_blocks(block, parts, replicas):
+def place_kernel(places, owned, me_ref, *refs):
+    pieces, out_ref, sem = refs[: len(places)], refs[-2], refs[-1]
+    copies = []
+    for i, ((mask, row), piece) in enumerate(zip(places, pieces)):
+        start = pl.multiple_of((me_ref[0, 0] ^ mask) * owned + row, 16)
+        rows = pl.ds(start, piece.shape[0])
+        copies.append(pltpu.make_async_copy(piece, out_ref.at[rows], sem.at[i]))
+    for copy in copies:
+        copy.start()
+    for copy in copies:
+        copy.wait()
+
+
+def place_pieces(items, owned, replicas, out, name):
+    places = [(mask, row) for mask, row, _ in items]
+    values = [piece for _, _, piece in items]
+    me = lax.axis_index("dp").astype(jnp.int32).reshape(1, 1)
+    operands, aliases = [me, *values], {}
+    specs = [pl.BlockSpec(memory_space=pltpu.SMEM)]
+    specs += [pl.BlockSpec(memory_space=pltpu.VMEM)] * len(values)
+    if out is not None:
+        aliases = {len(operands): 0}
+        operands.append(out)
+        specs.append(pl.BlockSpec(memory_space=pl.ANY))
+    width = values[0].shape[1]
+    return pl.pallas_call(
+        functools.partial(place_kernel, places, owned),
+        in_specs=specs,
+        out_specs=pl.BlockSpec(memory_space=pl.ANY),
+        out_shape=jax.ShapeDtypeStruct((replicas * owned, width), values[0].dtype),
+        scratch_shapes=[pltpu.SemaphoreType.DMA((len(values),))],
+        input_output_aliases=aliases,
+        compiler_params=pltpu.CompilerParams(vmem_limit_bytes=vmem_bytes),
+        name=name,
+    )(*operands)
+
+
+def gather_blocks(block, replicas):
     x_count = chips_along_x(replicas)
     near = replicas // 2
     me = lax.axis_index("dp")
     owned, width = block.shape
-    rows = owned // len(parts)
     along_x = range(1, x_count)
     along_z = range(x_count, near, x_count)
-    across = [swap(part, near) for part in parts]
-    pieces = [(near, p * rows, piece) for p, piece in enumerate(across)] + [(0, 0, block)]
+    far = swap(block, near)
     own_x = {x: swap(block, x) for x in along_x}
     own_z = {z: swap(block, z) for z in along_z}
+    pieces = [(near, 0, far), (0, 0, block)]
     pieces += [(mask, 0, piece) for mask, piece in (own_x | own_z).items()]
-    for p, piece in enumerate(across):
-        row = p * rows
-        moved = {z: swap(piece, z) for z in along_z}
-        pieces += [(near + z, row, value) for z, value in moved.items()]
-        moved[0] = piece
-        for z, value in moved.items():
-            pieces += [(near + z + x, row, swap(value, x)) for x in along_x]
+    aligned = [near + mask for mask in own_x | own_z]
+    rows = owned // 2
+    routes = []
+    for p, (firsts, seconds) in enumerate([(along_z, along_x), (along_x, along_z)]):
+        part = far[p * rows : (p + 1) * rows]
+        routes.append((p * rows, part, {m: swap(part, m) for m in firsts}, seconds))
+        pieces += [(near + m, p * rows, value) for m, value in routes[-1][2].items()]
+    for row, part, moved, seconds in routes:
+        pieces += [(near + k, row, swap(part, k)) for k in seconds]
     for x, piece in own_x.items():
-        piece, _ = lax.optimization_barrier((piece, across[-1]))
         pieces += [(x + z, 0, swap(piece, z)) for z in along_z]
-    out = jnp.zeros((replicas, owned, width), block.dtype)
-    for mask, row, piece in pieces:
-        out = lax.dynamic_update_slice(out, piece[None], (me ^ mask, row, 0))
+    for row, part, moved, seconds in routes:
+        for m, value in moved.items():
+            pieces += [(near + m + k, row, swap(value, k)) for k in seconds]
+    last = [item for item in pieces if item[0] >= near and item[0] not in (near, *aligned)]
+    early = [item for item in pieces if item not in last]
+    out = place_pieces(early, owned, replicas, None, "place_early")
+    out = place_pieces(last, owned, replicas, out, "place_last")
     return out.reshape(1, replicas * owned, width)
 
 
@@ -275,11 +313,9 @@
     squares = lax.all_to_all(squares, ("dp", "expert"), split_axis=0, concat_axis=0, tiled=True)
     limit = target_rms * math.sqrt(blocks * width * lax.axis_size("expert"))
     squares = squares.reshape(devices, lanes)
-    count = 2 if owned % 32 == 0 else 1
-    new_weights, *parts = pl.pallas_call(
+    new_weights = pl.pallas_call(
         functools.partial(weights_kernel, limit),
-        out_shape=[jax.ShapeDtypeStruct((owned, width), jnp.bfloat16)]
-        + [jax.ShapeDtypeStruct((owned // count, width), jnp.bfloat16)] * count,
+        out_shape=jax.ShapeDtypeStruct((owned, width), jnp.bfloat16),
         compiler_params=params,
         name="new_weights",
     )(squares, unrot, weights.reshape(owned, width), compensation.reshape(owned, width))
@@ -289,7 +325,7 @@
         compiler_params=params,
         name="update_grad",
     )(squares, unrot)
-    return gather_blocks(new_weights, parts, replicas), update_grad.reshape(weights.shape)
+    return gather_blocks(new_weights, replicas), update_grad.reshape(weights.shape)
 
 
 def solution(mesh):

time: 60.9 us -> 59.2 us (0.972)
  starting transfers between devices: 26.1 us -> 23.8 us
  Pallas kernels: 4.25 us -> 5.89 us
  local copies, waits for them, and re-layouts: 2.51 us -> 1.3 us
    ppermute x16 -> x15, starting transfers between devices: 17.4 us -> 15.1 us  [swap(): return lax.ppermute(value, 'dp', [(i, i ^ mask) for i in range(size)])]
    pallas_call x1 -> x3, Pallas kernels: 0.17 us -> 1.82 us  [the longest x2 1.66 us: place_pieces(): pl.pallas_call(functools.partial(place_kernel, places, owned), in_specs=s...]
    unnamed x12 -> x10, local copies, waits for them, and re-layouts: 0.99 us -> 0.02 us
    ppermute x16 -> x15, waiting for transfers between devices: 16.8 us -> 17.1 us  [swap(): return lax.ppermute(value, 'dp', [(i, i ^ mask) for i in range(size)])]
  transfers between devices with their start and end apart: 18 -> 17, of which waited for: 9 -> 9; matrix products, arithmetic and copies ran while one was open for 0% -> 0% of each run, Pallas kernels for 5% -> 7%
where the time goes in v13:
time: 59.2 us; the launch traced here: 59 us
  waiting for transfers between devices  27.2 us (46%)
  starting transfers between devices  23.8 us (40%)
  Pallas kernels  5.89 us (10%)
  local copies, waits for them, and re-layouts  1.3 us (2%)
  between operations  0.82 us (1%)
    ppermute x15, waiting for transfers between devices, swap(): return lax.ppermute(value, 'dp', [(i, i ^ mask) for i in range(size)])  17.1 us
    ppermute x15, starting transfers between devices, swap(): return lax.ppermute(value, 'dp', [(i, i ^ mask) for i in range(size)])  15.1 us
    all_to_all x1, waiting for transfers between devices, on_device(): lax.all_to_all(squares, ('dp', 'expert'), split_axis=0, concat_axis=0, ti...  6.72 us
    all_to_all x1, starting transfers between devices, on_device(): lax.all_to_all(sums.reshape(replicas, 1, 2 * owned), 'dp', split_axis=0,...  6.18 us
    all_to_all x1, waiting for transfers between devices, on_device(): lax.all_to_all(sums.reshape(replicas, 1, 2 * owned), 'dp', split_axis=0,...  3.39 us
    all_to_all x1, starting transfers between devices, on_device(): lax.all_to_all(squares, ('dp', 'expert'), split_axis=0, concat_axis=0, ti...  2.54 us
    pallas_call x2, Pallas kernels, place_pieces(): pl.pallas_call(functools.partial(place_kernel, places, owned), in_specs=s...  1.66 us
    reshape x1, local copies, waits for them, and re-layouts, pair_of(): lax.dynamic_slice_in_dim(halves, index % near, 1, 1)  1.25 us
  transfers between devices with their start and end apart: 17, of which 9 were waited for; matrix products, arithmetic and copies ran while one was open for 0% of the time, Pallas kernels for 7%

profile of v13, /device:TPU:0, one launch (start us, length us, event | category | flops | bytes accessed | tf_op | source)
XLA Modules:
  0.0 59.0 jit_solution(13603113490462174903)
XLA Ops:
  0.7 1.2 %dynamic-slice_bitcast_fusion = (bf16[2,64,1024]{2,1,0:T(8,128)(2,1)S(1)}, bf16[2,64,1024]{2,1,0:T(8,128)(2,1)S(1)}, bf16[2,64,1024]{2,1,0:T(8,128)(2,1)S(1)}) fusion(bf16[2,4,64,1024]{3,2,1,0:T(8,128)(2,1)} %bitcast.24, s32[]{:T(128)S(6)} %select_n.40, s32[]{:T(128)S(6)} %select_n.38, s32[]{:T(128)S(6)} %select_n.36), kind=kLoop, calls=%fused_computation | loop fusion | bytes 1572876 | tf_op jit(solution)/shard_map/reshape | solution.py:258
  1.9 3.1 %collective-permute-start.1 = (bf16[2,64,1024]{2,1,0:T(8,128)(2,1)S(1)}, bf16[2,64,1024]{2,1,0:T(8,128)(2,1)S(1)}, u32[]{:S(2)}, u32[]{:S(2)}) collective-permute-start(bf16[2,64,1024]{2,1,0:T(8,128)(2,1)S(1)} %get-tuple-element.12), channel_id=1, source_target_pairs={{0,8},{4,12},{8,0},{12,4},{16,24},{20,28},{24,16},{28,20},{1,9},{5... | collective-permute-start | bytes 786440 | tf_op jit(solution)/shard_map/ppermute | solution.py:168
  5.0 1.5 %collective-permute-start = (bf16[2,64,1024]{2,1,0:T(8,128)(2,1)S(1)}, bf16[2,64,1024]{2,1,0:T(8,128)(2,1)S(1)}, u32[]{:S(2)}, u32[]{:S(2)}) collective-permute-start(bf16[2,64,1024]{2,1,0:T(8,128)(2,1)S(1)} %get-tuple-element.13), channel_id=1, source_target_pairs={{0,4},{4,0},{8,12},{12,8},{16,20},{20,16},{24,28},{28,24},{1,5},{5... | collective-permute-start | bytes 786440 | tf_op jit(solution)/shard_map/ppermute | solution.py:168
  6.7 0.9 %sum_squares.1 = f32[2,4,1,128]{3,2,1,0:T(1,128)} custom-call(bf16[2,4,64,1024]{3,2,1,0:T(8,128)(2,1)S(1)} %bitcast.26), custom_call_target="tpu_custom_call" | custom-call | tf_op jit(solution)/shard_map/sum_squares/pallas_call | solution.py:269
  7.5 6.2 %all-to-all-start = ((f32[8,1,128]{2,1,0:T(1,128)}), f32[8,1,128]{2,1,0:T(1,128)S(1)}, u32[]{:S(2)}, u32[]{:S(2)}) async-start(f32[8,1,128]{2,1,0:T(1,128)} %bitcast.9), calls=%async_computation | async-start | bytes 8192 | tf_op jit(solution)/shard_map/all_to_all | solution.py:277
  13.7 3.0 %collective-permute-start.2 = (bf16[64,1024]{1,0:T(8,128)(2,1)S(1)}, bf16[64,1024]{1,0:T(8,128)(2,1)S(1)}, u32[]{:S(2)}, u32[]{:S(2)}) collective-permute-start(bf16[64,1024]{1,0:T(8,128)(2,1)S(1)} %dynamic-slice_bitcast_fusion.4), channel_id=1, source_target_pairs={{0,12},{4,8},{8,4},{12,0},{16,28},{20,24},{24,20},{28,16},{1,13},{... | collective-permute-start | bytes 393224 | tf_op jit(solution)/shard_map/ppermute | solution.py:168
  16.7 3.4 %all-to-all-done = f32[8,1,128]{2,1,0:T(1,128)S(1)} async-done(((f32[8,1,128]{2,1,0:T(1,128)}), f32[8,1,128]{2,1,0:T(1,128)S(1)}, u32[]{:S(2)}, u32[]{:S(2)}) %all-to-all-start) | async-done | bytes 4128 | tf_op jit(solution)/shard_map/all_to_all | solution.py:277
  20.7 0.6 %collective-permute-start.4 = (s16[64,1024]{1,0:T(8,128)(2,1)S(1)}, s16[64,1024]{1,0:T(8,128)(2,1)S(1)}, u32[]{:S(2)}, u32[]{:S(2)}) collective-permute-start(s16[64,1024]{1,0:T(8,128)(2,1)S(1)} %proxy_blocks.1), channel_id=1, source_target_pairs={{0,16},{4,20},{8,24},{12,28},{16,0},{20,4},{24,8},{28,12},{1,17},{... | collective-permute-start | bytes 393224 | tf_op jit(solution)/shard_map/ppermute | solution.py:168
  21.9 6.1 %collective-permute-done.4.far_ref = s16[64,1024]{1,0:T(8,128)(2,1)S(1)} collective-permute-done((s16[64,1024]{1,0:T(8,128)(2,1)S(1)}, s16[64,1024]{1,0:T(8,128)(2,1)S(1)}, u32[]{:S(2)}, u32[]{:S(2)}) %collective-permute-start.4) | collective-permute-done | bytes 131104 | tf_op jit(solution)/shard_map/ppermute | solution.py:168
  28.1 0.9 %finish_blocks.1 = (f32[64,1024]{1,0:T(8,128)S(1)}, f32[64,128]{1,0:T(8,128)S(1)}, f32[32,1,128]{2,1,0:T(1,128)}) custom-call(s32[1,1]{1,0:T(1,128)} %bitcast.1.half_ref, f32[64,1024]{1,0:T(8,128)S(1)} %owner_blocks.1.near_ref, s16[64,1024]{1,0:T(8,128)(2,1)S(1)} %collective-permute-done.4.far_ref, f32[8,128]{1,0:T(8,128)S(1)} %bitcast.34), custom_call_target="tpu_custom_call" | custom-call | tf_op jit(solution)/shard_map/finish_blocks/pallas_call | solution.py:296
  29.0 2.5 %all-to-all-start.1 = ((f32[32,1,128]{2,1,0:T(1,128)}), f32[32,1,128]{2,1,0:T(1,128)S(1)}, u32[]{:S(2)}, u32[]{:S(2)}) async-start(f32[32,1,128]{2,1,0:T(1,128)} %get-tuple-element.9), calls=%async_computation.1 | async-start | bytes 32768 | tf_op jit(solution)/shard_map/all_to_all | solution.py:313
  31.9 6.7 %all-to-all-done.1 = f32[32,1,128]{2,1,0:T(1,128)S(1)} async-done(((f32[32,1,128]{2,1,0:T(1,128)}), f32[32,1,128]{2,1,0:T(1,128)S(1)}, u32[]{:S(2)}, u32[]{:S(2)}) %all-to-all-start.1) | async-done | bytes 16416 | tf_op jit(solution)/shard_map/all_to_all | solution.py:313
  38.8 0.6 %collective-permute-start.10 = (bf16[64,1024]{1,0:T(8,128)(2,1)S(1)}, bf16[64,1024]{1,0:T(8,128)(2,1)S(1)}, u32[]{:S(2)}, u32[]{:S(2)}) collective-permute-start(bf16[64,1024]{1,0:T(8,128)(2,1)S(1)} %new_weights.1.refs_1_), channel_id=1, source_target_pairs={{0,4},{4,0},{8,12},{12,8},{16,20},{20,16},{24,28},{28,24},{1,5},{5... | collective-permute-start | bytes 393224 | tf_op jit(solution)/shard_map/ppermute | solution.py:168
  40.5 3.6 %collective-permute-done.10.refs_2_ = bf16[64,1024]{1,0:T(8,128)(2,1)S(1)} collective-permute-done((bf16[64,1024]{1,0:T(8,128)(2,1)S(1)}, bf16[64,1024]{1,0:T(8,128)(2,1)S(1)}, u32[]{:S(2)}, u32[]{:S(2)}) %collective-permute-start.10) | collective-permute-done | bytes 131104 | tf_op jit(solution)/shard_map/ppermute | solution.py:168
  44.5 3.6 %collective-permute-done.5.refs_0_ = bf16[64,1024]{1,0:T(8,128)(2,1)S(1)} collective-permute-done((bf16[64,1024]{1,0:T(8,128)(2,1)S(1)}, bf16[64,1024]{1,0:T(8,128)(2,1)S(1)}, u32[]{:S(2)}, u32[]{:S(2)}) %collective-permute-start.5) | collective-permute-done | bytes 131104 | tf_op jit(solution)/shard_map/ppermute | solution.py:168
  48.2 1.4 %collective-permute-start.8 = (bf16[32,1024]{1,0:T(8,128)(2,1)S(1)}, bf16[32,1024]{1,0:T(8,128)(2,1)S(1)}, u32[]{:S(2)}, u32[]{:S(2)}) collective-permute-start(bf16[32,1024]{1,0:T(8,128)(2,1)S(1)} %get-tuple-element.15), channel_id=1, source_target_pairs={{0,4},{4,0},{8,12},{12,8},{16,20},{20,16},{24,28},{28,24},{1,5},{5... | collective-permute-start | bytes 196616 | tf_op jit(solution)/shard_map/ppermute | solution.py:168
  49.6 2.0 %collective-permute-start.13 = (bf16[32,1024]{1,0:T(8,128)(2,1)S(1)}, bf16[32,1024]{1,0:T(8,128)(2,1)S(1)}, u32[]{:S(2)}, u32[]{:S(2)}) collective-permute-start(bf16[32,1024]{1,0:T(8,128)(2,1)S(1)} %get-tuple-element.15), channel_id=1, source_target_pairs={{0,8},{4,12},{8,0},{12,4},{16,24},{20,28},{24,16},{28,20},{1,9},{5... | collective-permute-start | bytes 196616 | tf_op jit(solution)/shard_map/ppermute | solution.py:168
  51.6 0.7 %collective-permute-start.12 = (bf16[32,1024]{1,0:T(8,128)(2,1)S(1)}, bf16[32,1024]{1,0:T(8,128)(2,1)S(1)}, u32[]{:S(2)}, u32[]{:S(2)}) collective-permute-start(bf16[32,1024]{1,0:T(8,128)(2,1)S(1)} %get-tuple-element.16), channel_id=1, source_target_pairs={{0,4},{4,0},{8,12},{12,8},{16,20},{20,16},{24,28},{28,24},{1,5},{5... | collective-permute-start | bytes 196616 | tf_op jit(solution)/shard_map/ppermute | solution.py:168
  52.5 1.6 %collective-permute-done.6.refs_4_ = bf16[32,1024]{1,0:T(8,128)(2,1)S(1)} collective-permute-done((bf16[32,1024]{1,0:T(8,128)(2,1)S(1)}, bf16[32,1024]{1,0:T(8,128)(2,1)S(1)}, u32[]{:S(2)}, u32[]{:S(2)}) %collective-permute-start.6) | collective-permute-done | bytes 65568 | tf_op jit(solution)/shard_map/ppermute | solution.py:168
  54.6 0.8 %update_grad.1 = f32[64,1024]{1,0:T(8,128)} custom-call(f32[32,128]{1,0:T(8,128)S(1)} %bitcast.29, f32[64,1024]{1,0:T(8,128)S(1)} %rotate_back.1.unrot_ref), custom_call_target="tpu_custom_call" | custom-call | tf_op jit(solution)/shard_map/update_grad/pallas_call | solution.py:322
  55.4 1.1 %collective-permute-done.12.refs_6_ = bf16[32,1024]{1,0:T(8,128)(2,1)S(1)} collective-permute-done((bf16[32,1024]{1,0:T(8,128)(2,1)S(1)}, bf16[32,1024]{1,0:T(8,128)(2,1)S(1)}, u32[]{:S(2)}, u32[]{:S(2)}) %collective-permute-start.12) | collective-permute-done | bytes 65568 | tf_op jit(solution)/shard_map/ppermute | solution.py:168
  56.5 1.0 %place_early.1.refs_2_ = bf16[512,1024]{1,0:T(8,128)(2,1)} custom-call(s32[1,1]{1,0:T(1,128)} %bitcast.me_ref, bf16[64,1024]{1,0:T(8,128)(2,1)S(1)} %collective-permute-done.5.refs_0_, bf16[64,1024]{1,0:T(8,128)(2,1)S(1)} %new_weights.1.refs_1_, bf16[64,1024]{1,0:T(8,128)(2,1)S(1)} %collective-permute-done.10.refs_2_, ...), custom_call_target="tpu_custom_call" | custom-call | tf_op jit(solution)/shard_map/place_early/pallas_call | solution.py:196
  57.6 0.8 %collective-permute-done.7.refs_0_ = bf16[32,1024]{1,0:T(8,128)(2,1)S(1)} collective-permute-done((bf16[32,1024]{1,0:T(8,128)(2,1)S(1)}, bf16[32,1024]{1,0:T(8,128)(2,1)S(1)}, u32[]{:S(2)}, u32[]{:S(2)}) %collective-permute-start.7) | collective-permute-done | bytes 65568 | tf_op jit(solution)/shard_map/ppermute | solution.py:168
  58.3 0.7 %place_last.1 = bf16[512,1024]{1,0:T(8,128)(2,1)} custom-call(s32[1,1]{1,0:T(1,128)} %bitcast.me_ref, bf16[32,1024]{1,0:T(8,128)(2,1)S(1)} %collective-permute-done.7.refs_0_, bf16[32,1024]{1,0:T(8,128)(2,1)S(1)} %collective-permute-done.9.refs_1_, bf16[512,1024]{1,0:T(8,128)(2,1)} %place_early.1.refs_2_), custom_call_target="tpu_custom_call", output_to_operand_aliasing={{}: (3, {})} | custom-call | tf_op jit(solution)/shard_map/place_last/pallas_call | solution.py:196
  (33 shorter events, 4.1 us)
Async XLA Ops:
  0.6 5.9 %copy-start = (bf16[1,1,512,1024]{3,2,1,0:T(8,128)(2,1)S(1)}, bf16[1,1,512,1024]{3,2,1,0:T(8,128)(2,1)}, u32[]{:S(2)}) copy-start(bf16[1,1,512,1024]{3,2,1,0:T(8,128)(2,1)} %param.5) | copy-start | bytes 3145732
  1.9 18.2 %collective-permute-start.1 = (bf16[2,64,1024]{2,1,0:T(8,128)(2,1)S(1)}, bf16[2,64,1024]{2,1,0:T(8,128)(2,1)S(1)}, u32[]{:S(2)}, u32[]{:S(2)}) collective-permute-start(bf16[2,64,1024]{2,1,0:T(8,128)(2,1)S(1)} %get-tuple-element.12), channel_id=1, source_target_pairs={{0,8},{4,12},{8,0},{12,4},{16,24},{20,28},{24,16},{28,20},{1,9},{5... | collective-permute-start | bytes 786440 | tf_op jit(solution)/shard_map/ppermute | solution.py:168
  5.0 15.1 %collective-permute-start = (bf16[2,64,1024]{2,1,0:T(8,128)(2,1)S(1)}, bf16[2,64,1024]{2,1,0:T(8,128)(2,1)S(1)}, u32[]{:S(2)}, u32[]{:S(2)}) collective-permute-start(bf16[2,64,1024]{2,1,0:T(8,128)(2,1)S(1)} %get-tuple-element.13), channel_id=1, source_target_pairs={{0,4},{4,0},{8,12},{12,8},{16,20},{20,16},{24,28},{28,24},{1,5},{5... | collective-permute-start | bytes 786440 | tf_op jit(solution)/shard_map/ppermute | solution.py:168
  6.5 13.6 %collective-permute-start.3 = (bf16[64,1024]{1,0:T(8,128)(2,1)S(1)}, bf16[64,1024]{1,0:T(8,128)(2,1)S(1)}, u32[]{:S(2)}, u32[]{:S(2)}) collective-permute-start(bf16[64,1024]{1,0:T(8,128)(2,1)S(1)} %dynamic-slice_bitcast_fusion.3), channel_id=1, source_target_pairs={{0,12},{4,8},{8,4},{12,0},{16,28},{20,24},{24,20},{28,16},{1,13},{... | collective-permute-start | bytes 393224 | tf_op jit(solution)/shard_map/ppermute | solution.py:168
  7.5 12.6 %all-to-all-start = ((f32[8,1,128]{2,1,0:T(1,128)}), f32[8,1,128]{2,1,0:T(1,128)S(1)}, u32[]{:S(2)}, u32[]{:S(2)}) async-start(f32[8,1,128]{2,1,0:T(1,128)} %bitcast.9), calls=%async_computation | async-start | bytes 8192 | tf_op jit(solution)/shard_map/all_to_all | solution.py:277
  13.7 6.4 %copy-start.1 = (bf16[256,256]{1,0:T(8,128)(2,1)S(1)}, bf16[256,256]{1,0:T(8,128)(2,1)}, u32[]{:S(2)}) copy-start(bf16[256,256]{1,0:T(8,128)(2,1)} %constant.48.clone.refs_6_.matrix_ref) | copy-start | bytes 393220
  13.7 7.6 %collective-permute-start.2 = (bf16[64,1024]{1,0:T(8,128)(2,1)S(1)}, bf16[64,1024]{1,0:T(8,128)(2,1)S(1)}, u32[]{:S(2)}, u32[]{:S(2)}) collective-permute-start(bf16[64,1024]{1,0:T(8,128)(2,1)S(1)} %dynamic-slice_bitcast_fusion.4), channel_id=1, source_target_pairs={{0,12},{4,8},{8,4},{12,0},{16,28},{20,24},{24,20},{28,16},{1,13},{... | collective-permute-start | bytes 393224 | tf_op jit(solution)/shard_map/ppermute | solution.py:168
  16.7 3.4 %copy-start.4 = (s32[1,1024]{1,0:T(1,128)S(1)}, s32[1,1024]{1,0:T(1,128)}, u32[]{:S(2)}) copy-start(s32[1,1024]{1,0:T(1,128)} %sign_ref.1) | copy-start | bytes 12292
  20.7 7.3 %collective-permute-start.4 = (s16[64,1024]{1,0:T(8,128)(2,1)S(1)}, s16[64,1024]{1,0:T(8,128)(2,1)S(1)}, u32[]{:S(2)}, u32[]{:S(2)}) collective-permute-start(s16[64,1024]{1,0:T(8,128)(2,1)S(1)} %proxy_blocks.1), channel_id=1, source_target_pairs={{0,16},{4,20},{8,24},{12,28},{16,0},{20,4},{24,8},{28,12},{1,17},{... | collective-permute-start | bytes 393224 | tf_op jit(solution)/shard_map/ppermute | solution.py:168
  29.0 9.6 %all-to-all-start.1 = ((f32[32,1,128]{2,1,0:T(1,128)}), f32[32,1,128]{2,1,0:T(1,128)S(1)}, u32[]{:S(2)}, u32[]{:S(2)}) async-start(f32[32,1,128]{2,1,0:T(1,128)} %get-tuple-element.9), calls=%async_computation.1 | async-start | bytes 32768 | tf_op jit(solution)/shard_map/all_to_all | solution.py:313
  31.5 7.1 %copy-start.2 = (bf16[1,64,1024]{2,1,0:T(8,128)(2,1)S(1)}, bf16[1,64,1024]{2,1,0:T(8,128)(2,1)}, u32[]{:S(2)}) copy-start(bf16[1,64,1024]{2,1,0:T(8,128)(2,1)} %param.7) | copy-start | bytes 393220
  31.5 7.1 %copy-start.3 = (bf16[1,64,1024]{2,1,0:T(8,128)(2,1)S(1)}, bf16[1,64,1024]{2,1,0:T(8,128)(2,1)}, u32[]{:S(2)}) copy-start(bf16[1,64,1024]{2,1,0:T(8,128)(2,1)} %param.8) | copy-start | bytes 393220
  38.8 5.3 %collective-permute-start.10 = (bf16[64,1024]{1,0:T(8,128)(2,1)S(1)}, bf16[64,1024]{1,0:T(8,128)(2,1)S(1)}, u32[]{:S(2)}, u32[]{:S(2)}) collective-permute-start(bf16[64,1024]{1,0:T(8,128)(2,1)S(1)} %new_weights.1.refs_1_), channel_id=1, source_target_pairs={{0,4},{4,0},{8,12},{12,8},{16,20},{20,16},{24,28},{28,24},{1,5},{5... | collective-permute-start | bytes 393224 | tf_op jit(solution)/shard_map/ppermute | solution.py:168
  39.4 8.7 %collective-permute-start.5 = (bf16[64,1024]{1,0:T(8,128)(2,1)S(1)}, bf16[64,1024]{1,0:T(8,128)(2,1)S(1)}, u32[]{:S(2)}, u32[]{:S(2)}) collective-permute-start(bf16[64,1024]{1,0:T(8,128)(2,1)S(1)} %new_weights.1.refs_1_), channel_id=1, source_target_pairs={{0,16},{4,20},{8,24},{12,28},{16,0},{20,4},{24,8},{28,12},{1,17},{... | collective-permute-start | bytes 393224 | tf_op jit(solution)/shard_map/ppermute | solution.py:168
  40.0 11.6 %collective-permute-start.11 = (bf16[64,1024]{1,0:T(8,128)(2,1)S(1)}, bf16[64,1024]{1,0:T(8,128)(2,1)S(1)}, u32[]{:S(2)}, u32[]{:S(2)}) collective-permute-start(bf16[64,1024]{1,0:T(8,128)(2,1)S(1)} %new_weights.1.refs_1_), channel_id=1, source_target_pairs={{0,8},{4,12},{8,0},{12,4},{16,24},{20,28},{24,16},{28,20},{1,9},{5... | collective-permute-start | bytes 393224 | tf_op jit(solution)/shard_map/ppermute | solution.py:168
  44.1 12.4 %collective-permute-start.14 = (bf16[64,1024]{1,0:T(8,128)(2,1)S(1)}, bf16[64,1024]{1,0:T(8,128)(2,1)S(1)}, u32[]{:S(2)}, u32[]{:S(2)}) collective-permute-start(bf16[64,1024]{1,0:T(8,128)(2,1)S(1)} %collective-permute-done.10.refs_2_), channel_id=1, source_target_pairs={{0,8},{4,12},{8,0},{12,4},{16,24},{20,28},{24,16},{28,20},{1,9},{5... | collective-permute-start | bytes 393224 | tf_op jit(solution)/shard_map/ppermute | solution.py:168
  48.2 4.3 %collective-permute-start.8 = (bf16[32,1024]{1,0:T(8,128)(2,1)S(1)}, bf16[32,1024]{1,0:T(8,128)(2,1)S(1)}, u32[]{:S(2)}, u32[]{:S(2)}) collective-permute-start(bf16[32,1024]{1,0:T(8,128)(2,1)S(1)} %get-tuple-element.15), channel_id=1, source_target_pairs={{0,4},{4,0},{8,12},{12,8},{16,20},{20,16},{24,28},{28,24},{1,5},{5... | collective-permute-start | bytes 196616 | tf_op jit(solution)/shard_map/ppermute | solution.py:168
  49.6 4.5 %collective-permute-start.6 = (bf16[32,1024]{1,0:T(8,128)(2,1)S(1)}, bf16[32,1024]{1,0:T(8,128)(2,1)S(1)}, u32[]{:S(2)}, u32[]{:S(2)}) collective-permute-start(bf16[32,1024]{1,0:T(8,128)(2,1)S(1)} %get-tuple-element.16), channel_id=1, source_target_pairs={{0,8},{4,12},{8,0},{12,4},{16,24},{20,28},{24,16},{28,20},{1,9},{5... | collective-permute-start | bytes 196616 | tf_op jit(solution)/shard_map/ppermute | solution.py:168
  49.6 5.8 %collective-permute-start.13 = (bf16[32,1024]{1,0:T(8,128)(2,1)S(1)}, bf16[32,1024]{1,0:T(8,128)(2,1)S(1)}, u32[]{:S(2)}, u32[]{:S(2)}) collective-permute-start(bf16[32,1024]{1,0:T(8,128)(2,1)S(1)} %get-tuple-element.15), channel_id=1, source_target_pairs={{0,8},{4,12},{8,0},{12,4},{16,24},{20,28},{24,16},{28,20},{1,9},{5... | collective-permute-start | bytes 196616 | tf_op jit(solution)/shard_map/ppermute | solution.py:168
  51.6 4.9 %collective-permute-start.12 = (bf16[32,1024]{1,0:T(8,128)(2,1)S(1)}, bf16[32,1024]{1,0:T(8,128)(2,1)S(1)}, u32[]{:S(2)}, u32[]{:S(2)}) collective-permute-start(bf16[32,1024]{1,0:T(8,128)(2,1)S(1)} %get-tuple-element.16), channel_id=1, source_target_pairs={{0,4},{4,0},{8,12},{12,8},{16,20},{20,16},{24,28},{28,24},{1,5},{5... | collective-permute-start | bytes 196616 | tf_op jit(solution)/shard_map/ppermute | solution.py:168
  52.5 5.1 %collective-permute-start.9 = (bf16[32,1024]{1,0:T(8,128)(2,1)S(1)}, bf16[32,1024]{1,0:T(8,128)(2,1)S(1)}, u32[]{:S(2)}, u32[]{:S(2)}) collective-permute-start(bf16[32,1024]{1,0:T(8,128)(2,1)S(1)} %collective-permute-done.8.refs_5_), channel_id=1, source_target_pairs={{0,8},{4,12},{8,0},{12,4},{16,24},{20,28},{24,16},{28,20},{1,9},{5... | collective-permute-start | bytes 196616 | tf_op jit(solution)/shard_map/ppermute | solution.py:168
  54.1 4.3 %collective-permute-start.7 = (bf16[32,1024]{1,0:T(8,128)(2,1)S(1)}, bf16[32,1024]{1,0:T(8,128)(2,1)S(1)}, u32[]{:S(2)}, u32[]{:S(2)}) collective-permute-start(bf16[32,1024]{1,0:T(8,128)(2,1)S(1)} %collective-permute-done.6.refs_4_), channel_id=1, source_target_pairs={{0,4},{4,0},{8,12},{12,8},{16,20},{20,16},{24,28},{28,24},{1,5},{5... | collective-permute-start | bytes 196616 | tf_op jit(solution)/shard_map/ppermute | solution.py:168

commit v14 on v13

--- a/solution.py
+++ b/solution.py
@@ -94,10 +94,10 @@
     return totals
 
 
-def proxy_kernel(near, base, half_ref, *refs):
+def proxy_kernel(near, base, *refs):
     pieces, (sums_ref, sign_ref, matrix_ref, sent_ref) = refs[:near], refs[near:]
     owned, width = sent_ref.shape
-    half = 1 - half_ref[0, 0]
+    half = 1 - lax.axis_index("dp") // near
     scale, step = scale_rows(sums_ref, half * owned, owned, width, near)
     totals = add_levels(pieces, half, scale, sign_ref, matrix_ref, base)
     for g, total in enumerate(totals):
@@ -105,10 +105,10 @@
         sent_ref[:, g * base : (g + 1) * base] = value.astype(jnp.int16)
 
 
-def owner_kernel(near, base, half_ref, *refs):
+def owner_kernel(near, base, *refs):
     pieces, (sums_ref, sign_ref, matrix_ref, total_ref) = refs[:near], refs[near:]
     owned, width = total_ref.shape
-    half = half_ref[0, 0]
+    half = lax.axis_index("dp") // near
     scale, _ = scale_rows(sums_ref, half * owned, owned, width, near)
     totals = add_levels(pieces, half, scale, sign_ref, matrix_ref, base)
     for g, total in enumerate(totals):
@@ -116,10 +116,12 @@
 
 
 def finish_kernel(
-    near, half_ref, near_ref, far_ref, sums_ref, total_ref, scale_ref, square_ref
+    near, near_ref, far_ref, sums_ref, total_ref, scale_ref, square_ref
 ):
     owned, width = near_ref.shape
-    scale, step = scale_rows(sums_ref, half_ref[0, 0] * owned, owned, width, near)
+    scale, step = scale_rows(
+        sums_ref, lax.axis_index("dp") // near * owned, owned, width, near
+    )
     total = near_ref[...] + far_ref[...].astype(jnp.float32) * step
     mean_scale = scale / (2 * near)
     mean_rot = total * mean_scale
@@ -168,11 +170,12 @@
     return lax.ppermute(value, "dp", [(i, i ^ mask) for i in range(size)])
 
 
-def place_kernel(places, owned, me_ref, *refs):
+def place_kernel(places, owned, *refs):
     pieces, out_ref, sem = refs[: len(places)], refs[-2], refs[-1]
+    me = lax.axis_index("dp")
     copies = []
     for i, ((mask, row), piece) in enumerate(zip(places, pieces)):
-        start = pl.multiple_of((me_ref[0, 0] ^ mask) * owned + row, 16)
+        start = pl.multiple_of((me ^ mask) * owned + row, 16)
         rows = pl.ds(start, piece.shape[0])
         copies.append(pltpu.make_async_copy(piece, out_ref.at[rows], sem.at[i]))
     for copy in copies:
@@ -184,10 +187,8 @@
 def place_pieces(items, owned, replicas, out, name):
     places = [(mask, row) for mask, row, _ in items]
     values = [piece for _, _, piece in items]
-    me = lax.axis_index("dp").astype(jnp.int32).reshape(1, 1)
-    operands, aliases = [me, *values], {}
-    specs = [pl.BlockSpec(memory_space=pltpu.SMEM)]
-    specs += [pl.BlockSpec(memory_space=pltpu.VMEM)] * len(values)
+    operands, aliases = list(values), {}
+    specs = [pl.BlockSpec(memory_space=pltpu.VMEM)] * len(values)
     if out is not None:
         aliases = {len(operands): 0}
         operands.append(out)
@@ -233,7 +234,10 @@
             pieces += [(near + m + k, row, swap(value, k)) for k in seconds]
     last = [item for item in pieces if item[0] >= near and item[0] not in (near, *aligned)]
     early = [item for item in pieces if item not in last]
-    out = place_pieces(early, owned, replicas, None, "place_early")
+    own = [item for item in early if item[0] < near]
+    early = [item for item in early if item not in own]
+    out = place_pieces(own, owned, replicas, None, "place_own")
+    out = place_pieces(early, owned, replicas, out, "place_early")
     out = place_pieces(last, owned, replicas, out, "place_last")
     return out.reshape(1, replicas * owned, width)
 
@@ -247,15 +251,12 @@
     matrix = jnp.asarray(hadamard(base), jnp.bfloat16)
     me = lax.axis_index("dp")
     near = replicas // 2
-    half = (me // near).astype(jnp.int32).reshape(1, 1)
     params = pltpu.CompilerParams(vmem_limit_bytes=vmem_bytes)
-    scalar = pl.BlockSpec(memory_space=pltpu.SMEM)
     array = pl.BlockSpec(memory_space=pltpu.VMEM)
 
-    halves = grads.reshape(2, near, owned, width)
-
-    def pair_of(index):
-        return lax.dynamic_slice_in_dim(halves, index % near, 1, 1).reshape(2, owned, width)
+    def pair_of(source, index):
+        source = source.reshape(2, near, owned, width)
+        return lax.dynamic_slice_in_dim(source, index % near, 1, 1).reshape(2, owned, width)
 
     def block_of(source, index):
         source = source.reshape(replicas, owned, width)
@@ -264,38 +265,40 @@
     x_count = chips_along_x(replicas)
     aligned = [m for m in range(1, near) if m % x_count == 0 or m < x_count]
     diagonal = [m for m in range(1, near) if m not in aligned]
-    pairs = [pair_of(me)] + [swap(pair_of(me ^ mask), mask) for mask in aligned]
-    far_pieces = pairs + [swap(block_of(grads, me ^ mask ^ near), mask) for mask in diagonal]
+    pairs = [swap(pair_of(grads, me ^ mask), mask) for mask in aligned]
+    far_pieces = [swap(block_of(grads, me ^ mask ^ near), mask) for mask in diagonal]
     sums = pl.pallas_call(
         sums_kernel,
         in_specs=[array],
         out_shape=jax.ShapeDtypeStruct((2, near, 1, 2 * owned), jnp.float32),
         compiler_params=params,
         name="sum_squares",
-    )(halves)
+    )(grads.reshape(2, near, owned, width))
     later, sums = lax.optimization_barrier((grads, sums))
     sums = lax.all_to_all(
         sums.reshape(replicas, 1, 2 * owned), "dp", split_axis=0, concat_axis=0, tiled=True
     ).reshape(replicas, 2 * owned)
+    pairs.append(pair_of(later, me))
+    far_pieces = pairs + far_pieces
     near_pieces = pairs + [swap(block_of(later, me ^ mask), mask) for mask in diagonal]
     sent = pl.pallas_call(
         functools.partial(proxy_kernel, near, base),
-        in_specs=[scalar] + [array] * (near + 3),
+        in_specs=[array] * (near + 3),
         out_shape=jax.ShapeDtypeStruct((owned, width), jnp.int16),
         compiler_params=params,
         name="proxy_blocks",
-    )(half, *far_pieces, sums, signs, matrix)
+    )(*far_pieces, sums, signs, matrix)
     far_total = swap(sent, near)
     near_total = pl.pallas_call(
         functools.partial(owner_kernel, near, base),
-        in_specs=[scalar] + [array] * (near + 3),
+        in_specs=[array] * (near + 3),
         out_shape=jax.ShapeDtypeStruct((owned, width), jnp.float32),
         compiler_params=params,
         name="owner_blocks",
-    )(half, *near_pieces, sums, signs, matrix)
+    )(*near_pieces, sums, signs, matrix)
     total, mean_scale, squares = pl.pallas_call(
         functools.partial(finish_kernel, near),
-        in_specs=[scalar] + [array] * 3,
+        in_specs=[array] * 3,
         out_shape=(
             jax.ShapeDtypeStruct((owned, width), jnp.float32),
             jax.ShapeDtypeStruct((owned, lanes), jnp.float32),
@@ -303,7 +306,7 @@
         ),
         compiler_params=params,
         name="finish_blocks",
-    )(half, near_total, far_total, sums)
+    )(near_total, far_total, sums)
     unrot = pl.pallas_call(
         functools.partial(back_kernel, base),
         out_shape=jax.ShapeDtypeStruct((owned, width), jnp.float32),

time: 59.2 us -> 59.1 us (level)
  waiting for transfers between devices: 27.2 us -> 24.6 us
  starting transfers between devices: 23.8 us -> 25.8 us
  Pallas kernels: 5.89 us -> 6.52 us
    ppermute x15, waiting for transfers between devices: 17.1 us -> 14.5 us  [swap(): return lax.ppermute(value, 'dp', [(i, i ^ mask) for i in range(size)])]
    ppermute x15, starting transfers between devices: 15.1 us -> 17 us  [swap(): return lax.ppermute(value, 'dp', [(i, i ^ mask) for i in range(size)])]
    pallas_call x2 -> x3, Pallas kernels: 1.66 us -> 2.28 us  [place_pieces(): pl.pallas_call(functools.partial(place_kernel, places, owned), in_specs=s...]
    reshape x1 -> x2, local copies, waits for them, and re-layouts: 1.25 us -> 1.17 us  [pair_of(): lax.dynamic_slice_in_dim(source, index % near, 1, 1)]
  transfers between devices with their start and end apart: 17 -> 17, of which waited for: 9 -> 7; matrix products, arithmetic and copies ran while one was open for 0% -> 0% of each run, Pallas kernels for 7% -> 8%
where the time goes in v14:
time: 59.1 us; the launch traced here: 58.9 us
  starting transfers between devices  25.8 us (44%)
  waiting for transfers between devices  24.6 us (42%)
  Pallas kernels  6.52 us (11%)
  local copies, waits for them, and re-layouts  1.22 us (2%)
  between operations  0.84 us (1%)
    ppermute x15, starting transfers between devices, swap(): return lax.ppermute(value, 'dp', [(i, i ^ mask) for i in range(size)])  17 us
    ppermute x15, waiting for transfers between devices, swap(): return lax.ppermute(value, 'dp', [(i, i ^ mask) for i in range(size)])  14.5 us
    all_to_all x1, waiting for transfers between devices, on_device(): lax.all_to_all(squares, ('dp', 'expert'), split_axis=0, concat_axis=0, ti...  6.73 us
    all_to_all x1, starting transfers between devices, on_device(): lax.all_to_all(sums.reshape(replicas, 1, 2 * owned), 'dp', split_axis=0,...  6.21 us
    all_to_all x1, waiting for transfers between devices, on_device(): lax.all_to_all(sums.reshape(replicas, 1, 2 * owned), 'dp', split_axis=0,...  3.36 us
    all_to_all x1, starting transfers between devices, on_device(): lax.all_to_all(squares, ('dp', 'expert'), split_axis=0, concat_axis=0, ti...  2.54 us
    pallas_call x3, Pallas kernels, place_pieces(): pl.pallas_call(functools.partial(place_kernel, places, owned), in_specs=s...  2.28 us
  transfers between devices with their start and end apart: 17, of which 7 were waited for; matrix products, arithmetic and copies ran while one was open for 0% of the time, Pallas kernels for 8%

profile of v14, /device:TPU:0, one launch (start us, length us, event | category | flops | bytes accessed | tf_op | source)
XLA Modules:
  0.0 58.9 jit_solution(680645333851199194)
XLA Ops:
  0.7 1.2 %dynamic-slice_bitcast_fusion.1 = (bf16[2,64,1024]{2,1,0:T(8,128)(2,1)S(1)}, bf16[2,64,1024]{2,1,0:T(8,128)(2,1)S(1)}) fusion(bf16[2,4,64,1024]{3,2,1,0:T(8,128)(2,1)} %bitcast.25, s32[]{:T(128)S(6)} %select_n.33, s32[]{:T(128)S(6)} %select_n.31), kind=kLoop, calls=%fused_computation.1 | loop fusion | bytes 1048584 | tf_op jit(solution)/shard_map/reshape | solution.py:259
  1.8 3.0 %collective-permute-start = (bf16[2,64,1024]{2,1,0:T(8,128)(2,1)S(1)}, bf16[2,64,1024]{2,1,0:T(8,128)(2,1)S(1)}, u32[]{:S(2)}, u32[]{:S(2)}) collective-permute-start(bf16[2,64,1024]{2,1,0:T(8,128)(2,1)S(1)} %get-tuple-element.13), channel_id=1, source_target_pairs={{0,4},{4,0},{8,12},{12,8},{16,20},{20,16},{24,28},{28,24},{1,5},{5... | collective-permute-start | bytes 786440 | tf_op jit(solution)/shard_map/ppermute | solution.py:170
  4.8 1.6 %collective-permute-start.1 = (bf16[2,64,1024]{2,1,0:T(8,128)(2,1)S(1)}, bf16[2,64,1024]{2,1,0:T(8,128)(2,1)S(1)}, u32[]{:S(2)}, u32[]{:S(2)}) collective-permute-start(bf16[2,64,1024]{2,1,0:T(8,128)(2,1)S(1)} %get-tuple-element.12), channel_id=1, source_target_pairs={{0,8},{4,12},{8,0},{12,4},{16,24},{20,28},{24,16},{28,20},{1,9},{5... | collective-permute-start | bytes 786440 | tf_op jit(solution)/shard_map/ppermute | solution.py:170
  6.5 0.9 %sum_squares.1 = f32[2,4,1,128]{3,2,1,0:T(1,128)} custom-call(bf16[2,4,64,1024]{3,2,1,0:T(8,128)(2,1)S(1)} %bitcast.27), custom_call_target="tpu_custom_call" | custom-call | tf_op jit(solution)/shard_map/sum_squares/pallas_call | solution.py:270
  7.4 6.2 %all-to-all-start = ((f32[8,1,128]{2,1,0:T(1,128)}), f32[8,1,128]{2,1,0:T(1,128)S(1)}, u32[]{:S(2)}, u32[]{:S(2)}) async-start(f32[8,1,128]{2,1,0:T(1,128)} %bitcast.8), calls=%async_computation | async-start | bytes 8192 | tf_op jit(solution)/shard_map/all_to_all | solution.py:278
  13.6 3.0 %collective-permute-start.2 = (bf16[64,1024]{1,0:T(8,128)(2,1)S(1)}, bf16[64,1024]{1,0:T(8,128)(2,1)S(1)}, u32[]{:S(2)}, u32[]{:S(2)}) collective-permute-start(bf16[64,1024]{1,0:T(8,128)(2,1)S(1)} %dynamic-slice_bitcast_fusion.4), channel_id=1, source_target_pairs={{0,12},{4,8},{8,4},{12,0},{16,28},{20,24},{24,20},{28,16},{1,13},{... | collective-permute-start | bytes 393224 | tf_op jit(solution)/shard_map/ppermute | solution.py:170
  16.6 3.4 %all-to-all-done = f32[8,1,128]{2,1,0:T(1,128)S(1)} async-done(((f32[8,1,128]{2,1,0:T(1,128)}), f32[8,1,128]{2,1,0:T(1,128)S(1)}, u32[]{:S(2)}, u32[]{:S(2)}) %all-to-all-start) | async-done | bytes 4128 | tf_op jit(solution)/shard_map/all_to_all | solution.py:278
  21.8 6.1 %collective-permute-done.4.far_ref = s16[64,1024]{1,0:T(8,128)(2,1)S(1)} collective-permute-done((s16[64,1024]{1,0:T(8,128)(2,1)S(1)}, s16[64,1024]{1,0:T(8,128)(2,1)S(1)}, u32[]{:S(2)}, u32[]{:S(2)}) %collective-permute-start.4) | collective-permute-done | bytes 131104 | tf_op jit(solution)/shard_map/ppermute | solution.py:170
  27.9 0.9 %finish_blocks.1 = (f32[64,1024]{1,0:T(8,128)S(1)}, f32[64,128]{1,0:T(8,128)S(1)}, f32[32,1,128]{2,1,0:T(1,128)}) custom-call(f32[64,1024]{1,0:T(8,128)S(1)} %owner_blocks.1.near_ref, s16[64,1024]{1,0:T(8,128)(2,1)S(1)} %collective-permute-done.4.far_ref, f32[8,128]{1,0:T(8,128)S(1)} %bitcast.36), custom_call_target="tpu_custom_call" | custom-call | tf_op jit(solution)/shard_map/finish_blocks/pallas_call | solution.py:299
  28.9 2.5 %all-to-all-start.1 = ((f32[32,1,128]{2,1,0:T(1,128)}), f32[32,1,128]{2,1,0:T(1,128)S(1)}, u32[]{:S(2)}, u32[]{:S(2)}) async-start(f32[32,1,128]{2,1,0:T(1,128)} %get-tuple-element.9), calls=%async_computation.1 | async-start | bytes 32768 | tf_op jit(solution)/shard_map/all_to_all | solution.py:316
  31.8 6.7 %all-to-all-done.1 = f32[32,1,128]{2,1,0:T(1,128)S(1)} async-done(((f32[32,1,128]{2,1,0:T(1,128)}), f32[32,1,128]{2,1,0:T(1,128)S(1)}, u32[]{:S(2)}, u32[]{:S(2)}) %all-to-all-start.1) | async-done | bytes 16416 | tf_op jit(solution)/shard_map/all_to_all | solution.py:316
  38.7 0.6 %collective-permute-start.12 = (bf16[64,1024]{1,0:T(8,128)(2,1)S(1)}, bf16[64,1024]{1,0:T(8,128)(2,1)S(1)}, u32[]{:S(2)}, u32[]{:S(2)}) collective-permute-start(bf16[64,1024]{1,0:T(8,128)(2,1)S(1)} %new_weights.1.refs_0_), channel_id=1, source_target_pairs={{0,4},{4,0},{8,12},{12,8},{16,20},{20,16},{24,28},{28,24},{1,5},{5... | collective-permute-start | bytes 393224 | tf_op jit(solution)/shard_map/ppermute | solution.py:170
  40.4 3.6 %collective-permute-done.12.refs_1_ = bf16[64,1024]{1,0:T(8,128)(2,1)S(1)} collective-permute-done((bf16[64,1024]{1,0:T(8,128)(2,1)S(1)}, bf16[64,1024]{1,0:T(8,128)(2,1)S(1)}, u32[]{:S(2)}, u32[]{:S(2)}) %collective-permute-start.12) | collective-permute-done | bytes 131104 | tf_op jit(solution)/shard_map/ppermute | solution.py:170
  44.5 3.6 %collective-permute-done.5.refs_0_ = bf16[64,1024]{1,0:T(8,128)(2,1)S(1)} collective-permute-done((bf16[64,1024]{1,0:T(8,128)(2,1)S(1)}, bf16[64,1024]{1,0:T(8,128)(2,1)S(1)}, u32[]{:S(2)}, u32[]{:S(2)}) %collective-permute-start.5) | collective-permute-done | bytes 131104 | tf_op jit(solution)/shard_map/ppermute | solution.py:170
  48.1 1.4 %collective-permute-start.8 = (bf16[32,1024]{1,0:T(8,128)(2,1)S(1)}, bf16[32,1024]{1,0:T(8,128)(2,1)S(1)}, u32[]{:S(2)}, u32[]{:S(2)}) collective-permute-start(bf16[32,1024]{1,0:T(8,128)(2,1)S(1)} %get-tuple-element.14), channel_id=1, source_target_pairs={{0,4},{4,0},{8,12},{12,8},{16,20},{20,16},{24,28},{28,24},{1,5},{5... | collective-permute-start | bytes 196616 | tf_op jit(solution)/shard_map/ppermute | solution.py:170
  49.5 0.7 %collective-permute-start.10 = (bf16[32,1024]{1,0:T(8,128)(2,1)S(1)}, bf16[32,1024]{1,0:T(8,128)(2,1)S(1)}, u32[]{:S(2)}, u32[]{:S(2)}) collective-permute-start(bf16[32,1024]{1,0:T(8,128)(2,1)S(1)} %get-tuple-element.15), channel_id=1, source_target_pairs={{0,4},{4,0},{8,12},{12,8},{16,20},{20,16},{24,28},{28,24},{1,5},{5... | collective-permute-start | bytes 196616 | tf_op jit(solution)/shard_map/ppermute | solution.py:170
  50.2 1.9 %collective-permute-start.11 = (bf16[32,1024]{1,0:T(8,128)(2,1)S(1)}, bf16[32,1024]{1,0:T(8,128)(2,1)S(1)}, u32[]{:S(2)}, u32[]{:S(2)}) collective-permute-start(bf16[32,1024]{1,0:T(8,128)(2,1)S(1)} %get-tuple-element.14), channel_id=1, source_target_pairs={{0,8},{4,12},{8,0},{12,4},{16,24},{20,28},{24,16},{28,20},{1,9},{5... | collective-permute-start | bytes 196616 | tf_op jit(solution)/shard_map/ppermute | solution.py:170
  52.6 1.3 %collective-permute-start.7 = (bf16[32,1024]{1,0:T(8,128)(2,1)S(1)}, bf16[32,1024]{1,0:T(8,128)(2,1)S(1)}, u32[]{:S(2)}, u32[]{:S(2)}) collective-permute-start(bf16[32,1024]{1,0:T(8,128)(2,1)S(1)} %collective-permute-done.6.refs_1_), channel_id=1, source_target_pairs={{0,4},{4,0},{8,12},{12,8},{16,20},{20,16},{24,28},{28,24},{1,5},{5... | collective-permute-start | bytes 196616 | tf_op jit(solution)/shard_map/ppermute | solution.py:170
  54.0 1.1 %collective-permute-start.9 = (bf16[32,1024]{1,0:T(8,128)(2,1)S(1)}, bf16[32,1024]{1,0:T(8,128)(2,1)S(1)}, u32[]{:S(2)}, u32[]{:S(2)}) collective-permute-start(bf16[32,1024]{1,0:T(8,128)(2,1)S(1)} %collective-permute-done.8.refs_2_), channel_id=1, source_target_pairs={{0,8},{4,12},{8,0},{12,4},{16,24},{20,28},{24,16},{28,20},{1,9},{5... | collective-permute-start | bytes 196616 | tf_op jit(solution)/shard_map/ppermute | solution.py:170
  55.1 0.8 %update_grad.1 = f32[64,1024]{1,0:T(8,128)} custom-call(f32[32,128]{1,0:T(8,128)S(1)} %bitcast.31, f32[64,1024]{1,0:T(8,128)S(1)} %rotate_back.1.unrot_ref), custom_call_target="tpu_custom_call" | custom-call | tf_op jit(solution)/shard_map/update_grad/pallas_call | solution.py:325
  55.9 0.8 %place_own.1.refs_5_ = bf16[512,1024]{1,0:T(8,128)(2,1)} custom-call(bf16[64,1024]{1,0:T(8,128)(2,1)S(1)} %new_weights.1.refs_0_, bf16[64,1024]{1,0:T(8,128)(2,1)S(1)} %collective-permute-done.12.refs_1_, bf16[64,1024]{1,0:T(8,128)(2,1)S(1)} %collective-permute-done.13.refs_2_, bf16[64,1024]{1,0:T(8,128)(2,1)S(1)} %collective-permute-done.14.refs_3_), custom_call_target="tpu_custom_call" | custom-call | tf_op jit(solution)/shard_map/place_own/pallas_call | solution.py:197
  56.8 0.8 %place_early.1.refs_2_ = bf16[512,1024]{1,0:T(8,128)(2,1)} custom-call(bf16[64,1024]{1,0:T(8,128)(2,1)S(1)} %collective-permute-done.5.refs_0_, bf16[32,1024]{1,0:T(8,128)(2,1)S(1)} %collective-permute-done.6.refs_1_, bf16[32,1024]{1,0:T(8,128)(2,1)S(1)} %collective-permute-done.8.refs_2_, ...), custom_call_target="tpu_custom_call", output_to_operand_aliasing={{}: (5, {})} | custom-call | tf_op jit(solution)/shard_map/place_early/pallas_call | solution.py:197
  57.6 0.6 %collective-permute-done.9.refs_1_ = bf16[32,1024]{1,0:T(8,128)(2,1)S(1)} collective-permute-done((bf16[32,1024]{1,0:T(8,128)(2,1)S(1)}, bf16[32,1024]{1,0:T(8,128)(2,1)S(1)}, u32[]{:S(2)}, u32[]{:S(2)}) %collective-permute-start.9) | collective-permute-done | bytes 65568 | tf_op jit(solution)/shard_map/ppermute | solution.py:170
  58.2 0.7 %place_last.1 = bf16[512,1024]{1,0:T(8,128)(2,1)} custom-call(bf16[32,1024]{1,0:T(8,128)(2,1)S(1)} %collective-permute-done.7.refs_0_, bf16[32,1024]{1,0:T(8,128)(2,1)S(1)} %collective-permute-done.9.refs_1_, bf16[512,1024]{1,0:T(8,128)(2,1)} %place_early.1.refs_2_), custom_call_target="tpu_custom_call", output_to_operand_aliasing={{}: (2, {})} | custom-call | tf_op jit(solution)/shard_map/place_last/pallas_call | solution.py:197
  (35 shorter events, 4.5 us)
Async XLA Ops:
  0.6 5.8 %copy-start = (bf16[1,1,512,1024]{3,2,1,0:T(8,128)(2,1)S(1)}, bf16[1,1,512,1024]{3,2,1,0:T(8,128)(2,1)}, u32[]{:S(2)}) copy-start(bf16[1,1,512,1024]{3,2,1,0:T(8,128)(2,1)} %param.5) | copy-start | bytes 3145732
  1.8 18.2 %collective-permute-start = (bf16[2,64,1024]{2,1,0:T(8,128)(2,1)S(1)}, bf16[2,64,1024]{2,1,0:T(8,128)(2,1)S(1)}, u32[]{:S(2)}, u32[]{:S(2)}) collective-permute-start(bf16[2,64,1024]{2,1,0:T(8,128)(2,1)S(1)} %get-tuple-element.13), channel_id=1, source_target_pairs={{0,4},{4,0},{8,12},{12,8},{16,20},{20,16},{24,28},{28,24},{1,5},{5... | collective-permute-start | bytes 786440 | tf_op jit(solution)/shard_map/ppermute | solution.py:170
  4.8 15.2 %collective-permute-start.1 = (bf16[2,64,1024]{2,1,0:T(8,128)(2,1)S(1)}, bf16[2,64,1024]{2,1,0:T(8,128)(2,1)S(1)}, u32[]{:S(2)}, u32[]{:S(2)}) collective-permute-start(bf16[2,64,1024]{2,1,0:T(8,128)(2,1)S(1)} %get-tuple-element.12), channel_id=1, source_target_pairs={{0,8},{4,12},{8,0},{12,4},{16,24},{20,28},{24,16},{28,20},{1,9},{5... | collective-permute-start | bytes 786440 | tf_op jit(solution)/shard_map/ppermute | solution.py:170
  6.4 13.6 %collective-permute-start.3 = (bf16[64,1024]{1,0:T(8,128)(2,1)S(1)}, bf16[64,1024]{1,0:T(8,128)(2,1)S(1)}, u32[]{:S(2)}, u32[]{:S(2)}) collective-permute-start(bf16[64,1024]{1,0:T(8,128)(2,1)S(1)} %dynamic-slice_bitcast_fusion.3), channel_id=1, source_target_pairs={{0,12},{4,8},{8,4},{12,0},{16,28},{20,24},{24,20},{28,16},{1,13},{... | collective-permute-start | bytes 393224 | tf_op jit(solution)/shard_map/ppermute | solution.py:170
  7.4 12.6 %all-to-all-start = ((f32[8,1,128]{2,1,0:T(1,128)}), f32[8,1,128]{2,1,0:T(1,128)S(1)}, u32[]{:S(2)}, u32[]{:S(2)}) async-start(f32[8,1,128]{2,1,0:T(1,128)} %bitcast.8), calls=%async_computation | async-start | bytes 8192 | tf_op jit(solution)/shard_map/all_to_all | solution.py:278
  13.6 7.6 %collective-permute-start.2 = (bf16[64,1024]{1,0:T(8,128)(2,1)S(1)}, bf16[64,1024]{1,0:T(8,128)(2,1)S(1)}, u32[]{:S(2)}, u32[]{:S(2)}) collective-permute-start(bf16[64,1024]{1,0:T(8,128)(2,1)S(1)} %dynamic-slice_bitcast_fusion.4), channel_id=1, source_target_pairs={{0,12},{4,8},{8,4},{12,0},{16,28},{20,24},{24,20},{28,16},{1,13},{... | collective-permute-start | bytes 393224 | tf_op jit(solution)/shard_map/ppermute | solution.py:170
  16.6 3.4 %copy-start.1 = (bf16[256,256]{1,0:T(8,128)(2,1)S(1)}, bf16[256,256]{1,0:T(8,128)(2,1)}, u32[]{:S(2)}) copy-start(bf16[256,256]{1,0:T(8,128)(2,1)} %constant.37.clone.refs_6_.matrix_ref) | copy-start | bytes 393220
  16.6 3.4 %copy-start.4 = (s32[1,1024]{1,0:T(1,128)S(1)}, s32[1,1024]{1,0:T(1,128)}, u32[]{:S(2)}) copy-start(s32[1,1024]{1,0:T(1,128)} %sign_ref.1) | copy-start | bytes 12292
  20.6 7.3 %collective-permute-start.4 = (s16[64,1024]{1,0:T(8,128)(2,1)S(1)}, s16[64,1024]{1,0:T(8,128)(2,1)S(1)}, u32[]{:S(2)}, u32[]{:S(2)}) collective-permute-start(s16[64,1024]{1,0:T(8,128)(2,1)S(1)} %proxy_blocks.1), channel_id=1, source_target_pairs={{0,16},{4,20},{8,24},{12,28},{16,0},{20,4},{24,8},{28,12},{1,17},{... | collective-permute-start | bytes 393224 | tf_op jit(solution)/shard_map/ppermute | solution.py:170
  28.9 9.6 %all-to-all-start.1 = ((f32[32,1,128]{2,1,0:T(1,128)}), f32[32,1,128]{2,1,0:T(1,128)S(1)}, u32[]{:S(2)}, u32[]{:S(2)}) async-start(f32[32,1,128]{2,1,0:T(1,128)} %get-tuple-element.9), calls=%async_computation.1 | async-start | bytes 32768 | tf_op jit(solution)/shard_map/all_to_all | solution.py:316
  31.4 7.1 %copy-start.2 = (bf16[1,64,1024]{2,1,0:T(8,128)(2,1)S(1)}, bf16[1,64,1024]{2,1,0:T(8,128)(2,1)}, u32[]{:S(2)}) copy-start(bf16[1,64,1024]{2,1,0:T(8,128)(2,1)} %param.7) | copy-start | bytes 393220
  31.4 7.1 %copy-start.3 = (bf16[1,64,1024]{2,1,0:T(8,128)(2,1)S(1)}, bf16[1,64,1024]{2,1,0:T(8,128)(2,1)}, u32[]{:S(2)}) copy-start(bf16[1,64,1024]{2,1,0:T(8,128)(2,1)} %param.8) | copy-start | bytes 393220
  38.7 5.3 %collective-permute-start.12 = (bf16[64,1024]{1,0:T(8,128)(2,1)S(1)}, bf16[64,1024]{1,0:T(8,128)(2,1)S(1)}, u32[]{:S(2)}, u32[]{:S(2)}) collective-permute-start(bf16[64,1024]{1,0:T(8,128)(2,1)S(1)} %new_weights.1.refs_0_), channel_id=1, source_target_pairs={{0,4},{4,0},{8,12},{12,8},{16,20},{20,16},{24,28},{28,24},{1,5},{5... | collective-permute-start | bytes 393224 | tf_op jit(solution)/shard_map/ppermute | solution.py:170
  39.3 8.7 %collective-permute-start.5 = (bf16[64,1024]{1,0:T(8,128)(2,1)S(1)}, bf16[64,1024]{1,0:T(8,128)(2,1)S(1)}, u32[]{:S(2)}, u32[]{:S(2)}) collective-permute-start(bf16[64,1024]{1,0:T(8,128)(2,1)S(1)} %new_weights.1.refs_0_), channel_id=1, source_target_pairs={{0,16},{4,20},{8,24},{12,28},{16,0},{20,4},{24,8},{28,12},{1,17},{... | collective-permute-start | bytes 393224 | tf_op jit(solution)/shard_map/ppermute | solution.py:170
  39.9 10.3 %collective-permute-start.13 = (bf16[64,1024]{1,0:T(8,128)(2,1)S(1)}, bf16[64,1024]{1,0:T(8,128)(2,1)S(1)}, u32[]{:S(2)}, u32[]{:S(2)}) collective-permute-start(bf16[64,1024]{1,0:T(8,128)(2,1)S(1)} %new_weights.1.refs_0_), channel_id=1, source_target_pairs={{0,8},{4,12},{8,0},{12,4},{16,24},{20,28},{24,16},{28,20},{1,9},{5... | collective-permute-start | bytes 393224 | tf_op jit(solution)/shard_map/ppermute | solution.py:170
  44.0 11.9 %collective-permute-start.14 = (bf16[64,1024]{1,0:T(8,128)(2,1)S(1)}, bf16[64,1024]{1,0:T(8,128)(2,1)S(1)}, u32[]{:S(2)}, u32[]{:S(2)}) collective-permute-start(bf16[64,1024]{1,0:T(8,128)(2,1)S(1)} %collective-permute-done.12.refs_1_), channel_id=1, source_target_pairs={{0,8},{4,12},{8,0},{12,4},{16,24},{20,28},{24,16},{28,20},{1,9},{5... | collective-permute-start | bytes 393224 | tf_op jit(solution)/shard_map/ppermute | solution.py:170
  48.0 4.6 %collective-permute-start.6 = (bf16[32,1024]{1,0:T(8,128)(2,1)S(1)}, bf16[32,1024]{1,0:T(8,128)(2,1)S(1)}, u32[]{:S(2)}, u32[]{:S(2)}) collective-permute-start(bf16[32,1024]{1,0:T(8,128)(2,1)S(1)} %get-tuple-element.15), channel_id=1, source_target_pairs={{0,8},{4,12},{8,0},{12,4},{16,24},{20,28},{24,16},{28,20},{1,9},{5... | collective-permute-start | bytes 196616 | tf_op jit(solution)/shard_map/ppermute | solution.py:170
  48.1 5.8 %collective-permute-start.8 = (bf16[32,1024]{1,0:T(8,128)(2,1)S(1)}, bf16[32,1024]{1,0:T(8,128)(2,1)S(1)}, u32[]{:S(2)}, u32[]{:S(2)}) collective-permute-start(bf16[32,1024]{1,0:T(8,128)(2,1)S(1)} %get-tuple-element.14), channel_id=1, source_target_pairs={{0,4},{4,0},{8,12},{12,8},{16,20},{20,16},{24,28},{28,24},{1,5},{5... | collective-permute-start | bytes 196616 | tf_op jit(solution)/shard_map/ppermute | solution.py:170
  49.5 7.2 %collective-permute-start.10 = (bf16[32,1024]{1,0:T(8,128)(2,1)S(1)}, bf16[32,1024]{1,0:T(8,128)(2,1)S(1)}, u32[]{:S(2)}, u32[]{:S(2)}) collective-permute-start(bf16[32,1024]{1,0:T(8,128)(2,1)S(1)} %get-tuple-element.15), channel_id=1, source_target_pairs={{0,4},{4,0},{8,12},{12,8},{16,20},{20,16},{24,28},{28,24},{1,5},{5... | collective-permute-start | bytes 196616 | tf_op jit(solution)/shard_map/ppermute | solution.py:170
  50.2 6.5 %collective-permute-start.11 = (bf16[32,1024]{1,0:T(8,128)(2,1)S(1)}, bf16[32,1024]{1,0:T(8,128)(2,1)S(1)}, u32[]{:S(2)}, u32[]{:S(2)}) collective-permute-start(bf16[32,1024]{1,0:T(8,128)(2,1)S(1)} %get-tuple-element.14), channel_id=1, source_target_pairs={{0,8},{4,12},{8,0},{12,4},{16,24},{20,28},{24,16},{28,20},{1,9},{5... | collective-permute-start | bytes 196616 | tf_op jit(solution)/shard_map/ppermute | solution.py:170
  52.6 4.9 %collective-permute-start.7 = (bf16[32,1024]{1,0:T(8,128)(2,1)S(1)}, bf16[32,1024]{1,0:T(8,128)(2,1)S(1)}, u32[]{:S(2)}, u32[]{:S(2)}) collective-permute-start(bf16[32,1024]{1,0:T(8,128)(2,1)S(1)} %collective-permute-done.6.refs_1_), channel_id=1, source_target_pairs={{0,4},{4,0},{8,12},{12,8},{16,20},{20,16},{24,28},{28,24},{1,5},{5... | collective-permute-start | bytes 196616 | tf_op jit(solution)/shard_map/ppermute | solution.py:170
  54.0 4.3 %collective-permute-start.9 = (bf16[32,1024]{1,0:T(8,128)(2,1)S(1)}, bf16[32,1024]{1,0:T(8,128)(2,1)S(1)}, u32[]{:S(2)}, u32[]{:S(2)}) collective-permute-start(bf16[32,1024]{1,0:T(8,128)(2,1)S(1)} %collective-permute-done.8.refs_2_), channel_id=1, source_target_pairs={{0,8},{4,12},{8,0},{12,4},{16,24},{20,28},{24,16},{28,20},{1,9},{5... | collective-permute-start | bytes 196616 | tf_op jit(solution)/shard_map/ppermute | solution.py:170

commit v15 on v14

--- a/solution.py
+++ b/solution.py
@@ -207,38 +207,13 @@
 
 
 def gather_blocks(block, replicas):
-    x_count = chips_along_x(replicas)
     near = replicas // 2
-    me = lax.axis_index("dp")
     owned, width = block.shape
-    along_x = range(1, x_count)
-    along_z = range(x_count, near, x_count)
     far = swap(block, near)
-    own_x = {x: swap(block, x) for x in along_x}
-    own_z = {z: swap(block, z) for z in along_z}
-    pieces = [(near, 0, far), (0, 0, block)]
-    pieces += [(mask, 0, piece) for mask, piece in (own_x | own_z).items()]
-    aligned = [near + mask for mask in own_x | own_z]
-    rows = owned // 2
-    routes = []
-    for p, (firsts, seconds) in enumerate([(along_z, along_x), (along_x, along_z)]):
-        part = far[p * rows : (p + 1) * rows]
-        routes.append((p * rows, part, {m: swap(part, m) for m in firsts}, seconds))
-        pieces += [(near + m, p * rows, value) for m, value in routes[-1][2].items()]
-    for row, part, moved, seconds in routes:
-        pieces += [(near + k, row, swap(part, k)) for k in seconds]
-    for x, piece in own_x.items():
-        pieces += [(x + z, 0, swap(piece, z)) for z in along_z]
-    for row, part, moved, seconds in routes:
-        for m, value in moved.items():
-            pieces += [(near + m + k, row, swap(value, k)) for k in seconds]
-    last = [item for item in pieces if item[0] >= near and item[0] not in (near, *aligned)]
-    early = [item for item in pieces if item not in last]
-    own = [item for item in early if item[0] < near]
-    early = [item for item in early if item not in own]
-    out = place_pieces(own, owned, replicas, None, "place_own")
-    out = place_pieces(early, owned, replicas, out, "place_early")
-    out = place_pieces(last, owned, replicas, out, "place_last")
+    own = [(0, 0, block)] + [(m, 0, swap(block, m)) for m in reversed(range(1, near))]
+    spread = [(near + m, 0, swap(far, m)) for m in range(1, near)]
+    out = place_pieces(own + [(near, 0, far)], owned, replicas, None, "place_own")
+    out = place_pieces(spread, owned, replicas, out, "place_far")
     return out.reshape(1, replicas * owned, width)
 
 

time: 59.1 us -> 64.7 us (1.095)
  waiting for transfers between devices: 24.6 us -> 27.9 us
  starting transfers between devices: 25.8 us -> 28.7 us
  Pallas kernels: 6.52 us -> 5.87 us
    ppermute x15 -> x12, waiting for transfers between devices: 14.5 us -> 21.2 us  [swap(): return lax.ppermute(value, 'dp', [(i, i ^ mask) for i in range(size)])]
    all_to_all x1, waiting for transfers between devices: 3.36 us -> 0.01 us  [on_device(): lax.all_to_all(sums.reshape(replicas, 1, 2 * owned), 'dp', split_axis=0,...]
    all_to_all x1, starting transfers between devices: 2.54 us -> 5.32 us  [on_device(): lax.all_to_all(squares, ('dp', 'expert'), split_axis=0, concat_axis=0, ti...]
    unnamed x10 -> x12, local copies, waits for them, and re-layouts: 0.02 us -> 1.24 us
    reshape x2, local copies, waits for them, and re-layouts: 1.17 us -> 0.06 us  [pair_of(): lax.dynamic_slice_in_dim(source, index % near, 1, 1)]
    all_to_all x1, starting transfers between devices: 6.21 us -> 7.25 us  [on_device(): lax.all_to_all(sums.reshape(replicas, 1, 2 * owned), 'dp', split_axis=0,...]
    ppermute x15 -> x12, starting transfers between devices: 17 us -> 16.1 us  [swap(): return lax.ppermute(value, 'dp', [(i, i ^ mask) for i in range(size)])]
    pallas_call x3 -> x2, Pallas kernels: 2.28 us -> 1.64 us  [place_pieces(): pl.pallas_call(functools.partial(place_kernel, places, owned), in_specs=s...]
  transfers between devices with their start and end apart: 17 -> 14, of which waited for: 7 -> 8; matrix products, arithmetic and copies ran while one was open for 0% -> 0% of each run, Pallas kernels for 8% -> 5%
where the time goes in v15:
time: 64.7 us; the launch traced here: 64.5 us
  starting transfers between devices  28.7 us (44%)
  waiting for transfers between devices  27.9 us (43%)
  Pallas kernels  5.87 us (9%)
  local copies, waits for them, and re-layouts  1.32 us (2%)
  between operations  0.74 us (1%)
    ppermute x12, waiting for transfers between devices, swap(): return lax.ppermute(value, 'dp', [(i, i ^ mask) for i in range(size)])  21.2 us
    ppermute x12, starting transfers between devices, swap(): return lax.ppermute(value, 'dp', [(i, i ^ mask) for i in range(size)])  16.1 us
    all_to_all x1, starting transfers between devices, on_device(): lax.all_to_all(sums.reshape(replicas, 1, 2 * owned), 'dp', split_axis=0,...  7.25 us
    all_to_all x1, waiting for transfers between devices, on_device(): lax.all_to_all(squares, ('dp', 'expert'), split_axis=0, concat_axis=0, ti...  6.72 us
    all_to_all x1, starting transfers between devices, on_device(): lax.all_to_all(squares, ('dp', 'expert'), split_axis=0, concat_axis=0, ti...  5.32 us
    pallas_call x2, Pallas kernels, place_pieces(): pl.pallas_call(functools.partial(place_kernel, places, owned), in_specs=s...  1.64 us
  transfers between devices with their start and end apart: 14, of which 8 were waited for; matrix products, arithmetic and copies ran while one was open for 0% of the time, Pallas kernels for 5%

profile of v15, /device:TPU:0, one launch (start us, length us, event | category | flops | bytes accessed | tf_op | source)
XLA Modules:
  0.0 64.5 jit_solution(3839961016049322473)
XLA Ops:
  0.6 1.2 %copy-done = bf16[1,1,512,1024]{3,2,1,0:T(8,128)(2,1)S(1)} copy-done((bf16[1,1,512,1024]{3,2,1,0:T(8,128)(2,1)S(1)}, bf16[1,1,512,1024]{3,2,1,0:T(8,128)(2,1)}, u32[]{:S(2)}) %copy-start) | copy-done | bytes 1048600
  1.9 0.9 %sum_squares.1 = f32[2,4,1,128]{3,2,1,0:T(1,128)} custom-call(bf16[2,4,64,1024]{3,2,1,0:T(8,128)(2,1)S(1)} %bitcast.25), custom_call_target="tpu_custom_call" | custom-call | tf_op jit(solution)/shard_map/sum_squares/pallas_call | solution.py:245
  2.7 7.3 %all-to-all-start = ((f32[8,1,128]{2,1,0:T(1,128)}), f32[8,1,128]{2,1,0:T(1,128)S(1)}, u32[]{:S(2)}, u32[]{:S(2)}) async-start(f32[8,1,128]{2,1,0:T(1,128)} %bitcast.8), calls=%async_computation | async-start | bytes 8192 | tf_op jit(solution)/shard_map/all_to_all | solution.py:253
  10.0 2.1 %collective-permute-start.1 = (bf16[2,64,1024]{2,1,0:T(8,128)(2,1)S(1)}, bf16[2,64,1024]{2,1,0:T(8,128)(2,1)S(1)}, u32[]{:S(2)}, u32[]{:S(2)}) collective-permute-start(bf16[2,64,1024]{2,1,0:T(8,128)(2,1)S(1)} %get-tuple-element.12), channel_id=1, source_target_pairs={{0,8},{4,12},{8,0},{12,4},{16,24},{20,28},{24,16},{28,20},{1,9},{5... | collective-permute-start | bytes 786440 | tf_op jit(solution)/shard_map/ppermute | solution.py:170
  12.1 1.5 %collective-permute-start = (bf16[2,64,1024]{2,1,0:T(8,128)(2,1)S(1)}, bf16[2,64,1024]{2,1,0:T(8,128)(2,1)S(1)}, u32[]{:S(2)}, u32[]{:S(2)}) collective-permute-start(bf16[2,64,1024]{2,1,0:T(8,128)(2,1)S(1)} %get-tuple-element.13), channel_id=1, source_target_pairs={{0,4},{4,0},{8,12},{12,8},{16,20},{20,16},{24,28},{28,24},{1,5},{5... | collective-permute-start | bytes 786440 | tf_op jit(solution)/shard_map/ppermute | solution.py:170
  13.7 2.9 %collective-permute-start.2 = (bf16[64,1024]{1,0:T(8,128)(2,1)S(1)}, bf16[64,1024]{1,0:T(8,128)(2,1)S(1)}, u32[]{:S(2)}, u32[]{:S(2)}) collective-permute-start(bf16[64,1024]{1,0:T(8,128)(2,1)S(1)} %dynamic-slice_bitcast_fusion.4), channel_id=1, source_target_pairs={{0,12},{4,8},{8,4},{12,0},{16,28},{20,24},{24,20},{28,16},{1,13},{... | collective-permute-start | bytes 393224 | tf_op jit(solution)/shard_map/ppermute | solution.py:170
  16.7 6.7 %collective-permute-done.3.refs_3_ = bf16[64,1024]{1,0:T(8,128)(2,1)S(1)} collective-permute-done((bf16[64,1024]{1,0:T(8,128)(2,1)S(1)}, bf16[64,1024]{1,0:T(8,128)(2,1)S(1)}, u32[]{:S(2)}, u32[]{:S(2)}) %collective-permute-start.3) | collective-permute-done | bytes 131104 | tf_op jit(solution)/shard_map/ppermute | solution.py:170
  23.4 1.1 %collective-permute-done.refs_0_ = bf16[2,64,1024]{2,1,0:T(8,128)(2,1)S(1)} collective-permute-done((bf16[2,64,1024]{2,1,0:T(8,128)(2,1)S(1)}, bf16[2,64,1024]{2,1,0:T(8,128)(2,1)S(1)}, u32[]{:S(2)}, u32[]{:S(2)}) %collective-permute-start) | collective-permute-done | bytes 262176 | tf_op jit(solution)/shard_map/ppermute | solution.py:170
  25.1 1.9 %collective-permute-start.4 = (s16[64,1024]{1,0:T(8,128)(2,1)S(1)}, s16[64,1024]{1,0:T(8,128)(2,1)S(1)}, u32[]{:S(2)}, u32[]{:S(2)}) collective-permute-start(s16[64,1024]{1,0:T(8,128)(2,1)S(1)} %proxy_blocks.1), channel_id=1, source_target_pairs={{0,16},{4,20},{8,24},{12,28},{16,0},{20,4},{24,8},{28,12},{1,17},{... | collective-permute-start | bytes 393224 | tf_op jit(solution)/shard_map/ppermute | solution.py:170
  27.6 4.6 %collective-permute-done.4.far_ref = s16[64,1024]{1,0:T(8,128)(2,1)S(1)} collective-permute-done((s16[64,1024]{1,0:T(8,128)(2,1)S(1)}, s16[64,1024]{1,0:T(8,128)(2,1)S(1)}, u32[]{:S(2)}, u32[]{:S(2)}) %collective-permute-start.4) | collective-permute-done | bytes 131104 | tf_op jit(solution)/shard_map/ppermute | solution.py:170
  32.1 0.9 %finish_blocks.1 = (f32[64,1024]{1,0:T(8,128)S(1)}, f32[64,128]{1,0:T(8,128)S(1)}, f32[32,1,128]{2,1,0:T(1,128)}) custom-call(f32[64,1024]{1,0:T(8,128)S(1)} %owner_blocks.1.near_ref, s16[64,1024]{1,0:T(8,128)(2,1)S(1)} %collective-permute-done.4.far_ref, f32[8,128]{1,0:T(8,128)S(1)} %bitcast.36), custom_call_target="tpu_custom_call" | custom-call | tf_op jit(solution)/shard_map/finish_blocks/pallas_call | solution.py:274
  33.1 5.3 %all-to-all-start.1 = ((f32[32,1,128]{2,1,0:T(1,128)}), f32[32,1,128]{2,1,0:T(1,128)S(1)}, u32[]{:S(2)}, u32[]{:S(2)}) async-start(f32[32,1,128]{2,1,0:T(1,128)} %get-tuple-element.9), calls=%async_computation.1 | async-start | bytes 32768 | tf_op jit(solution)/shard_map/all_to_all | solution.py:291
  38.7 6.7 %all-to-all-done.1 = f32[32,1,128]{2,1,0:T(1,128)S(1)} async-done(((f32[32,1,128]{2,1,0:T(1,128)}), f32[32,1,128]{2,1,0:T(1,128)S(1)}, u32[]{:S(2)}, u32[]{:S(2)}) %all-to-all-start.1) | async-done | bytes 16416 | tf_op jit(solution)/shard_map/all_to_all | solution.py:291
  45.6 0.7 %collective-permute-start.5 = (bf16[64,1024]{1,0:T(8,128)(2,1)S(1)}, bf16[64,1024]{1,0:T(8,128)(2,1)S(1)}, u32[]{:S(2)}, u32[]{:S(2)}) collective-permute-start(bf16[64,1024]{1,0:T(8,128)(2,1)S(1)} %new_weights.1.refs_0_), channel_id=1, source_target_pairs={{0,16},{4,20},{8,24},{12,28},{16,0},{20,4},{24,8},{28,12},{1,17},{... | collective-permute-start | bytes 393224 | tf_op jit(solution)/shard_map/ppermute | solution.py:170
  47.4 2.4 %collective-permute-start.9 = (bf16[64,1024]{1,0:T(8,128)(2,1)S(1)}, bf16[64,1024]{1,0:T(8,128)(2,1)S(1)}, u32[]{:S(2)}, u32[]{:S(2)}) collective-permute-start(bf16[64,1024]{1,0:T(8,128)(2,1)S(1)} %new_weights.1.refs_0_), channel_id=1, source_target_pairs={{0,12},{4,8},{8,4},{12,0},{16,28},{20,24},{24,20},{28,16},{1,13},{... | collective-permute-start | bytes 393224 | tf_op jit(solution)/shard_map/ppermute | solution.py:170
  49.8 4.9 %collective-permute-done.5.refs_4_ = bf16[64,1024]{1,0:T(8,128)(2,1)S(1)} collective-permute-done((bf16[64,1024]{1,0:T(8,128)(2,1)S(1)}, bf16[64,1024]{1,0:T(8,128)(2,1)S(1)}, u32[]{:S(2)}, u32[]{:S(2)}) %collective-permute-start.5) | collective-permute-done | bytes 131104 | tf_op jit(solution)/shard_map/ppermute | solution.py:170
  54.7 2.1 %collective-permute-start.7 = (bf16[64,1024]{1,0:T(8,128)(2,1)S(1)}, bf16[64,1024]{1,0:T(8,128)(2,1)S(1)}, u32[]{:S(2)}, u32[]{:S(2)}) collective-permute-start(bf16[64,1024]{1,0:T(8,128)(2,1)S(1)} %collective-permute-done.5.refs_4_), channel_id=1, source_target_pairs={{0,8},{4,12},{8,0},{12,4},{16,24},{20,28},{24,16},{28,20},{1,9},{5... | collective-permute-start | bytes 393224 | tf_op jit(solution)/shard_map/ppermute | solution.py:170
  56.8 1.4 %collective-permute-start.6 = (bf16[64,1024]{1,0:T(8,128)(2,1)S(1)}, bf16[64,1024]{1,0:T(8,128)(2,1)S(1)}, u32[]{:S(2)}, u32[]{:S(2)}) collective-permute-start(bf16[64,1024]{1,0:T(8,128)(2,1)S(1)} %collective-permute-done.5.refs_4_), channel_id=1, source_target_pairs={{0,4},{4,0},{8,12},{12,8},{16,20},{20,16},{24,28},{28,24},{1,5},{5... | collective-permute-start | bytes 393224 | tf_op jit(solution)/shard_map/ppermute | solution.py:170
  58.2 0.8 %update_grad.1 = f32[64,1024]{1,0:T(8,128)} custom-call(f32[32,128]{1,0:T(8,128)S(1)} %bitcast.31, f32[64,1024]{1,0:T(8,128)S(1)} %rotate_back.1.unrot_ref), custom_call_target="tpu_custom_call" | custom-call | tf_op jit(solution)/shard_map/update_grad/pallas_call | solution.py:300
  59.0 0.9 %place_own.1.refs_3_ = bf16[512,1024]{1,0:T(8,128)(2,1)} custom-call(bf16[64,1024]{1,0:T(8,128)(2,1)S(1)} %new_weights.1.refs_0_, bf16[64,1024]{1,0:T(8,128)(2,1)S(1)} %collective-permute-done.9.refs_1_, bf16[64,1024]{1,0:T(8,128)(2,1)S(1)} %collective-permute-done.10.refs_2_, bf16[64,1024]{1,0:T(8,128)(2,1)S(1)} %collective-permute-done.11.refs_3_, ...), custom_call_target="tpu_custom_call" | custom-call | tf_op jit(solution)/shard_map/place_own/pallas_call | solution.py:197
  59.9 2.1 %collective-permute-done.8.refs_2_ = bf16[64,1024]{1,0:T(8,128)(2,1)S(1)} collective-permute-done((bf16[64,1024]{1,0:T(8,128)(2,1)S(1)}, bf16[64,1024]{1,0:T(8,128)(2,1)S(1)}, u32[]{:S(2)}, u32[]{:S(2)}) %collective-permute-start.8) | collective-permute-done | bytes 131104 | tf_op jit(solution)/shard_map/ppermute | solution.py:170
  61.9 0.9 %collective-permute-done.7.refs_1_ = bf16[64,1024]{1,0:T(8,128)(2,1)S(1)} collective-permute-done((bf16[64,1024]{1,0:T(8,128)(2,1)S(1)}, bf16[64,1024]{1,0:T(8,128)(2,1)S(1)}, u32[]{:S(2)}, u32[]{:S(2)}) %collective-permute-start.7) | collective-permute-done | bytes 131104 | tf_op jit(solution)/shard_map/ppermute | solution.py:170
  62.9 0.9 %collective-permute-done.6.refs_0_ = bf16[64,1024]{1,0:T(8,128)(2,1)S(1)} collective-permute-done((bf16[64,1024]{1,0:T(8,128)(2,1)S(1)}, bf16[64,1024]{1,0:T(8,128)(2,1)S(1)}, u32[]{:S(2)}, u32[]{:S(2)}) %collective-permute-start.6) | collective-permute-done | bytes 131104 | tf_op jit(solution)/shard_map/ppermute | solution.py:170
  63.7 0.8 %place_far.1 = bf16[512,1024]{1,0:T(8,128)(2,1)} custom-call(bf16[64,1024]{1,0:T(8,128)(2,1)S(1)} %collective-permute-done.6.refs_0_, bf16[64,1024]{1,0:T(8,128)(2,1)S(1)} %collective-permute-done.7.refs_1_, bf16[64,1024]{1,0:T(8,128)(2,1)S(1)} %collective-permute-done.8.refs_2_, bf16[512,1024]{1,0:T(8,128)(2,1)} %place_own.1.refs_3_), custom_call_target="tpu_custom_call", output_to_operand_aliasing={{}: (3, {})} | custom-call | tf_op jit(solution)/shard_map/place_far/pallas_call | solution.py:197
  (29 shorter events, 3.0 us)
Async XLA Ops:
  0.6 1.2 %copy-start = (bf16[1,1,512,1024]{3,2,1,0:T(8,128)(2,1)S(1)}, bf16[1,1,512,1024]{3,2,1,0:T(8,128)(2,1)}, u32[]{:S(2)}) copy-start(bf16[1,1,512,1024]{3,2,1,0:T(8,128)(2,1)} %param.5) | copy-start | bytes 3145732
  1.9 8.1 %copy-start.1 = (bf16[1,1,512,1024]{3,2,1,0:T(8,128)(2,1)S(1)}, bf16[1,1,512,1024]{3,2,1,0:T(8,128)(2,1)}, u32[]{:S(2)}) copy-start(bf16[1,1,512,1024]{3,2,1,0:T(8,128)(2,1)} %param.5) | copy-start | bytes 3145732
  2.7 14.0 %all-to-all-start = ((f32[8,1,128]{2,1,0:T(1,128)}), f32[8,1,128]{2,1,0:T(1,128)S(1)}, u32[]{:S(2)}, u32[]{:S(2)}) async-start(f32[8,1,128]{2,1,0:T(1,128)} %bitcast.8), calls=%async_computation | async-start | bytes 8192 | tf_op jit(solution)/shard_map/all_to_all | solution.py:253
  10.0 13.4 %collective-permute-start.1 = (bf16[2,64,1024]{2,1,0:T(8,128)(2,1)S(1)}, bf16[2,64,1024]{2,1,0:T(8,128)(2,1)S(1)}, u32[]{:S(2)}, u32[]{:S(2)}) collective-permute-start(bf16[2,64,1024]{2,1,0:T(8,128)(2,1)S(1)} %get-tuple-element.12), channel_id=1, source_target_pairs={{0,8},{4,12},{8,0},{12,4},{16,24},{20,28},{24,16},{28,20},{1,9},{5... | collective-permute-start | bytes 786440 | tf_op jit(solution)/shard_map/ppermute | solution.py:170
  12.1 12.4 %collective-permute-start = (bf16[2,64,1024]{2,1,0:T(8,128)(2,1)S(1)}, bf16[2,64,1024]{2,1,0:T(8,128)(2,1)S(1)}, u32[]{:S(2)}, u32[]{:S(2)}) collective-permute-start(bf16[2,64,1024]{2,1,0:T(8,128)(2,1)S(1)} %get-tuple-element.13), channel_id=1, source_target_pairs={{0,4},{4,0},{8,12},{12,8},{16,20},{20,16},{24,28},{28,24},{1,5},{5... | collective-permute-start | bytes 786440 | tf_op jit(solution)/shard_map/ppermute | solution.py:170
  13.6 9.8 %collective-permute-start.3 = (bf16[64,1024]{1,0:T(8,128)(2,1)S(1)}, bf16[64,1024]{1,0:T(8,128)(2,1)S(1)}, u32[]{:S(2)}, u32[]{:S(2)}) collective-permute-start(bf16[64,1024]{1,0:T(8,128)(2,1)S(1)} %dynamic-slice_bitcast_fusion.3), channel_id=1, source_target_pairs={{0,12},{4,8},{8,4},{12,0},{16,28},{20,24},{24,20},{28,16},{1,13},{... | collective-permute-start | bytes 393224 | tf_op jit(solution)/shard_map/ppermute | solution.py:170
  13.7 13.2 %collective-permute-start.2 = (bf16[64,1024]{1,0:T(8,128)(2,1)S(1)}, bf16[64,1024]{1,0:T(8,128)(2,1)S(1)}, u32[]{:S(2)}, u32[]{:S(2)}) collective-permute-start(bf16[64,1024]{1,0:T(8,128)(2,1)S(1)} %dynamic-slice_bitcast_fusion.4), channel_id=1, source_target_pairs={{0,12},{4,8},{8,4},{12,0},{16,28},{20,24},{24,20},{28,16},{1,13},{... | collective-permute-start | bytes 393224 | tf_op jit(solution)/shard_map/ppermute | solution.py:170
  16.7 7.9 %copy-start.2 = (bf16[256,256]{1,0:T(8,128)(2,1)S(1)}, bf16[256,256]{1,0:T(8,128)(2,1)}, u32[]{:S(2)}) copy-start(bf16[256,256]{1,0:T(8,128)(2,1)} %constant.37.clone.refs_6_.matrix_ref) | copy-start | bytes 393220
  16.7 7.9 %copy-start.5 = (s32[1,1024]{1,0:T(1,128)S(1)}, s32[1,1024]{1,0:T(1,128)}, u32[]{:S(2)}) copy-start(s32[1,1024]{1,0:T(1,128)} %sign_ref.1) | copy-start | bytes 12292
  25.1 7.0 %collective-permute-start.4 = (s16[64,1024]{1,0:T(8,128)(2,1)S(1)}, s16[64,1024]{1,0:T(8,128)(2,1)S(1)}, u32[]{:S(2)}, u32[]{:S(2)}) collective-permute-start(s16[64,1024]{1,0:T(8,128)(2,1)S(1)} %proxy_blocks.1), channel_id=1, source_target_pairs={{0,16},{4,20},{8,24},{12,28},{16,0},{20,4},{24,8},{28,12},{1,17},{... | collective-permute-start | bytes 393224 | tf_op jit(solution)/shard_map/ppermute | solution.py:170
  33.1 12.4 %all-to-all-start.1 = ((f32[32,1,128]{2,1,0:T(1,128)}), f32[32,1,128]{2,1,0:T(1,128)S(1)}, u32[]{:S(2)}, u32[]{:S(2)}) async-start(f32[32,1,128]{2,1,0:T(1,128)} %get-tuple-element.9), calls=%async_computation.1 | async-start | bytes 32768 | tf_op jit(solution)/shard_map/all_to_all | solution.py:291
  38.4 7.1 %copy-start.3 = (bf16[1,64,1024]{2,1,0:T(8,128)(2,1)S(1)}, bf16[1,64,1024]{2,1,0:T(8,128)(2,1)}, u32[]{:S(2)}) copy-start(bf16[1,64,1024]{2,1,0:T(8,128)(2,1)} %param.7) | copy-start | bytes 393220
  38.4 7.1 %copy-start.4 = (bf16[1,64,1024]{2,1,0:T(8,128)(2,1)S(1)}, bf16[1,64,1024]{2,1,0:T(8,128)(2,1)}, u32[]{:S(2)}) copy-start(bf16[1,64,1024]{2,1,0:T(8,128)(2,1)} %param.8) | copy-start | bytes 393220
  45.6 9.0 %collective-permute-start.5 = (bf16[64,1024]{1,0:T(8,128)(2,1)S(1)}, bf16[64,1024]{1,0:T(8,128)(2,1)S(1)}, u32[]{:S(2)}, u32[]{:S(2)}) collective-permute-start(bf16[64,1024]{1,0:T(8,128)(2,1)S(1)} %new_weights.1.refs_0_), channel_id=1, source_target_pairs={{0,16},{4,20},{8,24},{12,28},{16,0},{20,4},{24,8},{28,12},{1,17},{... | collective-permute-start | bytes 393224 | tf_op jit(solution)/shard_map/ppermute | solution.py:170
  46.3 10.5 %collective-permute-start.11 = (bf16[64,1024]{1,0:T(8,128)(2,1)S(1)}, bf16[64,1024]{1,0:T(8,128)(2,1)S(1)}, u32[]{:S(2)}, u32[]{:S(2)}) collective-permute-start(bf16[64,1024]{1,0:T(8,128)(2,1)S(1)} %new_weights.1.refs_0_), channel_id=1, source_target_pairs={{0,4},{4,0},{8,12},{12,8},{16,20},{20,16},{24,28},{28,24},{1,5},{5... | collective-permute-start | bytes 393224 | tf_op jit(solution)/shard_map/ppermute | solution.py:170
  46.8 12.1 %collective-permute-start.10 = (bf16[64,1024]{1,0:T(8,128)(2,1)S(1)}, bf16[64,1024]{1,0:T(8,128)(2,1)S(1)}, u32[]{:S(2)}, u32[]{:S(2)}) collective-permute-start(bf16[64,1024]{1,0:T(8,128)(2,1)S(1)} %new_weights.1.refs_0_), channel_id=1, source_target_pairs={{0,8},{4,12},{8,0},{12,4},{16,24},{20,28},{24,16},{28,20},{1,9},{5... | collective-permute-start | bytes 393224 | tf_op jit(solution)/shard_map/ppermute | solution.py:170
  47.4 11.6 %collective-permute-start.9 = (bf16[64,1024]{1,0:T(8,128)(2,1)S(1)}, bf16[64,1024]{1,0:T(8,128)(2,1)S(1)}, u32[]{:S(2)}, u32[]{:S(2)}) collective-permute-start(bf16[64,1024]{1,0:T(8,128)(2,1)S(1)} %new_weights.1.refs_0_), channel_id=1, source_target_pairs={{0,12},{4,8},{8,4},{12,0},{16,28},{20,24},{24,20},{28,16},{1,13},{... | collective-permute-start | bytes 393224 | tf_op jit(solution)/shard_map/ppermute | solution.py:170
  54.7 7.3 %collective-permute-start.8 = (bf16[64,1024]{1,0:T(8,128)(2,1)S(1)}, bf16[64,1024]{1,0:T(8,128)(2,1)S(1)}, u32[]{:S(2)}, u32[]{:S(2)}) collective-permute-start(bf16[64,1024]{1,0:T(8,128)(2,1)S(1)} %collective-permute-done.5.refs_4_), channel_id=1, source_target_pairs={{0,12},{4,8},{8,4},{12,0},{16,28},{20,24},{24,20},{28,16},{1,13},{... | collective-permute-start | bytes 393224 | tf_op jit(solution)/shard_map/ppermute | solution.py:170
  54.7 8.2 %collective-permute-start.7 = (bf16[64,1024]{1,0:T(8,128)(2,1)S(1)}, bf16[64,1024]{1,0:T(8,128)(2,1)S(1)}, u32[]{:S(2)}, u32[]{:S(2)}) collective-permute-start(bf16[64,1024]{1,0:T(8,128)(2,1)S(1)} %collective-permute-done.5.refs_4_), channel_id=1, source_target_pairs={{0,8},{4,12},{8,0},{12,4},{16,24},{20,28},{24,16},{28,20},{1,9},{5... | collective-permute-start | bytes 393224 | tf_op jit(solution)/shard_map/ppermute | solution.py:170
  56.8 7.0 %collective-permute-start.6 = (bf16[64,1024]{1,0:T(8,128)(2,1)S(1)}, bf16[64,1024]{1,0:T(8,128)(2,1)S(1)}, u32[]{:S(2)}, u32[]{:S(2)}) collective-permute-start(bf16[64,1024]{1,0:T(8,128)(2,1)S(1)} %collective-permute-done.5.refs_4_), channel_id=1, source_target_pairs={{0,4},{4,0},{8,12},{12,8},{16,20},{20,16},{24,28},{28,24},{1,5},{5... | collective-permute-start | bytes 393224 | tf_op jit(solution)/shard_map/ppermute | solution.py:170

commit v16 on v15

--- a/solution.py
+++ b/solution.py
@@ -75,15 +75,14 @@
     return scale, step
 
 
-def add_levels(pieces, half, scale, sign_ref, matrix_ref, base):
-    width = pieces[0].shape[-1]
+def add_levels(pieces, scale, sign_ref, matrix_ref, base):
+    width = pieces[0].shape[1]
     signs = sign_ref[...].astype(jnp.float32).astype(jnp.bfloat16)
     matrix = matrix_ref[...]
     inverse = (1.0 / math.sqrt(width)) / scale
     totals = None
     for piece in pieces:
-        rows = piece[...] if len(piece.shape) == 2 else piece[half]
-        groups = rotate_groups([rows * signs], matrix, base)
+        groups = rotate_groups([piece[...] * signs], matrix, base)
         levels = [
             jnp.clip(group * inverse, -clamp_level, clamp_level)
             .astype(jnp.bfloat16)
@@ -99,7 +98,7 @@
     owned, width = sent_ref.shape
     half = 1 - lax.axis_index("dp") // near
     scale, step = scale_rows(sums_ref, half * owned, owned, width, near)
-    totals = add_levels(pieces, half, scale, sign_ref, matrix_ref, base)
+    totals = add_levels(pieces, scale, sign_ref, matrix_ref, base)
     for g, total in enumerate(totals):
         value = jnp.clip(jnp.round(total / step), -32767.0, 32767.0)
         sent_ref[:, g * base : (g + 1) * base] = value.astype(jnp.int16)
@@ -110,7 +109,7 @@
     owned, width = total_ref.shape
     half = lax.axis_index("dp") // near
     scale, _ = scale_rows(sums_ref, half * owned, owned, width, near)
-    totals = add_levels(pieces, half, scale, sign_ref, matrix_ref, base)
+    totals = add_levels(pieces, scale, sign_ref, matrix_ref, base)
     for g, total in enumerate(totals):
         total_ref[:, g * base : (g + 1) * base] = total
 
@@ -159,10 +158,6 @@
 
 def update_kernel(limit, square_ref, unrot_ref, update_ref):
     update_ref[...] = unrot_ref[...] * clip_factor(limit, square_ref)
-
-
-def chips_along_x(replicas):
-    return 1 << ((replicas.bit_length() - 1) // 2)
 
 
 def swap(value, mask):
@@ -229,19 +224,11 @@
     params = pltpu.CompilerParams(vmem_limit_bytes=vmem_bytes)
     array = pl.BlockSpec(memory_space=pltpu.VMEM)
 
-    def pair_of(source, index):
-        source = source.reshape(2, near, owned, width)
-        return lax.dynamic_slice_in_dim(source, index % near, 1, 1).reshape(2, owned, width)
-
     def block_of(source, index):
         source = source.reshape(replicas, owned, width)
         return lax.dynamic_slice_in_dim(source, index, 1, 0).reshape(owned, width)
 
-    x_count = chips_along_x(replicas)
-    aligned = [m for m in range(1, near) if m % x_count == 0 or m < x_count]
-    diagonal = [m for m in range(1, near) if m not in aligned]
-    pairs = [swap(pair_of(grads, me ^ mask), mask) for mask in aligned]
-    far_pieces = [swap(block_of(grads, me ^ mask ^ near), mask) for mask in diagonal]
+    far_pieces = [swap(block_of(grads, me ^ mask ^ near), mask) for mask in range(1, near)]
     sums = pl.pallas_call(
         sums_kernel,
         in_specs=[array],
@@ -253,9 +240,9 @@
     sums = lax.all_to_all(
         sums.reshape(replicas, 1, 2 * owned), "dp", split_axis=0, concat_axis=0, tiled=True
     ).reshape(replicas, 2 * owned)
-    pairs.append(pair_of(later, me))
-    far_pieces = pairs + far_pieces
-    near_pieces = pairs + [swap(block_of(later, me ^ mask), mask) for mask in diagonal]
+    near_pieces = [swap(block_of(later, me ^ mask), mask) for mask in range(1, near)]
+    far_pieces.append(block_of(later, me ^ near))
+    near_pieces.append(block_of(later, me))
     sent = pl.pallas_call(
         functools.partial(proxy_kernel, near, base),
         in_specs=[array] * (near + 3),

time: 64.7 us -> 59.6 us (0.921)
  waiting for transfers between devices: 27.9 us -> 24.4 us
  starting transfers between devices: 28.7 us -> 25.9 us
  local copies, waits for them, and re-layouts: 1.32 us -> 2.38 us
    ppermute x12 -> x14, waiting for transfers between devices: 21.2 us -> 14.9 us  [swap(): return lax.ppermute(value, 'dp', [(i, i ^ mask) for i in range(size)])]
    all_to_all x1, waiting for transfers between devices: 0.01 us -> 2.82 us  [on_device(): lax.all_to_all(sums.reshape(replicas, 1, 2 * owned), 'dp', split_axis=0,...]
    all_to_all x1, starting transfers between devices: 5.32 us -> 3.25 us  [on_device(): lax.all_to_all(squares, ('dp', 'expert'), split_axis=0, concat_axis=0, ti...]
    reshape x2, local copies, waits for them, and re-layouts: 0.02 us -> 1.13 us  [block_of(): return lax.dynamic_slice_in_dim(source, index, 1, 0).reshape(owned, width)]
    all_to_all x1, starting transfers between devices: 7.25 us -> 6.15 us  [on_device(): lax.all_to_all(sums.reshape(replicas, 1, 2 * owned), 'dp', split_axis=0,...]
    ppermute x12 -> x14, starting transfers between devices: 16.1 us -> 16.5 us  [swap(): return lax.ppermute(value, 'dp', [(i, i ^ mask) for i in range(size)])]
  transfers between devices with their start and end apart: 14 -> 16, of which waited for: 8 -> 8; matrix products, arithmetic and copies ran while one was open for 0% -> 0% of each run, Pallas kernels for 5% -> 7%
where the time goes in v16:
time: 59.6 us; the launch traced here: 59.3 us
  starting transfers between devices  25.9 us (43%)
  waiting for transfers between devices  24.4 us (41%)
  Pallas kernels  5.88 us (10%)
  local copies, waits for them, and re-layouts  2.38 us (4%)
  between operations  0.78 us (1%)
    ppermute x14, starting transfers between devices, swap(): return lax.ppermute(value, 'dp', [(i, i ^ mask) for i in range(size)])  16.5 us
    ppermute x14, waiting for transfers between devices, swap(): return lax.ppermute(value, 'dp', [(i, i ^ mask) for i in range(size)])  14.9 us
    all_to_all x1, waiting for transfers between devices, on_device(): lax.all_to_all(squares, ('dp', 'expert'), split_axis=0, concat_axis=0, ti...  6.72 us
    all_to_all x1, starting transfers between devices, on_device(): lax.all_to_all(sums.reshape(replicas, 1, 2 * owned), 'dp', split_axis=0,...  6.15 us
    all_to_all x1, starting transfers between devices, on_device(): lax.all_to_all(squares, ('dp', 'expert'), split_axis=0, concat_axis=0, ti...  3.25 us
    all_to_all x1, waiting for transfers between devices, on_device(): lax.all_to_all(sums.reshape(replicas, 1, 2 * owned), 'dp', split_axis=0,...  2.82 us
    pallas_call x2, Pallas kernels, place_pieces(): pl.pallas_call(functools.partial(place_kernel, places, owned), in_specs=s...  1.64 us
    unnamed x12, local copies, waits for them, and re-layouts  1.25 us
  transfers between devices with their start and end apart: 16, of which 8 were waited for; matrix products, arithmetic and copies ran while one was open for 0% of the time, Pallas kernels for 7%

profile of v16, /device:TPU:0, one launch (start us, length us, event | category | flops | bytes accessed | tf_op | source)
XLA Modules:
  0.0 59.3 jit_solution(6089376147060652567)
XLA Ops:
  0.7 1.1 %dynamic-slice_bitcast_fusion.1 = (bf16[64,1024]{1,0:T(8,128)(2,1)S(1)}, bf16[64,1024]{1,0:T(8,128)(2,1)S(1)}, bf16[64,1024]{1,0:T(8,128)(2,1)S(1)}) fusion(bf16[8,64,1024]{2,1,0:T(8,128)(2,1)} %bitcast.28, s32[]{:T(128)S(6)} %select_n.30, s32[]{:T(128)S(6)} %select_n.29, s32[]{:T(128)S(6)} %select_n.28), kind=kLoop, calls=%fused_computation.1 | loop fusion | bytes 786444 | tf_op jit(solution)/shard_map/reshape | solution.py:229
  1.7 4.0 %collective-permute-start.5 = (bf16[64,1024]{1,0:T(8,128)(2,1)S(1)}, bf16[64,1024]{1,0:T(8,128)(2,1)S(1)}, u32[]{:S(2)}, u32[]{:S(2)}) collective-permute-start(bf16[64,1024]{1,0:T(8,128)(2,1)S(1)} %get-tuple-element.17), channel_id=1, source_target_pairs={{0,12},{4,8},{8,4},{12,0},{16,28},{20,24},{24,20},{28,16},{1,13},{... | collective-permute-start | bytes 393224 | tf_op jit(solution)/shard_map/ppermute | solution.py:165
  6.4 1.2 %copy-done = bf16[1,1,512,1024]{3,2,1,0:T(8,128)(2,1)S(1)} copy-done((bf16[1,1,512,1024]{3,2,1,0:T(8,128)(2,1)S(1)}, bf16[1,1,512,1024]{3,2,1,0:T(8,128)(2,1)}, u32[]{:S(2)}) %copy-start) | copy-done | bytes 1048600
  7.6 0.9 %sum_squares.1 = f32[2,4,1,128]{3,2,1,0:T(1,128)} custom-call(bf16[2,4,64,1024]{3,2,1,0:T(8,128)(2,1)S(1)} %bitcast.29), custom_call_target="tpu_custom_call" | custom-call | tf_op jit(solution)/shard_map/sum_squares/pallas_call | solution.py:232
  8.5 6.1 %all-to-all-start = ((f32[8,1,128]{2,1,0:T(1,128)}), f32[8,1,128]{2,1,0:T(1,128)S(1)}, u32[]{:S(2)}, u32[]{:S(2)}) async-start(f32[8,1,128]{2,1,0:T(1,128)} %bitcast.7), calls=%async_computation | async-start | bytes 8192 | tf_op jit(solution)/shard_map/all_to_all | solution.py:240
  14.7 3.0 %collective-permute-start.2 = (bf16[64,1024]{1,0:T(8,128)(2,1)S(1)}, bf16[64,1024]{1,0:T(8,128)(2,1)S(1)}, u32[]{:S(2)}, u32[]{:S(2)}) collective-permute-start(bf16[64,1024]{1,0:T(8,128)(2,1)S(1)} %get-tuple-element.14), channel_id=1, source_target_pairs={{0,12},{4,8},{8,4},{12,0},{16,28},{20,24},{24,20},{28,16},{1,13},{... | collective-permute-start | bytes 393224 | tf_op jit(solution)/shard_map/ppermute | solution.py:165
  18.3 2.8 %all-to-all-done = f32[8,1,128]{2,1,0:T(1,128)S(1)} async-done(((f32[8,1,128]{2,1,0:T(1,128)}), f32[8,1,128]{2,1,0:T(1,128)S(1)}, u32[]{:S(2)}, u32[]{:S(2)}) %all-to-all-start) | async-done | bytes 4128 | tf_op jit(solution)/shard_map/all_to_all | solution.py:240
  21.2 0.6 %proxy_blocks.1 = s16[64,1024]{1,0:T(8,128)(2,1)S(1)} custom-call(bf16[64,1024]{1,0:T(8,128)(2,1)S(1)} %collective-permute-done.3.refs_0_, bf16[64,1024]{1,0:T(8,128)(2,1)S(1)} %collective-permute-done.4.refs_1_, bf16[64,1024]{1,0:T(8,128)(2,1)S(1)} %collective-permute-done.5.refs_2_, bf16[64,1024]{1,0:T(8,128)(2,1)S(1)} %get-tuple-element.12.refs_3_, ...), custom_call_target="tpu_custom_call" | custom-call | tf_op jit(solution)/shard_map/proxy_blocks/pallas_call | solution.py:246
  22.4 0.9 %collective-permute-done.1.refs_1_ = bf16[64,1024]{1,0:T(8,128)(2,1)S(1)} collective-permute-done((bf16[64,1024]{1,0:T(8,128)(2,1)S(1)}, bf16[64,1024]{1,0:T(8,128)(2,1)S(1)}, u32[]{:S(2)}, u32[]{:S(2)}) %collective-permute-start.1) | collective-permute-done | bytes 131104 | tf_op jit(solution)/shard_map/ppermute | solution.py:165
  23.8 5.2 %collective-permute-done.6.far_ref = s16[64,1024]{1,0:T(8,128)(2,1)S(1)} collective-permute-done((s16[64,1024]{1,0:T(8,128)(2,1)S(1)}, s16[64,1024]{1,0:T(8,128)(2,1)S(1)}, u32[]{:S(2)}, u32[]{:S(2)}) %collective-permute-start.6) | collective-permute-done | bytes 131104 | tf_op jit(solution)/shard_map/ppermute | solution.py:165
  29.0 0.9 %finish_blocks.1 = (f32[64,1024]{1,0:T(8,128)S(1)}, f32[64,128]{1,0:T(8,128)S(1)}, f32[32,1,128]{2,1,0:T(1,128)}) custom-call(f32[64,1024]{1,0:T(8,128)S(1)} %owner_blocks.1.near_ref, s16[64,1024]{1,0:T(8,128)(2,1)S(1)} %collective-permute-done.6.far_ref, f32[8,128]{1,0:T(8,128)S(1)} %bitcast.37), custom_call_target="tpu_custom_call" | custom-call | tf_op jit(solution)/shard_map/finish_blocks/pallas_call | solution.py:261
  30.0 3.3 %all-to-all-start.1 = ((f32[32,1,128]{2,1,0:T(1,128)}), f32[32,1,128]{2,1,0:T(1,128)S(1)}, u32[]{:S(2)}, u32[]{:S(2)}) async-start(f32[32,1,128]{2,1,0:T(1,128)} %get-tuple-element.9), calls=%async_computation.1 | async-start | bytes 32768 | tf_op jit(solution)/shard_map/all_to_all | solution.py:278
  33.6 6.7 %all-to-all-done.1 = f32[32,1,128]{2,1,0:T(1,128)S(1)} async-done(((f32[32,1,128]{2,1,0:T(1,128)}), f32[32,1,128]{2,1,0:T(1,128)S(1)}, u32[]{:S(2)}, u32[]{:S(2)}) %all-to-all-start.1) | async-done | bytes 16416 | tf_op jit(solution)/shard_map/all_to_all | solution.py:278
  40.5 0.7 %collective-permute-start.7 = (bf16[64,1024]{1,0:T(8,128)(2,1)S(1)}, bf16[64,1024]{1,0:T(8,128)(2,1)S(1)}, u32[]{:S(2)}, u32[]{:S(2)}) collective-permute-start(bf16[64,1024]{1,0:T(8,128)(2,1)S(1)} %new_weights.1.refs_0_), channel_id=1, source_target_pairs={{0,16},{4,20},{8,24},{12,28},{16,0},{20,4},{24,8},{28,12},{1,17},{... | collective-permute-start | bytes 393224 | tf_op jit(solution)/shard_map/ppermute | solution.py:165
  42.2 2.4 %collective-permute-start.11 = (bf16[64,1024]{1,0:T(8,128)(2,1)S(1)}, bf16[64,1024]{1,0:T(8,128)(2,1)S(1)}, u32[]{:S(2)}, u32[]{:S(2)}) collective-permute-start(bf16[64,1024]{1,0:T(8,128)(2,1)S(1)} %new_weights.1.refs_0_), channel_id=1, source_target_pairs={{0,12},{4,8},{8,4},{12,0},{16,28},{20,24},{24,20},{28,16},{1,13},{... | collective-permute-start | bytes 393224 | tf_op jit(solution)/shard_map/ppermute | solution.py:165
  44.6 4.9 %collective-permute-done.7.refs_4_ = bf16[64,1024]{1,0:T(8,128)(2,1)S(1)} collective-permute-done((bf16[64,1024]{1,0:T(8,128)(2,1)S(1)}, bf16[64,1024]{1,0:T(8,128)(2,1)S(1)}, u32[]{:S(2)}, u32[]{:S(2)}) %collective-permute-start.7) | collective-permute-done | bytes 131104 | tf_op jit(solution)/shard_map/ppermute | solution.py:165
  49.5 2.1 %collective-permute-start.9 = (bf16[64,1024]{1,0:T(8,128)(2,1)S(1)}, bf16[64,1024]{1,0:T(8,128)(2,1)S(1)}, u32[]{:S(2)}, u32[]{:S(2)}) collective-permute-start(bf16[64,1024]{1,0:T(8,128)(2,1)S(1)} %collective-permute-done.7.refs_4_), channel_id=1, source_target_pairs={{0,8},{4,12},{8,0},{12,4},{16,24},{20,28},{24,16},{28,20},{1,9},{5... | collective-permute-start | bytes 393224 | tf_op jit(solution)/shard_map/ppermute | solution.py:165
  51.6 1.4 %collective-permute-start.8 = (bf16[64,1024]{1,0:T(8,128)(2,1)S(1)}, bf16[64,1024]{1,0:T(8,128)(2,1)S(1)}, u32[]{:S(2)}, u32[]{:S(2)}) collective-permute-start(bf16[64,1024]{1,0:T(8,128)(2,1)S(1)} %collective-permute-done.7.refs_4_), channel_id=1, source_target_pairs={{0,4},{4,0},{8,12},{12,8},{16,20},{20,16},{24,28},{28,24},{1,5},{5... | collective-permute-start | bytes 393224 | tf_op jit(solution)/shard_map/ppermute | solution.py:165
  53.0 0.8 %update_grad.1 = f32[64,1024]{1,0:T(8,128)} custom-call(f32[32,128]{1,0:T(8,128)S(1)} %bitcast.32, f32[64,1024]{1,0:T(8,128)S(1)} %rotate_back.1.unrot_ref), custom_call_target="tpu_custom_call" | custom-call | tf_op jit(solution)/shard_map/update_grad/pallas_call | solution.py:287
  53.8 0.9 %place_own.1.refs_3_ = bf16[512,1024]{1,0:T(8,128)(2,1)} custom-call(bf16[64,1024]{1,0:T(8,128)(2,1)S(1)} %new_weights.1.refs_0_, bf16[64,1024]{1,0:T(8,128)(2,1)S(1)} %collective-permute-done.11.refs_1_, bf16[64,1024]{1,0:T(8,128)(2,1)S(1)} %collective-permute-done.12.refs_2_, bf16[64,1024]{1,0:T(8,128)(2,1)S(1)} %collective-permute-done.13.refs_3_, ...), custom_call_target="tpu_custom_call" | custom-call | tf_op jit(solution)/shard_map/place_own/pallas_call | solution.py:192
  54.7 2.1 %collective-permute-done.10.refs_2_ = bf16[64,1024]{1,0:T(8,128)(2,1)S(1)} collective-permute-done((bf16[64,1024]{1,0:T(8,128)(2,1)S(1)}, bf16[64,1024]{1,0:T(8,128)(2,1)S(1)}, u32[]{:S(2)}, u32[]{:S(2)}) %collective-permute-start.10) | collective-permute-done | bytes 131104 | tf_op jit(solution)/shard_map/ppermute | solution.py:165
  56.8 0.9 %collective-permute-done.9.refs_1_ = bf16[64,1024]{1,0:T(8,128)(2,1)S(1)} collective-permute-done((bf16[64,1024]{1,0:T(8,128)(2,1)S(1)}, bf16[64,1024]{1,0:T(8,128)(2,1)S(1)}, u32[]{:S(2)}, u32[]{:S(2)}) %collective-permute-start.9) | collective-permute-done | bytes 131104 | tf_op jit(solution)/shard_map/ppermute | solution.py:165
  57.7 0.9 %collective-permute-done.8.refs_0_ = bf16[64,1024]{1,0:T(8,128)(2,1)S(1)} collective-permute-done((bf16[64,1024]{1,0:T(8,128)(2,1)S(1)}, bf16[64,1024]{1,0:T(8,128)(2,1)S(1)}, u32[]{:S(2)}, u32[]{:S(2)}) %collective-permute-start.8) | collective-permute-done | bytes 131104 | tf_op jit(solution)/shard_map/ppermute | solution.py:165
  58.6 0.8 %place_far.1 = bf16[512,1024]{1,0:T(8,128)(2,1)} custom-call(bf16[64,1024]{1,0:T(8,128)(2,1)S(1)} %collective-permute-done.8.refs_0_, bf16[64,1024]{1,0:T(8,128)(2,1)S(1)} %collective-permute-done.9.refs_1_, bf16[64,1024]{1,0:T(8,128)(2,1)S(1)} %collective-permute-done.10.refs_2_, bf16[512,1024]{1,0:T(8,128)(2,1)} %place_own.1.refs_3_), custom_call_target="tpu_custom_call", output_to_operand_aliasing={{}: (3, {})} | custom-call | tf_op jit(solution)/shard_map/place_far/pallas_call | solution.py:192
  (31 shorter events, 4.1 us)
Async XLA Ops:
  1.7 16.5 %collective-permute-start.5 = (bf16[64,1024]{1,0:T(8,128)(2,1)S(1)}, bf16[64,1024]{1,0:T(8,128)(2,1)S(1)}, u32[]{:S(2)}, u32[]{:S(2)}) collective-permute-start(bf16[64,1024]{1,0:T(8,128)(2,1)S(1)} %get-tuple-element.17), channel_id=1, source_target_pairs={{0,12},{4,8},{8,4},{12,0},{16,28},{20,24},{24,20},{28,16},{1,13},{... | collective-permute-start | bytes 393224 | tf_op jit(solution)/shard_map/ppermute | solution.py:165
  5.7 15.4 %collective-permute-start.4 = (bf16[64,1024]{1,0:T(8,128)(2,1)S(1)}, bf16[64,1024]{1,0:T(8,128)(2,1)S(1)}, u32[]{:S(2)}, u32[]{:S(2)}) collective-permute-start(bf16[64,1024]{1,0:T(8,128)(2,1)S(1)} %get-tuple-element.18), channel_id=1, source_target_pairs={{0,8},{4,12},{8,0},{12,4},{16,24},{20,28},{24,16},{28,20},{1,9},{5... | collective-permute-start | bytes 393224 | tf_op jit(solution)/shard_map/ppermute | solution.py:165
  6.2 15.0 %collective-permute-start.3 = (bf16[64,1024]{1,0:T(8,128)(2,1)S(1)}, bf16[64,1024]{1,0:T(8,128)(2,1)S(1)}, u32[]{:S(2)}, u32[]{:S(2)}) collective-permute-start(bf16[64,1024]{1,0:T(8,128)(2,1)S(1)} %get-tuple-element.19), channel_id=1, source_target_pairs={{0,4},{4,0},{8,12},{12,8},{16,20},{20,16},{24,28},{28,24},{1,5},{5... | collective-permute-start | bytes 393224 | tf_op jit(solution)/shard_map/ppermute | solution.py:165
  6.4 1.2 %copy-start = (bf16[1,1,512,1024]{3,2,1,0:T(8,128)(2,1)S(1)}, bf16[1,1,512,1024]{3,2,1,0:T(8,128)(2,1)}, u32[]{:S(2)}) copy-start(bf16[1,1,512,1024]{3,2,1,0:T(8,128)(2,1)} %param.5) | copy-start | bytes 3145732
  7.6 7.0 %copy-start.1 = (bf16[1,1,512,1024]{3,2,1,0:T(8,128)(2,1)S(1)}, bf16[1,1,512,1024]{3,2,1,0:T(8,128)(2,1)}, u32[]{:S(2)}) copy-start(bf16[1,1,512,1024]{3,2,1,0:T(8,128)(2,1)} %param.5) | copy-start | bytes 3145732
  8.5 12.7 %all-to-all-start = ((f32[8,1,128]{2,1,0:T(1,128)}), f32[8,1,128]{2,1,0:T(1,128)S(1)}, u32[]{:S(2)}, u32[]{:S(2)}) async-start(f32[8,1,128]{2,1,0:T(1,128)} %bitcast.7), calls=%async_computation | async-start | bytes 8192 | tf_op jit(solution)/shard_map/all_to_all | solution.py:240
  14.6 6.5 %copy-start.2 = (bf16[256,256]{1,0:T(8,128)(2,1)S(1)}, bf16[256,256]{1,0:T(8,128)(2,1)}, u32[]{:S(2)}) copy-start(bf16[256,256]{1,0:T(8,128)(2,1)} %constant.20.clone.refs_6_.matrix_ref) | copy-start | bytes 393220
  14.7 6.5 %copy-start.5 = (s32[1,1024]{1,0:T(1,128)S(1)}, s32[1,1024]{1,0:T(1,128)}, u32[]{:S(2)}) copy-start(s32[1,1024]{1,0:T(1,128)} %sign_ref.1) | copy-start | bytes 12292
  14.7 7.6 %collective-permute-start.2 = (bf16[64,1024]{1,0:T(8,128)(2,1)S(1)}, bf16[64,1024]{1,0:T(8,128)(2,1)S(1)}, u32[]{:S(2)}, u32[]{:S(2)}) collective-permute-start(bf16[64,1024]{1,0:T(8,128)(2,1)S(1)} %get-tuple-element.14), channel_id=1, source_target_pairs={{0,12},{4,8},{8,4},{12,0},{16,28},{20,24},{24,20},{28,16},{1,13},{... | collective-permute-start | bytes 393224 | tf_op jit(solution)/shard_map/ppermute | solution.py:165
  17.7 5.6 %collective-permute-start.1 = (bf16[64,1024]{1,0:T(8,128)(2,1)S(1)}, bf16[64,1024]{1,0:T(8,128)(2,1)S(1)}, u32[]{:S(2)}, u32[]{:S(2)}) collective-permute-start(bf16[64,1024]{1,0:T(8,128)(2,1)S(1)} %get-tuple-element.15), channel_id=1, source_target_pairs={{0,8},{4,12},{8,0},{12,4},{16,24},{20,28},{24,16},{28,20},{1,9},{5... | collective-permute-start | bytes 393224 | tf_op jit(solution)/shard_map/ppermute | solution.py:165
  18.3 5.0 %collective-permute-start = (bf16[64,1024]{1,0:T(8,128)(2,1)S(1)}, bf16[64,1024]{1,0:T(8,128)(2,1)S(1)}, u32[]{:S(2)}, u32[]{:S(2)}) collective-permute-start(bf16[64,1024]{1,0:T(8,128)(2,1)S(1)} %get-tuple-element.16), channel_id=1, source_target_pairs={{0,4},{4,0},{8,12},{12,8},{16,20},{20,16},{24,28},{28,24},{1,5},{5... | collective-permute-start | bytes 393224 | tf_op jit(solution)/shard_map/ppermute | solution.py:165
  21.8 7.2 %collective-permute-start.6 = (s16[64,1024]{1,0:T(8,128)(2,1)S(1)}, s16[64,1024]{1,0:T(8,128)(2,1)S(1)}, u32[]{:S(2)}, u32[]{:S(2)}) collective-permute-start(s16[64,1024]{1,0:T(8,128)(2,1)S(1)} %proxy_blocks.1), channel_id=1, source_target_pairs={{0,16},{4,20},{8,24},{12,28},{16,0},{20,4},{24,8},{28,12},{1,17},{... | collective-permute-start | bytes 393224 | tf_op jit(solution)/shard_map/ppermute | solution.py:165
  30.0 10.3 %all-to-all-start.1 = ((f32[32,1,128]{2,1,0:T(1,128)}), f32[32,1,128]{2,1,0:T(1,128)S(1)}, u32[]{:S(2)}, u32[]{:S(2)}) async-start(f32[32,1,128]{2,1,0:T(1,128)} %get-tuple-element.9), calls=%async_computation.1 | async-start | bytes 32768 | tf_op jit(solution)/shard_map/all_to_all | solution.py:278
  33.2 7.1 %copy-start.3 = (bf16[1,64,1024]{2,1,0:T(8,128)(2,1)S(1)}, bf16[1,64,1024]{2,1,0:T(8,128)(2,1)}, u32[]{:S(2)}) copy-start(bf16[1,64,1024]{2,1,0:T(8,128)(2,1)} %param.7) | copy-start | bytes 393220
  33.2 7.1 %copy-start.4 = (bf16[1,64,1024]{2,1,0:T(8,128)(2,1)S(1)}, bf16[1,64,1024]{2,1,0:T(8,128)(2,1)}, u32[]{:S(2)}) copy-start(bf16[1,64,1024]{2,1,0:T(8,128)(2,1)} %param.8) | copy-start | bytes 393220
  40.5 9.0 %collective-permute-start.7 = (bf16[64,1024]{1,0:T(8,128)(2,1)S(1)}, bf16[64,1024]{1,0:T(8,128)(2,1)S(1)}, u32[]{:S(2)}, u32[]{:S(2)}) collective-permute-start(bf16[64,1024]{1,0:T(8,128)(2,1)S(1)} %new_weights.1.refs_0_), channel_id=1, source_target_pairs={{0,16},{4,20},{8,24},{12,28},{16,0},{20,4},{24,8},{28,12},{1,17},{... | collective-permute-start | bytes 393224 | tf_op jit(solution)/shard_map/ppermute | solution.py:165
  41.1 10.5 %collective-permute-start.13 = (bf16[64,1024]{1,0:T(8,128)(2,1)S(1)}, bf16[64,1024]{1,0:T(8,128)(2,1)S(1)}, u32[]{:S(2)}, u32[]{:S(2)}) collective-permute-start(bf16[64,1024]{1,0:T(8,128)(2,1)S(1)} %new_weights.1.refs_0_), channel_id=1, source_target_pairs={{0,4},{4,0},{8,12},{12,8},{16,20},{20,16},{24,28},{28,24},{1,5},{5... | collective-permute-start | bytes 393224 | tf_op jit(solution)/shard_map/ppermute | solution.py:165
  41.7 12.1 %collective-permute-start.12 = (bf16[64,1024]{1,0:T(8,128)(2,1)S(1)}, bf16[64,1024]{1,0:T(8,128)(2,1)S(1)}, u32[]{:S(2)}, u32[]{:S(2)}) collective-permute-start(bf16[64,1024]{1,0:T(8,128)(2,1)S(1)} %new_weights.1.refs_0_), channel_id=1, source_target_pairs={{0,8},{4,12},{8,0},{12,4},{16,24},{20,28},{24,16},{28,20},{1,9},{5... | collective-permute-start | bytes 393224 | tf_op jit(solution)/shard_map/ppermute | solution.py:165
  42.2 11.6 %collective-permute-start.11 = (bf16[64,1024]{1,0:T(8,128)(2,1)S(1)}, bf16[64,1024]{1,0:T(8,128)(2,1)S(1)}, u32[]{:S(2)}, u32[]{:S(2)}) collective-permute-start(bf16[64,1024]{1,0:T(8,128)(2,1)S(1)} %new_weights.1.refs_0_), channel_id=1, source_target_pairs={{0,12},{4,8},{8,4},{12,0},{16,28},{20,24},{24,20},{28,16},{1,13},{... | collective-permute-start | bytes 393224 | tf_op jit(solution)/shard_map/ppermute | solution.py:165
  49.5 7.3 %collective-permute-start.10 = (bf16[64,1024]{1,0:T(8,128)(2,1)S(1)}, bf16[64,1024]{1,0:T(8,128)(2,1)S(1)}, u32[]{:S(2)}, u32[]{:S(2)}) collective-permute-start(bf16[64,1024]{1,0:T(8,128)(2,1)S(1)} %collective-permute-done.7.refs_4_), channel_id=1, source_target_pairs={{0,12},{4,8},{8,4},{12,0},{16,28},{20,24},{24,20},{28,16},{1,13},{... | collective-permute-start | bytes 393224 | tf_op jit(solution)/shard_map/ppermute | solution.py:165
  49.5 8.2 %collective-permute-start.9 = (bf16[64,1024]{1,0:T(8,128)(2,1)S(1)}, bf16[64,1024]{1,0:T(8,128)(2,1)S(1)}, u32[]{:S(2)}, u32[]{:S(2)}) collective-permute-start(bf16[64,1024]{1,0:T(8,128)(2,1)S(1)} %collective-permute-done.7.refs_4_), channel_id=1, source_target_pairs={{0,8},{4,12},{8,0},{12,4},{16,24},{20,28},{24,16},{28,20},{1,9},{5... | collective-permute-start | bytes 393224 | tf_op jit(solution)/shard_map/ppermute | solution.py:165
  51.6 7.0 %collective-permute-start.8 = (bf16[64,1024]{1,0:T(8,128)(2,1)S(1)}, bf16[64,1024]{1,0:T(8,128)(2,1)S(1)}, u32[]{:S(2)}, u32[]{:S(2)}) collective-permute-start(bf16[64,1024]{1,0:T(8,128)(2,1)S(1)} %collective-permute-done.7.refs_4_), channel_id=1, source_target_pairs={{0,4},{4,0},{8,12},{12,8},{16,20},{20,16},{24,28},{28,24},{1,5},{5... | collective-permute-start | bytes 393224 | tf_op jit(solution)/shard_map/ppermute | solution.py:165

commit v17 on v15

--- a/solution.py
+++ b/solution.py
@@ -106,29 +106,30 @@
 
 
 def owner_kernel(near, base, *refs):
-    pieces, (sums_ref, sign_ref, matrix_ref, total_ref) = refs[:near], refs[near:]
+    pieces, rest = refs[:near], refs[near:]
+    sums_ref, sign_ref, matrix_ref, total_ref, scale_ref, step_ref = rest
     owned, width = total_ref.shape
     half = lax.axis_index("dp") // near
-    scale, _ = scale_rows(sums_ref, half * owned, owned, width, near)
+    scale, step = scale_rows(sums_ref, half * owned, owned, width, near)
     totals = add_levels(pieces, half, scale, sign_ref, matrix_ref, base)
     for g, total in enumerate(totals):
         total_ref[:, g * base : (g + 1) * base] = total
-
-
-def finish_kernel(
-    near, near_ref, far_ref, sums_ref, total_ref, scale_ref, square_ref
-):
-    owned, width = near_ref.shape
-    scale, step = scale_rows(
-        sums_ref, lax.axis_index("dp") // near * owned, owned, width, near
-    )
-    total = near_ref[...] + far_ref[...].astype(jnp.float32) * step
-    mean_scale = scale / (2 * near)
-    mean_rot = total * mean_scale
-    squares = jnp.sum(mean_rot * mean_rot)
+    scale_ref[...] = jnp.broadcast_to(scale / (2 * near), scale_ref.shape)
+    step_ref[...] = jnp.broadcast_to(step, step_ref.shape)
+
+
+def finish_kernel(near_ref, far_ref, scale_ref, step_ref, total_ref, square_ref):
+    width = near_ref.shape[1]
+    step = step_ref[...]
+    squares = None
+    for start in range(0, width, lanes):
+        cut = slice(start, start + lanes)
+        total = near_ref[:, cut] + far_ref[:, cut].astype(jnp.float32) * step
+        total_ref[:, cut] = total
+        squares = total * total if squares is None else squares + total * total
+    scale = scale_ref[...]
+    squares = jnp.sum(squares * (scale * scale))
     square_ref[...] = jnp.full(square_ref.shape, squares, jnp.float32)
-    total_ref[...] = total
-    scale_ref[...] = jnp.broadcast_to(mean_scale, scale_ref.shape)
 
 
 def back_kernel(base, total_ref, scale_ref, sign_ref, matrix_ref, unrot_ref):
@@ -241,7 +242,6 @@
     aligned = [m for m in range(1, near) if m % x_count == 0 or m < x_count]
     diagonal = [m for m in range(1, near) if m not in aligned]
     pairs = [swap(pair_of(grads, me ^ mask), mask) for mask in aligned]
-    far_pieces = [swap(block_of(grads, me ^ mask ^ near), mask) for mask in diagonal]
     sums = pl.pallas_call(
         sums_kernel,
         in_specs=[array],
@@ -253,9 +253,10 @@
     sums = lax.all_to_all(
         sums.reshape(replicas, 1, 2 * owned), "dp", split_axis=0, concat_axis=0, tiled=True
     ).reshape(replicas, 2 * owned)
+    far_pieces = [swap(block_of(later, me ^ mask ^ near), mask) for mask in diagonal]
+    near_pieces = [swap(block_of(later, me ^ mask), mask) for mask in diagonal]
     pairs.append(pair_of(later, me))
-    far_pieces = pairs + far_pieces
-    near_pieces = pairs + [swap(block_of(later, me ^ mask), mask) for mask in diagonal]
+    far_pieces, near_pieces = pairs + far_pieces, pairs + near_pieces
     sent = pl.pallas_call(
         functools.partial(proxy_kernel, near, base),
         in_specs=[array] * (near + 3),
@@ -264,24 +265,24 @@
         name="proxy_blocks",
     )(*far_pieces, sums, signs, matrix)
     far_total = swap(sent, near)
-    near_total = pl.pallas_call(
+    column = jax.ShapeDtypeStruct((owned, lanes), jnp.float32)
+    near_total, mean_scale, step = pl.pallas_call(
         functools.partial(owner_kernel, near, base),
         in_specs=[array] * (near + 3),
-        out_shape=jax.ShapeDtypeStruct((owned, width), jnp.float32),
+        out_shape=(jax.ShapeDtypeStruct((owned, width), jnp.float32), column, column),
         compiler_params=params,
         name="owner_blocks",
     )(*near_pieces, sums, signs, matrix)
-    total, mean_scale, squares = pl.pallas_call(
-        functools.partial(finish_kernel, near),
-        in_specs=[array] * 3,
+    total, squares = pl.pallas_call(
+        finish_kernel,
+        in_specs=[array] * 4,
         out_shape=(
             jax.ShapeDtypeStruct((owned, width), jnp.float32),
-            jax.ShapeDtypeStruct((owned, lanes), jnp.float32),
             jax.ShapeDtypeStruct((devices, 1, lanes), jnp.float32),
         ),
         compiler_params=params,
         name="finish_blocks",
-    )(near_total, far_total, sums)
+    )(near_total, far_total, mean_scale, step)
     unrot = pl.pallas_call(
         functools.partial(back_kernel, base),
         out_shape=jax.ShapeDtypeStruct((owned, width), jnp.float32),

time: 64.7 us -> 57.6 us (0.89)
  starting transfers between devices: 28.7 us -> 24.6 us
  waiting for transfers between devices: 27.9 us -> 25.1 us
    ppermute x12, waiting for transfers between devices: 21.2 us -> 14.9 us  [swap(): return lax.ppermute(value, 'dp', [(i, i ^ mask) for i in range(size)])]
    all_to_all x1, waiting for transfers between devices: 0.01 us -> 3.44 us  [on_device(): lax.all_to_all(sums.reshape(replicas, 1, 2 * owned), 'dp', split_axis=0,...]
    all_to_all x1, starting transfers between devices: 5.32 us -> 2.54 us  [on_device(): lax.all_to_all(squares, ('dp', 'expert'), split_axis=0, concat_axis=0, ti...]
    unnamed x12 -> x10, local copies, waits for them, and re-layouts: 1.24 us -> 0.02 us
    reshape x2, local copies, waits for them, and re-layouts: 0.06 us -> 1.17 us  [pair_of(): lax.dynamic_slice_in_dim(source, index % near, 1, 1)]
    all_to_all x1, starting transfers between devices: 7.25 us -> 6.18 us  [on_device(): lax.all_to_all(sums.reshape(replicas, 1, 2 * owned), 'dp', split_axis=0,...]
  transfers between devices with their start and end apart: 14 -> 14, of which waited for: 8 -> 7; matrix products, arithmetic and copies ran while one was open for 0% -> 0% of each run, Pallas kernels for 5% -> 7%
where the time goes in v17:
time: 57.6 us; the launch traced here: 57.4 us
  waiting for transfers between devices  25.1 us (44%)
  starting transfers between devices  24.6 us (43%)
  Pallas kernels  5.75 us (10%)
  local copies, waits for them, and re-layouts  1.21 us (2%)
  between operations  0.79 us (1%)
    ppermute x12, starting transfers between devices, swap(): return lax.ppermute(value, 'dp', [(i, i ^ mask) for i in range(size)])  15.9 us
    ppermute x12, waiting for transfers between devices, swap(): return lax.ppermute(value, 'dp', [(i, i ^ mask) for i in range(size)])  14.9 us
    all_to_all x1, waiting for transfers between devices, on_device(): lax.all_to_all(squares, ('dp', 'expert'), split_axis=0, concat_axis=0, ti...  6.72 us
    all_to_all x1, starting transfers between devices, on_device(): lax.all_to_all(sums.reshape(replicas, 1, 2 * owned), 'dp', split_axis=0,...  6.18 us
    all_to_all x1, waiting for transfers between devices, on_device(): lax.all_to_all(sums.reshape(replicas, 1, 2 * owned), 'dp', split_axis=0,...  3.44 us
    all_to_all x1, starting transfers between devices, on_device(): lax.all_to_all(squares, ('dp', 'expert'), split_axis=0, concat_axis=0, ti...  2.54 us
    pallas_call x2, Pallas kernels, place_pieces(): pl.pallas_call(functools.partial(place_kernel, places, owned), in_specs=s...  1.64 us
    reshape x2, local copies, waits for them, and re-layouts, pair_of(): lax.dynamic_slice_in_dim(source, index % near, 1, 1)  1.17 us
  transfers between devices with their start and end apart: 14, of which 7 were waited for; matrix products, arithmetic and copies ran while one was open for 0% of the time, Pallas kernels for 7%

profile of v17, /device:TPU:0, one launch (start us, length us, event | category | flops | bytes accessed | tf_op | source)
XLA Modules:
  0.0 57.4 jit_solution(3394756011972022048)
XLA Ops:
  0.7 1.2 %dynamic-slice_bitcast_fusion.1 = (bf16[2,64,1024]{2,1,0:T(8,128)(2,1)S(1)}, bf16[2,64,1024]{2,1,0:T(8,128)(2,1)S(1)}) fusion(bf16[2,4,64,1024]{3,2,1,0:T(8,128)(2,1)} %bitcast.24, s32[]{:T(128)S(6)} %select_n.33, s32[]{:T(128)S(6)} %select_n.31), kind=kLoop, calls=%fused_computation.1 | loop fusion | bytes 1048584 | tf_op jit(solution)/shard_map/reshape | solution.py:235
  1.8 3.1 %collective-permute-start.1 = (bf16[2,64,1024]{2,1,0:T(8,128)(2,1)S(1)}, bf16[2,64,1024]{2,1,0:T(8,128)(2,1)S(1)}, u32[]{:S(2)}, u32[]{:S(2)}) collective-permute-start(bf16[2,64,1024]{2,1,0:T(8,128)(2,1)S(1)} %get-tuple-element.18), channel_id=1, source_target_pairs={{0,8},{4,12},{8,0},{12,4},{16,24},{20,28},{24,16},{28,20},{1,9},{5... | collective-permute-start | bytes 786440 | tf_op jit(solution)/shard_map/ppermute | solution.py:171
  4.9 1.5 %collective-permute-start = (bf16[2,64,1024]{2,1,0:T(8,128)(2,1)S(1)}, bf16[2,64,1024]{2,1,0:T(8,128)(2,1)S(1)}, u32[]{:S(2)}, u32[]{:S(2)}) collective-permute-start(bf16[2,64,1024]{2,1,0:T(8,128)(2,1)S(1)} %get-tuple-element.19), channel_id=1, source_target_pairs={{0,4},{4,0},{8,12},{12,8},{16,20},{20,16},{24,28},{28,24},{1,5},{5... | collective-permute-start | bytes 786440 | tf_op jit(solution)/shard_map/ppermute | solution.py:171
  6.4 0.9 %sum_squares.1 = f32[2,4,1,128]{3,2,1,0:T(1,128)} custom-call(bf16[2,4,64,1024]{3,2,1,0:T(8,128)(2,1)S(1)} %bitcast.25), custom_call_target="tpu_custom_call" | custom-call | tf_op jit(solution)/shard_map/sum_squares/pallas_call | solution.py:245
  7.4 6.2 %all-to-all-start = ((f32[8,1,128]{2,1,0:T(1,128)}), f32[8,1,128]{2,1,0:T(1,128)S(1)}, u32[]{:S(2)}, u32[]{:S(2)}) async-start(f32[8,1,128]{2,1,0:T(1,128)} %bitcast.8), calls=%async_computation | async-start | bytes 8192 | tf_op jit(solution)/shard_map/all_to_all | solution.py:253
  13.6 2.9 %collective-permute-start.2 = (bf16[64,1024]{1,0:T(8,128)(2,1)S(1)}, bf16[64,1024]{1,0:T(8,128)(2,1)S(1)}, u32[]{:S(2)}, u32[]{:S(2)}) collective-permute-start(bf16[64,1024]{1,0:T(8,128)(2,1)S(1)} %get-tuple-element.17), channel_id=1, source_target_pairs={{0,12},{4,8},{8,4},{12,0},{16,28},{20,24},{24,20},{28,16},{1,13},{... | collective-permute-start | bytes 393224 | tf_op jit(solution)/shard_map/ppermute | solution.py:171
  16.6 3.4 %all-to-all-done = f32[8,1,128]{2,1,0:T(1,128)S(1)} async-done(((f32[8,1,128]{2,1,0:T(1,128)}), f32[8,1,128]{2,1,0:T(1,128)S(1)}, u32[]{:S(2)}, u32[]{:S(2)}) %all-to-all-start) | async-done | bytes 4128 | tf_op jit(solution)/shard_map/all_to_all | solution.py:253
  20.0 0.6 %proxy_blocks.1 = s16[64,1024]{1,0:T(8,128)(2,1)S(1)} custom-call(bf16[2,64,1024]{2,1,0:T(8,128)(2,1)S(1)} %collective-permute-done.refs_0_, bf16[2,64,1024]{2,1,0:T(8,128)(2,1)S(1)} %collective-permute-done.1.refs_1_, bf16[2,64,1024]{2,1,0:T(8,128)(2,1)S(1)} %dynamic-slice_bitcast_fusion.refs_2_, bf16[64,1024]{1,0:T(8,128)(2,1)S(1)} %collective-permute-done.3.refs_3_, ...), custom_call_target="tpu_custom_call" | custom-call | tf_op jit(solution)/shard_map/proxy_blocks/pallas_call | solution.py:260
  20.6 0.6 %collective-permute-start.4 = (s16[64,1024]{1,0:T(8,128)(2,1)S(1)}, s16[64,1024]{1,0:T(8,128)(2,1)S(1)}, u32[]{:S(2)}, u32[]{:S(2)}) collective-permute-start(s16[64,1024]{1,0:T(8,128)(2,1)S(1)} %proxy_blocks.1), channel_id=1, source_target_pairs={{0,16},{4,20},{8,24},{12,28},{16,0},{20,4},{24,8},{28,12},{1,17},{... | collective-permute-start | bytes 393224 | tf_op jit(solution)/shard_map/ppermute | solution.py:171
  21.8 6.1 %collective-permute-done.4.far_ref = s16[64,1024]{1,0:T(8,128)(2,1)S(1)} collective-permute-done((s16[64,1024]{1,0:T(8,128)(2,1)S(1)}, s16[64,1024]{1,0:T(8,128)(2,1)S(1)}, u32[]{:S(2)}, u32[]{:S(2)}) %collective-permute-start.4) | collective-permute-done | bytes 131104 | tf_op jit(solution)/shard_map/ppermute | solution.py:171
  28.0 0.8 %finish_blocks.1 = (f32[64,1024]{1,0:T(8,128)S(1)}, f32[32,1,128]{2,1,0:T(1,128)}) custom-call(f32[64,1024]{1,0:T(8,128)S(1)} %get-tuple-element.11.near_ref, s16[64,1024]{1,0:T(8,128)(2,1)S(1)} %collective-permute-done.4.far_ref, f32[64,128]{1,0:T(8,128)S(1)} %get-tuple-element.12.scale_ref, f32[64,128]{1,0:T(8,128)S(1)} %get-tuple-element.13.step_ref), custom_call_target="tpu_custom_call" | custom-call | tf_op jit(solution)/shard_map/finish_blocks/pallas_call | solution.py:276
  28.7 2.5 %all-to-all-start.1 = ((f32[32,1,128]{2,1,0:T(1,128)}), f32[32,1,128]{2,1,0:T(1,128)S(1)}, u32[]{:S(2)}, u32[]{:S(2)}) async-start(f32[32,1,128]{2,1,0:T(1,128)} %get-tuple-element.14), calls=%async_computation.1 | async-start | bytes 32768 | tf_op jit(solution)/shard_map/all_to_all | solution.py:292
  31.6 6.7 %all-to-all-done.1 = f32[32,1,128]{2,1,0:T(1,128)S(1)} async-done(((f32[32,1,128]{2,1,0:T(1,128)}), f32[32,1,128]{2,1,0:T(1,128)S(1)}, u32[]{:S(2)}, u32[]{:S(2)}) %all-to-all-start.1) | async-done | bytes 16416 | tf_op jit(solution)/shard_map/all_to_all | solution.py:292
  38.5 0.7 %collective-permute-start.5 = (bf16[64,1024]{1,0:T(8,128)(2,1)S(1)}, bf16[64,1024]{1,0:T(8,128)(2,1)S(1)}, u32[]{:S(2)}, u32[]{:S(2)}) collective-permute-start(bf16[64,1024]{1,0:T(8,128)(2,1)S(1)} %new_weights.1.refs_0_), channel_id=1, source_target_pairs={{0,16},{4,20},{8,24},{12,28},{16,0},{20,4},{24,8},{28,12},{1,17},{... | collective-permute-start | bytes 393224 | tf_op jit(solution)/shard_map/ppermute | solution.py:171
  40.2 2.5 %collective-permute-start.9 = (bf16[64,1024]{1,0:T(8,128)(2,1)S(1)}, bf16[64,1024]{1,0:T(8,128)(2,1)S(1)}, u32[]{:S(2)}, u32[]{:S(2)}) collective-permute-start(bf16[64,1024]{1,0:T(8,128)(2,1)S(1)} %new_weights.1.refs_0_), channel_id=1, source_target_pairs={{0,12},{4,8},{8,4},{12,0},{16,28},{20,24},{24,20},{28,16},{1,13},{... | collective-permute-start | bytes 393224 | tf_op jit(solution)/shard_map/ppermute | solution.py:171
  42.7 4.9 %collective-permute-done.5.refs_4_ = bf16[64,1024]{1,0:T(8,128)(2,1)S(1)} collective-permute-done((bf16[64,1024]{1,0:T(8,128)(2,1)S(1)}, bf16[64,1024]{1,0:T(8,128)(2,1)S(1)}, u32[]{:S(2)}, u32[]{:S(2)}) %collective-permute-start.5) | collective-permute-done | bytes 131104 | tf_op jit(solution)/shard_map/ppermute | solution.py:171
  47.6 2.1 %collective-permute-start.7 = (bf16[64,1024]{1,0:T(8,128)(2,1)S(1)}, bf16[64,1024]{1,0:T(8,128)(2,1)S(1)}, u32[]{:S(2)}, u32[]{:S(2)}) collective-permute-start(bf16[64,1024]{1,0:T(8,128)(2,1)S(1)} %collective-permute-done.5.refs_4_), channel_id=1, source_target_pairs={{0,8},{4,12},{8,0},{12,4},{16,24},{20,28},{24,16},{28,20},{1,9},{5... | collective-permute-start | bytes 393224 | tf_op jit(solution)/shard_map/ppermute | solution.py:171
  49.7 1.4 %collective-permute-start.6 = (bf16[64,1024]{1,0:T(8,128)(2,1)S(1)}, bf16[64,1024]{1,0:T(8,128)(2,1)S(1)}, u32[]{:S(2)}, u32[]{:S(2)}) collective-permute-start(bf16[64,1024]{1,0:T(8,128)(2,1)S(1)} %collective-permute-done.5.refs_4_), channel_id=1, source_target_pairs={{0,4},{4,0},{8,12},{12,8},{16,20},{20,16},{24,28},{28,24},{1,5},{5... | collective-permute-start | bytes 393224 | tf_op jit(solution)/shard_map/ppermute | solution.py:171
  51.1 0.8 %update_grad.1 = f32[64,1024]{1,0:T(8,128)} custom-call(f32[32,128]{1,0:T(8,128)S(1)} %bitcast.29, f32[64,1024]{1,0:T(8,128)S(1)} %rotate_back.1.unrot_ref), custom_call_target="tpu_custom_call" | custom-call | tf_op jit(solution)/shard_map/update_grad/pallas_call | solution.py:301
  51.9 0.9 %place_own.1.refs_3_ = bf16[512,1024]{1,0:T(8,128)(2,1)} custom-call(bf16[64,1024]{1,0:T(8,128)(2,1)S(1)} %new_weights.1.refs_0_, bf16[64,1024]{1,0:T(8,128)(2,1)S(1)} %collective-permute-done.9.refs_1_, bf16[64,1024]{1,0:T(8,128)(2,1)S(1)} %collective-permute-done.10.refs_2_, bf16[64,1024]{1,0:T(8,128)(2,1)S(1)} %collective-permute-done.11.refs_3_, ...), custom_call_target="tpu_custom_call" | custom-call | tf_op jit(solution)/shard_map/place_own/pallas_call | solution.py:198
  52.8 2.1 %collective-permute-done.8.refs_2_ = bf16[64,1024]{1,0:T(8,128)(2,1)S(1)} collective-permute-done((bf16[64,1024]{1,0:T(8,128)(2,1)S(1)}, bf16[64,1024]{1,0:T(8,128)(2,1)S(1)}, u32[]{:S(2)}, u32[]{:S(2)}) %collective-permute-start.8) | collective-permute-done | bytes 131104 | tf_op jit(solution)/shard_map/ppermute | solution.py:171
  54.8 0.9 %collective-permute-done.7.refs_1_ = bf16[64,1024]{1,0:T(8,128)(2,1)S(1)} collective-permute-done((bf16[64,1024]{1,0:T(8,128)(2,1)S(1)}, bf16[64,1024]{1,0:T(8,128)(2,1)S(1)}, u32[]{:S(2)}, u32[]{:S(2)}) %collective-permute-start.7) | collective-permute-done | bytes 131104 | tf_op jit(solution)/shard_map/ppermute | solution.py:171
  55.8 0.9 %collective-permute-done.6.refs_0_ = bf16[64,1024]{1,0:T(8,128)(2,1)S(1)} collective-permute-done((bf16[64,1024]{1,0:T(8,128)(2,1)S(1)}, bf16[64,1024]{1,0:T(8,128)(2,1)S(1)}, u32[]{:S(2)}, u32[]{:S(2)}) %collective-permute-start.6) | collective-permute-done | bytes 131104 | tf_op jit(solution)/shard_map/ppermute | solution.py:171
  56.6 0.8 %place_far.1 = bf16[512,1024]{1,0:T(8,128)(2,1)} custom-call(bf16[64,1024]{1,0:T(8,128)(2,1)S(1)} %collective-permute-done.6.refs_0_, bf16[64,1024]{1,0:T(8,128)(2,1)S(1)} %collective-permute-done.7.refs_1_, bf16[64,1024]{1,0:T(8,128)(2,1)S(1)} %collective-permute-done.8.refs_2_, bf16[512,1024]{1,0:T(8,128)(2,1)} %place_own.1.refs_3_), custom_call_target="tpu_custom_call", output_to_operand_aliasing={{}: (3, {})} | custom-call | tf_op jit(solution)/shard_map/place_far/pallas_call | solution.py:198
  (26 shorter events, 2.3 us)
Async XLA Ops:
  0.6 5.8 %copy-start = (bf16[1,1,512,1024]{3,2,1,0:T(8,128)(2,1)S(1)}, bf16[1,1,512,1024]{3,2,1,0:T(8,128)(2,1)}, u32[]{:S(2)}) copy-start(bf16[1,1,512,1024]{3,2,1,0:T(8,128)(2,1)} %param.5) | copy-start | bytes 3145732
  1.8 18.2 %collective-permute-start.1 = (bf16[2,64,1024]{2,1,0:T(8,128)(2,1)S(1)}, bf16[2,64,1024]{2,1,0:T(8,128)(2,1)S(1)}, u32[]{:S(2)}, u32[]{:S(2)}) collective-permute-start(bf16[2,64,1024]{2,1,0:T(8,128)(2,1)S(1)} %get-tuple-element.18), channel_id=1, source_target_pairs={{0,8},{4,12},{8,0},{12,4},{16,24},{20,28},{24,16},{28,20},{1,9},{5... | collective-permute-start | bytes 786440 | tf_op jit(solution)/shard_map/ppermute | solution.py:171
  4.9 15.1 %collective-permute-start = (bf16[2,64,1024]{2,1,0:T(8,128)(2,1)S(1)}, bf16[2,64,1024]{2,1,0:T(8,128)(2,1)S(1)}, u32[]{:S(2)}, u32[]{:S(2)}) collective-permute-start(bf16[2,64,1024]{2,1,0:T(8,128)(2,1)S(1)} %get-tuple-element.19), channel_id=1, source_target_pairs={{0,4},{4,0},{8,12},{12,8},{16,20},{20,16},{24,28},{28,24},{1,5},{5... | collective-permute-start | bytes 786440 | tf_op jit(solution)/shard_map/ppermute | solution.py:171
  7.3 12.7 %collective-permute-start.3 = (bf16[64,1024]{1,0:T(8,128)(2,1)S(1)}, bf16[64,1024]{1,0:T(8,128)(2,1)S(1)}, u32[]{:S(2)}, u32[]{:S(2)}) collective-permute-start(bf16[64,1024]{1,0:T(8,128)(2,1)S(1)} %get-tuple-element.16), channel_id=1, source_target_pairs={{0,12},{4,8},{8,4},{12,0},{16,28},{20,24},{24,20},{28,16},{1,13},{... | collective-permute-start | bytes 393224 | tf_op jit(solution)/shard_map/ppermute | solution.py:171
  7.4 12.6 %all-to-all-start = ((f32[8,1,128]{2,1,0:T(1,128)}), f32[8,1,128]{2,1,0:T(1,128)S(1)}, u32[]{:S(2)}, u32[]{:S(2)}) async-start(f32[8,1,128]{2,1,0:T(1,128)} %bitcast.8), calls=%async_computation | async-start | bytes 8192 | tf_op jit(solution)/shard_map/all_to_all | solution.py:253
  13.6 7.7 %collective-permute-start.2 = (bf16[64,1024]{1,0:T(8,128)(2,1)S(1)}, bf16[64,1024]{1,0:T(8,128)(2,1)S(1)}, u32[]{:S(2)}, u32[]{:S(2)}) collective-permute-start(bf16[64,1024]{1,0:T(8,128)(2,1)S(1)} %get-tuple-element.17), channel_id=1, source_target_pairs={{0,12},{4,8},{8,4},{12,0},{16,28},{20,24},{24,20},{28,16},{1,13},{... | collective-permute-start | bytes 393224 | tf_op jit(solution)/shard_map/ppermute | solution.py:171
  16.5 3.5 %copy-start.1 = (bf16[256,256]{1,0:T(8,128)(2,1)S(1)}, bf16[256,256]{1,0:T(8,128)(2,1)}, u32[]{:S(2)}) copy-start(bf16[256,256]{1,0:T(8,128)(2,1)} %constant.37.clone.refs_6_.matrix_ref) | copy-start | bytes 393220
  16.5 3.5 %copy-start.4 = (s32[1,1024]{1,0:T(1,128)S(1)}, s32[1,1024]{1,0:T(1,128)}, u32[]{:S(2)}) copy-start(s32[1,1024]{1,0:T(1,128)} %sign_ref.1) | copy-start | bytes 12292
  20.6 7.3 %collective-permute-start.4 = (s16[64,1024]{1,0:T(8,128)(2,1)S(1)}, s16[64,1024]{1,0:T(8,128)(2,1)S(1)}, u32[]{:S(2)}, u32[]{:S(2)}) collective-permute-start(s16[64,1024]{1,0:T(8,128)(2,1)S(1)} %proxy_blocks.1), channel_id=1, source_target_pairs={{0,16},{4,20},{8,24},{12,28},{16,0},{20,4},{24,8},{28,12},{1,17},{... | collective-permute-start | bytes 393224 | tf_op jit(solution)/shard_map/ppermute | solution.py:171
  28.7 9.6 %all-to-all-start.1 = ((f32[32,1,128]{2,1,0:T(1,128)}), f32[32,1,128]{2,1,0:T(1,128)S(1)}, u32[]{:S(2)}, u32[]{:S(2)}) async-start(f32[32,1,128]{2,1,0:T(1,128)} %get-tuple-element.14), calls=%async_computation.1 | async-start | bytes 32768 | tf_op jit(solution)/shard_map/all_to_all | solution.py:292
  31.3 7.1 %copy-start.2 = (bf16[1,64,1024]{2,1,0:T(8,128)(2,1)S(1)}, bf16[1,64,1024]{2,1,0:T(8,128)(2,1)}, u32[]{:S(2)}) copy-start(bf16[1,64,1024]{2,1,0:T(8,128)(2,1)} %param.7) | copy-start | bytes 393220
  31.3 7.1 %copy-start.3 = (bf16[1,64,1024]{2,1,0:T(8,128)(2,1)S(1)}, bf16[1,64,1024]{2,1,0:T(8,128)(2,1)}, u32[]{:S(2)}) copy-start(bf16[1,64,1024]{2,1,0:T(8,128)(2,1)} %param.8) | copy-start | bytes 393220
  38.5 9.0 %collective-permute-start.5 = (bf16[64,1024]{1,0:T(8,128)(2,1)S(1)}, bf16[64,1024]{1,0:T(8,128)(2,1)S(1)}, u32[]{:S(2)}, u32[]{:S(2)}) collective-permute-start(bf16[64,1024]{1,0:T(8,128)(2,1)S(1)} %new_weights.1.refs_0_), channel_id=1, source_target_pairs={{0,16},{4,20},{8,24},{12,28},{16,0},{20,4},{24,8},{28,12},{1,17},{... | collective-permute-start | bytes 393224 | tf_op jit(solution)/shard_map/ppermute | solution.py:171
  39.2 10.5 %collective-permute-start.11 = (bf16[64,1024]{1,0:T(8,128)(2,1)S(1)}, bf16[64,1024]{1,0:T(8,128)(2,1)S(1)}, u32[]{:S(2)}, u32[]{:S(2)}) collective-permute-start(bf16[64,1024]{1,0:T(8,128)(2,1)S(1)} %new_weights.1.refs_0_), channel_id=1, source_target_pairs={{0,4},{4,0},{8,12},{12,8},{16,20},{20,16},{24,28},{28,24},{1,5},{5... | collective-permute-start | bytes 393224 | tf_op jit(solution)/shard_map/ppermute | solution.py:171
  39.8 12.1 %collective-permute-start.10 = (bf16[64,1024]{1,0:T(8,128)(2,1)S(1)}, bf16[64,1024]{1,0:T(8,128)(2,1)S(1)}, u32[]{:S(2)}, u32[]{:S(2)}) collective-permute-start(bf16[64,1024]{1,0:T(8,128)(2,1)S(1)} %new_weights.1.refs_0_), channel_id=1, source_target_pairs={{0,8},{4,12},{8,0},{12,4},{16,24},{20,28},{24,16},{28,20},{1,9},{5... | collective-permute-start | bytes 393224 | tf_op jit(solution)/shard_map/ppermute | solution.py:171
  40.2 11.6 %collective-permute-start.9 = (bf16[64,1024]{1,0:T(8,128)(2,1)S(1)}, bf16[64,1024]{1,0:T(8,128)(2,1)S(1)}, u32[]{:S(2)}, u32[]{:S(2)}) collective-permute-start(bf16[64,1024]{1,0:T(8,128)(2,1)S(1)} %new_weights.1.refs_0_), channel_id=1, source_target_pairs={{0,12},{4,8},{8,4},{12,0},{16,28},{20,24},{24,20},{28,16},{1,13},{... | collective-permute-start | bytes 393224 | tf_op jit(solution)/shard_map/ppermute | solution.py:171
  47.6 7.3 %collective-permute-start.8 = (bf16[64,1024]{1,0:T(8,128)(2,1)S(1)}, bf16[64,1024]{1,0:T(8,128)(2,1)S(1)}, u32[]{:S(2)}, u32[]{:S(2)}) collective-permute-start(bf16[64,1024]{1,0:T(8,128)(2,1)S(1)} %collective-permute-done.5.refs_4_), channel_id=1, source_target_pairs={{0,12},{4,8},{8,4},{12,0},{16,28},{20,24},{24,20},{28,16},{1,13},{... | collective-permute-start | bytes 393224 | tf_op jit(solution)/shard_map/ppermute | solution.py:171
  47.6 8.2 %collective-permute-start.7 = (bf16[64,1024]{1,0:T(8,128)(2,1)S(1)}, bf16[64,1024]{1,0:T(8,128)(2,1)S(1)}, u32[]{:S(2)}, u32[]{:S(2)}) collective-permute-start(bf16[64,1024]{1,0:T(8,128)(2,1)S(1)} %collective-permute-done.5.refs_4_), channel_id=1, source_target_pairs={{0,8},{4,12},{8,0},{12,4},{16,24},{20,28},{24,16},{28,20},{1,9},{5... | collective-permute-start | bytes 393224 | tf_op jit(solution)/shard_map/ppermute | solution.py:171
  49.7 7.0 %collective-permute-start.6 = (bf16[64,1024]{1,0:T(8,128)(2,1)S(1)}, bf16[64,1024]{1,0:T(8,128)(2,1)S(1)}, u32[]{:S(2)}, u32[]{:S(2)}) collective-permute-start(bf16[64,1024]{1,0:T(8,128)(2,1)S(1)} %collective-permute-done.5.refs_4_), channel_id=1, source_target_pairs={{0,4},{4,0},{8,12},{12,8},{16,20},{20,16},{24,28},{28,24},{1,5},{5... | collective-permute-start | bytes 393224 | tf_op jit(solution)/shard_map/ppermute | solution.py:171

commit v18 on v17

--- a/solution.py
+++ b/solution.py
@@ -75,12 +75,9 @@
     return scale, step
 
 
-def add_levels(pieces, half, scale, sign_ref, matrix_ref, base):
-    width = pieces[0].shape[-1]
+def add_levels(pieces, half, inverse, sign_ref, matrix_ref, base, totals=None):
     signs = sign_ref[...].astype(jnp.float32).astype(jnp.bfloat16)
     matrix = matrix_ref[...]
-    inverse = (1.0 / math.sqrt(width)) / scale
-    totals = None
     for piece in pieces:
         rows = piece[...] if len(piece.shape) == 2 else piece[half]
         groups = rotate_groups([rows * signs], matrix, base)
@@ -94,15 +91,30 @@
     return totals
 
 
-def proxy_kernel(near, base, *refs):
-    pieces, (sums_ref, sign_ref, matrix_ref, sent_ref) = refs[:near], refs[near:]
-    owned, width = sent_ref.shape
+def proxy_pairs_kernel(near, count, base, *refs):
+    pieces, rest = refs[:count], refs[count:]
+    sums_ref, sign_ref, matrix_ref, total_ref, inverse_ref, step_ref = rest
+    owned, width = total_ref.shape
     half = 1 - lax.axis_index("dp") // near
     scale, step = scale_rows(sums_ref, half * owned, owned, width, near)
-    totals = add_levels(pieces, half, scale, sign_ref, matrix_ref, base)
+    inverse = (1.0 / math.sqrt(width)) / scale
+    totals = add_levels(pieces, half, inverse, sign_ref, matrix_ref, base)
     for g, total in enumerate(totals):
-        value = jnp.clip(jnp.round(total / step), -32767.0, 32767.0)
-        sent_ref[:, g * base : (g + 1) * base] = value.astype(jnp.int16)
+        total_ref[:, g * base : (g + 1) * base] = total
+    inverse_ref[...] = jnp.broadcast_to(inverse, inverse_ref.shape)
+    step_ref[...] = jnp.broadcast_to(1.0 / step, step_ref.shape)
+
+
+def proxy_kernel(count, base, *refs):
+    pieces, rest = refs[:count], refs[count:]
+    total_ref, inverse_ref, step_ref, sign_ref, matrix_ref, sent_ref = rest
+    cuts = [slice(start, start + base) for start in range(0, total_ref.shape[1], base)]
+    totals = [total_ref[:, cut] for cut in cuts]
+    totals = add_levels(pieces, 0, inverse_ref[:, 0:1], sign_ref, matrix_ref, base, totals)
+    steps = step_ref[:, 0:1]
+    for cut, total in zip(cuts, totals):
+        value = jnp.clip(jnp.round(total * steps), -32767.0, 32767.0)
+        sent_ref[:, cut] = value.astype(jnp.int16)
 
 
 def owner_kernel(near, base, *refs):
@@ -111,7 +123,8 @@
     owned, width = total_ref.shape
     half = lax.axis_index("dp") // near
     scale, step = scale_rows(sums_ref, half * owned, owned, width, near)
-    totals = add_levels(pieces, half, scale, sign_ref, matrix_ref, base)
+    inverse = (1.0 / math.sqrt(width)) / scale
+    totals = add_levels(pieces, half, inverse, sign_ref, matrix_ref, base)
     for g, total in enumerate(totals):
         total_ref[:, g * base : (g + 1) * base] = total
     scale_ref[...] = jnp.broadcast_to(scale / (2 * near), scale_ref.shape)
@@ -128,8 +141,8 @@
         total_ref[:, cut] = total
         squares = total * total if squares is None else squares + total * total
     scale = scale_ref[...]
-    squares = jnp.sum(squares * (scale * scale))
-    square_ref[...] = jnp.full(square_ref.shape, squares, jnp.float32)
+    squares = jnp.sum(squares * (scale * scale), axis=0, keepdims=True)
+    square_ref[...] = jnp.broadcast_to(squares[None], square_ref.shape)
 
 
 def back_kernel(base, total_ref, scale_ref, sign_ref, matrix_ref, unrot_ref):
@@ -146,7 +159,7 @@
 
 
 def clip_factor(limit, square_ref):
-    squares = jnp.sum(square_ref[...], axis=0, keepdims=True)[:, 0:1]
+    squares = jnp.sum(jnp.sum(square_ref[...], axis=0, keepdims=True), axis=1, keepdims=True)
     return limit / jnp.maximum(jnp.sqrt(squares), limit)
 
 
@@ -256,23 +269,30 @@
     far_pieces = [swap(block_of(later, me ^ mask ^ near), mask) for mask in diagonal]
     near_pieces = [swap(block_of(later, me ^ mask), mask) for mask in diagonal]
     pairs.append(pair_of(later, me))
-    far_pieces, near_pieces = pairs + far_pieces, pairs + near_pieces
+    whole = jax.ShapeDtypeStruct((owned, width), jnp.float32)
+    column = jax.ShapeDtypeStruct((owned, lanes), jnp.float32)
+    part, inverse, step = pl.pallas_call(
+        functools.partial(proxy_pairs_kernel, near, len(pairs), base),
+        in_specs=[array] * (len(pairs) + 3),
+        out_shape=(whole, column, column),
+        compiler_params=params,
+        name="proxy_pairs",
+    )(*pairs, sums, signs, matrix)
     sent = pl.pallas_call(
-        functools.partial(proxy_kernel, near, base),
-        in_specs=[array] * (near + 3),
+        functools.partial(proxy_kernel, len(far_pieces), base),
+        in_specs=[array] * (len(far_pieces) + 5),
         out_shape=jax.ShapeDtypeStruct((owned, width), jnp.int16),
         compiler_params=params,
         name="proxy_blocks",
-    )(*far_pieces, sums, signs, matrix)
+    )(*far_pieces, part, inverse, step, signs, matrix)
     far_total = swap(sent, near)
-    column = jax.ShapeDtypeStruct((owned, lanes), jnp.float32)
     near_total, mean_scale, step = pl.pallas_call(
         functools.partial(owner_kernel, near, base),
         in_specs=[array] * (near + 3),
-        out_shape=(jax.ShapeDtypeStruct((owned, width), jnp.float32), column, column),
+        out_shape=(whole, column, column),
         compiler_params=params,
         name="owner_blocks",
-    )(*near_pieces, sums, signs, matrix)
+    )(*pairs, *near_pieces, sums, signs, matrix)
     total, squares = pl.pallas_call(
         finish_kernel,
         in_specs=[array] * 4,

time: 57.6 us -> 57.7 us (level)
  no operation moved by 1% of the time
where the time goes in v18:
time: 57.7 us; the launch traced here: 57.4 us
  waiting for transfers between devices  25.1 us (44%)
  starting transfers between devices  24.6 us (43%)
  Pallas kernels  5.77 us (10%)
  local copies, waits for them, and re-layouts  1.21 us (2%)
  between operations  0.8 us (1%)
    ppermute x12, starting transfers between devices, swap(): return lax.ppermute(value, 'dp', [(i, i ^ mask) for i in range(size)])  15.9 us
    ppermute x12, waiting for transfers between devices, swap(): return lax.ppermute(value, 'dp', [(i, i ^ mask) for i in range(size)])  14.9 us
    all_to_all x1, waiting for transfers between devices, on_device(): lax.all_to_all(squares, ('dp', 'expert'), split_axis=0, concat_axis=0, ti...  6.72 us
    all_to_all x1, starting transfers between devices, on_device(): lax.all_to_all(sums.reshape(replicas, 1, 2 * owned), 'dp', split_axis=0,...  6.18 us
    all_to_all x1, waiting for transfers between devices, on_device(): lax.all_to_all(sums.reshape(replicas, 1, 2 * owned), 'dp', split_axis=0,...  3.44 us
    all_to_all x1, starting transfers between devices, on_device(): lax.all_to_all(squares, ('dp', 'expert'), split_axis=0, concat_axis=0, ti...  2.54 us
    pallas_call x2, Pallas kernels, place_pieces(): pl.pallas_call(functools.partial(place_kernel, places, owned), in_specs=s...  1.64 us
    reshape x2, local copies, waits for them, and re-layouts, pair_of(): lax.dynamic_slice_in_dim(source, index % near, 1, 1)  1.17 us
  transfers between devices with their start and end apart: 14, of which 7 were waited for; matrix products, arithmetic and copies ran while one was open for 0% of the time, Pallas kernels for 7%

profile of v18, /device:TPU:0, one launch (start us, length us, event | category | flops | bytes accessed | tf_op | source)
XLA Modules:
  0.0 57.4 jit_solution(4297659022441154338)
XLA Ops:
  0.7 1.2 %dynamic-slice_bitcast_fusion.1 = (bf16[2,64,1024]{2,1,0:T(8,128)(2,1)S(1)}, bf16[2,64,1024]{2,1,0:T(8,128)(2,1)S(1)}) fusion(bf16[2,4,64,1024]{3,2,1,0:T(8,128)(2,1)} %bitcast.24, s32[]{:T(128)S(6)} %select_n.33, s32[]{:T(128)S(6)} %select_n.31), kind=kLoop, calls=%fused_computation.1 | loop fusion | bytes 1048584 | tf_op jit(solution)/shard_map/reshape | solution.py:248
  1.8 3.1 %collective-permute-start.1 = (bf16[2,64,1024]{2,1,0:T(8,128)(2,1)S(1)}, bf16[2,64,1024]{2,1,0:T(8,128)(2,1)S(1)}, u32[]{:S(2)}, u32[]{:S(2)}) collective-permute-start(bf16[2,64,1024]{2,1,0:T(8,128)(2,1)S(1)} %get-tuple-element.24), channel_id=1, source_target_pairs={{0,8},{4,12},{8,0},{12,4},{16,24},{20,28},{24,16},{28,20},{1,9},{5... | collective-permute-start | bytes 786440 | tf_op jit(solution)/shard_map/ppermute | solution.py:184
  4.9 1.5 %collective-permute-start = (bf16[2,64,1024]{2,1,0:T(8,128)(2,1)S(1)}, bf16[2,64,1024]{2,1,0:T(8,128)(2,1)S(1)}, u32[]{:S(2)}, u32[]{:S(2)}) collective-permute-start(bf16[2,64,1024]{2,1,0:T(8,128)(2,1)S(1)} %get-tuple-element.25), channel_id=1, source_target_pairs={{0,4},{4,0},{8,12},{12,8},{16,20},{20,16},{24,28},{28,24},{1,5},{5... | collective-permute-start | bytes 786440 | tf_op jit(solution)/shard_map/ppermute | solution.py:184
  6.4 0.9 %sum_squares.1 = f32[2,4,1,128]{3,2,1,0:T(1,128)} custom-call(bf16[2,4,64,1024]{3,2,1,0:T(8,128)(2,1)S(1)} %bitcast.25), custom_call_target="tpu_custom_call" | custom-call | tf_op jit(solution)/shard_map/sum_squares/pallas_call | solution.py:258
  7.4 6.2 %all-to-all-start = ((f32[8,1,128]{2,1,0:T(1,128)}), f32[8,1,128]{2,1,0:T(1,128)S(1)}, u32[]{:S(2)}, u32[]{:S(2)}) async-start(f32[8,1,128]{2,1,0:T(1,128)} %bitcast.8), calls=%async_computation | async-start | bytes 8192 | tf_op jit(solution)/shard_map/all_to_all | solution.py:266
  13.6 2.9 %collective-permute-start.2 = (bf16[64,1024]{1,0:T(8,128)(2,1)S(1)}, bf16[64,1024]{1,0:T(8,128)(2,1)S(1)}, u32[]{:S(2)}, u32[]{:S(2)}) collective-permute-start(bf16[64,1024]{1,0:T(8,128)(2,1)S(1)} %get-tuple-element.23), channel_id=1, source_target_pairs={{0,12},{4,8},{8,4},{12,0},{16,28},{20,24},{24,20},{28,16},{1,13},{... | collective-permute-start | bytes 393224 | tf_op jit(solution)/shard_map/ppermute | solution.py:184
  16.6 3.4 %all-to-all-done = f32[8,1,128]{2,1,0:T(1,128)S(1)} async-done(((f32[8,1,128]{2,1,0:T(1,128)}), f32[8,1,128]{2,1,0:T(1,128)S(1)}, u32[]{:S(2)}, u32[]{:S(2)}) %all-to-all-start) | async-done | bytes 4128 | tf_op jit(solution)/shard_map/all_to_all | solution.py:266
  20.8 0.6 %collective-permute-start.4 = (s16[64,1024]{1,0:T(8,128)(2,1)S(1)}, s16[64,1024]{1,0:T(8,128)(2,1)S(1)}, u32[]{:S(2)}, u32[]{:S(2)}) collective-permute-start(s16[64,1024]{1,0:T(8,128)(2,1)S(1)} %proxy_blocks.1), channel_id=1, source_target_pairs={{0,16},{4,20},{8,24},{12,28},{16,0},{20,4},{24,8},{28,12},{1,17},{... | collective-permute-start | bytes 393224 | tf_op jit(solution)/shard_map/ppermute | solution.py:184
  22.0 6.1 %collective-permute-done.4.far_ref = s16[64,1024]{1,0:T(8,128)(2,1)S(1)} collective-permute-done((s16[64,1024]{1,0:T(8,128)(2,1)S(1)}, s16[64,1024]{1,0:T(8,128)(2,1)S(1)}, u32[]{:S(2)}, u32[]{:S(2)}) %collective-permute-start.4) | collective-permute-done | bytes 131104 | tf_op jit(solution)/shard_map/ppermute | solution.py:184
  28.1 0.7 %finish_blocks.1 = (f32[64,1024]{1,0:T(8,128)S(1)}, f32[32,1,128]{2,1,0:T(1,128)}) custom-call(f32[64,1024]{1,0:T(8,128)S(1)} %get-tuple-element.14.near_ref, s16[64,1024]{1,0:T(8,128)(2,1)S(1)} %collective-permute-done.4.far_ref, f32[64,128]{1,0:T(8,128)S(1)} %get-tuple-element.18.scale_ref, f32[64,128]{1,0:T(8,128)S(1)} %get-tuple-element.19.step_ref), custom_call_target="tpu_custom_call" | custom-call | tf_op jit(solution)/shard_map/finish_blocks/pallas_call | solution.py:296
  28.8 2.5 %all-to-all-start.1 = ((f32[32,1,128]{2,1,0:T(1,128)}), f32[32,1,128]{2,1,0:T(1,128)S(1)}, u32[]{:S(2)}, u32[]{:S(2)}) async-start(f32[32,1,128]{2,1,0:T(1,128)} %get-tuple-element.20), calls=%async_computation.1 | async-start | bytes 32768 | tf_op jit(solution)/shard_map/all_to_all | solution.py:312
  31.7 6.7 %all-to-all-done.1 = f32[32,1,128]{2,1,0:T(1,128)S(1)} async-done(((f32[32,1,128]{2,1,0:T(1,128)}), f32[32,1,128]{2,1,0:T(1,128)S(1)}, u32[]{:S(2)}, u32[]{:S(2)}) %all-to-all-start.1) | async-done | bytes 16416 | tf_op jit(solution)/shard_map/all_to_all | solution.py:312
  38.6 0.7 %collective-permute-start.5 = (bf16[64,1024]{1,0:T(8,128)(2,1)S(1)}, bf16[64,1024]{1,0:T(8,128)(2,1)S(1)}, u32[]{:S(2)}, u32[]{:S(2)}) collective-permute-start(bf16[64,1024]{1,0:T(8,128)(2,1)S(1)} %new_weights.1.refs_0_), channel_id=1, source_target_pairs={{0,16},{4,20},{8,24},{12,28},{16,0},{20,4},{24,8},{28,12},{1,17},{... | collective-permute-start | bytes 393224 | tf_op jit(solution)/shard_map/ppermute | solution.py:184
  39.2 0.6 collective-permute-start.11
  40.3 2.5 %collective-permute-start.9 = (bf16[64,1024]{1,0:T(8,128)(2,1)S(1)}, bf16[64,1024]{1,0:T(8,128)(2,1)S(1)}, u32[]{:S(2)}, u32[]{:S(2)}) collective-permute-start(bf16[64,1024]{1,0:T(8,128)(2,1)S(1)} %new_weights.1.refs_0_), channel_id=1, source_target_pairs={{0,12},{4,8},{8,4},{12,0},{16,28},{20,24},{24,20},{28,16},{1,13},{... | collective-permute-start | bytes 393224 | tf_op jit(solution)/shard_map/ppermute | solution.py:184
  42.7 4.9 %collective-permute-done.5.refs_4_ = bf16[64,1024]{1,0:T(8,128)(2,1)S(1)} collective-permute-done((bf16[64,1024]{1,0:T(8,128)(2,1)S(1)}, bf16[64,1024]{1,0:T(8,128)(2,1)S(1)}, u32[]{:S(2)}, u32[]{:S(2)}) %collective-permute-start.5) | collective-permute-done | bytes 131104 | tf_op jit(solution)/shard_map/ppermute | solution.py:184
  47.6 2.1 %collective-permute-start.7 = (bf16[64,1024]{1,0:T(8,128)(2,1)S(1)}, bf16[64,1024]{1,0:T(8,128)(2,1)S(1)}, u32[]{:S(2)}, u32[]{:S(2)}) collective-permute-start(bf16[64,1024]{1,0:T(8,128)(2,1)S(1)} %collective-permute-done.5.refs_4_), channel_id=1, source_target_pairs={{0,8},{4,12},{8,0},{12,4},{16,24},{20,28},{24,16},{28,20},{1,9},{5... | collective-permute-start | bytes 393224 | tf_op jit(solution)/shard_map/ppermute | solution.py:184
  49.7 1.4 %collective-permute-start.6 = (bf16[64,1024]{1,0:T(8,128)(2,1)S(1)}, bf16[64,1024]{1,0:T(8,128)(2,1)S(1)}, u32[]{:S(2)}, u32[]{:S(2)}) collective-permute-start(bf16[64,1024]{1,0:T(8,128)(2,1)S(1)} %collective-permute-done.5.refs_4_), channel_id=1, source_target_pairs={{0,4},{4,0},{8,12},{12,8},{16,20},{20,16},{24,28},{28,24},{1,5},{5... | collective-permute-start | bytes 393224 | tf_op jit(solution)/shard_map/ppermute | solution.py:184
  51.1 0.8 %update_grad.1 = f32[64,1024]{1,0:T(8,128)} custom-call(f32[32,128]{1,0:T(8,128)S(1)} %bitcast.29, f32[64,1024]{1,0:T(8,128)S(1)} %rotate_back.1.unrot_ref), custom_call_target="tpu_custom_call" | custom-call | tf_op jit(solution)/shard_map/update_grad/pallas_call | solution.py:321
  51.9 0.9 %place_own.1.refs_3_ = bf16[512,1024]{1,0:T(8,128)(2,1)} custom-call(bf16[64,1024]{1,0:T(8,128)(2,1)S(1)} %new_weights.1.refs_0_, bf16[64,1024]{1,0:T(8,128)(2,1)S(1)} %collective-permute-done.9.refs_1_, bf16[64,1024]{1,0:T(8,128)(2,1)S(1)} %collective-permute-done.10.refs_2_, bf16[64,1024]{1,0:T(8,128)(2,1)S(1)} %collective-permute-done.11.refs_3_, ...), custom_call_target="tpu_custom_call" | custom-call | tf_op jit(solution)/shard_map/place_own/pallas_call | solution.py:211
  52.8 2.1 %collective-permute-done.8.refs_2_ = bf16[64,1024]{1,0:T(8,128)(2,1)S(1)} collective-permute-done((bf16[64,1024]{1,0:T(8,128)(2,1)S(1)}, bf16[64,1024]{1,0:T(8,128)(2,1)S(1)}, u32[]{:S(2)}, u32[]{:S(2)}) %collective-permute-start.8) | collective-permute-done | bytes 131104 | tf_op jit(solution)/shard_map/ppermute | solution.py:184
  54.9 0.9 %collective-permute-done.7.refs_1_ = bf16[64,1024]{1,0:T(8,128)(2,1)S(1)} collective-permute-done((bf16[64,1024]{1,0:T(8,128)(2,1)S(1)}, bf16[64,1024]{1,0:T(8,128)(2,1)S(1)}, u32[]{:S(2)}, u32[]{:S(2)}) %collective-permute-start.7) | collective-permute-done | bytes 131104 | tf_op jit(solution)/shard_map/ppermute | solution.py:184
  55.8 0.9 %collective-permute-done.6.refs_0_ = bf16[64,1024]{1,0:T(8,128)(2,1)S(1)} collective-permute-done((bf16[64,1024]{1,0:T(8,128)(2,1)S(1)}, bf16[64,1024]{1,0:T(8,128)(2,1)S(1)}, u32[]{:S(2)}, u32[]{:S(2)}) %collective-permute-start.6) | collective-permute-done | bytes 131104 | tf_op jit(solution)/shard_map/ppermute | solution.py:184
  56.7 0.8 %place_far.1 = bf16[512,1024]{1,0:T(8,128)(2,1)} custom-call(bf16[64,1024]{1,0:T(8,128)(2,1)S(1)} %collective-permute-done.6.refs_0_, bf16[64,1024]{1,0:T(8,128)(2,1)S(1)} %collective-permute-done.7.refs_1_, bf16[64,1024]{1,0:T(8,128)(2,1)S(1)} %collective-permute-done.8.refs_2_, bf16[512,1024]{1,0:T(8,128)(2,1)} %place_own.1.refs_3_), custom_call_target="tpu_custom_call", output_to_operand_aliasing={{}: (3, {})} | custom-call | tf_op jit(solution)/shard_map/place_far/pallas_call | solution.py:211
  (27 shorter events, 2.4 us)
Async XLA Ops:
  0.6 5.8 %copy-start = (bf16[1,1,512,1024]{3,2,1,0:T(8,128)(2,1)S(1)}, bf16[1,1,512,1024]{3,2,1,0:T(8,128)(2,1)}, u32[]{:S(2)}) copy-start(bf16[1,1,512,1024]{3,2,1,0:T(8,128)(2,1)} %param.5) | copy-start | bytes 3145732
  1.8 18.2 %collective-permute-start.1 = (bf16[2,64,1024]{2,1,0:T(8,128)(2,1)S(1)}, bf16[2,64,1024]{2,1,0:T(8,128)(2,1)S(1)}, u32[]{:S(2)}, u32[]{:S(2)}) collective-permute-start(bf16[2,64,1024]{2,1,0:T(8,128)(2,1)S(1)} %get-tuple-element.24), channel_id=1, source_target_pairs={{0,8},{4,12},{8,0},{12,4},{16,24},{20,28},{24,16},{28,20},{1,9},{5... | collective-permute-start | bytes 786440 | tf_op jit(solution)/shard_map/ppermute | solution.py:184
  4.9 15.1 %collective-permute-start = (bf16[2,64,1024]{2,1,0:T(8,128)(2,1)S(1)}, bf16[2,64,1024]{2,1,0:T(8,128)(2,1)S(1)}, u32[]{:S(2)}, u32[]{:S(2)}) collective-permute-start(bf16[2,64,1024]{2,1,0:T(8,128)(2,1)S(1)} %get-tuple-element.25), channel_id=1, source_target_pairs={{0,4},{4,0},{8,12},{12,8},{16,20},{20,16},{24,28},{28,24},{1,5},{5... | collective-permute-start | bytes 786440 | tf_op jit(solution)/shard_map/ppermute | solution.py:184
  7.3 13.1 %collective-permute-start.3 = (bf16[64,1024]{1,0:T(8,128)(2,1)S(1)}, bf16[64,1024]{1,0:T(8,128)(2,1)S(1)}, u32[]{:S(2)}, u32[]{:S(2)}) collective-permute-start(bf16[64,1024]{1,0:T(8,128)(2,1)S(1)} %get-tuple-element.22), channel_id=1, source_target_pairs={{0,12},{4,8},{8,4},{12,0},{16,28},{20,24},{24,20},{28,16},{1,13},{... | collective-permute-start | bytes 393224 | tf_op jit(solution)/shard_map/ppermute | solution.py:184
  7.4 12.6 %all-to-all-start = ((f32[8,1,128]{2,1,0:T(1,128)}), f32[8,1,128]{2,1,0:T(1,128)S(1)}, u32[]{:S(2)}, u32[]{:S(2)}) async-start(f32[8,1,128]{2,1,0:T(1,128)} %bitcast.8), calls=%async_computation | async-start | bytes 8192 | tf_op jit(solution)/shard_map/all_to_all | solution.py:266
  13.6 7.8 %collective-permute-start.2 = (bf16[64,1024]{1,0:T(8,128)(2,1)S(1)}, bf16[64,1024]{1,0:T(8,128)(2,1)S(1)}, u32[]{:S(2)}, u32[]{:S(2)}) collective-permute-start(bf16[64,1024]{1,0:T(8,128)(2,1)S(1)} %get-tuple-element.23), channel_id=1, source_target_pairs={{0,12},{4,8},{8,4},{12,0},{16,28},{20,24},{24,20},{28,16},{1,13},{... | collective-permute-start | bytes 393224 | tf_op jit(solution)/shard_map/ppermute | solution.py:184
  16.5 3.5 %copy-start.1 = (bf16[256,256]{1,0:T(8,128)(2,1)S(1)}, bf16[256,256]{1,0:T(8,128)(2,1)}, u32[]{:S(2)}) copy-start(bf16[256,256]{1,0:T(8,128)(2,1)} %constant.37.clone.refs_6_.refs_5_.matrix_ref) | copy-start | bytes 393220
  16.5 3.5 %copy-start.4 = (s32[1,1024]{1,0:T(1,128)S(1)}, s32[1,1024]{1,0:T(1,128)}, u32[]{:S(2)}) copy-start(s32[1,1024]{1,0:T(1,128)} %sign_ref.1) | copy-start | bytes 12292
  20.8 7.3 %collective-permute-start.4 = (s16[64,1024]{1,0:T(8,128)(2,1)S(1)}, s16[64,1024]{1,0:T(8,128)(2,1)S(1)}, u32[]{:S(2)}, u32[]{:S(2)}) collective-permute-start(s16[64,1024]{1,0:T(8,128)(2,1)S(1)} %proxy_blocks.1), channel_id=1, source_target_pairs={{0,16},{4,20},{8,24},{12,28},{16,0},{20,4},{24,8},{28,12},{1,17},{... | collective-permute-start | bytes 393224 | tf_op jit(solution)/shard_map/ppermute | solution.py:184
  28.8 9.6 %all-to-all-start.1 = ((f32[32,1,128]{2,1,0:T(1,128)}), f32[32,1,128]{2,1,0:T(1,128)S(1)}, u32[]{:S(2)}, u32[]{:S(2)}) async-start(f32[32,1,128]{2,1,0:T(1,128)} %get-tuple-element.20), calls=%async_computation.1 | async-start | bytes 32768 | tf_op jit(solution)/shard_map/all_to_all | solution.py:312
  31.3 7.1 %copy-start.2 = (bf16[1,64,1024]{2,1,0:T(8,128)(2,1)S(1)}, bf16[1,64,1024]{2,1,0:T(8,128)(2,1)}, u32[]{:S(2)}) copy-start(bf16[1,64,1024]{2,1,0:T(8,128)(2,1)} %param.7) | copy-start | bytes 393220
  31.3 7.1 %copy-start.3 = (bf16[1,64,1024]{2,1,0:T(8,128)(2,1)S(1)}, bf16[1,64,1024]{2,1,0:T(8,128)(2,1)}, u32[]{:S(2)}) copy-start(bf16[1,64,1024]{2,1,0:T(8,128)(2,1)} %param.8) | copy-start | bytes 393220
  38.6 9.0 %collective-permute-start.5 = (bf16[64,1024]{1,0:T(8,128)(2,1)S(1)}, bf16[64,1024]{1,0:T(8,128)(2,1)S(1)}, u32[]{:S(2)}, u32[]{:S(2)}) collective-permute-start(bf16[64,1024]{1,0:T(8,128)(2,1)S(1)} %new_weights.1.refs_0_), channel_id=1, source_target_pairs={{0,16},{4,20},{8,24},{12,28},{16,0},{20,4},{24,8},{28,12},{1,17},{... | collective-permute-start | bytes 393224 | tf_op jit(solution)/shard_map/ppermute | solution.py:184
  39.2 10.5 %collective-permute-start.11 = (bf16[64,1024]{1,0:T(8,128)(2,1)S(1)}, bf16[64,1024]{1,0:T(8,128)(2,1)S(1)}, u32[]{:S(2)}, u32[]{:S(2)}) collective-permute-start(bf16[64,1024]{1,0:T(8,128)(2,1)S(1)} %new_weights.1.refs_0_), channel_id=1, source_target_pairs={{0,4},{4,0},{8,12},{12,8},{16,20},{20,16},{24,28},{28,24},{1,5},{5... | collective-permute-start | bytes 393224 | tf_op jit(solution)/shard_map/ppermute | solution.py:184
  39.8 12.1 %collective-permute-start.10 = (bf16[64,1024]{1,0:T(8,128)(2,1)S(1)}, bf16[64,1024]{1,0:T(8,128)(2,1)S(1)}, u32[]{:S(2)}, u32[]{:S(2)}) collective-permute-start(bf16[64,1024]{1,0:T(8,128)(2,1)S(1)} %new_weights.1.refs_0_), channel_id=1, source_target_pairs={{0,8},{4,12},{8,0},{12,4},{16,24},{20,28},{24,16},{28,20},{1,9},{5... | collective-permute-start | bytes 393224 | tf_op jit(solution)/shard_map/ppermute | solution.py:184
  40.3 11.7 %collective-permute-start.9 = (bf16[64,1024]{1,0:T(8,128)(2,1)S(1)}, bf16[64,1024]{1,0:T(8,128)(2,1)S(1)}, u32[]{:S(2)}, u32[]{:S(2)}) collective-permute-start(bf16[64,1024]{1,0:T(8,128)(2,1)S(1)} %new_weights.1.refs_0_), channel_id=1, source_target_pairs={{0,12},{4,8},{8,4},{12,0},{16,28},{20,24},{24,20},{28,16},{1,13},{... | collective-permute-start | bytes 393224 | tf_op jit(solution)/shard_map/ppermute | solution.py:184
  47.6 7.3 %collective-permute-start.8 = (bf16[64,1024]{1,0:T(8,128)(2,1)S(1)}, bf16[64,1024]{1,0:T(8,128)(2,1)S(1)}, u32[]{:S(2)}, u32[]{:S(2)}) collective-permute-start(bf16[64,1024]{1,0:T(8,128)(2,1)S(1)} %collective-permute-done.5.refs_4_), channel_id=1, source_target_pairs={{0,12},{4,8},{8,4},{12,0},{16,28},{20,24},{24,20},{28,16},{1,13},{... | collective-permute-start | bytes 393224 | tf_op jit(solution)/shard_map/ppermute | solution.py:184
  47.6 8.2 %collective-permute-start.7 = (bf16[64,1024]{1,0:T(8,128)(2,1)S(1)}, bf16[64,1024]{1,0:T(8,128)(2,1)S(1)}, u32[]{:S(2)}, u32[]{:S(2)}) collective-permute-start(bf16[64,1024]{1,0:T(8,128)(2,1)S(1)} %collective-permute-done.5.refs_4_), channel_id=1, source_target_pairs={{0,8},{4,12},{8,0},{12,4},{16,24},{20,28},{24,16},{28,20},{1,9},{5... | collective-permute-start | bytes 393224 | tf_op jit(solution)/shard_map/ppermute | solution.py:184
  49.7 7.0 %collective-permute-start.6 = (bf16[64,1024]{1,0:T(8,128)(2,1)S(1)}, bf16[64,1024]{1,0:T(8,128)(2,1)S(1)}, u32[]{:S(2)}, u32[]{:S(2)}) collective-permute-start(bf16[64,1024]{1,0:T(8,128)(2,1)S(1)} %collective-permute-done.5.refs_4_), channel_id=1, source_target_pairs={{0,4},{4,0},{8,12},{12,8},{16,20},{20,16},{24,28},{28,24},{1,5},{5... | collective-permute-start | bytes 393224 | tf_op jit(solution)/shard_map/ppermute | solution.py:184

commit v19 on v18

--- a/solution.py
+++ b/solution.py
@@ -221,10 +221,17 @@
 
 
 def gather_blocks(block, replicas):
+    x_count = chips_along_x(replicas)
     near = replicas // 2
     owned, width = block.shape
     far = swap(block, near)
-    own = [(0, 0, block)] + [(m, 0, swap(block, m)) for m in reversed(range(1, near))]
+    own = {0: block}
+    for m in range(1, near):
+        own[m] = swap(block, m) if m < x_count or m % x_count == 0 else None
+    for m in range(1, near):
+        if own[m] is None:
+            own[m] = swap(own[m - m % x_count], m % x_count)
+    own = [(m, 0, piece) for m, piece in own.items()]
     spread = [(near + m, 0, swap(far, m)) for m in range(1, near)]
     out = place_pieces(own + [(near, 0, far)], owned, replicas, None, "place_own")
     out = place_pieces(spread, owned, replicas, out, "place_far")

time: 57.7 us -> 56.5 us (0.979)
  starting transfers between devices: 24.6 us -> 22.7 us
  waiting for transfers between devices: 25.1 us -> 25.8 us
    ppermute x12, starting transfers between devices: 15.9 us -> 14 us  [swap(): return lax.ppermute(value, 'dp', [(i, i ^ mask) for i in range(size)])]
    ppermute x12, waiting for transfers between devices: 14.9 us -> 15.6 us  [swap(): return lax.ppermute(value, 'dp', [(i, i ^ mask) for i in range(size)])]
  transfers between devices with their start and end apart: 14 -> 14, of which waited for: 7 -> 9; matrix products, arithmetic and copies ran while one was open for 0% -> 0% of each run, Pallas kernels for 7% -> 7%
where the time goes in v19:
time: 56.5 us; the launch traced here: 56.3 us
  waiting for transfers between devices  25.8 us (46%)
  starting transfers between devices  22.7 us (40%)
  Pallas kernels  5.77 us (10%)
  local copies, waits for them, and re-layouts  1.21 us (2%)
  between operations  0.8 us (1%)
    ppermute x12, waiting for transfers between devices, swap(): return lax.ppermute(value, 'dp', [(i, i ^ mask) for i in range(size)])  15.6 us
    ppermute x12, starting transfers between devices, swap(): return lax.ppermute(value, 'dp', [(i, i ^ mask) for i in range(size)])  14 us
    all_to_all x1, waiting for transfers between devices, on_device(): lax.all_to_all(squares, ('dp', 'expert'), split_axis=0, concat_axis=0, ti...  6.72 us
    all_to_all x1, starting transfers between devices, on_device(): lax.all_to_all(sums.reshape(replicas, 1, 2 * owned), 'dp', split_axis=0,...  6.18 us
    all_to_all x1, waiting for transfers between devices, on_device(): lax.all_to_all(sums.reshape(replicas, 1, 2 * owned), 'dp', split_axis=0,...  3.44 us
    all_to_all x1, starting transfers between devices, on_device(): lax.all_to_all(squares, ('dp', 'expert'), split_axis=0, concat_axis=0, ti...  2.54 us
    pallas_call x2, Pallas kernels, place_pieces(): pl.pallas_call(functools.partial(place_kernel, places, owned), in_specs=s...  1.63 us
    reshape x2, local copies, waits for them, and re-layouts, pair_of(): lax.dynamic_slice_in_dim(source, index % near, 1, 1)  1.17 us
  transfers between devices with their start and end apart: 14, of which 9 were waited for; matrix products, arithmetic and copies ran while one was open for 0% of the time, Pallas kernels for 7%

profile of v19, /device:TPU:0, one launch (start us, length us, event | category | flops | bytes accessed | tf_op | source)
XLA Modules:
  0.0 56.3 jit_solution(8717058806908157571)
XLA Ops:
  0.7 1.2 %dynamic-slice_bitcast_fusion.1 = (bf16[2,64,1024]{2,1,0:T(8,128)(2,1)S(1)}, bf16[2,64,1024]{2,1,0:T(8,128)(2,1)S(1)}) fusion(bf16[2,4,64,1024]{3,2,1,0:T(8,128)(2,1)} %bitcast.24, s32[]{:T(128)S(6)} %select_n.33, s32[]{:T(128)S(6)} %select_n.31), kind=kLoop, calls=%fused_computation.1 | loop fusion | bytes 1048584 | tf_op jit(solution)/shard_map/reshape | solution.py:255
  1.8 3.1 %collective-permute-start.1 = (bf16[2,64,1024]{2,1,0:T(8,128)(2,1)S(1)}, bf16[2,64,1024]{2,1,0:T(8,128)(2,1)S(1)}, u32[]{:S(2)}, u32[]{:S(2)}) collective-permute-start(bf16[2,64,1024]{2,1,0:T(8,128)(2,1)S(1)} %get-tuple-element.24), channel_id=1, source_target_pairs={{0,8},{4,12},{8,0},{12,4},{16,24},{20,28},{24,16},{28,20},{1,9},{5... | collective-permute-start | bytes 786440 | tf_op jit(solution)/shard_map/ppermute | solution.py:184
  4.9 1.5 %collective-permute-start = (bf16[2,64,1024]{2,1,0:T(8,128)(2,1)S(1)}, bf16[2,64,1024]{2,1,0:T(8,128)(2,1)S(1)}, u32[]{:S(2)}, u32[]{:S(2)}) collective-permute-start(bf16[2,64,1024]{2,1,0:T(8,128)(2,1)S(1)} %get-tuple-element.25), channel_id=1, source_target_pairs={{0,4},{4,0},{8,12},{12,8},{16,20},{20,16},{24,28},{28,24},{1,5},{5... | collective-permute-start | bytes 786440 | tf_op jit(solution)/shard_map/ppermute | solution.py:184
  6.4 0.9 %sum_squares.1 = f32[2,4,1,128]{3,2,1,0:T(1,128)} custom-call(bf16[2,4,64,1024]{3,2,1,0:T(8,128)(2,1)S(1)} %bitcast.25), custom_call_target="tpu_custom_call" | custom-call | tf_op jit(solution)/shard_map/sum_squares/pallas_call | solution.py:265
  7.4 6.2 %all-to-all-start = ((f32[8,1,128]{2,1,0:T(1,128)}), f32[8,1,128]{2,1,0:T(1,128)S(1)}, u32[]{:S(2)}, u32[]{:S(2)}) async-start(f32[8,1,128]{2,1,0:T(1,128)} %bitcast.8), calls=%async_computation | async-start | bytes 8192 | tf_op jit(solution)/shard_map/all_to_all | solution.py:273
  13.6 2.9 %collective-permute-start.2 = (bf16[64,1024]{1,0:T(8,128)(2,1)S(1)}, bf16[64,1024]{1,0:T(8,128)(2,1)S(1)}, u32[]{:S(2)}, u32[]{:S(2)}) collective-permute-start(bf16[64,1024]{1,0:T(8,128)(2,1)S(1)} %get-tuple-element.23), channel_id=1, source_target_pairs={{0,12},{4,8},{8,4},{12,0},{16,28},{20,24},{24,20},{28,16},{1,13},{... | collective-permute-start | bytes 393224 | tf_op jit(solution)/shard_map/ppermute | solution.py:184
  16.6 3.4 %all-to-all-done = f32[8,1,128]{2,1,0:T(1,128)S(1)} async-done(((f32[8,1,128]{2,1,0:T(1,128)}), f32[8,1,128]{2,1,0:T(1,128)S(1)}, u32[]{:S(2)}, u32[]{:S(2)}) %all-to-all-start) | async-done | bytes 4128 | tf_op jit(solution)/shard_map/all_to_all | solution.py:273
  20.8 0.6 %collective-permute-start.4 = (s16[64,1024]{1,0:T(8,128)(2,1)S(1)}, s16[64,1024]{1,0:T(8,128)(2,1)S(1)}, u32[]{:S(2)}, u32[]{:S(2)}) collective-permute-start(s16[64,1024]{1,0:T(8,128)(2,1)S(1)} %proxy_blocks.1), channel_id=1, source_target_pairs={{0,16},{4,20},{8,24},{12,28},{16,0},{20,4},{24,8},{28,12},{1,17},{... | collective-permute-start | bytes 393224 | tf_op jit(solution)/shard_map/ppermute | solution.py:184
  21.4 0.6 owner_blocks.1
  22.0 6.1 %collective-permute-done.4.far_ref = s16[64,1024]{1,0:T(8,128)(2,1)S(1)} collective-permute-done((s16[64,1024]{1,0:T(8,128)(2,1)S(1)}, s16[64,1024]{1,0:T(8,128)(2,1)S(1)}, u32[]{:S(2)}, u32[]{:S(2)}) %collective-permute-start.4) | collective-permute-done | bytes 131104 | tf_op jit(solution)/shard_map/ppermute | solution.py:184
  28.1 0.7 %finish_blocks.1 = (f32[64,1024]{1,0:T(8,128)S(1)}, f32[32,1,128]{2,1,0:T(1,128)}) custom-call(f32[64,1024]{1,0:T(8,128)S(1)} %get-tuple-element.14.near_ref, s16[64,1024]{1,0:T(8,128)(2,1)S(1)} %collective-permute-done.4.far_ref, f32[64,128]{1,0:T(8,128)S(1)} %get-tuple-element.18.scale_ref, f32[64,128]{1,0:T(8,128)S(1)} %get-tuple-element.19.step_ref), custom_call_target="tpu_custom_call" | custom-call | tf_op jit(solution)/shard_map/finish_blocks/pallas_call | solution.py:303
  28.8 2.5 %all-to-all-start.1 = ((f32[32,1,128]{2,1,0:T(1,128)}), f32[32,1,128]{2,1,0:T(1,128)S(1)}, u32[]{:S(2)}, u32[]{:S(2)}) async-start(f32[32,1,128]{2,1,0:T(1,128)} %get-tuple-element.20), calls=%async_computation.1 | async-start | bytes 32768 | tf_op jit(solution)/shard_map/all_to_all | solution.py:319
  31.7 6.7 %all-to-all-done.1 = f32[32,1,128]{2,1,0:T(1,128)S(1)} async-done(((f32[32,1,128]{2,1,0:T(1,128)}), f32[32,1,128]{2,1,0:T(1,128)S(1)}, u32[]{:S(2)}, u32[]{:S(2)}) %all-to-all-start.1) | async-done | bytes 16416 | tf_op jit(solution)/shard_map/all_to_all | solution.py:319
  38.6 0.6 %collective-permute-start.10 = (bf16[64,1024]{1,0:T(8,128)(2,1)S(1)}, bf16[64,1024]{1,0:T(8,128)(2,1)S(1)}, u32[]{:S(2)}, u32[]{:S(2)}) collective-permute-start(bf16[64,1024]{1,0:T(8,128)(2,1)S(1)} %new_weights.1.refs_0_), channel_id=1, source_target_pairs={{0,8},{4,12},{8,0},{12,4},{16,24},{20,28},{24,16},{28,20},{1,9},{5... | collective-permute-start | bytes 393224 | tf_op jit(solution)/shard_map/ppermute | solution.py:184
  39.2 0.6 collective-permute-start.5
  40.3 5.2 %collective-permute-done.10.refs_2_ = bf16[64,1024]{1,0:T(8,128)(2,1)S(1)} collective-permute-done((bf16[64,1024]{1,0:T(8,128)(2,1)S(1)}, bf16[64,1024]{1,0:T(8,128)(2,1)S(1)}, u32[]{:S(2)}, u32[]{:S(2)}) %collective-permute-start.10) | collective-permute-done | bytes 131104 | tf_op jit(solution)/shard_map/ppermute | solution.py:184
  45.5 0.5 collective-permute-start.11
  46.1 1.8 %collective-permute-done.5.refs_4_ = bf16[64,1024]{1,0:T(8,128)(2,1)S(1)} collective-permute-done((bf16[64,1024]{1,0:T(8,128)(2,1)S(1)}, bf16[64,1024]{1,0:T(8,128)(2,1)S(1)}, u32[]{:S(2)}, u32[]{:S(2)}) %collective-permute-start.5) | collective-permute-done | bytes 131104 | tf_op jit(solution)/shard_map/ppermute | solution.py:184
  47.8 2.1 %collective-permute-start.7 = (bf16[64,1024]{1,0:T(8,128)(2,1)S(1)}, bf16[64,1024]{1,0:T(8,128)(2,1)S(1)}, u32[]{:S(2)}, u32[]{:S(2)}) collective-permute-start(bf16[64,1024]{1,0:T(8,128)(2,1)S(1)} %collective-permute-done.5.refs_4_), channel_id=1, source_target_pairs={{0,8},{4,12},{8,0},{12,4},{16,24},{20,28},{24,16},{28,20},{1,9},{5... | collective-permute-start | bytes 393224 | tf_op jit(solution)/shard_map/ppermute | solution.py:184
  49.9 1.4 %collective-permute-start.6 = (bf16[64,1024]{1,0:T(8,128)(2,1)S(1)}, bf16[64,1024]{1,0:T(8,128)(2,1)S(1)}, u32[]{:S(2)}, u32[]{:S(2)}) collective-permute-start(bf16[64,1024]{1,0:T(8,128)(2,1)S(1)} %collective-permute-done.5.refs_4_), channel_id=1, source_target_pairs={{0,4},{4,0},{8,12},{12,8},{16,20},{20,16},{24,28},{28,24},{1,5},{5... | collective-permute-start | bytes 393224 | tf_op jit(solution)/shard_map/ppermute | solution.py:184
  51.3 0.8 %update_grad.1 = f32[64,1024]{1,0:T(8,128)} custom-call(f32[32,128]{1,0:T(8,128)S(1)} %bitcast.29, f32[64,1024]{1,0:T(8,128)S(1)} %rotate_back.1.unrot_ref), custom_call_target="tpu_custom_call" | custom-call | tf_op jit(solution)/shard_map/update_grad/pallas_call | solution.py:328
  52.4 0.9 %place_own.1.refs_3_ = bf16[512,1024]{1,0:T(8,128)(2,1)} custom-call(bf16[64,1024]{1,0:T(8,128)(2,1)S(1)} %new_weights.1.refs_0_, bf16[64,1024]{1,0:T(8,128)(2,1)S(1)} %collective-permute-done.9.refs_1_, bf16[64,1024]{1,0:T(8,128)(2,1)S(1)} %collective-permute-done.10.refs_2_, bf16[64,1024]{1,0:T(8,128)(2,1)S(1)} %collective-permute-done.11.refs_3_, ...), custom_call_target="tpu_custom_call" | custom-call | tf_op jit(solution)/shard_map/place_own/pallas_call | solution.py:211
  54.3 1.2 %collective-permute-done.6.refs_0_ = bf16[64,1024]{1,0:T(8,128)(2,1)S(1)} collective-permute-done((bf16[64,1024]{1,0:T(8,128)(2,1)S(1)}, bf16[64,1024]{1,0:T(8,128)(2,1)S(1)}, u32[]{:S(2)}, u32[]{:S(2)}) %collective-permute-start.6) | collective-permute-done | bytes 131104 | tf_op jit(solution)/shard_map/ppermute | solution.py:184
  55.5 0.8 %place_far.1 = bf16[512,1024]{1,0:T(8,128)(2,1)} custom-call(bf16[64,1024]{1,0:T(8,128)(2,1)S(1)} %collective-permute-done.6.refs_0_, bf16[64,1024]{1,0:T(8,128)(2,1)S(1)} %collective-permute-done.7.refs_1_, bf16[64,1024]{1,0:T(8,128)(2,1)S(1)} %collective-permute-done.8.refs_2_, bf16[512,1024]{1,0:T(8,128)(2,1)} %place_own.1.refs_3_), custom_call_target="tpu_custom_call", output_to_operand_aliasing={{}: (3, {})} | custom-call | tf_op jit(solution)/shard_map/place_far/pallas_call | solution.py:211
  (27 shorter events, 3.1 us)
Async XLA Ops:
  0.6 5.8 %copy-start = (bf16[1,1,512,1024]{3,2,1,0:T(8,128)(2,1)S(1)}, bf16[1,1,512,1024]{3,2,1,0:T(8,128)(2,1)}, u32[]{:S(2)}) copy-start(bf16[1,1,512,1024]{3,2,1,0:T(8,128)(2,1)} %param.5) | copy-start | bytes 3145732
  1.8 18.2 %collective-permute-start.1 = (bf16[2,64,1024]{2,1,0:T(8,128)(2,1)S(1)}, bf16[2,64,1024]{2,1,0:T(8,128)(2,1)S(1)}, u32[]{:S(2)}, u32[]{:S(2)}) collective-permute-start(bf16[2,64,1024]{2,1,0:T(8,128)(2,1)S(1)} %get-tuple-element.24), channel_id=1, source_target_pairs={{0,8},{4,12},{8,0},{12,4},{16,24},{20,28},{24,16},{28,20},{1,9},{5... | collective-permute-start | bytes 786440 | tf_op jit(solution)/shard_map/ppermute | solution.py:184
  4.9 15.1 %collective-permute-start = (bf16[2,64,1024]{2,1,0:T(8,128)(2,1)S(1)}, bf16[2,64,1024]{2,1,0:T(8,128)(2,1)S(1)}, u32[]{:S(2)}, u32[]{:S(2)}) collective-permute-start(bf16[2,64,1024]{2,1,0:T(8,128)(2,1)S(1)} %get-tuple-element.25), channel_id=1, source_target_pairs={{0,4},{4,0},{8,12},{12,8},{16,20},{20,16},{24,28},{28,24},{1,5},{5... | collective-permute-start | bytes 786440 | tf_op jit(solution)/shard_map/ppermute | solution.py:184
  7.3 13.1 %collective-permute-start.3 = (bf16[64,1024]{1,0:T(8,128)(2,1)S(1)}, bf16[64,1024]{1,0:T(8,128)(2,1)S(1)}, u32[]{:S(2)}, u32[]{:S(2)}) collective-permute-start(bf16[64,1024]{1,0:T(8,128)(2,1)S(1)} %get-tuple-element.22), channel_id=1, source_target_pairs={{0,12},{4,8},{8,4},{12,0},{16,28},{20,24},{24,20},{28,16},{1,13},{... | collective-permute-start | bytes 393224 | tf_op jit(solution)/shard_map/ppermute | solution.py:184
  7.4 12.6 %all-to-all-start = ((f32[8,1,128]{2,1,0:T(1,128)}), f32[8,1,128]{2,1,0:T(1,128)S(1)}, u32[]{:S(2)}, u32[]{:S(2)}) async-start(f32[8,1,128]{2,1,0:T(1,128)} %bitcast.8), calls=%async_computation | async-start | bytes 8192 | tf_op jit(solution)/shard_map/all_to_all | solution.py:273
  13.6 7.8 %collective-permute-start.2 = (bf16[64,1024]{1,0:T(8,128)(2,1)S(1)}, bf16[64,1024]{1,0:T(8,128)(2,1)S(1)}, u32[]{:S(2)}, u32[]{:S(2)}) collective-permute-start(bf16[64,1024]{1,0:T(8,128)(2,1)S(1)} %get-tuple-element.23), channel_id=1, source_target_pairs={{0,12},{4,8},{8,4},{12,0},{16,28},{20,24},{24,20},{28,16},{1,13},{... | collective-permute-start | bytes 393224 | tf_op jit(solution)/shard_map/ppermute | solution.py:184
  16.5 3.5 %copy-start.1 = (bf16[256,256]{1,0:T(8,128)(2,1)S(1)}, bf16[256,256]{1,0:T(8,128)(2,1)}, u32[]{:S(2)}) copy-start(bf16[256,256]{1,0:T(8,128)(2,1)} %constant.37.clone.refs_6_.refs_5_.matrix_ref) | copy-start | bytes 393220
  16.5 3.5 %copy-start.4 = (s32[1,1024]{1,0:T(1,128)S(1)}, s32[1,1024]{1,0:T(1,128)}, u32[]{:S(2)}) copy-start(s32[1,1024]{1,0:T(1,128)} %sign_ref.1) | copy-start | bytes 12292
  20.8 7.3 %collective-permute-start.4 = (s16[64,1024]{1,0:T(8,128)(2,1)S(1)}, s16[64,1024]{1,0:T(8,128)(2,1)S(1)}, u32[]{:S(2)}, u32[]{:S(2)}) collective-permute-start(s16[64,1024]{1,0:T(8,128)(2,1)S(1)} %proxy_blocks.1), channel_id=1, source_target_pairs={{0,16},{4,20},{8,24},{12,28},{16,0},{20,4},{24,8},{28,12},{1,17},{... | collective-permute-start | bytes 393224 | tf_op jit(solution)/shard_map/ppermute | solution.py:184
  28.8 9.6 %all-to-all-start.1 = ((f32[32,1,128]{2,1,0:T(1,128)}), f32[32,1,128]{2,1,0:T(1,128)S(1)}, u32[]{:S(2)}, u32[]{:S(2)}) async-start(f32[32,1,128]{2,1,0:T(1,128)} %get-tuple-element.20), calls=%async_computation.1 | async-start | bytes 32768 | tf_op jit(solution)/shard_map/all_to_all | solution.py:319
  31.3 7.1 %copy-start.2 = (bf16[1,64,1024]{2,1,0:T(8,128)(2,1)S(1)}, bf16[1,64,1024]{2,1,0:T(8,128)(2,1)}, u32[]{:S(2)}) copy-start(bf16[1,64,1024]{2,1,0:T(8,128)(2,1)} %param.7) | copy-start | bytes 393220
  31.3 7.1 %copy-start.3 = (bf16[1,64,1024]{2,1,0:T(8,128)(2,1)S(1)}, bf16[1,64,1024]{2,1,0:T(8,128)(2,1)}, u32[]{:S(2)}) copy-start(bf16[1,64,1024]{2,1,0:T(8,128)(2,1)} %param.8) | copy-start | bytes 393220
  38.6 6.9 %collective-permute-start.10 = (bf16[64,1024]{1,0:T(8,128)(2,1)S(1)}, bf16[64,1024]{1,0:T(8,128)(2,1)S(1)}, u32[]{:S(2)}, u32[]{:S(2)}) collective-permute-start(bf16[64,1024]{1,0:T(8,128)(2,1)S(1)} %new_weights.1.refs_0_), channel_id=1, source_target_pairs={{0,8},{4,12},{8,0},{12,4},{16,24},{20,28},{24,16},{28,20},{1,9},{5... | collective-permute-start | bytes 393224 | tf_op jit(solution)/shard_map/ppermute | solution.py:184
  39.2 8.6 %collective-permute-start.5 = (bf16[64,1024]{1,0:T(8,128)(2,1)S(1)}, bf16[64,1024]{1,0:T(8,128)(2,1)S(1)}, u32[]{:S(2)}, u32[]{:S(2)}) collective-permute-start(bf16[64,1024]{1,0:T(8,128)(2,1)S(1)} %new_weights.1.refs_0_), channel_id=1, source_target_pairs={{0,16},{4,20},{8,24},{12,28},{16,0},{20,4},{24,8},{28,12},{1,17},{... | collective-permute-start | bytes 393224 | tf_op jit(solution)/shard_map/ppermute | solution.py:184
  39.8 12.4 %collective-permute-start.9 = (bf16[64,1024]{1,0:T(8,128)(2,1)S(1)}, bf16[64,1024]{1,0:T(8,128)(2,1)S(1)}, u32[]{:S(2)}, u32[]{:S(2)}) collective-permute-start(bf16[64,1024]{1,0:T(8,128)(2,1)S(1)} %new_weights.1.refs_0_), channel_id=1, source_target_pairs={{0,4},{4,0},{8,12},{12,8},{16,20},{20,16},{24,28},{28,24},{1,5},{5... | collective-permute-start | bytes 393224 | tf_op jit(solution)/shard_map/ppermute | solution.py:184
  45.5 6.9 %collective-permute-start.11 = (bf16[64,1024]{1,0:T(8,128)(2,1)S(1)}, bf16[64,1024]{1,0:T(8,128)(2,1)S(1)}, u32[]{:S(2)}, u32[]{:S(2)}) collective-permute-start(bf16[64,1024]{1,0:T(8,128)(2,1)S(1)} %collective-permute-done.10.refs_2_), channel_id=1, source_target_pairs={{0,4},{4,0},{8,12},{12,8},{16,20},{20,16},{24,28},{28,24},{1,5},{5... | collective-permute-start | bytes 393224 | tf_op jit(solution)/shard_map/ppermute | solution.py:184
  47.8 6.0 %collective-permute-start.8 = (bf16[64,1024]{1,0:T(8,128)(2,1)S(1)}, bf16[64,1024]{1,0:T(8,128)(2,1)S(1)}, u32[]{:S(2)}, u32[]{:S(2)}) collective-permute-start(bf16[64,1024]{1,0:T(8,128)(2,1)S(1)} %collective-permute-done.5.refs_4_), channel_id=1, source_target_pairs={{0,12},{4,8},{8,4},{12,0},{16,28},{20,24},{24,20},{28,16},{1,13},{... | collective-permute-start | bytes 393224 | tf_op jit(solution)/shard_map/ppermute | solution.py:184
  47.8 6.4 %collective-permute-start.7 = (bf16[64,1024]{1,0:T(8,128)(2,1)S(1)}, bf16[64,1024]{1,0:T(8,128)(2,1)S(1)}, u32[]{:S(2)}, u32[]{:S(2)}) collective-permute-start(bf16[64,1024]{1,0:T(8,128)(2,1)S(1)} %collective-permute-done.5.refs_4_), channel_id=1, source_target_pairs={{0,8},{4,12},{8,0},{12,4},{16,24},{20,28},{24,16},{28,20},{1,9},{5... | collective-permute-start | bytes 393224 | tf_op jit(solution)/shard_map/ppermute | solution.py:184
  49.9 5.6 %collective-permute-start.6 = (bf16[64,1024]{1,0:T(8,128)(2,1)S(1)}, bf16[64,1024]{1,0:T(8,128)(2,1)S(1)}, u32[]{:S(2)}, u32[]{:S(2)}) collective-permute-start(bf16[64,1024]{1,0:T(8,128)(2,1)S(1)} %collective-permute-done.5.refs_4_), channel_id=1, source_target_pairs={{0,4},{4,0},{8,12},{12,8},{16,20},{20,16},{24,28},{28,24},{1,5},{5... | collective-permute-start | bytes 393224 | tf_op jit(solution)/shard_map/ppermute | solution.py:184

commit v20 on v19

--- a/solution.py
+++ b/solution.py
@@ -232,7 +232,10 @@
         if own[m] is None:
             own[m] = swap(own[m - m % x_count], m % x_count)
     own = [(m, 0, piece) for m, piece in own.items()]
-    spread = [(near + m, 0, swap(far, m)) for m in range(1, near)]
+    order = [m for m in range(1, near) if m % x_count and m > x_count]
+    order += [m for m in range(1, near) if m < x_count]
+    order += [m for m in range(1, near) if m % x_count == 0]
+    spread = [(near + m, 0, swap(far, m)) for m in order]
     out = place_pieces(own + [(near, 0, far)], owned, replicas, None, "place_own")
     out = place_pieces(spread, owned, replicas, out, "place_far")
     return out.reshape(1, replicas * owned, width)

time: 56.5 us -> 56.8 us (level)
  transfers between devices with their start and end apart: 14 -> 14, of which waited for: 9 -> 7; matrix products, arithmetic and copies ran while one was open for 0% -> 0% of each run, Pallas kernels for 7% -> 7%
where the time goes in v20:
time: 56.8 us; the launch traced here: 56.6 us
  waiting for transfers between devices  26.1 us (46%)
  starting transfers between devices  22.7 us (40%)
  Pallas kernels  5.77 us (10%)
  local copies, waits for them, and re-layouts  1.21 us (2%)
  between operations  0.81 us (1%)
    ppermute x12, waiting for transfers between devices, swap(): return lax.ppermute(value, 'dp', [(i, i ^ mask) for i in range(size)])  16 us
    ppermute x12, starting transfers between devices, swap(): return lax.ppermute(value, 'dp', [(i, i ^ mask) for i in range(size)])  14 us
    all_to_all x1, waiting for transfers between devices, on_device(): lax.all_to_all(squares, ('dp', 'expert'), split_axis=0, concat_axis=0, ti...  6.72 us
    all_to_all x1, starting transfers between devices, on_device(): lax.all_to_all(sums.reshape(replicas, 1, 2 * owned), 'dp', split_axis=0,...  6.18 us
    all_to_all x1, waiting for transfers between devices, on_device(): lax.all_to_all(sums.reshape(replicas, 1, 2 * owned), 'dp', split_axis=0,...  3.44 us
    all_to_all x1, starting transfers between devices, on_device(): lax.all_to_all(squares, ('dp', 'expert'), split_axis=0, concat_axis=0, ti...  2.54 us
    pallas_call x2, Pallas kernels, place_pieces(): pl.pallas_call(functools.partial(place_kernel, places, owned), in_specs=s...  1.64 us
    reshape x2, local copies, waits for them, and re-layouts, pair_of(): lax.dynamic_slice_in_dim(source, index % near, 1, 1)  1.17 us
  transfers between devices with their start and end apart: 14, of which 7 were waited for; matrix products, arithmetic and copies ran while one was open for 0% of the time, Pallas kernels for 7%

profile of v20, /device:TPU:0, one launch (start us, length us, event | category | flops | bytes accessed | tf_op | source)
XLA Modules:
  0.0 56.6 jit_solution(6729275612357387962)
XLA Ops:
  0.7 1.2 %dynamic-slice_bitcast_fusion.1 = (bf16[2,64,1024]{2,1,0:T(8,128)(2,1)S(1)}, bf16[2,64,1024]{2,1,0:T(8,128)(2,1)S(1)}) fusion(bf16[2,4,64,1024]{3,2,1,0:T(8,128)(2,1)} %bitcast.24, s32[]{:T(128)S(6)} %select_n.33, s32[]{:T(128)S(6)} %select_n.31), kind=kLoop, calls=%fused_computation.1 | loop fusion | bytes 1048584 | tf_op jit(solution)/shard_map/reshape | solution.py:258
  1.8 3.1 %collective-permute-start.1 = (bf16[2,64,1024]{2,1,0:T(8,128)(2,1)S(1)}, bf16[2,64,1024]{2,1,0:T(8,128)(2,1)S(1)}, u32[]{:S(2)}, u32[]{:S(2)}) collective-permute-start(bf16[2,64,1024]{2,1,0:T(8,128)(2,1)S(1)} %get-tuple-element.24), channel_id=1, source_target_pairs={{0,8},{4,12},{8,0},{12,4},{16,24},{20,28},{24,16},{28,20},{1,9},{5... | collective-permute-start | bytes 786440 | tf_op jit(solution)/shard_map/ppermute | solution.py:184
  4.9 1.5 %collective-permute-start = (bf16[2,64,1024]{2,1,0:T(8,128)(2,1)S(1)}, bf16[2,64,1024]{2,1,0:T(8,128)(2,1)S(1)}, u32[]{:S(2)}, u32[]{:S(2)}) collective-permute-start(bf16[2,64,1024]{2,1,0:T(8,128)(2,1)S(1)} %get-tuple-element.25), channel_id=1, source_target_pairs={{0,4},{4,0},{8,12},{12,8},{16,20},{20,16},{24,28},{28,24},{1,5},{5... | collective-permute-start | bytes 786440 | tf_op jit(solution)/shard_map/ppermute | solution.py:184
  6.4 0.9 %sum_squares.1 = f32[2,4,1,128]{3,2,1,0:T(1,128)} custom-call(bf16[2,4,64,1024]{3,2,1,0:T(8,128)(2,1)S(1)} %bitcast.25), custom_call_target="tpu_custom_call" | custom-call | tf_op jit(solution)/shard_map/sum_squares/pallas_call | solution.py:268
  7.4 6.2 %all-to-all-start = ((f32[8,1,128]{2,1,0:T(1,128)}), f32[8,1,128]{2,1,0:T(1,128)S(1)}, u32[]{:S(2)}, u32[]{:S(2)}) async-start(f32[8,1,128]{2,1,0:T(1,128)} %bitcast.8), calls=%async_computation | async-start | bytes 8192 | tf_op jit(solution)/shard_map/all_to_all | solution.py:276
  13.6 2.9 %collective-permute-start.2 = (bf16[64,1024]{1,0:T(8,128)(2,1)S(1)}, bf16[64,1024]{1,0:T(8,128)(2,1)S(1)}, u32[]{:S(2)}, u32[]{:S(2)}) collective-permute-start(bf16[64,1024]{1,0:T(8,128)(2,1)S(1)} %get-tuple-element.23), channel_id=1, source_target_pairs={{0,12},{4,8},{8,4},{12,0},{16,28},{20,24},{24,20},{28,16},{1,13},{... | collective-permute-start | bytes 393224 | tf_op jit(solution)/shard_map/ppermute | solution.py:184
  16.6 3.4 %all-to-all-done = f32[8,1,128]{2,1,0:T(1,128)S(1)} async-done(((f32[8,1,128]{2,1,0:T(1,128)}), f32[8,1,128]{2,1,0:T(1,128)S(1)}, u32[]{:S(2)}, u32[]{:S(2)}) %all-to-all-start) | async-done | bytes 4128 | tf_op jit(solution)/shard_map/all_to_all | solution.py:276
  20.8 0.6 %collective-permute-start.4 = (s16[64,1024]{1,0:T(8,128)(2,1)S(1)}, s16[64,1024]{1,0:T(8,128)(2,1)S(1)}, u32[]{:S(2)}, u32[]{:S(2)}) collective-permute-start(s16[64,1024]{1,0:T(8,128)(2,1)S(1)} %proxy_blocks.1), channel_id=1, source_target_pairs={{0,16},{4,20},{8,24},{12,28},{16,0},{20,4},{24,8},{28,12},{1,17},{... | collective-permute-start | bytes 393224 | tf_op jit(solution)/shard_map/ppermute | solution.py:184
  21.4 0.6 owner_blocks.1
  22.0 6.1 %collective-permute-done.4.far_ref = s16[64,1024]{1,0:T(8,128)(2,1)S(1)} collective-permute-done((s16[64,1024]{1,0:T(8,128)(2,1)S(1)}, s16[64,1024]{1,0:T(8,128)(2,1)S(1)}, u32[]{:S(2)}, u32[]{:S(2)}) %collective-permute-start.4) | collective-permute-done | bytes 131104 | tf_op jit(solution)/shard_map/ppermute | solution.py:184
  28.1 0.7 %finish_blocks.1 = (f32[64,1024]{1,0:T(8,128)S(1)}, f32[32,1,128]{2,1,0:T(1,128)}) custom-call(f32[64,1024]{1,0:T(8,128)S(1)} %get-tuple-element.14.near_ref, s16[64,1024]{1,0:T(8,128)(2,1)S(1)} %collective-permute-done.4.far_ref, f32[64,128]{1,0:T(8,128)S(1)} %get-tuple-element.18.scale_ref, f32[64,128]{1,0:T(8,128)S(1)} %get-tuple-element.19.step_ref), custom_call_target="tpu_custom_call" | custom-call | tf_op jit(solution)/shard_map/finish_blocks/pallas_call | solution.py:306
  28.8 2.5 %all-to-all-start.1 = ((f32[32,1,128]{2,1,0:T(1,128)}), f32[32,1,128]{2,1,0:T(1,128)S(1)}, u32[]{:S(2)}, u32[]{:S(2)}) async-start(f32[32,1,128]{2,1,0:T(1,128)} %get-tuple-element.20), calls=%async_computation.1 | async-start | bytes 32768 | tf_op jit(solution)/shard_map/all_to_all | solution.py:322
  31.7 6.7 %all-to-all-done.1 = f32[32,1,128]{2,1,0:T(1,128)S(1)} async-done(((f32[32,1,128]{2,1,0:T(1,128)}), f32[32,1,128]{2,1,0:T(1,128)S(1)}, u32[]{:S(2)}, u32[]{:S(2)}) %all-to-all-start.1) | async-done | bytes 16416 | tf_op jit(solution)/shard_map/all_to_all | solution.py:322
  38.6 0.6 %collective-permute-start.10 = (bf16[64,1024]{1,0:T(8,128)(2,1)S(1)}, bf16[64,1024]{1,0:T(8,128)(2,1)S(1)}, u32[]{:S(2)}, u32[]{:S(2)}) collective-permute-start(bf16[64,1024]{1,0:T(8,128)(2,1)S(1)} %new_weights.1.refs_0_), channel_id=1, source_target_pairs={{0,8},{4,12},{8,0},{12,4},{16,24},{20,28},{24,16},{28,20},{1,9},{5... | collective-permute-start | bytes 393224 | tf_op jit(solution)/shard_map/ppermute | solution.py:184
  39.2 0.6 collective-permute-start.5
  40.3 5.2 %collective-permute-done.10.refs_2_ = bf16[64,1024]{1,0:T(8,128)(2,1)S(1)} collective-permute-done((bf16[64,1024]{1,0:T(8,128)(2,1)S(1)}, bf16[64,1024]{1,0:T(8,128)(2,1)S(1)}, u32[]{:S(2)}, u32[]{:S(2)}) %collective-permute-start.10) | collective-permute-done | bytes 131104 | tf_op jit(solution)/shard_map/ppermute | solution.py:184
  46.1 1.8 %collective-permute-done.5.refs_4_ = bf16[64,1024]{1,0:T(8,128)(2,1)S(1)} collective-permute-done((bf16[64,1024]{1,0:T(8,128)(2,1)S(1)}, bf16[64,1024]{1,0:T(8,128)(2,1)S(1)}, u32[]{:S(2)}, u32[]{:S(2)}) %collective-permute-start.5) | collective-permute-done | bytes 131104 | tf_op jit(solution)/shard_map/ppermute | solution.py:184
  47.9 0.5 collective-permute-start.7
  48.4 2.9 %collective-permute-start.6 = (bf16[64,1024]{1,0:T(8,128)(2,1)S(1)}, bf16[64,1024]{1,0:T(8,128)(2,1)S(1)}, u32[]{:S(2)}, u32[]{:S(2)}) collective-permute-start(bf16[64,1024]{1,0:T(8,128)(2,1)S(1)} %collective-permute-done.5.refs_4_), channel_id=1, source_target_pairs={{0,12},{4,8},{8,4},{12,0},{16,28},{20,24},{24,20},{28,16},{1,13},{... | collective-permute-start | bytes 393224 | tf_op jit(solution)/shard_map/ppermute | solution.py:184
  51.4 0.8 %update_grad.1 = f32[64,1024]{1,0:T(8,128)} custom-call(f32[32,128]{1,0:T(8,128)S(1)} %bitcast.29, f32[64,1024]{1,0:T(8,128)S(1)} %rotate_back.1.unrot_ref), custom_call_target="tpu_custom_call" | custom-call | tf_op jit(solution)/shard_map/update_grad/pallas_call | solution.py:331
  52.2 0.8 %collective-permute-done.11.refs_3_ = bf16[64,1024]{1,0:T(8,128)(2,1)S(1)} collective-permute-done((bf16[64,1024]{1,0:T(8,128)(2,1)S(1)}, bf16[64,1024]{1,0:T(8,128)(2,1)S(1)}, u32[]{:S(2)}, u32[]{:S(2)}) %collective-permute-start.11) | collective-permute-done | bytes 131104 | tf_op jit(solution)/shard_map/ppermute | solution.py:184
  53.0 0.9 %place_own.1.refs_3_ = bf16[512,1024]{1,0:T(8,128)(2,1)} custom-call(bf16[64,1024]{1,0:T(8,128)(2,1)S(1)} %new_weights.1.refs_0_, bf16[64,1024]{1,0:T(8,128)(2,1)S(1)} %collective-permute-done.9.refs_1_, bf16[64,1024]{1,0:T(8,128)(2,1)S(1)} %collective-permute-done.10.refs_2_, bf16[64,1024]{1,0:T(8,128)(2,1)S(1)} %collective-permute-done.11.refs_3_, ...), custom_call_target="tpu_custom_call" | custom-call | tf_op jit(solution)/shard_map/place_own/pallas_call | solution.py:211
  53.9 1.9 %collective-permute-done.7.refs_1_ = bf16[64,1024]{1,0:T(8,128)(2,1)S(1)} collective-permute-done((bf16[64,1024]{1,0:T(8,128)(2,1)S(1)}, bf16[64,1024]{1,0:T(8,128)(2,1)S(1)}, u32[]{:S(2)}, u32[]{:S(2)}) %collective-permute-start.7) | collective-permute-done | bytes 131104 | tf_op jit(solution)/shard_map/ppermute | solution.py:184
  55.8 0.8 %place_far.1 = bf16[512,1024]{1,0:T(8,128)(2,1)} custom-call(bf16[64,1024]{1,0:T(8,128)(2,1)S(1)} %collective-permute-done.6.refs_0_, bf16[64,1024]{1,0:T(8,128)(2,1)S(1)} %collective-permute-done.7.refs_1_, bf16[64,1024]{1,0:T(8,128)(2,1)S(1)} %collective-permute-done.8.refs_2_, bf16[512,1024]{1,0:T(8,128)(2,1)} %place_own.1.refs_3_), custom_call_target="tpu_custom_call", output_to_operand_aliasing={{}: (3, {})} | custom-call | tf_op jit(solution)/shard_map/place_far/pallas_call | solution.py:211
  (27 shorter events, 2.4 us)
Async XLA Ops:
  0.6 5.8 %copy-start = (bf16[1,1,512,1024]{3,2,1,0:T(8,128)(2,1)S(1)}, bf16[1,1,512,1024]{3,2,1,0:T(8,128)(2,1)}, u32[]{:S(2)}) copy-start(bf16[1,1,512,1024]{3,2,1,0:T(8,128)(2,1)} %param.5) | copy-start | bytes 3145732
  1.8 18.2 %collective-permute-start.1 = (bf16[2,64,1024]{2,1,0:T(8,128)(2,1)S(1)}, bf16[2,64,1024]{2,1,0:T(8,128)(2,1)S(1)}, u32[]{:S(2)}, u32[]{:S(2)}) collective-permute-start(bf16[2,64,1024]{2,1,0:T(8,128)(2,1)S(1)} %get-tuple-element.24), channel_id=1, source_target_pairs={{0,8},{4,12},{8,0},{12,4},{16,24},{20,28},{24,16},{28,20},{1,9},{5... | collective-permute-start | bytes 786440 | tf_op jit(solution)/shard_map/ppermute | solution.py:184
  4.9 15.1 %collective-permute-start = (bf16[2,64,1024]{2,1,0:T(8,128)(2,1)S(1)}, bf16[2,64,1024]{2,1,0:T(8,128)(2,1)S(1)}, u32[]{:S(2)}, u32[]{:S(2)}) collective-permute-start(bf16[2,64,1024]{2,1,0:T(8,128)(2,1)S(1)} %get-tuple-element.25), channel_id=1, source_target_pairs={{0,4},{4,0},{8,12},{12,8},{16,20},{20,16},{24,28},{28,24},{1,5},{5... | collective-permute-start | bytes 786440 | tf_op jit(solution)/shard_map/ppermute | solution.py:184
  7.3 13.1 %collective-permute-start.3 = (bf16[64,1024]{1,0:T(8,128)(2,1)S(1)}, bf16[64,1024]{1,0:T(8,128)(2,1)S(1)}, u32[]{:S(2)}, u32[]{:S(2)}) collective-permute-start(bf16[64,1024]{1,0:T(8,128)(2,1)S(1)} %get-tuple-element.22), channel_id=1, source_target_pairs={{0,12},{4,8},{8,4},{12,0},{16,28},{20,24},{24,20},{28,16},{1,13},{... | collective-permute-start | bytes 393224 | tf_op jit(solution)/shard_map/ppermute | solution.py:184
  7.4 12.6 %all-to-all-start = ((f32[8,1,128]{2,1,0:T(1,128)}), f32[8,1,128]{2,1,0:T(1,128)S(1)}, u32[]{:S(2)}, u32[]{:S(2)}) async-start(f32[8,1,128]{2,1,0:T(1,128)} %bitcast.8), calls=%async_computation | async-start | bytes 8192 | tf_op jit(solution)/shard_map/all_to_all | solution.py:276
  13.6 7.8 %collective-permute-start.2 = (bf16[64,1024]{1,0:T(8,128)(2,1)S(1)}, bf16[64,1024]{1,0:T(8,128)(2,1)S(1)}, u32[]{:S(2)}, u32[]{:S(2)}) collective-permute-start(bf16[64,1024]{1,0:T(8,128)(2,1)S(1)} %get-tuple-element.23), channel_id=1, source_target_pairs={{0,12},{4,8},{8,4},{12,0},{16,28},{20,24},{24,20},{28,16},{1,13},{... | collective-permute-start | bytes 393224 | tf_op jit(solution)/shard_map/ppermute | solution.py:184
  16.5 3.5 %copy-start.1 = (bf16[256,256]{1,0:T(8,128)(2,1)S(1)}, bf16[256,256]{1,0:T(8,128)(2,1)}, u32[]{:S(2)}) copy-start(bf16[256,256]{1,0:T(8,128)(2,1)} %constant.37.clone.refs_6_.refs_5_.matrix_ref) | copy-start | bytes 393220
  16.5 3.5 %copy-start.4 = (s32[1,1024]{1,0:T(1,128)S(1)}, s32[1,1024]{1,0:T(1,128)}, u32[]{:S(2)}) copy-start(s32[1,1024]{1,0:T(1,128)} %sign_ref.1) | copy-start | bytes 12292
  20.8 7.3 %collective-permute-start.4 = (s16[64,1024]{1,0:T(8,128)(2,1)S(1)}, s16[64,1024]{1,0:T(8,128)(2,1)S(1)}, u32[]{:S(2)}, u32[]{:S(2)}) collective-permute-start(s16[64,1024]{1,0:T(8,128)(2,1)S(1)} %proxy_blocks.1), channel_id=1, source_target_pairs={{0,16},{4,20},{8,24},{12,28},{16,0},{20,4},{24,8},{28,12},{1,17},{... | collective-permute-start | bytes 393224 | tf_op jit(solution)/shard_map/ppermute | solution.py:184
  28.8 9.6 %all-to-all-start.1 = ((f32[32,1,128]{2,1,0:T(1,128)}), f32[32,1,128]{2,1,0:T(1,128)S(1)}, u32[]{:S(2)}, u32[]{:S(2)}) async-start(f32[32,1,128]{2,1,0:T(1,128)} %get-tuple-element.20), calls=%async_computation.1 | async-start | bytes 32768 | tf_op jit(solution)/shard_map/all_to_all | solution.py:322
  31.3 7.1 %copy-start.2 = (bf16[1,64,1024]{2,1,0:T(8,128)(2,1)S(1)}, bf16[1,64,1024]{2,1,0:T(8,128)(2,1)}, u32[]{:S(2)}) copy-start(bf16[1,64,1024]{2,1,0:T(8,128)(2,1)} %param.7) | copy-start | bytes 393220
  31.3 7.1 %copy-start.3 = (bf16[1,64,1024]{2,1,0:T(8,128)(2,1)S(1)}, bf16[1,64,1024]{2,1,0:T(8,128)(2,1)}, u32[]{:S(2)}) copy-start(bf16[1,64,1024]{2,1,0:T(8,128)(2,1)} %param.8) | copy-start | bytes 393220
  38.6 6.9 %collective-permute-start.10 = (bf16[64,1024]{1,0:T(8,128)(2,1)S(1)}, bf16[64,1024]{1,0:T(8,128)(2,1)S(1)}, u32[]{:S(2)}, u32[]{:S(2)}) collective-permute-start(bf16[64,1024]{1,0:T(8,128)(2,1)S(1)} %new_weights.1.refs_0_), channel_id=1, source_target_pairs={{0,8},{4,12},{8,0},{12,4},{16,24},{20,28},{24,16},{28,20},{1,9},{5... | collective-permute-start | bytes 393224 | tf_op jit(solution)/shard_map/ppermute | solution.py:184
  39.2 8.7 %collective-permute-start.5 = (bf16[64,1024]{1,0:T(8,128)(2,1)S(1)}, bf16[64,1024]{1,0:T(8,128)(2,1)S(1)}, u32[]{:S(2)}, u32[]{:S(2)}) collective-permute-start(bf16[64,1024]{1,0:T(8,128)(2,1)S(1)} %new_weights.1.refs_0_), channel_id=1, source_target_pairs={{0,16},{4,20},{8,24},{12,28},{16,0},{20,4},{24,8},{28,12},{1,17},{... | collective-permute-start | bytes 393224 | tf_op jit(solution)/shard_map/ppermute | solution.py:184
  39.8 12.4 %collective-permute-start.9 = (bf16[64,1024]{1,0:T(8,128)(2,1)S(1)}, bf16[64,1024]{1,0:T(8,128)(2,1)S(1)}, u32[]{:S(2)}, u32[]{:S(2)}) collective-permute-start(bf16[64,1024]{1,0:T(8,128)(2,1)S(1)} %new_weights.1.refs_0_), channel_id=1, source_target_pairs={{0,4},{4,0},{8,12},{12,8},{16,20},{20,16},{24,28},{28,24},{1,5},{5... | collective-permute-start | bytes 393224 | tf_op jit(solution)/shard_map/ppermute | solution.py:184
  45.5 7.5 %collective-permute-start.11 = (bf16[64,1024]{1,0:T(8,128)(2,1)S(1)}, bf16[64,1024]{1,0:T(8,128)(2,1)S(1)}, u32[]{:S(2)}, u32[]{:S(2)}) collective-permute-start(bf16[64,1024]{1,0:T(8,128)(2,1)S(1)} %collective-permute-done.10.refs_2_), channel_id=1, source_target_pairs={{0,4},{4,0},{8,12},{12,8},{16,20},{20,16},{24,28},{28,24},{1,5},{5... | collective-permute-start | bytes 393224 | tf_op jit(solution)/shard_map/ppermute | solution.py:184
  47.9 6.0 %collective-permute-start.8 = (bf16[64,1024]{1,0:T(8,128)(2,1)S(1)}, bf16[64,1024]{1,0:T(8,128)(2,1)S(1)}, u32[]{:S(2)}, u32[]{:S(2)}) collective-permute-start(bf16[64,1024]{1,0:T(8,128)(2,1)S(1)} %collective-permute-done.5.refs_4_), channel_id=1, source_target_pairs={{0,8},{4,12},{8,0},{12,4},{16,24},{20,28},{24,16},{28,20},{1,9},{5... | collective-permute-start | bytes 393224 | tf_op jit(solution)/shard_map/ppermute | solution.py:184
  47.9 7.9 %collective-permute-start.7 = (bf16[64,1024]{1,0:T(8,128)(2,1)S(1)}, bf16[64,1024]{1,0:T(8,128)(2,1)S(1)}, u32[]{:S(2)}, u32[]{:S(2)}) collective-permute-start(bf16[64,1024]{1,0:T(8,128)(2,1)S(1)} %collective-permute-done.5.refs_4_), channel_id=1, source_target_pairs={{0,4},{4,0},{8,12},{12,8},{16,20},{20,16},{24,28},{28,24},{1,5},{5... | collective-permute-start | bytes 393224 | tf_op jit(solution)/shard_map/ppermute | solution.py:184
  48.4 7.4 %collective-permute-start.6 = (bf16[64,1024]{1,0:T(8,128)(2,1)S(1)}, bf16[64,1024]{1,0:T(8,128)(2,1)S(1)}, u32[]{:S(2)}, u32[]{:S(2)}) collective-permute-start(bf16[64,1024]{1,0:T(8,128)(2,1)S(1)} %collective-permute-done.5.refs_4_), channel_id=1, source_target_pairs={{0,12},{4,8},{8,4},{12,0},{16,28},{20,24},{24,20},{28,16},{1,13},{... | collective-permute-start | bytes 393224 | tf_op jit(solution)/shard_map/ppermute | solution.py:184

commit v21 on v19

--- a/solution.py
+++ b/solution.py
@@ -283,6 +283,9 @@
         in_specs=[array] * (len(pairs) + 3),
         out_shape=(whole, column, column),
         compiler_params=params,
+        cost_estimate=pl.CostEstimate(
+            flops=20000000000, bytes_accessed=4 * blocks * width, transcendentals=0
+        ),
         name="proxy_pairs",
     )(*pairs, sums, signs, matrix)
     sent = pl.pallas_call(

time: 56.5 us -> 57.2 us (1.012)
  starting transfers between devices: 22.7 us -> 25.7 us
  waiting for transfers between devices: 25.8 us -> 23.5 us
    all_to_all x1, starting transfers between devices: 2.54 us -> 5.36 us  [on_device(): lax.all_to_all(squares, ('dp', 'expert'), split_axis=0, concat_axis=0, ti...]
    ppermute x12, starting transfers between devices: 14 us -> 16.5 us  [swap(): return lax.ppermute(value, 'dp', [(i, i ^ mask) for i in range(size)])]
    all_to_all x1, starting transfers between devices: 6.18 us -> 3.87 us  [on_device(): lax.all_to_all(sums.reshape(replicas, 1, 2 * owned), 'dp', split_axis=0,...]
    ppermute x12, waiting for transfers between devices: 15.6 us -> 13.5 us  [swap(): return lax.ppermute(value, 'dp', [(i, i ^ mask) for i in range(size)])]
  transfers between devices with their start and end apart: 14 -> 14, of which waited for: 9 -> 10; matrix products, arithmetic and copies ran while one was open for 0% -> 0% of each run, Pallas kernels for 7% -> 7%
where the time goes in v21:
time: 57.2 us; the launch traced here: 57 us
  starting transfers between devices  25.7 us (45%)
  waiting for transfers between devices  23.5 us (41%)
  Pallas kernels  5.77 us (10%)
  local copies, waits for them, and re-layouts  1.21 us (2%)
  between operations  0.79 us (1%)
    ppermute x12, starting transfers between devices, swap(): return lax.ppermute(value, 'dp', [(i, i ^ mask) for i in range(size)])  16.5 us
    ppermute x12, waiting for transfers between devices, swap(): return lax.ppermute(value, 'dp', [(i, i ^ mask) for i in range(size)])  13.5 us
    all_to_all x1, waiting for transfers between devices, on_device(): lax.all_to_all(squares, ('dp', 'expert'), split_axis=0, concat_axis=0, ti...  6.72 us
    all_to_all x1, starting transfers between devices, on_device(): lax.all_to_all(squares, ('dp', 'expert'), split_axis=0, concat_axis=0, ti...  5.36 us
    all_to_all x1, starting transfers between devices, on_device(): lax.all_to_all(sums.reshape(replicas, 1, 2 * owned), 'dp', split_axis=0,...  3.87 us
    all_to_all x1, waiting for transfers between devices, on_device(): lax.all_to_all(sums.reshape(replicas, 1, 2 * owned), 'dp', split_axis=0,...  3.28 us
    pallas_call x2, Pallas kernels, place_pieces(): pl.pallas_call(functools.partial(place_kernel, places, owned), in_specs=s...  1.63 us
    reshape x2, local copies, waits for them, and re-layouts, pair_of(): lax.dynamic_slice_in_dim(source, index % near, 1, 1)  1.17 us
  transfers between devices with their start and end apart: 14, of which 10 were waited for; matrix products, arithmetic and copies ran while one was open for 0% of the time, Pallas kernels for 7%

profile of v21, /device:TPU:0, one launch (start us, length us, event | category | flops | bytes accessed | tf_op | source)
XLA Modules:
  0.0 57.0 jit_solution(1941397311725833024)
XLA Ops:
  0.7 1.2 %dynamic-slice_bitcast_fusion.1 = (bf16[2,64,1024]{2,1,0:T(8,128)(2,1)S(1)}, bf16[2,64,1024]{2,1,0:T(8,128)(2,1)S(1)}) fusion(bf16[2,4,64,1024]{3,2,1,0:T(8,128)(2,1)} %bitcast.24, s32[]{:T(128)S(6)} %select_n.33, s32[]{:T(128)S(6)} %select_n.31), kind=kLoop, calls=%fused_computation.1 | loop fusion | bytes 1048584 | tf_op jit(solution)/shard_map/reshape | solution.py:255
  1.8 3.1 %collective-permute-start.1 = (bf16[2,64,1024]{2,1,0:T(8,128)(2,1)S(1)}, bf16[2,64,1024]{2,1,0:T(8,128)(2,1)S(1)}, u32[]{:S(2)}, u32[]{:S(2)}) collective-permute-start(bf16[2,64,1024]{2,1,0:T(8,128)(2,1)S(1)} %get-tuple-element.24), channel_id=1, source_target_pairs={{0,8},{4,12},{8,0},{12,4},{16,24},{20,28},{24,16},{28,20},{1,9},{5... | collective-permute-start | bytes 786440 | tf_op jit(solution)/shard_map/ppermute | solution.py:184
  4.9 1.5 %collective-permute-start = (bf16[2,64,1024]{2,1,0:T(8,128)(2,1)S(1)}, bf16[2,64,1024]{2,1,0:T(8,128)(2,1)S(1)}, u32[]{:S(2)}, u32[]{:S(2)}) collective-permute-start(bf16[2,64,1024]{2,1,0:T(8,128)(2,1)S(1)} %get-tuple-element.25), channel_id=1, source_target_pairs={{0,4},{4,0},{8,12},{12,8},{16,20},{20,16},{24,28},{28,24},{1,5},{5... | collective-permute-start | bytes 786440 | tf_op jit(solution)/shard_map/ppermute | solution.py:184
  6.4 0.9 %sum_squares.1 = f32[2,4,1,128]{3,2,1,0:T(1,128)} custom-call(bf16[2,4,64,1024]{3,2,1,0:T(8,128)(2,1)S(1)} %bitcast.25), custom_call_target="tpu_custom_call" | custom-call | tf_op jit(solution)/shard_map/sum_squares/pallas_call | solution.py:265
  7.3 3.9 %all-to-all-start = ((f32[8,1,128]{2,1,0:T(1,128)}), f32[8,1,128]{2,1,0:T(1,128)S(1)}, u32[]{:S(2)}, u32[]{:S(2)}) async-start(f32[8,1,128]{2,1,0:T(1,128)} %bitcast.8), calls=%async_computation | async-start | bytes 8192 | tf_op jit(solution)/shard_map/all_to_all | solution.py:273
  11.2 3.0 %collective-permute-start.3 = (bf16[64,1024]{1,0:T(8,128)(2,1)S(1)}, bf16[64,1024]{1,0:T(8,128)(2,1)S(1)}, u32[]{:S(2)}, u32[]{:S(2)}) collective-permute-start(bf16[64,1024]{1,0:T(8,128)(2,1)S(1)} %get-tuple-element.22), channel_id=1, source_target_pairs={{0,12},{4,8},{8,4},{12,0},{16,28},{20,24},{24,20},{28,16},{1,13},{... | collective-permute-start | bytes 393224 | tf_op jit(solution)/shard_map/ppermute | solution.py:184
  14.3 3.3 %all-to-all-done = f32[8,1,128]{2,1,0:T(1,128)S(1)} async-done(((f32[8,1,128]{2,1,0:T(1,128)}), f32[8,1,128]{2,1,0:T(1,128)S(1)}, u32[]{:S(2)}, u32[]{:S(2)}) %all-to-all-start) | async-done | bytes 4128 | tf_op jit(solution)/shard_map/all_to_all | solution.py:273
  18.5 3.1 %collective-permute-start.4 = (s16[64,1024]{1,0:T(8,128)(2,1)S(1)}, s16[64,1024]{1,0:T(8,128)(2,1)S(1)}, u32[]{:S(2)}, u32[]{:S(2)}) collective-permute-start(s16[64,1024]{1,0:T(8,128)(2,1)S(1)} %proxy_blocks.1), channel_id=1, source_target_pairs={{0,16},{4,20},{8,24},{12,28},{16,0},{20,4},{24,8},{28,12},{1,17},{... | collective-permute-start | bytes 393224 | tf_op jit(solution)/shard_map/ppermute | solution.py:184
  21.6 0.6 owner_blocks.1
  22.2 3.8 %collective-permute-done.4.far_ref = s16[64,1024]{1,0:T(8,128)(2,1)S(1)} collective-permute-done((s16[64,1024]{1,0:T(8,128)(2,1)S(1)}, s16[64,1024]{1,0:T(8,128)(2,1)S(1)}, u32[]{:S(2)}, u32[]{:S(2)}) %collective-permute-start.4) | collective-permute-done | bytes 131104 | tf_op jit(solution)/shard_map/ppermute | solution.py:184
  26.0 0.7 %finish_blocks.1 = (f32[64,1024]{1,0:T(8,128)S(1)}, f32[32,1,128]{2,1,0:T(1,128)}) custom-call(f32[64,1024]{1,0:T(8,128)S(1)} %get-tuple-element.14.near_ref, s16[64,1024]{1,0:T(8,128)(2,1)S(1)} %collective-permute-done.4.far_ref, f32[64,128]{1,0:T(8,128)S(1)} %get-tuple-element.18.scale_ref, f32[64,128]{1,0:T(8,128)S(1)} %get-tuple-element.19.step_ref), custom_call_target="tpu_custom_call" | custom-call | tf_op jit(solution)/shard_map/finish_blocks/pallas_call | solution.py:306
  26.7 5.4 %all-to-all-start.1 = ((f32[32,1,128]{2,1,0:T(1,128)}), f32[32,1,128]{2,1,0:T(1,128)S(1)}, u32[]{:S(2)}, u32[]{:S(2)}) async-start(f32[32,1,128]{2,1,0:T(1,128)} %get-tuple-element.20), calls=%async_computation.1 | async-start | bytes 32768 | tf_op jit(solution)/shard_map/all_to_all | solution.py:322
  32.4 6.7 %all-to-all-done.1 = f32[32,1,128]{2,1,0:T(1,128)S(1)} async-done(((f32[32,1,128]{2,1,0:T(1,128)}), f32[32,1,128]{2,1,0:T(1,128)S(1)}, u32[]{:S(2)}, u32[]{:S(2)}) %all-to-all-start.1) | async-done | bytes 16416 | tf_op jit(solution)/shard_map/all_to_all | solution.py:322
  39.3 0.6 %collective-permute-start.10 = (bf16[64,1024]{1,0:T(8,128)(2,1)S(1)}, bf16[64,1024]{1,0:T(8,128)(2,1)S(1)}, u32[]{:S(2)}, u32[]{:S(2)}) collective-permute-start(bf16[64,1024]{1,0:T(8,128)(2,1)S(1)} %new_weights.1.refs_0_), channel_id=1, source_target_pairs={{0,8},{4,12},{8,0},{12,4},{16,24},{20,28},{24,16},{28,20},{1,9},{5... | collective-permute-start | bytes 393224 | tf_op jit(solution)/shard_map/ppermute | solution.py:184
  39.9 0.6 collective-permute-start.5
  41.0 5.2 %collective-permute-done.10.refs_2_ = bf16[64,1024]{1,0:T(8,128)(2,1)S(1)} collective-permute-done((bf16[64,1024]{1,0:T(8,128)(2,1)S(1)}, bf16[64,1024]{1,0:T(8,128)(2,1)S(1)}, u32[]{:S(2)}, u32[]{:S(2)}) %collective-permute-start.10) | collective-permute-done | bytes 131104 | tf_op jit(solution)/shard_map/ppermute | solution.py:184
  46.2 0.5 collective-permute-start.11
  46.8 1.8 %collective-permute-done.5.refs_4_ = bf16[64,1024]{1,0:T(8,128)(2,1)S(1)} collective-permute-done((bf16[64,1024]{1,0:T(8,128)(2,1)S(1)}, bf16[64,1024]{1,0:T(8,128)(2,1)S(1)}, u32[]{:S(2)}, u32[]{:S(2)}) %collective-permute-start.5) | collective-permute-done | bytes 131104 | tf_op jit(solution)/shard_map/ppermute | solution.py:184
  48.5 2.1 %collective-permute-start.7 = (bf16[64,1024]{1,0:T(8,128)(2,1)S(1)}, bf16[64,1024]{1,0:T(8,128)(2,1)S(1)}, u32[]{:S(2)}, u32[]{:S(2)}) collective-permute-start(bf16[64,1024]{1,0:T(8,128)(2,1)S(1)} %collective-permute-done.5.refs_4_), channel_id=1, source_target_pairs={{0,8},{4,12},{8,0},{12,4},{16,24},{20,28},{24,16},{28,20},{1,9},{5... | collective-permute-start | bytes 393224 | tf_op jit(solution)/shard_map/ppermute | solution.py:184
  50.6 1.4 %collective-permute-start.6 = (bf16[64,1024]{1,0:T(8,128)(2,1)S(1)}, bf16[64,1024]{1,0:T(8,128)(2,1)S(1)}, u32[]{:S(2)}, u32[]{:S(2)}) collective-permute-start(bf16[64,1024]{1,0:T(8,128)(2,1)S(1)} %collective-permute-done.5.refs_4_), channel_id=1, source_target_pairs={{0,4},{4,0},{8,12},{12,8},{16,20},{20,16},{24,28},{28,24},{1,5},{5... | collective-permute-start | bytes 393224 | tf_op jit(solution)/shard_map/ppermute | solution.py:184
  52.0 0.8 %update_grad.1 = f32[64,1024]{1,0:T(8,128)} custom-call(f32[32,128]{1,0:T(8,128)S(1)} %bitcast.29, f32[64,1024]{1,0:T(8,128)S(1)} %rotate_back.1.unrot_ref), custom_call_target="tpu_custom_call" | custom-call | tf_op jit(solution)/shard_map/update_grad/pallas_call | solution.py:331
  53.1 0.9 %place_own.1.refs_3_ = bf16[512,1024]{1,0:T(8,128)(2,1)} custom-call(bf16[64,1024]{1,0:T(8,128)(2,1)S(1)} %new_weights.1.refs_0_, bf16[64,1024]{1,0:T(8,128)(2,1)S(1)} %collective-permute-done.9.refs_1_, bf16[64,1024]{1,0:T(8,128)(2,1)S(1)} %collective-permute-done.10.refs_2_, bf16[64,1024]{1,0:T(8,128)(2,1)S(1)} %collective-permute-done.11.refs_3_, ...), custom_call_target="tpu_custom_call" | custom-call | tf_op jit(solution)/shard_map/place_own/pallas_call | solution.py:211
  55.0 1.2 %collective-permute-done.6.refs_0_ = bf16[64,1024]{1,0:T(8,128)(2,1)S(1)} collective-permute-done((bf16[64,1024]{1,0:T(8,128)(2,1)S(1)}, bf16[64,1024]{1,0:T(8,128)(2,1)S(1)}, u32[]{:S(2)}, u32[]{:S(2)}) %collective-permute-start.6) | collective-permute-done | bytes 131104 | tf_op jit(solution)/shard_map/ppermute | solution.py:184
  56.2 0.8 %place_far.1 = bf16[512,1024]{1,0:T(8,128)(2,1)} custom-call(bf16[64,1024]{1,0:T(8,128)(2,1)S(1)} %collective-permute-done.6.refs_0_, bf16[64,1024]{1,0:T(8,128)(2,1)S(1)} %collective-permute-done.7.refs_1_, bf16[64,1024]{1,0:T(8,128)(2,1)S(1)} %collective-permute-done.8.refs_2_, bf16[512,1024]{1,0:T(8,128)(2,1)} %place_own.1.refs_3_), custom_call_target="tpu_custom_call", output_to_operand_aliasing={{}: (3, {})} | custom-call | tf_op jit(solution)/shard_map/place_far/pallas_call | solution.py:211
  (27 shorter events, 3.4 us)
Async XLA Ops:
  0.6 5.8 %copy-start = (bf16[1,1,512,1024]{3,2,1,0:T(8,128)(2,1)S(1)}, bf16[1,1,512,1024]{3,2,1,0:T(8,128)(2,1)}, u32[]{:S(2)}) copy-start(bf16[1,1,512,1024]{3,2,1,0:T(8,128)(2,1)} %param.5) | copy-start | bytes 3145732
  1.8 15.7 %collective-permute-start.1 = (bf16[2,64,1024]{2,1,0:T(8,128)(2,1)S(1)}, bf16[2,64,1024]{2,1,0:T(8,128)(2,1)S(1)}, u32[]{:S(2)}, u32[]{:S(2)}) collective-permute-start(bf16[2,64,1024]{2,1,0:T(8,128)(2,1)S(1)} %get-tuple-element.24), channel_id=1, source_target_pairs={{0,8},{4,12},{8,0},{12,4},{16,24},{20,28},{24,16},{28,20},{1,9},{5... | collective-permute-start | bytes 786440 | tf_op jit(solution)/shard_map/ppermute | solution.py:184
  4.9 12.6 %collective-permute-start = (bf16[2,64,1024]{2,1,0:T(8,128)(2,1)S(1)}, bf16[2,64,1024]{2,1,0:T(8,128)(2,1)S(1)}, u32[]{:S(2)}, u32[]{:S(2)}) collective-permute-start(bf16[2,64,1024]{2,1,0:T(8,128)(2,1)S(1)} %get-tuple-element.25), channel_id=1, source_target_pairs={{0,4},{4,0},{8,12},{12,8},{16,20},{20,16},{24,28},{28,24},{1,5},{5... | collective-permute-start | bytes 786440 | tf_op jit(solution)/shard_map/ppermute | solution.py:184
  7.3 10.3 %all-to-all-start = ((f32[8,1,128]{2,1,0:T(1,128)}), f32[8,1,128]{2,1,0:T(1,128)S(1)}, u32[]{:S(2)}, u32[]{:S(2)}) async-start(f32[8,1,128]{2,1,0:T(1,128)} %bitcast.8), calls=%async_computation | async-start | bytes 8192 | tf_op jit(solution)/shard_map/all_to_all | solution.py:273
  11.2 7.1 %collective-permute-start.3 = (bf16[64,1024]{1,0:T(8,128)(2,1)S(1)}, bf16[64,1024]{1,0:T(8,128)(2,1)S(1)}, u32[]{:S(2)}, u32[]{:S(2)}) collective-permute-start(bf16[64,1024]{1,0:T(8,128)(2,1)S(1)} %get-tuple-element.22), channel_id=1, source_target_pairs={{0,12},{4,8},{8,4},{12,0},{16,28},{20,24},{24,20},{28,16},{1,13},{... | collective-permute-start | bytes 393224 | tf_op jit(solution)/shard_map/ppermute | solution.py:184
  14.2 7.5 %collective-permute-start.2 = (bf16[64,1024]{1,0:T(8,128)(2,1)S(1)}, bf16[64,1024]{1,0:T(8,128)(2,1)S(1)}, u32[]{:S(2)}, u32[]{:S(2)}) collective-permute-start(bf16[64,1024]{1,0:T(8,128)(2,1)S(1)} %get-tuple-element.23), channel_id=1, source_target_pairs={{0,12},{4,8},{8,4},{12,0},{16,28},{20,24},{24,20},{28,16},{1,13},{... | collective-permute-start | bytes 393224 | tf_op jit(solution)/shard_map/ppermute | solution.py:184
  14.2 3.3 %copy-start.1 = (bf16[256,256]{1,0:T(8,128)(2,1)S(1)}, bf16[256,256]{1,0:T(8,128)(2,1)}, u32[]{:S(2)}) copy-start(bf16[256,256]{1,0:T(8,128)(2,1)} %constant.37.clone.refs_6_.refs_5_.matrix_ref) | copy-start | bytes 393220
  14.3 3.3 %copy-start.4 = (s32[1,1024]{1,0:T(1,128)S(1)}, s32[1,1024]{1,0:T(1,128)}, u32[]{:S(2)}) copy-start(s32[1,1024]{1,0:T(1,128)} %sign_ref.1) | copy-start | bytes 12292
  18.5 7.4 %collective-permute-start.4 = (s16[64,1024]{1,0:T(8,128)(2,1)S(1)}, s16[64,1024]{1,0:T(8,128)(2,1)S(1)}, u32[]{:S(2)}, u32[]{:S(2)}) collective-permute-start(s16[64,1024]{1,0:T(8,128)(2,1)S(1)} %proxy_blocks.1), channel_id=1, source_target_pairs={{0,16},{4,20},{8,24},{12,28},{16,0},{20,4},{24,8},{28,12},{1,17},{... | collective-permute-start | bytes 393224 | tf_op jit(solution)/shard_map/ppermute | solution.py:184
  26.7 12.4 %all-to-all-start.1 = ((f32[32,1,128]{2,1,0:T(1,128)}), f32[32,1,128]{2,1,0:T(1,128)S(1)}, u32[]{:S(2)}, u32[]{:S(2)}) async-start(f32[32,1,128]{2,1,0:T(1,128)} %get-tuple-element.20), calls=%async_computation.1 | async-start | bytes 32768 | tf_op jit(solution)/shard_map/all_to_all | solution.py:322
  32.0 7.1 %copy-start.2 = (bf16[1,64,1024]{2,1,0:T(8,128)(2,1)S(1)}, bf16[1,64,1024]{2,1,0:T(8,128)(2,1)}, u32[]{:S(2)}) copy-start(bf16[1,64,1024]{2,1,0:T(8,128)(2,1)} %param.7) | copy-start | bytes 393220
  32.0 7.1 %copy-start.3 = (bf16[1,64,1024]{2,1,0:T(8,128)(2,1)S(1)}, bf16[1,64,1024]{2,1,0:T(8,128)(2,1)}, u32[]{:S(2)}) copy-start(bf16[1,64,1024]{2,1,0:T(8,128)(2,1)} %param.8) | copy-start | bytes 393220
  39.3 6.9 %collective-permute-start.10 = (bf16[64,1024]{1,0:T(8,128)(2,1)S(1)}, bf16[64,1024]{1,0:T(8,128)(2,1)S(1)}, u32[]{:S(2)}, u32[]{:S(2)}) collective-permute-start(bf16[64,1024]{1,0:T(8,128)(2,1)S(1)} %new_weights.1.refs_0_), channel_id=1, source_target_pairs={{0,8},{4,12},{8,0},{12,4},{16,24},{20,28},{24,16},{28,20},{1,9},{5... | collective-permute-start | bytes 393224 | tf_op jit(solution)/shard_map/ppermute | solution.py:184
  39.9 8.6 %collective-permute-start.5 = (bf16[64,1024]{1,0:T(8,128)(2,1)S(1)}, bf16[64,1024]{1,0:T(8,128)(2,1)S(1)}, u32[]{:S(2)}, u32[]{:S(2)}) collective-permute-start(bf16[64,1024]{1,0:T(8,128)(2,1)S(1)} %new_weights.1.refs_0_), channel_id=1, source_target_pairs={{0,16},{4,20},{8,24},{12,28},{16,0},{20,4},{24,8},{28,12},{1,17},{... | collective-permute-start | bytes 393224 | tf_op jit(solution)/shard_map/ppermute | solution.py:184
  40.5 12.4 %collective-permute-start.9 = (bf16[64,1024]{1,0:T(8,128)(2,1)S(1)}, bf16[64,1024]{1,0:T(8,128)(2,1)S(1)}, u32[]{:S(2)}, u32[]{:S(2)}) collective-permute-start(bf16[64,1024]{1,0:T(8,128)(2,1)S(1)} %new_weights.1.refs_0_), channel_id=1, source_target_pairs={{0,4},{4,0},{8,12},{12,8},{16,20},{20,16},{24,28},{28,24},{1,5},{5... | collective-permute-start | bytes 393224 | tf_op jit(solution)/shard_map/ppermute | solution.py:184
  46.2 6.9 %collective-permute-start.11 = (bf16[64,1024]{1,0:T(8,128)(2,1)S(1)}, bf16[64,1024]{1,0:T(8,128)(2,1)S(1)}, u32[]{:S(2)}, u32[]{:S(2)}) collective-permute-start(bf16[64,1024]{1,0:T(8,128)(2,1)S(1)} %collective-permute-done.10.refs_2_), channel_id=1, source_target_pairs={{0,4},{4,0},{8,12},{12,8},{16,20},{20,16},{24,28},{28,24},{1,5},{5... | collective-permute-start | bytes 393224 | tf_op jit(solution)/shard_map/ppermute | solution.py:184
  48.5 6.0 %collective-permute-start.8 = (bf16[64,1024]{1,0:T(8,128)(2,1)S(1)}, bf16[64,1024]{1,0:T(8,128)(2,1)S(1)}, u32[]{:S(2)}, u32[]{:S(2)}) collective-permute-start(bf16[64,1024]{1,0:T(8,128)(2,1)S(1)} %collective-permute-done.5.refs_4_), channel_id=1, source_target_pairs={{0,12},{4,8},{8,4},{12,0},{16,28},{20,24},{24,20},{28,16},{1,13},{... | collective-permute-start | bytes 393224 | tf_op jit(solution)/shard_map/ppermute | solution.py:184
  48.5 6.4 %collective-permute-start.7 = (bf16[64,1024]{1,0:T(8,128)(2,1)S(1)}, bf16[64,1024]{1,0:T(8,128)(2,1)S(1)}, u32[]{:S(2)}, u32[]{:S(2)}) collective-permute-start(bf16[64,1024]{1,0:T(8,128)(2,1)S(1)} %collective-permute-done.5.refs_4_), channel_id=1, source_target_pairs={{0,8},{4,12},{8,0},{12,4},{16,24},{20,28},{24,16},{28,20},{1,9},{5... | collective-permute-start | bytes 393224 | tf_op jit(solution)/shard_map/ppermute | solution.py:184
  50.6 5.6 %collective-permute-start.6 = (bf16[64,1024]{1,0:T(8,128)(2,1)S(1)}, bf16[64,1024]{1,0:T(8,128)(2,1)S(1)}, u32[]{:S(2)}, u32[]{:S(2)}) collective-permute-start(bf16[64,1024]{1,0:T(8,128)(2,1)S(1)} %collective-permute-done.5.refs_4_), channel_id=1, source_target_pairs={{0,4},{4,0},{8,12},{12,8},{16,20},{20,16},{24,28},{28,24},{1,5},{5... | collective-permute-start | bytes 393224 | tf_op jit(solution)/shard_map/ppermute | solution.py:184

commit v22 on v21

--- a/solution.py
+++ b/solution.py
@@ -274,7 +274,8 @@
         sums.reshape(replicas, 1, 2 * owned), "dp", split_axis=0, concat_axis=0, tiled=True
     ).reshape(replicas, 2 * owned)
     far_pieces = [swap(block_of(later, me ^ mask ^ near), mask) for mask in diagonal]
-    near_pieces = [swap(block_of(later, me ^ mask), mask) for mask in diagonal]
+    after, sums = lax.optimization_barrier((later, sums))
+    near_pieces = [swap(block_of(after, me ^ mask), mask) for mask in diagonal]
     pairs.append(pair_of(later, me))
     whole = jax.ShapeDtypeStruct((owned, width), jnp.float32)
     column = jax.ShapeDtypeStruct((owned, lanes), jnp.float32)

time: 57.2 us -> 63.5 us (1.11)
  waiting for transfers between devices: 23.5 us -> 30.3 us
    ppermute x12, waiting for transfers between devices: 13.5 us -> 20.9 us  [swap(): return lax.ppermute(value, 'dp', [(i, i ^ mask) for i in range(size)])]
    ppermute x12, starting transfers between devices: 16.5 us -> 12.3 us  [swap(): return lax.ppermute(value, 'dp', [(i, i ^ mask) for i in range(size)])]
    all_to_all x1, starting transfers between devices: 3.87 us -> 7.25 us  [on_device(): lax.all_to_all(sums.reshape(replicas, 1, 2 * owned), 'dp', split_axis=0,...]
    unnamed x10 -> x12, local copies, waits for them, and re-layouts: 0.02 us -> 1.24 us
    reshape x2, local copies, waits for them, and re-layouts: 1.17 us -> 0.06 us  [pair_of(): lax.dynamic_slice_in_dim(source, index % near, 1, 1)]
  transfers between devices with their start and end apart: 14 -> 14, of which waited for: 10 -> 11; matrix products, arithmetic and copies ran while one was open for 0% -> 0% of each run, Pallas kernels for 7% -> 5%
where the time goes in v22:
time: 63.5 us; the launch traced here: 63.2 us
  waiting for transfers between devices  30.3 us (48%)
  starting transfers between devices  25.1 us (40%)
  Pallas kernels  5.77 us (9%)
  local copies, waits for them, and re-layouts  1.32 us (2%)
  between operations  0.76 us (1%)
    ppermute x12, waiting for transfers between devices, swap(): return lax.ppermute(value, 'dp', [(i, i ^ mask) for i in range(size)])  20.9 us
    ppermute x12, starting transfers between devices, swap(): return lax.ppermute(value, 'dp', [(i, i ^ mask) for i in range(size)])  12.3 us
    all_to_all x1, starting transfers between devices, on_device(): lax.all_to_all(sums.reshape(replicas, 1, 2 * owned), 'dp', split_axis=0,...  7.25 us
    all_to_all x1, waiting for transfers between devices, on_device(): lax.all_to_all(squares, ('dp', 'expert'), split_axis=0, concat_axis=0, ti...  6.72 us
    all_to_all x1, starting transfers between devices, on_device(): lax.all_to_all(squares, ('dp', 'expert'), split_axis=0, concat_axis=0, ti...  5.55 us
    all_to_all x1, waiting for transfers between devices, on_device(): lax.all_to_all(sums.reshape(replicas, 1, 2 * owned), 'dp', split_axis=0,...  2.67 us
    pallas_call x2, Pallas kernels, place_pieces(): pl.pallas_call(functools.partial(place_kernel, places, owned), in_specs=s...  1.63 us
  transfers between devices with their start and end apart: 14, of which 11 were waited for; matrix products, arithmetic and copies ran while one was open for 0% of the time, Pallas kernels for 5%

profile of v22, /device:TPU:0, one launch (start us, length us, event | category | flops | bytes accessed | tf_op | source)
XLA Modules:
  0.0 63.2 jit_solution(2341357089257699675)
XLA Ops:
  0.6 1.2 %copy-done = bf16[1,1,512,1024]{3,2,1,0:T(8,128)(2,1)S(1)} copy-done((bf16[1,1,512,1024]{3,2,1,0:T(8,128)(2,1)S(1)}, bf16[1,1,512,1024]{3,2,1,0:T(8,128)(2,1)}, u32[]{:S(2)}) %copy-start) | copy-done | bytes 1048600
  1.9 0.9 %sum_squares.1 = f32[2,4,1,128]{3,2,1,0:T(1,128)} custom-call(bf16[2,4,64,1024]{3,2,1,0:T(8,128)(2,1)S(1)} %bitcast.25), custom_call_target="tpu_custom_call" | custom-call | tf_op jit(solution)/shard_map/sum_squares/pallas_call | solution.py:265
  2.7 7.3 %all-to-all-start = ((f32[8,1,128]{2,1,0:T(1,128)}), f32[8,1,128]{2,1,0:T(1,128)S(1)}, u32[]{:S(2)}, u32[]{:S(2)}) async-start(f32[8,1,128]{2,1,0:T(1,128)} %bitcast.6), calls=%async_computation | async-start | bytes 8192 | tf_op jit(solution)/shard_map/all_to_all | solution.py:273
  10.0 2.1 %collective-permute-start.1 = (bf16[2,64,1024]{2,1,0:T(8,128)(2,1)S(1)}, bf16[2,64,1024]{2,1,0:T(8,128)(2,1)S(1)}, u32[]{:S(2)}, u32[]{:S(2)}) collective-permute-start(bf16[2,64,1024]{2,1,0:T(8,128)(2,1)S(1)} %get-tuple-element.26), channel_id=1, source_target_pairs={{0,8},{4,12},{8,0},{12,4},{16,24},{20,28},{24,16},{28,20},{1,9},{5... | collective-permute-start | bytes 786440 | tf_op jit(solution)/shard_map/ppermute | solution.py:184
  12.1 1.5 %collective-permute-start = (bf16[2,64,1024]{2,1,0:T(8,128)(2,1)S(1)}, bf16[2,64,1024]{2,1,0:T(8,128)(2,1)S(1)}, u32[]{:S(2)}, u32[]{:S(2)}) collective-permute-start(bf16[2,64,1024]{2,1,0:T(8,128)(2,1)S(1)} %get-tuple-element.27), channel_id=1, source_target_pairs={{0,4},{4,0},{8,12},{12,8},{16,20},{20,16},{24,28},{28,24},{1,5},{5... | collective-permute-start | bytes 786440 | tf_op jit(solution)/shard_map/ppermute | solution.py:184
  13.8 2.7 %all-to-all-done = f32[8,1,128]{2,1,0:T(1,128)S(1)} async-done(((f32[8,1,128]{2,1,0:T(1,128)}), f32[8,1,128]{2,1,0:T(1,128)S(1)}, u32[]{:S(2)}, u32[]{:S(2)}) %all-to-all-start) | async-done | bytes 4128 | tf_op jit(solution)/shard_map/all_to_all | solution.py:273
  16.4 0.6 collective-permute-start.2
  17.1 2.3 %collective-permute-done.1.refs_1_ = bf16[2,64,1024]{2,1,0:T(8,128)(2,1)S(1)} collective-permute-done((bf16[2,64,1024]{2,1,0:T(8,128)(2,1)S(1)}, bf16[2,64,1024]{2,1,0:T(8,128)(2,1)S(1)}, u32[]{:S(2)}, u32[]{:S(2)}) %collective-permute-start.1) | collective-permute-done | bytes 262176 | tf_op jit(solution)/shard_map/ppermute | solution.py:184
  19.4 4.8 %collective-permute-done.refs_0_ = bf16[2,64,1024]{2,1,0:T(8,128)(2,1)S(1)} collective-permute-done((bf16[2,64,1024]{2,1,0:T(8,128)(2,1)S(1)}, bf16[2,64,1024]{2,1,0:T(8,128)(2,1)S(1)}, u32[]{:S(2)}, u32[]{:S(2)}) %collective-permute-start) | collective-permute-done | bytes 262176 | tf_op jit(solution)/shard_map/ppermute | solution.py:184
  24.9 2.2 %collective-permute-start.4 = (s16[64,1024]{1,0:T(8,128)(2,1)S(1)}, s16[64,1024]{1,0:T(8,128)(2,1)S(1)}, u32[]{:S(2)}, u32[]{:S(2)}) collective-permute-start(s16[64,1024]{1,0:T(8,128)(2,1)S(1)} %proxy_blocks.1), channel_id=1, source_target_pairs={{0,16},{4,20},{8,24},{12,28},{16,0},{20,4},{24,8},{28,12},{1,17},{... | collective-permute-start | bytes 393224 | tf_op jit(solution)/shard_map/ppermute | solution.py:184
  27.1 0.6 owner_blocks.1
  27.7 4.4 %collective-permute-done.4.far_ref = s16[64,1024]{1,0:T(8,128)(2,1)S(1)} collective-permute-done((s16[64,1024]{1,0:T(8,128)(2,1)S(1)}, s16[64,1024]{1,0:T(8,128)(2,1)S(1)}, u32[]{:S(2)}, u32[]{:S(2)}) %collective-permute-start.4) | collective-permute-done | bytes 131104 | tf_op jit(solution)/shard_map/ppermute | solution.py:184
  32.0 0.7 %finish_blocks.1 = (f32[64,1024]{1,0:T(8,128)S(1)}, f32[32,1,128]{2,1,0:T(1,128)}) custom-call(f32[64,1024]{1,0:T(8,128)S(1)} %get-tuple-element.18.near_ref, s16[64,1024]{1,0:T(8,128)(2,1)S(1)} %collective-permute-done.4.far_ref, f32[64,128]{1,0:T(8,128)S(1)} %get-tuple-element.22.scale_ref, f32[64,128]{1,0:T(8,128)S(1)} %get-tuple-element.23.step_ref), custom_call_target="tpu_custom_call" | custom-call | tf_op jit(solution)/shard_map/finish_blocks/pallas_call | solution.py:307
  32.7 5.6 %all-to-all-start.1 = ((f32[32,1,128]{2,1,0:T(1,128)}), f32[32,1,128]{2,1,0:T(1,128)S(1)}, u32[]{:S(2)}, u32[]{:S(2)}) async-start(f32[32,1,128]{2,1,0:T(1,128)} %get-tuple-element.24), calls=%async_computation.1 | async-start | bytes 32768 | tf_op jit(solution)/shard_map/all_to_all | solution.py:323
  38.6 6.7 %all-to-all-done.1 = f32[32,1,128]{2,1,0:T(1,128)S(1)} async-done(((f32[32,1,128]{2,1,0:T(1,128)}), f32[32,1,128]{2,1,0:T(1,128)S(1)}, u32[]{:S(2)}, u32[]{:S(2)}) %all-to-all-start.1) | async-done | bytes 16416 | tf_op jit(solution)/shard_map/all_to_all | solution.py:323
  45.5 0.6 %collective-permute-start.10 = (bf16[64,1024]{1,0:T(8,128)(2,1)S(1)}, bf16[64,1024]{1,0:T(8,128)(2,1)S(1)}, u32[]{:S(2)}, u32[]{:S(2)}) collective-permute-start(bf16[64,1024]{1,0:T(8,128)(2,1)S(1)} %new_weights.1.refs_0_), channel_id=1, source_target_pairs={{0,8},{4,12},{8,0},{12,4},{16,24},{20,28},{24,16},{28,20},{1,9},{5... | collective-permute-start | bytes 393224 | tf_op jit(solution)/shard_map/ppermute | solution.py:184
  47.3 5.2 %collective-permute-done.10.refs_2_ = bf16[64,1024]{1,0:T(8,128)(2,1)S(1)} collective-permute-done((bf16[64,1024]{1,0:T(8,128)(2,1)S(1)}, bf16[64,1024]{1,0:T(8,128)(2,1)S(1)}, u32[]{:S(2)}, u32[]{:S(2)}) %collective-permute-start.10) | collective-permute-done | bytes 131104 | tf_op jit(solution)/shard_map/ppermute | solution.py:184
  53.0 1.8 %collective-permute-done.5.refs_4_ = bf16[64,1024]{1,0:T(8,128)(2,1)S(1)} collective-permute-done((bf16[64,1024]{1,0:T(8,128)(2,1)S(1)}, bf16[64,1024]{1,0:T(8,128)(2,1)S(1)}, u32[]{:S(2)}, u32[]{:S(2)}) %collective-permute-start.5) | collective-permute-done | bytes 131104 | tf_op jit(solution)/shard_map/ppermute | solution.py:184
  54.8 2.1 %collective-permute-start.7 = (bf16[64,1024]{1,0:T(8,128)(2,1)S(1)}, bf16[64,1024]{1,0:T(8,128)(2,1)S(1)}, u32[]{:S(2)}, u32[]{:S(2)}) collective-permute-start(bf16[64,1024]{1,0:T(8,128)(2,1)S(1)} %collective-permute-done.5.refs_4_), channel_id=1, source_target_pairs={{0,8},{4,12},{8,0},{12,4},{16,24},{20,28},{24,16},{28,20},{1,9},{5... | collective-permute-start | bytes 393224 | tf_op jit(solution)/shard_map/ppermute | solution.py:184
  56.9 1.4 %collective-permute-start.6 = (bf16[64,1024]{1,0:T(8,128)(2,1)S(1)}, bf16[64,1024]{1,0:T(8,128)(2,1)S(1)}, u32[]{:S(2)}, u32[]{:S(2)}) collective-permute-start(bf16[64,1024]{1,0:T(8,128)(2,1)S(1)} %collective-permute-done.5.refs_4_), channel_id=1, source_target_pairs={{0,4},{4,0},{8,12},{12,8},{16,20},{20,16},{24,28},{28,24},{1,5},{5... | collective-permute-start | bytes 393224 | tf_op jit(solution)/shard_map/ppermute | solution.py:184
  58.3 0.8 %update_grad.1 = f32[64,1024]{1,0:T(8,128)} custom-call(f32[32,128]{1,0:T(8,128)S(1)} %bitcast.31, f32[64,1024]{1,0:T(8,128)S(1)} %rotate_back.1.unrot_ref), custom_call_target="tpu_custom_call" | custom-call | tf_op jit(solution)/shard_map/update_grad/pallas_call | solution.py:332
  59.4 0.9 %place_own.1.refs_3_ = bf16[512,1024]{1,0:T(8,128)(2,1)} custom-call(bf16[64,1024]{1,0:T(8,128)(2,1)S(1)} %new_weights.1.refs_0_, bf16[64,1024]{1,0:T(8,128)(2,1)S(1)} %collective-permute-done.9.refs_1_, bf16[64,1024]{1,0:T(8,128)(2,1)S(1)} %collective-permute-done.10.refs_2_, bf16[64,1024]{1,0:T(8,128)(2,1)S(1)} %collective-permute-done.11.refs_3_, ...), custom_call_target="tpu_custom_call" | custom-call | tf_op jit(solution)/shard_map/place_own/pallas_call | solution.py:211
  61.3 1.2 %collective-permute-done.6.refs_0_ = bf16[64,1024]{1,0:T(8,128)(2,1)S(1)} collective-permute-done((bf16[64,1024]{1,0:T(8,128)(2,1)S(1)}, bf16[64,1024]{1,0:T(8,128)(2,1)S(1)}, u32[]{:S(2)}, u32[]{:S(2)}) %collective-permute-start.6) | collective-permute-done | bytes 131104 | tf_op jit(solution)/shard_map/ppermute | solution.py:184
  62.5 0.8 %place_far.1 = bf16[512,1024]{1,0:T(8,128)(2,1)} custom-call(bf16[64,1024]{1,0:T(8,128)(2,1)S(1)} %collective-permute-done.6.refs_0_, bf16[64,1024]{1,0:T(8,128)(2,1)S(1)} %collective-permute-done.7.refs_1_, bf16[64,1024]{1,0:T(8,128)(2,1)S(1)} %collective-permute-done.8.refs_2_, bf16[512,1024]{1,0:T(8,128)(2,1)} %place_own.1.refs_3_), custom_call_target="tpu_custom_call", output_to_operand_aliasing={{}: (3, {})} | custom-call | tf_op jit(solution)/shard_map/place_far/pallas_call | solution.py:211
  (30 shorter events, 4.3 us)
Async XLA Ops:
  0.6 1.2 %copy-start = (bf16[1,1,512,1024]{3,2,1,0:T(8,128)(2,1)S(1)}, bf16[1,1,512,1024]{3,2,1,0:T(8,128)(2,1)}, u32[]{:S(2)}) copy-start(bf16[1,1,512,1024]{3,2,1,0:T(8,128)(2,1)} %param.5) | copy-start | bytes 3145732
  1.9 8.1 %copy-start.1 = (bf16[1,1,512,1024]{3,2,1,0:T(8,128)(2,1)S(1)}, bf16[1,1,512,1024]{3,2,1,0:T(8,128)(2,1)}, u32[]{:S(2)}) copy-start(bf16[1,1,512,1024]{3,2,1,0:T(8,128)(2,1)} %param.5) | copy-start | bytes 3145732
  2.7 13.7 %all-to-all-start = ((f32[8,1,128]{2,1,0:T(1,128)}), f32[8,1,128]{2,1,0:T(1,128)S(1)}, u32[]{:S(2)}, u32[]{:S(2)}) async-start(f32[8,1,128]{2,1,0:T(1,128)} %bitcast.6), calls=%async_computation | async-start | bytes 8192 | tf_op jit(solution)/shard_map/all_to_all | solution.py:273
  10.0 9.4 %collective-permute-start.1 = (bf16[2,64,1024]{2,1,0:T(8,128)(2,1)S(1)}, bf16[2,64,1024]{2,1,0:T(8,128)(2,1)S(1)}, u32[]{:S(2)}, u32[]{:S(2)}) collective-permute-start(bf16[2,64,1024]{2,1,0:T(8,128)(2,1)S(1)} %get-tuple-element.26), channel_id=1, source_target_pairs={{0,8},{4,12},{8,0},{12,4},{16,24},{20,28},{24,16},{28,20},{1,9},{5... | collective-permute-start | bytes 786440 | tf_op jit(solution)/shard_map/ppermute | solution.py:184
  12.1 12.1 %collective-permute-start = (bf16[2,64,1024]{2,1,0:T(8,128)(2,1)S(1)}, bf16[2,64,1024]{2,1,0:T(8,128)(2,1)S(1)}, u32[]{:S(2)}, u32[]{:S(2)}) collective-permute-start(bf16[2,64,1024]{2,1,0:T(8,128)(2,1)S(1)} %get-tuple-element.27), channel_id=1, source_target_pairs={{0,4},{4,0},{8,12},{12,8},{16,20},{20,16},{24,28},{28,24},{1,5},{5... | collective-permute-start | bytes 786440 | tf_op jit(solution)/shard_map/ppermute | solution.py:184
  13.6 11.0 %collective-permute-start.3 = (bf16[64,1024]{1,0:T(8,128)(2,1)S(1)}, bf16[64,1024]{1,0:T(8,128)(2,1)S(1)}, u32[]{:S(2)}, u32[]{:S(2)}) collective-permute-start(bf16[64,1024]{1,0:T(8,128)(2,1)S(1)} %dynamic-slice_bitcast_fusion.3), channel_id=1, source_target_pairs={{0,12},{4,8},{8,4},{12,0},{16,28},{20,24},{24,20},{28,16},{1,13},{... | collective-permute-start | bytes 393224 | tf_op jit(solution)/shard_map/ppermute | solution.py:184
  16.4 7.7 %copy-start.2 = (bf16[256,256]{1,0:T(8,128)(2,1)S(1)}, bf16[256,256]{1,0:T(8,128)(2,1)}, u32[]{:S(2)}) copy-start(bf16[256,256]{1,0:T(8,128)(2,1)} %constant.37.clone.refs_6_.refs_5_.matrix_ref) | copy-start | bytes 393220
  16.4 7.7 %copy-start.5 = (s32[1,1024]{1,0:T(1,128)S(1)}, s32[1,1024]{1,0:T(1,128)}, u32[]{:S(2)}) copy-start(s32[1,1024]{1,0:T(1,128)} %sign_ref.1) | copy-start | bytes 12292
  16.4 10.7 %collective-permute-start.2 = (bf16[64,1024]{1,0:T(8,128)(2,1)S(1)}, bf16[64,1024]{1,0:T(8,128)(2,1)S(1)}, u32[]{:S(2)}, u32[]{:S(2)}) collective-permute-start(bf16[64,1024]{1,0:T(8,128)(2,1)S(1)} %dynamic-slice_bitcast_fusion.4), channel_id=1, source_target_pairs={{0,12},{4,8},{8,4},{12,0},{16,28},{20,24},{24,20},{28,16},{1,13},{... | collective-permute-start | bytes 393224 | tf_op jit(solution)/shard_map/ppermute | solution.py:184
  24.9 7.1 %collective-permute-start.4 = (s16[64,1024]{1,0:T(8,128)(2,1)S(1)}, s16[64,1024]{1,0:T(8,128)(2,1)S(1)}, u32[]{:S(2)}, u32[]{:S(2)}) collective-permute-start(s16[64,1024]{1,0:T(8,128)(2,1)S(1)} %proxy_blocks.1), channel_id=1, source_target_pairs={{0,16},{4,20},{8,24},{12,28},{16,0},{20,4},{24,8},{28,12},{1,17},{... | collective-permute-start | bytes 393224 | tf_op jit(solution)/shard_map/ppermute | solution.py:184
  32.7 12.6 %all-to-all-start.1 = ((f32[32,1,128]{2,1,0:T(1,128)}), f32[32,1,128]{2,1,0:T(1,128)S(1)}, u32[]{:S(2)}, u32[]{:S(2)}) async-start(f32[32,1,128]{2,1,0:T(1,128)} %get-tuple-element.24), calls=%async_computation.1 | async-start | bytes 32768 | tf_op jit(solution)/shard_map/all_to_all | solution.py:323
  38.3 7.1 %copy-start.3 = (bf16[1,64,1024]{2,1,0:T(8,128)(2,1)S(1)}, bf16[1,64,1024]{2,1,0:T(8,128)(2,1)}, u32[]{:S(2)}) copy-start(bf16[1,64,1024]{2,1,0:T(8,128)(2,1)} %param.7) | copy-start | bytes 393220
  38.3 7.1 %copy-start.4 = (bf16[1,64,1024]{2,1,0:T(8,128)(2,1)S(1)}, bf16[1,64,1024]{2,1,0:T(8,128)(2,1)}, u32[]{:S(2)}) copy-start(bf16[1,64,1024]{2,1,0:T(8,128)(2,1)} %param.8) | copy-start | bytes 393220
  45.5 6.9 %collective-permute-start.10 = (bf16[64,1024]{1,0:T(8,128)(2,1)S(1)}, bf16[64,1024]{1,0:T(8,128)(2,1)S(1)}, u32[]{:S(2)}, u32[]{:S(2)}) collective-permute-start(bf16[64,1024]{1,0:T(8,128)(2,1)S(1)} %new_weights.1.refs_0_), channel_id=1, source_target_pairs={{0,8},{4,12},{8,0},{12,4},{16,24},{20,28},{24,16},{28,20},{1,9},{5... | collective-permute-start | bytes 393224 | tf_op jit(solution)/shard_map/ppermute | solution.py:184
  46.2 8.6 %collective-permute-start.5 = (bf16[64,1024]{1,0:T(8,128)(2,1)S(1)}, bf16[64,1024]{1,0:T(8,128)(2,1)S(1)}, u32[]{:S(2)}, u32[]{:S(2)}) collective-permute-start(bf16[64,1024]{1,0:T(8,128)(2,1)S(1)} %new_weights.1.refs_0_), channel_id=1, source_target_pairs={{0,16},{4,20},{8,24},{12,28},{16,0},{20,4},{24,8},{28,12},{1,17},{... | collective-permute-start | bytes 393224 | tf_op jit(solution)/shard_map/ppermute | solution.py:184
  46.7 12.4 %collective-permute-start.9 = (bf16[64,1024]{1,0:T(8,128)(2,1)S(1)}, bf16[64,1024]{1,0:T(8,128)(2,1)S(1)}, u32[]{:S(2)}, u32[]{:S(2)}) collective-permute-start(bf16[64,1024]{1,0:T(8,128)(2,1)S(1)} %new_weights.1.refs_0_), channel_id=1, source_target_pairs={{0,4},{4,0},{8,12},{12,8},{16,20},{20,16},{24,28},{28,24},{1,5},{5... | collective-permute-start | bytes 393224 | tf_op jit(solution)/shard_map/ppermute | solution.py:184
  52.5 6.9 %collective-permute-start.11 = (bf16[64,1024]{1,0:T(8,128)(2,1)S(1)}, bf16[64,1024]{1,0:T(8,128)(2,1)S(1)}, u32[]{:S(2)}, u32[]{:S(2)}) collective-permute-start(bf16[64,1024]{1,0:T(8,128)(2,1)S(1)} %collective-permute-done.10.refs_2_), channel_id=1, source_target_pairs={{0,4},{4,0},{8,12},{12,8},{16,20},{20,16},{24,28},{28,24},{1,5},{5... | collective-permute-start | bytes 393224 | tf_op jit(solution)/shard_map/ppermute | solution.py:184
  54.8 6.0 %collective-permute-start.8 = (bf16[64,1024]{1,0:T(8,128)(2,1)S(1)}, bf16[64,1024]{1,0:T(8,128)(2,1)S(1)}, u32[]{:S(2)}, u32[]{:S(2)}) collective-permute-start(bf16[64,1024]{1,0:T(8,128)(2,1)S(1)} %collective-permute-done.5.refs_4_), channel_id=1, source_target_pairs={{0,12},{4,8},{8,4},{12,0},{16,28},{20,24},{24,20},{28,16},{1,13},{... | collective-permute-start | bytes 393224 | tf_op jit(solution)/shard_map/ppermute | solution.py:184
  54.8 6.4 %collective-permute-start.7 = (bf16[64,1024]{1,0:T(8,128)(2,1)S(1)}, bf16[64,1024]{1,0:T(8,128)(2,1)S(1)}, u32[]{:S(2)}, u32[]{:S(2)}) collective-permute-start(bf16[64,1024]{1,0:T(8,128)(2,1)S(1)} %collective-permute-done.5.refs_4_), channel_id=1, source_target_pairs={{0,8},{4,12},{8,0},{12,4},{16,24},{20,28},{24,16},{28,20},{1,9},{5... | collective-permute-start | bytes 393224 | tf_op jit(solution)/shard_map/ppermute | solution.py:184
  56.9 5.6 %collective-permute-start.6 = (bf16[64,1024]{1,0:T(8,128)(2,1)S(1)}, bf16[64,1024]{1,0:T(8,128)(2,1)S(1)}, u32[]{:S(2)}, u32[]{:S(2)}) collective-permute-start(bf16[64,1024]{1,0:T(8,128)(2,1)S(1)} %collective-permute-done.5.refs_4_), channel_id=1, source_target_pairs={{0,4},{4,0},{8,12},{12,8},{16,20},{20,16},{24,28},{28,24},{1,5},{5... | collective-permute-start | bytes 393224 | tf_op jit(solution)/shard_map/ppermute | solution.py:184

commit v23 on v22

--- a/solution.py
+++ b/solution.py
@@ -284,9 +284,6 @@
         in_specs=[array] * (len(pairs) + 3),
         out_shape=(whole, column, column),
         compiler_params=params,
-        cost_estimate=pl.CostEstimate(
-            flops=20000000000, bytes_accessed=4 * blocks * width, transcendentals=0
-        ),
         name="proxy_pairs",
     )(*pairs, sums, signs, matrix)
     sent = pl.pallas_call(

time: 63.5 us -> 63.5 us (level)
  no operation moved by 1% of the time
where the time goes in v23:
time: 63.5 us; the launch traced here: 63.2 us
  waiting for transfers between devices  30.3 us (48%)
  starting transfers between devices  25.1 us (40%)
  Pallas kernels  5.77 us (9%)
  local copies, waits for them, and re-layouts  1.32 us (2%)
  between operations  0.76 us (1%)
    ppermute x12, waiting for transfers between devices, swap(): return lax.ppermute(value, 'dp', [(i, i ^ mask) for i in range(size)])  20.9 us
    ppermute x12, starting transfers between devices, swap(): return lax.ppermute(value, 'dp', [(i, i ^ mask) for i in range(size)])  12.3 us
    all_to_all x1, starting transfers between devices, on_device(): lax.all_to_all(sums.reshape(replicas, 1, 2 * owned), 'dp', split_axis=0,...  7.25 us
    all_to_all x1, waiting for transfers between devices, on_device(): lax.all_to_all(squares, ('dp', 'expert'), split_axis=0, concat_axis=0, ti...  6.72 us
    all_to_all x1, starting transfers between devices, on_device(): lax.all_to_all(squares, ('dp', 'expert'), split_axis=0, concat_axis=0, ti...  5.55 us
    all_to_all x1, waiting for transfers between devices, on_device(): lax.all_to_all(sums.reshape(replicas, 1, 2 * owned), 'dp', split_axis=0,...  2.67 us
    pallas_call x2, Pallas kernels, place_pieces(): pl.pallas_call(functools.partial(place_kernel, places, owned), in_specs=s...  1.63 us
  transfers between devices with their start and end apart: 14, of which 11 were waited for; matrix products, arithmetic and copies ran while one was open for 0% of the time, Pallas kernels for 5%

profile of v23, /device:TPU:0, one launch (start us, length us, event | category | flops | bytes accessed | tf_op | source)
XLA Modules:
  0.0 63.2 jit_solution(10824452740194609399)
XLA Ops:
  0.6 1.2 %copy-done = bf16[1,1,512,1024]{3,2,1,0:T(8,128)(2,1)S(1)} copy-done((bf16[1,1,512,1024]{3,2,1,0:T(8,128)(2,1)S(1)}, bf16[1,1,512,1024]{3,2,1,0:T(8,128)(2,1)}, u32[]{:S(2)}) %copy-start) | copy-done | bytes 1048600
  1.9 0.9 %sum_squares.1 = f32[2,4,1,128]{3,2,1,0:T(1,128)} custom-call(bf16[2,4,64,1024]{3,2,1,0:T(8,128)(2,1)S(1)} %bitcast.25), custom_call_target="tpu_custom_call" | custom-call | tf_op jit(solution)/shard_map/sum_squares/pallas_call | solution.py:265
  2.7 7.3 %all-to-all-start = ((f32[8,1,128]{2,1,0:T(1,128)}), f32[8,1,128]{2,1,0:T(1,128)S(1)}, u32[]{:S(2)}, u32[]{:S(2)}) async-start(f32[8,1,128]{2,1,0:T(1,128)} %bitcast.6), calls=%async_computation | async-start | bytes 8192 | tf_op jit(solution)/shard_map/all_to_all | solution.py:273
  10.0 2.1 %collective-permute-start.1 = (bf16[2,64,1024]{2,1,0:T(8,128)(2,1)S(1)}, bf16[2,64,1024]{2,1,0:T(8,128)(2,1)S(1)}, u32[]{:S(2)}, u32[]{:S(2)}) collective-permute-start(bf16[2,64,1024]{2,1,0:T(8,128)(2,1)S(1)} %get-tuple-element.26), channel_id=1, source_target_pairs={{0,8},{4,12},{8,0},{12,4},{16,24},{20,28},{24,16},{28,20},{1,9},{5... | collective-permute-start | bytes 786440 | tf_op jit(solution)/shard_map/ppermute | solution.py:184
  12.1 1.5 %collective-permute-start = (bf16[2,64,1024]{2,1,0:T(8,128)(2,1)S(1)}, bf16[2,64,1024]{2,1,0:T(8,128)(2,1)S(1)}, u32[]{:S(2)}, u32[]{:S(2)}) collective-permute-start(bf16[2,64,1024]{2,1,0:T(8,128)(2,1)S(1)} %get-tuple-element.27), channel_id=1, source_target_pairs={{0,4},{4,0},{8,12},{12,8},{16,20},{20,16},{24,28},{28,24},{1,5},{5... | collective-permute-start | bytes 786440 | tf_op jit(solution)/shard_map/ppermute | solution.py:184
  13.8 2.7 %all-to-all-done = f32[8,1,128]{2,1,0:T(1,128)S(1)} async-done(((f32[8,1,128]{2,1,0:T(1,128)}), f32[8,1,128]{2,1,0:T(1,128)S(1)}, u32[]{:S(2)}, u32[]{:S(2)}) %all-to-all-start) | async-done | bytes 4128 | tf_op jit(solution)/shard_map/all_to_all | solution.py:273
  16.4 0.6 collective-permute-start.2
  17.1 2.3 %collective-permute-done.1.refs_1_ = bf16[2,64,1024]{2,1,0:T(8,128)(2,1)S(1)} collective-permute-done((bf16[2,64,1024]{2,1,0:T(8,128)(2,1)S(1)}, bf16[2,64,1024]{2,1,0:T(8,128)(2,1)S(1)}, u32[]{:S(2)}, u32[]{:S(2)}) %collective-permute-start.1) | collective-permute-done | bytes 262176 | tf_op jit(solution)/shard_map/ppermute | solution.py:184
  19.4 4.8 %collective-permute-done.refs_0_ = bf16[2,64,1024]{2,1,0:T(8,128)(2,1)S(1)} collective-permute-done((bf16[2,64,1024]{2,1,0:T(8,128)(2,1)S(1)}, bf16[2,64,1024]{2,1,0:T(8,128)(2,1)S(1)}, u32[]{:S(2)}, u32[]{:S(2)}) %collective-permute-start) | collective-permute-done | bytes 262176 | tf_op jit(solution)/shard_map/ppermute | solution.py:184
  24.9 2.2 %collective-permute-start.4 = (s16[64,1024]{1,0:T(8,128)(2,1)S(1)}, s16[64,1024]{1,0:T(8,128)(2,1)S(1)}, u32[]{:S(2)}, u32[]{:S(2)}) collective-permute-start(s16[64,1024]{1,0:T(8,128)(2,1)S(1)} %proxy_blocks.1), channel_id=1, source_target_pairs={{0,16},{4,20},{8,24},{12,28},{16,0},{20,4},{24,8},{28,12},{1,17},{... | collective-permute-start | bytes 393224 | tf_op jit(solution)/shard_map/ppermute | solution.py:184
  27.1 0.6 owner_blocks.1
  27.7 4.4 %collective-permute-done.4.far_ref = s16[64,1024]{1,0:T(8,128)(2,1)S(1)} collective-permute-done((s16[64,1024]{1,0:T(8,128)(2,1)S(1)}, s16[64,1024]{1,0:T(8,128)(2,1)S(1)}, u32[]{:S(2)}, u32[]{:S(2)}) %collective-permute-start.4) | collective-permute-done | bytes 131104 | tf_op jit(solution)/shard_map/ppermute | solution.py:184
  32.0 0.7 %finish_blocks.1 = (f32[64,1024]{1,0:T(8,128)S(1)}, f32[32,1,128]{2,1,0:T(1,128)}) custom-call(f32[64,1024]{1,0:T(8,128)S(1)} %get-tuple-element.18.near_ref, s16[64,1024]{1,0:T(8,128)(2,1)S(1)} %collective-permute-done.4.far_ref, f32[64,128]{1,0:T(8,128)S(1)} %get-tuple-element.22.scale_ref, f32[64,128]{1,0:T(8,128)S(1)} %get-tuple-element.23.step_ref), custom_call_target="tpu_custom_call" | custom-call | tf_op jit(solution)/shard_map/finish_blocks/pallas_call | solution.py:304
  32.7 5.6 %all-to-all-start.1 = ((f32[32,1,128]{2,1,0:T(1,128)}), f32[32,1,128]{2,1,0:T(1,128)S(1)}, u32[]{:S(2)}, u32[]{:S(2)}) async-start(f32[32,1,128]{2,1,0:T(1,128)} %get-tuple-element.24), calls=%async_computation.1 | async-start | bytes 32768 | tf_op jit(solution)/shard_map/all_to_all | solution.py:320
  38.6 6.7 %all-to-all-done.1 = f32[32,1,128]{2,1,0:T(1,128)S(1)} async-done(((f32[32,1,128]{2,1,0:T(1,128)}), f32[32,1,128]{2,1,0:T(1,128)S(1)}, u32[]{:S(2)}, u32[]{:S(2)}) %all-to-all-start.1) | async-done | bytes 16416 | tf_op jit(solution)/shard_map/all_to_all | solution.py:320
  45.5 0.6 %collective-permute-start.10 = (bf16[64,1024]{1,0:T(8,128)(2,1)S(1)}, bf16[64,1024]{1,0:T(8,128)(2,1)S(1)}, u32[]{:S(2)}, u32[]{:S(2)}) collective-permute-start(bf16[64,1024]{1,0:T(8,128)(2,1)S(1)} %new_weights.1.refs_0_), channel_id=1, source_target_pairs={{0,8},{4,12},{8,0},{12,4},{16,24},{20,28},{24,16},{28,20},{1,9},{5... | collective-permute-start | bytes 393224 | tf_op jit(solution)/shard_map/ppermute | solution.py:184
  47.3 5.2 %collective-permute-done.10.refs_2_ = bf16[64,1024]{1,0:T(8,128)(2,1)S(1)} collective-permute-done((bf16[64,1024]{1,0:T(8,128)(2,1)S(1)}, bf16[64,1024]{1,0:T(8,128)(2,1)S(1)}, u32[]{:S(2)}, u32[]{:S(2)}) %collective-permute-start.10) | collective-permute-done | bytes 131104 | tf_op jit(solution)/shard_map/ppermute | solution.py:184
  53.0 1.8 %collective-permute-done.5.refs_4_ = bf16[64,1024]{1,0:T(8,128)(2,1)S(1)} collective-permute-done((bf16[64,1024]{1,0:T(8,128)(2,1)S(1)}, bf16[64,1024]{1,0:T(8,128)(2,1)S(1)}, u32[]{:S(2)}, u32[]{:S(2)}) %collective-permute-start.5) | collective-permute-done | bytes 131104 | tf_op jit(solution)/shard_map/ppermute | solution.py:184
  54.8 2.1 %collective-permute-start.7 = (bf16[64,1024]{1,0:T(8,128)(2,1)S(1)}, bf16[64,1024]{1,0:T(8,128)(2,1)S(1)}, u32[]{:S(2)}, u32[]{:S(2)}) collective-permute-start(bf16[64,1024]{1,0:T(8,128)(2,1)S(1)} %collective-permute-done.5.refs_4_), channel_id=1, source_target_pairs={{0,8},{4,12},{8,0},{12,4},{16,24},{20,28},{24,16},{28,20},{1,9},{5... | collective-permute-start | bytes 393224 | tf_op jit(solution)/shard_map/ppermute | solution.py:184
  56.9 1.4 %collective-permute-start.6 = (bf16[64,1024]{1,0:T(8,128)(2,1)S(1)}, bf16[64,1024]{1,0:T(8,128)(2,1)S(1)}, u32[]{:S(2)}, u32[]{:S(2)}) collective-permute-start(bf16[64,1024]{1,0:T(8,128)(2,1)S(1)} %collective-permute-done.5.refs_4_), channel_id=1, source_target_pairs={{0,4},{4,0},{8,12},{12,8},{16,20},{20,16},{24,28},{28,24},{1,5},{5... | collective-permute-start | bytes 393224 | tf_op jit(solution)/shard_map/ppermute | solution.py:184
  58.3 0.8 %update_grad.1 = f32[64,1024]{1,0:T(8,128)} custom-call(f32[32,128]{1,0:T(8,128)S(1)} %bitcast.31, f32[64,1024]{1,0:T(8,128)S(1)} %rotate_back.1.unrot_ref), custom_call_target="tpu_custom_call" | custom-call | tf_op jit(solution)/shard_map/update_grad/pallas_call | solution.py:329
  59.4 0.9 %place_own.1.refs_3_ = bf16[512,1024]{1,0:T(8,128)(2,1)} custom-call(bf16[64,1024]{1,0:T(8,128)(2,1)S(1)} %new_weights.1.refs_0_, bf16[64,1024]{1,0:T(8,128)(2,1)S(1)} %collective-permute-done.9.refs_1_, bf16[64,1024]{1,0:T(8,128)(2,1)S(1)} %collective-permute-done.10.refs_2_, bf16[64,1024]{1,0:T(8,128)(2,1)S(1)} %collective-permute-done.11.refs_3_, ...), custom_call_target="tpu_custom_call" | custom-call | tf_op jit(solution)/shard_map/place_own/pallas_call | solution.py:211
  61.3 1.2 %collective-permute-done.6.refs_0_ = bf16[64,1024]{1,0:T(8,128)(2,1)S(1)} collective-permute-done((bf16[64,1024]{1,0:T(8,128)(2,1)S(1)}, bf16[64,1024]{1,0:T(8,128)(2,1)S(1)}, u32[]{:S(2)}, u32[]{:S(2)}) %collective-permute-start.6) | collective-permute-done | bytes 131104 | tf_op jit(solution)/shard_map/ppermute | solution.py:184
  62.5 0.8 %place_far.1 = bf16[512,1024]{1,0:T(8,128)(2,1)} custom-call(bf16[64,1024]{1,0:T(8,128)(2,1)S(1)} %collective-permute-done.6.refs_0_, bf16[64,1024]{1,0:T(8,128)(2,1)S(1)} %collective-permute-done.7.refs_1_, bf16[64,1024]{1,0:T(8,128)(2,1)S(1)} %collective-permute-done.8.refs_2_, bf16[512,1024]{1,0:T(8,128)(2,1)} %place_own.1.refs_3_), custom_call_target="tpu_custom_call", output_to_operand_aliasing={{}: (3, {})} | custom-call | tf_op jit(solution)/shard_map/place_far/pallas_call | solution.py:211
  (30 shorter events, 4.3 us)
Async XLA Ops:
  0.6 1.2 %copy-start = (bf16[1,1,512,1024]{3,2,1,0:T(8,128)(2,1)S(1)}, bf16[1,1,512,1024]{3,2,1,0:T(8,128)(2,1)}, u32[]{:S(2)}) copy-start(bf16[1,1,512,1024]{3,2,1,0:T(8,128)(2,1)} %param.5) | copy-start | bytes 3145732
  1.9 8.1 %copy-start.1 = (bf16[1,1,512,1024]{3,2,1,0:T(8,128)(2,1)S(1)}, bf16[1,1,512,1024]{3,2,1,0:T(8,128)(2,1)}, u32[]{:S(2)}) copy-start(bf16[1,1,512,1024]{3,2,1,0:T(8,128)(2,1)} %param.5) | copy-start | bytes 3145732
  2.7 13.7 %all-to-all-start = ((f32[8,1,128]{2,1,0:T(1,128)}), f32[8,1,128]{2,1,0:T(1,128)S(1)}, u32[]{:S(2)}, u32[]{:S(2)}) async-start(f32[8,1,128]{2,1,0:T(1,128)} %bitcast.6), calls=%async_computation | async-start | bytes 8192 | tf_op jit(solution)/shard_map/all_to_all | solution.py:273
  10.0 9.4 %collective-permute-start.1 = (bf16[2,64,1024]{2,1,0:T(8,128)(2,1)S(1)}, bf16[2,64,1024]{2,1,0:T(8,128)(2,1)S(1)}, u32[]{:S(2)}, u32[]{:S(2)}) collective-permute-start(bf16[2,64,1024]{2,1,0:T(8,128)(2,1)S(1)} %get-tuple-element.26), channel_id=1, source_target_pairs={{0,8},{4,12},{8,0},{12,4},{16,24},{20,28},{24,16},{28,20},{1,9},{5... | collective-permute-start | bytes 786440 | tf_op jit(solution)/shard_map/ppermute | solution.py:184
  12.1 12.1 %collective-permute-start = (bf16[2,64,1024]{2,1,0:T(8,128)(2,1)S(1)}, bf16[2,64,1024]{2,1,0:T(8,128)(2,1)S(1)}, u32[]{:S(2)}, u32[]{:S(2)}) collective-permute-start(bf16[2,64,1024]{2,1,0:T(8,128)(2,1)S(1)} %get-tuple-element.27), channel_id=1, source_target_pairs={{0,4},{4,0},{8,12},{12,8},{16,20},{20,16},{24,28},{28,24},{1,5},{5... | collective-permute-start | bytes 786440 | tf_op jit(solution)/shard_map/ppermute | solution.py:184
  13.6 11.0 %collective-permute-start.3 = (bf16[64,1024]{1,0:T(8,128)(2,1)S(1)}, bf16[64,1024]{1,0:T(8,128)(2,1)S(1)}, u32[]{:S(2)}, u32[]{:S(2)}) collective-permute-start(bf16[64,1024]{1,0:T(8,128)(2,1)S(1)} %dynamic-slice_bitcast_fusion.3), channel_id=1, source_target_pairs={{0,12},{4,8},{8,4},{12,0},{16,28},{20,24},{24,20},{28,16},{1,13},{... | collective-permute-start | bytes 393224 | tf_op jit(solution)/shard_map/ppermute | solution.py:184
  16.4 7.7 %copy-start.2 = (bf16[256,256]{1,0:T(8,128)(2,1)S(1)}, bf16[256,256]{1,0:T(8,128)(2,1)}, u32[]{:S(2)}) copy-start(bf16[256,256]{1,0:T(8,128)(2,1)} %constant.37.clone.refs_6_.refs_5_.matrix_ref) | copy-start | bytes 393220
  16.4 7.7 %copy-start.5 = (s32[1,1024]{1,0:T(1,128)S(1)}, s32[1,1024]{1,0:T(1,128)}, u32[]{:S(2)}) copy-start(s32[1,1024]{1,0:T(1,128)} %sign_ref.1) | copy-start | bytes 12292
  16.4 10.7 %collective-permute-start.2 = (bf16[64,1024]{1,0:T(8,128)(2,1)S(1)}, bf16[64,1024]{1,0:T(8,128)(2,1)S(1)}, u32[]{:S(2)}, u32[]{:S(2)}) collective-permute-start(bf16[64,1024]{1,0:T(8,128)(2,1)S(1)} %dynamic-slice_bitcast_fusion.4), channel_id=1, source_target_pairs={{0,12},{4,8},{8,4},{12,0},{16,28},{20,24},{24,20},{28,16},{1,13},{... | collective-permute-start | bytes 393224 | tf_op jit(solution)/shard_map/ppermute | solution.py:184
  24.9 7.1 %collective-permute-start.4 = (s16[64,1024]{1,0:T(8,128)(2,1)S(1)}, s16[64,1024]{1,0:T(8,128)(2,1)S(1)}, u32[]{:S(2)}, u32[]{:S(2)}) collective-permute-start(s16[64,1024]{1,0:T(8,128)(2,1)S(1)} %proxy_blocks.1), channel_id=1, source_target_pairs={{0,16},{4,20},{8,24},{12,28},{16,0},{20,4},{24,8},{28,12},{1,17},{... | collective-permute-start | bytes 393224 | tf_op jit(solution)/shard_map/ppermute | solution.py:184
  32.7 12.6 %all-to-all-start.1 = ((f32[32,1,128]{2,1,0:T(1,128)}), f32[32,1,128]{2,1,0:T(1,128)S(1)}, u32[]{:S(2)}, u32[]{:S(2)}) async-start(f32[32,1,128]{2,1,0:T(1,128)} %get-tuple-element.24), calls=%async_computation.1 | async-start | bytes 32768 | tf_op jit(solution)/shard_map/all_to_all | solution.py:320
  38.3 7.1 %copy-start.3 = (bf16[1,64,1024]{2,1,0:T(8,128)(2,1)S(1)}, bf16[1,64,1024]{2,1,0:T(8,128)(2,1)}, u32[]{:S(2)}) copy-start(bf16[1,64,1024]{2,1,0:T(8,128)(2,1)} %param.7) | copy-start | bytes 393220
  38.3 7.1 %copy-start.4 = (bf16[1,64,1024]{2,1,0:T(8,128)(2,1)S(1)}, bf16[1,64,1024]{2,1,0:T(8,128)(2,1)}, u32[]{:S(2)}) copy-start(bf16[1,64,1024]{2,1,0:T(8,128)(2,1)} %param.8) | copy-start | bytes 393220
  45.5 6.9 %collective-permute-start.10 = (bf16[64,1024]{1,0:T(8,128)(2,1)S(1)}, bf16[64,1024]{1,0:T(8,128)(2,1)S(1)}, u32[]{:S(2)}, u32[]{:S(2)}) collective-permute-start(bf16[64,1024]{1,0:T(8,128)(2,1)S(1)} %new_weights.1.refs_0_), channel_id=1, source_target_pairs={{0,8},{4,12},{8,0},{12,4},{16,24},{20,28},{24,16},{28,20},{1,9},{5... | collective-permute-start | bytes 393224 | tf_op jit(solution)/shard_map/ppermute | solution.py:184
  46.2 8.6 %collective-permute-start.5 = (bf16[64,1024]{1,0:T(8,128)(2,1)S(1)}, bf16[64,1024]{1,0:T(8,128)(2,1)S(1)}, u32[]{:S(2)}, u32[]{:S(2)}) collective-permute-start(bf16[64,1024]{1,0:T(8,128)(2,1)S(1)} %new_weights.1.refs_0_), channel_id=1, source_target_pairs={{0,16},{4,20},{8,24},{12,28},{16,0},{20,4},{24,8},{28,12},{1,17},{... | collective-permute-start | bytes 393224 | tf_op jit(solution)/shard_map/ppermute | solution.py:184
  46.7 12.4 %collective-permute-start.9 = (bf16[64,1024]{1,0:T(8,128)(2,1)S(1)}, bf16[64,1024]{1,0:T(8,128)(2,1)S(1)}, u32[]{:S(2)}, u32[]{:S(2)}) collective-permute-start(bf16[64,1024]{1,0:T(8,128)(2,1)S(1)} %new_weights.1.refs_0_), channel_id=1, source_target_pairs={{0,4},{4,0},{8,12},{12,8},{16,20},{20,16},{24,28},{28,24},{1,5},{5... | collective-permute-start | bytes 393224 | tf_op jit(solution)/shard_map/ppermute | solution.py:184
  52.5 6.9 %collective-permute-start.11 = (bf16[64,1024]{1,0:T(8,128)(2,1)S(1)}, bf16[64,1024]{1,0:T(8,128)(2,1)S(1)}, u32[]{:S(2)}, u32[]{:S(2)}) collective-permute-start(bf16[64,1024]{1,0:T(8,128)(2,1)S(1)} %collective-permute-done.10.refs_2_), channel_id=1, source_target_pairs={{0,4},{4,0},{8,12},{12,8},{16,20},{20,16},{24,28},{28,24},{1,5},{5... | collective-permute-start | bytes 393224 | tf_op jit(solution)/shard_map/ppermute | solution.py:184
  54.8 6.0 %collective-permute-start.8 = (bf16[64,1024]{1,0:T(8,128)(2,1)S(1)}, bf16[64,1024]{1,0:T(8,128)(2,1)S(1)}, u32[]{:S(2)}, u32[]{:S(2)}) collective-permute-start(bf16[64,1024]{1,0:T(8,128)(2,1)S(1)} %collective-permute-done.5.refs_4_), channel_id=1, source_target_pairs={{0,12},{4,8},{8,4},{12,0},{16,28},{20,24},{24,20},{28,16},{1,13},{... | collective-permute-start | bytes 393224 | tf_op jit(solution)/shard_map/ppermute | solution.py:184
  54.8 6.4 %collective-permute-start.7 = (bf16[64,1024]{1,0:T(8,128)(2,1)S(1)}, bf16[64,1024]{1,0:T(8,128)(2,1)S(1)}, u32[]{:S(2)}, u32[]{:S(2)}) collective-permute-start(bf16[64,1024]{1,0:T(8,128)(2,1)S(1)} %collective-permute-done.5.refs_4_), channel_id=1, source_target_pairs={{0,8},{4,12},{8,0},{12,4},{16,24},{20,28},{24,16},{28,20},{1,9},{5... | collective-permute-start | bytes 393224 | tf_op jit(solution)/shard_map/ppermute | solution.py:184
  56.9 5.6 %collective-permute-start.6 = (bf16[64,1024]{1,0:T(8,128)(2,1)S(1)}, bf16[64,1024]{1,0:T(8,128)(2,1)S(1)}, u32[]{:S(2)}, u32[]{:S(2)}) collective-permute-start(bf16[64,1024]{1,0:T(8,128)(2,1)S(1)} %collective-permute-done.5.refs_4_), channel_id=1, source_target_pairs={{0,4},{4,0},{8,12},{12,8},{16,20},{20,16},{24,28},{28,24},{1,5},{5... | collective-permute-start | bytes 393224 | tf_op jit(solution)/shard_map/ppermute | solution.py:184

commit v24 on v19

--- a/solution.py
+++ b/solution.py
@@ -234,7 +234,8 @@
     own = [(m, 0, piece) for m, piece in own.items()]
     spread = [(near + m, 0, swap(far, m)) for m in range(1, near)]
     out = place_pieces(own + [(near, 0, far)], owned, replicas, None, "place_own")
-    out = place_pieces(spread, owned, replicas, out, "place_far")
+    out = place_pieces(spread[1:], owned, replicas, out, "place_far")
+    out = place_pieces(spread[:1], owned, replicas, out, "place_last")
     return out.reshape(1, replicas * owned, width)
 
 

time: 56.5 us -> 56.4 us (level)
  waiting for transfers between devices: 25.8 us -> 25.1 us
  Pallas kernels: 5.77 us -> 6.38 us
    ppermute x12, waiting for transfers between devices: 15.6 us -> 14.9 us  [swap(): return lax.ppermute(value, 'dp', [(i, i ^ mask) for i in range(size)])]
    pallas_call x2 -> x3, Pallas kernels: 1.63 us -> 2.25 us  [place_pieces(): pl.pallas_call(functools.partial(place_kernel, places, owned), in_specs=s...]
  transfers between devices with their start and end apart: 14 -> 14, of which waited for: 9 -> 9; matrix products, arithmetic and copies ran while one was open for 0% -> 0% of each run, Pallas kernels for 7% -> 9%
where the time goes in v24:
time: 56.4 us; the launch traced here: 56.2 us
  waiting for transfers between devices  25.1 us (45%)
  starting transfers between devices  22.7 us (40%)
  Pallas kernels  6.38 us (11%)
  local copies, waits for them, and re-layouts  1.21 us (2%)
  between operations  0.81 us (1%)
    ppermute x12, waiting for transfers between devices, swap(): return lax.ppermute(value, 'dp', [(i, i ^ mask) for i in range(size)])  14.9 us
    ppermute x12, starting transfers between devices, swap(): return lax.ppermute(value, 'dp', [(i, i ^ mask) for i in range(size)])  14 us
    all_to_all x1, waiting for transfers between devices, on_device(): lax.all_to_all(squares, ('dp', 'expert'), split_axis=0, concat_axis=0, ti...  6.72 us
    all_to_all x1, starting transfers between devices, on_device(): lax.all_to_all(sums.reshape(replicas, 1, 2 * owned), 'dp', split_axis=0,...  6.18 us
    all_to_all x1, waiting for transfers between devices, on_device(): lax.all_to_all(sums.reshape(replicas, 1, 2 * owned), 'dp', split_axis=0,...  3.44 us
    all_to_all x1, starting transfers between devices, on_device(): lax.all_to_all(squares, ('dp', 'expert'), split_axis=0, concat_axis=0, ti...  2.54 us
    pallas_call x3, Pallas kernels, place_pieces(): pl.pallas_call(functools.partial(place_kernel, places, owned), in_specs=s...  2.25 us
    reshape x2, local copies, waits for them, and re-layouts, pair_of(): lax.dynamic_slice_in_dim(source, index % near, 1, 1)  1.17 us
  transfers between devices with their start and end apart: 14, of which 9 were waited for; matrix products, arithmetic and copies ran while one was open for 0% of the time, Pallas kernels for 9%

profile of v24, /device:TPU:0, one launch (start us, length us, event | category | flops | bytes accessed | tf_op | source)
XLA Modules:
  0.0 56.2 jit_solution(13696248779182733407)
XLA Ops:
  0.7 1.2 %dynamic-slice_bitcast_fusion.1 = (bf16[2,64,1024]{2,1,0:T(8,128)(2,1)S(1)}, bf16[2,64,1024]{2,1,0:T(8,128)(2,1)S(1)}) fusion(bf16[2,4,64,1024]{3,2,1,0:T(8,128)(2,1)} %bitcast.24, s32[]{:T(128)S(6)} %select_n.33, s32[]{:T(128)S(6)} %select_n.31), kind=kLoop, calls=%fused_computation.1 | loop fusion | bytes 1048584 | tf_op jit(solution)/shard_map/reshape | solution.py:256
  1.8 3.1 %collective-permute-start.1 = (bf16[2,64,1024]{2,1,0:T(8,128)(2,1)S(1)}, bf16[2,64,1024]{2,1,0:T(8,128)(2,1)S(1)}, u32[]{:S(2)}, u32[]{:S(2)}) collective-permute-start(bf16[2,64,1024]{2,1,0:T(8,128)(2,1)S(1)} %get-tuple-element.24), channel_id=1, source_target_pairs={{0,8},{4,12},{8,0},{12,4},{16,24},{20,28},{24,16},{28,20},{1,9},{5... | collective-permute-start | bytes 786440 | tf_op jit(solution)/shard_map/ppermute | solution.py:184
  4.9 1.5 %collective-permute-start = (bf16[2,64,1024]{2,1,0:T(8,128)(2,1)S(1)}, bf16[2,64,1024]{2,1,0:T(8,128)(2,1)S(1)}, u32[]{:S(2)}, u32[]{:S(2)}) collective-permute-start(bf16[2,64,1024]{2,1,0:T(8,128)(2,1)S(1)} %get-tuple-element.25), channel_id=1, source_target_pairs={{0,4},{4,0},{8,12},{12,8},{16,20},{20,16},{24,28},{28,24},{1,5},{5... | collective-permute-start | bytes 786440 | tf_op jit(solution)/shard_map/ppermute | solution.py:184
  6.4 0.9 %sum_squares.1 = f32[2,4,1,128]{3,2,1,0:T(1,128)} custom-call(bf16[2,4,64,1024]{3,2,1,0:T(8,128)(2,1)S(1)} %bitcast.25), custom_call_target="tpu_custom_call" | custom-call | tf_op jit(solution)/shard_map/sum_squares/pallas_call | solution.py:266
  7.4 6.2 %all-to-all-start = ((f32[8,1,128]{2,1,0:T(1,128)}), f32[8,1,128]{2,1,0:T(1,128)S(1)}, u32[]{:S(2)}, u32[]{:S(2)}) async-start(f32[8,1,128]{2,1,0:T(1,128)} %bitcast.8), calls=%async_computation | async-start | bytes 8192 | tf_op jit(solution)/shard_map/all_to_all | solution.py:274
  13.6 2.9 %collective-permute-start.2 = (bf16[64,1024]{1,0:T(8,128)(2,1)S(1)}, bf16[64,1024]{1,0:T(8,128)(2,1)S(1)}, u32[]{:S(2)}, u32[]{:S(2)}) collective-permute-start(bf16[64,1024]{1,0:T(8,128)(2,1)S(1)} %get-tuple-element.23), channel_id=1, source_target_pairs={{0,12},{4,8},{8,4},{12,0},{16,28},{20,24},{24,20},{28,16},{1,13},{... | collective-permute-start | bytes 393224 | tf_op jit(solution)/shard_map/ppermute | solution.py:184
  16.6 3.4 %all-to-all-done = f32[8,1,128]{2,1,0:T(1,128)S(1)} async-done(((f32[8,1,128]{2,1,0:T(1,128)}), f32[8,1,128]{2,1,0:T(1,128)S(1)}, u32[]{:S(2)}, u32[]{:S(2)}) %all-to-all-start) | async-done | bytes 4128 | tf_op jit(solution)/shard_map/all_to_all | solution.py:274
  20.8 0.6 %collective-permute-start.4 = (s16[64,1024]{1,0:T(8,128)(2,1)S(1)}, s16[64,1024]{1,0:T(8,128)(2,1)S(1)}, u32[]{:S(2)}, u32[]{:S(2)}) collective-permute-start(s16[64,1024]{1,0:T(8,128)(2,1)S(1)} %proxy_blocks.1), channel_id=1, source_target_pairs={{0,16},{4,20},{8,24},{12,28},{16,0},{20,4},{24,8},{28,12},{1,17},{... | collective-permute-start | bytes 393224 | tf_op jit(solution)/shard_map/ppermute | solution.py:184
  21.4 0.6 owner_blocks.1
  22.0 6.1 %collective-permute-done.4.far_ref = s16[64,1024]{1,0:T(8,128)(2,1)S(1)} collective-permute-done((s16[64,1024]{1,0:T(8,128)(2,1)S(1)}, s16[64,1024]{1,0:T(8,128)(2,1)S(1)}, u32[]{:S(2)}, u32[]{:S(2)}) %collective-permute-start.4) | collective-permute-done | bytes 131104 | tf_op jit(solution)/shard_map/ppermute | solution.py:184
  28.1 0.7 %finish_blocks.1 = (f32[64,1024]{1,0:T(8,128)S(1)}, f32[32,1,128]{2,1,0:T(1,128)}) custom-call(f32[64,1024]{1,0:T(8,128)S(1)} %get-tuple-element.14.near_ref, s16[64,1024]{1,0:T(8,128)(2,1)S(1)} %collective-permute-done.4.far_ref, f32[64,128]{1,0:T(8,128)S(1)} %get-tuple-element.18.scale_ref, f32[64,128]{1,0:T(8,128)S(1)} %get-tuple-element.19.step_ref), custom_call_target="tpu_custom_call" | custom-call | tf_op jit(solution)/shard_map/finish_blocks/pallas_call | solution.py:304
  28.8 2.5 %all-to-all-start.1 = ((f32[32,1,128]{2,1,0:T(1,128)}), f32[32,1,128]{2,1,0:T(1,128)S(1)}, u32[]{:S(2)}, u32[]{:S(2)}) async-start(f32[32,1,128]{2,1,0:T(1,128)} %get-tuple-element.20), calls=%async_computation.1 | async-start | bytes 32768 | tf_op jit(solution)/shard_map/all_to_all | solution.py:320
  31.7 6.7 %all-to-all-done.1 = f32[32,1,128]{2,1,0:T(1,128)S(1)} async-done(((f32[32,1,128]{2,1,0:T(1,128)}), f32[32,1,128]{2,1,0:T(1,128)S(1)}, u32[]{:S(2)}, u32[]{:S(2)}) %all-to-all-start.1) | async-done | bytes 16416 | tf_op jit(solution)/shard_map/all_to_all | solution.py:320
  38.6 0.6 %collective-permute-start.10 = (bf16[64,1024]{1,0:T(8,128)(2,1)S(1)}, bf16[64,1024]{1,0:T(8,128)(2,1)S(1)}, u32[]{:S(2)}, u32[]{:S(2)}) collective-permute-start(bf16[64,1024]{1,0:T(8,128)(2,1)S(1)} %new_weights.1.refs_0_), channel_id=1, source_target_pairs={{0,8},{4,12},{8,0},{12,4},{16,24},{20,28},{24,16},{28,20},{1,9},{5... | collective-permute-start | bytes 393224 | tf_op jit(solution)/shard_map/ppermute | solution.py:184
  39.2 0.6 collective-permute-start.5
  40.3 5.2 %collective-permute-done.10.refs_2_ = bf16[64,1024]{1,0:T(8,128)(2,1)S(1)} collective-permute-done((bf16[64,1024]{1,0:T(8,128)(2,1)S(1)}, bf16[64,1024]{1,0:T(8,128)(2,1)S(1)}, u32[]{:S(2)}, u32[]{:S(2)}) %collective-permute-start.10) | collective-permute-done | bytes 131104 | tf_op jit(solution)/shard_map/ppermute | solution.py:184
  45.5 0.5 collective-permute-start.11
  46.1 1.8 %collective-permute-done.5.refs_4_ = bf16[64,1024]{1,0:T(8,128)(2,1)S(1)} collective-permute-done((bf16[64,1024]{1,0:T(8,128)(2,1)S(1)}, bf16[64,1024]{1,0:T(8,128)(2,1)S(1)}, u32[]{:S(2)}, u32[]{:S(2)}) %collective-permute-start.5) | collective-permute-done | bytes 131104 | tf_op jit(solution)/shard_map/ppermute | solution.py:184
  47.8 2.1 %collective-permute-start.7 = (bf16[64,1024]{1,0:T(8,128)(2,1)S(1)}, bf16[64,1024]{1,0:T(8,128)(2,1)S(1)}, u32[]{:S(2)}, u32[]{:S(2)}) collective-permute-start(bf16[64,1024]{1,0:T(8,128)(2,1)S(1)} %collective-permute-done.5.refs_4_), channel_id=1, source_target_pairs={{0,8},{4,12},{8,0},{12,4},{16,24},{20,28},{24,16},{28,20},{1,9},{5... | collective-permute-start | bytes 393224 | tf_op jit(solution)/shard_map/ppermute | solution.py:184
  49.9 1.4 %collective-permute-start.6 = (bf16[64,1024]{1,0:T(8,128)(2,1)S(1)}, bf16[64,1024]{1,0:T(8,128)(2,1)S(1)}, u32[]{:S(2)}, u32[]{:S(2)}) collective-permute-start(bf16[64,1024]{1,0:T(8,128)(2,1)S(1)} %collective-permute-done.5.refs_4_), channel_id=1, source_target_pairs={{0,4},{4,0},{8,12},{12,8},{16,20},{20,16},{24,28},{28,24},{1,5},{5... | collective-permute-start | bytes 393224 | tf_op jit(solution)/shard_map/ppermute | solution.py:184
  51.3 0.8 %update_grad.1 = f32[64,1024]{1,0:T(8,128)} custom-call(f32[32,128]{1,0:T(8,128)S(1)} %bitcast.29, f32[64,1024]{1,0:T(8,128)S(1)} %rotate_back.1.unrot_ref), custom_call_target="tpu_custom_call" | custom-call | tf_op jit(solution)/shard_map/update_grad/pallas_call | solution.py:329
  52.4 0.9 %place_own.1.refs_2_ = bf16[512,1024]{1,0:T(8,128)(2,1)} custom-call(bf16[64,1024]{1,0:T(8,128)(2,1)S(1)} %new_weights.1.refs_0_, bf16[64,1024]{1,0:T(8,128)(2,1)S(1)} %collective-permute-done.9.refs_1_, bf16[64,1024]{1,0:T(8,128)(2,1)S(1)} %collective-permute-done.10.refs_2_, bf16[64,1024]{1,0:T(8,128)(2,1)S(1)} %collective-permute-done.11.refs_3_, ...), custom_call_target="tpu_custom_call" | custom-call | tf_op jit(solution)/shard_map/place_own/pallas_call | solution.py:211
  54.3 0.7 %place_far.1.refs_1_ = bf16[512,1024]{1,0:T(8,128)(2,1)} custom-call(bf16[64,1024]{1,0:T(8,128)(2,1)S(1)} %collective-permute-done.7.refs_0_, bf16[64,1024]{1,0:T(8,128)(2,1)S(1)} %collective-permute-done.8.refs_1_, bf16[512,1024]{1,0:T(8,128)(2,1)} %place_own.1.refs_2_), custom_call_target="tpu_custom_call", output_to_operand_aliasing={{}: (2, {})} | custom-call | tf_op jit(solution)/shard_map/place_far/pallas_call | solution.py:211
  55.5 0.7 %place_last.1 = bf16[512,1024]{1,0:T(8,128)(2,1)} custom-call(bf16[64,1024]{1,0:T(8,128)(2,1)S(1)} %collective-permute-done.6.refs_0_, bf16[512,1024]{1,0:T(8,128)(2,1)} %place_far.1.refs_1_), custom_call_target="tpu_custom_call", output_to_operand_aliasing={{}: (1, {})} | custom-call | tf_op jit(solution)/shard_map/place_last/pallas_call | solution.py:211
  (28 shorter events, 3.7 us)
Async XLA Ops:
  0.6 5.8 %copy-start = (bf16[1,1,512,1024]{3,2,1,0:T(8,128)(2,1)S(1)}, bf16[1,1,512,1024]{3,2,1,0:T(8,128)(2,1)}, u32[]{:S(2)}) copy-start(bf16[1,1,512,1024]{3,2,1,0:T(8,128)(2,1)} %param.5) | copy-start | bytes 3145732
  1.8 18.2 %collective-permute-start.1 = (bf16[2,64,1024]{2,1,0:T(8,128)(2,1)S(1)}, bf16[2,64,1024]{2,1,0:T(8,128)(2,1)S(1)}, u32[]{:S(2)}, u32[]{:S(2)}) collective-permute-start(bf16[2,64,1024]{2,1,0:T(8,128)(2,1)S(1)} %get-tuple-element.24), channel_id=1, source_target_pairs={{0,8},{4,12},{8,0},{12,4},{16,24},{20,28},{24,16},{28,20},{1,9},{5... | collective-permute-start | bytes 786440 | tf_op jit(solution)/shard_map/ppermute | solution.py:184
  4.9 15.1 %collective-permute-start = (bf16[2,64,1024]{2,1,0:T(8,128)(2,1)S(1)}, bf16[2,64,1024]{2,1,0:T(8,128)(2,1)S(1)}, u32[]{:S(2)}, u32[]{:S(2)}) collective-permute-start(bf16[2,64,1024]{2,1,0:T(8,128)(2,1)S(1)} %get-tuple-element.25), channel_id=1, source_target_pairs={{0,4},{4,0},{8,12},{12,8},{16,20},{20,16},{24,28},{28,24},{1,5},{5... | collective-permute-start | bytes 786440 | tf_op jit(solution)/shard_map/ppermute | solution.py:184
  7.3 13.1 %collective-permute-start.3 = (bf16[64,1024]{1,0:T(8,128)(2,1)S(1)}, bf16[64,1024]{1,0:T(8,128)(2,1)S(1)}, u32[]{:S(2)}, u32[]{:S(2)}) collective-permute-start(bf16[64,1024]{1,0:T(8,128)(2,1)S(1)} %get-tuple-element.22), channel_id=1, source_target_pairs={{0,12},{4,8},{8,4},{12,0},{16,28},{20,24},{24,20},{28,16},{1,13},{... | collective-permute-start | bytes 393224 | tf_op jit(solution)/shard_map/ppermute | solution.py:184
  7.4 12.6 %all-to-all-start = ((f32[8,1,128]{2,1,0:T(1,128)}), f32[8,1,128]{2,1,0:T(1,128)S(1)}, u32[]{:S(2)}, u32[]{:S(2)}) async-start(f32[8,1,128]{2,1,0:T(1,128)} %bitcast.8), calls=%async_computation | async-start | bytes 8192 | tf_op jit(solution)/shard_map/all_to_all | solution.py:274
  13.6 7.8 %collective-permute-start.2 = (bf16[64,1024]{1,0:T(8,128)(2,1)S(1)}, bf16[64,1024]{1,0:T(8,128)(2,1)S(1)}, u32[]{:S(2)}, u32[]{:S(2)}) collective-permute-start(bf16[64,1024]{1,0:T(8,128)(2,1)S(1)} %get-tuple-element.23), channel_id=1, source_target_pairs={{0,12},{4,8},{8,4},{12,0},{16,28},{20,24},{24,20},{28,16},{1,13},{... | collective-permute-start | bytes 393224 | tf_op jit(solution)/shard_map/ppermute | solution.py:184
  16.5 3.5 %copy-start.1 = (bf16[256,256]{1,0:T(8,128)(2,1)S(1)}, bf16[256,256]{1,0:T(8,128)(2,1)}, u32[]{:S(2)}) copy-start(bf16[256,256]{1,0:T(8,128)(2,1)} %constant.37.clone.refs_6_.refs_5_.matrix_ref) | copy-start | bytes 393220
  16.5 3.5 %copy-start.4 = (s32[1,1024]{1,0:T(1,128)S(1)}, s32[1,1024]{1,0:T(1,128)}, u32[]{:S(2)}) copy-start(s32[1,1024]{1,0:T(1,128)} %sign_ref.1) | copy-start | bytes 12292
  20.8 7.3 %collective-permute-start.4 = (s16[64,1024]{1,0:T(8,128)(2,1)S(1)}, s16[64,1024]{1,0:T(8,128)(2,1)S(1)}, u32[]{:S(2)}, u32[]{:S(2)}) collective-permute-start(s16[64,1024]{1,0:T(8,128)(2,1)S(1)} %proxy_blocks.1), channel_id=1, source_target_pairs={{0,16},{4,20},{8,24},{12,28},{16,0},{20,4},{24,8},{28,12},{1,17},{... | collective-permute-start | bytes 393224 | tf_op jit(solution)/shard_map/ppermute | solution.py:184
  28.8 9.6 %all-to-all-start.1 = ((f32[32,1,128]{2,1,0:T(1,128)}), f32[32,1,128]{2,1,0:T(1,128)S(1)}, u32[]{:S(2)}, u32[]{:S(2)}) async-start(f32[32,1,128]{2,1,0:T(1,128)} %get-tuple-element.20), calls=%async_computation.1 | async-start | bytes 32768 | tf_op jit(solution)/shard_map/all_to_all | solution.py:320
  31.3 7.1 %copy-start.2 = (bf16[1,64,1024]{2,1,0:T(8,128)(2,1)S(1)}, bf16[1,64,1024]{2,1,0:T(8,128)(2,1)}, u32[]{:S(2)}) copy-start(bf16[1,64,1024]{2,1,0:T(8,128)(2,1)} %param.7) | copy-start | bytes 393220
  31.3 7.1 %copy-start.3 = (bf16[1,64,1024]{2,1,0:T(8,128)(2,1)S(1)}, bf16[1,64,1024]{2,1,0:T(8,128)(2,1)}, u32[]{:S(2)}) copy-start(bf16[1,64,1024]{2,1,0:T(8,128)(2,1)} %param.8) | copy-start | bytes 393220
  38.6 6.9 %collective-permute-start.10 = (bf16[64,1024]{1,0:T(8,128)(2,1)S(1)}, bf16[64,1024]{1,0:T(8,128)(2,1)S(1)}, u32[]{:S(2)}, u32[]{:S(2)}) collective-permute-start(bf16[64,1024]{1,0:T(8,128)(2,1)S(1)} %new_weights.1.refs_0_), channel_id=1, source_target_pairs={{0,8},{4,12},{8,0},{12,4},{16,24},{20,28},{24,16},{28,20},{1,9},{5... | collective-permute-start | bytes 393224 | tf_op jit(solution)/shard_map/ppermute | solution.py:184
  39.2 8.6 %collective-permute-start.5 = (bf16[64,1024]{1,0:T(8,128)(2,1)S(1)}, bf16[64,1024]{1,0:T(8,128)(2,1)S(1)}, u32[]{:S(2)}, u32[]{:S(2)}) collective-permute-start(bf16[64,1024]{1,0:T(8,128)(2,1)S(1)} %new_weights.1.refs_0_), channel_id=1, source_target_pairs={{0,16},{4,20},{8,24},{12,28},{16,0},{20,4},{24,8},{28,12},{1,17},{... | collective-permute-start | bytes 393224 | tf_op jit(solution)/shard_map/ppermute | solution.py:184
  39.8 12.4 %collective-permute-start.9 = (bf16[64,1024]{1,0:T(8,128)(2,1)S(1)}, bf16[64,1024]{1,0:T(8,128)(2,1)S(1)}, u32[]{:S(2)}, u32[]{:S(2)}) collective-permute-start(bf16[64,1024]{1,0:T(8,128)(2,1)S(1)} %new_weights.1.refs_0_), channel_id=1, source_target_pairs={{0,4},{4,0},{8,12},{12,8},{16,20},{20,16},{24,28},{28,24},{1,5},{5... | collective-permute-start | bytes 393224 | tf_op jit(solution)/shard_map/ppermute | solution.py:184
  45.5 6.9 %collective-permute-start.11 = (bf16[64,1024]{1,0:T(8,128)(2,1)S(1)}, bf16[64,1024]{1,0:T(8,128)(2,1)S(1)}, u32[]{:S(2)}, u32[]{:S(2)}) collective-permute-start(bf16[64,1024]{1,0:T(8,128)(2,1)S(1)} %collective-permute-done.10.refs_2_), channel_id=1, source_target_pairs={{0,4},{4,0},{8,12},{12,8},{16,20},{20,16},{24,28},{28,24},{1,5},{5... | collective-permute-start | bytes 393224 | tf_op jit(solution)/shard_map/ppermute | solution.py:184
  47.8 6.0 %collective-permute-start.8 = (bf16[64,1024]{1,0:T(8,128)(2,1)S(1)}, bf16[64,1024]{1,0:T(8,128)(2,1)S(1)}, u32[]{:S(2)}, u32[]{:S(2)}) collective-permute-start(bf16[64,1024]{1,0:T(8,128)(2,1)S(1)} %collective-permute-done.5.refs_4_), channel_id=1, source_target_pairs={{0,12},{4,8},{8,4},{12,0},{16,28},{20,24},{24,20},{28,16},{1,13},{... | collective-permute-start | bytes 393224 | tf_op jit(solution)/shard_map/ppermute | solution.py:184
  47.8 6.4 %collective-permute-start.7 = (bf16[64,1024]{1,0:T(8,128)(2,1)S(1)}, bf16[64,1024]{1,0:T(8,128)(2,1)S(1)}, u32[]{:S(2)}, u32[]{:S(2)}) collective-permute-start(bf16[64,1024]{1,0:T(8,128)(2,1)S(1)} %collective-permute-done.5.refs_4_), channel_id=1, source_target_pairs={{0,8},{4,12},{8,0},{12,4},{16,24},{20,28},{24,16},{28,20},{1,9},{5... | collective-permute-start | bytes 393224 | tf_op jit(solution)/shard_map/ppermute | solution.py:184
  49.9 5.6 %collective-permute-start.6 = (bf16[64,1024]{1,0:T(8,128)(2,1)S(1)}, bf16[64,1024]{1,0:T(8,128)(2,1)S(1)}, u32[]{:S(2)}, u32[]{:S(2)}) collective-permute-start(bf16[64,1024]{1,0:T(8,128)(2,1)S(1)} %collective-permute-done.5.refs_4_), channel_id=1, source_target_pairs={{0,4},{4,0},{8,12},{12,8},{16,20},{20,16},{24,28},{28,24},{1,5},{5... | collective-permute-start | bytes 393224 | tf_op jit(solution)/shard_map/ppermute | solution.py:184

commit v25 on v19

--- a/solution.py
+++ b/solution.py
@@ -54,9 +54,11 @@
     shape = (2 * owned, 2 * owned)
     row, lane = (lax.broadcasted_iota(jnp.int32, shape, axis) for axis in (0, 1))
     for j in range(near):
-        rows = x_ref[:, j].reshape(2 * owned, width).astype(jnp.float32)
-        squares = jnp.sum(rows * rows, axis=1, keepdims=True)
-        line = jnp.sum(jnp.where(row == lane, squares, 0.0), axis=0, keepdims=True)
+        rows = x_ref[:, j].reshape(2 * owned, width)
+        products = lax.dot_general(
+            rows, rows, (((1,), (1,)), ((), ())), preferred_element_type=jnp.float32
+        )
+        line = jnp.sum(jnp.where(row == lane, products, 0.0), axis=0, keepdims=True)
         sums_ref[0, j] = line
         sums_ref[1, j] = line
 

time: 56.5 us -> 56.7 us (level)
  transfers between devices with their start and end apart: 14 -> 14, of which waited for: 9 -> 9; matrix products, arithmetic and copies ran while one was open for 0% -> 0% of each run, Pallas kernels for 7% -> 8%
where the time goes in v25:
time: 56.7 us; the launch traced here: 56.4 us
  waiting for transfers between devices  25.8 us (46%)
  starting transfers between devices  22.7 us (40%)
  Pallas kernels  5.94 us (10%)
  local copies, waits for them, and re-layouts  1.21 us (2%)
  between operations  0.8 us (1%)
    ppermute x12, waiting for transfers between devices, swap(): return lax.ppermute(value, 'dp', [(i, i ^ mask) for i in range(size)])  15.6 us
    ppermute x12, starting transfers between devices, swap(): return lax.ppermute(value, 'dp', [(i, i ^ mask) for i in range(size)])  14 us
    all_to_all x1, waiting for transfers between devices, on_device(): lax.all_to_all(squares, ('dp', 'expert'), split_axis=0, concat_axis=0, ti...  6.72 us
    all_to_all x1, starting transfers between devices, on_device(): lax.all_to_all(sums.reshape(replicas, 1, 2 * owned), 'dp', split_axis=0,...  6.18 us
    all_to_all x1, waiting for transfers between devices, on_device(): lax.all_to_all(sums.reshape(replicas, 1, 2 * owned), 'dp', split_axis=0,...  3.44 us
    all_to_all x1, starting transfers between devices, on_device(): lax.all_to_all(squares, ('dp', 'expert'), split_axis=0, concat_axis=0, ti...  2.54 us
    pallas_call x2, Pallas kernels, place_pieces(): pl.pallas_call(functools.partial(place_kernel, places, owned), in_specs=s...  1.63 us
    reshape x2, local copies, waits for them, and re-layouts, pair_of(): lax.dynamic_slice_in_dim(source, index % near, 1, 1)  1.17 us
  transfers between devices with their start and end apart: 14, of which 9 were waited for; matrix products, arithmetic and copies ran while one was open for 0% of the time, Pallas kernels for 8%

profile of v25, /device:TPU:0, one launch (start us, length us, event | category | flops | bytes accessed | tf_op | source)
XLA Modules:
  0.0 56.4 jit_solution(1996666450412258107)
XLA Ops:
  0.7 1.2 %dynamic-slice_bitcast_fusion.1 = (bf16[2,64,1024]{2,1,0:T(8,128)(2,1)S(1)}, bf16[2,64,1024]{2,1,0:T(8,128)(2,1)S(1)}) fusion(bf16[2,4,64,1024]{3,2,1,0:T(8,128)(2,1)} %bitcast.24, s32[]{:T(128)S(6)} %select_n.33, s32[]{:T(128)S(6)} %select_n.31), kind=kLoop, calls=%fused_computation.1 | loop fusion | bytes 1048584 | tf_op jit(solution)/shard_map/reshape | solution.py:257
  1.8 3.1 %collective-permute-start.1 = (bf16[2,64,1024]{2,1,0:T(8,128)(2,1)S(1)}, bf16[2,64,1024]{2,1,0:T(8,128)(2,1)S(1)}, u32[]{:S(2)}, u32[]{:S(2)}) collective-permute-start(bf16[2,64,1024]{2,1,0:T(8,128)(2,1)S(1)} %get-tuple-element.24), channel_id=1, source_target_pairs={{0,8},{4,12},{8,0},{12,4},{16,24},{20,28},{24,16},{28,20},{1,9},{5... | collective-permute-start | bytes 786440 | tf_op jit(solution)/shard_map/ppermute | solution.py:186
  4.9 1.5 %collective-permute-start = (bf16[2,64,1024]{2,1,0:T(8,128)(2,1)S(1)}, bf16[2,64,1024]{2,1,0:T(8,128)(2,1)S(1)}, u32[]{:S(2)}, u32[]{:S(2)}) collective-permute-start(bf16[2,64,1024]{2,1,0:T(8,128)(2,1)S(1)} %get-tuple-element.25), channel_id=1, source_target_pairs={{0,4},{4,0},{8,12},{12,8},{16,20},{20,16},{24,28},{28,24},{1,5},{5... | collective-permute-start | bytes 786440 | tf_op jit(solution)/shard_map/ppermute | solution.py:186
  6.4 1.0 %sum_squares.1 = f32[2,4,1,128]{3,2,1,0:T(1,128)} custom-call(bf16[2,4,64,1024]{3,2,1,0:T(8,128)(2,1)S(1)} %bitcast.25), custom_call_target="tpu_custom_call" | custom-call | tf_op jit(solution)/shard_map/sum_squares/pallas_call | solution.py:267
  7.6 6.2 %all-to-all-start = ((f32[8,1,128]{2,1,0:T(1,128)}), f32[8,1,128]{2,1,0:T(1,128)S(1)}, u32[]{:S(2)}, u32[]{:S(2)}) async-start(f32[8,1,128]{2,1,0:T(1,128)} %bitcast.8), calls=%async_computation | async-start | bytes 8192 | tf_op jit(solution)/shard_map/all_to_all | solution.py:275
  13.8 2.9 %collective-permute-start.2 = (bf16[64,1024]{1,0:T(8,128)(2,1)S(1)}, bf16[64,1024]{1,0:T(8,128)(2,1)S(1)}, u32[]{:S(2)}, u32[]{:S(2)}) collective-permute-start(bf16[64,1024]{1,0:T(8,128)(2,1)S(1)} %get-tuple-element.23), channel_id=1, source_target_pairs={{0,12},{4,8},{8,4},{12,0},{16,28},{20,24},{24,20},{28,16},{1,13},{... | collective-permute-start | bytes 393224 | tf_op jit(solution)/shard_map/ppermute | solution.py:186
  16.7 3.4 %all-to-all-done = f32[8,1,128]{2,1,0:T(1,128)S(1)} async-done(((f32[8,1,128]{2,1,0:T(1,128)}), f32[8,1,128]{2,1,0:T(1,128)S(1)}, u32[]{:S(2)}, u32[]{:S(2)}) %all-to-all-start) | async-done | bytes 4128 | tf_op jit(solution)/shard_map/all_to_all | solution.py:275
  20.9 0.6 %collective-permute-start.4 = (s16[64,1024]{1,0:T(8,128)(2,1)S(1)}, s16[64,1024]{1,0:T(8,128)(2,1)S(1)}, u32[]{:S(2)}, u32[]{:S(2)}) collective-permute-start(s16[64,1024]{1,0:T(8,128)(2,1)S(1)} %proxy_blocks.1), channel_id=1, source_target_pairs={{0,16},{4,20},{8,24},{12,28},{16,0},{20,4},{24,8},{28,12},{1,17},{... | collective-permute-start | bytes 393224 | tf_op jit(solution)/shard_map/ppermute | solution.py:186
  21.5 0.6 owner_blocks.1
  22.1 6.1 %collective-permute-done.4.far_ref = s16[64,1024]{1,0:T(8,128)(2,1)S(1)} collective-permute-done((s16[64,1024]{1,0:T(8,128)(2,1)S(1)}, s16[64,1024]{1,0:T(8,128)(2,1)S(1)}, u32[]{:S(2)}, u32[]{:S(2)}) %collective-permute-start.4) | collective-permute-done | bytes 131104 | tf_op jit(solution)/shard_map/ppermute | solution.py:186
  28.2 0.7 %finish_blocks.1 = (f32[64,1024]{1,0:T(8,128)S(1)}, f32[32,1,128]{2,1,0:T(1,128)}) custom-call(f32[64,1024]{1,0:T(8,128)S(1)} %get-tuple-element.14.near_ref, s16[64,1024]{1,0:T(8,128)(2,1)S(1)} %collective-permute-done.4.far_ref, f32[64,128]{1,0:T(8,128)S(1)} %get-tuple-element.18.scale_ref, f32[64,128]{1,0:T(8,128)S(1)} %get-tuple-element.19.step_ref), custom_call_target="tpu_custom_call" | custom-call | tf_op jit(solution)/shard_map/finish_blocks/pallas_call | solution.py:305
  28.9 2.5 %all-to-all-start.1 = ((f32[32,1,128]{2,1,0:T(1,128)}), f32[32,1,128]{2,1,0:T(1,128)S(1)}, u32[]{:S(2)}, u32[]{:S(2)}) async-start(f32[32,1,128]{2,1,0:T(1,128)} %get-tuple-element.20), calls=%async_computation.1 | async-start | bytes 32768 | tf_op jit(solution)/shard_map/all_to_all | solution.py:321
  31.8 6.7 %all-to-all-done.1 = f32[32,1,128]{2,1,0:T(1,128)S(1)} async-done(((f32[32,1,128]{2,1,0:T(1,128)}), f32[32,1,128]{2,1,0:T(1,128)S(1)}, u32[]{:S(2)}, u32[]{:S(2)}) %all-to-all-start.1) | async-done | bytes 16416 | tf_op jit(solution)/shard_map/all_to_all | solution.py:321
  38.7 0.6 %collective-permute-start.10 = (bf16[64,1024]{1,0:T(8,128)(2,1)S(1)}, bf16[64,1024]{1,0:T(8,128)(2,1)S(1)}, u32[]{:S(2)}, u32[]{:S(2)}) collective-permute-start(bf16[64,1024]{1,0:T(8,128)(2,1)S(1)} %new_weights.1.refs_0_), channel_id=1, source_target_pairs={{0,8},{4,12},{8,0},{12,4},{16,24},{20,28},{24,16},{28,20},{1,9},{5... | collective-permute-start | bytes 393224 | tf_op jit(solution)/shard_map/ppermute | solution.py:186
  39.4 0.6 collective-permute-start.5
  40.4 5.2 %collective-permute-done.10.refs_2_ = bf16[64,1024]{1,0:T(8,128)(2,1)S(1)} collective-permute-done((bf16[64,1024]{1,0:T(8,128)(2,1)S(1)}, bf16[64,1024]{1,0:T(8,128)(2,1)S(1)}, u32[]{:S(2)}, u32[]{:S(2)}) %collective-permute-start.10) | collective-permute-done | bytes 131104 | tf_op jit(solution)/shard_map/ppermute | solution.py:186
  45.7 0.5 collective-permute-start.11
  46.2 1.8 %collective-permute-done.5.refs_4_ = bf16[64,1024]{1,0:T(8,128)(2,1)S(1)} collective-permute-done((bf16[64,1024]{1,0:T(8,128)(2,1)S(1)}, bf16[64,1024]{1,0:T(8,128)(2,1)S(1)}, u32[]{:S(2)}, u32[]{:S(2)}) %collective-permute-start.5) | collective-permute-done | bytes 131104 | tf_op jit(solution)/shard_map/ppermute | solution.py:186
  48.0 2.1 %collective-permute-start.7 = (bf16[64,1024]{1,0:T(8,128)(2,1)S(1)}, bf16[64,1024]{1,0:T(8,128)(2,1)S(1)}, u32[]{:S(2)}, u32[]{:S(2)}) collective-permute-start(bf16[64,1024]{1,0:T(8,128)(2,1)S(1)} %collective-permute-done.5.refs_4_), channel_id=1, source_target_pairs={{0,8},{4,12},{8,0},{12,4},{16,24},{20,28},{24,16},{28,20},{1,9},{5... | collective-permute-start | bytes 393224 | tf_op jit(solution)/shard_map/ppermute | solution.py:186
  50.0 1.4 %collective-permute-start.6 = (bf16[64,1024]{1,0:T(8,128)(2,1)S(1)}, bf16[64,1024]{1,0:T(8,128)(2,1)S(1)}, u32[]{:S(2)}, u32[]{:S(2)}) collective-permute-start(bf16[64,1024]{1,0:T(8,128)(2,1)S(1)} %collective-permute-done.5.refs_4_), channel_id=1, source_target_pairs={{0,4},{4,0},{8,12},{12,8},{16,20},{20,16},{24,28},{28,24},{1,5},{5... | collective-permute-start | bytes 393224 | tf_op jit(solution)/shard_map/ppermute | solution.py:186
  51.5 0.8 %update_grad.1 = f32[64,1024]{1,0:T(8,128)} custom-call(f32[32,128]{1,0:T(8,128)S(1)} %bitcast.29, f32[64,1024]{1,0:T(8,128)S(1)} %rotate_back.1.unrot_ref), custom_call_target="tpu_custom_call" | custom-call | tf_op jit(solution)/shard_map/update_grad/pallas_call | solution.py:330
  52.6 0.9 %place_own.1.refs_3_ = bf16[512,1024]{1,0:T(8,128)(2,1)} custom-call(bf16[64,1024]{1,0:T(8,128)(2,1)S(1)} %new_weights.1.refs_0_, bf16[64,1024]{1,0:T(8,128)(2,1)S(1)} %collective-permute-done.9.refs_1_, bf16[64,1024]{1,0:T(8,128)(2,1)S(1)} %collective-permute-done.10.refs_2_, bf16[64,1024]{1,0:T(8,128)(2,1)S(1)} %collective-permute-done.11.refs_3_, ...), custom_call_target="tpu_custom_call" | custom-call | tf_op jit(solution)/shard_map/place_own/pallas_call | solution.py:213
  54.4 1.2 %collective-permute-done.6.refs_0_ = bf16[64,1024]{1,0:T(8,128)(2,1)S(1)} collective-permute-done((bf16[64,1024]{1,0:T(8,128)(2,1)S(1)}, bf16[64,1024]{1,0:T(8,128)(2,1)S(1)}, u32[]{:S(2)}, u32[]{:S(2)}) %collective-permute-start.6) | collective-permute-done | bytes 131104 | tf_op jit(solution)/shard_map/ppermute | solution.py:186
  55.7 0.8 %place_far.1 = bf16[512,1024]{1,0:T(8,128)(2,1)} custom-call(bf16[64,1024]{1,0:T(8,128)(2,1)S(1)} %collective-permute-done.6.refs_0_, bf16[64,1024]{1,0:T(8,128)(2,1)S(1)} %collective-permute-done.7.refs_1_, bf16[64,1024]{1,0:T(8,128)(2,1)S(1)} %collective-permute-done.8.refs_2_, bf16[512,1024]{1,0:T(8,128)(2,1)} %place_own.1.refs_3_), custom_call_target="tpu_custom_call", output_to_operand_aliasing={{}: (3, {})} | custom-call | tf_op jit(solution)/shard_map/place_far/pallas_call | solution.py:213
  (27 shorter events, 3.1 us)
Async XLA Ops:
  0.6 5.8 %copy-start = (bf16[1,1,512,1024]{3,2,1,0:T(8,128)(2,1)S(1)}, bf16[1,1,512,1024]{3,2,1,0:T(8,128)(2,1)}, u32[]{:S(2)}) copy-start(bf16[1,1,512,1024]{3,2,1,0:T(8,128)(2,1)} %param.5) | copy-start | bytes 3145732
  1.8 18.3 %collective-permute-start.1 = (bf16[2,64,1024]{2,1,0:T(8,128)(2,1)S(1)}, bf16[2,64,1024]{2,1,0:T(8,128)(2,1)S(1)}, u32[]{:S(2)}, u32[]{:S(2)}) collective-permute-start(bf16[2,64,1024]{2,1,0:T(8,128)(2,1)S(1)} %get-tuple-element.24), channel_id=1, source_target_pairs={{0,8},{4,12},{8,0},{12,4},{16,24},{20,28},{24,16},{28,20},{1,9},{5... | collective-permute-start | bytes 786440 | tf_op jit(solution)/shard_map/ppermute | solution.py:186
  4.9 15.2 %collective-permute-start = (bf16[2,64,1024]{2,1,0:T(8,128)(2,1)S(1)}, bf16[2,64,1024]{2,1,0:T(8,128)(2,1)S(1)}, u32[]{:S(2)}, u32[]{:S(2)}) collective-permute-start(bf16[2,64,1024]{2,1,0:T(8,128)(2,1)S(1)} %get-tuple-element.25), channel_id=1, source_target_pairs={{0,4},{4,0},{8,12},{12,8},{16,20},{20,16},{24,28},{28,24},{1,5},{5... | collective-permute-start | bytes 786440 | tf_op jit(solution)/shard_map/ppermute | solution.py:186
  7.5 13.1 %collective-permute-start.3 = (bf16[64,1024]{1,0:T(8,128)(2,1)S(1)}, bf16[64,1024]{1,0:T(8,128)(2,1)S(1)}, u32[]{:S(2)}, u32[]{:S(2)}) collective-permute-start(bf16[64,1024]{1,0:T(8,128)(2,1)S(1)} %get-tuple-element.22), channel_id=1, source_target_pairs={{0,12},{4,8},{8,4},{12,0},{16,28},{20,24},{24,20},{28,16},{1,13},{... | collective-permute-start | bytes 393224 | tf_op jit(solution)/shard_map/ppermute | solution.py:186
  7.6 12.6 %all-to-all-start = ((f32[8,1,128]{2,1,0:T(1,128)}), f32[8,1,128]{2,1,0:T(1,128)S(1)}, u32[]{:S(2)}, u32[]{:S(2)}) async-start(f32[8,1,128]{2,1,0:T(1,128)} %bitcast.8), calls=%async_computation | async-start | bytes 8192 | tf_op jit(solution)/shard_map/all_to_all | solution.py:275
  13.8 7.8 %collective-permute-start.2 = (bf16[64,1024]{1,0:T(8,128)(2,1)S(1)}, bf16[64,1024]{1,0:T(8,128)(2,1)S(1)}, u32[]{:S(2)}, u32[]{:S(2)}) collective-permute-start(bf16[64,1024]{1,0:T(8,128)(2,1)S(1)} %get-tuple-element.23), channel_id=1, source_target_pairs={{0,12},{4,8},{8,4},{12,0},{16,28},{20,24},{24,20},{28,16},{1,13},{... | collective-permute-start | bytes 393224 | tf_op jit(solution)/shard_map/ppermute | solution.py:186
  16.7 3.5 %copy-start.1 = (bf16[256,256]{1,0:T(8,128)(2,1)S(1)}, bf16[256,256]{1,0:T(8,128)(2,1)}, u32[]{:S(2)}) copy-start(bf16[256,256]{1,0:T(8,128)(2,1)} %constant.37.clone.refs_6_.refs_5_.matrix_ref) | copy-start | bytes 393220
  16.7 3.5 %copy-start.4 = (s32[1,1024]{1,0:T(1,128)S(1)}, s32[1,1024]{1,0:T(1,128)}, u32[]{:S(2)}) copy-start(s32[1,1024]{1,0:T(1,128)} %sign_ref.1) | copy-start | bytes 12292
  20.9 7.3 %collective-permute-start.4 = (s16[64,1024]{1,0:T(8,128)(2,1)S(1)}, s16[64,1024]{1,0:T(8,128)(2,1)S(1)}, u32[]{:S(2)}, u32[]{:S(2)}) collective-permute-start(s16[64,1024]{1,0:T(8,128)(2,1)S(1)} %proxy_blocks.1), channel_id=1, source_target_pairs={{0,16},{4,20},{8,24},{12,28},{16,0},{20,4},{24,8},{28,12},{1,17},{... | collective-permute-start | bytes 393224 | tf_op jit(solution)/shard_map/ppermute | solution.py:186
  28.9 9.6 %all-to-all-start.1 = ((f32[32,1,128]{2,1,0:T(1,128)}), f32[32,1,128]{2,1,0:T(1,128)S(1)}, u32[]{:S(2)}, u32[]{:S(2)}) async-start(f32[32,1,128]{2,1,0:T(1,128)} %get-tuple-element.20), calls=%async_computation.1 | async-start | bytes 32768 | tf_op jit(solution)/shard_map/all_to_all | solution.py:321
  31.5 7.1 %copy-start.2 = (bf16[1,64,1024]{2,1,0:T(8,128)(2,1)S(1)}, bf16[1,64,1024]{2,1,0:T(8,128)(2,1)}, u32[]{:S(2)}) copy-start(bf16[1,64,1024]{2,1,0:T(8,128)(2,1)} %param.7) | copy-start | bytes 393220
  31.5 7.1 %copy-start.3 = (bf16[1,64,1024]{2,1,0:T(8,128)(2,1)S(1)}, bf16[1,64,1024]{2,1,0:T(8,128)(2,1)}, u32[]{:S(2)}) copy-start(bf16[1,64,1024]{2,1,0:T(8,128)(2,1)} %param.8) | copy-start | bytes 393220
  38.7 6.9 %collective-permute-start.10 = (bf16[64,1024]{1,0:T(8,128)(2,1)S(1)}, bf16[64,1024]{1,0:T(8,128)(2,1)S(1)}, u32[]{:S(2)}, u32[]{:S(2)}) collective-permute-start(bf16[64,1024]{1,0:T(8,128)(2,1)S(1)} %new_weights.1.refs_0_), channel_id=1, source_target_pairs={{0,8},{4,12},{8,0},{12,4},{16,24},{20,28},{24,16},{28,20},{1,9},{5... | collective-permute-start | bytes 393224 | tf_op jit(solution)/shard_map/ppermute | solution.py:186
  39.4 8.6 %collective-permute-start.5 = (bf16[64,1024]{1,0:T(8,128)(2,1)S(1)}, bf16[64,1024]{1,0:T(8,128)(2,1)S(1)}, u32[]{:S(2)}, u32[]{:S(2)}) collective-permute-start(bf16[64,1024]{1,0:T(8,128)(2,1)S(1)} %new_weights.1.refs_0_), channel_id=1, source_target_pairs={{0,16},{4,20},{8,24},{12,28},{16,0},{20,4},{24,8},{28,12},{1,17},{... | collective-permute-start | bytes 393224 | tf_op jit(solution)/shard_map/ppermute | solution.py:186
  39.9 12.4 %collective-permute-start.9 = (bf16[64,1024]{1,0:T(8,128)(2,1)S(1)}, bf16[64,1024]{1,0:T(8,128)(2,1)S(1)}, u32[]{:S(2)}, u32[]{:S(2)}) collective-permute-start(bf16[64,1024]{1,0:T(8,128)(2,1)S(1)} %new_weights.1.refs_0_), channel_id=1, source_target_pairs={{0,4},{4,0},{8,12},{12,8},{16,20},{20,16},{24,28},{28,24},{1,5},{5... | collective-permute-start | bytes 393224 | tf_op jit(solution)/shard_map/ppermute | solution.py:186
  45.7 6.9 %collective-permute-start.11 = (bf16[64,1024]{1,0:T(8,128)(2,1)S(1)}, bf16[64,1024]{1,0:T(8,128)(2,1)S(1)}, u32[]{:S(2)}, u32[]{:S(2)}) collective-permute-start(bf16[64,1024]{1,0:T(8,128)(2,1)S(1)} %collective-permute-done.10.refs_2_), channel_id=1, source_target_pairs={{0,4},{4,0},{8,12},{12,8},{16,20},{20,16},{24,28},{28,24},{1,5},{5... | collective-permute-start | bytes 393224 | tf_op jit(solution)/shard_map/ppermute | solution.py:186
  48.0 6.0 %collective-permute-start.8 = (bf16[64,1024]{1,0:T(8,128)(2,1)S(1)}, bf16[64,1024]{1,0:T(8,128)(2,1)S(1)}, u32[]{:S(2)}, u32[]{:S(2)}) collective-permute-start(bf16[64,1024]{1,0:T(8,128)(2,1)S(1)} %collective-permute-done.5.refs_4_), channel_id=1, source_target_pairs={{0,12},{4,8},{8,4},{12,0},{16,28},{20,24},{24,20},{28,16},{1,13},{... | collective-permute-start | bytes 393224 | tf_op jit(solution)/shard_map/ppermute | solution.py:186
  48.0 6.4 %collective-permute-start.7 = (bf16[64,1024]{1,0:T(8,128)(2,1)S(1)}, bf16[64,1024]{1,0:T(8,128)(2,1)S(1)}, u32[]{:S(2)}, u32[]{:S(2)}) collective-permute-start(bf16[64,1024]{1,0:T(8,128)(2,1)S(1)} %collective-permute-done.5.refs_4_), channel_id=1, source_target_pairs={{0,8},{4,12},{8,0},{12,4},{16,24},{20,28},{24,16},{28,20},{1,9},{5... | collective-permute-start | bytes 393224 | tf_op jit(solution)/shard_map/ppermute | solution.py:186
  50.0 5.6 %collective-permute-start.6 = (bf16[64,1024]{1,0:T(8,128)(2,1)S(1)}, bf16[64,1024]{1,0:T(8,128)(2,1)S(1)}, u32[]{:S(2)}, u32[]{:S(2)}) collective-permute-start(bf16[64,1024]{1,0:T(8,128)(2,1)S(1)} %collective-permute-done.5.refs_4_), channel_id=1, source_target_pairs={{0,4},{4,0},{8,12},{12,8},{16,20},{20,16},{24,28},{28,24},{1,5},{5... | collective-permute-start | bytes 393224 | tf_op jit(solution)/shard_map/ppermute | solution.py:186

commit v26 on v19

--- a/solution.py
+++ b/solution.py
@@ -131,27 +131,25 @@
     step_ref[...] = jnp.broadcast_to(step, step_ref.shape)
 
 
-def finish_kernel(near_ref, far_ref, scale_ref, step_ref, total_ref, square_ref):
+def finish_kernel(near_ref, far_ref, scale_ref, step_ref, square_ref):
     width = near_ref.shape[1]
     step = step_ref[...]
     squares = None
     for start in range(0, width, lanes):
         cut = slice(start, start + lanes)
         total = near_ref[:, cut] + far_ref[:, cut].astype(jnp.float32) * step
-        total_ref[:, cut] = total
         squares = total * total if squares is None else squares + total * total
     scale = scale_ref[...]
     squares = jnp.sum(squares * (scale * scale), axis=0, keepdims=True)
     square_ref[...] = jnp.broadcast_to(squares[None], square_ref.shape)
 
 
-def back_kernel(base, total_ref, scale_ref, sign_ref, matrix_ref, unrot_ref):
-    owned, width = total_ref.shape
-    total = total_ref[...]
+def back_kernel(base, near_ref, far_ref, scale_ref, step_ref, sign_ref, matrix_ref, unrot_ref):
+    total = near_ref[...] + far_ref[...].astype(jnp.float32) * step_ref[:, 0:1]
     high = total.astype(jnp.bfloat16)
     low = (total - high.astype(jnp.float32)).astype(jnp.bfloat16)
     groups = rotate_groups([high, low], matrix_ref[...], base)
-    back = scale_ref[:, 0:1] * (1.0 / math.sqrt(width))
+    back = scale_ref[:, 0:1] * (1.0 / math.sqrt(total.shape[1]))
     signs = sign_ref[...].astype(jnp.float32)
     for g, group in enumerate(groups):
         cut = slice(g * base, (g + 1) * base)
@@ -300,13 +298,10 @@
         compiler_params=params,
         name="owner_blocks",
     )(*pairs, *near_pieces, sums, signs, matrix)
-    total, squares = pl.pallas_call(
+    squares = pl.pallas_call(
         finish_kernel,
         in_specs=[array] * 4,
-        out_shape=(
-            jax.ShapeDtypeStruct((owned, width), jnp.float32),
-            jax.ShapeDtypeStruct((devices, 1, lanes), jnp.float32),
-        ),
+        out_shape=jax.ShapeDtypeStruct((devices, 1, lanes), jnp.float32),
         compiler_params=params,
         name="finish_blocks",
     )(near_total, far_total, mean_scale, step)
@@ -315,7 +310,7 @@
         out_shape=jax.ShapeDtypeStruct((owned, width), jnp.float32),
         compiler_params=params,
         name="rotate_back",
-    )(total, mean_scale, signs, matrix)
+    )(near_total, far_total, mean_scale, step, signs, matrix)
     squares = lax.all_to_all(squares, ("dp", "expert"), split_axis=0, concat_axis=0, tiled=True)
     limit = target_rms * math.sqrt(blocks * width * lax.axis_size("expert"))
     squares = squares.reshape(devices, lanes)

time: 56.5 us -> 56.5 us (level)
  no operation moved by 1% of the time
where the time goes in v26:
time: 56.5 us; the launch traced here: 56.3 us
  waiting for transfers between devices  25.8 us (46%)
  starting transfers between devices  22.7 us (40%)
  Pallas kernels  5.81 us (10%)
  local copies, waits for them, and re-layouts  1.21 us (2%)
  between operations  0.8 us (1%)
    ppermute x12, waiting for transfers between devices, swap(): return lax.ppermute(value, 'dp', [(i, i ^ mask) for i in range(size)])  15.6 us
    ppermute x12, starting transfers between devices, swap(): return lax.ppermute(value, 'dp', [(i, i ^ mask) for i in range(size)])  14 us
    all_to_all x1, waiting for transfers between devices, on_device(): lax.all_to_all(squares, ('dp', 'expert'), split_axis=0, concat_axis=0, ti...  6.68 us
    all_to_all x1, starting transfers between devices, on_device(): lax.all_to_all(sums.reshape(replicas, 1, 2 * owned), 'dp', split_axis=0,...  6.18 us
    all_to_all x1, waiting for transfers between devices, on_device(): lax.all_to_all(sums.reshape(replicas, 1, 2 * owned), 'dp', split_axis=0,...  3.44 us
    all_to_all x1, starting transfers between devices, on_device(): lax.all_to_all(squares, ('dp', 'expert'), split_axis=0, concat_axis=0, ti...  2.54 us
    pallas_call x2, Pallas kernels, place_pieces(): pl.pallas_call(functools.partial(place_kernel, places, owned), in_specs=s...  1.63 us
    reshape x2, local copies, waits for them, and re-layouts, pair_of(): lax.dynamic_slice_in_dim(source, index % near, 1, 1)  1.17 us
  transfers between devices with their start and end apart: 14, of which 9 were waited for; matrix products, arithmetic and copies ran while one was open for 0% of the time, Pallas kernels for 7%

profile of v26, /device:TPU:0, one launch (start us, length us, event | category | flops | bytes accessed | tf_op | source)
XLA Modules:
  0.0 56.3 jit_solution(3685714256521299680)
XLA Ops:
  0.7 1.2 %dynamic-slice_bitcast_fusion.1 = (bf16[2,64,1024]{2,1,0:T(8,128)(2,1)S(1)}, bf16[2,64,1024]{2,1,0:T(8,128)(2,1)S(1)}) fusion(bf16[2,4,64,1024]{3,2,1,0:T(8,128)(2,1)} %bitcast.24, s32[]{:T(128)S(6)} %select_n.33, s32[]{:T(128)S(6)} %select_n.31), kind=kLoop, calls=%fused_computation.1 | loop fusion | bytes 1048584 | tf_op jit(solution)/shard_map/reshape | solution.py:253
  1.8 3.1 %collective-permute-start.1 = (bf16[2,64,1024]{2,1,0:T(8,128)(2,1)S(1)}, bf16[2,64,1024]{2,1,0:T(8,128)(2,1)S(1)}, u32[]{:S(2)}, u32[]{:S(2)}) collective-permute-start(bf16[2,64,1024]{2,1,0:T(8,128)(2,1)S(1)} %get-tuple-element.20), channel_id=1, source_target_pairs={{0,8},{4,12},{8,0},{12,4},{16,24},{20,28},{24,16},{28,20},{1,9},{5... | collective-permute-start | bytes 786440 | tf_op jit(solution)/shard_map/ppermute | solution.py:182
  4.9 1.5 %collective-permute-start = (bf16[2,64,1024]{2,1,0:T(8,128)(2,1)S(1)}, bf16[2,64,1024]{2,1,0:T(8,128)(2,1)S(1)}, u32[]{:S(2)}, u32[]{:S(2)}) collective-permute-start(bf16[2,64,1024]{2,1,0:T(8,128)(2,1)S(1)} %get-tuple-element.21), channel_id=1, source_target_pairs={{0,4},{4,0},{8,12},{12,8},{16,20},{20,16},{24,28},{28,24},{1,5},{5... | collective-permute-start | bytes 786440 | tf_op jit(solution)/shard_map/ppermute | solution.py:182
  6.4 0.9 %sum_squares.1 = f32[2,4,1,128]{3,2,1,0:T(1,128)} custom-call(bf16[2,4,64,1024]{3,2,1,0:T(8,128)(2,1)S(1)} %bitcast.25), custom_call_target="tpu_custom_call" | custom-call | tf_op jit(solution)/shard_map/sum_squares/pallas_call | solution.py:263
  7.4 6.2 %all-to-all-start = ((f32[8,1,128]{2,1,0:T(1,128)}), f32[8,1,128]{2,1,0:T(1,128)S(1)}, u32[]{:S(2)}, u32[]{:S(2)}) async-start(f32[8,1,128]{2,1,0:T(1,128)} %bitcast.8), calls=%async_computation | async-start | bytes 8192 | tf_op jit(solution)/shard_map/all_to_all | solution.py:271
  13.6 2.9 %collective-permute-start.2 = (bf16[64,1024]{1,0:T(8,128)(2,1)S(1)}, bf16[64,1024]{1,0:T(8,128)(2,1)S(1)}, u32[]{:S(2)}, u32[]{:S(2)}) collective-permute-start(bf16[64,1024]{1,0:T(8,128)(2,1)S(1)} %get-tuple-element.19), channel_id=1, source_target_pairs={{0,12},{4,8},{8,4},{12,0},{16,28},{20,24},{24,20},{28,16},{1,13},{... | collective-permute-start | bytes 393224 | tf_op jit(solution)/shard_map/ppermute | solution.py:182
  16.6 3.4 %all-to-all-done = f32[8,1,128]{2,1,0:T(1,128)S(1)} async-done(((f32[8,1,128]{2,1,0:T(1,128)}), f32[8,1,128]{2,1,0:T(1,128)S(1)}, u32[]{:S(2)}, u32[]{:S(2)}) %all-to-all-start) | async-done | bytes 4128 | tf_op jit(solution)/shard_map/all_to_all | solution.py:271
  20.8 0.6 %collective-permute-start.4 = (s16[64,1024]{1,0:T(8,128)(2,1)S(1)}, s16[64,1024]{1,0:T(8,128)(2,1)S(1)}, u32[]{:S(2)}, u32[]{:S(2)}) collective-permute-start(s16[64,1024]{1,0:T(8,128)(2,1)S(1)} %proxy_blocks.1), channel_id=1, source_target_pairs={{0,16},{4,20},{8,24},{12,28},{16,0},{20,4},{24,8},{28,12},{1,17},{... | collective-permute-start | bytes 393224 | tf_op jit(solution)/shard_map/ppermute | solution.py:182
  21.4 0.6 owner_blocks.1
  22.0 6.1 %collective-permute-done.4.far_ref = s16[64,1024]{1,0:T(8,128)(2,1)S(1)} collective-permute-done((s16[64,1024]{1,0:T(8,128)(2,1)S(1)}, s16[64,1024]{1,0:T(8,128)(2,1)S(1)}, u32[]{:S(2)}, u32[]{:S(2)}) %collective-permute-start.4) | collective-permute-done | bytes 131104 | tf_op jit(solution)/shard_map/ppermute | solution.py:182
  28.1 0.7 %finish_blocks.1 = f32[32,1,128]{2,1,0:T(1,128)} custom-call(f32[64,1024]{1,0:T(8,128)S(1)} %get-tuple-element.12.near_ref, s16[64,1024]{1,0:T(8,128)(2,1)S(1)} %collective-permute-done.4.far_ref, f32[64,128]{1,0:T(8,128)S(1)} %get-tuple-element.16.scale_ref, f32[64,128]{1,0:T(8,128)S(1)} %get-tuple-element.17.step_ref), custom_call_target="tpu_custom_call" | custom-call | tf_op jit(solution)/shard_map/finish_blocks/pallas_call | solution.py:301
  28.8 2.5 %all-to-all-start.1 = ((f32[32,1,128]{2,1,0:T(1,128)}), f32[32,1,128]{2,1,0:T(1,128)S(1)}, u32[]{:S(2)}, u32[]{:S(2)}) async-start(f32[32,1,128]{2,1,0:T(1,128)} %finish_blocks.1), calls=%async_computation.1 | async-start | bytes 32768 | tf_op jit(solution)/shard_map/all_to_all | solution.py:314
  31.7 6.7 %all-to-all-done.1 = f32[32,1,128]{2,1,0:T(1,128)S(1)} async-done(((f32[32,1,128]{2,1,0:T(1,128)}), f32[32,1,128]{2,1,0:T(1,128)S(1)}, u32[]{:S(2)}, u32[]{:S(2)}) %all-to-all-start.1) | async-done | bytes 16416 | tf_op jit(solution)/shard_map/all_to_all | solution.py:314
  38.6 0.6 %collective-permute-start.10 = (bf16[64,1024]{1,0:T(8,128)(2,1)S(1)}, bf16[64,1024]{1,0:T(8,128)(2,1)S(1)}, u32[]{:S(2)}, u32[]{:S(2)}) collective-permute-start(bf16[64,1024]{1,0:T(8,128)(2,1)S(1)} %new_weights.1.refs_0_), channel_id=1, source_target_pairs={{0,8},{4,12},{8,0},{12,4},{16,24},{20,28},{24,16},{28,20},{1,9},{5... | collective-permute-start | bytes 393224 | tf_op jit(solution)/shard_map/ppermute | solution.py:182
  39.2 0.6 collective-permute-start.5
  40.3 5.2 %collective-permute-done.10.refs_2_ = bf16[64,1024]{1,0:T(8,128)(2,1)S(1)} collective-permute-done((bf16[64,1024]{1,0:T(8,128)(2,1)S(1)}, bf16[64,1024]{1,0:T(8,128)(2,1)S(1)}, u32[]{:S(2)}, u32[]{:S(2)}) %collective-permute-start.10) | collective-permute-done | bytes 131104 | tf_op jit(solution)/shard_map/ppermute | solution.py:182
  45.5 0.5 collective-permute-start.11
  46.1 1.8 %collective-permute-done.5.refs_4_ = bf16[64,1024]{1,0:T(8,128)(2,1)S(1)} collective-permute-done((bf16[64,1024]{1,0:T(8,128)(2,1)S(1)}, bf16[64,1024]{1,0:T(8,128)(2,1)S(1)}, u32[]{:S(2)}, u32[]{:S(2)}) %collective-permute-start.5) | collective-permute-done | bytes 131104 | tf_op jit(solution)/shard_map/ppermute | solution.py:182
  47.8 2.1 %collective-permute-start.7 = (bf16[64,1024]{1,0:T(8,128)(2,1)S(1)}, bf16[64,1024]{1,0:T(8,128)(2,1)S(1)}, u32[]{:S(2)}, u32[]{:S(2)}) collective-permute-start(bf16[64,1024]{1,0:T(8,128)(2,1)S(1)} %collective-permute-done.5.refs_4_), channel_id=1, source_target_pairs={{0,8},{4,12},{8,0},{12,4},{16,24},{20,28},{24,16},{28,20},{1,9},{5... | collective-permute-start | bytes 393224 | tf_op jit(solution)/shard_map/ppermute | solution.py:182
  49.9 1.4 %collective-permute-start.6 = (bf16[64,1024]{1,0:T(8,128)(2,1)S(1)}, bf16[64,1024]{1,0:T(8,128)(2,1)S(1)}, u32[]{:S(2)}, u32[]{:S(2)}) collective-permute-start(bf16[64,1024]{1,0:T(8,128)(2,1)S(1)} %collective-permute-done.5.refs_4_), channel_id=1, source_target_pairs={{0,4},{4,0},{8,12},{12,8},{16,20},{20,16},{24,28},{28,24},{1,5},{5... | collective-permute-start | bytes 393224 | tf_op jit(solution)/shard_map/ppermute | solution.py:182
  51.3 0.8 %update_grad.1 = f32[64,1024]{1,0:T(8,128)} custom-call(f32[32,128]{1,0:T(8,128)S(1)} %bitcast.29, f32[64,1024]{1,0:T(8,128)S(1)} %rotate_back.1.unrot_ref), custom_call_target="tpu_custom_call" | custom-call | tf_op jit(solution)/shard_map/update_grad/pallas_call | solution.py:323
  52.4 0.9 %place_own.1.refs_3_ = bf16[512,1024]{1,0:T(8,128)(2,1)} custom-call(bf16[64,1024]{1,0:T(8,128)(2,1)S(1)} %new_weights.1.refs_0_, bf16[64,1024]{1,0:T(8,128)(2,1)S(1)} %collective-permute-done.9.refs_1_, bf16[64,1024]{1,0:T(8,128)(2,1)S(1)} %collective-permute-done.10.refs_2_, bf16[64,1024]{1,0:T(8,128)(2,1)S(1)} %collective-permute-done.11.refs_3_, ...), custom_call_target="tpu_custom_call" | custom-call | tf_op jit(solution)/shard_map/place_own/pallas_call | solution.py:209
  54.3 1.2 %collective-permute-done.6.refs_0_ = bf16[64,1024]{1,0:T(8,128)(2,1)S(1)} collective-permute-done((bf16[64,1024]{1,0:T(8,128)(2,1)S(1)}, bf16[64,1024]{1,0:T(8,128)(2,1)S(1)}, u32[]{:S(2)}, u32[]{:S(2)}) %collective-permute-start.6) | collective-permute-done | bytes 131104 | tf_op jit(solution)/shard_map/ppermute | solution.py:182
  55.5 0.8 %place_far.1 = bf16[512,1024]{1,0:T(8,128)(2,1)} custom-call(bf16[64,1024]{1,0:T(8,128)(2,1)S(1)} %collective-permute-done.6.refs_0_, bf16[64,1024]{1,0:T(8,128)(2,1)S(1)} %collective-permute-done.7.refs_1_, bf16[64,1024]{1,0:T(8,128)(2,1)S(1)} %collective-permute-done.8.refs_2_, bf16[512,1024]{1,0:T(8,128)(2,1)} %place_own.1.refs_3_), custom_call_target="tpu_custom_call", output_to_operand_aliasing={{}: (3, {})} | custom-call | tf_op jit(solution)/shard_map/place_far/pallas_call | solution.py:209
  (27 shorter events, 3.2 us)
Async XLA Ops:
  0.6 5.8 %copy-start = (bf16[1,1,512,1024]{3,2,1,0:T(8,128)(2,1)S(1)}, bf16[1,1,512,1024]{3,2,1,0:T(8,128)(2,1)}, u32[]{:S(2)}) copy-start(bf16[1,1,512,1024]{3,2,1,0:T(8,128)(2,1)} %param.5) | copy-start | bytes 3145732
  1.8 18.2 %collective-permute-start.1 = (bf16[2,64,1024]{2,1,0:T(8,128)(2,1)S(1)}, bf16[2,64,1024]{2,1,0:T(8,128)(2,1)S(1)}, u32[]{:S(2)}, u32[]{:S(2)}) collective-permute-start(bf16[2,64,1024]{2,1,0:T(8,128)(2,1)S(1)} %get-tuple-element.20), channel_id=1, source_target_pairs={{0,8},{4,12},{8,0},{12,4},{16,24},{20,28},{24,16},{28,20},{1,9},{5... | collective-permute-start | bytes 786440 | tf_op jit(solution)/shard_map/ppermute | solution.py:182
  4.9 15.1 %collective-permute-start = (bf16[2,64,1024]{2,1,0:T(8,128)(2,1)S(1)}, bf16[2,64,1024]{2,1,0:T(8,128)(2,1)S(1)}, u32[]{:S(2)}, u32[]{:S(2)}) collective-permute-start(bf16[2,64,1024]{2,1,0:T(8,128)(2,1)S(1)} %get-tuple-element.21), channel_id=1, source_target_pairs={{0,4},{4,0},{8,12},{12,8},{16,20},{20,16},{24,28},{28,24},{1,5},{5... | collective-permute-start | bytes 786440 | tf_op jit(solution)/shard_map/ppermute | solution.py:182
  7.3 13.1 %collective-permute-start.3 = (bf16[64,1024]{1,0:T(8,128)(2,1)S(1)}, bf16[64,1024]{1,0:T(8,128)(2,1)S(1)}, u32[]{:S(2)}, u32[]{:S(2)}) collective-permute-start(bf16[64,1024]{1,0:T(8,128)(2,1)S(1)} %get-tuple-element.18), channel_id=1, source_target_pairs={{0,12},{4,8},{8,4},{12,0},{16,28},{20,24},{24,20},{28,16},{1,13},{... | collective-permute-start | bytes 393224 | tf_op jit(solution)/shard_map/ppermute | solution.py:182
  7.4 12.6 %all-to-all-start = ((f32[8,1,128]{2,1,0:T(1,128)}), f32[8,1,128]{2,1,0:T(1,128)S(1)}, u32[]{:S(2)}, u32[]{:S(2)}) async-start(f32[8,1,128]{2,1,0:T(1,128)} %bitcast.8), calls=%async_computation | async-start | bytes 8192 | tf_op jit(solution)/shard_map/all_to_all | solution.py:271
  13.6 7.8 %collective-permute-start.2 = (bf16[64,1024]{1,0:T(8,128)(2,1)S(1)}, bf16[64,1024]{1,0:T(8,128)(2,1)S(1)}, u32[]{:S(2)}, u32[]{:S(2)}) collective-permute-start(bf16[64,1024]{1,0:T(8,128)(2,1)S(1)} %get-tuple-element.19), channel_id=1, source_target_pairs={{0,12},{4,8},{8,4},{12,0},{16,28},{20,24},{24,20},{28,16},{1,13},{... | collective-permute-start | bytes 393224 | tf_op jit(solution)/shard_map/ppermute | solution.py:182
  16.5 3.5 %copy-start.1 = (bf16[256,256]{1,0:T(8,128)(2,1)S(1)}, bf16[256,256]{1,0:T(8,128)(2,1)}, u32[]{:S(2)}) copy-start(bf16[256,256]{1,0:T(8,128)(2,1)} %constant.37.clone.refs_6_.refs_5_.matrix_ref) | copy-start | bytes 393220
  16.5 3.5 %copy-start.4 = (s32[1,1024]{1,0:T(1,128)S(1)}, s32[1,1024]{1,0:T(1,128)}, u32[]{:S(2)}) copy-start(s32[1,1024]{1,0:T(1,128)} %sign_ref.1) | copy-start | bytes 12292
  20.8 7.3 %collective-permute-start.4 = (s16[64,1024]{1,0:T(8,128)(2,1)S(1)}, s16[64,1024]{1,0:T(8,128)(2,1)S(1)}, u32[]{:S(2)}, u32[]{:S(2)}) collective-permute-start(s16[64,1024]{1,0:T(8,128)(2,1)S(1)} %proxy_blocks.1), channel_id=1, source_target_pairs={{0,16},{4,20},{8,24},{12,28},{16,0},{20,4},{24,8},{28,12},{1,17},{... | collective-permute-start | bytes 393224 | tf_op jit(solution)/shard_map/ppermute | solution.py:182
  28.8 9.6 %all-to-all-start.1 = ((f32[32,1,128]{2,1,0:T(1,128)}), f32[32,1,128]{2,1,0:T(1,128)S(1)}, u32[]{:S(2)}, u32[]{:S(2)}) async-start(f32[32,1,128]{2,1,0:T(1,128)} %finish_blocks.1), calls=%async_computation.1 | async-start | bytes 32768 | tf_op jit(solution)/shard_map/all_to_all | solution.py:314
  31.3 7.1 %copy-start.2 = (bf16[1,64,1024]{2,1,0:T(8,128)(2,1)S(1)}, bf16[1,64,1024]{2,1,0:T(8,128)(2,1)}, u32[]{:S(2)}) copy-start(bf16[1,64,1024]{2,1,0:T(8,128)(2,1)} %param.7) | copy-start | bytes 393220
  31.3 7.1 %copy-start.3 = (bf16[1,64,1024]{2,1,0:T(8,128)(2,1)S(1)}, bf16[1,64,1024]{2,1,0:T(8,128)(2,1)}, u32[]{:S(2)}) copy-start(bf16[1,64,1024]{2,1,0:T(8,128)(2,1)} %param.8) | copy-start | bytes 393220
  38.6 6.9 %collective-permute-start.10 = (bf16[64,1024]{1,0:T(8,128)(2,1)S(1)}, bf16[64,1024]{1,0:T(8,128)(2,1)S(1)}, u32[]{:S(2)}, u32[]{:S(2)}) collective-permute-start(bf16[64,1024]{1,0:T(8,128)(2,1)S(1)} %new_weights.1.refs_0_), channel_id=1, source_target_pairs={{0,8},{4,12},{8,0},{12,4},{16,24},{20,28},{24,16},{28,20},{1,9},{5... | collective-permute-start | bytes 393224 | tf_op jit(solution)/shard_map/ppermute | solution.py:182
  39.2 8.6 %collective-permute-start.5 = (bf16[64,1024]{1,0:T(8,128)(2,1)S(1)}, bf16[64,1024]{1,0:T(8,128)(2,1)S(1)}, u32[]{:S(2)}, u32[]{:S(2)}) collective-permute-start(bf16[64,1024]{1,0:T(8,128)(2,1)S(1)} %new_weights.1.refs_0_), channel_id=1, source_target_pairs={{0,16},{4,20},{8,24},{12,28},{16,0},{20,4},{24,8},{28,12},{1,17},{... | collective-permute-start | bytes 393224 | tf_op jit(solution)/shard_map/ppermute | solution.py:182
  39.8 12.4 %collective-permute-start.9 = (bf16[64,1024]{1,0:T(8,128)(2,1)S(1)}, bf16[64,1024]{1,0:T(8,128)(2,1)S(1)}, u32[]{:S(2)}, u32[]{:S(2)}) collective-permute-start(bf16[64,1024]{1,0:T(8,128)(2,1)S(1)} %new_weights.1.refs_0_), channel_id=1, source_target_pairs={{0,4},{4,0},{8,12},{12,8},{16,20},{20,16},{24,28},{28,24},{1,5},{5... | collective-permute-start | bytes 393224 | tf_op jit(solution)/shard_map/ppermute | solution.py:182
  45.5 6.9 %collective-permute-start.11 = (bf16[64,1024]{1,0:T(8,128)(2,1)S(1)}, bf16[64,1024]{1,0:T(8,128)(2,1)S(1)}, u32[]{:S(2)}, u32[]{:S(2)}) collective-permute-start(bf16[64,1024]{1,0:T(8,128)(2,1)S(1)} %collective-permute-done.10.refs_2_), channel_id=1, source_target_pairs={{0,4},{4,0},{8,12},{12,8},{16,20},{20,16},{24,28},{28,24},{1,5},{5... | collective-permute-start | bytes 393224 | tf_op jit(solution)/shard_map/ppermute | solution.py:182
  47.8 6.0 %collective-permute-start.8 = (bf16[64,1024]{1,0:T(8,128)(2,1)S(1)}, bf16[64,1024]{1,0:T(8,128)(2,1)S(1)}, u32[]{:S(2)}, u32[]{:S(2)}) collective-permute-start(bf16[64,1024]{1,0:T(8,128)(2,1)S(1)} %collective-permute-done.5.refs_4_), channel_id=1, source_target_pairs={{0,12},{4,8},{8,4},{12,0},{16,28},{20,24},{24,20},{28,16},{1,13},{... | collective-permute-start | bytes 393224 | tf_op jit(solution)/shard_map/ppermute | solution.py:182
  47.8 6.4 %collective-permute-start.7 = (bf16[64,1024]{1,0:T(8,128)(2,1)S(1)}, bf16[64,1024]{1,0:T(8,128)(2,1)S(1)}, u32[]{:S(2)}, u32[]{:S(2)}) collective-permute-start(bf16[64,1024]{1,0:T(8,128)(2,1)S(1)} %collective-permute-done.5.refs_4_), channel_id=1, source_target_pairs={{0,8},{4,12},{8,0},{12,4},{16,24},{20,28},{24,16},{28,20},{1,9},{5... | collective-permute-start | bytes 393224 | tf_op jit(solution)/shard_map/ppermute | solution.py:182
  49.9 5.6 %collective-permute-start.6 = (bf16[64,1024]{1,0:T(8,128)(2,1)S(1)}, bf16[64,1024]{1,0:T(8,128)(2,1)S(1)}, u32[]{:S(2)}, u32[]{:S(2)}) collective-permute-start(bf16[64,1024]{1,0:T(8,128)(2,1)S(1)} %collective-permute-done.5.refs_4_), channel_id=1, source_target_pairs={{0,4},{4,0},{8,12},{12,8},{16,20},{20,16},{24,28},{28,24},{1,5},{5... | collective-permute-start | bytes 393224 | tf_op jit(solution)/shard_map/ppermute | solution.py:182

commit v27 on v19

--- a/solution.py
+++ b/solution.py
@@ -230,7 +230,8 @@
         own[m] = swap(block, m) if m < x_count or m % x_count == 0 else None
     for m in range(1, near):
         if own[m] is None:
-            own[m] = swap(own[m - m % x_count], m % x_count)
+            held, far = lax.optimization_barrier((own[m - m % x_count], far))
+            own[m] = swap(held, m % x_count)
     own = [(m, 0, piece) for m, piece in own.items()]
     spread = [(near + m, 0, swap(far, m)) for m in range(1, near)]
     out = place_pieces(own + [(near, 0, far)], owned, replicas, None, "place_own")

time: 56.5 us -> 59.5 us (1.053)
  waiting for transfers between devices: 25.8 us -> 28.7 us
    ppermute x12, waiting for transfers between devices: 15.6 us -> 18.6 us  [swap(): return lax.ppermute(value, 'dp', [(i, i ^ mask) for i in range(size)])]
  transfers between devices with their start and end apart: 14 -> 14, of which waited for: 9 -> 6; matrix products, arithmetic and copies ran while one was open for 0% -> 0% of each run, Pallas kernels for 7% -> 7%
where the time goes in v27:
time: 59.5 us; the launch traced here: 59.3 us
  waiting for transfers between devices  28.7 us (48%)
  starting transfers between devices  22.8 us (38%)
  Pallas kernels  5.77 us (10%)
  local copies, waits for them, and re-layouts  1.21 us (2%)
  between operations  0.81 us (1%)
    ppermute x12, waiting for transfers between devices, swap(): return lax.ppermute(value, 'dp', [(i, i ^ mask) for i in range(size)])  18.6 us
    ppermute x12, starting transfers between devices, swap(): return lax.ppermute(value, 'dp', [(i, i ^ mask) for i in range(size)])  14 us
    all_to_all x1, waiting for transfers between devices, on_device(): lax.all_to_all(squares, ('dp', 'expert'), split_axis=0, concat_axis=0, ti...  6.72 us
    all_to_all x1, starting transfers between devices, on_device(): lax.all_to_all(sums.reshape(replicas, 1, 2 * owned), 'dp', split_axis=0,...  6.18 us
    all_to_all x1, waiting for transfers between devices, on_device(): lax.all_to_all(sums.reshape(replicas, 1, 2 * owned), 'dp', split_axis=0,...  3.44 us
    all_to_all x1, starting transfers between devices, on_device(): lax.all_to_all(squares, ('dp', 'expert'), split_axis=0, concat_axis=0, ti...  2.54 us
    pallas_call x2, Pallas kernels, place_pieces(): pl.pallas_call(functools.partial(place_kernel, places, owned), in_specs=s...  1.63 us
  transfers between devices with their start and end apart: 14, of which 6 were waited for; matrix products, arithmetic and copies ran while one was open for 0% of the time, Pallas kernels for 7%

profile of v27, /device:TPU:0, one launch (start us, length us, event | category | flops | bytes accessed | tf_op | source)
XLA Modules:
  0.0 59.3 jit_solution(17899315414181184459)
XLA Ops:
  0.7 1.2 %dynamic-slice_bitcast_fusion.1 = (bf16[2,64,1024]{2,1,0:T(8,128)(2,1)S(1)}, bf16[2,64,1024]{2,1,0:T(8,128)(2,1)S(1)}) fusion(bf16[2,4,64,1024]{3,2,1,0:T(8,128)(2,1)} %bitcast.24, s32[]{:T(128)S(6)} %select_n.33, s32[]{:T(128)S(6)} %select_n.31), kind=kLoop, calls=%fused_computation.1 | loop fusion | bytes 1048584 | tf_op jit(solution)/shard_map/reshape | solution.py:256
  1.8 3.1 %collective-permute-start.1 = (bf16[2,64,1024]{2,1,0:T(8,128)(2,1)S(1)}, bf16[2,64,1024]{2,1,0:T(8,128)(2,1)S(1)}, u32[]{:S(2)}, u32[]{:S(2)}) collective-permute-start(bf16[2,64,1024]{2,1,0:T(8,128)(2,1)S(1)} %get-tuple-element.28), channel_id=1, source_target_pairs={{0,8},{4,12},{8,0},{12,4},{16,24},{20,28},{24,16},{28,20},{1,9},{5... | collective-permute-start | bytes 786440 | tf_op jit(solution)/shard_map/ppermute | solution.py:184
  4.9 1.5 %collective-permute-start = (bf16[2,64,1024]{2,1,0:T(8,128)(2,1)S(1)}, bf16[2,64,1024]{2,1,0:T(8,128)(2,1)S(1)}, u32[]{:S(2)}, u32[]{:S(2)}) collective-permute-start(bf16[2,64,1024]{2,1,0:T(8,128)(2,1)S(1)} %get-tuple-element.29), channel_id=1, source_target_pairs={{0,4},{4,0},{8,12},{12,8},{16,20},{20,16},{24,28},{28,24},{1,5},{5... | collective-permute-start | bytes 786440 | tf_op jit(solution)/shard_map/ppermute | solution.py:184
  6.4 0.9 %sum_squares.1 = f32[2,4,1,128]{3,2,1,0:T(1,128)} custom-call(bf16[2,4,64,1024]{3,2,1,0:T(8,128)(2,1)S(1)} %bitcast.25), custom_call_target="tpu_custom_call" | custom-call | tf_op jit(solution)/shard_map/sum_squares/pallas_call | solution.py:266
  7.4 6.2 %all-to-all-start = ((f32[8,1,128]{2,1,0:T(1,128)}), f32[8,1,128]{2,1,0:T(1,128)S(1)}, u32[]{:S(2)}, u32[]{:S(2)}) async-start(f32[8,1,128]{2,1,0:T(1,128)} %bitcast.8), calls=%async_computation | async-start | bytes 8192 | tf_op jit(solution)/shard_map/all_to_all | solution.py:274
  13.6 2.9 %collective-permute-start.2 = (bf16[64,1024]{1,0:T(8,128)(2,1)S(1)}, bf16[64,1024]{1,0:T(8,128)(2,1)S(1)}, u32[]{:S(2)}, u32[]{:S(2)}) collective-permute-start(bf16[64,1024]{1,0:T(8,128)(2,1)S(1)} %get-tuple-element.27), channel_id=1, source_target_pairs={{0,12},{4,8},{8,4},{12,0},{16,28},{20,24},{24,20},{28,16},{1,13},{... | collective-permute-start | bytes 393224 | tf_op jit(solution)/shard_map/ppermute | solution.py:184
  16.6 3.4 %all-to-all-done = f32[8,1,128]{2,1,0:T(1,128)S(1)} async-done(((f32[8,1,128]{2,1,0:T(1,128)}), f32[8,1,128]{2,1,0:T(1,128)S(1)}, u32[]{:S(2)}, u32[]{:S(2)}) %all-to-all-start) | async-done | bytes 4128 | tf_op jit(solution)/shard_map/all_to_all | solution.py:274
  20.8 0.6 %collective-permute-start.4 = (s16[64,1024]{1,0:T(8,128)(2,1)S(1)}, s16[64,1024]{1,0:T(8,128)(2,1)S(1)}, u32[]{:S(2)}, u32[]{:S(2)}) collective-permute-start(s16[64,1024]{1,0:T(8,128)(2,1)S(1)} %proxy_blocks.1), channel_id=1, source_target_pairs={{0,16},{4,20},{8,24},{12,28},{16,0},{20,4},{24,8},{28,12},{1,17},{... | collective-permute-start | bytes 393224 | tf_op jit(solution)/shard_map/ppermute | solution.py:184
  21.4 0.6 owner_blocks.1
  22.0 6.1 %collective-permute-done.4.far_ref = s16[64,1024]{1,0:T(8,128)(2,1)S(1)} collective-permute-done((s16[64,1024]{1,0:T(8,128)(2,1)S(1)}, s16[64,1024]{1,0:T(8,128)(2,1)S(1)}, u32[]{:S(2)}, u32[]{:S(2)}) %collective-permute-start.4) | collective-permute-done | bytes 131104 | tf_op jit(solution)/shard_map/ppermute | solution.py:184
  28.1 0.7 %finish_blocks.1 = (f32[64,1024]{1,0:T(8,128)S(1)}, f32[32,1,128]{2,1,0:T(1,128)}) custom-call(f32[64,1024]{1,0:T(8,128)S(1)} %get-tuple-element.16.near_ref, s16[64,1024]{1,0:T(8,128)(2,1)S(1)} %collective-permute-done.4.far_ref, f32[64,128]{1,0:T(8,128)S(1)} %get-tuple-element.20.scale_ref, f32[64,128]{1,0:T(8,128)S(1)} %get-tuple-element.21.step_ref), custom_call_target="tpu_custom_call" | custom-call | tf_op jit(solution)/shard_map/finish_blocks/pallas_call | solution.py:304
  28.8 2.5 %all-to-all-start.1 = ((f32[32,1,128]{2,1,0:T(1,128)}), f32[32,1,128]{2,1,0:T(1,128)S(1)}, u32[]{:S(2)}, u32[]{:S(2)}) async-start(f32[32,1,128]{2,1,0:T(1,128)} %get-tuple-element.22), calls=%async_computation.1 | async-start | bytes 32768 | tf_op jit(solution)/shard_map/all_to_all | solution.py:320
  31.7 6.7 %all-to-all-done.1 = f32[32,1,128]{2,1,0:T(1,128)S(1)} async-done(((f32[32,1,128]{2,1,0:T(1,128)}), f32[32,1,128]{2,1,0:T(1,128)S(1)}, u32[]{:S(2)}, u32[]{:S(2)}) %all-to-all-start.1) | async-done | bytes 16416 | tf_op jit(solution)/shard_map/all_to_all | solution.py:320
  38.6 0.7 %collective-permute-start.6 = (bf16[64,1024]{1,0:T(8,128)(2,1)S(1)}, bf16[64,1024]{1,0:T(8,128)(2,1)S(1)}, u32[]{:S(2)}, u32[]{:S(2)}) collective-permute-start(bf16[64,1024]{1,0:T(8,128)(2,1)S(1)} %new_weights.1.refs_0_), channel_id=1, source_target_pairs={{0,16},{4,20},{8,24},{12,28},{16,0},{20,4},{24,8},{28,12},{1,17},{... | collective-permute-start | bytes 393224 | tf_op jit(solution)/shard_map/ppermute | solution.py:184
  40.3 7.2 %collective-permute-done.6.refs_4_ = bf16[64,1024]{1,0:T(8,128)(2,1)S(1)} collective-permute-done((bf16[64,1024]{1,0:T(8,128)(2,1)S(1)}, bf16[64,1024]{1,0:T(8,128)(2,1)S(1)}, u32[]{:S(2)}, u32[]{:S(2)}) %collective-permute-start.6) | collective-permute-done | bytes 131104 | tf_op jit(solution)/shard_map/ppermute | solution.py:184
  47.5 0.6 %collective-permute-start.11 = (bf16[64,1024]{1,0:T(8,128)(2,1)S(1)}, bf16[64,1024]{1,0:T(8,128)(2,1)S(1)}, u32[]{:S(2)}, u32[]{:S(2)}) collective-permute-start(bf16[64,1024]{1,0:T(8,128)(2,1)S(1)} %collective-permute-done.5.refs_2_), channel_id=1, source_target_pairs={{0,4},{4,0},{8,12},{12,8},{16,20},{20,16},{24,28},{28,24},{1,5},{5... | collective-permute-start | bytes 393224 | tf_op jit(solution)/shard_map/ppermute | solution.py:184
  48.1 0.6 collective-permute-start.9
  48.7 2.3 %collective-permute-start.8 = (bf16[64,1024]{1,0:T(8,128)(2,1)S(1)}, bf16[64,1024]{1,0:T(8,128)(2,1)S(1)}, u32[]{:S(2)}, u32[]{:S(2)}) collective-permute-start(bf16[64,1024]{1,0:T(8,128)(2,1)S(1)} %collective-permute-done.6.refs_4_), channel_id=1, source_target_pairs={{0,8},{4,12},{8,0},{12,4},{16,24},{20,28},{24,16},{28,20},{1,9},{5... | collective-permute-start | bytes 393224 | tf_op jit(solution)/shard_map/ppermute | solution.py:184
  51.0 0.6 %collective-permute-start.7 = (bf16[64,1024]{1,0:T(8,128)(2,1)S(1)}, bf16[64,1024]{1,0:T(8,128)(2,1)S(1)}, u32[]{:S(2)}, u32[]{:S(2)}) collective-permute-start(bf16[64,1024]{1,0:T(8,128)(2,1)S(1)} %collective-permute-done.6.refs_4_), channel_id=1, source_target_pairs={{0,4},{4,0},{8,12},{12,8},{16,20},{20,16},{24,28},{28,24},{1,5},{5... | collective-permute-start | bytes 393224 | tf_op jit(solution)/shard_map/ppermute | solution.py:184
  51.6 0.8 %update_grad.1 = f32[64,1024]{1,0:T(8,128)} custom-call(f32[32,128]{1,0:T(8,128)S(1)} %bitcast.29, f32[64,1024]{1,0:T(8,128)S(1)} %rotate_back.1.unrot_ref), custom_call_target="tpu_custom_call" | custom-call | tf_op jit(solution)/shard_map/update_grad/pallas_call | solution.py:329
  52.4 4.2 %collective-permute-done.11.refs_3_ = bf16[64,1024]{1,0:T(8,128)(2,1)S(1)} collective-permute-done((bf16[64,1024]{1,0:T(8,128)(2,1)S(1)}, bf16[64,1024]{1,0:T(8,128)(2,1)S(1)}, u32[]{:S(2)}, u32[]{:S(2)}) %collective-permute-start.11) | collective-permute-done | bytes 131104 | tf_op jit(solution)/shard_map/ppermute | solution.py:184
  56.7 0.9 %place_own.1.refs_3_ = bf16[512,1024]{1,0:T(8,128)(2,1)} custom-call(bf16[64,1024]{1,0:T(8,128)(2,1)S(1)} %new_weights.1.refs_0_, bf16[64,1024]{1,0:T(8,128)(2,1)S(1)} %collective-permute-done.10.refs_1_, bf16[64,1024]{1,0:T(8,128)(2,1)S(1)} %collective-permute-done.5.refs_2_, bf16[64,1024]{1,0:T(8,128)(2,1)S(1)} %collective-permute-done.11.refs_3_, ...), custom_call_target="tpu_custom_call" | custom-call | tf_op jit(solution)/shard_map/place_own/pallas_call | solution.py:211
  57.6 1.0 %collective-permute-done.7.refs_0_ = bf16[64,1024]{1,0:T(8,128)(2,1)S(1)} collective-permute-done((bf16[64,1024]{1,0:T(8,128)(2,1)S(1)}, bf16[64,1024]{1,0:T(8,128)(2,1)S(1)}, u32[]{:S(2)}, u32[]{:S(2)}) %collective-permute-start.7) | collective-permute-done | bytes 131104 | tf_op jit(solution)/shard_map/ppermute | solution.py:184
  58.5 0.8 %place_far.1 = bf16[512,1024]{1,0:T(8,128)(2,1)} custom-call(bf16[64,1024]{1,0:T(8,128)(2,1)S(1)} %collective-permute-done.7.refs_0_, bf16[64,1024]{1,0:T(8,128)(2,1)S(1)} %collective-permute-done.8.refs_1_, bf16[64,1024]{1,0:T(8,128)(2,1)S(1)} %collective-permute-done.9.refs_2_, bf16[512,1024]{1,0:T(8,128)(2,1)} %place_own.1.refs_3_), custom_call_target="tpu_custom_call", output_to_operand_aliasing={{}: (3, {})} | custom-call | tf_op jit(solution)/shard_map/place_far/pallas_call | solution.py:211
  (27 shorter events, 2.4 us)
Async XLA Ops:
  0.6 5.8 %copy-start = (bf16[1,1,512,1024]{3,2,1,0:T(8,128)(2,1)S(1)}, bf16[1,1,512,1024]{3,2,1,0:T(8,128)(2,1)}, u32[]{:S(2)}) copy-start(bf16[1,1,512,1024]{3,2,1,0:T(8,128)(2,1)} %param.5) | copy-start | bytes 3145732
  1.8 18.2 %collective-permute-start.1 = (bf16[2,64,1024]{2,1,0:T(8,128)(2,1)S(1)}, bf16[2,64,1024]{2,1,0:T(8,128)(2,1)S(1)}, u32[]{:S(2)}, u32[]{:S(2)}) collective-permute-start(bf16[2,64,1024]{2,1,0:T(8,128)(2,1)S(1)} %get-tuple-element.28), channel_id=1, source_target_pairs={{0,8},{4,12},{8,0},{12,4},{16,24},{20,28},{24,16},{28,20},{1,9},{5... | collective-permute-start | bytes 786440 | tf_op jit(solution)/shard_map/ppermute | solution.py:184
  4.9 15.1 %collective-permute-start = (bf16[2,64,1024]{2,1,0:T(8,128)(2,1)S(1)}, bf16[2,64,1024]{2,1,0:T(8,128)(2,1)S(1)}, u32[]{:S(2)}, u32[]{:S(2)}) collective-permute-start(bf16[2,64,1024]{2,1,0:T(8,128)(2,1)S(1)} %get-tuple-element.29), channel_id=1, source_target_pairs={{0,4},{4,0},{8,12},{12,8},{16,20},{20,16},{24,28},{28,24},{1,5},{5... | collective-permute-start | bytes 786440 | tf_op jit(solution)/shard_map/ppermute | solution.py:184
  7.3 13.1 %collective-permute-start.3 = (bf16[64,1024]{1,0:T(8,128)(2,1)S(1)}, bf16[64,1024]{1,0:T(8,128)(2,1)S(1)}, u32[]{:S(2)}, u32[]{:S(2)}) collective-permute-start(bf16[64,1024]{1,0:T(8,128)(2,1)S(1)} %get-tuple-element.26), channel_id=1, source_target_pairs={{0,12},{4,8},{8,4},{12,0},{16,28},{20,24},{24,20},{28,16},{1,13},{... | collective-permute-start | bytes 393224 | tf_op jit(solution)/shard_map/ppermute | solution.py:184
  7.4 12.6 %all-to-all-start = ((f32[8,1,128]{2,1,0:T(1,128)}), f32[8,1,128]{2,1,0:T(1,128)S(1)}, u32[]{:S(2)}, u32[]{:S(2)}) async-start(f32[8,1,128]{2,1,0:T(1,128)} %bitcast.8), calls=%async_computation | async-start | bytes 8192 | tf_op jit(solution)/shard_map/all_to_all | solution.py:274
  13.6 7.8 %collective-permute-start.2 = (bf16[64,1024]{1,0:T(8,128)(2,1)S(1)}, bf16[64,1024]{1,0:T(8,128)(2,1)S(1)}, u32[]{:S(2)}, u32[]{:S(2)}) collective-permute-start(bf16[64,1024]{1,0:T(8,128)(2,1)S(1)} %get-tuple-element.27), channel_id=1, source_target_pairs={{0,12},{4,8},{8,4},{12,0},{16,28},{20,24},{24,20},{28,16},{1,13},{... | collective-permute-start | bytes 393224 | tf_op jit(solution)/shard_map/ppermute | solution.py:184
  16.5 3.5 %copy-start.1 = (bf16[256,256]{1,0:T(8,128)(2,1)S(1)}, bf16[256,256]{1,0:T(8,128)(2,1)}, u32[]{:S(2)}) copy-start(bf16[256,256]{1,0:T(8,128)(2,1)} %constant.37.clone.refs_6_.refs_5_.matrix_ref) | copy-start | bytes 393220
  16.5 3.5 %copy-start.4 = (s32[1,1024]{1,0:T(1,128)S(1)}, s32[1,1024]{1,0:T(1,128)}, u32[]{:S(2)}) copy-start(s32[1,1024]{1,0:T(1,128)} %sign_ref.1) | copy-start | bytes 12292
  20.8 7.3 %collective-permute-start.4 = (s16[64,1024]{1,0:T(8,128)(2,1)S(1)}, s16[64,1024]{1,0:T(8,128)(2,1)S(1)}, u32[]{:S(2)}, u32[]{:S(2)}) collective-permute-start(s16[64,1024]{1,0:T(8,128)(2,1)S(1)} %proxy_blocks.1), channel_id=1, source_target_pairs={{0,16},{4,20},{8,24},{12,28},{16,0},{20,4},{24,8},{28,12},{1,17},{... | collective-permute-start | bytes 393224 | tf_op jit(solution)/shard_map/ppermute | solution.py:184
  28.8 9.6 %all-to-all-start.1 = ((f32[32,1,128]{2,1,0:T(1,128)}), f32[32,1,128]{2,1,0:T(1,128)S(1)}, u32[]{:S(2)}, u32[]{:S(2)}) async-start(f32[32,1,128]{2,1,0:T(1,128)} %get-tuple-element.22), calls=%async_computation.1 | async-start | bytes 32768 | tf_op jit(solution)/shard_map/all_to_all | solution.py:320
  31.3 7.1 %copy-start.2 = (bf16[1,64,1024]{2,1,0:T(8,128)(2,1)S(1)}, bf16[1,64,1024]{2,1,0:T(8,128)(2,1)}, u32[]{:S(2)}) copy-start(bf16[1,64,1024]{2,1,0:T(8,128)(2,1)} %param.7) | copy-start | bytes 393220
  31.3 7.1 %copy-start.3 = (bf16[1,64,1024]{2,1,0:T(8,128)(2,1)S(1)}, bf16[1,64,1024]{2,1,0:T(8,128)(2,1)}, u32[]{:S(2)}) copy-start(bf16[1,64,1024]{2,1,0:T(8,128)(2,1)} %param.8) | copy-start | bytes 393220
  38.6 8.9 %collective-permute-start.6 = (bf16[64,1024]{1,0:T(8,128)(2,1)S(1)}, bf16[64,1024]{1,0:T(8,128)(2,1)S(1)}, u32[]{:S(2)}, u32[]{:S(2)}) collective-permute-start(bf16[64,1024]{1,0:T(8,128)(2,1)S(1)} %new_weights.1.refs_0_), channel_id=1, source_target_pairs={{0,16},{4,20},{8,24},{12,28},{16,0},{20,4},{24,8},{28,12},{1,17},{... | collective-permute-start | bytes 393224 | tf_op jit(solution)/shard_map/ppermute | solution.py:184
  39.2 8.3 %collective-permute-start.5 = (bf16[64,1024]{1,0:T(8,128)(2,1)S(1)}, bf16[64,1024]{1,0:T(8,128)(2,1)S(1)}, u32[]{:S(2)}, u32[]{:S(2)}) collective-permute-start(bf16[64,1024]{1,0:T(8,128)(2,1)S(1)} %new_weights.1.refs_0_), channel_id=1, source_target_pairs={{0,8},{4,12},{8,0},{12,4},{16,24},{20,28},{24,16},{28,20},{1,9},{5... | collective-permute-start | bytes 393224 | tf_op jit(solution)/shard_map/ppermute | solution.py:184
  39.8 12.7 %collective-permute-start.10 = (bf16[64,1024]{1,0:T(8,128)(2,1)S(1)}, bf16[64,1024]{1,0:T(8,128)(2,1)S(1)}, u32[]{:S(2)}, u32[]{:S(2)}) collective-permute-start(bf16[64,1024]{1,0:T(8,128)(2,1)S(1)} %new_weights.1.refs_0_), channel_id=1, source_target_pairs={{0,4},{4,0},{8,12},{12,8},{16,20},{20,16},{24,28},{28,24},{1,5},{5... | collective-permute-start | bytes 393224 | tf_op jit(solution)/shard_map/ppermute | solution.py:184
  47.5 9.2 %collective-permute-start.11 = (bf16[64,1024]{1,0:T(8,128)(2,1)S(1)}, bf16[64,1024]{1,0:T(8,128)(2,1)S(1)}, u32[]{:S(2)}, u32[]{:S(2)}) collective-permute-start(bf16[64,1024]{1,0:T(8,128)(2,1)S(1)} %collective-permute-done.5.refs_2_), channel_id=1, source_target_pairs={{0,4},{4,0},{8,12},{12,8},{16,20},{20,16},{24,28},{28,24},{1,5},{5... | collective-permute-start | bytes 393224 | tf_op jit(solution)/shard_map/ppermute | solution.py:184
  48.1 9.4 %collective-permute-start.9 = (bf16[64,1024]{1,0:T(8,128)(2,1)S(1)}, bf16[64,1024]{1,0:T(8,128)(2,1)S(1)}, u32[]{:S(2)}, u32[]{:S(2)}) collective-permute-start(bf16[64,1024]{1,0:T(8,128)(2,1)S(1)} %collective-permute-done.6.refs_4_), channel_id=1, source_target_pairs={{0,12},{4,8},{8,4},{12,0},{16,28},{20,24},{24,20},{28,16},{1,13},{... | collective-permute-start | bytes 393224 | tf_op jit(solution)/shard_map/ppermute | solution.py:184
  48.7 8.9 %collective-permute-start.8 = (bf16[64,1024]{1,0:T(8,128)(2,1)S(1)}, bf16[64,1024]{1,0:T(8,128)(2,1)S(1)}, u32[]{:S(2)}, u32[]{:S(2)}) collective-permute-start(bf16[64,1024]{1,0:T(8,128)(2,1)S(1)} %collective-permute-done.6.refs_4_), channel_id=1, source_target_pairs={{0,8},{4,12},{8,0},{12,4},{16,24},{20,28},{24,16},{28,20},{1,9},{5... | collective-permute-start | bytes 393224 | tf_op jit(solution)/shard_map/ppermute | solution.py:184
  51.0 7.5 %collective-permute-start.7 = (bf16[64,1024]{1,0:T(8,128)(2,1)S(1)}, bf16[64,1024]{1,0:T(8,128)(2,1)S(1)}, u32[]{:S(2)}, u32[]{:S(2)}) collective-permute-start(bf16[64,1024]{1,0:T(8,128)(2,1)S(1)} %collective-permute-done.6.refs_4_), channel_id=1, source_target_pairs={{0,4},{4,0},{8,12},{12,8},{16,20},{20,16},{24,28},{28,24},{1,5},{5... | collective-permute-start | bytes 393224 | tf_op jit(solution)/shard_map/ppermute | solution.py:184

commit v28 on v19

--- a/solution.py
+++ b/solution.py
@@ -261,7 +261,7 @@
     x_count = chips_along_x(replicas)
     aligned = [m for m in range(1, near) if m % x_count == 0 or m < x_count]
     diagonal = [m for m in range(1, near) if m not in aligned]
-    pairs = [swap(pair_of(grads, me ^ mask), mask) for mask in aligned]
+    pairs = [swap(pair_of(grads, me ^ mask), mask) for mask in reversed(aligned)]
     sums = pl.pallas_call(
         sums_kernel,
         in_specs=[array],

time: 56.5 us -> 56.5 us (level)
  no operation moved by 1% of the time
where the time goes in v28:
time: 56.5 us; the launch traced here: 56.3 us
  waiting for transfers between devices  25.8 us (46%)
  starting transfers between devices  22.7 us (40%)
  Pallas kernels  5.77 us (10%)
  local copies, waits for them, and re-layouts  1.21 us (2%)
  between operations  0.81 us (1%)
    ppermute x12, waiting for transfers between devices, swap(): return lax.ppermute(value, 'dp', [(i, i ^ mask) for i in range(size)])  15.6 us
    ppermute x12, starting transfers between devices, swap(): return lax.ppermute(value, 'dp', [(i, i ^ mask) for i in range(size)])  13.9 us
    all_to_all x1, waiting for transfers between devices, on_device(): lax.all_to_all(squares, ('dp', 'expert'), split_axis=0, concat_axis=0, ti...  6.72 us
    all_to_all x1, starting transfers between devices, on_device(): lax.all_to_all(sums.reshape(replicas, 1, 2 * owned), 'dp', split_axis=0,...  6.21 us
    all_to_all x1, waiting for transfers between devices, on_device(): lax.all_to_all(sums.reshape(replicas, 1, 2 * owned), 'dp', split_axis=0,...  3.44 us
    all_to_all x1, starting transfers between devices, on_device(): lax.all_to_all(squares, ('dp', 'expert'), split_axis=0, concat_axis=0, ti...  2.54 us
    pallas_call x2, Pallas kernels, place_pieces(): pl.pallas_call(functools.partial(place_kernel, places, owned), in_specs=s...  1.63 us
    reshape x2, local copies, waits for them, and re-layouts, pair_of(): lax.dynamic_slice_in_dim(source, index % near, 1, 1)  1.17 us
  transfers between devices with their start and end apart: 14, of which 9 were waited for; matrix products, arithmetic and copies ran while one was open for 0% of the time, Pallas kernels for 7%

profile of v28, /device:TPU:0, one launch (start us, length us, event | category | flops | bytes accessed | tf_op | source)
XLA Modules:
  0.0 56.3 jit_solution(8226674904949463433)
XLA Ops:
  0.7 1.2 %dynamic-slice_bitcast_fusion.1 = (bf16[2,64,1024]{2,1,0:T(8,128)(2,1)S(1)}, bf16[2,64,1024]{2,1,0:T(8,128)(2,1)S(1)}) fusion(bf16[2,4,64,1024]{3,2,1,0:T(8,128)(2,1)} %bitcast.24, s32[]{:T(128)S(6)} %select_n.33, s32[]{:T(128)S(6)} %select_n.31), kind=kLoop, calls=%fused_computation.1 | loop fusion | bytes 1048584 | tf_op jit(solution)/shard_map/reshape | solution.py:255
  1.8 3.0 %collective-permute-start.1 = (bf16[2,64,1024]{2,1,0:T(8,128)(2,1)S(1)}, bf16[2,64,1024]{2,1,0:T(8,128)(2,1)S(1)}, u32[]{:S(2)}, u32[]{:S(2)}) collective-permute-start(bf16[2,64,1024]{2,1,0:T(8,128)(2,1)S(1)} %get-tuple-element.24), channel_id=1, source_target_pairs={{0,4},{4,0},{8,12},{12,8},{16,20},{20,16},{24,28},{28,24},{1,5},{5... | collective-permute-start | bytes 786440 | tf_op jit(solution)/shard_map/ppermute | solution.py:184
  4.8 1.6 %collective-permute-start = (bf16[2,64,1024]{2,1,0:T(8,128)(2,1)S(1)}, bf16[2,64,1024]{2,1,0:T(8,128)(2,1)S(1)}, u32[]{:S(2)}, u32[]{:S(2)}) collective-permute-start(bf16[2,64,1024]{2,1,0:T(8,128)(2,1)S(1)} %get-tuple-element.25), channel_id=1, source_target_pairs={{0,8},{4,12},{8,0},{12,4},{16,24},{20,28},{24,16},{28,20},{1,9},{5... | collective-permute-start | bytes 786440 | tf_op jit(solution)/shard_map/ppermute | solution.py:184
  6.4 0.9 %sum_squares.1 = f32[2,4,1,128]{3,2,1,0:T(1,128)} custom-call(bf16[2,4,64,1024]{3,2,1,0:T(8,128)(2,1)S(1)} %bitcast.25), custom_call_target="tpu_custom_call" | custom-call | tf_op jit(solution)/shard_map/sum_squares/pallas_call | solution.py:265
  7.4 6.2 %all-to-all-start = ((f32[8,1,128]{2,1,0:T(1,128)}), f32[8,1,128]{2,1,0:T(1,128)S(1)}, u32[]{:S(2)}, u32[]{:S(2)}) async-start(f32[8,1,128]{2,1,0:T(1,128)} %bitcast.8), calls=%async_computation | async-start | bytes 8192 | tf_op jit(solution)/shard_map/all_to_all | solution.py:273
  13.6 2.9 %collective-permute-start.2 = (bf16[64,1024]{1,0:T(8,128)(2,1)S(1)}, bf16[64,1024]{1,0:T(8,128)(2,1)S(1)}, u32[]{:S(2)}, u32[]{:S(2)}) collective-permute-start(bf16[64,1024]{1,0:T(8,128)(2,1)S(1)} %get-tuple-element.23), channel_id=1, source_target_pairs={{0,12},{4,8},{8,4},{12,0},{16,28},{20,24},{24,20},{28,16},{1,13},{... | collective-permute-start | bytes 393224 | tf_op jit(solution)/shard_map/ppermute | solution.py:184
  16.6 3.4 %all-to-all-done = f32[8,1,128]{2,1,0:T(1,128)S(1)} async-done(((f32[8,1,128]{2,1,0:T(1,128)}), f32[8,1,128]{2,1,0:T(1,128)S(1)}, u32[]{:S(2)}, u32[]{:S(2)}) %all-to-all-start) | async-done | bytes 4128 | tf_op jit(solution)/shard_map/all_to_all | solution.py:273
  20.8 0.6 %collective-permute-start.4 = (s16[64,1024]{1,0:T(8,128)(2,1)S(1)}, s16[64,1024]{1,0:T(8,128)(2,1)S(1)}, u32[]{:S(2)}, u32[]{:S(2)}) collective-permute-start(s16[64,1024]{1,0:T(8,128)(2,1)S(1)} %proxy_blocks.1), channel_id=1, source_target_pairs={{0,16},{4,20},{8,24},{12,28},{16,0},{20,4},{24,8},{28,12},{1,17},{... | collective-permute-start | bytes 393224 | tf_op jit(solution)/shard_map/ppermute | solution.py:184
  21.4 0.6 owner_blocks.1
  22.0 6.1 %collective-permute-done.4.far_ref = s16[64,1024]{1,0:T(8,128)(2,1)S(1)} collective-permute-done((s16[64,1024]{1,0:T(8,128)(2,1)S(1)}, s16[64,1024]{1,0:T(8,128)(2,1)S(1)}, u32[]{:S(2)}, u32[]{:S(2)}) %collective-permute-start.4) | collective-permute-done | bytes 131104 | tf_op jit(solution)/shard_map/ppermute | solution.py:184
  28.1 0.7 %finish_blocks.1 = (f32[64,1024]{1,0:T(8,128)S(1)}, f32[32,1,128]{2,1,0:T(1,128)}) custom-call(f32[64,1024]{1,0:T(8,128)S(1)} %get-tuple-element.14.near_ref, s16[64,1024]{1,0:T(8,128)(2,1)S(1)} %collective-permute-done.4.far_ref, f32[64,128]{1,0:T(8,128)S(1)} %get-tuple-element.18.scale_ref, f32[64,128]{1,0:T(8,128)S(1)} %get-tuple-element.19.step_ref), custom_call_target="tpu_custom_call" | custom-call | tf_op jit(solution)/shard_map/finish_blocks/pallas_call | solution.py:303
  28.8 2.5 %all-to-all-start.1 = ((f32[32,1,128]{2,1,0:T(1,128)}), f32[32,1,128]{2,1,0:T(1,128)S(1)}, u32[]{:S(2)}, u32[]{:S(2)}) async-start(f32[32,1,128]{2,1,0:T(1,128)} %get-tuple-element.20), calls=%async_computation.1 | async-start | bytes 32768 | tf_op jit(solution)/shard_map/all_to_all | solution.py:319
  31.7 6.7 %all-to-all-done.1 = f32[32,1,128]{2,1,0:T(1,128)S(1)} async-done(((f32[32,1,128]{2,1,0:T(1,128)}), f32[32,1,128]{2,1,0:T(1,128)S(1)}, u32[]{:S(2)}, u32[]{:S(2)}) %all-to-all-start.1) | async-done | bytes 16416 | tf_op jit(solution)/shard_map/all_to_all | solution.py:319
  38.6 0.6 %collective-permute-start.10 = (bf16[64,1024]{1,0:T(8,128)(2,1)S(1)}, bf16[64,1024]{1,0:T(8,128)(2,1)S(1)}, u32[]{:S(2)}, u32[]{:S(2)}) collective-permute-start(bf16[64,1024]{1,0:T(8,128)(2,1)S(1)} %new_weights.1.refs_0_), channel_id=1, source_target_pairs={{0,8},{4,12},{8,0},{12,4},{16,24},{20,28},{24,16},{28,20},{1,9},{5... | collective-permute-start | bytes 393224 | tf_op jit(solution)/shard_map/ppermute | solution.py:184
  39.2 0.6 collective-permute-start.5
  40.3 5.2 %collective-permute-done.10.refs_2_ = bf16[64,1024]{1,0:T(8,128)(2,1)S(1)} collective-permute-done((bf16[64,1024]{1,0:T(8,128)(2,1)S(1)}, bf16[64,1024]{1,0:T(8,128)(2,1)S(1)}, u32[]{:S(2)}, u32[]{:S(2)}) %collective-permute-start.10) | collective-permute-done | bytes 131104 | tf_op jit(solution)/shard_map/ppermute | solution.py:184
  45.5 0.5 collective-permute-start.11
  46.1 1.8 %collective-permute-done.5.refs_4_ = bf16[64,1024]{1,0:T(8,128)(2,1)S(1)} collective-permute-done((bf16[64,1024]{1,0:T(8,128)(2,1)S(1)}, bf16[64,1024]{1,0:T(8,128)(2,1)S(1)}, u32[]{:S(2)}, u32[]{:S(2)}) %collective-permute-start.5) | collective-permute-done | bytes 131104 | tf_op jit(solution)/shard_map/ppermute | solution.py:184
  47.8 2.1 %collective-permute-start.7 = (bf16[64,1024]{1,0:T(8,128)(2,1)S(1)}, bf16[64,1024]{1,0:T(8,128)(2,1)S(1)}, u32[]{:S(2)}, u32[]{:S(2)}) collective-permute-start(bf16[64,1024]{1,0:T(8,128)(2,1)S(1)} %collective-permute-done.5.refs_4_), channel_id=1, source_target_pairs={{0,8},{4,12},{8,0},{12,4},{16,24},{20,28},{24,16},{28,20},{1,9},{5... | collective-permute-start | bytes 393224 | tf_op jit(solution)/shard_map/ppermute | solution.py:184
  49.9 1.4 %collective-permute-start.6 = (bf16[64,1024]{1,0:T(8,128)(2,1)S(1)}, bf16[64,1024]{1,0:T(8,128)(2,1)S(1)}, u32[]{:S(2)}, u32[]{:S(2)}) collective-permute-start(bf16[64,1024]{1,0:T(8,128)(2,1)S(1)} %collective-permute-done.5.refs_4_), channel_id=1, source_target_pairs={{0,4},{4,0},{8,12},{12,8},{16,20},{20,16},{24,28},{28,24},{1,5},{5... | collective-permute-start | bytes 393224 | tf_op jit(solution)/shard_map/ppermute | solution.py:184
  51.3 0.8 %update_grad.1 = f32[64,1024]{1,0:T(8,128)} custom-call(f32[32,128]{1,0:T(8,128)S(1)} %bitcast.29, f32[64,1024]{1,0:T(8,128)S(1)} %rotate_back.1.unrot_ref), custom_call_target="tpu_custom_call" | custom-call | tf_op jit(solution)/shard_map/update_grad/pallas_call | solution.py:328
  52.4 0.9 %place_own.1.refs_3_ = bf16[512,1024]{1,0:T(8,128)(2,1)} custom-call(bf16[64,1024]{1,0:T(8,128)(2,1)S(1)} %new_weights.1.refs_0_, bf16[64,1024]{1,0:T(8,128)(2,1)S(1)} %collective-permute-done.9.refs_1_, bf16[64,1024]{1,0:T(8,128)(2,1)S(1)} %collective-permute-done.10.refs_2_, bf16[64,1024]{1,0:T(8,128)(2,1)S(1)} %collective-permute-done.11.refs_3_, ...), custom_call_target="tpu_custom_call" | custom-call | tf_op jit(solution)/shard_map/place_own/pallas_call | solution.py:211
  54.3 1.2 %collective-permute-done.6.refs_0_ = bf16[64,1024]{1,0:T(8,128)(2,1)S(1)} collective-permute-done((bf16[64,1024]{1,0:T(8,128)(2,1)S(1)}, bf16[64,1024]{1,0:T(8,128)(2,1)S(1)}, u32[]{:S(2)}, u32[]{:S(2)}) %collective-permute-start.6) | collective-permute-done | bytes 131104 | tf_op jit(solution)/shard_map/ppermute | solution.py:184
  55.5 0.8 %place_far.1 = bf16[512,1024]{1,0:T(8,128)(2,1)} custom-call(bf16[64,1024]{1,0:T(8,128)(2,1)S(1)} %collective-permute-done.6.refs_0_, bf16[64,1024]{1,0:T(8,128)(2,1)S(1)} %collective-permute-done.7.refs_1_, bf16[64,1024]{1,0:T(8,128)(2,1)S(1)} %collective-permute-done.8.refs_2_, bf16[512,1024]{1,0:T(8,128)(2,1)} %place_own.1.refs_3_), custom_call_target="tpu_custom_call", output_to_operand_aliasing={{}: (3, {})} | custom-call | tf_op jit(solution)/shard_map/place_far/pallas_call | solution.py:211
  (27 shorter events, 3.1 us)
Async XLA Ops:
  0.6 5.8 %copy-start = (bf16[1,1,512,1024]{3,2,1,0:T(8,128)(2,1)S(1)}, bf16[1,1,512,1024]{3,2,1,0:T(8,128)(2,1)}, u32[]{:S(2)}) copy-start(bf16[1,1,512,1024]{3,2,1,0:T(8,128)(2,1)} %param.5) | copy-start | bytes 3145732
  1.8 18.2 %collective-permute-start.1 = (bf16[2,64,1024]{2,1,0:T(8,128)(2,1)S(1)}, bf16[2,64,1024]{2,1,0:T(8,128)(2,1)S(1)}, u32[]{:S(2)}, u32[]{:S(2)}) collective-permute-start(bf16[2,64,1024]{2,1,0:T(8,128)(2,1)S(1)} %get-tuple-element.24), channel_id=1, source_target_pairs={{0,4},{4,0},{8,12},{12,8},{16,20},{20,16},{24,28},{28,24},{1,5},{5... | collective-permute-start | bytes 786440 | tf_op jit(solution)/shard_map/ppermute | solution.py:184
  4.8 15.2 %collective-permute-start = (bf16[2,64,1024]{2,1,0:T(8,128)(2,1)S(1)}, bf16[2,64,1024]{2,1,0:T(8,128)(2,1)S(1)}, u32[]{:S(2)}, u32[]{:S(2)}) collective-permute-start(bf16[2,64,1024]{2,1,0:T(8,128)(2,1)S(1)} %get-tuple-element.25), channel_id=1, source_target_pairs={{0,8},{4,12},{8,0},{12,4},{16,24},{20,28},{24,16},{28,20},{1,9},{5... | collective-permute-start | bytes 786440 | tf_op jit(solution)/shard_map/ppermute | solution.py:184
  7.3 13.1 %collective-permute-start.3 = (bf16[64,1024]{1,0:T(8,128)(2,1)S(1)}, bf16[64,1024]{1,0:T(8,128)(2,1)S(1)}, u32[]{:S(2)}, u32[]{:S(2)}) collective-permute-start(bf16[64,1024]{1,0:T(8,128)(2,1)S(1)} %get-tuple-element.22), channel_id=1, source_target_pairs={{0,12},{4,8},{8,4},{12,0},{16,28},{20,24},{24,20},{28,16},{1,13},{... | collective-permute-start | bytes 393224 | tf_op jit(solution)/shard_map/ppermute | solution.py:184
  7.4 12.6 %all-to-all-start = ((f32[8,1,128]{2,1,0:T(1,128)}), f32[8,1,128]{2,1,0:T(1,128)S(1)}, u32[]{:S(2)}, u32[]{:S(2)}) async-start(f32[8,1,128]{2,1,0:T(1,128)} %bitcast.8), calls=%async_computation | async-start | bytes 8192 | tf_op jit(solution)/shard_map/all_to_all | solution.py:273
  13.6 7.8 %collective-permute-start.2 = (bf16[64,1024]{1,0:T(8,128)(2,1)S(1)}, bf16[64,1024]{1,0:T(8,128)(2,1)S(1)}, u32[]{:S(2)}, u32[]{:S(2)}) collective-permute-start(bf16[64,1024]{1,0:T(8,128)(2,1)S(1)} %get-tuple-element.23), channel_id=1, source_target_pairs={{0,12},{4,8},{8,4},{12,0},{16,28},{20,24},{24,20},{28,16},{1,13},{... | collective-permute-start | bytes 393224 | tf_op jit(solution)/shard_map/ppermute | solution.py:184
  16.5 3.5 %copy-start.1 = (bf16[256,256]{1,0:T(8,128)(2,1)S(1)}, bf16[256,256]{1,0:T(8,128)(2,1)}, u32[]{:S(2)}) copy-start(bf16[256,256]{1,0:T(8,128)(2,1)} %constant.37.clone.refs_6_.refs_5_.matrix_ref) | copy-start | bytes 393220
  16.5 3.5 %copy-start.4 = (s32[1,1024]{1,0:T(1,128)S(1)}, s32[1,1024]{1,0:T(1,128)}, u32[]{:S(2)}) copy-start(s32[1,1024]{1,0:T(1,128)} %sign_ref.1) | copy-start | bytes 12292
  20.8 7.3 %collective-permute-start.4 = (s16[64,1024]{1,0:T(8,128)(2,1)S(1)}, s16[64,1024]{1,0:T(8,128)(2,1)S(1)}, u32[]{:S(2)}, u32[]{:S(2)}) collective-permute-start(s16[64,1024]{1,0:T(8,128)(2,1)S(1)} %proxy_blocks.1), channel_id=1, source_target_pairs={{0,16},{4,20},{8,24},{12,28},{16,0},{20,4},{24,8},{28,12},{1,17},{... | collective-permute-start | bytes 393224 | tf_op jit(solution)/shard_map/ppermute | solution.py:184
  28.8 9.6 %all-to-all-start.1 = ((f32[32,1,128]{2,1,0:T(1,128)}), f32[32,1,128]{2,1,0:T(1,128)S(1)}, u32[]{:S(2)}, u32[]{:S(2)}) async-start(f32[32,1,128]{2,1,0:T(1,128)} %get-tuple-element.20), calls=%async_computation.1 | async-start | bytes 32768 | tf_op jit(solution)/shard_map/all_to_all | solution.py:319
  31.3 7.1 %copy-start.2 = (bf16[1,64,1024]{2,1,0:T(8,128)(2,1)S(1)}, bf16[1,64,1024]{2,1,0:T(8,128)(2,1)}, u32[]{:S(2)}) copy-start(bf16[1,64,1024]{2,1,0:T(8,128)(2,1)} %param.7) | copy-start | bytes 393220
  31.3 7.1 %copy-start.3 = (bf16[1,64,1024]{2,1,0:T(8,128)(2,1)S(1)}, bf16[1,64,1024]{2,1,0:T(8,128)(2,1)}, u32[]{:S(2)}) copy-start(bf16[1,64,1024]{2,1,0:T(8,128)(2,1)} %param.8) | copy-start | bytes 393220
  38.6 6.9 %collective-permute-start.10 = (bf16[64,1024]{1,0:T(8,128)(2,1)S(1)}, bf16[64,1024]{1,0:T(8,128)(2,1)S(1)}, u32[]{:S(2)}, u32[]{:S(2)}) collective-permute-start(bf16[64,1024]{1,0:T(8,128)(2,1)S(1)} %new_weights.1.refs_0_), channel_id=1, source_target_pairs={{0,8},{4,12},{8,0},{12,4},{16,24},{20,28},{24,16},{28,20},{1,9},{5... | collective-permute-start | bytes 393224 | tf_op jit(solution)/shard_map/ppermute | solution.py:184
  39.2 8.6 %collective-permute-start.5 = (bf16[64,1024]{1,0:T(8,128)(2,1)S(1)}, bf16[64,1024]{1,0:T(8,128)(2,1)S(1)}, u32[]{:S(2)}, u32[]{:S(2)}) collective-permute-start(bf16[64,1024]{1,0:T(8,128)(2,1)S(1)} %new_weights.1.refs_0_), channel_id=1, source_target_pairs={{0,16},{4,20},{8,24},{12,28},{16,0},{20,4},{24,8},{28,12},{1,17},{... | collective-permute-start | bytes 393224 | tf_op jit(solution)/shard_map/ppermute | solution.py:184
  39.8 12.4 %collective-permute-start.9 = (bf16[64,1024]{1,0:T(8,128)(2,1)S(1)}, bf16[64,1024]{1,0:T(8,128)(2,1)S(1)}, u32[]{:S(2)}, u32[]{:S(2)}) collective-permute-start(bf16[64,1024]{1,0:T(8,128)(2,1)S(1)} %new_weights.1.refs_0_), channel_id=1, source_target_pairs={{0,4},{4,0},{8,12},{12,8},{16,20},{20,16},{24,28},{28,24},{1,5},{5... | collective-permute-start | bytes 393224 | tf_op jit(solution)/shard_map/ppermute | solution.py:184
  45.5 6.9 %collective-permute-start.11 = (bf16[64,1024]{1,0:T(8,128)(2,1)S(1)}, bf16[64,1024]{1,0:T(8,128)(2,1)S(1)}, u32[]{:S(2)}, u32[]{:S(2)}) collective-permute-start(bf16[64,1024]{1,0:T(8,128)(2,1)S(1)} %collective-permute-done.10.refs_2_), channel_id=1, source_target_pairs={{0,4},{4,0},{8,12},{12,8},{16,20},{20,16},{24,28},{28,24},{1,5},{5... | collective-permute-start | bytes 393224 | tf_op jit(solution)/shard_map/ppermute | solution.py:184
  47.8 6.0 %collective-permute-start.8 = (bf16[64,1024]{1,0:T(8,128)(2,1)S(1)}, bf16[64,1024]{1,0:T(8,128)(2,1)S(1)}, u32[]{:S(2)}, u32[]{:S(2)}) collective-permute-start(bf16[64,1024]{1,0:T(8,128)(2,1)S(1)} %collective-permute-done.5.refs_4_), channel_id=1, source_target_pairs={{0,12},{4,8},{8,4},{12,0},{16,28},{20,24},{24,20},{28,16},{1,13},{... | collective-permute-start | bytes 393224 | tf_op jit(solution)/shard_map/ppermute | solution.py:184
  47.8 6.4 %collective-permute-start.7 = (bf16[64,1024]{1,0:T(8,128)(2,1)S(1)}, bf16[64,1024]{1,0:T(8,128)(2,1)S(1)}, u32[]{:S(2)}, u32[]{:S(2)}) collective-permute-start(bf16[64,1024]{1,0:T(8,128)(2,1)S(1)} %collective-permute-done.5.refs_4_), channel_id=1, source_target_pairs={{0,8},{4,12},{8,0},{12,4},{16,24},{20,28},{24,16},{28,20},{1,9},{5... | collective-permute-start | bytes 393224 | tf_op jit(solution)/shard_map/ppermute | solution.py:184
  49.9 5.6 %collective-permute-start.6 = (bf16[64,1024]{1,0:T(8,128)(2,1)S(1)}, bf16[64,1024]{1,0:T(8,128)(2,1)S(1)}, u32[]{:S(2)}, u32[]{:S(2)}) collective-permute-start(bf16[64,1024]{1,0:T(8,128)(2,1)S(1)} %collective-permute-done.5.refs_4_), channel_id=1, source_target_pairs={{0,4},{4,0},{8,12},{12,8},{16,20},{20,16},{24,28},{28,24},{1,5},{5... | collective-permute-start | bytes 393224 | tf_op jit(solution)/shard_map/ppermute | solution.py:184

commit v29 on v26

--- a/solution.py
+++ b/solution.py
@@ -232,7 +232,8 @@
     own = [(m, 0, piece) for m, piece in own.items()]
     spread = [(near + m, 0, swap(far, m)) for m in range(1, near)]
     out = place_pieces(own + [(near, 0, far)], owned, replicas, None, "place_own")
-    out = place_pieces(spread, owned, replicas, out, "place_far")
+    out = place_pieces(spread[1:], owned, replicas, out, "place_far")
+    out = place_pieces(spread[:1], owned, replicas, out, "place_last")
     return out.reshape(1, replicas * owned, width)
 
 

time: 56.5 us -> 56.4 us (level)
  waiting for transfers between devices: 25.8 us -> 25 us
  Pallas kernels: 5.81 us -> 6.42 us
    ppermute x12, waiting for transfers between devices: 15.6 us -> 14.9 us  [swap(): return lax.ppermute(value, 'dp', [(i, i ^ mask) for i in range(size)])]
    pallas_call x2 -> x3, Pallas kernels: 1.63 us -> 2.25 us  [place_pieces(): pl.pallas_call(functools.partial(place_kernel, places, owned), in_specs=s...]
  transfers between devices with their start and end apart: 14 -> 14, of which waited for: 9 -> 9; matrix products, arithmetic and copies ran while one was open for 0% -> 0% of each run, Pallas kernels for 7% -> 9%
where the time goes in v29:
time: 56.4 us; the launch traced here: 56.2 us
  waiting for transfers between devices  25 us (44%)
  starting transfers between devices  22.7 us (40%)
  Pallas kernels  6.42 us (11%)
  local copies, waits for them, and re-layouts  1.21 us (2%)
  between operations  0.81 us (1%)
    ppermute x12, waiting for transfers between devices, swap(): return lax.ppermute(value, 'dp', [(i, i ^ mask) for i in range(size)])  14.9 us
    ppermute x12, starting transfers between devices, swap(): return lax.ppermute(value, 'dp', [(i, i ^ mask) for i in range(size)])  14 us
    all_to_all x1, waiting for transfers between devices, on_device(): lax.all_to_all(squares, ('dp', 'expert'), split_axis=0, concat_axis=0, ti...  6.68 us
    all_to_all x1, starting transfers between devices, on_device(): lax.all_to_all(sums.reshape(replicas, 1, 2 * owned), 'dp', split_axis=0,...  6.18 us
    all_to_all x1, waiting for transfers between devices, on_device(): lax.all_to_all(sums.reshape(replicas, 1, 2 * owned), 'dp', split_axis=0,...  3.44 us
    all_to_all x1, starting transfers between devices, on_device(): lax.all_to_all(squares, ('dp', 'expert'), split_axis=0, concat_axis=0, ti...  2.54 us
    pallas_call x3, Pallas kernels, place_pieces(): pl.pallas_call(functools.partial(place_kernel, places, owned), in_specs=s...  2.25 us
    reshape x2, local copies, waits for them, and re-layouts, pair_of(): lax.dynamic_slice_in_dim(source, index % near, 1, 1)  1.17 us
  transfers between devices with their start and end apart: 14, of which 9 were waited for; matrix products, arithmetic and copies ran while one was open for 0% of the time, Pallas kernels for 9%

profile of v29, /device:TPU:0, one launch (start us, length us, event | category | flops | bytes accessed | tf_op | source)
XLA Modules:
  0.0 56.2 jit_solution(1467161438635000920)
XLA Ops:
  0.7 1.2 %dynamic-slice_bitcast_fusion.1 = (bf16[2,64,1024]{2,1,0:T(8,128)(2,1)S(1)}, bf16[2,64,1024]{2,1,0:T(8,128)(2,1)S(1)}) fusion(bf16[2,4,64,1024]{3,2,1,0:T(8,128)(2,1)} %bitcast.24, s32[]{:T(128)S(6)} %select_n.33, s32[]{:T(128)S(6)} %select_n.31), kind=kLoop, calls=%fused_computation.1 | loop fusion | bytes 1048584 | tf_op jit(solution)/shard_map/reshape | solution.py:254
  1.8 3.1 %collective-permute-start.1 = (bf16[2,64,1024]{2,1,0:T(8,128)(2,1)S(1)}, bf16[2,64,1024]{2,1,0:T(8,128)(2,1)S(1)}, u32[]{:S(2)}, u32[]{:S(2)}) collective-permute-start(bf16[2,64,1024]{2,1,0:T(8,128)(2,1)S(1)} %get-tuple-element.20), channel_id=1, source_target_pairs={{0,8},{4,12},{8,0},{12,4},{16,24},{20,28},{24,16},{28,20},{1,9},{5... | collective-permute-start | bytes 786440 | tf_op jit(solution)/shard_map/ppermute | solution.py:182
  4.9 1.5 %collective-permute-start = (bf16[2,64,1024]{2,1,0:T(8,128)(2,1)S(1)}, bf16[2,64,1024]{2,1,0:T(8,128)(2,1)S(1)}, u32[]{:S(2)}, u32[]{:S(2)}) collective-permute-start(bf16[2,64,1024]{2,1,0:T(8,128)(2,1)S(1)} %get-tuple-element.21), channel_id=1, source_target_pairs={{0,4},{4,0},{8,12},{12,8},{16,20},{20,16},{24,28},{28,24},{1,5},{5... | collective-permute-start | bytes 786440 | tf_op jit(solution)/shard_map/ppermute | solution.py:182
  6.4 0.9 %sum_squares.1 = f32[2,4,1,128]{3,2,1,0:T(1,128)} custom-call(bf16[2,4,64,1024]{3,2,1,0:T(8,128)(2,1)S(1)} %bitcast.25), custom_call_target="tpu_custom_call" | custom-call | tf_op jit(solution)/shard_map/sum_squares/pallas_call | solution.py:264
  7.4 6.2 %all-to-all-start = ((f32[8,1,128]{2,1,0:T(1,128)}), f32[8,1,128]{2,1,0:T(1,128)S(1)}, u32[]{:S(2)}, u32[]{:S(2)}) async-start(f32[8,1,128]{2,1,0:T(1,128)} %bitcast.8), calls=%async_computation | async-start | bytes 8192 | tf_op jit(solution)/shard_map/all_to_all | solution.py:272
  13.6 2.9 %collective-permute-start.2 = (bf16[64,1024]{1,0:T(8,128)(2,1)S(1)}, bf16[64,1024]{1,0:T(8,128)(2,1)S(1)}, u32[]{:S(2)}, u32[]{:S(2)}) collective-permute-start(bf16[64,1024]{1,0:T(8,128)(2,1)S(1)} %get-tuple-element.19), channel_id=1, source_target_pairs={{0,12},{4,8},{8,4},{12,0},{16,28},{20,24},{24,20},{28,16},{1,13},{... | collective-permute-start | bytes 393224 | tf_op jit(solution)/shard_map/ppermute | solution.py:182
  16.6 3.4 %all-to-all-done = f32[8,1,128]{2,1,0:T(1,128)S(1)} async-done(((f32[8,1,128]{2,1,0:T(1,128)}), f32[8,1,128]{2,1,0:T(1,128)S(1)}, u32[]{:S(2)}, u32[]{:S(2)}) %all-to-all-start) | async-done | bytes 4128 | tf_op jit(solution)/shard_map/all_to_all | solution.py:272
  20.8 0.6 %collective-permute-start.4 = (s16[64,1024]{1,0:T(8,128)(2,1)S(1)}, s16[64,1024]{1,0:T(8,128)(2,1)S(1)}, u32[]{:S(2)}, u32[]{:S(2)}) collective-permute-start(s16[64,1024]{1,0:T(8,128)(2,1)S(1)} %proxy_blocks.1), channel_id=1, source_target_pairs={{0,16},{4,20},{8,24},{12,28},{16,0},{20,4},{24,8},{28,12},{1,17},{... | collective-permute-start | bytes 393224 | tf_op jit(solution)/shard_map/ppermute | solution.py:182
  21.4 0.6 owner_blocks.1
  22.0 6.1 %collective-permute-done.4.far_ref = s16[64,1024]{1,0:T(8,128)(2,1)S(1)} collective-permute-done((s16[64,1024]{1,0:T(8,128)(2,1)S(1)}, s16[64,1024]{1,0:T(8,128)(2,1)S(1)}, u32[]{:S(2)}, u32[]{:S(2)}) %collective-permute-start.4) | collective-permute-done | bytes 131104 | tf_op jit(solution)/shard_map/ppermute | solution.py:182
  28.1 0.7 %finish_blocks.1 = f32[32,1,128]{2,1,0:T(1,128)} custom-call(f32[64,1024]{1,0:T(8,128)S(1)} %get-tuple-element.12.near_ref, s16[64,1024]{1,0:T(8,128)(2,1)S(1)} %collective-permute-done.4.far_ref, f32[64,128]{1,0:T(8,128)S(1)} %get-tuple-element.16.scale_ref, f32[64,128]{1,0:T(8,128)S(1)} %get-tuple-element.17.step_ref), custom_call_target="tpu_custom_call" | custom-call | tf_op jit(solution)/shard_map/finish_blocks/pallas_call | solution.py:302
  28.8 2.5 %all-to-all-start.1 = ((f32[32,1,128]{2,1,0:T(1,128)}), f32[32,1,128]{2,1,0:T(1,128)S(1)}, u32[]{:S(2)}, u32[]{:S(2)}) async-start(f32[32,1,128]{2,1,0:T(1,128)} %finish_blocks.1), calls=%async_computation.1 | async-start | bytes 32768 | tf_op jit(solution)/shard_map/all_to_all | solution.py:315
  31.7 6.7 %all-to-all-done.1 = f32[32,1,128]{2,1,0:T(1,128)S(1)} async-done(((f32[32,1,128]{2,1,0:T(1,128)}), f32[32,1,128]{2,1,0:T(1,128)S(1)}, u32[]{:S(2)}, u32[]{:S(2)}) %all-to-all-start.1) | async-done | bytes 16416 | tf_op jit(solution)/shard_map/all_to_all | solution.py:315
  38.6 0.6 %collective-permute-start.10 = (bf16[64,1024]{1,0:T(8,128)(2,1)S(1)}, bf16[64,1024]{1,0:T(8,128)(2,1)S(1)}, u32[]{:S(2)}, u32[]{:S(2)}) collective-permute-start(bf16[64,1024]{1,0:T(8,128)(2,1)S(1)} %new_weights.1.refs_0_), channel_id=1, source_target_pairs={{0,8},{4,12},{8,0},{12,4},{16,24},{20,28},{24,16},{28,20},{1,9},{5... | collective-permute-start | bytes 393224 | tf_op jit(solution)/shard_map/ppermute | solution.py:182
  39.2 0.6 collective-permute-start.5
  40.3 5.2 %collective-permute-done.10.refs_2_ = bf16[64,1024]{1,0:T(8,128)(2,1)S(1)} collective-permute-done((bf16[64,1024]{1,0:T(8,128)(2,1)S(1)}, bf16[64,1024]{1,0:T(8,128)(2,1)S(1)}, u32[]{:S(2)}, u32[]{:S(2)}) %collective-permute-start.10) | collective-permute-done | bytes 131104 | tf_op jit(solution)/shard_map/ppermute | solution.py:182
  45.5 0.5 collective-permute-start.11
  46.1 1.8 %collective-permute-done.5.refs_4_ = bf16[64,1024]{1,0:T(8,128)(2,1)S(1)} collective-permute-done((bf16[64,1024]{1,0:T(8,128)(2,1)S(1)}, bf16[64,1024]{1,0:T(8,128)(2,1)S(1)}, u32[]{:S(2)}, u32[]{:S(2)}) %collective-permute-start.5) | collective-permute-done | bytes 131104 | tf_op jit(solution)/shard_map/ppermute | solution.py:182
  47.8 2.1 %collective-permute-start.7 = (bf16[64,1024]{1,0:T(8,128)(2,1)S(1)}, bf16[64,1024]{1,0:T(8,128)(2,1)S(1)}, u32[]{:S(2)}, u32[]{:S(2)}) collective-permute-start(bf16[64,1024]{1,0:T(8,128)(2,1)S(1)} %collective-permute-done.5.refs_4_), channel_id=1, source_target_pairs={{0,8},{4,12},{8,0},{12,4},{16,24},{20,28},{24,16},{28,20},{1,9},{5... | collective-permute-start | bytes 393224 | tf_op jit(solution)/shard_map/ppermute | solution.py:182
  49.9 1.4 %collective-permute-start.6 = (bf16[64,1024]{1,0:T(8,128)(2,1)S(1)}, bf16[64,1024]{1,0:T(8,128)(2,1)S(1)}, u32[]{:S(2)}, u32[]{:S(2)}) collective-permute-start(bf16[64,1024]{1,0:T(8,128)(2,1)S(1)} %collective-permute-done.5.refs_4_), channel_id=1, source_target_pairs={{0,4},{4,0},{8,12},{12,8},{16,20},{20,16},{24,28},{28,24},{1,5},{5... | collective-permute-start | bytes 393224 | tf_op jit(solution)/shard_map/ppermute | solution.py:182
  51.3 0.8 %update_grad.1 = f32[64,1024]{1,0:T(8,128)} custom-call(f32[32,128]{1,0:T(8,128)S(1)} %bitcast.29, f32[64,1024]{1,0:T(8,128)S(1)} %rotate_back.1.unrot_ref), custom_call_target="tpu_custom_call" | custom-call | tf_op jit(solution)/shard_map/update_grad/pallas_call | solution.py:324
  52.4 0.9 %place_own.1.refs_2_ = bf16[512,1024]{1,0:T(8,128)(2,1)} custom-call(bf16[64,1024]{1,0:T(8,128)(2,1)S(1)} %new_weights.1.refs_0_, bf16[64,1024]{1,0:T(8,128)(2,1)S(1)} %collective-permute-done.9.refs_1_, bf16[64,1024]{1,0:T(8,128)(2,1)S(1)} %collective-permute-done.10.refs_2_, bf16[64,1024]{1,0:T(8,128)(2,1)S(1)} %collective-permute-done.11.refs_3_, ...), custom_call_target="tpu_custom_call" | custom-call | tf_op jit(solution)/shard_map/place_own/pallas_call | solution.py:209
  54.3 0.7 %place_far.1.refs_1_ = bf16[512,1024]{1,0:T(8,128)(2,1)} custom-call(bf16[64,1024]{1,0:T(8,128)(2,1)S(1)} %collective-permute-done.7.refs_0_, bf16[64,1024]{1,0:T(8,128)(2,1)S(1)} %collective-permute-done.8.refs_1_, bf16[512,1024]{1,0:T(8,128)(2,1)} %place_own.1.refs_2_), custom_call_target="tpu_custom_call", output_to_operand_aliasing={{}: (2, {})} | custom-call | tf_op jit(solution)/shard_map/place_far/pallas_call | solution.py:209
  55.5 0.7 %place_last.1 = bf16[512,1024]{1,0:T(8,128)(2,1)} custom-call(bf16[64,1024]{1,0:T(8,128)(2,1)S(1)} %collective-permute-done.6.refs_0_, bf16[512,1024]{1,0:T(8,128)(2,1)} %place_far.1.refs_1_), custom_call_target="tpu_custom_call", output_to_operand_aliasing={{}: (1, {})} | custom-call | tf_op jit(solution)/shard_map/place_last/pallas_call | solution.py:209
  (28 shorter events, 3.7 us)
Async XLA Ops:
  0.6 5.8 %copy-start = (bf16[1,1,512,1024]{3,2,1,0:T(8,128)(2,1)S(1)}, bf16[1,1,512,1024]{3,2,1,0:T(8,128)(2,1)}, u32[]{:S(2)}) copy-start(bf16[1,1,512,1024]{3,2,1,0:T(8,128)(2,1)} %param.5) | copy-start | bytes 3145732
  1.8 18.2 %collective-permute-start.1 = (bf16[2,64,1024]{2,1,0:T(8,128)(2,1)S(1)}, bf16[2,64,1024]{2,1,0:T(8,128)(2,1)S(1)}, u32[]{:S(2)}, u32[]{:S(2)}) collective-permute-start(bf16[2,64,1024]{2,1,0:T(8,128)(2,1)S(1)} %get-tuple-element.20), channel_id=1, source_target_pairs={{0,8},{4,12},{8,0},{12,4},{16,24},{20,28},{24,16},{28,20},{1,9},{5... | collective-permute-start | bytes 786440 | tf_op jit(solution)/shard_map/ppermute | solution.py:182
  4.9 15.1 %collective-permute-start = (bf16[2,64,1024]{2,1,0:T(8,128)(2,1)S(1)}, bf16[2,64,1024]{2,1,0:T(8,128)(2,1)S(1)}, u32[]{:S(2)}, u32[]{:S(2)}) collective-permute-start(bf16[2,64,1024]{2,1,0:T(8,128)(2,1)S(1)} %get-tuple-element.21), channel_id=1, source_target_pairs={{0,4},{4,0},{8,12},{12,8},{16,20},{20,16},{24,28},{28,24},{1,5},{5... | collective-permute-start | bytes 786440 | tf_op jit(solution)/shard_map/ppermute | solution.py:182
  7.3 13.1 %collective-permute-start.3 = (bf16[64,1024]{1,0:T(8,128)(2,1)S(1)}, bf16[64,1024]{1,0:T(8,128)(2,1)S(1)}, u32[]{:S(2)}, u32[]{:S(2)}) collective-permute-start(bf16[64,1024]{1,0:T(8,128)(2,1)S(1)} %get-tuple-element.18), channel_id=1, source_target_pairs={{0,12},{4,8},{8,4},{12,0},{16,28},{20,24},{24,20},{28,16},{1,13},{... | collective-permute-start | bytes 393224 | tf_op jit(solution)/shard_map/ppermute | solution.py:182
  7.4 12.6 %all-to-all-start = ((f32[8,1,128]{2,1,0:T(1,128)}), f32[8,1,128]{2,1,0:T(1,128)S(1)}, u32[]{:S(2)}, u32[]{:S(2)}) async-start(f32[8,1,128]{2,1,0:T(1,128)} %bitcast.8), calls=%async_computation | async-start | bytes 8192 | tf_op jit(solution)/shard_map/all_to_all | solution.py:272
  13.6 7.8 %collective-permute-start.2 = (bf16[64,1024]{1,0:T(8,128)(2,1)S(1)}, bf16[64,1024]{1,0:T(8,128)(2,1)S(1)}, u32[]{:S(2)}, u32[]{:S(2)}) collective-permute-start(bf16[64,1024]{1,0:T(8,128)(2,1)S(1)} %get-tuple-element.19), channel_id=1, source_target_pairs={{0,12},{4,8},{8,4},{12,0},{16,28},{20,24},{24,20},{28,16},{1,13},{... | collective-permute-start | bytes 393224 | tf_op jit(solution)/shard_map/ppermute | solution.py:182
  16.5 3.5 %copy-start.1 = (bf16[256,256]{1,0:T(8,128)(2,1)S(1)}, bf16[256,256]{1,0:T(8,128)(2,1)}, u32[]{:S(2)}) copy-start(bf16[256,256]{1,0:T(8,128)(2,1)} %constant.37.clone.refs_6_.refs_5_.matrix_ref) | copy-start | bytes 393220
  16.5 3.5 %copy-start.4 = (s32[1,1024]{1,0:T(1,128)S(1)}, s32[1,1024]{1,0:T(1,128)}, u32[]{:S(2)}) copy-start(s32[1,1024]{1,0:T(1,128)} %sign_ref.1) | copy-start | bytes 12292
  20.8 7.3 %collective-permute-start.4 = (s16[64,1024]{1,0:T(8,128)(2,1)S(1)}, s16[64,1024]{1,0:T(8,128)(2,1)S(1)}, u32[]{:S(2)}, u32[]{:S(2)}) collective-permute-start(s16[64,1024]{1,0:T(8,128)(2,1)S(1)} %proxy_blocks.1), channel_id=1, source_target_pairs={{0,16},{4,20},{8,24},{12,28},{16,0},{20,4},{24,8},{28,12},{1,17},{... | collective-permute-start | bytes 393224 | tf_op jit(solution)/shard_map/ppermute | solution.py:182
  28.8 9.6 %all-to-all-start.1 = ((f32[32,1,128]{2,1,0:T(1,128)}), f32[32,1,128]{2,1,0:T(1,128)S(1)}, u32[]{:S(2)}, u32[]{:S(2)}) async-start(f32[32,1,128]{2,1,0:T(1,128)} %finish_blocks.1), calls=%async_computation.1 | async-start | bytes 32768 | tf_op jit(solution)/shard_map/all_to_all | solution.py:315
  31.3 7.1 %copy-start.2 = (bf16[1,64,1024]{2,1,0:T(8,128)(2,1)S(1)}, bf16[1,64,1024]{2,1,0:T(8,128)(2,1)}, u32[]{:S(2)}) copy-start(bf16[1,64,1024]{2,1,0:T(8,128)(2,1)} %param.7) | copy-start | bytes 393220
  31.3 7.1 %copy-start.3 = (bf16[1,64,1024]{2,1,0:T(8,128)(2,1)S(1)}, bf16[1,64,1024]{2,1,0:T(8,128)(2,1)}, u32[]{:S(2)}) copy-start(bf16[1,64,1024]{2,1,0:T(8,128)(2,1)} %param.8) | copy-start | bytes 393220
  38.6 6.9 %collective-permute-start.10 = (bf16[64,1024]{1,0:T(8,128)(2,1)S(1)}, bf16[64,1024]{1,0:T(8,128)(2,1)S(1)}, u32[]{:S(2)}, u32[]{:S(2)}) collective-permute-start(bf16[64,1024]{1,0:T(8,128)(2,1)S(1)} %new_weights.1.refs_0_), channel_id=1, source_target_pairs={{0,8},{4,12},{8,0},{12,4},{16,24},{20,28},{24,16},{28,20},{1,9},{5... | collective-permute-start | bytes 393224 | tf_op jit(solution)/shard_map/ppermute | solution.py:182
  39.2 8.6 %collective-permute-start.5 = (bf16[64,1024]{1,0:T(8,128)(2,1)S(1)}, bf16[64,1024]{1,0:T(8,128)(2,1)S(1)}, u32[]{:S(2)}, u32[]{:S(2)}) collective-permute-start(bf16[64,1024]{1,0:T(8,128)(2,1)S(1)} %new_weights.1.refs_0_), channel_id=1, source_target_pairs={{0,16},{4,20},{8,24},{12,28},{16,0},{20,4},{24,8},{28,12},{1,17},{... | collective-permute-start | bytes 393224 | tf_op jit(solution)/shard_map/ppermute | solution.py:182
  39.8 12.4 %collective-permute-start.9 = (bf16[64,1024]{1,0:T(8,128)(2,1)S(1)}, bf16[64,1024]{1,0:T(8,128)(2,1)S(1)}, u32[]{:S(2)}, u32[]{:S(2)}) collective-permute-start(bf16[64,1024]{1,0:T(8,128)(2,1)S(1)} %new_weights.1.refs_0_), channel_id=1, source_target_pairs={{0,4},{4,0},{8,12},{12,8},{16,20},{20,16},{24,28},{28,24},{1,5},{5... | collective-permute-start | bytes 393224 | tf_op jit(solution)/shard_map/ppermute | solution.py:182
  45.5 6.9 %collective-permute-start.11 = (bf16[64,1024]{1,0:T(8,128)(2,1)S(1)}, bf16[64,1024]{1,0:T(8,128)(2,1)S(1)}, u32[]{:S(2)}, u32[]{:S(2)}) collective-permute-start(bf16[64,1024]{1,0:T(8,128)(2,1)S(1)} %collective-permute-done.10.refs_2_), channel_id=1, source_target_pairs={{0,4},{4,0},{8,12},{12,8},{16,20},{20,16},{24,28},{28,24},{1,5},{5... | collective-permute-start | bytes 393224 | tf_op jit(solution)/shard_map/ppermute | solution.py:182
  47.8 6.0 %collective-permute-start.8 = (bf16[64,1024]{1,0:T(8,128)(2,1)S(1)}, bf16[64,1024]{1,0:T(8,128)(2,1)S(1)}, u32[]{:S(2)}, u32[]{:S(2)}) collective-permute-start(bf16[64,1024]{1,0:T(8,128)(2,1)S(1)} %collective-permute-done.5.refs_4_), channel_id=1, source_target_pairs={{0,12},{4,8},{8,4},{12,0},{16,28},{20,24},{24,20},{28,16},{1,13},{... | collective-permute-start | bytes 393224 | tf_op jit(solution)/shard_map/ppermute | solution.py:182
  47.8 6.4 %collective-permute-start.7 = (bf16[64,1024]{1,0:T(8,128)(2,1)S(1)}, bf16[64,1024]{1,0:T(8,128)(2,1)S(1)}, u32[]{:S(2)}, u32[]{:S(2)}) collective-permute-start(bf16[64,1024]{1,0:T(8,128)(2,1)S(1)} %collective-permute-done.5.refs_4_), channel_id=1, source_target_pairs={{0,8},{4,12},{8,0},{12,4},{16,24},{20,28},{24,16},{28,20},{1,9},{5... | collective-permute-start | bytes 393224 | tf_op jit(solution)/shard_map/ppermute | solution.py:182
  49.9 5.6 %collective-permute-start.6 = (bf16[64,1024]{1,0:T(8,128)(2,1)S(1)}, bf16[64,1024]{1,0:T(8,128)(2,1)S(1)}, u32[]{:S(2)}, u32[]{:S(2)}) collective-permute-start(bf16[64,1024]{1,0:T(8,128)(2,1)S(1)} %collective-permute-done.5.refs_4_), channel_id=1, source_target_pairs={{0,4},{4,0},{8,12},{12,8},{16,20},{20,16},{24,28},{28,24},{1,5},{5... | collective-permute-start | bytes 393224 | tf_op jit(solution)/shard_map/ppermute | solution.py:182
